TPU v7x, 32 devices: a whole 2x2x4 slice. The times are simulated.
32 devices in a mesh: stream: 4 (over z), radial: 4 (over y, core), snap: 2 (over x).
Axes of the slice: x: 2, y: 2, z: 4, core: 2. Of those that a mesh axis runs over, the one named last changes fastest.
Arguments:
- fields: bfloat16 [2, 8, 32, 32, 128], P('snap', None, 'stream', 'radial'), may hold values from -6 to 6
- first_weight: bfloat16 [27, 16, 8], replicated, may hold values from -0.4375 to 0.4375
- first_bias: float32 [16], replicated, may hold values from -3 to 3
- second_weight: bfloat16 [27, 16, 16], replicated, may hold values from -0.3125 to 0.3125
- second_bias: float32 [16], replicated, may hold values from -3 to 3
- cotangent: bfloat16 [2, 16, 32, 32, 128], P('snap', None, 'stream', 'radial'), may hold values from -6 to 6
Outputs:
- closure: bfloat16 [2, 16, 32, 32, 128], P('snap', None, 'stream', 'radial')
- first_grad: float32 [27, 16, 8], replicated
- second_grad: float32 [27, 16, 16], replicated
- bias_grad: float32 [16], replicated
All inputs are finite; a program needn't handle non-finite values.
Results may differ from a plain program's by a relative error of at most 0.017.
Values may be sent and summed in bfloat16 or wider, within the bound.
No kernel may reach another device: no remote copies, remote signals or barrier semaphores. Data moves between devices by JAX's collectives and lax.ppermute only.
A program may use at most 128 MiB of HBM per device.

v0:
```python
import functools

import numpy as np
import jax
import jax.numpy as jnp
from jax import lax
from jax.experimental import pallas as pl
from jax.experimental.pallas import tpu as pltpu
from jax.sharding import PartitionSpec as P

F32 = jnp.float32
BF16 = jnp.bfloat16
YB = 8
Z = 128
CI = 8
CH = 16
FR = CI * 16
HR = 256


def lane_rows():
    one = np.concatenate([np.tile(np.arange(8), CI), np.tile(np.arange(-4, 0), CI), np.tile(np.arange(8, 12), CI)])
    chan = np.concatenate([np.repeat(np.arange(CI), 8), np.repeat(np.arange(CI), 4), np.repeat(np.arange(CI), 4)])
    y1 = np.tile(one, 3)
    e1 = np.zeros((3 * CI, 3 * FR), np.float32)
    for c in range(3):
        e1[c * CI + chan, c * FR + np.arange(FR)] = 1
    halo_y = np.concatenate([np.tile([-2, -1], CH), np.tile([8, 9], CH)])
    halo_c = np.concatenate([np.repeat(np.arange(CH), 2)] * 2)
    y2 = np.concatenate([np.tile(np.tile(np.arange(8), CH), 3), np.tile(halo_y, 3), np.full(64, 100)])
    e2 = np.zeros((3 * CH, 640), np.float32)
    for c in range(3):
        e2[c * CH + np.repeat(np.arange(CH), 8), c * 128 + np.arange(128)] = 1
        e2[c * CH + halo_c, 384 + c * 64 + np.arange(64)] = 1
    rows_y = np.concatenate([np.tile(np.arange(8), CH), halo_y])
    rows_c = np.concatenate([np.repeat(np.arange(CH), 8), halo_c])
    expand = np.zeros((192, CH), np.float32)
    expand[np.arange(192), rows_c] = 1
    return e1, y1, e2, y2, rows_y, expand


def pick_rows():
    pick = np.zeros((128, 192), np.float32)
    row = 0
    for base in (0, 4):
        for ch in range(CI):
            for y in range(4):
                pick[row, ch * 8 + base + y] = 1
                row += 1
        for ch in range(CH):
            for y in range(2):
                pick[row, 64 + ch * 8 + (0 if base == 0 else 6) + y] = 1
                row += 1
    return pick


def plane(ref, x):
    v = ref[0, :, x].astype(F32)
    return v.reshape(v.shape[0] * v.shape[1], v.shape[2])


def pack_kernel(fields, cot, pick, low, high):
    for x in range(fields.shape[2]):
        rows = jnp.concatenate([plane(fields, x), plane(cot, x)], axis=0).astype(BF16)
        got = jnp.dot(pick[...], rows, preferred_element_type=F32).astype(BF16)
        low[x] = got[:64]
        high[x] = got[64:]


def band_kernel(w1, w2, wb, e1, e2, expand, y1, y2, rows_y, t1, t2, tb):
    ry = rows_y[...]
    for w, e, ys, t, rows in ((w1, e1, y1, t1, 192), (w2, e2, y2, t2, 128), (wb, e2, y2, tb, 128)):
        width = e.shape[1]
        wide = jnp.dot(w[...], e[...], preferred_element_type=F32).astype(BF16)
        for a in range(3):
            total = jnp.zeros((rows, width), F32)
            for b in range(3):
                part = jnp.dot(expand[:rows], wide[(a * 3 + b) * CH:(a * 3 + b + 1) * CH], preferred_element_type=F32)
                total = jnp.where(ys[...] == ry[:rows] + float(2 * (b - 1)), part, total)
            t[:, a * width:(a + 1) * width] = total.astype(BF16)


def shifted(v):
    lane = lax.broadcasted_iota(jnp.int32, v.shape, 1)
    before = jnp.where(lane >= 2, pltpu.roll(v, 2, 1), 0.0)
    after = jnp.where(lane < Z - 2, pltpu.roll(v, Z - 2, 1), 0.0)
    return before.astype(BF16), v.astype(BF16), after.astype(BF16)


def store_wide(ref, pair, side, v):
    at = slice(side * Z, (side + 1) * Z)
    for c, piece in enumerate(shifted(v)):
        base = pair * 640
        ref[base + c * 128:base + (c + 1) * 128, at] = piece[:128]
        ref[base + 384 + c * 64:base + 384 + (c + 1) * 64, at] = piece[128:]


def main_kernel(counts, fields, cot, rlo, rhi, xlo, xhi, t1, t2, tb, b1, b2, e1t, e2t, y1, y2, yo,
                closure, payload, fs, hs, cs, slope):
    stream, radial = lax.axis_index("stream"), lax.axis_index("radial")
    zeros = jnp.zeros((64, 256), BF16)
    for pair in range(6):
        hs[pair * 640 + 576:(pair + 1) * 640] = zeros
        cs[pair * 640 + 576:(pair + 1) * 640] = zeros
    for p in range(16):
        x = p - 4
        if x < 0:
            v = xlo[p * 128:(p + 1) * 128].astype(F32)
        elif x >= 8:
            v = xhi[(x - 8) * 128:(x - 7) * 128].astype(F32)
        else:
            v = jnp.concatenate([plane(fields, x), rlo[x, :32].astype(F32), rhi[x, :32].astype(F32)], axis=0)
        at = slice((p % 2) * Z, (p % 2 + 1) * Z)
        for c, piece in enumerate(shifted(v)):
            fs[(p // 2) * 384 + c * 128:(p // 2) * 384 + (c + 1) * 128, at] = piece
    for p in range(12):
        x = p - 2
        if x < 0:
            v = xlo[512 + p * 192:512 + (p + 1) * 192].astype(F32)
        elif x >= 8:
            v = xhi[512 + (x - 8) * 192:512 + (x - 7) * 192].astype(F32)
        else:
            v = jnp.concatenate([plane(cot, x), rlo[x, 32:].astype(F32), rhi[x, 32:].astype(F32)], axis=0)
        store_wide(cs, p // 2, p % 2, v)
    keep_low = jnp.where(radial > 0, 1.0, 0.0)
    keep_high = jnp.where(radial < counts[1] - 1, 1.0, 0.0)
    keep_first = jnp.where(stream > 0, 1.0, 0.0)
    keep_last = jnp.where(stream < counts[0] - 1, 1.0, 0.0)
    for k in range(6):
        pre = jnp.dot(t1[...], fs[k * 384:(k + 3) * 384], preferred_element_type=F32) + b1[...]
        phi = 0.5 * (1.0 + lax.erf(pre * 0.7071067811865476))
        hidden = pre * phi
        if 1 <= k <= 4:
            local, share = pre[:128], phi[:128]
            slope[k - 1] = share + local * jnp.exp(-0.5 * local * local) * 0.3989422804014327
        hidden = jnp.concatenate([hidden[:128], hidden[128:160] * keep_low, hidden[160:] * keep_high], axis=0)
        if k == 0:
            hidden = hidden * keep_first
        if k == 5:
            hidden = hidden * keep_last
        hidden = hidden.astype(BF16).astype(F32)
        for side in range(2):
            store_wide(hs, k, side, hidden[:, side * Z:(side + 1) * Z])
    g1 = jnp.zeros((128, 1152), F32)
    g2 = jnp.zeros((128, 1920), F32)
    bias = jnp.zeros((128, 256), F32)
    over_lanes = (((1,), (1,)), ((), ()))
    for k in range(4):
        back = jnp.dot(tb[...], cs[k * 640:(k + 3) * 640], preferred_element_type=F32)
        dpre = (back * slope[k]).astype(BF16)
        bias = bias + dpre.astype(F32)
        g1 = g1 + lax.dot_general(dpre, fs[(k + 1) * 384:(k + 4) * 384], over_lanes, preferred_element_type=F32)
        here = cs[(k + 1) * 640 + 128:(k + 1) * 640 + 256]
        g2 = g2 + lax.dot_general(here, hs[k * 640:(k + 3) * 640], over_lanes, preferred_element_type=F32)
    bias = jnp.sum(bias, axis=1, keepdims=True)
    spot = lax.broadcasted_iota(jnp.int32, (128, 128), 1) == 120
    for a in range(3):
        for b in range(3):
            off = float(2 * (b - 1))
            one = jnp.where(y1[...] == yo[...] + off, g1[:, a * 384:(a + 1) * 384], 0.0).astype(BF16)
            two = jnp.where(y2[...] == yo[...] + off, g2[:, a * 640:(a + 1) * 640], 0.0).astype(BF16)
            both = jnp.dot(one, e1t[...], preferred_element_type=F32) + jnp.dot(two, e2t[...], preferred_element_type=F32)
            if a == 0 and b == 0:
                both = jnp.where(spot, bias, both)
            payload[(a * 3 + b) * CH:(a * 3 + b + 1) * CH] = jnp.sum(both.reshape(CH, 8, 128), axis=1).astype(BF16)
    for k in range(4):
        out = (jnp.dot(t2[...], hs[k * 640:(k + 3) * 640], preferred_element_type=F32) + b2[...]).astype(BF16)
        for side in range(2):
            closure[0, :, 2 * k + side] = out[:, side * Z:(side + 1) * Z].reshape(CH, 8, Z)


def add_kernel(norm, parts, total):
    acc = parts[0].astype(F32)
    for d in range(1, parts.shape[0]):
        acc = acc + parts[d].astype(F32)
    total[...] = acc * norm


def call(kernel, outs, name, scratch=(), flops=10_000_000):
    return pl.pallas_call(
        kernel,
        out_shape=outs,
        scratch_shapes=list(scratch),
        compiler_params=pltpu.CompilerParams(vmem_limit_bytes=48 * 1024 * 1024),
        cost_estimate=pl.CostEstimate(flops=flops, bytes_accessed=1_000_000, transcendentals=0),
        name=name,
    )


def shape(*dims, dtype=BF16):
    return jax.ShapeDtypeStruct(dims, dtype)


def exchange(low, high, axis):
    count = lax.axis_size(axis)
    up = [(i, i + 1) for i in range(count - 1)]
    down = [(j, i) for i, j in up]
    return lax.ppermute(high, axis, up), lax.ppermute(low, axis, down)


def local(fields, first_weight, first_bias, second_weight, second_bias, cotangent):
    e1, y1, e2, y2, rows_y, expand = lane_rows()
    y1 = jnp.asarray(y1[None], F32)
    y2 = jnp.asarray(y2[None], F32)
    ry = jnp.asarray(rows_y[:, None], F32)
    lanes_x = fields.shape[2]
    low, high = call(pack_kernel, (shape(lanes_x, 64, Z),) * 2, "pack_strips")(fields, cotangent, jnp.asarray(pick_rows(), BF16))
    rlo, rhi = exchange(low, high, "radial")

    w1 = first_weight.reshape(3, 3, 3, CH, CI).transpose(0, 1, 3, 2, 4).reshape(9 * CH, 3 * CI)
    w2 = second_weight.reshape(3, 3, 3, CH, CH)
    wb = w2[::-1, ::-1, ::-1].transpose(0, 1, 4, 2, 3).reshape(9 * CH, 3 * CH)
    w2 = w2.transpose(0, 1, 3, 2, 4).reshape(9 * CH, 3 * CH)
    t1, t2, tb = call(band_kernel, (shape(192, 1152), shape(128, 1920), shape(128, 1920)), "band_weights")(
        w1, w2, wb, jnp.asarray(e1, BF16), jnp.asarray(e2, BF16), jnp.asarray(expand, BF16), y1, y2, ry)

    def strip(xs, qs):
        pieces = []
        for x in xs:
            pieces += [fields[0, :, x].reshape(64, Z), rlo[x, :32], rhi[x, :32]]
        for x in qs:
            pieces += [cotangent[0, :, x].reshape(128, Z), rlo[x, 32:], rhi[x, 32:]]
        return jnp.concatenate(pieces, axis=0)

    xlo, xhi = exchange(strip((0, 1, 2, 3), (0, 1)), strip((4, 5, 6, 7), (6, 7)), "stream")
    e1t = np.zeros((384, 128), np.float32)
    e1t[:, :24] = e1.T
    e2t = np.zeros((640, 128), np.float32)
    e2t[:, 64:112] = e2.T
    rows_o = np.argmax(expand, axis=1)
    b1 = first_bias[rows_o][:, None]
    b2 = second_bias[rows_o[:128]][:, None]
    counts = (lax.axis_size("stream"), lax.axis_size("radial"))
    closure, payload = call(
        functools.partial(main_kernel, counts),
        (shape(*cotangent.shape), shape(9 * CH, 128)),
        "layers",
        (
            pltpu.VMEM((8 * 384, 256), BF16),
            pltpu.VMEM((6 * 640, 256), BF16),
            pltpu.VMEM((6 * 640, 256), BF16),
            pltpu.VMEM((4, 128, 256), F32),
        ),
        flops=3_000_000_000,
    )(fields, cotangent, rlo, rhi, xlo, xhi, t1, t2, tb, b1, b2, jnp.asarray(e1t, BF16), jnp.asarray(e2t, BF16), y1, y2, ry[:128])
    parts = lax.all_gather(payload, ("stream", "radial", "snap"))
    count = fields.shape[0] * lax.axis_size("snap") * fields.shape[2] * counts[0] * fields.shape[3] * counts[1] * fields.shape[4]
    norm = float(1.0 / np.sqrt(np.float32(count)))
    total = call(functools.partial(add_kernel, norm), shape(9 * CH, 128, dtype=F32), "add_parts")(parts)
    total = total.reshape(3, 3, CH, 128)
    first = total[..., :24].reshape(3, 3, CH, 3, CI).transpose(0, 1, 3, 2, 4).reshape(27, CH, CI)
    second = total[..., 64:112].reshape(3, 3, CH, 3, CH).transpose(0, 1, 3, 2, 4).reshape(27, CH, CH)
    return (closure, first, second, total[0, 0, :, 120])


def solution(mesh):
    split = P("snap", None, "stream", "radial", None)
    return jax.shard_map(
        local,
        mesh=mesh,
        in_specs=(split, P(), P(), P(), P(), split),
        out_specs=(split, P(), P(), P()),
        check_vma=False,
    )
```

profile of v0, /device:TPU:0, one launch (start us, length us, event | category | flops | bytes accessed | tf_op | source)
XLA Modules:
  0.0 124.7 jit_solution(6923332731611969894)
XLA Ops:
  7.2 0.0 copy-start.16
  7.2 0.0 copy-start.17
  7.2 0.0 copy-start.18
  7.2 0.0 copy-start.19
  7.2 0.0 copy-start.20
  7.2 0.0 copy-start.21
  7.2 0.0 copy-start.22
  7.3 0.0 copy-start.23
  7.3 0.0 copy-start.24
  7.3 0.0 copy-start.25
  7.3 0.0 copy-start.26
  7.3 0.0 copy-start.27
  7.3 0.0 copy-start.28
  7.3 0.0 copy-start.29
  7.3 0.0 copy-start.30
  7.4 0.0 all-gather.3.cloned.1.call-start
  7.4 0.9 copy-done.1
  8.4 0.9 copy-done.3
  9.3 0.8 copy-done.6
  10.1 0.3 pack_strips.1
  10.4 2.4 %collective-permute-start = (bf16[8,64,128]{2,1,0:T(8,128)(2,1)S(1)}, bf16[8,64,128]{2,1,0:T(8,128)(2,1)S(1)}, u32[]{:S(2)}, u32[]{:S(2)}) collective-permute-start(bf16[8,64,128]{2,1,0:T(8,128)(2,1)S(1)} %get-tuple-element.11), channel_id=1, source_target_pairs={{0,2},{2,4},{4,6},{1,3},{3,5},{5,7},{8,10},{10,12},{12,14},{9,11},... | collective-permute-start | bytes 393224 | tf_op jit(solution)/shard_map/ppermute | solution.py:198
  12.8 1.3 %collective-permute-start.1 = (bf16[8,64,128]{2,1,0:T(8,128)(2,1)S(1)}, bf16[8,64,128]{2,1,0:T(8,128)(2,1)S(1)}, u32[]{:S(2)}, u32[]{:S(2)}) collective-permute-start(bf16[8,64,128]{2,1,0:T(8,128)(2,1)S(1)} %get-tuple-element.12), channel_id=1, source_target_pairs={{2,0},{4,2},{6,4},{3,1},{5,3},{7,5},{10,8},{12,10},{14,12},{11,9},... | collective-permute-start | bytes 393224 | tf_op jit(solution)/shard_map/ppermute | solution.py:198
  14.1 1.9 %fusion = (f32[1]{0:T(128)}, f32[1]{0:T(128)}, f32[1]{0:T(128)}, f32[1]{0:T(128)}, f32[1]{0:T(128)}, /*index=5*/f32[1]{0:T(128)}, f32[1]{0:T(128)}, f32[1]{0:T(1...) fusion(f32[16]{0:T(128)} %param.23), kind=kLoop, calls=%fused_computation.63 | loop fusion | bytes 128 | tf_op jit(solution)/shard_map/gather | solution.py:232
  16.0 10.9 %select_bitcast_fusion = f32[128,1]{0,1:T(1,128)S(1)} fusion(pred[128]{0:T(512)(128)(4,1)} %constant.96, pred[128]{0:T(512)(128)(4,1)} %constant.97, pred[128]{0:T(512)(128)(4,1)} %constant.98, pred[128]{0:T(512)(128)(4,1)} %constant.99, pred[128]{0:T(512)(128)(4,1)} %constant.100, pred[128]{0:T(512)(128)(4,1)} %constant.101, pred[128]{0:T(512)(128)(4,1)} %constant.102, ...), kind=kLoop, calls=%fused_computation.62 | loop fusion | flops 1920 | bytes 2496 | tf_op jit(solution)/shard_map/broadcast_in_dim | solution.py:232
  26.9 0.9 copy.30
  27.8 0.1 reshape.39
  27.9 0.1 copy.35.w1
  28.1 0.1 copy.39.b2
  28.2 1.9 %fusion.1 = (f32[1]{0:T(128)}, f32[1]{0:T(128)}, f32[1]{0:T(128)}, f32[1]{0:T(128)}, f32[1]{0:T(128)}, /*index=5*/f32[1]{0:T(128)}, f32[1]{0:T(128)}, f32[1]{0:T...) fusion(f32[16]{0:T(128)} %param.21), kind=kLoop, calls=%fused_computation.64 | loop fusion | bytes 128 | tf_op jit(solution)/shard_map/gather | solution.py:231
  30.1 0.0 collective-permute-done.rlo
  30.2 0.0 copy-start.5
  30.2 0.0 copy-start.7
  30.2 0.0 copy-start.8
  30.2 0.0 copy-start.9
  30.2 0.0 copy-start.10
  30.2 0.0 copy-start.11
  30.2 0.0 collective-permute-done.1.rhi
  30.3 0.8 constant_dynamic-update-slice_fusion.32
  31.1 0.0 copy-start.12
  31.1 0.0 copy-start.13
  31.1 0.0 copy-start.14
  31.3 1.3 %collective-permute-start.3 = (bf16[896,128]{1,0:T(8,128)(2,1)S(1)}, bf16[896,128]{1,0:T(8,128)(2,1)S(1)}, u32[]{:S(2)}, u32[]{:S(2)}) collective-permute-start(bf16[896,128]{1,0:T(8,128)(2,1)S(1)} %get-tuple-element.26), channel_id=1, source_target_pairs={{8,0},{16,8},{24,16},{9,1},{17,9},{25,17},{10,2},{18,10},{26,18},{... | collective-permute-start | bytes 688136 | tf_op jit(solution)/shard_map/ppermute | solution.py:198
  32.6 5.0 %collective-permute-start.2 = (bf16[896,128]{1,0:T(8,128)(2,1)S(1)}, bf16[896,128]{1,0:T(8,128)(2,1)S(1)}, u32[]{:S(2)}, u32[]{:S(2)}) collective-permute-start(bf16[896,128]{1,0:T(8,128)(2,1)S(1)} %get-tuple-element.27), channel_id=1, source_target_pairs={{0,8},{8,16},{16,24},{1,9},{9,17},{17,25},{2,10},{10,18},{18,26},{... | collective-permute-start | bytes 688136 | tf_op jit(solution)/shard_map/ppermute | solution.py:198
  37.7 10.0 %select_select_fusion = f32[192]{0:T(256)S(1)} fusion(pred[192]{0:T(512)(128)(4,1)S(1)} %copy-done.30, pred[192]{0:T(512)(128)(4,1)S(1)} %copy-done.29, pred[192]{0:T(512)(128)(4,1)S(1)} %copy-done.28, pred[192]{0:T(512)(128)(4,1)S(1)} %copy-done.27, pred[192]{0:T(512)(128)(4,1)S(1)} %copy-done.26, pred[192]{0:T(512)(128)(4,1)S(1)} %copy-done.25, ...), kind=kLoop, calls=%fused_computation.61 | loop fusion | flops 2880 | bytes 3712 | tf_op jit(solution)/shard_map/gather | solution.py:231
  47.8 0.1 copy.38.b1
  47.9 0.2 copy.32
  48.1 0.1 copy.46
  48.3 0.1 reshape.96.wb
  48.4 0.1 copy.45
  48.5 0.1 reshape.95.w2
  48.6 1.7 %band_weights.1 = (bf16[192,1152]{1,0:T(8,128)(2,1)S(1)}, bf16[128,1920]{1,0:T(8,128)(2,1)S(1)}, bf16[128,1920]{1,0:T(8,128)(2,1)S(1)}) custom-call(bf16[144,24]{1,0:T(8,128)(2,1)S(1)} %copy.35.w1, bf16[144,48]{1,0:T(8,128)(2,1)S(1)} %reshape.95.w2, bf16[144,48]{1,0:T(8,128)(2,1)S(1)} %reshape.96.wb, bf16[24,384]{1,0:T(8,128)(2,1)S(1)} %copy-done.9, ...), custom_call_target="tpu_custom_call" | custom-call | flops 10000000 | bytes 1000000 | tf_op jit(solution)/shard_map/band_weights/pallas_call | solution.py:214
  50.3 0.0 collective-permute-done.3.xhi
  50.4 5.9 %layers.1 = (bf16[1,16,8,8,128]{4,3,2,1,0:T(8,128)(2,1)}, bf16[144,128]{1,0:T(8,128)(2,1)}) custom-call(bf16[1,8,8,8,128]{4,3,2,1,0:T(8,128)(2,1)S(1)} %copy-done.4, bf16[1,16,8,8,128]{4,3,2,1,0:T(8,128)(2,1)S(1)} %copy-done.2, bf16[8,64,128]{2,1,0:T(8,128)(2,1)S(1)} %collective-permute-done.rlo, bf16[8,64,128]{2,1,0:T(8,128)(2,1)S(1)} %collective-permute-done.1.rhi, ...), custom_call_target="tpu_custom_call" | custom-call | flops 3000000000 | bytes 1000000 | tf_op jit(solution)/shard_map/layers/pallas_call | solution.py:234
  56.3 0.0 all-gather.3.cloned.1.call-update
  56.3 57.5 %all-gather.3.cloned.1.call-done = bf16[4608,128]{1,0:T(8,128)(2,1)} async-done(((bf16[144,128]{1,0:T(8,128)(2,1)}), bf16[4608,128]{1,0:T(8,128)(2,1)}) %all-gather.3.cloned.1.call-update) | async-done | bytes 1179664 | tf_op jit(solution)/shard_map/all_gather | solution.py:246
  113.8 1.3 %copy-done = bf16[4608,128]{1,0:T(8,128)(2,1)S(1)} copy-done((bf16[4608,128]{1,0:T(8,128)(2,1)S(1)}, bf16[4608,128]{1,0:T(8,128)(2,1)}, u32[]{:S(2)}) %copy-start) | copy-done | bytes 1179672
  115.1 0.2 add_parts.1
  115.2 0.1 slice.220
  115.3 0.1 slice.219
  115.4 0.6 copy.50
  116.0 0.1 copy.49
  116.1 0.8 copy.43
  116.8 0.2 reshape.46
  117.0 0.8 copy.44
  (55 shorter events, 0.3 us)
Async XLA Ops:
  7.2 30.4 %copy-start.16 = (pred[192]{0:T(512)(128)(4,1)S(1)}, pred[192]{0:T(512)(128)(4,1)}, u32[]{:S(2)}) copy-start(pred[192]{0:T(512)(128)(4,1)} %constant.93) | copy-start | bytes 580
  7.2 30.4 %copy-start.17 = (pred[192]{0:T(512)(128)(4,1)S(1)}, pred[192]{0:T(512)(128)(4,1)}, u32[]{:S(2)}) copy-start(pred[192]{0:T(512)(128)(4,1)} %constant.92) | copy-start | bytes 580
  7.2 30.4 %copy-start.18 = (pred[192]{0:T(512)(128)(4,1)S(1)}, pred[192]{0:T(512)(128)(4,1)}, u32[]{:S(2)}) copy-start(pred[192]{0:T(512)(128)(4,1)} %constant.91) | copy-start | bytes 580
  7.2 30.4 %copy-start.19 = (pred[192]{0:T(512)(128)(4,1)S(1)}, pred[192]{0:T(512)(128)(4,1)}, u32[]{:S(2)}) copy-start(pred[192]{0:T(512)(128)(4,1)} %constant.90) | copy-start | bytes 580
  7.2 30.4 %copy-start.20 = (pred[192]{0:T(512)(128)(4,1)S(1)}, pred[192]{0:T(512)(128)(4,1)}, u32[]{:S(2)}) copy-start(pred[192]{0:T(512)(128)(4,1)} %constant.89) | copy-start | bytes 580
  7.2 30.4 %copy-start.21 = (pred[192]{0:T(512)(128)(4,1)S(1)}, pred[192]{0:T(512)(128)(4,1)}, u32[]{:S(2)}) copy-start(pred[192]{0:T(512)(128)(4,1)} %constant.88) | copy-start | bytes 580
  7.2 30.4 %copy-start.22 = (pred[192]{0:T(512)(128)(4,1)S(1)}, pred[192]{0:T(512)(128)(4,1)}, u32[]{:S(2)}) copy-start(pred[192]{0:T(512)(128)(4,1)} %constant.87) | copy-start | bytes 580
  7.3 30.4 %copy-start.23 = (pred[192]{0:T(512)(128)(4,1)S(1)}, pred[192]{0:T(512)(128)(4,1)}, u32[]{:S(2)}) copy-start(pred[192]{0:T(512)(128)(4,1)} %constant.86) | copy-start | bytes 580
  7.3 30.4 %copy-start.24 = (pred[192]{0:T(512)(128)(4,1)S(1)}, pred[192]{0:T(512)(128)(4,1)}, u32[]{:S(2)}) copy-start(pred[192]{0:T(512)(128)(4,1)} %constant.85) | copy-start | bytes 580
  7.3 30.4 %copy-start.25 = (pred[192]{0:T(512)(128)(4,1)S(1)}, pred[192]{0:T(512)(128)(4,1)}, u32[]{:S(2)}) copy-start(pred[192]{0:T(512)(128)(4,1)} %constant.84) | copy-start | bytes 580
  7.3 30.4 %copy-start.26 = (pred[192]{0:T(512)(128)(4,1)S(1)}, pred[192]{0:T(512)(128)(4,1)}, u32[]{:S(2)}) copy-start(pred[192]{0:T(512)(128)(4,1)} %constant.83) | copy-start | bytes 580
  7.3 30.4 %copy-start.27 = (pred[192]{0:T(512)(128)(4,1)S(1)}, pred[192]{0:T(512)(128)(4,1)}, u32[]{:S(2)}) copy-start(pred[192]{0:T(512)(128)(4,1)} %constant.82) | copy-start | bytes 580
  7.3 30.4 %copy-start.28 = (pred[192]{0:T(512)(128)(4,1)S(1)}, pred[192]{0:T(512)(128)(4,1)}, u32[]{:S(2)}) copy-start(pred[192]{0:T(512)(128)(4,1)} %constant.81) | copy-start | bytes 580
  7.3 30.4 %copy-start.29 = (pred[192]{0:T(512)(128)(4,1)S(1)}, pred[192]{0:T(512)(128)(4,1)}, u32[]{:S(2)}) copy-start(pred[192]{0:T(512)(128)(4,1)} %constant.80) | copy-start | bytes 580
  7.3 30.4 %copy-start.30 = (pred[192]{0:T(512)(128)(4,1)S(1)}, pred[192]{0:T(512)(128)(4,1)}, u32[]{:S(2)}) copy-start(pred[192]{0:T(512)(128)(4,1)} %constant.79) | copy-start | bytes 580
  7.4 106.4 %all-gather.3.cloned.1.call-start = ((), (), s32[]{:S(2)}) async-start(), calls=%async_computation | async-start | bytes 1216512 | tf_op jit(solution)/shard_map/all_gather | solution.py:246
  7.4 1.0 copy-start.1
  8.4 0.9 copy-start.3
  9.3 0.8 copy-start.6
  10.1 21.0 %copy-start.4 = (bf16[1,8,8,8,128]{4,3,2,1,0:T(8,128)(2,1)S(1)}, bf16[1,8,8,8,128]{4,3,2,1,0:T(8,128)(2,1)}, u32[]{:S(2)}) copy-start(bf16[1,8,8,8,128]{4,3,2,1,0:T(8,128)(2,1)} %fields.3) | copy-start | bytes 393220
  10.1 21.1 %copy-start.2 = (bf16[1,16,8,8,128]{4,3,2,1,0:T(8,128)(2,1)S(1)}, bf16[1,16,8,8,128]{4,3,2,1,0:T(8,128)(2,1)}, u32[]{:S(2)}) copy-start(bf16[1,16,8,8,128]{4,3,2,1,0:T(8,128)(2,1)} %cot.3) | copy-start | bytes 786436
  10.1 37.8 %copy-start.15 = (bf16[27,16,16]{0,2,1:T(8,128)(2,1)S(1)}, bf16[27,16,16]{0,2,1:T(8,128)(2,1)}, u32[]{:S(2)}) copy-start(bf16[27,16,16]{0,2,1:T(8,128)(2,1)} %param.22) | copy-start | bytes 41476
  10.4 19.7 %collective-permute-start = (bf16[8,64,128]{2,1,0:T(8,128)(2,1)S(1)}, bf16[8,64,128]{2,1,0:T(8,128)(2,1)S(1)}, u32[]{:S(2)}, u32[]{:S(2)}) collective-permute-start(bf16[8,64,128]{2,1,0:T(8,128)(2,1)S(1)} %get-tuple-element.11), channel_id=1, source_target_pairs={{0,2},{2,4},{4,6},{1,3},{3,5},{5,7},{8,10},{10,12},{12,14},{9,11},... | collective-permute-start | bytes 393224 | tf_op jit(solution)/shard_map/ppermute | solution.py:198
  12.8 17.5 %collective-permute-start.1 = (bf16[8,64,128]{2,1,0:T(8,128)(2,1)S(1)}, bf16[8,64,128]{2,1,0:T(8,128)(2,1)S(1)}, u32[]{:S(2)}, u32[]{:S(2)}) collective-permute-start(bf16[8,64,128]{2,1,0:T(8,128)(2,1)S(1)} %get-tuple-element.12), channel_id=1, source_target_pairs={{2,0},{4,2},{6,4},{3,1},{5,3},{7,5},{10,8},{12,10},{14,12},{11,9},... | collective-permute-start | bytes 393224 | tf_op jit(solution)/shard_map/ppermute | solution.py:198
  30.2 18.4 %copy-start.5 = (f32[192,1]{1,0:T(8,128)S(1)}, f32[192,1]{1,0:T(8,128)}, u32[]{:S(2)}) copy-start(f32[192,1]{1,0:T(8,128)} %constant.31.clone.rows_y) | copy-start | bytes 2308
  30.2 18.4 %copy-start.7 = (bf16[48,640]{1,0:T(8,128)(2,1)S(1)}, bf16[48,640]{1,0:T(8,128)(2,1)}, u32[]{:S(2)}) copy-start(bf16[48,640]{1,0:T(8,128)(2,1)} %constant.34.clone.e2) | copy-start | bytes 184324
  30.2 18.4 %copy-start.8 = (bf16[192,16]{1,0:T(8,128)(2,1)S(1)}, bf16[192,16]{1,0:T(8,128)(2,1)}, u32[]{:S(2)}) copy-start(bf16[192,16]{1,0:T(8,128)(2,1)} %constant.35.clone.expand) | copy-start | bytes 18436
  30.2 18.4 %copy-start.9 = (bf16[24,384]{1,0:T(8,128)(2,1)S(1)}, bf16[24,384]{1,0:T(8,128)(2,1)}, u32[]{:S(2)}) copy-start(bf16[24,384]{1,0:T(8,128)(2,1)} %constant.33.clone.e1) | copy-start | bytes 55300
  30.2 18.4 %copy-start.10 = (f32[1,640]{1,0:T(1,128)S(1)}, f32[1,640]{1,0:T(1,128)}, u32[]{:S(2)}) copy-start(f32[1,640]{1,0:T(1,128)} %constant.30.clone.y2) | copy-start | bytes 7684
  30.2 18.4 %copy-start.11 = (f32[1,384]{1,0:T(1,128)S(1)}, f32[1,384]{1,0:T(1,128)}, u32[]{:S(2)}) copy-start(f32[1,384]{1,0:T(1,128)} %constant.14.clone.y1) | copy-start | bytes 4612
  31.1 19.2 %copy-start.12 = (bf16[640,128]{1,0:T(8,128)(2,1)S(1)}, bf16[640,128]{1,0:T(8,128)(2,1)}, u32[]{:S(2)}) copy-start(bf16[640,128]{1,0:T(8,128)(2,1)} %constant.40.clone.e2t) | copy-start | bytes 491524
  31.1 19.2 %copy-start.13 = (bf16[384,128]{1,0:T(8,128)(2,1)S(1)}, bf16[384,128]{1,0:T(8,128)(2,1)}, u32[]{:S(2)}) copy-start(bf16[384,128]{1,0:T(8,128)(2,1)} %constant.39.clone.e1t) | copy-start | bytes 294916
  31.1 19.2 %copy-start.14 = (f32[128,1]{1,0:T(8,128)S(1)}, f32[128,1]{1,0:T(8,128)}, u32[]{:S(2)}) copy-start(f32[128,1]{1,0:T(8,128)} %constant.45.yo) | copy-start | bytes 1540
  31.3 19.0 %collective-permute-start.3 = (bf16[896,128]{1,0:T(8,128)(2,1)S(1)}, bf16[896,128]{1,0:T(8,128)(2,1)S(1)}, u32[]{:S(2)}, u32[]{:S(2)}) collective-permute-start(bf16[896,128]{1,0:T(8,128)(2,1)S(1)} %get-tuple-element.26), channel_id=1, source_target_pairs={{8,0},{16,8},{24,16},{9,1},{17,9},{25,17},{10,2},{18,10},{26,18},{... | collective-permute-start | bytes 688136 | tf_op jit(solution)/shard_map/ppermute | solution.py:198
  32.6 17.7 %collective-permute-start.2 = (bf16[896,128]{1,0:T(8,128)(2,1)S(1)}, bf16[896,128]{1,0:T(8,128)(2,1)S(1)}, u32[]{:S(2)}, u32[]{:S(2)}) collective-permute-start(bf16[896,128]{1,0:T(8,128)(2,1)S(1)} %get-tuple-element.27), channel_id=1, source_target_pairs={{0,8},{8,16},{16,24},{1,9},{9,17},{17,25},{2,10},{10,18},{18,26},{... | collective-permute-start | bytes 688136 | tf_op jit(solution)/shard_map/ppermute | solution.py:198
  113.8 1.3 %copy-start = (bf16[4608,128]{1,0:T(8,128)(2,1)S(1)}, bf16[4608,128]{1,0:T(8,128)(2,1)}, u32[]{:S(2)}) copy-start(bf16[4608,128]{1,0:T(8,128)(2,1)} %all-gather.3.cloned.1.call-done) | copy-start | bytes 3538948
Sparse Core Ops, SparseCore 0:
  56.4 57.3 all-gather.2
where the time goes:
time: 125 us
  waiting for transfers between devices  57.5 us (46%)
  other arithmetic  20.9 us (17%)
  between operations  14.7 us (12%)
  local copies, waits for them, and re-layouts  13.6 us (11%)
  starting transfers between devices  9.94 us (8%)
  Pallas kernels  8.02 us (6%)
    all_gather x1, waiting for transfers between devices, local(): parts = lax.all_gather(payload, ('stream', 'radial', 'snap'))  57.5 us
    broadcast_in_dim x1, other arithmetic, local(): b2 = second_bias[rows_o[:128]][:, None]  10.9 us
    gather x1, other arithmetic, local(): b1 = first_bias[rows_o][:, None]  10 us
    ppermute x4, starting transfers between devices, exchange(): return (lax.ppermute(high, axis, up), lax.ppermute(low, axis, down))  9.91 us
    unnamed x85, local copies, waits for them, and re-layouts  8.48 us
    pallas_call x1, Pallas kernels, local(): call(functools.partial(main_kernel, counts), (shape(*cotangent.shape), sh...  5.9 us
  transfers between devices with their start and end apart: 5, of which 1 were waited for; matrix products, arithmetic and copies ran while one was open for 22% of the time, Pallas kernels for 1%

commit v1 on v0

--- a/solution.py
+++ b/solution.py
@@ -39,35 +39,47 @@
     return e1, y1, e2, y2, rows_y, expand
 
 
-def pick_rows():
-    pick = np.zeros((128, 192), np.float32)
-    row = 0
-    for base in (0, 4):
-        for ch in range(CI):
-            for y in range(4):
-                pick[row, ch * 8 + base + y] = 1
-                row += 1
-        for ch in range(CH):
-            for y in range(2):
-                pick[row, 64 + ch * 8 + (0 if base == 0 else 6) + y] = 1
-                row += 1
-    return pick
-
-
 def plane(ref, x):
     v = ref[0, :, x].astype(F32)
     return v.reshape(v.shape[0] * v.shape[1], v.shape[2])
 
 
-def pack_kernel(fields, cot, pick, low, high):
+def pack_kernel(fields, cot, low, high, fields_here, cot_here, sems):
+    copies = [
+        pltpu.make_async_copy(fields, fields_here, sems.at[0]),
+        pltpu.make_async_copy(cot, cot_here, sems.at[1]),
+    ]
+    for copy in copies:
+        copy.start()
+    row = lax.broadcasted_iota(jnp.int32, (128, 192), 0)
+    col = lax.broadcasted_iota(jnp.int32, (128, 192), 1)
+    side, q = row // 64, row % 64
+    from_fields = (q // 4) * 8 + 4 * side + q % 4
+    from_cot = 64 + ((q - 32) // 2) * 8 + 6 * side + q % 2
+    pick = jnp.where(col == jnp.where(q < 32, from_fields, from_cot), 1.0, 0.0).astype(BF16)
+    for copy in copies:
+        copy.wait()
     for x in range(fields.shape[2]):
-        rows = jnp.concatenate([plane(fields, x), plane(cot, x)], axis=0).astype(BF16)
-        got = jnp.dot(pick[...], rows, preferred_element_type=F32).astype(BF16)
+        rows = jnp.concatenate([plane(fields_here, x), plane(cot_here, x)], axis=0).astype(BF16)
+        got = jnp.dot(pick, rows, preferred_element_type=F32).astype(BF16)
         low[x] = got[:64]
         high[x] = got[64:]
 
 
-def band_kernel(w1, w2, wb, e1, e2, expand, y1, y2, rows_y, t1, t2, tb):
+def join_kernel(fields, cot, rlo, rhi, low, high):
+    for out, xs, qs in ((low, (0, 1, 2, 3), (0, 1)), (high, (4, 5, 6, 7), (6, 7))):
+        for n, x in enumerate(xs):
+            out[n * 128:n * 128 + 64] = plane(fields, x).astype(BF16)
+            out[n * 128 + 64:n * 128 + 96] = rlo[x, :32]
+            out[n * 128 + 96:n * 128 + 128] = rhi[x, :32]
+        for n, x in enumerate(qs):
+            base = 512 + n * 192
+            out[base:base + 128] = plane(cot, x).astype(BF16)
+            out[base + 128:base + 160] = rlo[x, 32:]
+            out[base + 160:base + 192] = rhi[x, 32:]
+
+
+def band_kernel(w1, w2, wb, e1, e2, expand, y1, y2, rows_y, first_bias, second_bias, t1, t2, tb, b1, b2):
     ry = rows_y[...]
     for w, e, ys, t, rows in ((w1, e1, y1, t1, 192), (w2, e2, y2, t2, 128), (wb, e2, y2, tb, 128)):
         width = e.shape[1]
@@ -78,6 +90,10 @@
                 part = jnp.dot(expand[:rows], wide[(a * 3 + b) * CH:(a * 3 + b + 1) * CH], preferred_element_type=F32)
                 total = jnp.where(ys[...] == ry[:rows] + float(2 * (b - 1)), part, total)
             t[:, a * width:(a + 1) * width] = total.astype(BF16)
+    for bias, out in ((first_bias, b1), (second_bias, b2)):
+        rows = out.shape[0]
+        column = jnp.sum(expand[:rows].astype(F32) * bias[...], axis=1, keepdims=True)
+        out[...] = jnp.broadcast_to(column, (rows, 256))
 
 
 def shifted(v):
@@ -95,7 +111,7 @@
         ref[base + 384 + c * 64:base + 384 + (c + 1) * 64, at] = piece[128:]
 
 
-def main_kernel(counts, fields, cot, rlo, rhi, xlo, xhi, t1, t2, tb, b1, b2, e1t, e2t, y1, y2, yo,
+def main_kernel(counts, fields, cot, rlo, rhi, xlo, xhi, t1, t2, tb, b1, b2, er1, er2, y1, y2, yo,
                 closure, payload, fs, hs, cs, slope):
     stream, radial = lax.axis_index("stream"), lax.axis_index("radial")
     zeros = jnp.zeros((64, 256), BF16)
@@ -153,33 +169,48 @@
         here = cs[(k + 1) * 640 + 128:(k + 1) * 640 + 256]
         g2 = g2 + lax.dot_general(here, hs[k * 640:(k + 3) * 640], over_lanes, preferred_element_type=F32)
     bias = jnp.sum(bias, axis=1, keepdims=True)
-    spot = lax.broadcasted_iota(jnp.int32, (128, 128), 1) == 120
+    lane = lax.broadcasted_iota(jnp.int32, (8, 256), 1)
+
+    def diagonal(rows, place):
+        total = jnp.zeros((8, rows.shape[1]), F32)
+        for o in range(CH):
+            total = jnp.where(place == o, rows[o * 8:(o + 1) * 8], total)
+        return jnp.sum(total, axis=0, keepdims=True)
+
+    payload[24:] = jnp.zeros((8, 384), F32)
+    payload[27:28, :128] = diagonal(jnp.broadcast_to(bias, (128, 128)), lane[:, :128])
     for a in range(3):
         for b in range(3):
             off = float(2 * (b - 1))
             one = jnp.where(y1[...] == yo[...] + off, g1[:, a * 384:(a + 1) * 384], 0.0).astype(BF16)
             two = jnp.where(y2[...] == yo[...] + off, g2[:, a * 640:(a + 1) * 640], 0.0).astype(BF16)
-            both = jnp.dot(one, e1t[...], preferred_element_type=F32) + jnp.dot(two, e2t[...], preferred_element_type=F32)
-            if a == 0 and b == 0:
-                both = jnp.where(spot, bias, both)
-            payload[(a * 3 + b) * CH:(a * 3 + b + 1) * CH] = jnp.sum(both.reshape(CH, 8, 128), axis=1).astype(BF16)
+            for c in range(3):
+                tap = (a * 3 + b) * 3 + c
+                r1 = jnp.dot(one[:, c * 128:(c + 1) * 128], er1[...], preferred_element_type=F32)
+                rim = 384 + (c // 2) * 128
+                both = jnp.concatenate([two[:, c * 128:(c + 1) * 128], two[:, rim:rim + 128]], axis=1)
+                r2 = jnp.dot(both, er2[c % 2], preferred_element_type=F32)
+                payload[tap:tap + 1, :128] = diagonal(r1, lane[:, :128] // CI)
+                payload[tap:tap + 1, 128:] = diagonal(r2, lane // CH)
     for k in range(4):
         out = (jnp.dot(t2[...], hs[k * 640:(k + 3) * 640], preferred_element_type=F32) + b2[...]).astype(BF16)
         for side in range(2):
             closure[0, :, 2 * k + side] = out[:, side * Z:(side + 1) * Z].reshape(CH, 8, Z)
 
 
-def add_kernel(norm, parts, total):
-    acc = parts[0].astype(F32)
-    for d in range(1, parts.shape[0]):
-        acc = acc + parts[d].astype(F32)
-    total[...] = acc * norm
-
-
-def call(kernel, outs, name, scratch=(), flops=10_000_000):
+def finish_kernel(norm, total, first, second, bias):
+    scaled = total[...] * norm
+    flipped = jnp.transpose(scaled)
+    first[...] = flipped[:128, :27]
+    second[...] = flipped[128:, :27]
+    bias[...] = scaled[27:28, :CH]
+
+
+def call(kernel, outs, name, scratch=(), flops=10_000_000, **specs):
     return pl.pallas_call(
         kernel,
         out_shape=outs,
+        **specs,
         scratch_shapes=list(scratch),
         compiler_params=pltpu.CompilerParams(vmem_limit_bytes=48 * 1024 * 1024),
         cost_estimate=pl.CostEstimate(flops=flops, bytes_accessed=1_000_000, transcendentals=0),
@@ -198,42 +229,51 @@
     return lax.ppermute(high, axis, up), lax.ppermute(low, axis, down)
 
 
+def reduce_all(v, axes):
+    for axis in axes:
+        count = lax.axis_size(axis)
+        step = 1
+        while step < count:
+            v = v + lax.ppermute(v, axis, [(i, i ^ step) for i in range(count)])
+            step *= 2
+    return v
+
+
 def local(fields, first_weight, first_bias, second_weight, second_bias, cotangent):
     e1, y1, e2, y2, rows_y, expand = lane_rows()
     y1 = jnp.asarray(y1[None], F32)
     y2 = jnp.asarray(y2[None], F32)
     ry = jnp.asarray(rows_y[:, None], F32)
-    lanes_x = fields.shape[2]
-    low, high = call(pack_kernel, (shape(lanes_x, 64, Z),) * 2, "pack_strips")(fields, cotangent, jnp.asarray(pick_rows(), BF16))
+    low, high = call(
+        pack_kernel,
+        (shape(fields.shape[2], 64, Z),) * 2,
+        "pack_strips",
+        (pltpu.VMEM(fields.shape, BF16), pltpu.VMEM(cotangent.shape, BF16), pltpu.SemaphoreType.DMA((2,))),
+        in_specs=[pl.BlockSpec(memory_space=pl.ANY)] * 2,
+    )(fields, cotangent)
     rlo, rhi = exchange(low, high, "radial")
 
     w1 = first_weight.reshape(3, 3, 3, CH, CI).transpose(0, 1, 3, 2, 4).reshape(9 * CH, 3 * CI)
     w2 = second_weight.reshape(3, 3, 3, CH, CH)
     wb = w2[::-1, ::-1, ::-1].transpose(0, 1, 4, 2, 3).reshape(9 * CH, 3 * CH)
     w2 = w2.transpose(0, 1, 3, 2, 4).reshape(9 * CH, 3 * CH)
-    t1, t2, tb = call(band_kernel, (shape(192, 1152), shape(128, 1920), shape(128, 1920)), "band_weights")(
-        w1, w2, wb, jnp.asarray(e1, BF16), jnp.asarray(e2, BF16), jnp.asarray(expand, BF16), y1, y2, ry)
-
-    def strip(xs, qs):
-        pieces = []
-        for x in xs:
-            pieces += [fields[0, :, x].reshape(64, Z), rlo[x, :32], rhi[x, :32]]
-        for x in qs:
-            pieces += [cotangent[0, :, x].reshape(128, Z), rlo[x, 32:], rhi[x, 32:]]
-        return jnp.concatenate(pieces, axis=0)
-
-    xlo, xhi = exchange(strip((0, 1, 2, 3), (0, 1)), strip((4, 5, 6, 7), (6, 7)), "stream")
-    e1t = np.zeros((384, 128), np.float32)
-    e1t[:, :24] = e1.T
-    e2t = np.zeros((640, 128), np.float32)
-    e2t[:, 64:112] = e2.T
-    rows_o = np.argmax(expand, axis=1)
-    b1 = first_bias[rows_o][:, None]
-    b2 = second_bias[rows_o[:128]][:, None]
+    t1, t2, tb, b1, b2 = call(
+        band_kernel,
+        (shape(192, 1152), shape(128, 1920), shape(128, 1920), shape(192, 256, dtype=F32), shape(128, 256, dtype=F32)),
+        "band_weights",
+    )(w1, w2, wb, jnp.asarray(e1, BF16), jnp.asarray(e2, BF16), jnp.asarray(expand, BF16), y1, y2, ry, first_bias[None], second_bias[None])
+
+    low, high = call(join_kernel, (shape(896, Z),) * 2, "join_strips")(fields, cotangent, rlo, rhi)
+    xlo, xhi = exchange(low, high, "stream")
+    er1 = np.tile(e1[:CI, :128].T, (1, CH))
+    er2 = np.zeros((2, 256, 256), np.float32)
+    for half in range(2):
+        er2[half, :128] = np.tile(e2[:CH, :128].T, (1, CH))
+        er2[half, 128 + half * 64:192 + half * 64] = np.tile(e2[:CH, 384:448].T, (1, CH))
     counts = (lax.axis_size("stream"), lax.axis_size("radial"))
     closure, payload = call(
         functools.partial(main_kernel, counts),
-        (shape(*cotangent.shape), shape(9 * CH, 128)),
+        (shape(*cotangent.shape), shape(32, 384, dtype=F32)),
         "layers",
         (
             pltpu.VMEM((8 * 384, 256), BF16),
@@ -242,15 +282,18 @@
             pltpu.VMEM((4, 128, 256), F32),
         ),
         flops=3_000_000_000,
-    )(fields, cotangent, rlo, rhi, xlo, xhi, t1, t2, tb, b1, b2, jnp.asarray(e1t, BF16), jnp.asarray(e2t, BF16), y1, y2, ry[:128])
-    parts = lax.all_gather(payload, ("stream", "radial", "snap"))
+    )(fields, cotangent, rlo, rhi, xlo, xhi, t1, t2, tb, b1, b2, jnp.asarray(er1, BF16), jnp.asarray(er2, BF16), y1, y2, ry[:128])
+    total = reduce_all(payload, ("radial", "snap", "stream"))
     count = fields.shape[0] * lax.axis_size("snap") * fields.shape[2] * counts[0] * fields.shape[3] * counts[1] * fields.shape[4]
     norm = float(1.0 / np.sqrt(np.float32(count)))
-    total = call(functools.partial(add_kernel, norm), shape(9 * CH, 128, dtype=F32), "add_parts")(parts)
-    total = total.reshape(3, 3, CH, 128)
-    first = total[..., :24].reshape(3, 3, CH, 3, CI).transpose(0, 1, 3, 2, 4).reshape(27, CH, CI)
-    second = total[..., 64:112].reshape(3, 3, CH, 3, CH).transpose(0, 1, 3, 2, 4).reshape(27, CH, CH)
-    return (closure, first, second, total[0, 0, :, 120])
+    first, second, bias = call(
+        functools.partial(finish_kernel, norm),
+        (shape(CH * CI, 27, dtype=F32), shape(CH * CH, 27, dtype=F32), shape(1, CH, dtype=F32)),
+        "finish",
+    )(total)
+    first = first.reshape(CH, CI, 27).transpose(2, 0, 1)
+    second = second.reshape(CH, CH, 27).transpose(2, 0, 1)
+    return (closure, first, second, bias[0])
 
 
 def solution(mesh):

time: 125 us -> 50.6 us (0.40)
  waiting for transfers between devices: 57.5 us -> 17.3 us
  other arithmetic: 20.9 us -> 0.04 us
  between operations: 14.7 us -> 0.94 us
  local copies, waits for them, and re-layouts: 13.6 us -> 4.2 us
  starting transfers between devices: 9.94 us -> 18.3 us
  Pallas kernels: 8.02 us -> 9.37 us
    all_gather x1 -> x0, waiting for transfers between devices: 57.5 us -> none  [local(): parts = lax.all_gather(payload, ('stream', 'radial', 'snap'))]
    broadcast_in_dim x1 -> x0, other arithmetic: 10.9 us -> none  [local(): b2 = second_bias[rows_o[:128]][:, None]]
    ppermute x0 -> x5, waiting for transfers between devices: none -> 10.8 us  [reduce_all(): v = v + lax.ppermute(v, axis, [(i, i ^ step) for i in range(count)])]
    gather x1 -> x0, other arithmetic: 10 us -> none  [local(): b1 = first_bias[rows_o][:, None]]
    ppermute x0 -> x5, starting transfers between devices: none -> 9.91 us  [reduce_all(): v = v + lax.ppermute(v, axis, [(i, i ^ step) for i in range(count)])]
    ppermute x4, waiting for transfers between devices: 0.01 us -> 6.57 us  [exchange(): return (lax.ppermute(high, axis, up), lax.ppermute(low, axis, down))]
    unnamed x85 -> x36, local copies, waits for them, and re-layouts: 8.48 us -> 3.48 us
    gather x2 -> x0, local copies, waits for them, and re-layouts: 3.89 us -> none  [the longest x1 1.95 us: local(): b2 = second_bias[rows_o[:128]][:, None]]
  transfers between devices with their start and end apart: 5 -> 9, of which waited for: 1 -> 7; matrix products, arithmetic and copies ran while one was open for 22% -> 2% of each run, Pallas kernels for 1% -> 3%
where the time goes in v1:
time: 50.6 us; the launch traced here: 50.2 us
  starting transfers between devices  18.3 us (36%)
  waiting for transfers between devices  17.3 us (34%)
  Pallas kernels  9.37 us (19%)
  local copies, waits for them, and re-layouts  4.2 us (8%)
  between operations  0.94 us (2%)
    ppermute x5, waiting for transfers between devices, reduce_all(): v = v + lax.ppermute(v, axis, [(i, i ^ step) for i in range(count)])  10.8 us
    ppermute x5, starting transfers between devices, reduce_all(): v = v + lax.ppermute(v, axis, [(i, i ^ step) for i in range(count)])  9.91 us
    ppermute x4, starting transfers between devices, exchange(): return (lax.ppermute(high, axis, up), lax.ppermute(low, axis, down))  8.44 us
    ppermute x4, waiting for transfers between devices, exchange(): return (lax.ppermute(high, axis, up), lax.ppermute(low, axis, down))  6.57 us
    pallas_call x1, Pallas kernels, local(): call(functools.partial(main_kernel, counts), (shape(*cotangent.shape), sh...  6.34 us
    unnamed x36, local copies, waits for them, and re-layouts  3.48 us
    pallas_call x1, Pallas kernels, local(): call(band_kernel, (shape(192, 1152), shape(128, 1920), shape(128, 1920),...  1.67 us
  transfers between devices with their start and end apart: 9, of which 7 were waited for; matrix products, arithmetic and copies ran while one was open for 2% of the time, Pallas kernels for 3%

profile of v1, /device:TPU:0, one launch (start us, length us, event | category | flops | bytes accessed | tf_op | source)
XLA Modules:
  0.0 50.2 jit_solution(17667965038619569464)
XLA Ops:
  0.6 0.0 copy-start
  0.6 0.9 %copy-done = bf16[1,16,8,8,128]{4,3,2,1,0:T(8,128)(2,1)S(1)} copy-done((bf16[1,16,8,8,128]{4,3,2,1,0:T(8,128)(2,1)S(1)}, bf16[1,16,8,8,128]{4,3,2,1,0:T(8,128)(2,1)}, u32[]{:S(2)}) %copy-start) | copy-done | bytes 262168
  1.6 0.9 %copy-done.2 = bf16[1,8,8,8,128]{4,3,2,1,0:T(8,128)(2,1)S(1)} copy-done((bf16[1,8,8,8,128]{4,3,2,1,0:T(8,128)(2,1)S(1)}, bf16[1,8,8,8,128]{4,3,2,1,0:T(8,128)(2,1)}, u32[]{:S(2)}) %copy-start.2) | copy-done | bytes 131096
  2.5 0.5 %pack_strips.1 = (bf16[8,64,128]{2,1,0:T(8,128)(2,1)S(1)}, bf16[8,64,128]{2,1,0:T(8,128)(2,1)S(1)}) custom-call(bf16[1,8,8,8,128]{4,3,2,1,0:T(8,128)(2,1)S(1)} %copy-done.2, bf16[1,16,8,8,128]{4,3,2,1,0:T(8,128)(2,1)S(1)} %copy-done), custom_call_target="tpu_custom_call" | custom-call | flops 10000000 | bytes 1000000 | tf_op jit(solution)/shard_map/pack_strips/pallas_call | solution.py:247
  3.0 2.4 %collective-permute-start = (bf16[8,64,128]{2,1,0:T(8,128)(2,1)S(1)}, bf16[8,64,128]{2,1,0:T(8,128)(2,1)S(1)}, u32[]{:S(2)}, u32[]{:S(2)}) collective-permute-start(bf16[8,64,128]{2,1,0:T(8,128)(2,1)S(1)} %get-tuple-element.18), channel_id=1, source_target_pairs={{0,2},{2,4},{4,6},{1,3},{3,5},{5,7},{8,10},{10,12},{12,14},{9,11},... | collective-permute-start | bytes 393224 | tf_op jit(solution)/shard_map/ppermute | solution.py:229
  5.4 0.0 copy-start.16
  5.4 1.3 %collective-permute-start.1 = (bf16[8,64,128]{2,1,0:T(8,128)(2,1)S(1)}, bf16[8,64,128]{2,1,0:T(8,128)(2,1)S(1)}, u32[]{:S(2)}, u32[]{:S(2)}) collective-permute-start(bf16[8,64,128]{2,1,0:T(8,128)(2,1)S(1)} %get-tuple-element.19), channel_id=1, source_target_pairs={{2,0},{4,2},{6,4},{3,1},{5,3},{7,5},{10,8},{12,10},{14,12},{11,9},... | collective-permute-start | bytes 393224 | tf_op jit(solution)/shard_map/ppermute | solution.py:229
  6.7 0.0 collective-permute-done.rlo
  6.7 4.1 %collective-permute-done.1.rhi = bf16[8,64,128]{2,1,0:T(8,128)(2,1)S(1)} collective-permute-done((bf16[8,64,128]{2,1,0:T(8,128)(2,1)S(1)}, bf16[8,64,128]{2,1,0:T(8,128)(2,1)S(1)}, u32[]{:S(2)}, u32[]{:S(2)}) %collective-permute-start.1) | collective-permute-done | bytes 131104 | tf_op jit(solution)/shard_map/ppermute | solution.py:229
  10.8 0.1 join_strips.1
  10.8 3.5 %collective-permute-start.2 = (bf16[896,128]{1,0:T(8,128)(2,1)S(1)}, bf16[896,128]{1,0:T(8,128)(2,1)S(1)}, u32[]{:S(2)}, u32[]{:S(2)}) collective-permute-start(bf16[896,128]{1,0:T(8,128)(2,1)S(1)} %get-tuple-element.20), channel_id=1, source_target_pairs={{0,8},{8,16},{16,24},{1,9},{9,17},{17,25},{2,10},{10,18},{18,26},{... | collective-permute-start | bytes 688136 | tf_op jit(solution)/shard_map/ppermute | solution.py:229
  14.3 1.3 %collective-permute-start.3 = (bf16[896,128]{1,0:T(8,128)(2,1)S(1)}, bf16[896,128]{1,0:T(8,128)(2,1)S(1)}, u32[]{:S(2)}, u32[]{:S(2)}) collective-permute-start(bf16[896,128]{1,0:T(8,128)(2,1)S(1)} %get-tuple-element.21), channel_id=1, source_target_pairs={{8,0},{16,8},{24,16},{9,1},{17,9},{25,17},{10,2},{18,10},{26,18},{... | collective-permute-start | bytes 688136 | tf_op jit(solution)/shard_map/ppermute | solution.py:229
  15.6 0.0 copy-done.16
  15.6 0.1 copy.21
  15.8 0.0 copy-start.15
  15.8 0.1 reshape.30
  15.9 0.1 copy.26.w1
  16.1 0.6 %copy-done.15 = bf16[27,16,16]{0,2,1:T(8,128)(2,1)S(1)} copy-done((bf16[27,16,16]{0,2,1:T(8,128)(2,1)S(1)}, bf16[27,16,16]{0,2,1:T(8,128)(2,1)}, u32[]{:S(2)}) %copy-start.15) | copy-done | bytes 13848
  16.7 0.2 copy.23
  16.9 0.0 copy-start.14
  16.9 0.1 copy.30
  17.0 0.0 copy-start.12
  17.1 0.1 reshape.37.wb
  17.2 0.0 copy-start.4
  17.2 0.0 copy-start.5
  17.2 0.0 copy-start.6
  17.2 0.0 copy-start.7
  17.2 0.0 copy-start.8
  17.2 0.0 copy-start.9
  17.3 0.0 copy-start.10
  17.3 0.0 copy-start.11
  17.3 0.1 copy.29
  17.3 0.0 copy-start.1
  17.4 0.1 reshape.36.w2
  17.5 0.6 %copy-done.4 = f32[192,1]{1,0:T(8,128)S(1)} copy-done((f32[192,1]{1,0:T(8,128)S(1)}, f32[192,1]{1,0:T(8,128)}, u32[]{:S(2)}) %copy-start.4) | copy-done | bytes 792
  18.1 0.0 copy-done.5
  18.1 0.0 copy-done.6
  18.1 0.0 copy-done.7
  18.1 0.0 copy-done.8
  18.1 0.0 copy-done.9
  18.1 0.0 copy-done.10
  18.1 0.0 copy-done.11
  18.1 0.0 copy-start.3
  18.1 0.0 copy-start.13
  18.1 1.7 %band_weights.1 = (bf16[192,1152]{1,0:T(8,128)(2,1)S(1)}, bf16[128,1920]{1,0:T(8,128)(2,1)S(1)}, bf16[128,1920]{1,0:T(8,128)(2,1)S(1)}, f32[192,256]{1,0:T(8,128)S(1)}, f32[128,256]{1,0:T(8,128)S(1)}) custom-call(bf16[144,24]{1,0:T(8,128)(2,1)S(1)} %copy.26.w1, bf16[144,48]{1,0:T(8,128)(2,1)S(1)} %reshape.36.w2, bf16[144,48]{1,0:T(8,128)(2,1)S(1)} %reshape.37.wb, ...), custom_call_target="tpu_custom_call" | custom-call | flops 10000000 | bytes 1000000 | tf_op jit(solution)/shard_map/band_weights/pallas_call | solution.py:260
  19.8 0.0 collective-permute-done.2.xlo
  19.8 2.5 %collective-permute-done.3.xhi = bf16[896,128]{1,0:T(8,128)(2,1)S(1)} collective-permute-done((bf16[896,128]{1,0:T(8,128)(2,1)S(1)}, bf16[896,128]{1,0:T(8,128)(2,1)S(1)}, u32[]{:S(2)}, u32[]{:S(2)}) %collective-permute-start.3) | collective-permute-done | bytes 229408 | tf_op jit(solution)/shard_map/ppermute | solution.py:229
  22.3 0.0 copy-done.14
  22.3 0.0 copy-done.12
  22.3 0.0 copy-done.1
  22.3 0.0 copy-done.3
  22.4 0.0 copy-done.13
  22.4 6.3 %layers.1 = (bf16[1,16,8,8,128]{4,3,2,1,0:T(8,128)(2,1)}, f32[32,384]{1,0:T(8,128)S(1)}) custom-call(bf16[1,8,8,8,128]{4,3,2,1,0:T(8,128)(2,1)S(1)} %copy-done.3, bf16[1,16,8,8,128]{4,3,2,1,0:T(8,128)(2,1)S(1)} %copy-done.1, bf16[8,64,128]{2,1,0:T(8,128)(2,1)S(1)} %collective-permute-done.rlo, bf16[8,64,128]{2,1,0:T(8,128)(2,1)S(1)} %collective-permute-done.1.rhi, ...), custom_call_target="tpu_custom_call" | custom-call | flops 3000000000 | bytes 1000000 | tf_op jit(solution)/shard_map/layers/pallas_call | solution.py:274
  28.7 2.2 %collective-permute-start.4 = (f32[32,384]{1,0:T(8,128)S(1)}, f32[32,384]{1,0:T(8,128)S(1)}, u32[]{:S(2)}, u32[]{:S(2)}) collective-permute-start(f32[32,384]{1,0:T(8,128)S(1)} %get-tuple-element.28), channel_id=1, source_target_pairs={{0,2},{2,0},{4,6},{6,4},{1,3},{3,1},{5,7},{7,5},{8,10},{10,8},{12,... | collective-permute-start | bytes 147464 | tf_op jit(solution)/shard_map/ppermute | solution.py:237
  30.9 0.9 %collective-permute-done.4 = f32[32,384]{1,0:T(8,128)S(1)} collective-permute-done((f32[32,384]{1,0:T(8,128)S(1)}, f32[32,384]{1,0:T(8,128)S(1)}, u32[]{:S(2)}, u32[]{:S(2)}) %collective-permute-start.4) | collective-permute-done | bytes 49184 | tf_op jit(solution)/shard_map/ppermute | solution.py:237
  31.8 1.4 %collective-permute-start.5 = (f32[32,384]{1,0:T(8,128)S(1)}, f32[32,384]{1,0:T(8,128)S(1)}, u32[]{:S(2)}, u32[]{:S(2)}) collective-permute-start(f32[32,384]{1,0:T(8,128)S(1)} %add.15), channel_id=1, source_target_pairs={{0,4},{2,6},{4,0},{6,2},{1,5},{3,7},{5,1},{7,3},{8,12},{10,14},{12... | collective-permute-start | bytes 147464 | tf_op jit(solution)/shard_map/ppermute | solution.py:237
  33.2 2.7 %collective-permute-done.5 = f32[32,384]{1,0:T(8,128)S(1)} collective-permute-done((f32[32,384]{1,0:T(8,128)S(1)}, f32[32,384]{1,0:T(8,128)S(1)}, u32[]{:S(2)}, u32[]{:S(2)}) %collective-permute-start.5) | collective-permute-done | bytes 49184 | tf_op jit(solution)/shard_map/ppermute | solution.py:237
  35.9 1.5 %collective-permute-start.6 = (f32[32,384]{1,0:T(8,128)S(1)}, f32[32,384]{1,0:T(8,128)S(1)}, u32[]{:S(2)}, u32[]{:S(2)}) collective-permute-start(f32[32,384]{1,0:T(8,128)S(1)} %add.16), channel_id=1, source_target_pairs={{0,1},{1,0},{2,3},{3,2},{4,5},{5,4},{6,7},{7,6},{8,9},{9,8},{10,11... | collective-permute-start | bytes 147464 | tf_op jit(solution)/shard_map/ppermute | solution.py:237
  37.5 2.6 %collective-permute-done.6 = f32[32,384]{1,0:T(8,128)S(1)} collective-permute-done((f32[32,384]{1,0:T(8,128)S(1)}, f32[32,384]{1,0:T(8,128)S(1)}, u32[]{:S(2)}, u32[]{:S(2)}) %collective-permute-start.6) | collective-permute-done | bytes 49184 | tf_op jit(solution)/shard_map/ppermute | solution.py:237
  40.1 1.6 %collective-permute-start.7 = (f32[32,384]{1,0:T(8,128)S(1)}, f32[32,384]{1,0:T(8,128)S(1)}, u32[]{:S(2)}, u32[]{:S(2)}) collective-permute-start(f32[32,384]{1,0:T(8,128)S(1)} %add.17), channel_id=1, source_target_pairs={{0,8},{8,0},{16,24},{24,16},{1,9},{9,1},{17,25},{25,17},{2,10},{10... | collective-permute-start | bytes 147464 | tf_op jit(solution)/shard_map/ppermute | solution.py:237
  41.7 2.5 %collective-permute-done.7 = f32[32,384]{1,0:T(8,128)S(1)} collective-permute-done((f32[32,384]{1,0:T(8,128)S(1)}, f32[32,384]{1,0:T(8,128)S(1)}, u32[]{:S(2)}, u32[]{:S(2)}) %collective-permute-start.7) | collective-permute-done | bytes 49184 | tf_op jit(solution)/shard_map/ppermute | solution.py:237
  44.2 3.1 %collective-permute-start.8 = (f32[32,384]{1,0:T(8,128)S(1)}, f32[32,384]{1,0:T(8,128)S(1)}, u32[]{:S(2)}, u32[]{:S(2)}) collective-permute-start(f32[32,384]{1,0:T(8,128)S(1)} %add.18), channel_id=1, source_target_pairs={{0,16},{8,24},{16,0},{24,8},{1,17},{9,25},{17,1},{25,9},{2,18},{10... | collective-permute-start | bytes 147464 | tf_op jit(solution)/shard_map/ppermute | solution.py:237
  47.4 2.1 %collective-permute-done.8 = f32[32,384]{1,0:T(8,128)S(1)} collective-permute-done((f32[32,384]{1,0:T(8,128)S(1)}, f32[32,384]{1,0:T(8,128)S(1)}, u32[]{:S(2)}, u32[]{:S(2)}) %collective-permute-start.8) | collective-permute-done | bytes 49184 | tf_op jit(solution)/shard_map/ppermute | solution.py:237
  49.4 0.8 %finish.1 = (f32[128,27]{1,0:T(8,128)}, f32[256,27]{1,0:T(8,128)}, f32[1,16]{1,0:T(1,128)}) custom-call(f32[32,384]{1,0:T(8,128)S(1)} %add.19.total), custom_call_target="tpu_custom_call" | custom-call | flops 10000000 | bytes 1000000 | tf_op jit(solution)/shard_map/finish/pallas_call | solution.py:289
  (8 shorter events, 0.1 us)
Async XLA Ops:
  0.6 1.0 %copy-start = (bf16[1,16,8,8,128]{4,3,2,1,0:T(8,128)(2,1)S(1)}, bf16[1,16,8,8,128]{4,3,2,1,0:T(8,128)(2,1)}, u32[]{:S(2)}) copy-start(bf16[1,16,8,8,128]{4,3,2,1,0:T(8,128)(2,1)} %cot.5) | copy-start | bytes 786436
  1.6 0.9 %copy-start.2 = (bf16[1,8,8,8,128]{4,3,2,1,0:T(8,128)(2,1)S(1)}, bf16[1,8,8,8,128]{4,3,2,1,0:T(8,128)(2,1)}, u32[]{:S(2)}) copy-start(bf16[1,8,8,8,128]{4,3,2,1,0:T(8,128)(2,1)} %fields.5) | copy-start | bytes 393220
  3.0 3.7 %collective-permute-start = (bf16[8,64,128]{2,1,0:T(8,128)(2,1)S(1)}, bf16[8,64,128]{2,1,0:T(8,128)(2,1)S(1)}, u32[]{:S(2)}, u32[]{:S(2)}) collective-permute-start(bf16[8,64,128]{2,1,0:T(8,128)(2,1)S(1)} %get-tuple-element.18), channel_id=1, source_target_pairs={{0,2},{2,4},{4,6},{1,3},{3,5},{5,7},{8,10},{10,12},{12,14},{9,11},... | collective-permute-start | bytes 393224 | tf_op jit(solution)/shard_map/ppermute | solution.py:229
  5.4 10.3 %copy-start.16 = (bf16[27,16,8]{0,2,1:T(8,128)(2,1)S(1)}, bf16[27,16,8]{0,2,1:T(8,128)(2,1)}, u32[]{:S(2)}) copy-start(bf16[27,16,8]{0,2,1:T(8,128)(2,1)} %param.15) | copy-start | bytes 20740
  5.4 5.4 %collective-permute-start.1 = (bf16[8,64,128]{2,1,0:T(8,128)(2,1)S(1)}, bf16[8,64,128]{2,1,0:T(8,128)(2,1)S(1)}, u32[]{:S(2)}, u32[]{:S(2)}) collective-permute-start(bf16[8,64,128]{2,1,0:T(8,128)(2,1)S(1)} %get-tuple-element.19), channel_id=1, source_target_pairs={{2,0},{4,2},{6,4},{3,1},{5,3},{7,5},{10,8},{12,10},{14,12},{11,9},... | collective-permute-start | bytes 393224 | tf_op jit(solution)/shard_map/ppermute | solution.py:229
  10.8 9.0 %collective-permute-start.2 = (bf16[896,128]{1,0:T(8,128)(2,1)S(1)}, bf16[896,128]{1,0:T(8,128)(2,1)S(1)}, u32[]{:S(2)}, u32[]{:S(2)}) collective-permute-start(bf16[896,128]{1,0:T(8,128)(2,1)S(1)} %get-tuple-element.20), channel_id=1, source_target_pairs={{0,8},{8,16},{16,24},{1,9},{9,17},{17,25},{2,10},{10,18},{18,26},{... | collective-permute-start | bytes 688136 | tf_op jit(solution)/shard_map/ppermute | solution.py:229
  14.3 8.0 %collective-permute-start.3 = (bf16[896,128]{1,0:T(8,128)(2,1)S(1)}, bf16[896,128]{1,0:T(8,128)(2,1)S(1)}, u32[]{:S(2)}, u32[]{:S(2)}) collective-permute-start(bf16[896,128]{1,0:T(8,128)(2,1)S(1)} %get-tuple-element.21), channel_id=1, source_target_pairs={{8,0},{16,8},{24,16},{9,1},{17,9},{25,17},{10,2},{18,10},{26,18},{... | collective-permute-start | bytes 688136 | tf_op jit(solution)/shard_map/ppermute | solution.py:229
  15.8 0.8 %copy-start.15 = (bf16[27,16,16]{0,2,1:T(8,128)(2,1)S(1)}, bf16[27,16,16]{0,2,1:T(8,128)(2,1)}, u32[]{:S(2)}) copy-start(bf16[27,16,16]{0,2,1:T(8,128)(2,1)} %param.17) | copy-start | bytes 41476
  16.9 5.5 %copy-start.14 = (bf16[128,128]{1,0:T(8,128)(2,1)S(1)}, bf16[128,128]{1,0:T(8,128)(2,1)}, u32[]{:S(2)}) copy-start(bf16[128,128]{1,0:T(8,128)(2,1)} %constant.22.clone.er1) | copy-start | bytes 98308
  17.0 5.3 %copy-start.12 = (bf16[2,256,256]{2,1,0:T(8,128)(2,1)S(1)}, bf16[2,256,256]{2,1,0:T(8,128)(2,1)}, u32[]{:S(2)}) copy-start(bf16[2,256,256]{2,1,0:T(8,128)(2,1)} %constant.23.clone.er2) | copy-start | bytes 786436
  17.2 0.9 %copy-start.4 = (f32[192,1]{1,0:T(8,128)S(1)}, f32[192,1]{1,0:T(8,128)}, u32[]{:S(2)}) copy-start(f32[192,1]{1,0:T(8,128)} %constant.18.clone.rows_y) | copy-start | bytes 2308
  17.2 0.9 %copy-start.5 = (bf16[48,640]{1,0:T(8,128)(2,1)S(1)}, bf16[48,640]{1,0:T(8,128)(2,1)}, u32[]{:S(2)}) copy-start(bf16[48,640]{1,0:T(8,128)(2,1)} %constant.20.clone.e2) | copy-start | bytes 184324
  17.2 0.9 %copy-start.6 = (bf16[192,16]{1,0:T(8,128)(2,1)S(1)}, bf16[192,16]{1,0:T(8,128)(2,1)}, u32[]{:S(2)}) copy-start(bf16[192,16]{1,0:T(8,128)(2,1)} %constant.21.clone.expand) | copy-start | bytes 18436
  17.2 0.9 %copy-start.7 = (bf16[24,384]{1,0:T(8,128)(2,1)S(1)}, bf16[24,384]{1,0:T(8,128)(2,1)}, u32[]{:S(2)}) copy-start(bf16[24,384]{1,0:T(8,128)(2,1)} %constant.19.clone.e1) | copy-start | bytes 55300
  17.2 0.9 %copy-start.8 = (f32[1,640]{1,0:T(1,128)S(1)}, f32[1,640]{1,0:T(1,128)}, u32[]{:S(2)}) copy-start(f32[1,640]{1,0:T(1,128)} %constant.17.clone.y2) | copy-start | bytes 7684
  17.2 0.8 %copy-start.9 = (f32[1,384]{1,0:T(1,128)S(1)}, f32[1,384]{1,0:T(1,128)}, u32[]{:S(2)}) copy-start(f32[1,384]{1,0:T(1,128)} %constant.16.clone.y1) | copy-start | bytes 4612
  17.3 0.8 %copy-start.10 = (f32[16]{0:T(128)S(1)}, f32[16]{0:T(128)}, u32[]{:S(2)}) copy-start(f32[16]{0:T(128)} %param.16) | copy-start | bytes 196
  17.3 0.8 %copy-start.11 = (f32[16]{0:T(128)S(1)}, f32[16]{0:T(128)}, u32[]{:S(2)}) copy-start(f32[16]{0:T(128)} %param.18) | copy-start | bytes 196
  17.3 5.0 %copy-start.1 = (bf16[1,16,8,8,128]{4,3,2,1,0:T(8,128)(2,1)S(1)}, bf16[1,16,8,8,128]{4,3,2,1,0:T(8,128)(2,1)}, u32[]{:S(2)}) copy-start(bf16[1,16,8,8,128]{4,3,2,1,0:T(8,128)(2,1)} %cot.5) | copy-start | bytes 786436
  18.1 4.2 %copy-start.3 = (bf16[1,8,8,8,128]{4,3,2,1,0:T(8,128)(2,1)S(1)}, bf16[1,8,8,8,128]{4,3,2,1,0:T(8,128)(2,1)}, u32[]{:S(2)}) copy-start(bf16[1,8,8,8,128]{4,3,2,1,0:T(8,128)(2,1)} %fields.5) | copy-start | bytes 393220
  18.1 4.2 %copy-start.13 = (f32[128,1]{1,0:T(8,128)S(1)}, f32[128,1]{1,0:T(8,128)}, u32[]{:S(2)}) copy-start(f32[128,1]{1,0:T(8,128)} %constant.26.yo) | copy-start | bytes 1540
  28.7 3.1 %collective-permute-start.4 = (f32[32,384]{1,0:T(8,128)S(1)}, f32[32,384]{1,0:T(8,128)S(1)}, u32[]{:S(2)}, u32[]{:S(2)}) collective-permute-start(f32[32,384]{1,0:T(8,128)S(1)} %get-tuple-element.28), channel_id=1, source_target_pairs={{0,2},{2,0},{4,6},{6,4},{1,3},{3,1},{5,7},{7,5},{8,10},{10,8},{12,... | collective-permute-start | bytes 147464 | tf_op jit(solution)/shard_map/ppermute | solution.py:237
  31.8 4.1 %collective-permute-start.5 = (f32[32,384]{1,0:T(8,128)S(1)}, f32[32,384]{1,0:T(8,128)S(1)}, u32[]{:S(2)}, u32[]{:S(2)}) collective-permute-start(f32[32,384]{1,0:T(8,128)S(1)} %add.15), channel_id=1, source_target_pairs={{0,4},{2,6},{4,0},{6,2},{1,5},{3,7},{5,1},{7,3},{8,12},{10,14},{12... | collective-permute-start | bytes 147464 | tf_op jit(solution)/shard_map/ppermute | solution.py:237
  35.9 4.2 %collective-permute-start.6 = (f32[32,384]{1,0:T(8,128)S(1)}, f32[32,384]{1,0:T(8,128)S(1)}, u32[]{:S(2)}, u32[]{:S(2)}) collective-permute-start(f32[32,384]{1,0:T(8,128)S(1)} %add.16), channel_id=1, source_target_pairs={{0,1},{1,0},{2,3},{3,2},{4,5},{5,4},{6,7},{7,6},{8,9},{9,8},{10,11... | collective-permute-start | bytes 147464 | tf_op jit(solution)/shard_map/ppermute | solution.py:237
  40.1 4.2 %collective-permute-start.7 = (f32[32,384]{1,0:T(8,128)S(1)}, f32[32,384]{1,0:T(8,128)S(1)}, u32[]{:S(2)}, u32[]{:S(2)}) collective-permute-start(f32[32,384]{1,0:T(8,128)S(1)} %add.17), channel_id=1, source_target_pairs={{0,8},{8,0},{16,24},{24,16},{1,9},{9,1},{17,25},{25,17},{2,10},{10... | collective-permute-start | bytes 147464 | tf_op jit(solution)/shard_map/ppermute | solution.py:237
  44.2 5.2 %collective-permute-start.8 = (f32[32,384]{1,0:T(8,128)S(1)}, f32[32,384]{1,0:T(8,128)S(1)}, u32[]{:S(2)}, u32[]{:S(2)}) collective-permute-start(f32[32,384]{1,0:T(8,128)S(1)} %add.18), channel_id=1, source_target_pairs={{0,16},{8,24},{16,0},{24,8},{1,17},{9,25},{17,1},{25,9},{2,18},{10... | collective-permute-start | bytes 147464 | tf_op jit(solution)/shard_map/ppermute | solution.py:237

commit v2 on v1

v2 whole, which is shorter than its diff:
```python
import functools

import numpy as np
import jax
import jax.numpy as jnp
from jax import lax
from jax.experimental import pallas as pl
from jax.experimental.pallas import tpu as pltpu
from jax.sharding import PartitionSpec as P

F32 = jnp.float32
BF16 = jnp.bfloat16
Z = 128
CI = 8
CH = 16
FAR = 100


def block(channels, width):
    own = (np.repeat(np.arange(channels), 8), np.tile(np.arange(8), channels))
    rim_c = np.concatenate([np.repeat(np.arange(channels), 2)] * 2)
    rim_y = np.concatenate([np.tile([-2, -1], channels), np.tile([8, 9], channels)])
    return own, (rim_c, rim_y)


def tables():
    own, rim = block(CI, 128)
    e1 = np.zeros((3 * CI, 384), np.float32)
    y1 = np.full(384, FAR)
    for c in range(3):
        for (ch, y), at in ((own, c * 128), (rim, c * 128 + 64)):
            e1[c * CI + ch, at + np.arange(len(ch))] = 1
            y1[at:at + len(ch)] = y
    own, rim = block(CH, 192)
    e2 = np.zeros((3 * CH, 640), np.float32)
    y2 = np.full(640, FAR)
    for c in range(3):
        for (ch, y), at in ((own, c * 128), (rim, 384 + c * 64)):
            e2[c * CH + ch, at + np.arange(len(ch))] = 1
            y2[at:at + len(ch)] = y
    expand = np.zeros((128, CH), np.float32)
    expand[np.arange(128), own[0]] = 1
    return e1, y1, e2, y2, own[1], expand


def plane(ref, x):
    v = ref[0, :, x].astype(F32)
    return v.reshape(v.shape[0] * v.shape[1], v.shape[2])


def pick_rows(rims, rows):
    half = rims // 2
    row = lax.broadcasted_iota(jnp.int32, (rims, rows), 0)
    col = lax.broadcasted_iota(jnp.int32, (rims, rows), 1)
    side = jnp.where(row >= half, 1, 0)
    q = row - side * half
    return jnp.where(col == (q // 2) * 8 + 6 * side + q % 2, 1.0, 0.0).astype(BF16)


def pack_kernel(fields, cot, low, high, fields_here, cot_here, sems):
    copies = [
        pltpu.make_async_copy(fields, fields_here, sems.at[0]),
        pltpu.make_async_copy(cot, cot_here, sems.at[1]),
    ]
    for copy in copies:
        copy.start()
    for copy in copies:
        copy.wait()
    last = fields.shape[2] - 2
    for out, x in ((low, 0), (high, last)):
        for n in range(2):
            out[n, :64] = plane(fields_here, x + n).astype(BF16)
            out[n, 64:] = plane(cot_here, x + n).astype(BF16)


def join_kernel(fields, cot, xlo, xhi, low, high):
    pick = pick_rows(96, 192)
    count = fields.shape[2]
    for p in range(count + 4):
        x = p - 2
        if x < 0:
            rows = xlo[p]
        elif x >= count:
            rows = xhi[x - count]
        else:
            rows = jnp.concatenate([plane(fields, x), plane(cot, x)], axis=0).astype(BF16)
        got = jnp.dot(pick, rows, preferred_element_type=F32).astype(BF16)
        low[p] = got[:48]
        high[p] = got[48:]


def join_hidden_kernel(hidden, xlo, xhi, low, high):
    pick = pick_rows(64, 128)
    count = hidden.shape[0]
    for p in range(count + 4):
        x = p - 2
        rows = xlo[p] if x < 0 else xhi[x - count] if x >= count else hidden[x]
        got = jnp.dot(pick, rows, preferred_element_type=F32).astype(BF16)
        low[p] = got[:32]
        high[p] = got[32:]


def band(w, e, expand, ys, rows_y, t):
    width = e.shape[1]
    wide = jnp.dot(w[...], e[...], preferred_element_type=F32).astype(BF16)
    for a in range(3):
        total = jnp.zeros((128, width), F32)
        for b in range(3):
            part = jnp.dot(expand[...], wide[(a * 3 + b) * CH:(a * 3 + b + 1) * CH], preferred_element_type=F32)
            total = jnp.where(ys[...] == rows_y[...] + float(2 * (b - 1)), part, total)
        t[:, a * width:(a + 1) * width] = total.astype(BF16)


def repeat_bias(bias, expand, out):
    column = jnp.sum(expand[...].astype(F32) * bias[...], axis=1, keepdims=True)
    out[...] = jnp.broadcast_to(column, out.shape)


def band_first_kernel(w1, wb, bias, e1, e2, expand, y1, y2, rows_y, t1, tb, b1):
    band(w1, e1, expand, y1, rows_y, t1)
    band(wb, e2, expand, y2, rows_y, tb)
    repeat_bias(bias, expand, b1)


def band_second_kernel(w2, bias, e2, expand, y2, rows_y, t2, b2):
    band(w2, e2, expand, y2, rows_y, t2)
    repeat_bias(bias, expand, b2)


def shifted(v):
    lane = lax.broadcasted_iota(jnp.int32, v.shape, 1)
    before = jnp.where(lane >= 2, pltpu.roll(v, 2, 1), 0.0)
    after = jnp.where(lane < Z - 2, pltpu.roll(v, Z - 2, 1), 0.0)
    return before.astype(BF16), v.astype(BF16), after.astype(BF16)


def store_wide(ref, p, v):
    at = slice(p * Z, (p + 1) * Z)
    for c, piece in enumerate(shifted(v)):
        ref[c * 128:(c + 1) * 128, at] = piece[:128]
        ref[384 + c * 64:384 + (c + 1) * 64, at] = piece[128:]
    ref[576:, at] = jnp.zeros((64, Z), BF16)


def stacked(ref, lanes):
    return jnp.concatenate([ref[:, a * 256:a * 256 + lanes] for a in range(3)], axis=0)


def first_kernel(fields, cot, xlo, xhi, rlo, rhi, t1, tb, b1, er1, er2, y1, y2, yo,
                 hidden_out, hidden_low, hidden_high, payload, fs, cs):
    count = fields.shape[2]
    lanes = count * Z
    zeros = jnp.zeros((32, Z), F32)
    for p in range(count + 4):
        x = p - 2
        if x < 0:
            own = xlo[p].astype(F32)
        elif x >= count:
            own = xhi[x - count].astype(F32)
        else:
            own = jnp.concatenate([plane(fields, x), plane(cot, x)], axis=0)
        low, high = rlo[p].astype(F32), rhi[p].astype(F32)
        for c, piece in enumerate(shifted(jnp.concatenate([own[:64], low[:16], high[:16], zeros], axis=0))):
            fs[c * 128:(c + 1) * 128, p * Z:(p + 1) * Z] = piece
        store_wide(cs, p, jnp.concatenate([own[64:], low[16:], high[16:]], axis=0))
    pre = jnp.dot(t1[...], stacked(fs, lanes), preferred_element_type=F32) + b1[...]
    share = 0.5 * (1.0 + lax.erf(pre * 0.7071067811865476))
    hidden = (pre * share).astype(BF16)
    for x in range(count):
        hidden_out[x] = hidden[:, x * Z:(x + 1) * Z]
    for n in range(2):
        hidden_low[n] = hidden[:, n * Z:(n + 1) * Z]
        hidden_high[n] = hidden[:, (count - 2 + n) * Z:(count - 1 + n) * Z]
    back = jnp.dot(tb[...], stacked(cs, lanes), preferred_element_type=F32)
    dpre = (back * (share + pre * jnp.exp(-0.5 * pre * pre) * 0.3989422804014327)).astype(BF16)
    bias = jnp.sum(dpre.astype(F32), axis=1, keepdims=True)
    lane = lax.broadcasted_iota(jnp.int32, (8, 256), 1)

    def diagonal(rows, place):
        total = jnp.zeros((8, rows.shape[1]), F32)
        for o in range(CH):
            total = jnp.where(place == o, rows[o * 8:(o + 1) * 8], total)
        return jnp.sum(total, axis=0, keepdims=True)

    payload[24:] = jnp.zeros((8, 384), F32)
    payload[27:28, :128] = diagonal(jnp.broadcast_to(bias, (128, 128)), lane[:, :128])
    over_lanes = (((1,), (1,)), ((), ()))
    for a in range(3):
        g1 = lax.dot_general(dpre, fs[:, a * 256:a * 256 + lanes], over_lanes, preferred_element_type=F32)
        g2 = lax.dot_general(hidden, cs[:, a * 256:a * 256 + lanes], over_lanes, preferred_element_type=F32)
        for b in range(3):
            off = float(2 * (b - 1))
            one = jnp.where(y1[...] == yo[...] + off, g1, 0.0).astype(BF16)
            two = jnp.where(y2[...] == yo[...] + off, g2, 0.0).astype(BF16)
            for c in range(3):
                tap = (a * 3 + b) * 3 + c
                r1 = jnp.dot(one[:, c * 128:(c + 1) * 128], er1[...], preferred_element_type=F32)
                rim = 384 + (c // 2) * 128
                both = jnp.concatenate([two[:, c * 128:(c + 1) * 128], two[:, rim:rim + 128]], axis=1)
                r2 = jnp.dot(both, er2[c % 2], preferred_element_type=F32)
                payload[tap:tap + 1, :128] = diagonal(r1, lane[:, :128] // CI)
                payload[26 - tap:27 - tap, 128:] = diagonal(r2, lane % CH)


def closure_kernel(hidden, xlo, xhi, rlo, rhi, t2, b2, closure, hs):
    count = hidden.shape[0]
    for p in range(count + 4):
        x = p - 2
        own = xlo[p] if x < 0 else xhi[x - count] if x >= count else hidden[x]
        store_wide(hs, p, jnp.concatenate([own, rlo[p], rhi[p]], axis=0).astype(F32))
    out = (jnp.dot(t2[...], stacked(hs, count * Z), preferred_element_type=F32) + b2[...]).astype(BF16)
    for x in range(count):
        closure[0, :, x] = out[:, x * Z:(x + 1) * Z].reshape(CH, 8, Z)


def finish_kernel(norm, total, first, second, bias):
    scaled = total[...] * norm
    flipped = jnp.transpose(scaled)
    first[...] = flipped[:128, :27]
    second[...] = flipped[128:, :27]
    bias[...] = scaled[27:28, :CH]


def call(kernel, outs, name, scratch=(), flops=10_000_000, **specs):
    return pl.pallas_call(
        kernel,
        out_shape=outs,
        **specs,
        scratch_shapes=list(scratch),
        compiler_params=pltpu.CompilerParams(vmem_limit_bytes=48 * 1024 * 1024),
        cost_estimate=pl.CostEstimate(flops=flops, bytes_accessed=1_000_000, transcendentals=0),
        name=name,
    )


def shape(*dims, dtype=BF16):
    return jax.ShapeDtypeStruct(dims, dtype)


def exchange(low, high, axis):
    count = lax.axis_size(axis)
    up = [(i, i + 1) for i in range(count - 1)]
    down = [(j, i) for i, j in up]
    return lax.ppermute(high, axis, up), lax.ppermute(low, axis, down)


def reduce_all(v, axes):
    for axis in axes:
        count = lax.axis_size(axis)
        if count & (count - 1):
            v = lax.psum(v, axis)
            continue

        def swapped(mask):
            return lax.ppermute(v, axis, [(i, i ^ mask) for i in range(count)])

        step = 1
        while step < count:
            if step * 4 <= count:
                one, two, three = swapped(step), swapped(2 * step), swapped(3 * step)
                v = (v + one) + (two + three)
                step *= 4
            else:
                v = v + swapped(step)
                step *= 2
    return v


def local(fields, first_weight, first_bias, second_weight, second_bias, cotangent):
    e1, y1, e2, y2, rows_y, expand = tables()
    er1 = np.tile(e1[:CI, :128].T, (1, CH))
    er2 = np.zeros((2, 256, 256), np.float32)
    for half in range(2):
        er2[half, :128] = np.repeat(e2[:CH, :128].T, CH, axis=1)
        er2[half, 128 + half * 64:192 + half * 64] = np.repeat(e2[:CH, 384:448].T, CH, axis=1)
    e1, e2, er1, er2, expand = (jnp.asarray(v, BF16) for v in (e1, e2, er1, er2, expand))
    y1, y2, rows_y = (jnp.asarray(v, F32) for v in (y1[None], y2[None], rows_y[:, None]))
    planes = fields.shape[2]
    low, high = call(
        pack_kernel,
        (shape(2, 192, Z),) * 2,
        "pack_strips",
        (pltpu.VMEM(fields.shape, BF16), pltpu.VMEM(cotangent.shape, BF16), pltpu.SemaphoreType.DMA((2,))),
        in_specs=[pl.BlockSpec(memory_space=pl.ANY)] * 2,
    )(fields, cotangent)
    xlo, xhi = exchange(low, high, "stream")

    w1 = first_weight.reshape(3, 3, 3, CH, CI).transpose(0, 1, 3, 2, 4).reshape(9 * CH, 3 * CI)
    w2 = second_weight.reshape(3, 3, 3, CH, CH)
    wb = w2[::-1, ::-1, ::-1].transpose(0, 1, 4, 2, 3).reshape(9 * CH, 3 * CH)
    w2 = w2.transpose(0, 1, 3, 2, 4).reshape(9 * CH, 3 * CH)
    spread = shape(128, planes * Z, dtype=F32)
    t1, tb, b1 = call(band_first_kernel, (shape(128, 1152), shape(128, 1920), spread), "band_first")(
        w1, wb, first_bias[None], e1, e2, expand, y1, y2, rows_y)

    low, high = call(join_kernel, (shape(planes + 4, 48, Z),) * 2, "join_strips")(fields, cotangent, xlo, xhi)
    rlo, rhi = exchange(low, high, "radial")
    wide = (planes + 4) * Z
    hidden, low, high, payload = call(
        first_kernel,
        (shape(planes, 128, Z), shape(2, 128, Z), shape(2, 128, Z), shape(32, 384, dtype=F32)),
        "gradients",
        (pltpu.VMEM((384, wide), BF16), pltpu.VMEM((640, wide), BF16)),
        flops=2_000_000_000,
    )(fields, cotangent, xlo, xhi, rlo, rhi, t1, tb, b1, er1, er2, y1, y2, rows_y)
    total = reduce_all(payload, ("radial", "stream", "snap"))

    xlo, xhi = exchange(low, high, "stream")
    low, high = call(join_hidden_kernel, (shape(planes + 4, 32, Z),) * 2, "join_hidden")(hidden, xlo, xhi)
    rlo, rhi = exchange(low, high, "radial")
    t2, b2 = call(band_second_kernel, (shape(128, 1920), spread), "band_second")(
        w2, second_bias[None], e2, expand, y2, rows_y)
    closure = call(
        closure_kernel, shape(*cotangent.shape), "closure", (pltpu.VMEM((640, wide), BF16),), flops=1_000_000_000
    )(hidden, xlo, xhi, rlo, rhi, t2, b2)

    cells = fields.shape[0] * fields.shape[2] * fields.shape[3] * fields.shape[4]
    for axis in ("stream", "radial", "snap"):
        cells *= lax.axis_size(axis)
    norm = float(1.0 / np.sqrt(np.float32(cells)))
    first, second, bias = call(
        functools.partial(finish_kernel, norm),
        (shape(CH * CI, 27, dtype=F32), shape(CH * CH, 27, dtype=F32), shape(1, CH, dtype=F32)),
        "finish",
    )(total)
    first = first.reshape(CH, CI, 27).transpose(2, 0, 1)
    second = second.reshape(CH, CH, 27).transpose(2, 0, 1)
    return (closure, first, second, bias[0])


def solution(mesh):
    split = P("snap", None, "stream", "radial", None)
    return jax.shard_map(
        local,
        mesh=mesh,
        in_specs=(split, P(), P(), P(), P(), split),
        out_specs=(split, P(), P(), P()),
        check_vma=False,
    )
```

time: 50.6 us -> 52.1 us (1.030)
  starting transfers between devices: 18.3 us -> 28.4 us
  waiting for transfers between devices: 17.3 us -> 8.66 us
    ppermute x5 -> x7, waiting for transfers between devices: 10.8 us -> 2.82 us  [swapped(): return lax.ppermute(v, axis, [(i, i ^ mask) for i in range(count)])]
    ppermute x4 -> x8, starting transfers between devices: 8.44 us -> 16.3 us  [exchange(): return (lax.ppermute(high, axis, up), lax.ppermute(low, axis, down))]
    ppermute x5 -> x7, starting transfers between devices: 9.91 us -> 12.1 us  [swapped(): return lax.ppermute(v, axis, [(i, i ^ mask) for i in range(count)])]
    ppermute x4 -> x8, waiting for transfers between devices: 6.57 us -> 5.84 us  [exchange(): return (lax.ppermute(high, axis, up), lax.ppermute(low, axis, down))]
    unnamed x36 -> x34, local copies, waits for them, and re-layouts: 3.48 us -> 3.92 us
    pallas_call x4 -> x7, Pallas kernels: 8.58 us -> 8.2 us  [the longest x1 4.14 us: local(): call(first_kernel, (shape(planes, 128, Z), shape(2, 128, Z), shape(2, 128...]
  transfers between devices with their start and end apart: 9 -> 15, of which waited for: 7 -> 6; matrix products, arithmetic and copies ran while one was open for 2% -> 2% of each run, Pallas kernels for 3% -> 5%
where the time goes in v2:
time: 52.1 us; the launch traced here: 51.7 us
  starting transfers between devices  28.4 us (55%)
  Pallas kernels  8.99 us (17%)
  waiting for transfers between devices  8.66 us (17%)
  local copies, waits for them, and re-layouts  4.63 us (9%)
  between operations  0.96 us (2%)
    ppermute x8, starting transfers between devices, exchange(): return (lax.ppermute(high, axis, up), lax.ppermute(low, axis, down))  16.3 us
    ppermute x7, starting transfers between devices, swapped(): return lax.ppermute(v, axis, [(i, i ^ mask) for i in range(count)])  12.1 us
    ppermute x8, waiting for transfers between devices, exchange(): return (lax.ppermute(high, axis, up), lax.ppermute(low, axis, down))  5.84 us
    pallas_call x1, Pallas kernels, local(): call(first_kernel, (shape(planes, 128, Z), shape(2, 128, Z), shape(2, 128...  4.14 us
    unnamed x34, local copies, waits for them, and re-layouts  3.92 us
    ppermute x7, waiting for transfers between devices, swapped(): return lax.ppermute(v, axis, [(i, i ^ mask) for i in range(count)])  2.82 us
    pallas_call x1, Pallas kernels, local(): call(closure_kernel, shape(*cotangent.shape), 'closure', (pltpu.VMEM((640...  1.59 us
  transfers between devices with their start and end apart: 15, of which 6 were waited for; matrix products, arithmetic and copies ran while one was open for 2% of the time, Pallas kernels for 5%

profile of v2, /device:TPU:0, one launch (start us, length us, event | category | flops | bytes accessed | tf_op | source)
XLA Modules:
  0.0 51.7 jit_solution(7636956147879694913)
XLA Ops:
  0.6 0.0 copy-start
  0.6 0.9 %copy-done = bf16[1,16,8,8,128]{4,3,2,1,0:T(8,128)(2,1)S(1)} copy-done((bf16[1,16,8,8,128]{4,3,2,1,0:T(8,128)(2,1)S(1)}, bf16[1,16,8,8,128]{4,3,2,1,0:T(8,128)(2,1)}, u32[]{:S(2)}) %copy-start) | copy-done | bytes 262168
  1.6 0.9 %copy-done.2 = bf16[1,8,8,8,128]{4,3,2,1,0:T(8,128)(2,1)S(1)} copy-done((bf16[1,8,8,8,128]{4,3,2,1,0:T(8,128)(2,1)S(1)}, bf16[1,8,8,8,128]{4,3,2,1,0:T(8,128)(2,1)}, u32[]{:S(2)}) %copy-start.2) | copy-done | bytes 131096
  2.5 0.2 pack_strips.1
  2.7 4.9 %collective-permute-start = (bf16[2,192,128]{2,1,0:T(8,128)(2,1)S(1)}, bf16[2,192,128]{2,1,0:T(8,128)(2,1)S(1)}, u32[]{:S(2)}, u32[]{:S(2)}) collective-permute-start(bf16[2,192,128]{2,1,0:T(8,128)(2,1)S(1)} %get-tuple-element.22), channel_id=1, source_target_pairs={{0,8},{8,16},{16,24},{1,9},{9,17},{17,25},{2,10},{10,18},{18,26},{... | collective-permute-start | bytes 294920 | tf_op jit(solution)/shard_map/ppermute | solution.py:244
  7.6 0.0 copy-start.14
  7.7 1.4 %collective-permute-start.1 = (bf16[2,192,128]{2,1,0:T(8,128)(2,1)S(1)}, bf16[2,192,128]{2,1,0:T(8,128)(2,1)S(1)}, u32[]{:S(2)}, u32[]{:S(2)}) collective-permute-start(bf16[2,192,128]{2,1,0:T(8,128)(2,1)S(1)} %get-tuple-element.23), channel_id=1, source_target_pairs={{8,0},{16,8},{24,16},{9,1},{17,9},{25,17},{10,2},{18,10},{26,18},{... | collective-permute-start | bytes 294920 | tf_op jit(solution)/shard_map/ppermute | solution.py:244
  9.1 0.7 %collective-permute-done.xlo = bf16[2,192,128]{2,1,0:T(8,128)(2,1)S(1)} collective-permute-done((bf16[2,192,128]{2,1,0:T(8,128)(2,1)S(1)}, bf16[2,192,128]{2,1,0:T(8,128)(2,1)S(1)}, u32[]{:S(2)}, u32[]{:S(2)}) %collective-permute-start) | collective-permute-done | bytes 98336 | tf_op jit(solution)/shard_map/ppermute | solution.py:244
  9.8 4.5 %collective-permute-done.1.xhi = bf16[2,192,128]{2,1,0:T(8,128)(2,1)S(1)} collective-permute-done((bf16[2,192,128]{2,1,0:T(8,128)(2,1)S(1)}, bf16[2,192,128]{2,1,0:T(8,128)(2,1)S(1)}, u32[]{:S(2)}, u32[]{:S(2)}) %collective-permute-start.1) | collective-permute-done | bytes 98336 | tf_op jit(solution)/shard_map/ppermute | solution.py:244
  14.3 0.3 join_strips.1
  14.6 1.3 %collective-permute-start.2 = (bf16[12,48,128]{2,1,0:T(8,128)(2,1)S(1)}, bf16[12,48,128]{2,1,0:T(8,128)(2,1)S(1)}, u32[]{:S(2)}, u32[]{:S(2)}) collective-permute-start(bf16[12,48,128]{2,1,0:T(8,128)(2,1)S(1)} %get-tuple-element.24), channel_id=1, source_target_pairs={{0,2},{2,4},{4,6},{1,3},{3,5},{5,7},{8,10},{10,12},{12,14},{9,11},... | collective-permute-start | bytes 442376 | tf_op jit(solution)/shard_map/ppermute | solution.py:244
  15.9 1.3 %collective-permute-start.3 = (bf16[12,48,128]{2,1,0:T(8,128)(2,1)S(1)}, bf16[12,48,128]{2,1,0:T(8,128)(2,1)S(1)}, u32[]{:S(2)}, u32[]{:S(2)}) collective-permute-start(bf16[12,48,128]{2,1,0:T(8,128)(2,1)S(1)} %get-tuple-element.25), channel_id=1, source_target_pairs={{2,0},{4,2},{6,4},{3,1},{5,3},{7,5},{10,8},{12,10},{14,12},{11,9},... | collective-permute-start | bytes 442376 | tf_op jit(solution)/shard_map/ppermute | solution.py:244
  17.2 0.2 copy.23
  17.5 0.0 copy-start.12
  17.5 0.1 copy.29
  17.6 0.0 copy-start.15
  17.6 0.1 reshape.36.wb
  17.8 0.6 %copy-done.15 = bf16[27,16,8]{0,2,1:T(8,128)(2,1)S(1)} copy-done((bf16[27,16,8]{0,2,1:T(8,128)(2,1)S(1)}, bf16[27,16,8]{0,2,1:T(8,128)(2,1)}, u32[]{:S(2)}) %copy-start.15) | copy-done | bytes 6936
  18.4 0.0 copy-start.8
  18.4 0.0 copy-start.9
  18.4 0.0 copy-start.10
  18.4 0.1 copy.21
  18.6 0.0 copy-start.1
  18.6 0.1 reshape.30
  18.7 0.1 copy.25.w1
  18.9 0.4 copy-done.4
  19.2 0.0 copy-done.5
  19.2 0.0 copy-done.9
  19.3 0.0 copy-start.3
  19.3 0.0 copy-start.13
  19.3 1.0 %band_first.1 = (bf16[128,1152]{1,0:T(8,128)(2,1)S(1)}, bf16[128,1920]{1,0:T(8,128)(2,1)S(1)}, f32[128,1024]{1,0:T(8,128)S(1)}) custom-call(bf16[144,24]{1,0:T(8,128)(2,1)S(1)} %copy.25.w1, bf16[144,48]{1,0:T(8,128)(2,1)S(1)} %reshape.36.wb, f32[1,16]{1,0:T(1,128)S(1)} %bitcast.19, bf16[24,384]{1,0:T(8,128)(2,1)S(1)} %copy-done.7, ...), custom_call_target="tpu_custom_call" | custom-call | flops 10000000 | bytes 1000000 | tf_op jit(solution)/shard_map/band_first/pallas_call | solution.py:293
  20.3 0.0 collective-permute-done.2.rlo
  20.3 0.6 %collective-permute-done.3.rhi = bf16[12,48,128]{2,1,0:T(8,128)(2,1)S(1)} collective-permute-done((bf16[12,48,128]{2,1,0:T(8,128)(2,1)S(1)}, bf16[12,48,128]{2,1,0:T(8,128)(2,1)S(1)}, u32[]{:S(2)}, u32[]{:S(2)}) %collective-permute-start.3) | collective-permute-done | bytes 147488 | tf_op jit(solution)/shard_map/ppermute | solution.py:244
  21.0 4.1 %gradients.1 = (bf16[8,128,128]{2,1,0:T(8,128)(2,1)S(1)}, bf16[2,128,128]{2,1,0:T(8,128)(2,1)S(1)}, bf16[2,128,128]{2,1,0:T(8,128)(2,1)S(1)}, f32[32,384]{1,0:T(8,128)S(1)}) custom-call(bf16[1,8,8,8,128]{4,3,2,1,0:T(8,128)(2,1)S(1)} %copy-done.3, bf16[1,16,8,8,128]{4,3,2,1,0:T(8,128)(2,1)S(1)} %copy-done.1, ...), custom_call_target="tpu_custom_call" | custom-call | flops 2000000000 | bytes 1000000 | tf_op jit(solution)/shard_map/gradients/pallas_call | solution.py:299
  25.1 2.4 %collective-permute-start.10 = (f32[32,384]{1,0:T(8,128)S(1)}, f32[32,384]{1,0:T(8,128)S(1)}, u32[]{:S(2)}, u32[]{:S(2)}) collective-permute-start(f32[32,384]{1,0:T(8,128)S(1)} %get-tuple-element.36), channel_id=1, source_target_pairs={{0,6},{2,4},{4,2},{6,0},{1,7},{3,5},{5,3},{7,1},{8,14},{10,12},{12... | collective-permute-start | bytes 147464 | tf_op jit(solution)/shard_map/ppermute | solution.py:255
  27.5 1.7 %collective-permute-start.8 = (f32[32,384]{1,0:T(8,128)S(1)}, f32[32,384]{1,0:T(8,128)S(1)}, u32[]{:S(2)}, u32[]{:S(2)}) collective-permute-start(f32[32,384]{1,0:T(8,128)S(1)} %get-tuple-element.36), channel_id=1, source_target_pairs={{0,2},{2,0},{4,6},{6,4},{1,3},{3,1},{5,7},{7,5},{8,10},{10,8},{12,... | collective-permute-start | bytes 147464 | tf_op jit(solution)/shard_map/ppermute | solution.py:255
  29.2 1.3 %collective-permute-start.9 = (f32[32,384]{1,0:T(8,128)S(1)}, f32[32,384]{1,0:T(8,128)S(1)}, u32[]{:S(2)}, u32[]{:S(2)}) collective-permute-start(f32[32,384]{1,0:T(8,128)S(1)} %get-tuple-element.36), channel_id=1, source_target_pairs={{0,4},{2,6},{4,0},{6,2},{1,5},{3,7},{5,1},{7,3},{8,12},{10,14},{12... | collective-permute-start | bytes 147464 | tf_op jit(solution)/shard_map/ppermute | solution.py:255
  30.5 3.5 %collective-permute-start.4 = (bf16[2,128,128]{2,1,0:T(8,128)(2,1)S(1)}, bf16[2,128,128]{2,1,0:T(8,128)(2,1)S(1)}, u32[]{:S(2)}, u32[]{:S(2)}) collective-permute-start(bf16[2,128,128]{2,1,0:T(8,128)(2,1)S(1)} %get-tuple-element.30), channel_id=1, source_target_pairs={{0,8},{8,16},{16,24},{1,9},{9,17},{17,25},{2,10},{10,18},{18,26},{... | collective-permute-start | bytes 196616 | tf_op jit(solution)/shard_map/ppermute | solution.py:244
  34.0 1.3 %collective-permute-start.5 = (bf16[2,128,128]{2,1,0:T(8,128)(2,1)S(1)}, bf16[2,128,128]{2,1,0:T(8,128)(2,1)S(1)}, u32[]{:S(2)}, u32[]{:S(2)}) collective-permute-start(bf16[2,128,128]{2,1,0:T(8,128)(2,1)S(1)} %get-tuple-element.31), channel_id=1, source_target_pairs={{8,0},{16,8},{24,16},{9,1},{17,9},{25,17},{10,2},{18,10},{26,18},{... | collective-permute-start | bytes 196616 | tf_op jit(solution)/shard_map/ppermute | solution.py:244
  35.3 0.0 collective-permute-done.10
  35.3 0.0 collective-permute-done.8
  35.3 0.0 collective-permute-done.9
  35.3 2.7 %collective-permute-start.11 = (f32[32,384]{1,0:T(8,128)S(1)}, f32[32,384]{1,0:T(8,128)S(1)}, u32[]{:S(2)}, u32[]{:S(2)}) collective-permute-start(f32[32,384]{1,0:T(8,128)S(1)} %add_add_fusion.1), channel_id=1, source_target_pairs={{0,8},{8,0},{16,24},{24,16},{1,9},{9,1},{17,25},{25,17},{2,10},{10... | collective-permute-start | bytes 147464 | tf_op jit(solution)/shard_map/ppermute | solution.py:255
  38.0 1.1 %collective-permute-start.12 = (f32[32,384]{1,0:T(8,128)S(1)}, f32[32,384]{1,0:T(8,128)S(1)}, u32[]{:S(2)}, u32[]{:S(2)}) collective-permute-start(f32[32,384]{1,0:T(8,128)S(1)} %add_add_fusion.1), channel_id=1, source_target_pairs={{0,16},{8,24},{16,0},{24,8},{1,17},{9,25},{17,1},{25,9},{2,18},{10... | collective-permute-start | bytes 147464 | tf_op jit(solution)/shard_map/ppermute | solution.py:255
  39.1 1.4 %collective-permute-start.13 = (f32[32,384]{1,0:T(8,128)S(1)}, f32[32,384]{1,0:T(8,128)S(1)}, u32[]{:S(2)}, u32[]{:S(2)}) collective-permute-start(f32[32,384]{1,0:T(8,128)S(1)} %add_add_fusion.1), channel_id=1, source_target_pairs={{0,24},{8,16},{16,8},{24,0},{1,25},{9,17},{17,9},{25,1},{2,26},{10... | collective-permute-start | bytes 147464 | tf_op jit(solution)/shard_map/ppermute | solution.py:255
  40.5 0.0 collective-permute-done.4.xlo
  40.5 0.0 collective-permute-done.5.xhi
  40.5 0.2 join_hidden.1
  40.8 1.3 %collective-permute-start.6 = (bf16[12,32,128]{2,1,0:T(8,128)(2,1)S(1)}, bf16[12,32,128]{2,1,0:T(8,128)(2,1)S(1)}, u32[]{:S(2)}, u32[]{:S(2)}) collective-permute-start(bf16[12,32,128]{2,1,0:T(8,128)(2,1)S(1)} %get-tuple-element.32), channel_id=1, source_target_pairs={{0,2},{2,4},{4,6},{1,3},{3,5},{5,7},{8,10},{10,12},{12,14},{9,11},... | collective-permute-start | bytes 294920 | tf_op jit(solution)/shard_map/ppermute | solution.py:244
  42.1 1.3 %collective-permute-start.7 = (bf16[12,32,128]{2,1,0:T(8,128)(2,1)S(1)}, bf16[12,32,128]{2,1,0:T(8,128)(2,1)S(1)}, u32[]{:S(2)}, u32[]{:S(2)}) collective-permute-start(bf16[12,32,128]{2,1,0:T(8,128)(2,1)S(1)} %get-tuple-element.33), channel_id=1, source_target_pairs={{2,0},{4,2},{6,4},{3,1},{5,3},{7,5},{10,8},{12,10},{14,12},{11,9},... | collective-permute-start | bytes 294920 | tf_op jit(solution)/shard_map/ppermute | solution.py:244
  43.4 0.0 collective-permute-done.11
  43.4 0.9 %collective-permute-done.12 = f32[32,384]{1,0:T(8,128)S(1)} collective-permute-done((f32[32,384]{1,0:T(8,128)S(1)}, f32[32,384]{1,0:T(8,128)S(1)}, u32[]{:S(2)}, u32[]{:S(2)}) %collective-permute-start.12) | collective-permute-done | bytes 49184 | tf_op jit(solution)/shard_map/ppermute | solution.py:255
  44.3 0.8 %collective-permute-done.13 = f32[32,384]{1,0:T(8,128)S(1)} collective-permute-done((f32[32,384]{1,0:T(8,128)S(1)}, f32[32,384]{1,0:T(8,128)S(1)}, u32[]{:S(2)}, u32[]{:S(2)}) %collective-permute-start.13) | collective-permute-done | bytes 49184 | tf_op jit(solution)/shard_map/ppermute | solution.py:255
  45.2 1.6 %collective-permute-start.14 = (f32[32,384]{1,0:T(8,128)S(1)}, f32[32,384]{1,0:T(8,128)S(1)}, u32[]{:S(2)}, u32[]{:S(2)}) collective-permute-start(f32[32,384]{1,0:T(8,128)S(1)} %add_add_fusion), channel_id=1, source_target_pairs={{0,1},{1,0},{2,3},{3,2},{4,5},{5,4},{6,7},{7,6},{8,9},{9,8},{10,11... | collective-permute-start | bytes 147464 | tf_op jit(solution)/shard_map/ppermute | solution.py:255
  46.7 0.1 copy.30
  46.8 0.1 reshape.37.w2
  46.9 0.0 copy-start.11
  46.9 0.6 %copy-done.11 = f32[16]{0:T(128)S(1)} copy-done((f32[16]{0:T(128)S(1)}, f32[16]{0:T(128)}, u32[]{:S(2)}) %copy-start.11) | copy-done | bytes 88
  47.6 0.7 %band_second.1 = (bf16[128,1920]{1,0:T(8,128)(2,1)S(1)}, f32[128,1024]{1,0:T(8,128)S(1)}) custom-call(bf16[144,48]{1,0:T(8,128)(2,1)S(1)} %reshape.37.w2, f32[1,16]{1,0:T(1,128)S(1)} %bitcast.20, bf16[48,640]{1,0:T(8,128)(2,1)S(1)} %copy-done.5, bf16[128,16]{1,0:T(8,128)(2,1)S(1)} %copy-done.6, f32[1,640]{1,0:T(1,128)S(1)} %copy-done.8, f32[128,1]{1,0:T(8,128)S(1)} %copy-done.4), custom_call_target="tpu_custom_call" | custom-call | flops 10000000 | bytes 1000000 | tf_op jit(solution)/shard_map/band_second/pallas_call | solution.py:311
  48.3 1.1 %collective-permute-done.14 = f32[32,384]{1,0:T(8,128)S(1)} collective-permute-done((f32[32,384]{1,0:T(8,128)S(1)}, f32[32,384]{1,0:T(8,128)S(1)}, u32[]{:S(2)}, u32[]{:S(2)}) %collective-permute-start.14) | collective-permute-done | bytes 49184 | tf_op jit(solution)/shard_map/ppermute | solution.py:255
  49.3 0.8 %finish.1 = (f32[128,27]{1,0:T(8,128)}, f32[256,27]{1,0:T(8,128)}, f32[1,16]{1,0:T(1,128)}) custom-call(f32[32,384]{1,0:T(8,128)S(1)} %add.27.total), custom_call_target="tpu_custom_call" | custom-call | flops 10000000 | bytes 1000000 | tf_op jit(solution)/shard_map/finish/pallas_call | solution.py:321
  50.1 0.0 collective-permute-done.6.rlo
  50.1 0.0 collective-permute-done.7.rhi
  50.1 1.6 %closure.1 = bf16[1,16,8,8,128]{4,3,2,1,0:T(8,128)(2,1)} custom-call(bf16[8,128,128]{2,1,0:T(8,128)(2,1)S(1)} %get-tuple-element.29.hidden, bf16[2,128,128]{2,1,0:T(8,128)(2,1)S(1)} %collective-permute-done.4.xlo, bf16[2,128,128]{2,1,0:T(8,128)(2,1)S(1)} %collective-permute-done.5.xhi, bf16[12,32,128]{2,1,0:T(8,128)(2,1)S(1)} %collective-permute-done.6.rlo, ...), custom_call_target="tpu_custom_call" | custom-call | flops 1000000000 | bytes 1000000 | tf_op jit(solution)/shard_map/closure/pallas_call | solution.py:313
  (19 shorter events, 0.1 us)
Async XLA Ops:
  0.6 1.0 %copy-start = (bf16[1,16,8,8,128]{4,3,2,1,0:T(8,128)(2,1)S(1)}, bf16[1,16,8,8,128]{4,3,2,1,0:T(8,128)(2,1)}, u32[]{:S(2)}) copy-start(bf16[1,16,8,8,128]{4,3,2,1,0:T(8,128)(2,1)} %cot.5) | copy-start | bytes 786436
  1.6 0.9 %copy-start.2 = (bf16[1,8,8,8,128]{4,3,2,1,0:T(8,128)(2,1)S(1)}, bf16[1,8,8,8,128]{4,3,2,1,0:T(8,128)(2,1)}, u32[]{:S(2)}) copy-start(bf16[1,8,8,8,128]{4,3,2,1,0:T(8,128)(2,1)} %fields.5) | copy-start | bytes 393220
  2.7 7.1 %collective-permute-start = (bf16[2,192,128]{2,1,0:T(8,128)(2,1)S(1)}, bf16[2,192,128]{2,1,0:T(8,128)(2,1)S(1)}, u32[]{:S(2)}, u32[]{:S(2)}) collective-permute-start(bf16[2,192,128]{2,1,0:T(8,128)(2,1)S(1)} %get-tuple-element.22), channel_id=1, source_target_pairs={{0,8},{8,16},{16,24},{1,9},{9,17},{17,25},{2,10},{10,18},{18,26},{... | collective-permute-start | bytes 294920 | tf_op jit(solution)/shard_map/ppermute | solution.py:244
  7.6 9.6 %copy-start.14 = (bf16[27,16,16]{0,2,1:T(8,128)(2,1)S(1)}, bf16[27,16,16]{0,2,1:T(8,128)(2,1)}, u32[]{:S(2)}) copy-start(bf16[27,16,16]{0,2,1:T(8,128)(2,1)} %param.17) | copy-start | bytes 41476
  7.7 6.6 %collective-permute-start.1 = (bf16[2,192,128]{2,1,0:T(8,128)(2,1)S(1)}, bf16[2,192,128]{2,1,0:T(8,128)(2,1)S(1)}, u32[]{:S(2)}, u32[]{:S(2)}) collective-permute-start(bf16[2,192,128]{2,1,0:T(8,128)(2,1)S(1)} %get-tuple-element.23), channel_id=1, source_target_pairs={{8,0},{16,8},{24,16},{9,1},{17,9},{25,17},{10,2},{18,10},{26,18},{... | collective-permute-start | bytes 294920 | tf_op jit(solution)/shard_map/ppermute | solution.py:244
  14.6 5.7 %collective-permute-start.2 = (bf16[12,48,128]{2,1,0:T(8,128)(2,1)S(1)}, bf16[12,48,128]{2,1,0:T(8,128)(2,1)S(1)}, u32[]{:S(2)}, u32[]{:S(2)}) collective-permute-start(bf16[12,48,128]{2,1,0:T(8,128)(2,1)S(1)} %get-tuple-element.24), channel_id=1, source_target_pairs={{0,2},{2,4},{4,6},{1,3},{3,5},{5,7},{8,10},{10,12},{12,14},{9,11},... | collective-permute-start | bytes 442376 | tf_op jit(solution)/shard_map/ppermute | solution.py:244
  15.9 5.0 %collective-permute-start.3 = (bf16[12,48,128]{2,1,0:T(8,128)(2,1)S(1)}, bf16[12,48,128]{2,1,0:T(8,128)(2,1)S(1)}, u32[]{:S(2)}, u32[]{:S(2)}) collective-permute-start(bf16[12,48,128]{2,1,0:T(8,128)(2,1)S(1)} %get-tuple-element.25), channel_id=1, source_target_pairs={{2,0},{4,2},{6,4},{3,1},{5,3},{7,5},{10,8},{12,10},{14,12},{11,9},... | collective-permute-start | bytes 442376 | tf_op jit(solution)/shard_map/ppermute | solution.py:244
  17.5 3.5 %copy-start.12 = (bf16[2,256,256]{2,1,0:T(8,128)(2,1)S(1)}, bf16[2,256,256]{2,1,0:T(8,128)(2,1)}, u32[]{:S(2)}) copy-start(bf16[2,256,256]{2,1,0:T(8,128)(2,1)} %constant.19.clone.er2) | copy-start | bytes 786436
  17.6 0.8 %copy-start.15 = (bf16[27,16,8]{0,2,1:T(8,128)(2,1)S(1)}, bf16[27,16,8]{0,2,1:T(8,128)(2,1)}, u32[]{:S(2)}) copy-start(bf16[27,16,8]{0,2,1:T(8,128)(2,1)} %param.15) | copy-start | bytes 20740
  18.4 0.8 %copy-start.4 = (f32[128,1]{1,0:T(8,128)S(1)}, f32[128,1]{1,0:T(8,128)}, u32[]{:S(2)}) copy-start(f32[128,1]{1,0:T(8,128)} %constant.23.clone.rows_y.yo) | copy-start | bytes 1540
  18.4 0.9 %copy-start.5 = (bf16[48,640]{1,0:T(8,128)(2,1)S(1)}, bf16[48,640]{1,0:T(8,128)(2,1)}, u32[]{:S(2)}) copy-start(bf16[48,640]{1,0:T(8,128)(2,1)} %constant.17.clone.e2) | copy-start | bytes 184324
  18.4 0.9 %copy-start.6 = (bf16[128,16]{1,0:T(8,128)(2,1)S(1)}, bf16[128,16]{1,0:T(8,128)(2,1)}, u32[]{:S(2)}) copy-start(bf16[128,16]{1,0:T(8,128)(2,1)} %constant.20.clone.expand) | copy-start | bytes 12292
  18.4 0.9 %copy-start.7 = (bf16[24,384]{1,0:T(8,128)(2,1)S(1)}, bf16[24,384]{1,0:T(8,128)(2,1)}, u32[]{:S(2)}) copy-start(bf16[24,384]{1,0:T(8,128)(2,1)} %constant.16.clone.e1) | copy-start | bytes 55300
  18.4 0.9 %copy-start.8 = (f32[1,640]{1,0:T(1,128)S(1)}, f32[1,640]{1,0:T(1,128)}, u32[]{:S(2)}) copy-start(f32[1,640]{1,0:T(1,128)} %constant.22.clone.y2) | copy-start | bytes 7684
  18.4 0.8 %copy-start.9 = (f32[1,384]{1,0:T(1,128)S(1)}, f32[1,384]{1,0:T(1,128)}, u32[]{:S(2)}) copy-start(f32[1,384]{1,0:T(1,128)} %constant.21.clone.y1) | copy-start | bytes 4612
  18.4 0.8 %copy-start.10 = (f32[16]{0:T(128)S(1)}, f32[16]{0:T(128)}, u32[]{:S(2)}) copy-start(f32[16]{0:T(128)} %param.16) | copy-start | bytes 196
  18.6 2.4 %copy-start.1 = (bf16[1,16,8,8,128]{4,3,2,1,0:T(8,128)(2,1)S(1)}, bf16[1,16,8,8,128]{4,3,2,1,0:T(8,128)(2,1)}, u32[]{:S(2)}) copy-start(bf16[1,16,8,8,128]{4,3,2,1,0:T(8,128)(2,1)} %cot.5) | copy-start | bytes 786436
  19.3 1.7 %copy-start.3 = (bf16[1,8,8,8,128]{4,3,2,1,0:T(8,128)(2,1)S(1)}, bf16[1,8,8,8,128]{4,3,2,1,0:T(8,128)(2,1)}, u32[]{:S(2)}) copy-start(bf16[1,8,8,8,128]{4,3,2,1,0:T(8,128)(2,1)} %fields.5) | copy-start | bytes 393220
  19.3 1.7 %copy-start.13 = (bf16[128,128]{1,0:T(8,128)(2,1)S(1)}, bf16[128,128]{1,0:T(8,128)(2,1)}, u32[]{:S(2)}) copy-start(bf16[128,128]{1,0:T(8,128)(2,1)} %constant.18.clone.er1) | copy-start | bytes 98308
  25.1 10.2 %collective-permute-start.10 = (f32[32,384]{1,0:T(8,128)S(1)}, f32[32,384]{1,0:T(8,128)S(1)}, u32[]{:S(2)}, u32[]{:S(2)}) collective-permute-start(f32[32,384]{1,0:T(8,128)S(1)} %get-tuple-element.36), channel_id=1, source_target_pairs={{0,6},{2,4},{4,2},{6,0},{1,7},{3,5},{5,3},{7,1},{8,14},{10,12},{12... | collective-permute-start | bytes 147464 | tf_op jit(solution)/shard_map/ppermute | solution.py:255
  27.5 7.8 %collective-permute-start.8 = (f32[32,384]{1,0:T(8,128)S(1)}, f32[32,384]{1,0:T(8,128)S(1)}, u32[]{:S(2)}, u32[]{:S(2)}) collective-permute-start(f32[32,384]{1,0:T(8,128)S(1)} %get-tuple-element.36), channel_id=1, source_target_pairs={{0,2},{2,0},{4,6},{6,4},{1,3},{3,1},{5,7},{7,5},{8,10},{10,8},{12,... | collective-permute-start | bytes 147464 | tf_op jit(solution)/shard_map/ppermute | solution.py:255
  29.2 6.1 %collective-permute-start.9 = (f32[32,384]{1,0:T(8,128)S(1)}, f32[32,384]{1,0:T(8,128)S(1)}, u32[]{:S(2)}, u32[]{:S(2)}) collective-permute-start(f32[32,384]{1,0:T(8,128)S(1)} %get-tuple-element.36), channel_id=1, source_target_pairs={{0,4},{2,6},{4,0},{6,2},{1,5},{3,7},{5,1},{7,3},{8,12},{10,14},{12... | collective-permute-start | bytes 147464 | tf_op jit(solution)/shard_map/ppermute | solution.py:255
  30.5 10.0 %collective-permute-start.4 = (bf16[2,128,128]{2,1,0:T(8,128)(2,1)S(1)}, bf16[2,128,128]{2,1,0:T(8,128)(2,1)S(1)}, u32[]{:S(2)}, u32[]{:S(2)}) collective-permute-start(bf16[2,128,128]{2,1,0:T(8,128)(2,1)S(1)} %get-tuple-element.30), channel_id=1, source_target_pairs={{0,8},{8,16},{16,24},{1,9},{9,17},{17,25},{2,10},{10,18},{18,26},{... | collective-permute-start | bytes 196616 | tf_op jit(solution)/shard_map/ppermute | solution.py:244
  34.0 6.5 %collective-permute-start.5 = (bf16[2,128,128]{2,1,0:T(8,128)(2,1)S(1)}, bf16[2,128,128]{2,1,0:T(8,128)(2,1)S(1)}, u32[]{:S(2)}, u32[]{:S(2)}) collective-permute-start(bf16[2,128,128]{2,1,0:T(8,128)(2,1)S(1)} %get-tuple-element.31), channel_id=1, source_target_pairs={{8,0},{16,8},{24,16},{9,1},{17,9},{25,17},{10,2},{18,10},{26,18},{... | collective-permute-start | bytes 196616 | tf_op jit(solution)/shard_map/ppermute | solution.py:244
  35.3 8.0 %collective-permute-start.11 = (f32[32,384]{1,0:T(8,128)S(1)}, f32[32,384]{1,0:T(8,128)S(1)}, u32[]{:S(2)}, u32[]{:S(2)}) collective-permute-start(f32[32,384]{1,0:T(8,128)S(1)} %add_add_fusion.1), channel_id=1, source_target_pairs={{0,8},{8,0},{16,24},{24,16},{1,9},{9,1},{17,25},{25,17},{2,10},{10... | collective-permute-start | bytes 147464 | tf_op jit(solution)/shard_map/ppermute | solution.py:255
  38.0 6.3 %collective-permute-start.12 = (f32[32,384]{1,0:T(8,128)S(1)}, f32[32,384]{1,0:T(8,128)S(1)}, u32[]{:S(2)}, u32[]{:S(2)}) collective-permute-start(f32[32,384]{1,0:T(8,128)S(1)} %add_add_fusion.1), channel_id=1, source_target_pairs={{0,16},{8,24},{16,0},{24,8},{1,17},{9,25},{17,1},{25,9},{2,18},{10... | collective-permute-start | bytes 147464 | tf_op jit(solution)/shard_map/ppermute | solution.py:255
  39.1 6.0 %collective-permute-start.13 = (f32[32,384]{1,0:T(8,128)S(1)}, f32[32,384]{1,0:T(8,128)S(1)}, u32[]{:S(2)}, u32[]{:S(2)}) collective-permute-start(f32[32,384]{1,0:T(8,128)S(1)} %add_add_fusion.1), channel_id=1, source_target_pairs={{0,24},{8,16},{16,8},{24,0},{1,25},{9,17},{17,9},{25,1},{2,26},{10... | collective-permute-start | bytes 147464 | tf_op jit(solution)/shard_map/ppermute | solution.py:255
  40.8 9.3 %collective-permute-start.6 = (bf16[12,32,128]{2,1,0:T(8,128)(2,1)S(1)}, bf16[12,32,128]{2,1,0:T(8,128)(2,1)S(1)}, u32[]{:S(2)}, u32[]{:S(2)}) collective-permute-start(bf16[12,32,128]{2,1,0:T(8,128)(2,1)S(1)} %get-tuple-element.32), channel_id=1, source_target_pairs={{0,2},{2,4},{4,6},{1,3},{3,5},{5,7},{8,10},{10,12},{12,14},{9,11},... | collective-permute-start | bytes 294920 | tf_op jit(solution)/shard_map/ppermute | solution.py:244
  42.1 8.0 %collective-permute-start.7 = (bf16[12,32,128]{2,1,0:T(8,128)(2,1)S(1)}, bf16[12,32,128]{2,1,0:T(8,128)(2,1)S(1)}, u32[]{:S(2)}, u32[]{:S(2)}) collective-permute-start(bf16[12,32,128]{2,1,0:T(8,128)(2,1)S(1)} %get-tuple-element.33), channel_id=1, source_target_pairs={{2,0},{4,2},{6,4},{3,1},{5,3},{7,5},{10,8},{12,10},{14,12},{11,9},... | collective-permute-start | bytes 294920 | tf_op jit(solution)/shard_map/ppermute | solution.py:244
  45.2 4.2 %collective-permute-start.14 = (f32[32,384]{1,0:T(8,128)S(1)}, f32[32,384]{1,0:T(8,128)S(1)}, u32[]{:S(2)}, u32[]{:S(2)}) collective-permute-start(f32[32,384]{1,0:T(8,128)S(1)} %add_add_fusion), channel_id=1, source_target_pairs={{0,1},{1,0},{2,3},{3,2},{4,5},{5,4},{6,7},{7,6},{8,9},{9,8},{10,11... | collective-permute-start | bytes 147464 | tf_op jit(solution)/shard_map/ppermute | solution.py:255
  46.9 0.7 %copy-start.11 = (f32[16]{0:T(128)S(1)}, f32[16]{0:T(128)}, u32[]{:S(2)}) copy-start(f32[16]{0:T(128)} %param.18) | copy-start | bytes 196

commit v3 on v2

v3 whole, which is shorter than its diff:
```python
import functools

import numpy as np
import jax
import jax.numpy as jnp
from jax import lax
from jax.experimental import pallas as pl
from jax.experimental.pallas import tpu as pltpu
from jax.sharding import PartitionSpec as P

F32 = jnp.float32
BF16 = jnp.bfloat16
Z = 128
CI = 8
CH = 16
FAR = 100


def block(channels, width):
    own = (np.repeat(np.arange(channels), 8), np.tile(np.arange(8), channels))
    rim_c = np.concatenate([np.repeat(np.arange(channels), width)] * 2)
    rim_y = np.concatenate([np.tile(np.arange(-width, 0), channels), np.tile(np.arange(8, 8 + width), channels)])
    return own, (rim_c, rim_y)


def tables():
    own, rim = block(CI, 4)
    e1 = np.zeros((3 * CI, 384), np.float32)
    y1 = np.full(384, FAR)
    for c in range(3):
        for (ch, y), at in ((own, c * 128), (rim, c * 128 + 64)):
            e1[c * CI + ch, at + np.arange(len(ch))] = 1
            y1[at:at + len(ch)] = y
    own, rim = block(CH, 2)
    e2 = np.zeros((3 * CH, 640), np.float32)
    y2 = np.full(640, FAR)
    for c in range(3):
        for (ch, y), at in ((own, c * 128), (rim, 384 + c * 64)):
            e2[c * CH + ch, at + np.arange(len(ch))] = 1
            y2[at:at + len(ch)] = y
    rows_y = np.concatenate([own[1], rim[1]])
    expand = np.zeros((192, CH), np.float32)
    expand[np.arange(192), np.concatenate([own[0], rim[0]])] = 1
    return e1, y1, e2, y2, rows_y, expand


def plane(ref, x):
    v = ref[0, :, x].astype(F32)
    return v.reshape(v.shape[0] * v.shape[1], v.shape[2])


def pick_rows(channels, width):
    half = channels * width
    row = lax.broadcasted_iota(jnp.int32, (2 * half, channels * 8), 0)
    col = lax.broadcasted_iota(jnp.int32, (2 * half, channels * 8), 1)
    side = jnp.where(row >= half, 1, 0)
    q = row - side * half
    return jnp.where(col == (q // width) * 8 + (8 - width) * side + q % width, 1.0, 0.0).astype(BF16)


def partners(index, count):
    return index % 2 == 0, index > 0, index < count - 1


def sides(index, count, near, far):
    near_above, below, above = partners(index, count)
    low = jnp.where(near_above, far, near).astype(F32)
    high = jnp.where(near_above, near, far).astype(F32)
    return jnp.where(below, low, 0.0), jnp.where(above, high, 0.0)


def pack_kernel(fields, cot, near, far, fields_here, cot_here, sems):
    copies = [
        pltpu.make_async_copy(fields, fields_here, sems.at[0]),
        pltpu.make_async_copy(cot, cot_here, sems.at[1]),
    ]
    for copy in copies:
        copy.start()
    for copy in copies:
        copy.wait()
    up_first = lax.axis_index("stream") % 2 == 0
    count = fields.shape[2]
    for here, width, at, rows in ((fields_here, 4, 0, 64), (cot_here, 2, 256, 128)):
        for n in range(width):
            low, high = plane(here, n), plane(here, count - width + n)
            part = slice(at + n * rows, at + (n + 1) * rows)
            near[part] = jnp.where(up_first, high, low).astype(BF16)
            far[part] = jnp.where(up_first, low, high).astype(BF16)


def x_planes(count, fields, cot, xnear, xfar, size):
    index = lax.axis_index("stream")
    inner = [plane(fields, x) for x in range(count)]
    rims = [sides(index, size, xnear[n * 64:(n + 1) * 64], xfar[n * 64:(n + 1) * 64]) for n in range(4)]
    f = [low for low, _ in rims] + inner + [high for _, high in rims]
    inner = [plane(cot, x) for x in range(count)]
    rims = [sides(index, size, xnear[256 + n * 128:384 + n * 128], xfar[256 + n * 128:384 + n * 128]) for n in range(2)]
    return f, [low for low, _ in rims] + inner + [high for _, high in rims]


def join_kernel(counts, fields, cot, xnear, xfar, near, far):
    up_first = lax.axis_index("radial") % 2 == 0
    f, c = x_planes(fields.shape[2], fields, cot, xnear, xfar, counts[0])
    at = 0
    for rows, pick in ((f, pick_rows(CI, 4)), (c, pick_rows(CH, 2))):
        for v in rows:
            got = jnp.dot(pick, v.astype(BF16), preferred_element_type=F32)
            near[at:at + 32] = jnp.where(up_first, got[32:], got[:32]).astype(BF16)
            far[at:at + 32] = jnp.where(up_first, got[:32], got[32:]).astype(BF16)
            at += 32


def band(w, e, expand, ys, rows_y, t):
    rows, width = t.shape[0], e.shape[1]
    wide = jnp.dot(w[...], e[...], preferred_element_type=F32).astype(BF16)
    for a in range(3):
        total = jnp.zeros((rows, width), F32)
        for b in range(3):
            part = jnp.dot(expand[:rows], wide[(a * 3 + b) * CH:(a * 3 + b + 1) * CH], preferred_element_type=F32)
            total = jnp.where(ys[...] == rows_y[:rows] + float(2 * (b - 1)), part, total)
        t[:, a * width:(a + 1) * width] = total.astype(BF16)


def repeat_bias(bias, expand, out):
    column = jnp.sum(expand[:out.shape[0]].astype(F32) * bias[...], axis=1, keepdims=True)
    out[...] = jnp.broadcast_to(column, out.shape)


def band_first_kernel(w1, wb, bias, e1, e2, expand, y1, y2, rows_y, t1, tb, b1):
    band(w1, e1, expand, y1, rows_y, t1)
    band(wb, e2, expand, y2, rows_y, tb)
    repeat_bias(bias, expand, b1)


def band_second_kernel(w2, bias, e2, expand, y2, rows_y, t2, b2):
    band(w2, e2, expand, y2, rows_y, t2)
    repeat_bias(bias, expand, b2)


def shifted(v):
    lane = lax.broadcasted_iota(jnp.int32, v.shape, 1)
    before = jnp.where(lane >= 2, pltpu.roll(v, 2, 1), 0.0)
    after = jnp.where(lane < Z - 2, pltpu.roll(v, Z - 2, 1), 0.0)
    return before.astype(BF16), v.astype(BF16), after.astype(BF16)


def store_wide(ref, p, v):
    at = slice(p * Z, (p + 1) * Z)
    for c, piece in enumerate(shifted(v)):
        ref[c * 128:(c + 1) * 128, at] = piece[:128]
        ref[384 + c * 64:384 + (c + 1) * 64, at] = piece[128:]
    ref[576:, at] = jnp.zeros((64, Z), BF16)


def stacked(ref, lanes):
    return jnp.concatenate([ref[:, a * 256:a * 256 + lanes] for a in range(3)], axis=0)


def first_kernel(counts, fields, cot, xnear, xfar, rnear, rfar, t1, tb, b1, er1, er2, y1, y2, yo,
                 hidden_out, payload, fs, cs):
    count = fields.shape[2]
    lanes = count * Z
    stream, radial = lax.axis_index("stream"), lax.axis_index("radial")
    f, c = x_planes(count, fields, cot, xnear, xfar, counts[0])
    at = 0
    for p, v in enumerate(f):
        low, high = sides(radial, counts[1], rnear[at:at + 32], rfar[at:at + 32])
        for n, piece in enumerate(shifted(jnp.concatenate([v, low, high], axis=0))):
            fs[n * 128:(n + 1) * 128, p * Z:(p + 1) * Z] = piece
        at += 32
    for p, v in enumerate(c):
        low, high = sides(radial, counts[1], rnear[at:at + 32], rfar[at:at + 32])
        store_wide(cs, p, jnp.concatenate([v, low, high], axis=0))
        at += 32
    pre = jnp.dot(t1[...], stacked(fs, lanes + 4 * Z), preferred_element_type=F32) + b1[...]
    share = 0.5 * (1.0 + lax.erf(pre * 0.7071067811865476))
    hidden = (pre * share).astype(BF16)
    zero = jnp.zeros((), BF16)
    rims = (jnp.where(radial > 0, hidden[128:160], zero), jnp.where(radial < counts[1] - 1, hidden[160:], zero))
    for p in range(count + 4):
        at = slice(p * Z, (p + 1) * Z)
        rows = jnp.concatenate([hidden[:128, at], rims[0][:, at], rims[1][:, at]], axis=0)
        if p < 2:
            rows = jnp.where(stream > 0, rows, zero)
        elif p >= count + 2:
            rows = jnp.where(stream < counts[0] - 1, rows, zero)
        hidden_out[p] = rows
    at = slice(2 * Z, 2 * Z + lanes)
    pre, share, hidden = pre[:128, at], share[:128, at], hidden[:128, at]
    back = jnp.dot(tb[...], stacked(cs, lanes), preferred_element_type=F32)
    dpre = (back * (share + pre * jnp.exp(-0.5 * pre * pre) * 0.3989422804014327)).astype(BF16)
    bias = jnp.sum(dpre.astype(F32), axis=1, keepdims=True)
    lane = lax.broadcasted_iota(jnp.int32, (8, 256), 1)

    def diagonal(rows, place):
        total = jnp.zeros((8, rows.shape[1]), F32)
        for o in range(CH):
            total = jnp.where(place == o, rows[o * 8:(o + 1) * 8], total)
        return jnp.sum(total, axis=0, keepdims=True)

    payload[...] = jnp.zeros(payload.shape, F32)
    payload[27, :1] = diagonal(jnp.broadcast_to(bias, (128, 128)), lane[:, :128])
    over_lanes = (((1,), (1,)), ((), ()))
    for a in range(3):
        g1 = lax.dot_general(dpre, fs[:, (a + 1) * 256:(a + 1) * 256 + lanes], over_lanes, preferred_element_type=F32)
        g2 = lax.dot_general(hidden, cs[:, a * 256:a * 256 + lanes], over_lanes, preferred_element_type=F32)
        for b in range(3):
            off = float(2 * (b - 1))
            one = jnp.where(y1[...] == yo[...] + off, g1, 0.0).astype(BF16)
            two = jnp.where(y2[...] == yo[...] + off, g2, 0.0).astype(BF16)
            for c in range(3):
                tap = (a * 3 + b) * 3 + c
                r1 = jnp.dot(one[:, c * 128:(c + 1) * 128], er1[...], preferred_element_type=F32)
                rim = 384 + (c // 2) * 128
                both = jnp.concatenate([two[:, c * 128:(c + 1) * 128], two[:, rim:rim + 128]], axis=1)
                r2 = jnp.dot(both, er2[c % 2], preferred_element_type=F32)
                payload[tap, :1] = diagonal(r1, lane[:, :128] // CI)
                second = diagonal(r2, lane % CH)
                payload[26 - tap, 1:2] = second[:, :128]
                payload[26 - tap, 2:3] = second[:, 128:]


def closure_kernel(hidden, t2, b2, closure, hs):
    count = closure.shape[2]
    for p in range(count + 4):
        store_wide(hs, p, hidden[p].astype(F32))
    out = (jnp.dot(t2[...], stacked(hs, count * Z), preferred_element_type=F32) + b2[...]).astype(BF16)
    for x in range(count):
        closure[0, :, x] = out[:, x * Z:(x + 1) * Z].reshape(CH, 8, Z)


def add_kernel(parts, total):
    acc = parts[0]
    for d in range(1, parts.shape[0]):
        acc = acc + parts[d]
    for d in range(total.shape[0]):
        total[d] = acc


def finish_kernel(norm, total, first, second, bias):
    parts = [total[:, n] * norm for n in range(3)]
    first[...] = jnp.transpose(parts[0])[:, :27]
    second[:128] = jnp.transpose(parts[1])[:, :27]
    second[128:] = jnp.transpose(parts[2])[:, :27]
    bias[...] = parts[0][27:28, :CH]


def call(kernel, outs, name, scratch=(), flops=10_000_000, **specs):
    return pl.pallas_call(
        kernel,
        out_shape=outs,
        **specs,
        scratch_shapes=list(scratch),
        compiler_params=pltpu.CompilerParams(vmem_limit_bytes=48 * 1024 * 1024),
        cost_estimate=pl.CostEstimate(flops=flops, bytes_accessed=1_000_000, transcendentals=0),
        name=name,
    )


def shape(*dims, dtype=BF16):
    return jax.ShapeDtypeStruct(dims, dtype)


def exchange(near, far, axis):
    count = lax.axis_size(axis)
    shifted_pairs = [(i, min(max(i - 1 + 2 * (i % 2), 0), count - 1)) for i in range(count)]
    return lax.ppermute(near, axis, [(i, i ^ 1) for i in range(count)]), lax.ppermute(far, axis, shifted_pairs)


def reduce_all(v, axes):
    devices = 1
    for axis in axes:
        devices *= lax.axis_size(axis)
    rows = v.reshape(devices, -1, *v.shape[-1:]) if v.size // v.shape[-1] % devices == 0 else v.reshape(devices, 1, -1)
    mine = lax.all_to_all(rows, axes, 0, 0, tiled=True)
    mine = call(add_kernel, shape(*rows.shape, dtype=F32), "add_rows")(mine)
    return lax.all_to_all(mine, axes, 0, 0, tiled=True).reshape(v.shape)


def local(fields, first_weight, first_bias, second_weight, second_bias, cotangent):
    e1, y1, e2, y2, rows_y, expand = tables()
    er1 = np.tile(e1[:CI, :128].T, (1, CH))
    er2 = np.zeros((2, 256, 256), np.float32)
    for half in range(2):
        er2[half, :128] = np.repeat(e2[:CH, :128].T, CH, axis=1)
        er2[half, 128 + half * 64:192 + half * 64] = np.repeat(e2[:CH, 384:448].T, CH, axis=1)
    e1, e2, er1, er2, expand = (jnp.asarray(v, BF16) for v in (e1, e2, er1, er2, expand))
    y1, y2, rows_y = (jnp.asarray(v, F32) for v in (y1[None], y2[None], rows_y[:, None]))
    planes = fields.shape[2]
    near, far = call(
        pack_kernel,
        (shape(512, Z),) * 2,
        "pack_strips",
        (pltpu.VMEM(fields.shape, BF16), pltpu.VMEM(cotangent.shape, BF16), pltpu.SemaphoreType.DMA((2,))),
        in_specs=[pl.BlockSpec(memory_space=pltpu.HBM)] * 2,
    )(fields, cotangent)
    xnear, xfar = exchange(near, far, "stream")

    w1 = first_weight.reshape(3, 3, 3, CH, CI).transpose(0, 1, 3, 2, 4).reshape(9 * CH, 3 * CI)
    w2 = second_weight.reshape(3, 3, 3, CH, CH)
    wb = w2[::-1, ::-1, ::-1].transpose(0, 1, 4, 2, 3).reshape(9 * CH, 3 * CH)
    w2 = w2.transpose(0, 1, 3, 2, 4).reshape(9 * CH, 3 * CH)
    wide = (planes + 4) * Z
    t1, tb, b1 = call(
        band_first_kernel, (shape(192, 1152), shape(128, 1920), shape(192, wide, dtype=F32)), "band_first"
    )(w1, wb, first_bias[None], e1, e2, expand, y1, y2, rows_y)

    counts = (lax.axis_size("stream"), lax.axis_size("radial"))
    near, far = call(functools.partial(join_kernel, counts), (shape((2 * planes + 12) * 32, Z),) * 2, "join_strips")(
        fields, cotangent, xnear, xfar)
    rnear, rfar = exchange(near, far, "radial")
    hidden, payload = call(
        functools.partial(first_kernel, counts),
        (shape(planes + 4, 192, Z), shape(32, 4, 128, dtype=F32)),
        "gradients",
        (pltpu.VMEM((384, wide + 4 * Z), BF16), pltpu.VMEM((640, wide), BF16)),
        flops=2_000_000_000,
    )(fields, cotangent, xnear, xfar, rnear, rfar, t1, tb, b1, er1, er2, y1, y2, rows_y[:128])
    total = reduce_all(payload, ("stream", "radial", "snap"))

    t2, b2 = call(band_second_kernel, (shape(128, 1920), shape(128, planes * Z, dtype=F32)), "band_second")(
        w2, second_bias[None], e2, expand, y2, rows_y)
    closure = call(
        closure_kernel, shape(*cotangent.shape), "closure", (pltpu.VMEM((640, wide), BF16),), flops=1_000_000_000
    )(hidden, t2, b2)

    cells = fields.shape[0] * fields.shape[2] * fields.shape[3] * fields.shape[4]
    for axis in ("stream", "radial", "snap"):
        cells *= lax.axis_size(axis)
    norm = float(1.0 / np.sqrt(np.float32(cells)))
    first, second, bias = call(
        functools.partial(finish_kernel, norm),
        (shape(CH * CI, 27, dtype=F32), shape(CH * CH, 27, dtype=F32), shape(1, CH, dtype=F32)),
        "finish",
    )(total)
    first = first.reshape(CH, CI, 27).transpose(2, 0, 1)
    second = second.reshape(CH, CH, 27).transpose(2, 0, 1)
    return (closure, first, second, bias[0])


def solution(mesh):
    split = P("snap", None, "stream", "radial", None)
    return jax.shard_map(
        local,
        mesh=mesh,
        in_specs=(split, P(), P(), P(), P(), split),
        out_specs=(split, P(), P(), P()),
        check_vma=False,
    )
```

time: 52.1 us -> 49.6 us (0.952)
  starting transfers between devices: 28.4 us -> 7.06 us
  blocking collectives: 0 us -> 19.2 us
  Pallas kernels: 8.99 us -> 10.2 us
  local copies, waits for them, and re-layouts: 4.63 us -> 3.82 us
  waiting for transfers between devices: 8.66 us -> 7.97 us
    ppermute x15 -> x4, starting transfers between devices: 28.4 us -> 4.49 us  [the longest x2 3.16 us: exchange(): lax.ppermute(near, axis, [(i, i ^ 1) for i in range(count)])]
    all_to_all x0 -> x1, blocking collectives: none -> 19.2 us  [reduce_all(): mine = lax.all_to_all(rows, axes, 0, 0, tiled=True)]
    ppermute x15 -> x4, waiting for transfers between devices: 8.66 us -> 2.84 us  [the longest x2 2.83 us: exchange(): lax.ppermute(near, axis, [(i, i ^ 1) for i in range(count)])]
    all_to_all x0 -> x1, waiting for transfers between devices: none -> 5.13 us  [reduce_all(): return lax.all_to_all(mine, axes, 0, 0, tiled=True).reshape(v.shape)]
    all_to_all x0 -> x1, starting transfers between devices: none -> 2.57 us  [reduce_all(): return lax.all_to_all(mine, axes, 0, 0, tiled=True).reshape(v.shape)]
    pallas_call x6, Pallas kernels: 6.61 us -> 7.85 us  [the longest x1 4.75 us: local(): call(functools.partial(first_kernel, counts), (shape(planes + 4, 192, Z),...]
    unnamed x34, local copies, waits for them, and re-layouts: 3.92 us -> 3.11 us
  transfers between devices with their start and end apart: 15 -> 5, of which waited for: 6 -> 2; matrix products, arithmetic and copies ran while one was open for 2% -> 4% of each run, Pallas kernels for 5% -> 7%
where the time goes in v3:
time: 49.6 us; the launch traced here: 49.3 us
  blocking collectives  19.2 us (39%)
  Pallas kernels  10.2 us (21%)
  waiting for transfers between devices  7.97 us (16%)
  starting transfers between devices  7.06 us (14%)
  local copies, waits for them, and re-layouts  3.82 us (8%)
  between operations  0.96 us (2%)
    all_to_all x1, blocking collectives, reduce_all(): mine = lax.all_to_all(rows, axes, 0, 0, tiled=True)  19.2 us
    all_to_all x1, waiting for transfers between devices, reduce_all(): return lax.all_to_all(mine, axes, 0, 0, tiled=True).reshape(v.shape)  5.13 us
    pallas_call x1, Pallas kernels, local(): call(functools.partial(first_kernel, counts), (shape(planes + 4, 192, Z),...  4.75 us
    ppermute x2, starting transfers between devices, exchange(): lax.ppermute(near, axis, [(i, i ^ 1) for i in range(count)])  3.16 us
    unnamed x34, local copies, waits for them, and re-layouts  3.11 us
    ppermute x2, waiting for transfers between devices, exchange(): lax.ppermute(near, axis, [(i, i ^ 1) for i in range(count)])  2.83 us
    all_to_all x1, starting transfers between devices, reduce_all(): return lax.all_to_all(mine, axes, 0, 0, tiled=True).reshape(v.shape)  2.57 us
    pallas_call x1, Pallas kernels, local(): call(closure_kernel, shape(*cotangent.shape), 'closure', (pltpu.VMEM((640...  1.58 us
  transfers between devices with their start and end apart: 5, of which 2 were waited for; matrix products, arithmetic and copies ran while one was open for 4% of the time, Pallas kernels for 7%

profile of v3, /device:TPU:0, one launch (start us, length us, event | category | flops | bytes accessed | tf_op | source)
XLA Modules:
  0.0 49.3 jit_solution(6094704464505771172)
XLA Ops:
  0.6 0.0 copy-start.9
  0.6 0.0 copy-start.8
  0.7 0.0 copy-start
  0.7 0.9 %copy-done = bf16[1,16,8,8,128]{4,3,2,1,0:T(8,128)(2,1)S(1)} copy-done((bf16[1,16,8,8,128]{4,3,2,1,0:T(8,128)(2,1)S(1)}, bf16[1,16,8,8,128]{4,3,2,1,0:T(8,128)(2,1)}, u32[]{:S(2)}) %copy-start) | copy-done | bytes 262168
  1.6 0.0 copy-start.2
  1.6 0.9 %copy-done.2 = bf16[1,8,8,8,128]{4,3,2,1,0:T(8,128)(2,1)S(1)} copy-done((bf16[1,8,8,8,128]{4,3,2,1,0:T(8,128)(2,1)S(1)}, bf16[1,8,8,8,128]{4,3,2,1,0:T(8,128)(2,1)}, u32[]{:S(2)}) %copy-start.2) | copy-done | bytes 131096
  2.5 0.0 copy-start.15
  2.5 0.0 copy-start.4
  2.5 0.0 copy-start.5
  2.5 0.0 copy-start.6
  2.5 0.0 copy-start.7
  2.5 0.0 copy-start.10
  2.6 0.3 pack_strips.1
  2.8 0.0 copy-start.1
  2.8 0.0 copy-start.3
  2.8 0.0 copy-start.12
  2.9 0.0 copy-start.13
  2.9 0.0 copy-start.14
  2.9 3.1 %collective-permute-start = (bf16[512,128]{1,0:T(8,128)(2,1)S(1)}, bf16[512,128]{1,0:T(8,128)(2,1)S(1)}, u32[]{:S(2)}, u32[]{:S(2)}) collective-permute-start(bf16[512,128]{1,0:T(8,128)(2,1)S(1)} %get-tuple-element.18), channel_id=1, source_target_pairs={{0,8},{8,0},{16,24},{24,16},{1,9},{9,1},{17,25},{25,17},{2,10},{10... | collective-permute-start | bytes 393224 | tf_op jit(solution)/shard_map/ppermute | solution.py:267
  6.0 0.7 %collective-permute-start.1 = (bf16[512,128]{1,0:T(8,128)(2,1)S(1)}, bf16[512,128]{1,0:T(8,128)(2,1)S(1)}, u32[]{:S(2)}, u32[]{:S(2)}) collective-permute-start(bf16[512,128]{1,0:T(8,128)(2,1)S(1)} %get-tuple-element.19), channel_id=1, source_target_pairs={{0,0},{8,16},{16,8},{24,24},{1,1},{9,17},{17,9},{25,25},{2,2},{10,... | collective-permute-start | bytes 393224 | tf_op jit(solution)/shard_map/ppermute | solution.py:267
  6.6 2.8 %collective-permute-done.xnear = bf16[512,128]{1,0:T(8,128)(2,1)S(1)} collective-permute-done((bf16[512,128]{1,0:T(8,128)(2,1)S(1)}, bf16[512,128]{1,0:T(8,128)(2,1)S(1)}, u32[]{:S(2)}, u32[]{:S(2)}) %collective-permute-start) | collective-permute-done | bytes 131104 | tf_op jit(solution)/shard_map/ppermute | solution.py:267
  9.5 0.0 collective-permute-done.1.xfar
  9.5 0.3 join_strips.1
  9.8 0.1 collective-permute-start.2
  9.9 0.7 %collective-permute-start.3 = (bf16[896,128]{1,0:T(8,128)(2,1)S(1)}, bf16[896,128]{1,0:T(8,128)(2,1)S(1)}, u32[]{:S(2)}, u32[]{:S(2)}) collective-permute-start(bf16[896,128]{1,0:T(8,128)(2,1)S(1)} %get-tuple-element.21), channel_id=1, source_target_pairs={{0,0},{2,4},{4,2},{6,6},{1,1},{3,5},{5,3},{7,7},{8,8},{10,12},{12,... | collective-permute-start | bytes 688136 | tf_op jit(solution)/shard_map/ppermute | solution.py:267
  10.6 1.0 %copy.23 = bf16[27,16,16]{2,1,0:T(8,128)(2,1)S(1)} copy(bf16[27,16,16]{0,2,1:T(8,128)(2,1)} %param.17) | data formatting | bytes 27648 | tf_op args[3]
  11.6 0.1 copy.29
  11.8 0.1 reshape.36.wb
  11.9 0.0 copy-done.15
  11.9 0.1 copy.21
  12.1 0.1 reshape.30
  12.2 0.1 copy.25.w1
  12.3 0.0 copy-done.9
  12.3 0.0 copy-done.8
  12.3 0.0 copy-done.4
  12.3 0.0 copy-done.5
  12.4 0.0 copy-done.6
  12.4 0.0 copy-done.7
  12.4 0.0 copy-done.10
  12.4 1.2 %band_first.1 = (bf16[192,1152]{1,0:T(8,128)(2,1)S(1)}, bf16[128,1920]{1,0:T(8,128)(2,1)S(1)}, f32[192,1536]{1,0:T(8,128)S(1)}) custom-call(bf16[144,24]{1,0:T(8,128)(2,1)S(1)} %copy.25.w1, bf16[144,48]{1,0:T(8,128)(2,1)S(1)} %reshape.36.wb, f32[1,16]{1,0:T(1,128)S(1)} %bitcast.19, bf16[24,384]{1,0:T(8,128)(2,1)S(1)} %copy-done.7, ...), custom_call_target="tpu_custom_call" | custom-call | flops 10000000 | bytes 1000000 | tf_op jit(solution)/shard_map/band_first/pallas_call | solution.py:304
  13.5 0.0 collective-permute-done.2.rnear
  13.6 0.0 collective-permute-done.3.rfar
  13.6 0.0 copy-done.1
  13.6 0.0 copy-done.3
  13.6 0.0 copy-done.12
  13.6 0.0 copy-done.13
  13.6 0.0 copy-done.14
  13.6 0.0 copy-start.11
  13.6 4.7 %gradients.1 = (bf16[12,192,128]{2,1,0:T(8,128)(2,1)S(1)}, f32[32,4,128]{2,1,0:T(4,128)S(1)}) custom-call(bf16[1,8,8,8,128]{4,3,2,1,0:T(8,128)(2,1)S(1)} %copy-done.3, bf16[1,16,8,8,128]{4,3,2,1,0:T(8,128)(2,1)S(1)} %copy-done.1, bf16[512,128]{1,0:T(8,128)(2,1)S(1)} %collective-permute-done.xnear, bf16[512,128]{1,0:T(8,128)(2,1)S(1)} %collective-permute-done.1.xfar, ...), custom_call_target="tpu_custom_call" | custom-call | flops 2000000000 | bytes 1000000 | tf_op jit(solution)/shard_map/gradients/pallas_call | solution.py:312
  18.4 19.2 %all_to_all.10.parts = f32[32,4,128]{2,1,0:T(4,128)S(1)} all-to-all(f32[32,4,128]{2,1,0:T(4,128)S(1)} %get-tuple-element.28), channel_id=1, replica_groups=mesh['stream'=4,'radial'=4,'snap'=2] {'stream','radial','snap'}, dimensions={0} | all-to-all | bytes 131072 | tf_op jit(solution)/shard_map/all_to_all | solution.py:275
  37.6 0.7 %add_rows.1 = f32[32,4,128]{2,1,0:T(4,128)} custom-call(f32[32,4,128]{2,1,0:T(4,128)S(1)} %all_to_all.10.parts), custom_call_target="tpu_custom_call" | custom-call | flops 10000000 | bytes 1000000 | tf_op jit(solution)/shard_map/add_rows/pallas_call | solution.py:276
  38.3 2.6 %all-to-all-start.1 = ((f32[32,4,128]{2,1,0:T(4,128)}), f32[32,4,128]{2,1,0:T(4,128)S(1)}, u32[]{:S(2)}, u32[]{:S(2)}) async-start(f32[32,4,128]{2,1,0:T(4,128)} %add_rows.1), calls=%async_computation.1 | async-start | bytes 131072 | tf_op jit(solution)/shard_map/all_to_all | solution.py:277
  40.9 0.1 copy.30
  40.9 0.1 reshape.37.w2
  41.1 0.0 copy-done.11
  41.1 0.7 %band_second.1 = (bf16[128,1920]{1,0:T(8,128)(2,1)S(1)}, f32[128,1024]{1,0:T(8,128)S(1)}) custom-call(bf16[144,48]{1,0:T(8,128)(2,1)S(1)} %reshape.37.w2, f32[1,16]{1,0:T(1,128)S(1)} %bitcast.20, bf16[48,640]{1,0:T(8,128)(2,1)S(1)} %copy-done.5, bf16[192,16]{1,0:T(8,128)(2,1)S(1)} %copy-done.6, f32[1,640]{1,0:T(1,128)S(1)} %copy-done.8, f32[192,1]{1,0:T(8,128)S(1)} %copy-done.4), custom_call_target="tpu_custom_call" | custom-call | flops 10000000 | bytes 1000000 | tf_op jit(solution)/shard_map/band_second/pallas_call | solution.py:321
  41.8 1.6 %closure.1 = bf16[1,16,8,8,128]{4,3,2,1,0:T(8,128)(2,1)} custom-call(bf16[12,192,128]{2,1,0:T(8,128)(2,1)S(1)} %get-tuple-element.25.hidden, bf16[128,1920]{1,0:T(8,128)(2,1)S(1)} %get-tuple-element.26.t2, f32[128,1024]{1,0:T(8,128)S(1)} %get-tuple-element.27.b2), custom_call_target="tpu_custom_call" | custom-call | flops 1000000000 | bytes 1000000 | tf_op jit(solution)/shard_map/closure/pallas_call | solution.py:323
  43.4 5.1 %all-to-all-done.1.total = f32[32,4,128]{2,1,0:T(4,128)S(1)} async-done(((f32[32,4,128]{2,1,0:T(4,128)}), f32[32,4,128]{2,1,0:T(4,128)S(1)}, u32[]{:S(2)}, u32[]{:S(2)}) %all-to-all-start.1) | async-done | bytes 65568 | tf_op jit(solution)/shard_map/all_to_all | solution.py:277
  48.5 0.8 %finish.1 = (f32[128,27]{1,0:T(8,128)}, f32[256,27]{1,0:T(8,128)}, f32[1,16]{1,0:T(1,128)}) custom-call(f32[32,4,128]{2,1,0:T(4,128)S(1)} %all-to-all-done.1.total), custom_call_target="tpu_custom_call" | custom-call | flops 10000000 | bytes 1000000 | tf_op jit(solution)/shard_map/finish/pallas_call | solution.py:331
  (2 shorter events, 0.0 us)
Async XLA Ops:
  0.6 11.7 %copy-start.9 = (f32[1,384]{1,0:T(1,128)S(1)}, f32[1,384]{1,0:T(1,128)}, u32[]{:S(2)}) copy-start(f32[1,384]{1,0:T(1,128)} %constant.21.clone.y1) | copy-start | bytes 4612
  0.6 11.7 %copy-start.8 = (f32[1,640]{1,0:T(1,128)S(1)}, f32[1,640]{1,0:T(1,128)}, u32[]{:S(2)}) copy-start(f32[1,640]{1,0:T(1,128)} %constant.22.clone.y2) | copy-start | bytes 7684
  0.7 1.0 %copy-start = (bf16[1,16,8,8,128]{4,3,2,1,0:T(8,128)(2,1)S(1)}, bf16[1,16,8,8,128]{4,3,2,1,0:T(8,128)(2,1)}, u32[]{:S(2)}) copy-start(bf16[1,16,8,8,128]{4,3,2,1,0:T(8,128)(2,1)} %cot.5) | copy-start | bytes 786436
  1.6 0.9 %copy-start.2 = (bf16[1,8,8,8,128]{4,3,2,1,0:T(8,128)(2,1)S(1)}, bf16[1,8,8,8,128]{4,3,2,1,0:T(8,128)(2,1)}, u32[]{:S(2)}) copy-start(bf16[1,8,8,8,128]{4,3,2,1,0:T(8,128)(2,1)} %fields.5) | copy-start | bytes 393220
  2.5 9.4 %copy-start.15 = (bf16[27,16,8]{0,2,1:T(8,128)(2,1)S(1)}, bf16[27,16,8]{0,2,1:T(8,128)(2,1)}, u32[]{:S(2)}) copy-start(bf16[27,16,8]{0,2,1:T(8,128)(2,1)} %param.15) | copy-start | bytes 20740
  2.5 9.8 %copy-start.4 = (f32[192,1]{1,0:T(8,128)S(1)}, f32[192,1]{1,0:T(8,128)}, u32[]{:S(2)}) copy-start(f32[192,1]{1,0:T(8,128)} %constant.23.clone.rows_y) | copy-start | bytes 2308
  2.5 9.8 %copy-start.5 = (bf16[48,640]{1,0:T(8,128)(2,1)S(1)}, bf16[48,640]{1,0:T(8,128)(2,1)}, u32[]{:S(2)}) copy-start(bf16[48,640]{1,0:T(8,128)(2,1)} %constant.17.clone.e2) | copy-start | bytes 184324
  2.5 9.8 %copy-start.6 = (bf16[192,16]{1,0:T(8,128)(2,1)S(1)}, bf16[192,16]{1,0:T(8,128)(2,1)}, u32[]{:S(2)}) copy-start(bf16[192,16]{1,0:T(8,128)(2,1)} %constant.20.clone.expand) | copy-start | bytes 18436
  2.5 9.8 %copy-start.7 = (bf16[24,384]{1,0:T(8,128)(2,1)S(1)}, bf16[24,384]{1,0:T(8,128)(2,1)}, u32[]{:S(2)}) copy-start(bf16[24,384]{1,0:T(8,128)(2,1)} %constant.16.clone.e1) | copy-start | bytes 55300
  2.5 9.8 %copy-start.10 = (f32[16]{0:T(128)S(1)}, f32[16]{0:T(128)}, u32[]{:S(2)}) copy-start(f32[16]{0:T(128)} %param.16) | copy-start | bytes 196
  2.8 10.7 %copy-start.1 = (bf16[1,16,8,8,128]{4,3,2,1,0:T(8,128)(2,1)S(1)}, bf16[1,16,8,8,128]{4,3,2,1,0:T(8,128)(2,1)}, u32[]{:S(2)}) copy-start(bf16[1,16,8,8,128]{4,3,2,1,0:T(8,128)(2,1)} %cot.5) | copy-start | bytes 786436
  2.8 10.7 %copy-start.3 = (bf16[1,8,8,8,128]{4,3,2,1,0:T(8,128)(2,1)S(1)}, bf16[1,8,8,8,128]{4,3,2,1,0:T(8,128)(2,1)}, u32[]{:S(2)}) copy-start(bf16[1,8,8,8,128]{4,3,2,1,0:T(8,128)(2,1)} %fields.5) | copy-start | bytes 393220
  2.8 10.7 %copy-start.12 = (bf16[2,256,256]{2,1,0:T(8,128)(2,1)S(1)}, bf16[2,256,256]{2,1,0:T(8,128)(2,1)}, u32[]{:S(2)}) copy-start(bf16[2,256,256]{2,1,0:T(8,128)(2,1)} %constant.19.clone.er2) | copy-start | bytes 786436
  2.9 10.7 %copy-start.13 = (f32[128,1]{1,0:T(8,128)S(1)}, f32[128,1]{1,0:T(8,128)}, u32[]{:S(2)}) copy-start(f32[128,1]{1,0:T(8,128)} %constant.26.yo) | copy-start | bytes 1540
  2.9 10.7 %copy-start.14 = (bf16[128,128]{1,0:T(8,128)(2,1)S(1)}, bf16[128,128]{1,0:T(8,128)(2,1)}, u32[]{:S(2)}) copy-start(bf16[128,128]{1,0:T(8,128)(2,1)} %constant.18.clone.er1) | copy-start | bytes 98308
  2.9 6.6 %collective-permute-start = (bf16[512,128]{1,0:T(8,128)(2,1)S(1)}, bf16[512,128]{1,0:T(8,128)(2,1)S(1)}, u32[]{:S(2)}, u32[]{:S(2)}) collective-permute-start(bf16[512,128]{1,0:T(8,128)(2,1)S(1)} %get-tuple-element.18), channel_id=1, source_target_pairs={{0,8},{8,0},{16,24},{24,16},{1,9},{9,1},{17,25},{25,17},{2,10},{10... | collective-permute-start | bytes 393224 | tf_op jit(solution)/shard_map/ppermute | solution.py:267
  6.0 3.5 %collective-permute-start.1 = (bf16[512,128]{1,0:T(8,128)(2,1)S(1)}, bf16[512,128]{1,0:T(8,128)(2,1)S(1)}, u32[]{:S(2)}, u32[]{:S(2)}) collective-permute-start(bf16[512,128]{1,0:T(8,128)(2,1)S(1)} %get-tuple-element.19), channel_id=1, source_target_pairs={{0,0},{8,16},{16,8},{24,24},{1,1},{9,17},{17,9},{25,25},{2,2},{10,... | collective-permute-start | bytes 393224 | tf_op jit(solution)/shard_map/ppermute | solution.py:267
  9.8 3.7 %collective-permute-start.2 = (bf16[896,128]{1,0:T(8,128)(2,1)S(1)}, bf16[896,128]{1,0:T(8,128)(2,1)S(1)}, u32[]{:S(2)}, u32[]{:S(2)}) collective-permute-start(bf16[896,128]{1,0:T(8,128)(2,1)S(1)} %get-tuple-element.20), channel_id=1, source_target_pairs={{0,2},{2,0},{4,6},{6,4},{1,3},{3,1},{5,7},{7,5},{8,10},{10,8},{12,... | collective-permute-start | bytes 688136 | tf_op jit(solution)/shard_map/ppermute | solution.py:267
  9.9 3.7 %collective-permute-start.3 = (bf16[896,128]{1,0:T(8,128)(2,1)S(1)}, bf16[896,128]{1,0:T(8,128)(2,1)S(1)}, u32[]{:S(2)}, u32[]{:S(2)}) collective-permute-start(bf16[896,128]{1,0:T(8,128)(2,1)S(1)} %get-tuple-element.21), channel_id=1, source_target_pairs={{0,0},{2,4},{4,2},{6,6},{1,1},{3,5},{5,3},{7,7},{8,8},{10,12},{12,... | collective-permute-start | bytes 688136 | tf_op jit(solution)/shard_map/ppermute | solution.py:267
  13.6 27.5 %copy-start.11 = (f32[16]{0:T(128)S(1)}, f32[16]{0:T(128)}, u32[]{:S(2)}) copy-start(f32[16]{0:T(128)} %param.18) | copy-start | bytes 196
  38.3 10.2 %all-to-all-start.1 = ((f32[32,4,128]{2,1,0:T(4,128)}), f32[32,4,128]{2,1,0:T(4,128)S(1)}, u32[]{:S(2)}, u32[]{:S(2)}) async-start(f32[32,4,128]{2,1,0:T(4,128)} %add_rows.1), calls=%async_computation.1 | async-start | bytes 131072 | tf_op jit(solution)/shard_map/all_to_all | solution.py:277

commit v4 on v3

--- a/solution.py
+++ b/solution.py
@@ -198,8 +198,8 @@
             total = jnp.where(place == o, rows[o * 8:(o + 1) * 8], total)
         return jnp.sum(total, axis=0, keepdims=True)
 
-    payload[...] = jnp.zeros(payload.shape, F32)
-    payload[27, :1] = diagonal(jnp.broadcast_to(bias, (128, 128)), lane[:, :128])
+    ones, twos = [None] * 32, [None] * 32
+    ones[27] = diagonal(jnp.broadcast_to(bias, (128, 128)), lane[:, :128])
     over_lanes = (((1,), (1,)), ((), ()))
     for a in range(3):
         g1 = lax.dot_general(dpre, fs[:, (a + 1) * 256:(a + 1) * 256 + lanes], over_lanes, preferred_element_type=F32)
@@ -214,10 +214,11 @@
                 rim = 384 + (c // 2) * 128
                 both = jnp.concatenate([two[:, c * 128:(c + 1) * 128], two[:, rim:rim + 128]], axis=1)
                 r2 = jnp.dot(both, er2[c % 2], preferred_element_type=F32)
-                payload[tap, :1] = diagonal(r1, lane[:, :128] // CI)
-                second = diagonal(r2, lane % CH)
-                payload[26 - tap, 1:2] = second[:, :128]
-                payload[26 - tap, 2:3] = second[:, 128:]
+                ones[tap] = diagonal(r1, lane[:, :128] // CI)
+                twos[26 - tap] = diagonal(r2, lane % CH)
+    for rows, at, width in ((ones, 0, 128), (twos, 128, 256)):
+        rows = [jnp.zeros((1, width), F32) if v is None else v for v in rows]
+        payload[:, at:at + width] = jnp.concatenate(rows, axis=0).astype(BF16)
 
 
 def closure_kernel(hidden, t2, b2, closure, hs):
@@ -229,20 +230,12 @@
         closure[0, :, x] = out[:, x * Z:(x + 1) * Z].reshape(CH, 8, Z)
 
 
-def add_kernel(parts, total):
-    acc = parts[0]
-    for d in range(1, parts.shape[0]):
-        acc = acc + parts[d]
-    for d in range(total.shape[0]):
-        total[d] = acc
-
-
-def finish_kernel(norm, total, first, second, bias):
-    parts = [total[:, n] * norm for n in range(3)]
-    first[...] = jnp.transpose(parts[0])[:, :27]
-    second[:128] = jnp.transpose(parts[1])[:, :27]
-    second[128:] = jnp.transpose(parts[2])[:, :27]
-    bias[...] = parts[0][27:28, :CH]
+def finish_kernel(norm, total, last, first, second, bias):
+    scaled = (total[...].astype(F32) + last[...].astype(F32)) * norm
+    flipped = jnp.transpose(scaled)
+    first[...] = flipped[:128, :27]
+    second[...] = flipped[128:, :27]
+    bias[...] = scaled[27:28, :CH]
 
 
 def call(kernel, outs, name, scratch=(), flops=10_000_000, **specs):
@@ -267,14 +260,12 @@
     return lax.ppermute(near, axis, [(i, i ^ 1) for i in range(count)]), lax.ppermute(far, axis, shifted_pairs)
 
 
-def reduce_all(v, axes):
-    devices = 1
-    for axis in axes:
-        devices *= lax.axis_size(axis)
-    rows = v.reshape(devices, -1, *v.shape[-1:]) if v.size // v.shape[-1] % devices == 0 else v.reshape(devices, 1, -1)
-    mine = lax.all_to_all(rows, axes, 0, 0, tiled=True)
-    mine = call(add_kernel, shape(*rows.shape, dtype=F32), "add_rows")(mine)
-    return lax.all_to_all(mine, axes, 0, 0, tiled=True).reshape(v.shape)
+def swap(v, axis, mask):
+    return lax.ppermute(v, axis, [(i, i ^ mask) for i in range(lax.axis_size(axis))])
+
+
+def add(v, w):
+    return (v.astype(F32) + w.astype(F32)).astype(BF16)
 
 
 def local(fields, first_weight, first_bias, second_weight, second_bias, cotangent):
@@ -287,42 +278,50 @@
     e1, e2, er1, er2, expand = (jnp.asarray(v, BF16) for v in (e1, e2, er1, er2, expand))
     y1, y2, rows_y = (jnp.asarray(v, F32) for v in (y1[None], y2[None], rows_y[:, None]))
     planes = fields.shape[2]
+
+    w1 = first_weight.reshape(3, 3, 3, CH, CI).transpose(0, 1, 3, 2, 4).reshape(9 * CH, 3 * CI)
+    wb = second_weight.reshape(3, 3, 3, CH, CH)[::-1, ::-1, ::-1].transpose(0, 1, 4, 2, 3).reshape(9 * CH, 3 * CH)
+    w1, wb, fields_first, cot_first = lax.optimization_barrier((w1, wb, fields, cotangent))
     near, far = call(
         pack_kernel,
         (shape(512, Z),) * 2,
         "pack_strips",
         (pltpu.VMEM(fields.shape, BF16), pltpu.VMEM(cotangent.shape, BF16), pltpu.SemaphoreType.DMA((2,))),
         in_specs=[pl.BlockSpec(memory_space=pltpu.HBM)] * 2,
-    )(fields, cotangent)
+    )(fields_first, cot_first)
     xnear, xfar = exchange(near, far, "stream")
-
-    w1 = first_weight.reshape(3, 3, 3, CH, CI).transpose(0, 1, 3, 2, 4).reshape(9 * CH, 3 * CI)
-    w2 = second_weight.reshape(3, 3, 3, CH, CH)
-    wb = w2[::-1, ::-1, ::-1].transpose(0, 1, 4, 2, 3).reshape(9 * CH, 3 * CH)
-    w2 = w2.transpose(0, 1, 3, 2, 4).reshape(9 * CH, 3 * CH)
     wide = (planes + 4) * Z
     t1, tb, b1 = call(
         band_first_kernel, (shape(192, 1152), shape(128, 1920), shape(192, wide, dtype=F32)), "band_first"
     )(w1, wb, first_bias[None], e1, e2, expand, y1, y2, rows_y)
 
     counts = (lax.axis_size("stream"), lax.axis_size("radial"))
+    t1, tb, b1, xnear, xfar = lax.optimization_barrier((t1, tb, b1, xnear, xfar))
     near, far = call(functools.partial(join_kernel, counts), (shape((2 * planes + 12) * 32, Z),) * 2, "join_strips")(
         fields, cotangent, xnear, xfar)
     rnear, rfar = exchange(near, far, "radial")
     hidden, payload = call(
         functools.partial(first_kernel, counts),
-        (shape(planes + 4, 192, Z), shape(32, 4, 128, dtype=F32)),
+        (shape(planes + 4, 192, Z), shape(32, 384)),
         "gradients",
         (pltpu.VMEM((384, wide + 4 * Z), BF16), pltpu.VMEM((640, wide), BF16)),
         flops=2_000_000_000,
     )(fields, cotangent, xnear, xfar, rnear, rfar, t1, tb, b1, er1, er2, y1, y2, rows_y[:128])
-    total = reduce_all(payload, ("stream", "radial", "snap"))
-
+
+    steps = [(axis, 1 << n) for axis in ("radial", "stream", "snap") for n in range((lax.axis_size(axis) - 1).bit_length())]
+    payload, weight = lax.optimization_barrier((payload, second_weight))
+    arrived = swap(payload, *steps[0])
+    w2 = weight.reshape(3, 3, 3, CH, CH).transpose(0, 1, 3, 2, 4).reshape(9 * CH, 3 * CH)
     t2, b2 = call(band_second_kernel, (shape(128, 1920), shape(128, planes * Z, dtype=F32)), "band_second")(
         w2, second_bias[None], e2, expand, y2, rows_y)
+    payload, t2, b2 = lax.optimization_barrier((add(payload, arrived), t2, b2))
+    arrived = swap(payload, *steps[1])
     closure = call(
         closure_kernel, shape(*cotangent.shape), "closure", (pltpu.VMEM((640, wide), BF16),), flops=1_000_000_000
     )(hidden, t2, b2)
+    for step in steps[2:]:
+        payload = add(payload, arrived)
+        arrived = swap(payload, *step)
 
     cells = fields.shape[0] * fields.shape[2] * fields.shape[3] * fields.shape[4]
     for axis in ("stream", "radial", "snap"):
@@ -332,7 +331,7 @@
         functools.partial(finish_kernel, norm),
         (shape(CH * CI, 27, dtype=F32), shape(CH * CH, 27, dtype=F32), shape(1, CH, dtype=F32)),
         "finish",
-    )(total)
+    )(payload, arrived)
     first = first.reshape(CH, CI, 27).transpose(2, 0, 1)
     second = second.reshape(CH, CH, 27).transpose(2, 0, 1)
     return (closure, first, second, bias[0])

time: 49.6 us -> 44.9 us (0.905)
  blocking collectives: 19.2 us -> 0 us
  starting transfers between devices: 7.06 us -> 22.2 us
  waiting for transfers between devices: 7.97 us -> 8.91 us
  local copies, waits for them, and re-layouts: 3.82 us -> 3.04 us
  Pallas kernels: 10.2 us -> 9.54 us
    all_to_all x1 -> x0, blocking collectives: 19.2 us -> none  [reduce_all(): mine = lax.all_to_all(rows, axes, 0, 0, tiled=True)]
    ppermute x0 -> x5, starting transfers between devices: none -> 17.5 us  [swap(): lax.ppermute(v, axis, [(i, i ^ mask) for i in range(lax.axis_size(axis))])]
    ppermute x0 -> x5, waiting for transfers between devices: none -> 6.89 us  [swap(): lax.ppermute(v, axis, [(i, i ^ mask) for i in range(lax.axis_size(axis))])]
    all_to_all x1 -> x0, waiting for transfers between devices: 5.13 us -> none  [reduce_all(): return lax.all_to_all(mine, axes, 0, 0, tiled=True).reshape(v.shape)]
    all_to_all x1 -> x0, starting transfers between devices: 2.57 us -> none  [reduce_all(): return lax.all_to_all(mine, axes, 0, 0, tiled=True).reshape(v.shape)]
    unnamed x34 -> x30, local copies, waits for them, and re-layouts: 3.11 us -> 2.1 us
    ppermute x2, waiting for transfers between devices: 2.83 us -> 2.01 us  [exchange(): lax.ppermute(near, axis, [(i, i ^ 1) for i in range(count)])]
    pallas_call x1 -> x0, Pallas kernels: 0.67 us -> none  [reduce_all(): mine = call(add_kernel, shape(*rows.shape, dtype=F32), 'add_rows')(mine)]
  transfers between devices with their start and end apart: 5 -> 9, of which waited for: 2 -> 6; matrix products, arithmetic and copies ran while one was open for 4% -> 1% of each run, Pallas kernels for 7% -> 8%
where the time goes in v4:
time: 44.9 us; the launch traced here: 44.7 us
  starting transfers between devices  22.2 us (49%)
  Pallas kernels  9.54 us (21%)
  waiting for transfers between devices  8.91 us (20%)
  local copies, waits for them, and re-layouts  3.04 us (7%)
  between operations  0.97 us (2%)
    ppermute x5, starting transfers between devices, swap(): lax.ppermute(v, axis, [(i, i ^ mask) for i in range(lax.axis_size(axis))])  17.5 us
    ppermute x5, waiting for transfers between devices, swap(): lax.ppermute(v, axis, [(i, i ^ mask) for i in range(lax.axis_size(axis))])  6.89 us
    pallas_call x1, Pallas kernels, local(): call(functools.partial(first_kernel, counts), (shape(planes + 4, 192, Z),...  4.74 us
    ppermute x2, starting transfers between devices, exchange(): lax.ppermute(near, axis, [(i, i ^ 1) for i in range(count)])  3.16 us
    unnamed x30, local copies, waits for them, and re-layouts  2.1 us
    ppermute x2, waiting for transfers between devices, exchange(): lax.ppermute(near, axis, [(i, i ^ 1) for i in range(count)])  2.01 us
    pallas_call x1, Pallas kernels, local(): call(closure_kernel, shape(*cotangent.shape), 'closure', (pltpu.VMEM((640...  1.58 us
    ppermute x2, starting transfers between devices, exchange(): lax.ppermute(far, axis, shifted_pairs)  1.46 us
  transfers between devices with their start and end apart: 9, of which 6 were waited for; matrix products, arithmetic and copies ran while one was open for 1% of the time, Pallas kernels for 8%

profile of v4, /device:TPU:0, one launch (start us, length us, event | category | flops | bytes accessed | tf_op | source)
XLA Modules:
  0.0 44.7 jit_solution(5720603033103303970)
XLA Ops:
  0.6 0.0 copy-start.6
  0.6 0.0 copy-start.2
  0.7 0.0 copy-start.7
  0.7 0.0 copy-start.4
  0.7 0.0 copy-start.3
  0.7 0.0 copy-start.5
  0.7 0.0 copy-start
  0.7 0.0 copy-start.1
  0.7 0.0 copy-start.8
  0.7 1.0 %copy.21 = bf16[27,16,8]{1,2,0:T(8,128)(2,1)S(1)} copy(bf16[27,16,8]{0,2,1:T(8,128)(2,1)} %param.15) | data formatting | bytes 13824 | tf_op args[1]
  1.8 0.0 copy-start.10
  1.8 0.0 copy-start.11
  1.8 0.0 copy-start.12
  1.8 0.1 reshape.33
  1.9 1.0 %copy.23 = bf16[27,16,16]{2,1,0:T(8,128)(2,1)S(1)} copy(bf16[27,16,16]{0,2,1:T(8,128)(2,1)} %param.17) | data formatting | bytes 27648 | tf_op args[3]
  3.0 0.1 copy.24
  3.0 0.1 reshape.35
  3.2 0.0 copy-done
  3.2 0.0 copy-done.1
  3.2 0.3 pack_strips.1
  3.4 3.1 %collective-permute-start = (bf16[512,128]{1,0:T(8,128)(2,1)S(1)}, bf16[512,128]{1,0:T(8,128)(2,1)S(1)}, u32[]{:S(2)}, u32[]{:S(2)}) collective-permute-start(bf16[512,128]{1,0:T(8,128)(2,1)S(1)} %get-tuple-element.39), channel_id=1, source_target_pairs={{0,8},{8,0},{16,24},{24,16},{1,9},{9,1},{17,25},{25,17},{2,10},{10... | collective-permute-start | bytes 393224 | tf_op jit(solution)/shard_map/ppermute | solution.py:260
  6.5 0.7 %collective-permute-start.1 = (bf16[512,128]{1,0:T(8,128)(2,1)S(1)}, bf16[512,128]{1,0:T(8,128)(2,1)S(1)}, u32[]{:S(2)}, u32[]{:S(2)}) collective-permute-start(bf16[512,128]{1,0:T(8,128)(2,1)S(1)} %get-tuple-element.40), channel_id=1, source_target_pairs={{0,0},{8,16},{16,8},{24,24},{1,1},{9,17},{17,9},{25,25},{2,2},{10,... | collective-permute-start | bytes 393224 | tf_op jit(solution)/shard_map/ppermute | solution.py:260
  7.2 0.1 copy.25.w1
  7.3 0.1 copy.26.wb
  7.4 0.0 copy-done.6
  7.4 0.0 copy-done.2
  7.4 0.0 copy-done.7
  7.5 0.0 copy-done.4
  7.5 0.0 copy-done.3
  7.5 0.0 copy-done.5
  7.5 0.0 copy-done.8
  7.5 1.2 %band_first.1 = (bf16[192,1152]{1,0:T(8,128)(2,1)S(1)}, bf16[128,1920]{1,0:T(8,128)(2,1)S(1)}, f32[192,1536]{1,0:T(8,128)S(1)}) custom-call(bf16[144,24]{1,0:T(8,128)(2,1)S(1)} %copy.25.w1, bf16[144,48]{1,0:T(8,128)(2,1)S(1)} %copy.26.wb, f32[1,16]{1,0:T(1,128)S(1)} %bitcast.22, bf16[24,384]{1,0:T(8,128)(2,1)S(1)} %copy-done.5, ...), custom_call_target="tpu_custom_call" | custom-call | flops 10000000 | bytes 1000000 | tf_op jit(solution)/shard_map/band_first/pallas_call | solution.py:294
  8.7 1.4 %collective-permute-done.xnear = bf16[512,128]{1,0:T(8,128)(2,1)S(1)} collective-permute-done((bf16[512,128]{1,0:T(8,128)(2,1)S(1)}, bf16[512,128]{1,0:T(8,128)(2,1)S(1)}, u32[]{:S(2)}, u32[]{:S(2)}) %collective-permute-start) | collective-permute-done | bytes 131104 | tf_op jit(solution)/shard_map/ppermute | solution.py:260
  10.0 0.0 collective-permute-done.1.xfar
  10.0 0.3 join_strips.1
  10.4 0.1 collective-permute-start.2
  10.4 0.0 copy-start.13
  10.5 0.0 copy-start.9
  10.5 0.8 %collective-permute-start.3 = (bf16[896,128]{1,0:T(8,128)(2,1)S(1)}, bf16[896,128]{1,0:T(8,128)(2,1)S(1)}, u32[]{:S(2)}, u32[]{:S(2)}) collective-permute-start(bf16[896,128]{1,0:T(8,128)(2,1)S(1)} %get-tuple-element.44), channel_id=1, source_target_pairs={{0,0},{2,4},{4,2},{6,6},{1,1},{3,5},{5,3},{7,7},{8,8},{10,12},{12,... | collective-permute-start | bytes 688136 | tf_op jit(solution)/shard_map/ppermute | solution.py:260
  11.3 0.6 %collective-permute-done.2.rnear = bf16[896,128]{1,0:T(8,128)(2,1)S(1)} collective-permute-done((bf16[896,128]{1,0:T(8,128)(2,1)S(1)}, bf16[896,128]{1,0:T(8,128)(2,1)S(1)}, u32[]{:S(2)}, u32[]{:S(2)}) %collective-permute-start.2) | collective-permute-done | bytes 229408 | tf_op jit(solution)/shard_map/ppermute | solution.py:260
  11.9 0.0 collective-permute-done.3.rfar
  11.9 0.0 copy-done.10
  11.9 0.0 copy-done.11
  11.9 0.0 copy-done.12
  11.9 4.7 %gradients.1 = (bf16[12,192,128]{2,1,0:T(8,128)(2,1)S(1)}, bf16[32,384]{1,0:T(8,128)(2,1)S(1)}) custom-call(bf16[1,8,8,8,128]{4,3,2,1,0:T(8,128)(2,1)S(1)} %copy-done.1, bf16[1,16,8,8,128]{4,3,2,1,0:T(8,128)(2,1)S(1)} %copy-done, bf16[512,128]{1,0:T(8,128)(2,1)S(1)} %collective-permute-done.xnear, bf16[512,128]{1,0:T(8,128)(2,1)S(1)} %collective-permute-done.1.xfar, ...), custom_call_target="tpu_custom_call" | custom-call | flops 2000000000 | bytes 1000000 | tf_op jit(solution)/shard_map/gradients/pallas_call | solution.py:303
  16.7 6.5 %collective-permute-start.4 = (bf16[32,384]{1,0:T(8,128)(2,1)S(1)}, bf16[32,384]{1,0:T(8,128)(2,1)S(1)}, u32[]{:S(2)}, u32[]{:S(2)}) collective-permute-start(bf16[32,384]{1,0:T(8,128)(2,1)S(1)} %get-tuple-element.50), channel_id=1, source_target_pairs={{0,2},{2,0},{4,6},{6,4},{1,3},{3,1},{5,7},{7,5},{8,10},{10,8},{12,... | collective-permute-start | bytes 73736 | tf_op jit(solution)/shard_map/ppermute | solution.py:264
  23.2 0.0 copy-done.13
  23.2 0.2 copy.27
  23.4 0.1 copy.30
  23.5 0.1 reshape.40.w2
  23.6 0.0 copy-done.9
  23.6 0.7 %band_second.1 = (bf16[128,1920]{1,0:T(8,128)(2,1)S(1)}, f32[128,1024]{1,0:T(8,128)S(1)}) custom-call(bf16[144,48]{1,0:T(8,128)(2,1)S(1)} %reshape.40.w2, f32[1,16]{1,0:T(1,128)S(1)} %bitcast.23, bf16[48,640]{1,0:T(8,128)(2,1)S(1)} %copy-done.3, bf16[192,16]{1,0:T(8,128)(2,1)S(1)} %copy-done.4, f32[1,640]{1,0:T(1,128)S(1)} %copy-done.6, f32[192,1]{1,0:T(8,128)S(1)} %copy-done.2), custom_call_target="tpu_custom_call" | custom-call | flops 10000000 | bytes 1000000 | tf_op jit(solution)/shard_map/band_second/pallas_call | solution.py:315
  24.3 0.0 collective-permute-done.4
  24.3 1.4 %collective-permute-start.5 = (bf16[32,384]{1,0:T(8,128)(2,1)S(1)}, bf16[32,384]{1,0:T(8,128)(2,1)S(1)}, u32[]{:S(2)}, u32[]{:S(2)}) collective-permute-start(bf16[32,384]{1,0:T(8,128)(2,1)S(1)} %add_convert_fusion.3), channel_id=1, source_target_pairs={{0,4},{2,6},{4,0},{6,2},{1,5},{3,7},{5,1},{7,3},{8,12},{10,14},{12... | collective-permute-start | bytes 73736 | tf_op jit(solution)/shard_map/ppermute | solution.py:264
  25.7 2.5 %collective-permute-done.5 = bf16[32,384]{1,0:T(8,128)(2,1)S(1)} collective-permute-done((bf16[32,384]{1,0:T(8,128)(2,1)S(1)}, bf16[32,384]{1,0:T(8,128)(2,1)S(1)}, u32[]{:S(2)}, u32[]{:S(2)}) %collective-permute-start.5) | collective-permute-done | bytes 24608 | tf_op jit(solution)/shard_map/ppermute | solution.py:264
  28.3 4.8 %collective-permute-start.6 = (bf16[32,384]{1,0:T(8,128)(2,1)S(1)}, bf16[32,384]{1,0:T(8,128)(2,1)S(1)}, u32[]{:S(2)}, u32[]{:S(2)}) collective-permute-start(bf16[32,384]{1,0:T(8,128)(2,1)S(1)} %add_convert_fusion.2), channel_id=1, source_target_pairs={{0,8},{8,0},{16,24},{24,16},{1,9},{9,1},{17,25},{25,17},{2,10},{10... | collective-permute-start | bytes 73736 | tf_op jit(solution)/shard_map/ppermute | solution.py:264
  33.1 1.8 %collective-permute-done.6 = bf16[32,384]{1,0:T(8,128)(2,1)S(1)} collective-permute-done((bf16[32,384]{1,0:T(8,128)(2,1)S(1)}, bf16[32,384]{1,0:T(8,128)(2,1)S(1)}, u32[]{:S(2)}, u32[]{:S(2)}) %collective-permute-start.6) | collective-permute-done | bytes 24608 | tf_op jit(solution)/shard_map/ppermute | solution.py:264
  34.9 3.3 %collective-permute-start.7 = (bf16[32,384]{1,0:T(8,128)(2,1)S(1)}, bf16[32,384]{1,0:T(8,128)(2,1)S(1)}, u32[]{:S(2)}, u32[]{:S(2)}) collective-permute-start(bf16[32,384]{1,0:T(8,128)(2,1)S(1)} %add_convert_fusion.1), channel_id=1, source_target_pairs={{0,16},{8,24},{16,0},{24,8},{1,17},{9,25},{17,1},{25,9},{2,18},{10... | collective-permute-start | bytes 73736 | tf_op jit(solution)/shard_map/ppermute | solution.py:264
  38.2 1.8 %collective-permute-done.7 = bf16[32,384]{1,0:T(8,128)(2,1)S(1)} collective-permute-done((bf16[32,384]{1,0:T(8,128)(2,1)S(1)}, bf16[32,384]{1,0:T(8,128)(2,1)S(1)}, u32[]{:S(2)}, u32[]{:S(2)}) %collective-permute-start.7) | collective-permute-done | bytes 24608 | tf_op jit(solution)/shard_map/ppermute | solution.py:264
  40.0 1.6 %collective-permute-start.8 = (bf16[32,384]{1,0:T(8,128)(2,1)S(1)}, bf16[32,384]{1,0:T(8,128)(2,1)S(1)}, u32[]{:S(2)}, u32[]{:S(2)}) collective-permute-start(bf16[32,384]{1,0:T(8,128)(2,1)S(1)} %add_convert_fusion.total), channel_id=1, source_target_pairs={{0,1},{1,0},{2,3},{3,2},{4,5},{5,4},{6,7},{7,6},{8,9},{9,8},{10,11... | collective-permute-start | bytes 73736 | tf_op jit(solution)/shard_map/ppermute | solution.py:264
  41.5 1.6 %closure.1 = bf16[1,16,8,8,128]{4,3,2,1,0:T(8,128)(2,1)} custom-call(bf16[12,192,128]{2,1,0:T(8,128)(2,1)S(1)} %get-tuple-element.48.hidden, bf16[128,1920]{1,0:T(8,128)(2,1)S(1)} %get-tuple-element.54.t2, f32[128,1024]{1,0:T(8,128)S(1)} %get-tuple-element.55.b2), custom_call_target="tpu_custom_call" | custom-call | flops 1000000000 | bytes 1000000 | tf_op jit(solution)/shard_map/closure/pallas_call | solution.py:319
  43.1 0.8 %collective-permute-done.8.last = bf16[32,384]{1,0:T(8,128)(2,1)S(1)} collective-permute-done((bf16[32,384]{1,0:T(8,128)(2,1)S(1)}, bf16[32,384]{1,0:T(8,128)(2,1)S(1)}, u32[]{:S(2)}, u32[]{:S(2)}) %collective-permute-start.8) | collective-permute-done | bytes 24608 | tf_op jit(solution)/shard_map/ppermute | solution.py:264
  43.9 0.8 %finish.1 = (f32[128,27]{1,0:T(8,128)}, f32[256,27]{1,0:T(8,128)}, f32[1,16]{1,0:T(1,128)}) custom-call(bf16[32,384]{1,0:T(8,128)(2,1)S(1)} %add_convert_fusion.total, bf16[32,384]{1,0:T(8,128)(2,1)S(1)} %collective-permute-done.8.last), custom_call_target="tpu_custom_call" | custom-call | flops 10000000 | bytes 1000000 | tf_op jit(solution)/shard_map/finish/pallas_call | solution.py:330
  (6 shorter events, 0.1 us)
Async XLA Ops:
  0.6 6.8 %copy-start.6 = (f32[1,640]{1,0:T(1,128)S(1)}, f32[1,640]{1,0:T(1,128)}, u32[]{:S(2)}) copy-start(f32[1,640]{1,0:T(1,128)} %constant.22.clone.y2) | copy-start | bytes 7684
  0.6 6.8 %copy-start.2 = (f32[192,1]{1,0:T(8,128)S(1)}, f32[192,1]{1,0:T(8,128)}, u32[]{:S(2)}) copy-start(f32[192,1]{1,0:T(8,128)} %constant.23.clone.rows_y) | copy-start | bytes 2308
  0.7 6.8 %copy-start.7 = (f32[1,384]{1,0:T(1,128)S(1)}, f32[1,384]{1,0:T(1,128)}, u32[]{:S(2)}) copy-start(f32[1,384]{1,0:T(1,128)} %constant.21.clone.y1) | copy-start | bytes 4612
  0.7 6.8 %copy-start.4 = (bf16[192,16]{1,0:T(8,128)(2,1)S(1)}, bf16[192,16]{1,0:T(8,128)(2,1)}, u32[]{:S(2)}) copy-start(bf16[192,16]{1,0:T(8,128)(2,1)} %constant.20.clone.expand) | copy-start | bytes 18436
  0.7 6.8 %copy-start.3 = (bf16[48,640]{1,0:T(8,128)(2,1)S(1)}, bf16[48,640]{1,0:T(8,128)(2,1)}, u32[]{:S(2)}) copy-start(bf16[48,640]{1,0:T(8,128)(2,1)} %constant.17.clone.e2) | copy-start | bytes 184324
  0.7 6.8 %copy-start.5 = (bf16[24,384]{1,0:T(8,128)(2,1)S(1)}, bf16[24,384]{1,0:T(8,128)(2,1)}, u32[]{:S(2)}) copy-start(bf16[24,384]{1,0:T(8,128)(2,1)} %constant.16.clone.e1) | copy-start | bytes 55300
  0.7 2.5 %copy-start = (bf16[1,16,8,8,128]{4,3,2,1,0:T(8,128)(2,1)S(1)}, bf16[1,16,8,8,128]{4,3,2,1,0:T(8,128)(2,1)}, u32[]{:S(2)}) copy-start(bf16[1,16,8,8,128]{4,3,2,1,0:T(8,128)(2,1)} %cot.4) | copy-start | bytes 786436
  0.7 2.4 %copy-start.1 = (bf16[1,8,8,8,128]{4,3,2,1,0:T(8,128)(2,1)S(1)}, bf16[1,8,8,8,128]{4,3,2,1,0:T(8,128)(2,1)}, u32[]{:S(2)}) copy-start(bf16[1,8,8,8,128]{4,3,2,1,0:T(8,128)(2,1)} %fields.4) | copy-start | bytes 393220
  0.7 6.8 %copy-start.8 = (f32[16]{0:T(128)S(1)}, f32[16]{0:T(128)}, u32[]{:S(2)}) copy-start(f32[16]{0:T(128)} %param.16) | copy-start | bytes 196
  1.8 10.2 %copy-start.10 = (bf16[2,256,256]{2,1,0:T(8,128)(2,1)S(1)}, bf16[2,256,256]{2,1,0:T(8,128)(2,1)}, u32[]{:S(2)}) copy-start(bf16[2,256,256]{2,1,0:T(8,128)(2,1)} %constant.19.clone.er2) | copy-start | bytes 786436
  1.8 10.1 %copy-start.11 = (f32[128,1]{1,0:T(8,128)S(1)}, f32[128,1]{1,0:T(8,128)}, u32[]{:S(2)}) copy-start(f32[128,1]{1,0:T(8,128)} %constant.26.yo) | copy-start | bytes 1540
  1.8 10.1 %copy-start.12 = (bf16[128,128]{1,0:T(8,128)(2,1)S(1)}, bf16[128,128]{1,0:T(8,128)(2,1)}, u32[]{:S(2)}) copy-start(bf16[128,128]{1,0:T(8,128)(2,1)} %constant.18.clone.er1) | copy-start | bytes 98308
  3.4 6.6 %collective-permute-start = (bf16[512,128]{1,0:T(8,128)(2,1)S(1)}, bf16[512,128]{1,0:T(8,128)(2,1)S(1)}, u32[]{:S(2)}, u32[]{:S(2)}) collective-permute-start(bf16[512,128]{1,0:T(8,128)(2,1)S(1)} %get-tuple-element.39), channel_id=1, source_target_pairs={{0,8},{8,0},{16,24},{24,16},{1,9},{9,1},{17,25},{25,17},{2,10},{10... | collective-permute-start | bytes 393224 | tf_op jit(solution)/shard_map/ppermute | solution.py:260
  6.5 3.5 %collective-permute-start.1 = (bf16[512,128]{1,0:T(8,128)(2,1)S(1)}, bf16[512,128]{1,0:T(8,128)(2,1)S(1)}, u32[]{:S(2)}, u32[]{:S(2)}) collective-permute-start(bf16[512,128]{1,0:T(8,128)(2,1)S(1)} %get-tuple-element.40), channel_id=1, source_target_pairs={{0,0},{8,16},{16,8},{24,24},{1,1},{9,17},{17,9},{25,25},{2,2},{10,... | collective-permute-start | bytes 393224 | tf_op jit(solution)/shard_map/ppermute | solution.py:260
  10.4 1.6 %collective-permute-start.2 = (bf16[896,128]{1,0:T(8,128)(2,1)S(1)}, bf16[896,128]{1,0:T(8,128)(2,1)S(1)}, u32[]{:S(2)}, u32[]{:S(2)}) collective-permute-start(bf16[896,128]{1,0:T(8,128)(2,1)S(1)} %get-tuple-element.43), channel_id=1, source_target_pairs={{0,2},{2,0},{4,6},{6,4},{1,3},{3,1},{5,7},{7,5},{8,10},{10,8},{12,... | collective-permute-start | bytes 688136 | tf_op jit(solution)/shard_map/ppermute | solution.py:260
  10.4 12.8 %copy-start.13 = (bf16[27,16,16]{0,2,1:T(8,128)(2,1)S(1)}, bf16[27,16,16]{0,2,1:T(8,128)(2,1)}, u32[]{:S(2)}) copy-start(bf16[27,16,16]{0,2,1:T(8,128)(2,1)} %param.17) | copy-start | bytes 41476
  10.5 13.2 %copy-start.9 = (f32[16]{0:T(128)S(1)}, f32[16]{0:T(128)}, u32[]{:S(2)}) copy-start(f32[16]{0:T(128)} %param.18) | copy-start | bytes 196
  10.5 1.5 %collective-permute-start.3 = (bf16[896,128]{1,0:T(8,128)(2,1)S(1)}, bf16[896,128]{1,0:T(8,128)(2,1)S(1)}, u32[]{:S(2)}, u32[]{:S(2)}) collective-permute-start(bf16[896,128]{1,0:T(8,128)(2,1)S(1)} %get-tuple-element.44), channel_id=1, source_target_pairs={{0,0},{2,4},{4,2},{6,6},{1,1},{3,5},{5,3},{7,7},{8,8},{10,12},{12,... | collective-permute-start | bytes 688136 | tf_op jit(solution)/shard_map/ppermute | solution.py:260
  16.7 7.6 %collective-permute-start.4 = (bf16[32,384]{1,0:T(8,128)(2,1)S(1)}, bf16[32,384]{1,0:T(8,128)(2,1)S(1)}, u32[]{:S(2)}, u32[]{:S(2)}) collective-permute-start(bf16[32,384]{1,0:T(8,128)(2,1)S(1)} %get-tuple-element.50), channel_id=1, source_target_pairs={{0,2},{2,0},{4,6},{6,4},{1,3},{3,1},{5,7},{7,5},{8,10},{10,8},{12,... | collective-permute-start | bytes 73736 | tf_op jit(solution)/shard_map/ppermute | solution.py:264
  24.3 3.9 %collective-permute-start.5 = (bf16[32,384]{1,0:T(8,128)(2,1)S(1)}, bf16[32,384]{1,0:T(8,128)(2,1)S(1)}, u32[]{:S(2)}, u32[]{:S(2)}) collective-permute-start(bf16[32,384]{1,0:T(8,128)(2,1)S(1)} %add_convert_fusion.3), channel_id=1, source_target_pairs={{0,4},{2,6},{4,0},{6,2},{1,5},{3,7},{5,1},{7,3},{8,12},{10,14},{12... | collective-permute-start | bytes 73736 | tf_op jit(solution)/shard_map/ppermute | solution.py:264
  28.3 6.6 %collective-permute-start.6 = (bf16[32,384]{1,0:T(8,128)(2,1)S(1)}, bf16[32,384]{1,0:T(8,128)(2,1)S(1)}, u32[]{:S(2)}, u32[]{:S(2)}) collective-permute-start(bf16[32,384]{1,0:T(8,128)(2,1)S(1)} %add_convert_fusion.2), channel_id=1, source_target_pairs={{0,8},{8,0},{16,24},{24,16},{1,9},{9,1},{17,25},{25,17},{2,10},{10... | collective-permute-start | bytes 73736 | tf_op jit(solution)/shard_map/ppermute | solution.py:264
  34.9 5.1 %collective-permute-start.7 = (bf16[32,384]{1,0:T(8,128)(2,1)S(1)}, bf16[32,384]{1,0:T(8,128)(2,1)S(1)}, u32[]{:S(2)}, u32[]{:S(2)}) collective-permute-start(bf16[32,384]{1,0:T(8,128)(2,1)S(1)} %add_convert_fusion.1), channel_id=1, source_target_pairs={{0,16},{8,24},{16,0},{24,8},{1,17},{9,25},{17,1},{25,9},{2,18},{10... | collective-permute-start | bytes 73736 | tf_op jit(solution)/shard_map/ppermute | solution.py:264
  40.0 3.9 %collective-permute-start.8 = (bf16[32,384]{1,0:T(8,128)(2,1)S(1)}, bf16[32,384]{1,0:T(8,128)(2,1)S(1)}, u32[]{:S(2)}, u32[]{:S(2)}) collective-permute-start(bf16[32,384]{1,0:T(8,128)(2,1)S(1)} %add_convert_fusion.total), channel_id=1, source_target_pairs={{0,1},{1,0},{2,3},{3,2},{4,5},{5,4},{6,7},{7,6},{8,9},{9,8},{10,11... | collective-permute-start | bytes 73736 | tf_op jit(solution)/shard_map/ppermute | solution.py:264

commit v5 on v4

--- a/solution.py
+++ b/solution.py
@@ -268,6 +268,15 @@
     return (v.astype(F32) + w.astype(F32)).astype(BF16)
 
 
+def gather(v, axis):
+    count = lax.axis_size(axis)
+    return lax.all_to_all(jnp.broadcast_to(v[None], (count, *v.shape)), axis, 0, 0)
+
+
+def merge(parts):
+    return jnp.sum(parts.astype(F32), axis=0).astype(BF16)
+
+
 def local(fields, first_weight, first_bias, second_weight, second_bias, cotangent):
     e1, y1, e2, y2, rows_y, expand = tables()
     er1 = np.tile(e1[:CI, :128].T, (1, CH))
@@ -308,20 +317,21 @@
         flops=2_000_000_000,
     )(fields, cotangent, xnear, xfar, rnear, rfar, t1, tb, b1, er1, er2, y1, y2, rows_y[:128])
 
-    steps = [(axis, 1 << n) for axis in ("radial", "stream", "snap") for n in range((lax.axis_size(axis) - 1).bit_length())]
     payload, weight = lax.optimization_barrier((payload, second_weight))
-    arrived = swap(payload, *steps[0])
+    parts = gather(payload, "radial")
     w2 = weight.reshape(3, 3, 3, CH, CH).transpose(0, 1, 3, 2, 4).reshape(9 * CH, 3 * CH)
     t2, b2 = call(band_second_kernel, (shape(128, 1920), shape(128, planes * Z, dtype=F32)), "band_second")(
         w2, second_bias[None], e2, expand, y2, rows_y)
-    payload, t2, b2 = lax.optimization_barrier((add(payload, arrived), t2, b2))
-    arrived = swap(payload, *steps[1])
+    payload, t2, b2 = lax.optimization_barrier((merge(parts), t2, b2))
+    parts = gather(payload, "stream")
     closure = call(
         closure_kernel, shape(*cotangent.shape), "closure", (pltpu.VMEM((640, wide), BF16),), flops=1_000_000_000
     )(hidden, t2, b2)
-    for step in steps[2:]:
-        payload = add(payload, arrived)
-        arrived = swap(payload, *step)
+    payload = merge(parts)
+    for n in range((lax.axis_size("snap") - 1).bit_length()):
+        if n:
+            payload = add(payload, arrived)
+        arrived = swap(payload, "snap", 1 << n)
 
     cells = fields.shape[0] * fields.shape[2] * fields.shape[3] * fields.shape[4]
     for axis in ("stream", "radial", "snap"):

time: 44.9 us -> 48.3 us (1.076)
  blocking collectives: 0 us -> 12.7 us
  starting transfers between devices: 22.2 us -> 15.1 us
  waiting for transfers between devices: 8.91 us -> 5.89 us
  local copies, waits for them, and re-layouts: 3.04 us -> 3.7 us
    ppermute x5 -> x1, starting transfers between devices: 17.5 us -> 1.55 us  [swap(): lax.ppermute(v, axis, [(i, i ^ mask) for i in range(lax.axis_size(axis))])]
    all_to_all x0 -> x1, blocking collectives: none -> 12.7 us  [gather(): lax.all_to_all(jnp.broadcast_to(v[None], (count, *v.shape)), axis, 0, 0)]
    all_to_all x0 -> x1, starting transfers between devices: none -> 8.96 us  [gather(): lax.all_to_all(jnp.broadcast_to(v[None], (count, *v.shape)), axis, 0, 0)]
    ppermute x5 -> x1, waiting for transfers between devices: 6.89 us -> 0.68 us  [swap(): lax.ppermute(v, axis, [(i, i ^ mask) for i in range(lax.axis_size(axis))])]
    all_to_all x0 -> x1, waiting for transfers between devices: none -> 3.2 us  [gather(): lax.all_to_all(jnp.broadcast_to(v[None], (count, *v.shape)), axis, 0, 0)]
    broadcast_in_dim x0 -> x2, local copies, waits for them, and re-layouts: none -> 0.66 us  [gather(): jnp.broadcast_to(v[None], (count, *v.shape))]
  transfers between devices with their start and end apart: 9 -> 6, of which waited for: 6 -> 4; matrix products, arithmetic and copies ran while one was open for 1% -> 1% of each run, Pallas kernels for 8% -> 7%
where the time goes in v5:
time: 48.3 us; the launch traced here: 48 us
  starting transfers between devices  15.1 us (31%)
  blocking collectives  12.7 us (26%)
  Pallas kernels  9.62 us (20%)
  waiting for transfers between devices  5.89 us (12%)
  local copies, waits for them, and re-layouts  3.7 us (8%)
  between operations  0.95 us (2%)
    all_to_all x1, blocking collectives, gather(): lax.all_to_all(jnp.broadcast_to(v[None], (count, *v.shape)), axis, 0, 0)  12.7 us
    all_to_all x1, starting transfers between devices, gather(): lax.all_to_all(jnp.broadcast_to(v[None], (count, *v.shape)), axis, 0, 0)  8.96 us
    pallas_call x1, Pallas kernels, local(): call(functools.partial(first_kernel, counts), (shape(planes + 4, 192, Z),...  4.74 us
    all_to_all x1, waiting for transfers between devices, gather(): lax.all_to_all(jnp.broadcast_to(v[None], (count, *v.shape)), axis, 0, 0)  3.2 us
    ppermute x2, starting transfers between devices, exchange(): lax.ppermute(near, axis, [(i, i ^ 1) for i in range(count)])  3.16 us
    unnamed x30, local copies, waits for them, and re-layouts  2.1 us
    ppermute x2, waiting for transfers between devices, exchange(): lax.ppermute(near, axis, [(i, i ^ 1) for i in range(count)])  2.01 us
    pallas_call x1, Pallas kernels, local(): call(closure_kernel, shape(*cotangent.shape), 'closure', (pltpu.VMEM((640...  1.65 us
  transfers between devices with their start and end apart: 6, of which 4 were waited for; matrix products, arithmetic and copies ran while one was open for 1% of the time, Pallas kernels for 7%

profile of v5, /device:TPU:0, one launch (start us, length us, event | category | flops | bytes accessed | tf_op | source)
XLA Modules:
  0.0 48.0 jit_solution(14112983365272271143)
XLA Ops:
  0.6 0.0 copy-start.6
  0.6 0.0 copy-start.2
  0.7 0.0 copy-start.7
  0.7 0.0 copy-start.4
  0.7 0.0 copy-start.3
  0.7 0.0 copy-start.5
  0.7 0.0 copy-start
  0.7 0.0 copy-start.1
  0.7 0.0 copy-start.8
  0.7 1.0 %copy.30 = bf16[27,16,8]{1,2,0:T(8,128)(2,1)S(1)} copy(bf16[27,16,8]{0,2,1:T(8,128)(2,1)} %param.15) | data formatting | bytes 13824 | tf_op args[1]
  1.8 0.0 copy-start.10
  1.8 0.0 copy-start.11
  1.8 0.0 copy-start.12
  1.8 0.1 reshape.35
  1.9 1.0 %copy.32 = bf16[27,16,16]{2,1,0:T(8,128)(2,1)S(1)} copy(bf16[27,16,16]{0,2,1:T(8,128)(2,1)} %param.17) | data formatting | bytes 27648 | tf_op args[3]
  3.0 0.1 copy.33
  3.0 0.1 reshape.37
  3.2 0.0 copy-done
  3.2 0.0 copy-done.1
  3.2 0.3 pack_strips.1
  3.4 3.1 %collective-permute-start = (bf16[512,128]{1,0:T(8,128)(2,1)S(1)}, bf16[512,128]{1,0:T(8,128)(2,1)S(1)}, u32[]{:S(2)}, u32[]{:S(2)}) collective-permute-start(bf16[512,128]{1,0:T(8,128)(2,1)S(1)} %get-tuple-element.39), channel_id=1, source_target_pairs={{0,8},{8,0},{16,24},{24,16},{1,9},{9,1},{17,25},{25,17},{2,10},{10... | collective-permute-start | bytes 393224 | tf_op jit(solution)/shard_map/ppermute | solution.py:260
  6.5 0.7 %collective-permute-start.1 = (bf16[512,128]{1,0:T(8,128)(2,1)S(1)}, bf16[512,128]{1,0:T(8,128)(2,1)S(1)}, u32[]{:S(2)}, u32[]{:S(2)}) collective-permute-start(bf16[512,128]{1,0:T(8,128)(2,1)S(1)} %get-tuple-element.40), channel_id=1, source_target_pairs={{0,0},{8,16},{16,8},{24,24},{1,1},{9,17},{17,9},{25,25},{2,2},{10,... | collective-permute-start | bytes 393224 | tf_op jit(solution)/shard_map/ppermute | solution.py:260
  7.2 0.1 copy.34.w1
  7.3 0.1 copy.35.wb
  7.4 0.0 copy-done.6
  7.4 0.0 copy-done.2
  7.4 0.0 copy-done.7
  7.5 0.0 copy-done.4
  7.5 0.0 copy-done.3
  7.5 0.0 copy-done.5
  7.5 0.0 copy-done.8
  7.5 1.2 %band_first.1 = (bf16[192,1152]{1,0:T(8,128)(2,1)S(1)}, bf16[128,1920]{1,0:T(8,128)(2,1)S(1)}, f32[192,1536]{1,0:T(8,128)S(1)}) custom-call(bf16[144,24]{1,0:T(8,128)(2,1)S(1)} %copy.34.w1, bf16[144,48]{1,0:T(8,128)(2,1)S(1)} %copy.35.wb, f32[1,16]{1,0:T(1,128)S(1)} %bitcast.22, bf16[24,384]{1,0:T(8,128)(2,1)S(1)} %copy-done.5, ...), custom_call_target="tpu_custom_call" | custom-call | flops 10000000 | bytes 1000000 | tf_op jit(solution)/shard_map/band_first/pallas_call | solution.py:303
  8.7 1.4 %collective-permute-done.xnear = bf16[512,128]{1,0:T(8,128)(2,1)S(1)} collective-permute-done((bf16[512,128]{1,0:T(8,128)(2,1)S(1)}, bf16[512,128]{1,0:T(8,128)(2,1)S(1)}, u32[]{:S(2)}, u32[]{:S(2)}) %collective-permute-start) | collective-permute-done | bytes 131104 | tf_op jit(solution)/shard_map/ppermute | solution.py:260
  10.0 0.0 collective-permute-done.1.xfar
  10.0 0.3 join_strips.1
  10.4 0.1 collective-permute-start.2
  10.4 0.0 copy-start.13
  10.5 0.0 copy-start.9
  10.5 0.8 %collective-permute-start.3 = (bf16[896,128]{1,0:T(8,128)(2,1)S(1)}, bf16[896,128]{1,0:T(8,128)(2,1)S(1)}, u32[]{:S(2)}, u32[]{:S(2)}) collective-permute-start(bf16[896,128]{1,0:T(8,128)(2,1)S(1)} %get-tuple-element.44), channel_id=1, source_target_pairs={{0,0},{2,4},{4,2},{6,6},{1,1},{3,5},{5,3},{7,7},{8,8},{10,12},{12,... | collective-permute-start | bytes 688136 | tf_op jit(solution)/shard_map/ppermute | solution.py:260
  11.3 0.6 %collective-permute-done.2.rnear = bf16[896,128]{1,0:T(8,128)(2,1)S(1)} collective-permute-done((bf16[896,128]{1,0:T(8,128)(2,1)S(1)}, bf16[896,128]{1,0:T(8,128)(2,1)S(1)}, u32[]{:S(2)}, u32[]{:S(2)}) %collective-permute-start.2) | collective-permute-done | bytes 229408 | tf_op jit(solution)/shard_map/ppermute | solution.py:260
  11.9 0.0 collective-permute-done.3.rfar
  11.9 0.0 copy-done.10
  11.9 0.0 copy-done.11
  11.9 0.0 copy-done.12
  11.9 4.7 %gradients.1 = (bf16[12,192,128]{2,1,0:T(8,128)(2,1)S(1)}, bf16[32,384]{1,0:T(8,128)(2,1)S(1)}) custom-call(bf16[1,8,8,8,128]{4,3,2,1,0:T(8,128)(2,1)S(1)} %copy-done.1, bf16[1,16,8,8,128]{4,3,2,1,0:T(8,128)(2,1)S(1)} %copy-done, bf16[512,128]{1,0:T(8,128)(2,1)S(1)} %collective-permute-done.xnear, bf16[512,128]{1,0:T(8,128)(2,1)S(1)} %collective-permute-done.1.xfar, ...), custom_call_target="tpu_custom_call" | custom-call | flops 2000000000 | bytes 1000000 | tf_op jit(solution)/shard_map/gradients/pallas_call | solution.py:312
  16.7 0.7 %broadcast_in_dim.9 = bf16[4,32,384]{2,1,0:T(8,128)(2,1)} broadcast(bf16[32,384]{1,0:T(8,128)(2,1)S(1)} %get-tuple-element.50), dimensions={1,2} | broadcast | bytes 122880 | tf_op jit(solution)/shard_map/broadcast_in_dim | solution.py:273
  17.3 9.0 %all-to-all-start = ((bf16[4,32,384]{2,1,0:T(8,128)(2,1)}), bf16[4,32,384]{2,1,0:T(8,128)(2,1)S(1)}, u32[]{:S(2)}, u32[]{:S(2)}) async-start(bf16[4,32,384]{2,1,0:T(8,128)(2,1)} %broadcast_in_dim.9), calls=%async_computation | async-start | bytes 196608 | tf_op jit(solution)/shard_map/all_to_all | solution.py:273
  26.3 0.0 copy-done.13
  26.3 0.2 copy.36
  26.5 0.1 copy.39
  26.6 0.1 reshape.42.w2
  26.7 0.0 copy-done.9
  26.7 0.7 %band_second.1 = (bf16[128,1920]{1,0:T(8,128)(2,1)S(1)}, f32[128,1024]{1,0:T(8,128)S(1)}) custom-call(bf16[144,48]{1,0:T(8,128)(2,1)S(1)} %reshape.42.w2, f32[1,16]{1,0:T(1,128)S(1)} %bitcast.23, bf16[48,640]{1,0:T(8,128)(2,1)S(1)} %copy-done.3, bf16[192,16]{1,0:T(8,128)(2,1)S(1)} %copy-done.4, f32[1,640]{1,0:T(1,128)S(1)} %copy-done.6, f32[192,1]{1,0:T(8,128)S(1)} %copy-done.2), custom_call_target="tpu_custom_call" | custom-call | flops 10000000 | bytes 1000000 | tf_op jit(solution)/shard_map/band_second/pallas_call | solution.py:323
  27.4 3.2 %all-to-all-done = bf16[4,32,384]{2,1,0:T(8,128)(2,1)S(1)} async-done(((bf16[4,32,384]{2,1,0:T(8,128)(2,1)}), bf16[4,32,384]{2,1,0:T(8,128)(2,1)S(1)}, u32[]{:S(2)}, u32[]{:S(2)}) %all-to-all-start) | async-done | bytes 98336 | tf_op jit(solution)/shard_map/all_to_all | solution.py:273
  30.6 12.7 %all_to_all.10 = bf16[4,32,384]{2,1,0:T(8,128)(2,1)S(1)} all-to-all(bf16[4,32,384]{2,1,0:T(8,128)(2,1)S(1)} %broadcast_in_dim.21), channel_id=1, replica_groups=mesh['stream'=4,'radial'=4,'snap'=2] {'stream'}, dimensions={0} | all-to-all | bytes 196608 | tf_op jit(solution)/shard_map/all_to_all | solution.py:273
  43.3 1.6 %collective-permute-start.4 = (bf16[32,384]{1,0:T(8,128)(2,1)S(1)}, bf16[32,384]{1,0:T(8,128)(2,1)S(1)}, u32[]{:S(2)}, u32[]{:S(2)}) collective-permute-start(bf16[32,384]{1,0:T(8,128)(2,1)S(1)} %reduce_sum.25.total), channel_id=1, source_target_pairs={{0,1},{1,0},{2,3},{3,2},{4,5},{5,4},{6,7},{7,6},{8,9},{9,8},{10,11... | collective-permute-start | bytes 73736 | tf_op jit(solution)/shard_map/ppermute | solution.py:264
  44.9 1.7 %closure.1 = bf16[1,16,8,8,128]{4,3,2,1,0:T(8,128)(2,1)} custom-call(bf16[12,192,128]{2,1,0:T(8,128)(2,1)S(1)} %get-tuple-element.48.hidden, bf16[128,1920]{1,0:T(8,128)(2,1)S(1)} %get-tuple-element.54.t2, f32[128,1024]{1,0:T(8,128)S(1)} %get-tuple-element.55.b2), custom_call_target="tpu_custom_call" | custom-call | flops 1000000000 | bytes 1000000 | tf_op jit(solution)/shard_map/closure/pallas_call | solution.py:327
  46.5 0.7 %collective-permute-done.4.last = bf16[32,384]{1,0:T(8,128)(2,1)S(1)} collective-permute-done((bf16[32,384]{1,0:T(8,128)(2,1)S(1)}, bf16[32,384]{1,0:T(8,128)(2,1)S(1)}, u32[]{:S(2)}, u32[]{:S(2)}) %collective-permute-start.4) | collective-permute-done | bytes 24608 | tf_op jit(solution)/shard_map/ppermute | solution.py:264
  47.2 0.8 %finish.1 = (f32[128,27]{1,0:T(8,128)}, f32[256,27]{1,0:T(8,128)}, f32[1,16]{1,0:T(1,128)}) custom-call(bf16[32,384]{1,0:T(8,128)(2,1)S(1)} %reduce_sum.25.total, bf16[32,384]{1,0:T(8,128)(2,1)S(1)} %collective-permute-done.4.last), custom_call_target="tpu_custom_call" | custom-call | flops 10000000 | bytes 1000000 | tf_op jit(solution)/shard_map/finish/pallas_call | solution.py:340
  (5 shorter events, 0.1 us)
Async XLA Ops:
  0.6 6.8 %copy-start.6 = (f32[1,640]{1,0:T(1,128)S(1)}, f32[1,640]{1,0:T(1,128)}, u32[]{:S(2)}) copy-start(f32[1,640]{1,0:T(1,128)} %constant.26.clone.y2) | copy-start | bytes 7684
  0.6 6.8 %copy-start.2 = (f32[192,1]{1,0:T(8,128)S(1)}, f32[192,1]{1,0:T(8,128)}, u32[]{:S(2)}) copy-start(f32[192,1]{1,0:T(8,128)} %constant.27.clone.rows_y) | copy-start | bytes 2308
  0.7 6.8 %copy-start.7 = (f32[1,384]{1,0:T(1,128)S(1)}, f32[1,384]{1,0:T(1,128)}, u32[]{:S(2)}) copy-start(f32[1,384]{1,0:T(1,128)} %constant.25.clone.y1) | copy-start | bytes 4612
  0.7 6.8 %copy-start.4 = (bf16[192,16]{1,0:T(8,128)(2,1)S(1)}, bf16[192,16]{1,0:T(8,128)(2,1)}, u32[]{:S(2)}) copy-start(bf16[192,16]{1,0:T(8,128)(2,1)} %constant.24.clone.expand) | copy-start | bytes 18436
  0.7 6.8 %copy-start.3 = (bf16[48,640]{1,0:T(8,128)(2,1)S(1)}, bf16[48,640]{1,0:T(8,128)(2,1)}, u32[]{:S(2)}) copy-start(bf16[48,640]{1,0:T(8,128)(2,1)} %constant.21.clone.e2) | copy-start | bytes 184324
  0.7 6.8 %copy-start.5 = (bf16[24,384]{1,0:T(8,128)(2,1)S(1)}, bf16[24,384]{1,0:T(8,128)(2,1)}, u32[]{:S(2)}) copy-start(bf16[24,384]{1,0:T(8,128)(2,1)} %constant.20.clone.e1) | copy-start | bytes 55300
  0.7 2.5 %copy-start = (bf16[1,16,8,8,128]{4,3,2,1,0:T(8,128)(2,1)S(1)}, bf16[1,16,8,8,128]{4,3,2,1,0:T(8,128)(2,1)}, u32[]{:S(2)}) copy-start(bf16[1,16,8,8,128]{4,3,2,1,0:T(8,128)(2,1)} %cot.4) | copy-start | bytes 786436
  0.7 2.4 %copy-start.1 = (bf16[1,8,8,8,128]{4,3,2,1,0:T(8,128)(2,1)S(1)}, bf16[1,8,8,8,128]{4,3,2,1,0:T(8,128)(2,1)}, u32[]{:S(2)}) copy-start(bf16[1,8,8,8,128]{4,3,2,1,0:T(8,128)(2,1)} %fields.4) | copy-start | bytes 393220
  0.7 6.8 %copy-start.8 = (f32[16]{0:T(128)S(1)}, f32[16]{0:T(128)}, u32[]{:S(2)}) copy-start(f32[16]{0:T(128)} %param.16) | copy-start | bytes 196
  1.8 10.2 %copy-start.10 = (bf16[2,256,256]{2,1,0:T(8,128)(2,1)S(1)}, bf16[2,256,256]{2,1,0:T(8,128)(2,1)}, u32[]{:S(2)}) copy-start(bf16[2,256,256]{2,1,0:T(8,128)(2,1)} %constant.23.clone.er2) | copy-start | bytes 786436
  1.8 10.1 %copy-start.11 = (f32[128,1]{1,0:T(8,128)S(1)}, f32[128,1]{1,0:T(8,128)}, u32[]{:S(2)}) copy-start(f32[128,1]{1,0:T(8,128)} %constant.30.yo) | copy-start | bytes 1540
  1.8 10.1 %copy-start.12 = (bf16[128,128]{1,0:T(8,128)(2,1)S(1)}, bf16[128,128]{1,0:T(8,128)(2,1)}, u32[]{:S(2)}) copy-start(bf16[128,128]{1,0:T(8,128)(2,1)} %constant.22.clone.er1) | copy-start | bytes 98308
  3.4 6.6 %collective-permute-start = (bf16[512,128]{1,0:T(8,128)(2,1)S(1)}, bf16[512,128]{1,0:T(8,128)(2,1)S(1)}, u32[]{:S(2)}, u32[]{:S(2)}) collective-permute-start(bf16[512,128]{1,0:T(8,128)(2,1)S(1)} %get-tuple-element.39), channel_id=1, source_target_pairs={{0,8},{8,0},{16,24},{24,16},{1,9},{9,1},{17,25},{25,17},{2,10},{10... | collective-permute-start | bytes 393224 | tf_op jit(solution)/shard_map/ppermute | solution.py:260
  6.5 3.5 %collective-permute-start.1 = (bf16[512,128]{1,0:T(8,128)(2,1)S(1)}, bf16[512,128]{1,0:T(8,128)(2,1)S(1)}, u32[]{:S(2)}, u32[]{:S(2)}) collective-permute-start(bf16[512,128]{1,0:T(8,128)(2,1)S(1)} %get-tuple-element.40), channel_id=1, source_target_pairs={{0,0},{8,16},{16,8},{24,24},{1,1},{9,17},{17,9},{25,25},{2,2},{10,... | collective-permute-start | bytes 393224 | tf_op jit(solution)/shard_map/ppermute | solution.py:260
  10.4 1.6 %collective-permute-start.2 = (bf16[896,128]{1,0:T(8,128)(2,1)S(1)}, bf16[896,128]{1,0:T(8,128)(2,1)S(1)}, u32[]{:S(2)}, u32[]{:S(2)}) collective-permute-start(bf16[896,128]{1,0:T(8,128)(2,1)S(1)} %get-tuple-element.43), channel_id=1, source_target_pairs={{0,2},{2,0},{4,6},{6,4},{1,3},{3,1},{5,7},{7,5},{8,10},{10,8},{12,... | collective-permute-start | bytes 688136 | tf_op jit(solution)/shard_map/ppermute | solution.py:260
  10.4 15.9 %copy-start.13 = (bf16[27,16,16]{0,2,1:T(8,128)(2,1)S(1)}, bf16[27,16,16]{0,2,1:T(8,128)(2,1)}, u32[]{:S(2)}) copy-start(bf16[27,16,16]{0,2,1:T(8,128)(2,1)} %param.17) | copy-start | bytes 41476
  10.5 16.2 %copy-start.9 = (f32[16]{0:T(128)S(1)}, f32[16]{0:T(128)}, u32[]{:S(2)}) copy-start(f32[16]{0:T(128)} %param.18) | copy-start | bytes 196
  10.5 1.5 %collective-permute-start.3 = (bf16[896,128]{1,0:T(8,128)(2,1)S(1)}, bf16[896,128]{1,0:T(8,128)(2,1)S(1)}, u32[]{:S(2)}, u32[]{:S(2)}) collective-permute-start(bf16[896,128]{1,0:T(8,128)(2,1)S(1)} %get-tuple-element.44), channel_id=1, source_target_pairs={{0,0},{2,4},{4,2},{6,6},{1,1},{3,5},{5,3},{7,7},{8,8},{10,12},{12,... | collective-permute-start | bytes 688136 | tf_op jit(solution)/shard_map/ppermute | solution.py:260
  17.3 13.3 %all-to-all-start = ((bf16[4,32,384]{2,1,0:T(8,128)(2,1)}), bf16[4,32,384]{2,1,0:T(8,128)(2,1)S(1)}, u32[]{:S(2)}, u32[]{:S(2)}) async-start(bf16[4,32,384]{2,1,0:T(8,128)(2,1)} %broadcast_in_dim.9), calls=%async_computation | async-start | bytes 196608 | tf_op jit(solution)/shard_map/all_to_all | solution.py:273
  43.3 3.9 %collective-permute-start.4 = (bf16[32,384]{1,0:T(8,128)(2,1)S(1)}, bf16[32,384]{1,0:T(8,128)(2,1)S(1)}, u32[]{:S(2)}, u32[]{:S(2)}) collective-permute-start(bf16[32,384]{1,0:T(8,128)(2,1)S(1)} %reduce_sum.25.total), channel_id=1, source_target_pairs={{0,1},{1,0},{2,3},{3,2},{4,5},{5,4},{6,7},{7,6},{8,9},{9,8},{10,11... | collective-permute-start | bytes 73736 | tf_op jit(solution)/shard_map/ppermute | solution.py:264

commit v6 on v4

v6 whole, which is shorter than its diff:
```python
import functools

import numpy as np
import jax
import jax.numpy as jnp
from jax import lax
from jax.experimental import pallas as pl
from jax.experimental.pallas import tpu as pltpu
from jax.sharding import PartitionSpec as P

F32 = jnp.float32
BF16 = jnp.bfloat16
Z = 128
CI = 8
CH = 16
FAR = 100


def block(channels, width, y_first=False):
    own = (np.repeat(np.arange(channels), 8), np.tile(np.arange(8), channels))
    if y_first:
        own = (np.tile(np.arange(channels), 8), np.repeat(np.arange(8), channels))
    rim_c = np.concatenate([np.repeat(np.arange(channels), width)] * 2)
    rim_y = np.concatenate([np.tile(np.arange(-width, 0), channels), np.tile(np.arange(8, 8 + width), channels)])
    return own, (rim_c, rim_y)


def lanes_of(channels, total, places):
    e = np.zeros((3 * channels, total), np.float32)
    ys = np.full((1, total), FAR, np.float32)
    for c in range(3):
        for (ch, y), start, step in places:
            at = start + c * step + np.arange(len(ch))
            e[c * channels + ch, at] = 1
            ys[0, at] = y
    return e, ys


def rows_of(own, rim):
    ch, y = (np.concatenate([a, b]) for a, b in zip(own, rim))
    return np.eye(CH, dtype=np.float32)[ch], y[:, None].astype(np.float32)


def plane(ref, x):
    v = ref[0, :, x].astype(F32)
    return v.reshape(v.shape[0] * v.shape[1], v.shape[2])


def pick_rows(channels, width):
    half = channels * width
    row = lax.broadcasted_iota(jnp.int32, (2 * half, channels * 8), 0)
    col = lax.broadcasted_iota(jnp.int32, (2 * half, channels * 8), 1)
    side = jnp.where(row >= half, 1, 0)
    q = row - side * half
    return jnp.where(col == (q // width) * 8 + (8 - width) * side + q % width, 1.0, 0.0).astype(BF16)


def partners(index, count):
    return index % 2 == 0, index > 0, index < count - 1


def sides(index, count, near, far):
    near_above, below, above = partners(index, count)
    low = jnp.where(near_above, far, near).astype(F32)
    high = jnp.where(near_above, near, far).astype(F32)
    return jnp.where(below, low, 0.0), jnp.where(above, high, 0.0)


def strips(here, width, near, far, at):
    up_first = lax.axis_index("stream") % 2 == 0
    count, rows = here.shape[2], here.shape[1] * here.shape[3]
    for n in range(width):
        low, high = plane(here, n), plane(here, count - width + n)
        part = slice(at + n * rows, at + (n + 1) * rows)
        near[part] = jnp.where(up_first, high, low).astype(BF16)
        far[part] = jnp.where(up_first, low, high).astype(BF16)


def pack_kernel(fields, cot, near, far):
    strips(fields, 4, near, far, 0)
    strips(cot, 2, near, far, 256)


def x_planes(count, fields, cot, xnear, xfar, size):
    index = lax.axis_index("stream")
    inner = [plane(fields, x) for x in range(count)]
    rims = [sides(index, size, xnear[n * 64:(n + 1) * 64], xfar[n * 64:(n + 1) * 64]) for n in range(4)]
    f = [low for low, _ in rims] + inner + [high for _, high in rims]
    inner = [plane(cot, x) for x in range(count)]
    rims = [sides(index, size, xnear[256 + n * 128:384 + n * 128], xfar[256 + n * 128:384 + n * 128]) for n in range(2)]
    return f, [low for low, _ in rims] + inner + [high for _, high in rims]


def join_kernel(counts, fields, cot, xnear, xfar, near, far):
    up_first = lax.axis_index("radial") % 2 == 0
    f, c = x_planes(fields.shape[2], fields, cot, xnear, xfar, counts[0])
    at = 0
    for rows, pick in ((f, pick_rows(CI, 4)), (c, pick_rows(CH, 2))):
        for v in rows:
            got = jnp.dot(pick, v.astype(BF16), preferred_element_type=F32)
            near[at:at + 32] = jnp.where(up_first, got[32:], got[:32]).astype(BF16)
            far[at:at + 32] = jnp.where(up_first, got[:32], got[32:]).astype(BF16)
            at += 32


def band(w, e, expand, ys, rows_y, t):
    rows, width = t.shape[0], e.shape[1]
    wide = jnp.dot(w[...], e[...], preferred_element_type=F32).astype(BF16)
    for a in range(3):
        total = jnp.zeros((rows, width), F32)
        for b in range(3):
            part = jnp.dot(expand[:rows], wide[(a * 3 + b) * CH:(a * 3 + b + 1) * CH], preferred_element_type=F32)
            total = jnp.where(ys[...] == rows_y[:rows] + float(2 * (b - 1)), part, total)
        t[:, a * width:(a + 1) * width] = total.astype(BF16)


def repeat_bias(bias, expand, out):
    column = jnp.sum(expand[:out.shape[0]].astype(F32) * bias[...], axis=1, keepdims=True)
    out[...] = jnp.broadcast_to(column, out.shape)


def band_first_kernel(w1, wb, bias, e1o, e1r, e2o, e2r, expand, y1o, y1r, y2o, y2r, rows_y, t1o, t1r, tbo, tbr, b1):
    band(w1, e1o, expand, y1o, rows_y, t1o)
    band(w1, e1r, expand, y1r, rows_y, t1r)
    band(wb, e2o, expand, y2o, rows_y, tbo)
    band(wb, e2r, expand, y2r, rows_y, tbr)
    repeat_bias(bias, expand, b1)


def band_second_kernel(w2, bias, e2, expand, y2, rows_y, t2, b2):
    band(w2, e2, expand, y2, rows_y, t2)
    repeat_bias(bias, expand, b2)


def shifted(v):
    lane = lax.broadcasted_iota(jnp.int32, v.shape, 1)
    before = jnp.where(lane >= 2, pltpu.roll(v, 2, 1), 0.0)
    after = jnp.where(lane < Z - 2, pltpu.roll(v, Z - 2, 1), 0.0)
    return before.astype(BF16), v.astype(BF16), after.astype(BF16)


def store_wide(ref, p, v):
    at = slice(p * Z, (p + 1) * Z)
    for c, piece in enumerate(shifted(v)):
        ref[c * 128:(c + 1) * 128, at] = piece[:128]
        ref[384 + c * 64:384 + (c + 1) * 64, at] = piece[128:]
    ref[576:, at] = jnp.zeros((64, Z), BF16)


def stacked(ref, lanes):
    return jnp.concatenate([ref[:, a * 256:a * 256 + lanes] for a in range(3)], axis=0)


def own_kernel(counts, fields, cot, xnear, xfar, t1, tb, b1, fs, cs, pre, back):
    count = fields.shape[2]
    f, c = x_planes(count, fields, cot, xnear, xfar, counts[0])
    for ref, rows in ((fs, f), (cs, c)):
        for p, v in enumerate(rows):
            for n, piece in enumerate(shifted(v)):
                ref[n * v.shape[0]:(n + 1) * v.shape[0], p * Z:(p + 1) * Z] = piece
    fs[192:] = jnp.zeros((64, fs.shape[1]), BF16)
    pre[...] = jnp.dot(t1[...], stacked(fs, pre.shape[1]), preferred_element_type=F32) + b1[...]
    back[...] = jnp.dot(tb[...], stacked(cs, back.shape[1]), preferred_element_type=F32)


def two_dots(v, w):
    high = v.astype(BF16)
    low = (v - high.astype(F32)).astype(BF16)
    return jnp.dot(high, w, preferred_element_type=F32) + jnp.dot(low, w, preferred_element_type=F32)


def rim_kernel(counts, rnear, rfar, fs, cs, pre_own, back_own, t1, tb, e1t, e2t, rep1, rep2, y1, y2,
               hidden_out, payload, fr, cr, taps):
    count = hidden_out.shape[0] - 4
    lanes = count * Z
    stream, radial = lax.axis_index("stream"), lax.axis_index("radial")
    at = 0
    for ref in (fr, cr):
        for p in range(ref.shape[1] // Z):
            low, high = sides(radial, counts[1], rnear[at:at + 32], rfar[at:at + 32])
            for n, piece in enumerate(shifted(jnp.concatenate([low, high], axis=0))):
                ref[n * 64:(n + 1) * 64, p * Z:(p + 1) * Z] = piece
            at += 32
        ref[192:] = jnp.zeros((64, ref.shape[1]), BF16)
    pre = pre_own[...] + jnp.dot(t1[...], stacked(fr, lanes + 4 * Z), preferred_element_type=F32)
    share = 0.5 * (1.0 + lax.erf(pre * 0.7071067811865476))
    hidden = (pre * share).astype(BF16)
    zero = jnp.zeros((), BF16)
    rims = (jnp.where(radial > 0, hidden[128:160], zero), jnp.where(radial < counts[1] - 1, hidden[160:], zero))
    for p in range(count + 4):
        at = slice(p * Z, (p + 1) * Z)
        rows = jnp.concatenate([hidden[:128, at], rims[0][:, at], rims[1][:, at]], axis=0)
        if p < 2:
            rows = jnp.where(stream > 0, rows, zero)
        elif p >= count + 2:
            rows = jnp.where(stream < counts[0] - 1, rows, zero)
        hidden_out[p] = rows
    at = slice(2 * Z, 2 * Z + lanes)
    pre, share, hidden = pre[:128, at], share[:128, at], hidden[:128, at]
    back = back_own[...] + jnp.dot(tb[...], stacked(cr, lanes), preferred_element_type=F32)
    dpre = (back * (share + pre * jnp.exp(-0.5 * pre * pre) * 0.3989422804014327)).astype(BF16)
    over_lanes = (((1,), (1,)), ((), ()))
    ones, twos = [], []
    for a in range(3):
        at = slice((a + 1) * 256, (a + 1) * 256 + lanes)
        rows = [ref[n * 64:(n + 1) * 64, at] for n in range(3) for ref in (fs, fr)]
        g1 = lax.dot_general(dpre, jnp.concatenate(rows, axis=0), over_lanes, preferred_element_type=F32)
        at = slice(a * 256, a * 256 + lanes)
        rows = jnp.concatenate([cs[:, at], cr[:, at]], axis=0)
        g2 = lax.dot_general(hidden, rows, over_lanes, preferred_element_type=F32)
        for b in range(3):
            for g, ys, out in ((g1, y1, ones), (g2, y2, twos)):
                total = jnp.zeros((CH, g.shape[1]), F32)
                for y in range(8):
                    total = jnp.where(ys[...] == float(y + 2 * (b - 1)), g[y * CH:(y + 1) * CH], total)
                out.append(total)
    taps[:, 24:] = jnp.zeros((3, 8, 128), F32)
    for parts, et, rep, at, width in ((ones, e1t, rep1, 0, 128), (twos[::-1], e2t, rep2, 1, 256)):
        sums = two_dots(jnp.concatenate(parts, axis=0), et[...])
        wide = two_dots(sums, rep[...])
        row = lax.broadcasted_iota(jnp.int32, wide.shape, 0) % CH
        lane = lax.broadcasted_iota(jnp.int32, wide.shape, 1) % width
        mine = row == (lane // CI if width == 128 else lane % CH)
        total = jnp.sum(jnp.where(mine, wide, 0.0).reshape(9, CH, 3 * width), axis=1)
        for c in range(3):
            first = c if width == 128 else 2 - c
            for n in range(width // 128):
                taps[at + n, pl.ds(first, 9, stride=3)] = total[:, c * width + n * 128:c * width + (n + 1) * 128]
    bias = jnp.sum(dpre.astype(F32), axis=1, keepdims=True)
    bias = sum(bias[y * CH:(y + 1) * CH] for y in range(8))
    row = lax.broadcasted_iota(jnp.int32, (CH, 128), 0)
    lane = lax.broadcasted_iota(jnp.int32, (CH, 128), 1)
    taps[0, 27:28] = jnp.sum(jnp.where(row == lane, bias, 0.0), axis=0, keepdims=True)
    payload[...] = jnp.concatenate([taps[n] for n in range(3)], axis=1)


def closure_kernel(hidden, t2, b2, closure, hs):
    count = closure.shape[2]
    for p in range(count + 4):
        store_wide(hs, p, hidden[p].astype(F32))
    out = (jnp.dot(t2[...], stacked(hs, count * Z), preferred_element_type=F32) + b2[...]).astype(BF16)
    for x in range(count):
        closure[0, :, x] = out[:, x * Z:(x + 1) * Z].reshape(CH, 8, Z)


def add_kernel(here, there, total):
    s = here[...].astype(F32) + there[...].astype(F32)
    lost = s - s.astype(BF16).astype(F32)
    row = lax.broadcasted_iota(jnp.int32, s.shape, 0)
    total[...] = (s + jnp.where(row == 28, pltpu.roll(lost, 1, 0), 0.0)).astype(BF16)


def finish_kernel(norm, total, last, first, second, bias):
    scaled = (total[...].astype(F32) + last[...].astype(F32)) * norm
    flipped = jnp.transpose(scaled)
    first[...] = flipped[:128, :27]
    second[...] = flipped[128:, :27]
    bias[...] = scaled[27:28, :CH] + scaled[28:29, :CH]


def call(kernel, outs, name, scratch=(), flops=10_000_000, **specs):
    return pl.pallas_call(
        kernel,
        out_shape=outs,
        **specs,
        scratch_shapes=list(scratch),
        compiler_params=pltpu.CompilerParams(vmem_limit_bytes=48 * 1024 * 1024),
        cost_estimate=pl.CostEstimate(flops=flops, bytes_accessed=1_000_000, transcendentals=0),
        name=name,
    )


def shape(*dims, dtype=BF16):
    return jax.ShapeDtypeStruct(dims, dtype)


def exchange(near, far, axis):
    count = lax.axis_size(axis)
    shifted_pairs = [(i, min(max(i - 1 + 2 * (i % 2), 0), count - 1)) for i in range(count)]
    far = lax.ppermute(far, axis, shifted_pairs)
    return lax.ppermute(near, axis, [(i, i ^ 1) for i in range(count)]), far


def swap(v, axis, mask):
    return lax.ppermute(v, axis, [(i, i ^ mask) for i in range(lax.axis_size(axis))])


def add(v, w):
    return call(add_kernel, shape(*v.shape), "add_parts")(v, w)


def local(fields, first_weight, first_bias, second_weight, second_bias, cotangent):
    own, rim = block(CI, 4)
    e1, y1 = lanes_of(CI, 384, ((own, 0, 128), (rim, 64, 128)))
    e1o, y1o = lanes_of(CI, 256, ((own, 0, 64),))
    e1r, y1r = lanes_of(CI, 256, ((rim, 0, 64),))
    own, rim = block(CH, 2)
    e2, y2 = lanes_of(CH, 640, ((own, 0, 128), (rim, 384, 64)))
    e2o, y2o, e2r, y2r = e2[:, :384], y2[:, :384], e2[:, 384:], y2[:, 384:]
    expand2, rows_y2 = rows_of(own, rim)
    own, _ = block(CH, 2, y_first=True)
    e2h, y2h = lanes_of(CH, 640, ((own, 0, 128), (rim, 384, 64)))
    expand1, rows_y1 = rows_of(own, rim)
    e1t, e2t = np.zeros((384, 128), np.float32), np.zeros((640, 128), np.float32)
    e1t[:, :3 * CI], e2t[:, :3 * CH] = e1.T, e2.T
    rep1, rep2 = np.zeros((128, 384), np.float32), np.zeros((128, 768), np.float32)
    for c in range(3):
        rep1[c * CI:(c + 1) * CI, c * 128:(c + 1) * 128] = np.tile(np.eye(CI), (1, CH))
        rep2[c * CH:(c + 1) * CH, c * 256:(c + 1) * 256] = np.repeat(np.eye(CH), CH, axis=1)

    def const(*arrays, dtype=BF16):
        return [jnp.asarray(v, dtype) for v in arrays]

    planes = fields.shape[2]

    w1 = first_weight.reshape(3, 3, 3, CH, CI).transpose(0, 1, 3, 2, 4).reshape(9 * CH, 3 * CI)
    near, far = call(pack_kernel, (shape(512, Z),) * 2, "pack_strips")(fields, cotangent)
    xnear, xfar = exchange(near, far, "stream")
    wide = (planes + 4) * Z
    counts = (lax.axis_size("stream"), lax.axis_size("radial"))
    near, far = call(functools.partial(join_kernel, counts), (shape((2 * planes + 12) * 32, Z),) * 2, "join_strips")(
        fields, cotangent, xnear, xfar)
    near, far, weight = lax.optimization_barrier((near, far, second_weight))
    rnear, rfar = exchange(near, far, "radial")
    wb = weight.reshape(3, 3, 3, CH, CH)[::-1, ::-1, ::-1].transpose(0, 1, 4, 2, 3).reshape(9 * CH, 3 * CH)
    t1o, t1r, tbo, tbr, b1 = call(
        band_first_kernel,
        (shape(192, 768), shape(192, 768), shape(128, 1152), shape(128, 768), shape(192, wide, dtype=F32)),
        "band_first",
    )(w1, wb, first_bias[None], *const(e1o, e1r, e2o, e2r, expand1), *const(y1o, y1r, y2o, y2r, rows_y1, dtype=F32))
    fs, cs, pre, back = call(
        functools.partial(own_kernel, counts),
        (shape(256, wide + 4 * Z), shape(384, wide), shape(192, wide, dtype=F32), shape(128, planes * Z, dtype=F32)),
        "own_rows",
        flops=1_000_000_000,
    )(fields, cotangent, xnear, xfar, t1o, tbo, b1)
    hidden, payload = call(
        functools.partial(rim_kernel, counts),
        (shape(planes + 4, 192, Z), shape(32, 384, dtype=F32)),
        "gradients",
        (pltpu.VMEM((256, wide + 4 * Z), BF16), pltpu.VMEM((256, wide), BF16), pltpu.VMEM((3, 32, 128), F32)),
        flops=2_000_000_000,
    )(rnear, rfar, fs, cs, pre, back, t1r, tbr, *const(e1t, e2t, rep1, rep2), *const(y1, y2, dtype=F32))

    steps = [(axis, 1 << n) for axis in ("radial", "stream", "snap") for n in range((lax.axis_size(axis) - 1).bit_length())]
    payload, weight = lax.optimization_barrier((payload, second_weight))
    arrived = swap(payload, *steps[0])
    w2 = weight.reshape(3, 3, 3, CH, CH).transpose(0, 1, 3, 2, 4).reshape(9 * CH, 3 * CH)
    t2, b2 = call(band_second_kernel, (shape(128, 1920), shape(128, planes * Z, dtype=F32)), "band_second")(
        w2, second_bias[None], *const(e2h, expand2), *const(y2h, rows_y2, dtype=F32))
    payload, t2, b2 = lax.optimization_barrier((add(payload, arrived), t2, b2))
    arrived = swap(payload, *steps[1])
    closure = call(
        closure_kernel, shape(*cotangent.shape), "closure", (pltpu.VMEM((640, wide), BF16),), flops=1_000_000_000
    )(hidden, t2, b2)
    for step in steps[2:]:
        payload = add(payload, arrived)
        arrived = swap(payload, *step)

    cells = fields.shape[0] * fields.shape[2] * fields.shape[3] * fields.shape[4]
    for axis in ("stream", "radial", "snap"):
        cells *= lax.axis_size(axis)
    norm = float(1.0 / np.sqrt(np.float32(cells)))
    first, second, bias = call(
        functools.partial(finish_kernel, norm),
        (shape(CH * CI, 27, dtype=F32), shape(CH * CH, 27, dtype=F32), shape(1, CH, dtype=F32)),
        "finish",
    )(payload, arrived)
    first = first.reshape(CH, CI, 27).transpose(2, 0, 1)
    second = second.reshape(CH, CH, 27).transpose(2, 0, 1)
    return (closure, first, second, bias[0])


def solution(mesh):
    split = P("snap", None, "stream", "radial", None)
    return jax.shard_map(
        local,
        mesh=mesh,
        in_specs=(split, P(), P(), P(), P(), split),
        out_specs=(split, P(), P(), P()),
        check_vma=False,
    )
```

time: 44.9 us -> 45.9 us (1.022)
  starting transfers between devices: 22.2 us -> 17.5 us
  local copies, waits for them, and re-layouts: 3.04 us -> 5.05 us
  waiting for transfers between devices: 8.91 us -> 10.7 us
  Pallas kernels: 9.54 us -> 11.2 us
    ppermute x5, starting transfers between devices: 17.5 us -> 13 us  [swap(): lax.ppermute(v, axis, [(i, i ^ mask) for i in range(lax.axis_size(axis))])]
    unnamed x30 -> x57, local copies, waits for them, and re-layouts: 2.1 us -> 3.94 us
    pallas_call x3 -> x8, Pallas kernels: 6.15 us -> 7.86 us  [the longest x1 3.65 us: local(): call(functools.partial(rim_kernel, counts), (shape(planes + 4, 192, Z), s...]
    ppermute x5, waiting for transfers between devices: 6.89 us -> 7.84 us  [swap(): lax.ppermute(v, axis, [(i, i ^ mask) for i in range(lax.axis_size(axis))])]
    ppermute x4, waiting for transfers between devices: 2.01 us -> 2.84 us  [the longest x2 2.83 us: exchange(): return (lax.ppermute(near, axis, [(i, i ^ 1) for i in range(count)]), far)]
  transfers between devices with their start and end apart: 9 -> 9, of which waited for: 6 -> 5; matrix products, arithmetic and copies ran while one was open for 1% -> 4% of each run, Pallas kernels for 8% -> 14%
where the time goes in v6:
time: 45.9 us; the launch traced here: 45.6 us
  starting transfers between devices  17.5 us (38%)
  Pallas kernels  11.2 us (24%)
  waiting for transfers between devices  10.7 us (23%)
  local copies, waits for them, and re-layouts  5.05 us (11%)
  between operations  1.15 us (3%)
    ppermute x5, starting transfers between devices, swap(): lax.ppermute(v, axis, [(i, i ^ mask) for i in range(lax.axis_size(axis))])  13 us
    ppermute x5, waiting for transfers between devices, swap(): lax.ppermute(v, axis, [(i, i ^ mask) for i in range(lax.axis_size(axis))])  7.84 us
    unnamed x57, local copies, waits for them, and re-layouts  3.94 us
    pallas_call x1, Pallas kernels, local(): call(functools.partial(rim_kernel, counts), (shape(planes + 4, 192, Z), s...  3.65 us
    ppermute x2, starting transfers between devices, exchange(): return (lax.ppermute(near, axis, [(i, i ^ 1) for i in range(count)]), far)  3.16 us
    ppermute x2, waiting for transfers between devices, exchange(): return (lax.ppermute(near, axis, [(i, i ^ 1) for i in range(count)]), far)  2.83 us
    pallas_call x1, Pallas kernels, local(): call(functools.partial(own_kernel, counts), (shape(256, wide + 4 * Z), sh...  2.49 us
    pallas_call x1, Pallas kernels, local(): call(band_first_kernel, (shape(192, 768), shape(192, 768), shape(128, 115...  1.58 us
  transfers between devices with their start and end apart: 9, of which 5 were waited for; matrix products, arithmetic and copies ran while one was open for 4% of the time, Pallas kernels for 14%

profile of v6, /device:TPU:0, one launch (start us, length us, event | category | flops | bytes accessed | tf_op | source)
XLA Modules:
  0.0 45.6 jit_solution(1559841743368254659)
XLA Ops:
  0.6 0.0 copy-start.15
  0.6 0.0 copy-start.14
  0.7 0.0 copy-start.16
  0.7 0.0 copy-start.17
  0.7 0.0 copy-start.10
  0.7 0.0 copy-start
  0.7 1.0 %copy-done = bf16[1,16,8,8,128]{4,3,2,1,0:T(8,128)(2,1)S(1)} copy-done((bf16[1,16,8,8,128]{4,3,2,1,0:T(8,128)(2,1)S(1)}, bf16[1,16,8,8,128]{4,3,2,1,0:T(8,128)(2,1)}, u32[]{:S(2)}) %copy-start) | copy-done | bytes 262168
  1.7 0.9 %copy-done.2 = bf16[1,8,8,8,128]{4,3,2,1,0:T(8,128)(2,1)S(1)} copy-done((bf16[1,8,8,8,128]{4,3,2,1,0:T(8,128)(2,1)S(1)}, bf16[1,8,8,8,128]{4,3,2,1,0:T(8,128)(2,1)}, u32[]{:S(2)}) %copy-start.2) | copy-done | bytes 131096
  2.6 0.0 copy-start.11
  2.6 0.0 copy-start.12
  2.6 0.0 copy-start.18
  2.6 0.1 pack_strips.1
  2.7 0.0 copy-start.1
  2.7 0.0 copy-start.3
  2.7 3.1 %collective-permute-start = (bf16[512,128]{1,0:T(8,128)(2,1)S(1)}, bf16[512,128]{1,0:T(8,128)(2,1)S(1)}, u32[]{:S(2)}, u32[]{:S(2)}) collective-permute-start(bf16[512,128]{1,0:T(8,128)(2,1)S(1)} %get-tuple-element.32), channel_id=1, source_target_pairs={{0,8},{8,0},{16,24},{24,16},{1,9},{9,1},{17,25},{25,17},{2,10},{10... | collective-permute-start | bytes 393224 | tf_op jit(solution)/shard_map/ppermute | solution.py:281
  5.8 0.7 %collective-permute-start.1 = (bf16[512,128]{1,0:T(8,128)(2,1)S(1)}, bf16[512,128]{1,0:T(8,128)(2,1)S(1)}, u32[]{:S(2)}, u32[]{:S(2)}) collective-permute-start(bf16[512,128]{1,0:T(8,128)(2,1)S(1)} %get-tuple-element.33), channel_id=1, source_target_pairs={{0,0},{8,16},{16,8},{24,24},{1,1},{9,17},{17,9},{25,25},{2,2},{10,... | collective-permute-start | bytes 393224 | tf_op jit(solution)/shard_map/ppermute | solution.py:280
  6.5 2.8 %collective-permute-done.xnear = bf16[512,128]{1,0:T(8,128)(2,1)S(1)} collective-permute-done((bf16[512,128]{1,0:T(8,128)(2,1)S(1)}, bf16[512,128]{1,0:T(8,128)(2,1)S(1)}, u32[]{:S(2)}, u32[]{:S(2)}) %collective-permute-start) | collective-permute-done | bytes 131104 | tf_op jit(solution)/shard_map/ppermute | solution.py:281
  9.3 0.0 collective-permute-done.1.xfar
  9.3 0.3 join_strips.1
  9.6 0.1 collective-permute-start.2
  9.7 0.7 %collective-permute-start.3 = (bf16[896,128]{1,0:T(8,128)(2,1)S(1)}, bf16[896,128]{1,0:T(8,128)(2,1)S(1)}, u32[]{:S(2)}, u32[]{:S(2)}) collective-permute-start(bf16[896,128]{1,0:T(8,128)(2,1)S(1)} %get-tuple-element.37), channel_id=1, source_target_pairs={{0,0},{2,4},{4,2},{6,6},{1,1},{3,5},{5,3},{7,7},{8,8},{10,12},{12,... | collective-permute-start | bytes 688136 | tf_op jit(solution)/shard_map/ppermute | solution.py:280
  10.4 0.9 %copy.33 = bf16[27,16,8]{1,2,0:T(8,128)(2,1)S(1)} copy(bf16[27,16,8]{0,2,1:T(8,128)(2,1)} %param.27) | data formatting | bytes 13824 | tf_op args[1]
  11.4 0.1 reshape.33
  11.5 0.1 copy.37.w1
  11.6 0.0 copy-done.27
  11.6 0.2 copy.35
  11.8 0.1 copy.42
  12.0 0.1 reshape.40.wb
  12.1 0.0 copy-done.15
  12.1 0.0 copy-done.14
  12.1 0.0 copy-done.16
  12.1 0.0 copy-done.17
  12.2 1.6 %band_first.1 = (bf16[192,768]{1,0:T(8,128)(2,1)S(1)}, bf16[192,768]{1,0:T(8,128)(2,1)S(1)}, bf16[128,1152]{1,0:T(8,128)(2,1)S(1)}, bf16[128,768]{1,0:T(8,128)(2,1)S(1)}, f32[192,1536]{1,0:T(8,128)S(1)}) custom-call(bf16[144,24]{1,0:T(8,128)(2,1)S(1)} %copy.37.w1, bf16[144,48]{1,0:T(8,128)(2,1)S(1)} %reshape.40.wb, f32[1,16]{1,0:T(1,128)S(1)} %bitcast.20, ...), custom_call_target="tpu_custom_call" | custom-call | flops 10000000 | bytes 1000000 | tf_op jit(solution)/shard_map/band_first/pallas_call | solution.py:326
  13.8 1.0 %copy-done.20 = f32[192,1536]{1,0:T(8,128)} copy-done((f32[192,1536]{1,0:T(8,128)}, f32[192,1536]{1,0:T(8,128)S(1)}, u32[]{:S(2)}) %copy-start.20) | copy-done | bytes 1179672
  14.8 0.0 copy-done.3
  14.8 0.0 copy-start.23
  14.8 0.0 copy-start.24
  14.8 0.0 copy-start.25
  14.9 0.0 copy-start.26
  14.9 2.5 %own_rows.1 = (bf16[256,2048]{1,0:T(8,128)(2,1)S(1)}, bf16[384,1536]{1,0:T(8,128)(2,1)S(1)}, f32[192,1536]{1,0:T(8,128)S(1)}, f32[128,1024]{1,0:T(8,128)S(1)}) custom-call(bf16[1,8,8,8,128]{4,3,2,1,0:T(8,128)(2,1)S(1)} %copy-done.3, bf16[1,16,8,8,128]{4,3,2,1,0:T(8,128)(2,1)S(1)} %copy-done.1, bf16[512,128]{1,0:T(8,128)(2,1)S(1)} %collective-permute-done.xnear, ...), custom_call_target="tpu_custom_call" | custom-call | flops 1000000000 | bytes 1000000 | tf_op jit(solution)/shard_map/own_rows/pallas_call | solution.py:331
  17.4 0.0 collective-permute-done.2.rnear
  17.4 0.0 collective-permute-done.3.rfar
  17.4 0.0 copy-start.5
  17.5 0.0 copy-start.6
  17.5 0.0 copy-start.8
  17.5 0.0 copy-start.13
  17.5 0.0 copy-start.19
  17.5 3.7 %gradients.1 = (bf16[12,192,128]{2,1,0:T(8,128)(2,1)S(1)}, f32[32,384]{1,0:T(8,128)S(1)}) custom-call(bf16[896,128]{1,0:T(8,128)(2,1)S(1)} %collective-permute-done.2.rnear, bf16[896,128]{1,0:T(8,128)(2,1)S(1)} %collective-permute-done.3.rfar, bf16[256,2048]{1,0:T(8,128)(2,1)S(1)} %get-tuple-element.42.fs, bf16[384,1536]{1,0:T(8,128)(2,1)S(1)} %get-tuple-element.43.cs, ...), custom_call_target="tpu_custom_call" | custom-call | flops 2000000000 | bytes 1000000 | tf_op jit(solution)/shard_map/gradients/pallas_call | solution.py:337
  21.2 3.1 %collective-permute-start.4 = (f32[32,384]{1,0:T(8,128)S(1)}, f32[32,384]{1,0:T(8,128)S(1)}, u32[]{:S(2)}, u32[]{:S(2)}) collective-permute-start(f32[32,384]{1,0:T(8,128)S(1)} %get-tuple-element.50.here), channel_id=1, source_target_pairs={{0,2},{2,0},{4,6},{6,4},{1,3},{3,1},{5,7},{7,5},{8,10},{10,8},{12,... | collective-permute-start | bytes 147464 | tf_op jit(solution)/shard_map/ppermute | solution.py:285
  24.3 0.2 copy.39
  24.4 0.1 copy.43
  24.5 0.1 reshape.41.w2
  24.7 0.7 %band_second.1 = (bf16[128,1920]{1,0:T(8,128)(2,1)S(1)}, f32[128,1024]{1,0:T(8,128)S(1)}) custom-call(bf16[144,48]{1,0:T(8,128)(2,1)S(1)} %reshape.41.w2, f32[1,16]{1,0:T(1,128)S(1)} %bitcast.21, bf16[48,640]{1,0:T(8,128)(2,1)S(1)} %copy-done.6, bf16[192,16]{1,0:T(8,128)(2,1)S(1)} %copy-done.8, f32[1,640]{1,0:T(1,128)S(1)} %copy-done.13, f32[192,1]{1,0:T(8,128)S(1)} %copy-done.5), custom_call_target="tpu_custom_call" | custom-call | flops 10000000 | bytes 1000000 | tf_op jit(solution)/shard_map/band_second/pallas_call | solution.py:349
  25.4 0.0 collective-permute-done.4.there
  25.4 0.5 %collective-permute-start.5 = (bf16[32,384]{1,0:T(8,128)(2,1)S(1)}, bf16[32,384]{1,0:T(8,128)(2,1)S(1)}, u32[]{:S(2)}, u32[]{:S(2)}) collective-permute-start(bf16[32,384]{1,0:T(8,128)(2,1)S(1)} %add_parts.4.here), channel_id=1, source_target_pairs={{0,4},{2,6},{4,0},{6,2},{1,5},{3,7},{5,1},{7,3},{8,12},{10,14},{12... | collective-permute-start | bytes 73736 | tf_op jit(solution)/shard_map/ppermute | solution.py:285
  25.9 3.4 %collective-permute-done.5.there = bf16[32,384]{1,0:T(8,128)(2,1)S(1)} collective-permute-done((bf16[32,384]{1,0:T(8,128)(2,1)S(1)}, bf16[32,384]{1,0:T(8,128)(2,1)S(1)}, u32[]{:S(2)}, u32[]{:S(2)}) %collective-permute-start.5) | collective-permute-done | bytes 24608 | tf_op jit(solution)/shard_map/ppermute | solution.py:285
  29.3 4.7 %collective-permute-start.6 = (bf16[32,384]{1,0:T(8,128)(2,1)S(1)}, bf16[32,384]{1,0:T(8,128)(2,1)S(1)}, u32[]{:S(2)}, u32[]{:S(2)}) collective-permute-start(bf16[32,384]{1,0:T(8,128)(2,1)S(1)} %add_parts.5.here), channel_id=1, source_target_pairs={{0,8},{8,0},{16,24},{24,16},{1,9},{9,1},{17,25},{25,17},{2,10},{10... | collective-permute-start | bytes 73736 | tf_op jit(solution)/shard_map/ppermute | solution.py:285
  34.0 1.8 %collective-permute-done.6.there = bf16[32,384]{1,0:T(8,128)(2,1)S(1)} collective-permute-done((bf16[32,384]{1,0:T(8,128)(2,1)S(1)}, bf16[32,384]{1,0:T(8,128)(2,1)S(1)}, u32[]{:S(2)}, u32[]{:S(2)}) %collective-permute-start.6) | collective-permute-done | bytes 24608 | tf_op jit(solution)/shard_map/ppermute | solution.py:285
  35.8 3.3 %collective-permute-start.7 = (bf16[32,384]{1,0:T(8,128)(2,1)S(1)}, bf16[32,384]{1,0:T(8,128)(2,1)S(1)}, u32[]{:S(2)}, u32[]{:S(2)}) collective-permute-start(bf16[32,384]{1,0:T(8,128)(2,1)S(1)} %add_parts.6.here), channel_id=1, source_target_pairs={{0,16},{8,24},{16,0},{24,8},{1,17},{9,25},{17,1},{25,9},{2,18},{10... | collective-permute-start | bytes 73736 | tf_op jit(solution)/shard_map/ppermute | solution.py:285
  39.1 1.8 %collective-permute-done.7.there = bf16[32,384]{1,0:T(8,128)(2,1)S(1)} collective-permute-done((bf16[32,384]{1,0:T(8,128)(2,1)S(1)}, bf16[32,384]{1,0:T(8,128)(2,1)S(1)}, u32[]{:S(2)}, u32[]{:S(2)}) %collective-permute-start.7) | collective-permute-done | bytes 24608 | tf_op jit(solution)/shard_map/ppermute | solution.py:285
  40.9 1.5 %collective-permute-start.8 = (bf16[32,384]{1,0:T(8,128)(2,1)S(1)}, bf16[32,384]{1,0:T(8,128)(2,1)S(1)}, u32[]{:S(2)}, u32[]{:S(2)}) collective-permute-start(bf16[32,384]{1,0:T(8,128)(2,1)S(1)} %add_parts.7.total), channel_id=1, source_target_pairs={{0,1},{1,0},{2,3},{3,2},{4,5},{5,4},{6,7},{7,6},{8,9},{9,8},{10,11... | collective-permute-start | bytes 73736 | tf_op jit(solution)/shard_map/ppermute | solution.py:285
  42.5 1.6 %closure.1 = bf16[1,16,8,8,128]{4,3,2,1,0:T(8,128)(2,1)} custom-call(bf16[12,192,128]{2,1,0:T(8,128)(2,1)S(1)} %get-tuple-element.48.hidden, bf16[128,1920]{1,0:T(8,128)(2,1)S(1)} %get-tuple-element.54.t2, f32[128,1024]{1,0:T(8,128)S(1)} %get-tuple-element.55.b2), custom_call_target="tpu_custom_call" | custom-call | flops 1000000000 | bytes 1000000 | tf_op jit(solution)/shard_map/closure/pallas_call | solution.py:353
  44.0 0.8 %collective-permute-done.8.last = bf16[32,384]{1,0:T(8,128)(2,1)S(1)} collective-permute-done((bf16[32,384]{1,0:T(8,128)(2,1)S(1)}, bf16[32,384]{1,0:T(8,128)(2,1)S(1)}, u32[]{:S(2)}, u32[]{:S(2)}) %collective-permute-start.8) | collective-permute-done | bytes 24608 | tf_op jit(solution)/shard_map/ppermute | solution.py:285
  44.8 0.8 %finish.1 = (f32[128,27]{1,0:T(8,128)}, f32[256,27]{1,0:T(8,128)}, f32[1,16]{1,0:T(1,128)}) custom-call(bf16[32,384]{1,0:T(8,128)(2,1)S(1)} %add_parts.7.total, bf16[32,384]{1,0:T(8,128)(2,1)S(1)} %collective-permute-done.8.last), custom_call_target="tpu_custom_call" | custom-call | flops 10000000 | bytes 1000000 | tf_op jit(solution)/shard_map/finish/pallas_call | solution.py:364
  (33 shorter events, 0.2 us)
Async XLA Ops:
  0.6 11.4 %copy-start.15 = (f32[1,256]{1,0:T(1,128)S(1)}, f32[1,256]{1,0:T(1,128)}, u32[]{:S(2)}) copy-start(f32[1,256]{1,0:T(1,128)} %constant.48.clone.y2r) | copy-start | bytes 3076
  0.6 11.4 %copy-start.14 = (f32[1,384]{1,0:T(1,128)S(1)}, f32[1,384]{1,0:T(1,128)}, u32[]{:S(2)}) copy-start(f32[1,384]{1,0:T(1,128)} %constant.47.clone.y2o) | copy-start | bytes 4612
  0.7 11.4 %copy-start.16 = (f32[1,256]{1,0:T(1,128)S(1)}, f32[1,256]{1,0:T(1,128)}, u32[]{:S(2)}) copy-start(f32[1,256]{1,0:T(1,128)} %constant.46.clone.y1r) | copy-start | bytes 3076
  0.7 11.4 %copy-start.17 = (f32[1,256]{1,0:T(1,128)S(1)}, f32[1,256]{1,0:T(1,128)}, u32[]{:S(2)}) copy-start(f32[1,256]{1,0:T(1,128)} %constant.45.clone.y1o) | copy-start | bytes 3076
  0.7 11.4 %copy-start.10 = (bf16[48,256]{1,0:T(8,128)(2,1)S(1)}, bf16[48,256]{1,0:T(8,128)(2,1)}, u32[]{:S(2)}) copy-start(bf16[48,256]{1,0:T(8,128)(2,1)} %constant.43.clone.e2r) | copy-start | bytes 73732
  0.7 1.0 %copy-start = (bf16[1,16,8,8,128]{4,3,2,1,0:T(8,128)(2,1)S(1)}, bf16[1,16,8,8,128]{4,3,2,1,0:T(8,128)(2,1)}, u32[]{:S(2)}) copy-start(bf16[1,16,8,8,128]{4,3,2,1,0:T(8,128)(2,1)} %cot.5) | copy-start | bytes 786436
  1.7 0.9 %copy-start.2 = (bf16[1,8,8,8,128]{4,3,2,1,0:T(8,128)(2,1)S(1)}, bf16[1,8,8,8,128]{4,3,2,1,0:T(8,128)(2,1)}, u32[]{:S(2)}) copy-start(bf16[1,8,8,8,128]{4,3,2,1,0:T(8,128)(2,1)} %fields.5) | copy-start | bytes 393220
  2.6 9.0 %copy-start.27 = (bf16[27,16,16]{0,2,1:T(8,128)(2,1)S(1)}, bf16[27,16,16]{0,2,1:T(8,128)(2,1)}, u32[]{:S(2)}) copy-start(bf16[27,16,16]{0,2,1:T(8,128)(2,1)} %param.29) | copy-start | bytes 41476
  2.6 9.6 %copy-start.4 = (f32[192,1]{1,0:T(8,128)S(1)}, f32[192,1]{1,0:T(8,128)}, u32[]{:S(2)}) copy-start(f32[192,1]{1,0:T(8,128)} %constant.49.clone.rows_y) | copy-start | bytes 2308
  2.6 9.6 %copy-start.7 = (bf16[192,16]{1,0:T(8,128)(2,1)S(1)}, bf16[192,16]{1,0:T(8,128)(2,1)}, u32[]{:S(2)}) copy-start(bf16[192,16]{1,0:T(8,128)(2,1)} %constant.44.clone.expand) | copy-start | bytes 18436
  2.6 9.6 %copy-start.9 = (bf16[48,384]{1,0:T(8,128)(2,1)S(1)}, bf16[48,384]{1,0:T(8,128)(2,1)}, u32[]{:S(2)}) copy-start(bf16[48,384]{1,0:T(8,128)(2,1)} %constant.42.clone.e2o) | copy-start | bytes 110596
  2.6 9.6 %copy-start.11 = (bf16[24,256]{1,0:T(8,128)(2,1)S(1)}, bf16[24,256]{1,0:T(8,128)(2,1)}, u32[]{:S(2)}) copy-start(bf16[24,256]{1,0:T(8,128)(2,1)} %constant.41.clone.e1r) | copy-start | bytes 36868
  2.6 9.6 %copy-start.12 = (bf16[24,256]{1,0:T(8,128)(2,1)S(1)}, bf16[24,256]{1,0:T(8,128)(2,1)}, u32[]{:S(2)}) copy-start(bf16[24,256]{1,0:T(8,128)(2,1)} %constant.40.clone.e1o) | copy-start | bytes 36868
  2.6 9.6 %copy-start.18 = (f32[16]{0:T(128)S(1)}, f32[16]{0:T(128)}, u32[]{:S(2)}) copy-start(f32[16]{0:T(128)} %param.28) | copy-start | bytes 196
  2.7 12.1 %copy-start.1 = (bf16[1,16,8,8,128]{4,3,2,1,0:T(8,128)(2,1)S(1)}, bf16[1,16,8,8,128]{4,3,2,1,0:T(8,128)(2,1)}, u32[]{:S(2)}) copy-start(bf16[1,16,8,8,128]{4,3,2,1,0:T(8,128)(2,1)} %cot.5) | copy-start | bytes 786436
  2.7 12.1 %copy-start.3 = (bf16[1,8,8,8,128]{4,3,2,1,0:T(8,128)(2,1)S(1)}, bf16[1,8,8,8,128]{4,3,2,1,0:T(8,128)(2,1)}, u32[]{:S(2)}) copy-start(bf16[1,8,8,8,128]{4,3,2,1,0:T(8,128)(2,1)} %fields.5) | copy-start | bytes 393220
  2.7 6.6 %collective-permute-start = (bf16[512,128]{1,0:T(8,128)(2,1)S(1)}, bf16[512,128]{1,0:T(8,128)(2,1)S(1)}, u32[]{:S(2)}, u32[]{:S(2)}) collective-permute-start(bf16[512,128]{1,0:T(8,128)(2,1)S(1)} %get-tuple-element.32), channel_id=1, source_target_pairs={{0,8},{8,0},{16,24},{24,16},{1,9},{9,1},{17,25},{25,17},{2,10},{10... | collective-permute-start | bytes 393224 | tf_op jit(solution)/shard_map/ppermute | solution.py:281
  5.8 3.5 %collective-permute-start.1 = (bf16[512,128]{1,0:T(8,128)(2,1)S(1)}, bf16[512,128]{1,0:T(8,128)(2,1)S(1)}, u32[]{:S(2)}, u32[]{:S(2)}) collective-permute-start(bf16[512,128]{1,0:T(8,128)(2,1)S(1)} %get-tuple-element.33), channel_id=1, source_target_pairs={{0,0},{8,16},{16,8},{24,24},{1,1},{9,17},{17,9},{25,25},{2,2},{10,... | collective-permute-start | bytes 393224 | tf_op jit(solution)/shard_map/ppermute | solution.py:280
  9.6 7.7 %collective-permute-start.2 = (bf16[896,128]{1,0:T(8,128)(2,1)S(1)}, bf16[896,128]{1,0:T(8,128)(2,1)S(1)}, u32[]{:S(2)}, u32[]{:S(2)}) collective-permute-start(bf16[896,128]{1,0:T(8,128)(2,1)S(1)} %get-tuple-element.36), channel_id=1, source_target_pairs={{0,2},{2,0},{4,6},{6,4},{1,3},{3,1},{5,7},{7,5},{8,10},{10,8},{12,... | collective-permute-start | bytes 688136 | tf_op jit(solution)/shard_map/ppermute | solution.py:281
  9.7 7.7 %collective-permute-start.3 = (bf16[896,128]{1,0:T(8,128)(2,1)S(1)}, bf16[896,128]{1,0:T(8,128)(2,1)S(1)}, u32[]{:S(2)}, u32[]{:S(2)}) collective-permute-start(bf16[896,128]{1,0:T(8,128)(2,1)S(1)} %get-tuple-element.37), channel_id=1, source_target_pairs={{0,0},{2,4},{4,2},{6,6},{1,1},{3,5},{5,3},{7,7},{8,8},{10,12},{12,... | collective-permute-start | bytes 688136 | tf_op jit(solution)/shard_map/ppermute | solution.py:280
  13.8 1.0 %copy-start.20 = (f32[192,1536]{1,0:T(8,128)}, f32[192,1536]{1,0:T(8,128)S(1)}, u32[]{:S(2)}) copy-start(f32[192,1536]{1,0:T(8,128)S(1)} %get-tuple-element.41.b1) | copy-start | bytes 3538948
  14.8 2.6 %copy-start.21 = (bf16[128,768]{1,0:T(8,128)(2,1)S(1)}, bf16[128,768]{1,0:T(8,128)(2,1)}, u32[]{:S(2)}) copy-start(bf16[128,768]{1,0:T(8,128)(2,1)} %constant.53.clone.rep2) | copy-start | bytes 589828
  14.8 2.6 %copy-start.22 = (bf16[640,128]{1,0:T(8,128)(2,1)S(1)}, bf16[640,128]{1,0:T(8,128)(2,1)}, u32[]{:S(2)}) copy-start(bf16[640,128]{1,0:T(8,128)(2,1)} %constant.51.clone.e2t) | copy-start | bytes 491524
  14.8 2.6 %copy-start.23 = (bf16[128,384]{1,0:T(8,128)(2,1)S(1)}, bf16[128,384]{1,0:T(8,128)(2,1)}, u32[]{:S(2)}) copy-start(bf16[128,384]{1,0:T(8,128)(2,1)} %constant.52.clone.rep1) | copy-start | bytes 294916
  14.8 2.6 %copy-start.24 = (bf16[384,128]{1,0:T(8,128)(2,1)S(1)}, bf16[384,128]{1,0:T(8,128)(2,1)}, u32[]{:S(2)}) copy-start(bf16[384,128]{1,0:T(8,128)(2,1)} %constant.50.clone.e1t) | copy-start | bytes 294916
  14.8 2.6 %copy-start.25 = (f32[1,640]{1,0:T(1,128)S(1)}, f32[1,640]{1,0:T(1,128)}, u32[]{:S(2)}) copy-start(f32[1,640]{1,0:T(1,128)} %constant.55.clone.y2) | copy-start | bytes 7684
  14.9 2.6 %copy-start.26 = (f32[1,384]{1,0:T(1,128)S(1)}, f32[1,384]{1,0:T(1,128)}, u32[]{:S(2)}) copy-start(f32[1,384]{1,0:T(1,128)} %constant.54.clone.y1) | copy-start | bytes 4612
  17.4 7.2 %copy-start.5 = (f32[192,1]{1,0:T(8,128)S(1)}, f32[192,1]{1,0:T(8,128)}, u32[]{:S(2)}) copy-start(f32[192,1]{1,0:T(8,128)} %constant.59.clone.rows_y) | copy-start | bytes 2308
  17.5 7.2 %copy-start.6 = (bf16[48,640]{1,0:T(8,128)(2,1)S(1)}, bf16[48,640]{1,0:T(8,128)(2,1)}, u32[]{:S(2)}) copy-start(bf16[48,640]{1,0:T(8,128)(2,1)} %constant.56.clone.e2) | copy-start | bytes 184324
  17.5 7.2 %copy-start.8 = (bf16[192,16]{1,0:T(8,128)(2,1)S(1)}, bf16[192,16]{1,0:T(8,128)(2,1)}, u32[]{:S(2)}) copy-start(bf16[192,16]{1,0:T(8,128)(2,1)} %constant.57.clone.expand) | copy-start | bytes 18436
  17.5 7.2 %copy-start.13 = (f32[1,640]{1,0:T(1,128)S(1)}, f32[1,640]{1,0:T(1,128)}, u32[]{:S(2)}) copy-start(f32[1,640]{1,0:T(1,128)} %constant.58.clone.y2) | copy-start | bytes 7684
  17.5 7.2 %copy-start.19 = (f32[16]{0:T(128)S(1)}, f32[16]{0:T(128)}, u32[]{:S(2)}) copy-start(f32[16]{0:T(128)} %param.30) | copy-start | bytes 196
  21.2 4.2 %collective-permute-start.4 = (f32[32,384]{1,0:T(8,128)S(1)}, f32[32,384]{1,0:T(8,128)S(1)}, u32[]{:S(2)}, u32[]{:S(2)}) collective-permute-start(f32[32,384]{1,0:T(8,128)S(1)} %get-tuple-element.50.here), channel_id=1, source_target_pairs={{0,2},{2,0},{4,6},{6,4},{1,3},{3,1},{5,7},{7,5},{8,10},{10,8},{12,... | collective-permute-start | bytes 147464 | tf_op jit(solution)/shard_map/ppermute | solution.py:285
  25.4 3.9 %collective-permute-start.5 = (bf16[32,384]{1,0:T(8,128)(2,1)S(1)}, bf16[32,384]{1,0:T(8,128)(2,1)S(1)}, u32[]{:S(2)}, u32[]{:S(2)}) collective-permute-start(bf16[32,384]{1,0:T(8,128)(2,1)S(1)} %add_parts.4.here), channel_id=1, source_target_pairs={{0,4},{2,6},{4,0},{6,2},{1,5},{3,7},{5,1},{7,3},{8,12},{10,14},{12... | collective-permute-start | bytes 73736 | tf_op jit(solution)/shard_map/ppermute | solution.py:285
  29.3 6.5 %collective-permute-start.6 = (bf16[32,384]{1,0:T(8,128)(2,1)S(1)}, bf16[32,384]{1,0:T(8,128)(2,1)S(1)}, u32[]{:S(2)}, u32[]{:S(2)}) collective-permute-start(bf16[32,384]{1,0:T(8,128)(2,1)S(1)} %add_parts.5.here), channel_id=1, source_target_pairs={{0,8},{8,0},{16,24},{24,16},{1,9},{9,1},{17,25},{25,17},{2,10},{10... | collective-permute-start | bytes 73736 | tf_op jit(solution)/shard_map/ppermute | solution.py:285
  35.8 5.1 %collective-permute-start.7 = (bf16[32,384]{1,0:T(8,128)(2,1)S(1)}, bf16[32,384]{1,0:T(8,128)(2,1)S(1)}, u32[]{:S(2)}, u32[]{:S(2)}) collective-permute-start(bf16[32,384]{1,0:T(8,128)(2,1)S(1)} %add_parts.6.here), channel_id=1, source_target_pairs={{0,16},{8,24},{16,0},{24,8},{1,17},{9,25},{17,1},{25,9},{2,18},{10... | collective-permute-start | bytes 73736 | tf_op jit(solution)/shard_map/ppermute | solution.py:285
  40.9 3.9 %collective-permute-start.8 = (bf16[32,384]{1,0:T(8,128)(2,1)S(1)}, bf16[32,384]{1,0:T(8,128)(2,1)S(1)}, u32[]{:S(2)}, u32[]{:S(2)}) collective-permute-start(bf16[32,384]{1,0:T(8,128)(2,1)S(1)} %add_parts.7.total), channel_id=1, source_target_pairs={{0,1},{1,0},{2,3},{3,2},{4,5},{5,4},{6,7},{7,6},{8,9},{9,8},{10,11... | collective-permute-start | bytes 73736 | tf_op jit(solution)/shard_map/ppermute | solution.py:285

commit v7 on v6

--- a/solution.py
+++ b/solution.py
@@ -16,29 +16,59 @@
 FAR = 100
 
 
-def block(channels, width, y_first=False):
-    own = (np.repeat(np.arange(channels), 8), np.tile(np.arange(8), channels))
-    if y_first:
-        own = (np.tile(np.arange(channels), 8), np.repeat(np.arange(8), channels))
-    rim_c = np.concatenate([np.repeat(np.arange(channels), width)] * 2)
-    rim_y = np.concatenate([np.tile(np.arange(-width, 0), channels), np.tile(np.arange(8, 8 + width), channels)])
-    return own, (rim_c, rim_y)
-
-
-def lanes_of(channels, total, places):
-    e = np.zeros((3 * channels, total), np.float32)
+def natural(n):
+    return n // 8, n % 8
+
+
+def y_first(n):
+    return n % CH, n // CH
+
+
+def rim(width):
+    def of(n):
+        side, n = n // 32, n % 32
+        return n // width, n % width + side * (8 + width) - width
+    return of
+
+
+def table(channels, total, places):
+    e = np.zeros((total, 128), np.float32)
     ys = np.full((1, total), FAR, np.float32)
     for c in range(3):
-        for (ch, y), start, step in places:
-            at = start + c * step + np.arange(len(ch))
-            e[c * channels + ch, at] = 1
+        for of, count, start in places:
+            ch, y = of(np.arange(count))
+            at = start + c * (128 if start == 0 or channels == CI else 64) + np.arange(count)
+            e[at, c * channels + ch] = 1
             ys[0, at] = y
     return e, ys
 
 
-def rows_of(own, rim):
-    ch, y = (np.concatenate([a, b]) for a, b in zip(own, rim))
-    return np.eye(CH, dtype=np.float32)[ch], y[:, None].astype(np.float32)
+def iota(rows, columns):
+    return [lax.broadcasted_iota(jnp.int32, (rows, columns), d) for d in range(2)]
+
+
+def one_hot(where):
+    return jnp.where(where, 1.0, 0.0).astype(BF16)
+
+
+def lane_y(of, width, step):
+    lane = lax.broadcasted_iota(jnp.int32, (1, width), 1)
+    return jnp.where(lane < 3 * step, of(lane % step)[1], FAR)
+
+
+def place(rows, wanted, of, side=None):
+    row, lane = iota(rows, 128)
+    if side is None:
+        return one_hot(of(lane)[0] == wanted(row))
+    return one_hot((of(lane % 64)[0] == wanted(row)) & (lane // 64 == side))
+
+
+def row_table(rows, own):
+    row, lane = iota(rows, CH)
+    own_c, own_y = own(row)
+    rim_c, rim_y = rim(2)(row - 128)
+    channel, y = jnp.where(row < 128, own_c, rim_c), jnp.where(row < 128, own_y, rim_y)
+    return one_hot(channel == lane), y[:, :1]
 
 
 def plane(ref, x):
@@ -66,34 +96,33 @@
     return jnp.where(below, low, 0.0), jnp.where(above, high, 0.0)
 
 
-def strips(here, width, near, far, at):
+def pack_kernel(fields, cot, near, far, f_rows, c_rows):
     up_first = lax.axis_index("stream") % 2 == 0
-    count, rows = here.shape[2], here.shape[1] * here.shape[3]
-    for n in range(width):
-        low, high = plane(here, n), plane(here, count - width + n)
-        part = slice(at + n * rows, at + (n + 1) * rows)
-        near[part] = jnp.where(up_first, high, low).astype(BF16)
-        far[part] = jnp.where(up_first, low, high).astype(BF16)
-
-
-def pack_kernel(fields, cot, near, far):
-    strips(fields, 4, near, far, 0)
-    strips(cot, 2, near, far, 256)
+    count, at = fields.shape[2], 0
+    for ref, out, width in ((fields, f_rows, 4), (cot, c_rows, 2)):
+        rows = [plane(ref, x) for x in range(count)]
+        for x, v in enumerate(rows):
+            out[x] = v.astype(BF16)
+        for low, high in zip(rows[:width], rows[count - width:]):
+            part = slice(at, at + low.shape[0])
+            near[part] = jnp.where(up_first, high, low).astype(BF16)
+            far[part] = jnp.where(up_first, low, high).astype(BF16)
+            at += low.shape[0]
 
 
 def x_planes(count, fields, cot, xnear, xfar, size):
     index = lax.axis_index("stream")
-    inner = [plane(fields, x) for x in range(count)]
+    inner = [fields[x].astype(F32) for x in range(count)]
     rims = [sides(index, size, xnear[n * 64:(n + 1) * 64], xfar[n * 64:(n + 1) * 64]) for n in range(4)]
     f = [low for low, _ in rims] + inner + [high for _, high in rims]
-    inner = [plane(cot, x) for x in range(count)]
+    inner = [cot[x].astype(F32) for x in range(count)]
     rims = [sides(index, size, xnear[256 + n * 128:384 + n * 128], xfar[256 + n * 128:384 + n * 128]) for n in range(2)]
     return f, [low for low, _ in rims] + inner + [high for _, high in rims]
 
 
-def join_kernel(counts, fields, cot, xnear, xfar, near, far):
+def join_kernel(counts, xfar, xnear, fields, cot, near, far):
     up_first = lax.axis_index("radial") % 2 == 0
-    f, c = x_planes(fields.shape[2], fields, cot, xnear, xfar, counts[0])
+    f, c = x_planes(fields.shape[0], fields, cot, xnear, xfar, counts[0])
     at = 0
     for rows, pick in ((f, pick_rows(CI, 4)), (c, pick_rows(CH, 2))):
         for v in rows:
@@ -103,32 +132,72 @@
             at += 32
 
 
-def band(w, e, expand, ys, rows_y, t):
-    rows, width = t.shape[0], e.shape[1]
-    wide = jnp.dot(w[...], e[...], preferred_element_type=F32).astype(BF16)
+def spread(w, by_row, flip):
+    taps = jnp.transpose(w[...].astype(F32))
+    width = taps.shape[1]
+    row = lax.broadcasted_iota(jnp.int32, (CH, width), 0)
+    lane = lax.broadcasted_iota(jnp.int32, (CH, width), 1)
+    mine = row == (lane // (width // CH) if by_row else lane % CH)
+    found = []
+    for c in range(3):
+        rows = []
+        for ab in range(9):
+            t = 26 - (ab * 3 + c) if flip else ab * 3 + c
+            rows.append(jnp.where(mine, jnp.broadcast_to(taps[t:t + 1], (CH, width)), 0.0))
+        found.append(jnp.concatenate(rows, axis=0).astype(BF16))
+    return found
+
+
+def dots(pairs):
+    total = None
+    for v, w in pairs:
+        part = jnp.dot(v, w, preferred_element_type=F32)
+        total = part if total is None else total + part
+    return total.astype(BF16)
+
+
+def halves(parts, wanted, of):
+    left, right = (place(parts[0].shape[1], wanted, of, side) for side in range(2))
+    return jnp.concatenate([dots([(parts[0], left), (parts[1], right)]), dots([(parts[2], left)])], axis=1)
+
+
+def wholes(parts, wanted, of):
+    at = place(parts[0].shape[1], wanted, of)
+    return jnp.concatenate([dots([(v, at)]) for v in parts], axis=1)
+
+
+def band(wide, expand, ys, rows_y, t):
+    rows, width = t.shape[0], wide.shape[1]
     for a in range(3):
         total = jnp.zeros((rows, width), F32)
         for b in range(3):
             part = jnp.dot(expand[:rows], wide[(a * 3 + b) * CH:(a * 3 + b + 1) * CH], preferred_element_type=F32)
-            total = jnp.where(ys[...] == rows_y[:rows] + float(2 * (b - 1)), part, total)
+            total = jnp.where(ys == rows_y[:rows] + 2 * (b - 1), part, total)
         t[:, a * width:(a + 1) * width] = total.astype(BF16)
 
 
 def repeat_bias(bias, expand, out):
-    column = jnp.sum(expand[:out.shape[0]].astype(F32) * bias[...], axis=1, keepdims=True)
+    column = jnp.sum(expand.astype(F32) * bias[...], axis=1, keepdims=True)
     out[...] = jnp.broadcast_to(column, out.shape)
 
 
-def band_first_kernel(w1, wb, bias, e1o, e1r, e2o, e2r, expand, y1o, y1r, y2o, y2r, rows_y, t1o, t1r, tbo, tbr, b1):
-    band(w1, e1o, expand, y1o, rows_y, t1o)
-    band(w1, e1r, expand, y1r, rows_y, t1r)
-    band(wb, e2o, expand, y2o, rows_y, tbo)
-    band(wb, e2r, expand, y2r, rows_y, tbr)
+def band_first_kernel(w1, w2, bias, t1o, t1r, tbo, tbr, b1):
+    expand, rows_y = row_table(192, y_first)
+    parts = spread(w1, True, False)
+    band(halves(parts, lambda n: n % CI, natural), expand, lane_y(natural, 256, 64), rows_y, t1o)
+    band(halves(parts, lambda n: n % CI, rim(4)), expand, lane_y(rim(4), 256, 64), rows_y, t1r)
+    parts = spread(w2, False, True)
+    band(wholes(parts, lambda n: n // CH, natural), expand, lane_y(natural, 384, 128), rows_y, tbo)
+    band(halves(parts, lambda n: n // CH, rim(2)), expand, lane_y(rim(2), 256, 64), rows_y, tbr)
     repeat_bias(bias, expand, b1)
 
 
-def band_second_kernel(w2, bias, e2, expand, y2, rows_y, t2, b2):
-    band(w2, e2, expand, y2, rows_y, t2)
+def band_second_kernel(w2, bias, t2, b2):
+    expand, rows_y = row_table(128, natural)
+    parts = spread(w2, True, False)
+    wide = [wholes(parts, lambda n: n % CH, y_first), halves(parts, lambda n: n % CH, rim(2))]
+    ys = jnp.concatenate([lane_y(y_first, 384, 128), lane_y(rim(2), 256, 64)], axis=1)
+    band(jnp.concatenate(wide, axis=1), expand, ys, rows_y, t2)
     repeat_bias(bias, expand, b2)
 
 
@@ -151,15 +220,15 @@
     return jnp.concatenate([ref[:, a * 256:a * 256 + lanes] for a in range(3)], axis=0)
 
 
-def own_kernel(counts, fields, cot, xnear, xfar, t1, tb, b1, fs, cs, pre, back):
-    count = fields.shape[2]
+def own_kernel(counts, xfar, xnear, fields, cot, t1, tb, b1, fs, cs, pre, back):
+    count = fields.shape[0]
     f, c = x_planes(count, fields, cot, xnear, xfar, counts[0])
     for ref, rows in ((fs, f), (cs, c)):
         for p, v in enumerate(rows):
             for n, piece in enumerate(shifted(v)):
                 ref[n * v.shape[0]:(n + 1) * v.shape[0], p * Z:(p + 1) * Z] = piece
     fs[192:] = jnp.zeros((64, fs.shape[1]), BF16)
-    pre[...] = jnp.dot(t1[...], stacked(fs, pre.shape[1]), preferred_element_type=F32) + b1[...]
+    pre[...] = jnp.dot(t1[...], stacked(fs, pre.shape[1]), preferred_element_type=F32) + b1[:, :1]
     back[...] = jnp.dot(tb[...], stacked(cs, back.shape[1]), preferred_element_type=F32)
 
 
@@ -169,7 +238,7 @@
     return jnp.dot(high, w, preferred_element_type=F32) + jnp.dot(low, w, preferred_element_type=F32)
 
 
-def rim_kernel(counts, rnear, rfar, fs, cs, pre_own, back_own, t1, tb, e1t, e2t, rep1, rep2, y1, y2,
+def rim_kernel(counts, rfar, rnear, fs, cs, pre_own, back_own, t1, tb, e1t, e2t, rep1, rep2, y1, y2,
                hidden_out, payload, fr, cr, taps):
     count = hidden_out.shape[0] - 4
     lanes = count * Z
@@ -238,7 +307,7 @@
     count = closure.shape[2]
     for p in range(count + 4):
         store_wide(hs, p, hidden[p].astype(F32))
-    out = (jnp.dot(t2[...], stacked(hs, count * Z), preferred_element_type=F32) + b2[...]).astype(BF16)
+    out = (jnp.dot(t2[...], stacked(hs, count * Z), preferred_element_type=F32) + b2[:, :1]).astype(BF16)
     for x in range(count):
         closure[0, :, x] = out[:, x * Z:(x + 1) * Z].reshape(CH, 8, Z)
 
@@ -264,7 +333,7 @@
         out_shape=outs,
         **specs,
         scratch_shapes=list(scratch),
-        compiler_params=pltpu.CompilerParams(vmem_limit_bytes=48 * 1024 * 1024),
+        compiler_params=pltpu.CompilerParams(vmem_limit_bytes=32 * 1024 * 1024),
         cost_estimate=pl.CostEstimate(flops=flops, bytes_accessed=1_000_000, transcendentals=0),
         name=name,
     )
@@ -290,19 +359,8 @@
 
 
 def local(fields, first_weight, first_bias, second_weight, second_bias, cotangent):
-    own, rim = block(CI, 4)
-    e1, y1 = lanes_of(CI, 384, ((own, 0, 128), (rim, 64, 128)))
-    e1o, y1o = lanes_of(CI, 256, ((own, 0, 64),))
-    e1r, y1r = lanes_of(CI, 256, ((rim, 0, 64),))
-    own, rim = block(CH, 2)
-    e2, y2 = lanes_of(CH, 640, ((own, 0, 128), (rim, 384, 64)))
-    e2o, y2o, e2r, y2r = e2[:, :384], y2[:, :384], e2[:, 384:], y2[:, 384:]
-    expand2, rows_y2 = rows_of(own, rim)
-    own, _ = block(CH, 2, y_first=True)
-    e2h, y2h = lanes_of(CH, 640, ((own, 0, 128), (rim, 384, 64)))
-    expand1, rows_y1 = rows_of(own, rim)
-    e1t, e2t = np.zeros((384, 128), np.float32), np.zeros((640, 128), np.float32)
-    e1t[:, :3 * CI], e2t[:, :3 * CH] = e1.T, e2.T
+    e1t, y1 = table(CI, 384, ((natural, 64, 0), (rim(4), 64, 64)))
+    e2t, y2 = table(CH, 640, ((natural, 128, 0), (rim(2), 64, 384)))
     rep1, rep2 = np.zeros((128, 384), np.float32), np.zeros((128, 768), np.float32)
     for c in range(3):
         rep1[c * CI:(c + 1) * CI, c * 128:(c + 1) * 128] = np.tile(np.eye(CI), (1, CH))
@@ -312,42 +370,46 @@
         return [jnp.asarray(v, dtype) for v in arrays]
 
     planes = fields.shape[2]
-
-    w1 = first_weight.reshape(3, 3, 3, CH, CI).transpose(0, 1, 3, 2, 4).reshape(9 * CH, 3 * CI)
-    near, far = call(pack_kernel, (shape(512, Z),) * 2, "pack_strips")(fields, cotangent)
+    w1 = first_weight.transpose(1, 2, 0).reshape(CH * CI, 27)
+    w2 = second_weight.transpose(1, 2, 0).reshape(CH * CH, 27)
+    near, far, f_rows, c_rows = call(
+        pack_kernel,
+        (shape(512, Z), shape(512, Z), shape(planes, CI * 8, Z), shape(planes, CH * 8, Z)),
+        "pack_strips",
+        flops=4_000_000_000,
+    )(fields, cotangent)
     xnear, xfar = exchange(near, far, "stream")
     wide = (planes + 4) * Z
     counts = (lax.axis_size("stream"), lax.axis_size("radial"))
-    near, far = call(functools.partial(join_kernel, counts), (shape((2 * planes + 12) * 32, Z),) * 2, "join_strips")(
-        fields, cotangent, xnear, xfar)
-    near, far, weight = lax.optimization_barrier((near, far, second_weight))
-    rnear, rfar = exchange(near, far, "radial")
-    wb = weight.reshape(3, 3, 3, CH, CH)[::-1, ::-1, ::-1].transpose(0, 1, 4, 2, 3).reshape(9 * CH, 3 * CH)
     t1o, t1r, tbo, tbr, b1 = call(
         band_first_kernel,
-        (shape(192, 768), shape(192, 768), shape(128, 1152), shape(128, 768), shape(192, wide, dtype=F32)),
+        (shape(192, 768), shape(192, 768), shape(128, 1152), shape(128, 768), shape(192, 128, dtype=F32)),
         "band_first",
-    )(w1, wb, first_bias[None], *const(e1o, e1r, e2o, e2r, expand1), *const(y1o, y1r, y2o, y2r, rows_y1, dtype=F32))
+        flops=4_000_000_000,
+    )(w1, w2, first_bias[None])
+    xfar, xnear, t1o, tbo = lax.optimization_barrier((xfar, xnear, t1o, tbo))
+    near, far = call(functools.partial(join_kernel, counts), (shape((2 * planes + 12) * 32, Z),) * 2, "join_strips")(
+        xfar, xnear, f_rows, c_rows)
+    rnear, rfar = exchange(near, far, "radial")
     fs, cs, pre, back = call(
         functools.partial(own_kernel, counts),
         (shape(256, wide + 4 * Z), shape(384, wide), shape(192, wide, dtype=F32), shape(128, planes * Z, dtype=F32)),
         "own_rows",
         flops=1_000_000_000,
-    )(fields, cotangent, xnear, xfar, t1o, tbo, b1)
+    )(xfar, xnear, f_rows, c_rows, t1o, tbo, b1)
     hidden, payload = call(
         functools.partial(rim_kernel, counts),
         (shape(planes + 4, 192, Z), shape(32, 384, dtype=F32)),
         "gradients",
         (pltpu.VMEM((256, wide + 4 * Z), BF16), pltpu.VMEM((256, wide), BF16), pltpu.VMEM((3, 32, 128), F32)),
         flops=2_000_000_000,
-    )(rnear, rfar, fs, cs, pre, back, t1r, tbr, *const(e1t, e2t, rep1, rep2), *const(y1, y2, dtype=F32))
+    )(rfar, rnear, fs, cs, pre, back, t1r, tbr, *const(e1t, e2t, rep1, rep2), *const(y1, y2, dtype=F32))
 
     steps = [(axis, 1 << n) for axis in ("radial", "stream", "snap") for n in range((lax.axis_size(axis) - 1).bit_length())]
-    payload, weight = lax.optimization_barrier((payload, second_weight))
+    payload, w2 = lax.optimization_barrier((payload, w2))
     arrived = swap(payload, *steps[0])
-    w2 = weight.reshape(3, 3, 3, CH, CH).transpose(0, 1, 3, 2, 4).reshape(9 * CH, 3 * CH)
-    t2, b2 = call(band_second_kernel, (shape(128, 1920), shape(128, planes * Z, dtype=F32)), "band_second")(
-        w2, second_bias[None], *const(e2h, expand2), *const(y2h, rows_y2, dtype=F32))
+    t2, b2 = call(band_second_kernel, (shape(128, 1920), shape(128, 128, dtype=F32)), "band_second")(
+        w2, second_bias[None])
     payload, t2, b2 = lax.optimization_barrier((add(payload, arrived), t2, b2))
     arrived = swap(payload, *steps[1])
     closure = call(

time: 45.9 us -> 42.3 us (0.922)
  local copies, waits for them, and re-layouts: 5.05 us -> 1.92 us
  starting transfers between devices: 17.5 us -> 19.7 us
  waiting for transfers between devices: 10.7 us -> 9.28 us
  Pallas kernels: 11.2 us -> 10.3 us
    ppermute x2, starting transfers between devices: 3.16 us -> 8.84 us  [exchange(): return (lax.ppermute(near, axis, [(i, i ^ 1) for i in range(count)]), far)]
    ppermute x5, starting transfers between devices: 13 us -> 9.53 us  [swap(): lax.ppermute(v, axis, [(i, i ^ mask) for i in range(lax.axis_size(axis))])]
    unnamed x57 -> x24, local copies, waits for them, and re-layouts: 3.94 us -> 1.92 us
    ppermute x2, waiting for transfers between devices: 2.83 us -> 1.42 us  [exchange(): return (lax.ppermute(near, axis, [(i, i ^ 1) for i in range(count)]), far)]
    pallas_call x1, Pallas kernels: 2.49 us -> 1.18 us  [local(): call(functools.partial(own_kernel, counts), (shape(256, wide + 4 * Z), sh...]
    reshape x6 -> x0, local copies, waits for them, and re-layouts: 0.68 us -> none  [the longest x2 0.27 us: local(): weight.reshape(3, 3, 3, CH, CH)[::-1, ::-1, ::-1].transpose(0, 1, 4, 2, 3)]
  transfers between devices with their start and end apart: 9 -> 9, of which waited for: 5 -> 5; matrix products, arithmetic and copies ran while one was open for 4% -> 0% of each run, Pallas kernels for 14% -> 13%
where the time goes in v7:
time: 42.3 us; the launch traced here: 42.1 us
  starting transfers between devices  19.7 us (47%)
  Pallas kernels  10.3 us (24%)
  waiting for transfers between devices  9.28 us (22%)
  local copies, waits for them, and re-layouts  1.92 us (5%)
  between operations  0.82 us (2%)
    ppermute x5, starting transfers between devices, swap(): lax.ppermute(v, axis, [(i, i ^ mask) for i in range(lax.axis_size(axis))])  9.53 us
    ppermute x2, starting transfers between devices, exchange(): return (lax.ppermute(near, axis, [(i, i ^ 1) for i in range(count)]), far)  8.84 us
    ppermute x5, waiting for transfers between devices, swap(): lax.ppermute(v, axis, [(i, i ^ mask) for i in range(lax.axis_size(axis))])  7.85 us
    pallas_call x1, Pallas kernels, local(): call(functools.partial(rim_kernel, counts), (shape(planes + 4, 192, Z), s...  3.68 us
    unnamed x24, local copies, waits for them, and re-layouts  1.92 us
    pallas_call x1, Pallas kernels, local(): call(band_first_kernel, (shape(192, 768), shape(192, 768), shape(128, 115...  1.77 us
    pallas_call x1, Pallas kernels, local(): call(closure_kernel, shape(*cotangent.shape), 'closure', (pltpu.VMEM((640...  1.56 us
    ppermute x2, waiting for transfers between devices, exchange(): return (lax.ppermute(near, axis, [(i, i ^ 1) for i in range(count)]), far)  1.42 us
  transfers between devices with their start and end apart: 9, of which 5 were waited for; matrix products, arithmetic and copies ran while one was open for 0% of the time, Pallas kernels for 13%

profile of v7, /device:TPU:0, one launch (start us, length us, event | category | flops | bytes accessed | tf_op | source)
XLA Modules:
  0.0 42.1 jit_solution(7056694831804678720)
XLA Ops:
  0.6 0.0 copy-start
  0.6 0.0 copy-start.2
  0.7 1.0 %copy-done.2 = bf16[1,16,8,8,128]{4,3,2,1,0:T(8,128)(2,1)S(1)} copy-done((bf16[1,16,8,8,128]{4,3,2,1,0:T(8,128)(2,1)S(1)}, bf16[1,16,8,8,128]{4,3,2,1,0:T(8,128)(2,1)}, u32[]{:S(2)}) %copy-start.2) | copy-done | bytes 262168
  1.6 0.0 copy-start.3
  1.6 0.9 %copy-done.3 = bf16[1,8,8,8,128]{4,3,2,1,0:T(8,128)(2,1)S(1)} copy-done((bf16[1,8,8,8,128]{4,3,2,1,0:T(8,128)(2,1)S(1)}, bf16[1,8,8,8,128]{4,3,2,1,0:T(8,128)(2,1)}, u32[]{:S(2)}) %copy-start.3) | copy-done | bytes 131096
  2.5 0.0 copy-start.4
  2.5 0.0 copy-start.5
  2.5 0.1 pack_strips.1
  2.7 0.7 %collective-permute-start = (bf16[512,128]{1,0:T(8,128)(2,1)S(1)}, bf16[512,128]{1,0:T(8,128)(2,1)S(1)}, u32[]{:S(2)}, u32[]{:S(2)}) collective-permute-start(bf16[512,128]{1,0:T(8,128)(2,1)S(1)} %get-tuple-element.35), channel_id=1, source_target_pairs={{0,0},{8,16},{16,8},{24,24},{1,1},{9,17},{17,9},{25,25},{2,2},{10,... | collective-permute-start | bytes 393224 | tf_op jit(solution)/shard_map/ppermute | solution.py:349
  3.3 5.9 %collective-permute-start.1 = (bf16[512,128]{1,0:T(8,128)(2,1)S(1)}, bf16[512,128]{1,0:T(8,128)(2,1)S(1)}, u32[]{:S(2)}, u32[]{:S(2)}) collective-permute-start(bf16[512,128]{1,0:T(8,128)(2,1)S(1)} %get-tuple-element.36), channel_id=1, source_target_pairs={{0,8},{8,0},{16,24},{24,16},{1,9},{9,1},{17,25},{25,17},{2,10},{10... | collective-permute-start | bytes 393224 | tf_op jit(solution)/shard_map/ppermute | solution.py:350
  9.2 0.0 copy-done
  9.2 0.0 copy-done.4
  9.2 0.0 copy-done.5
  9.2 1.8 %band_first.1 = (bf16[192,768]{1,0:T(8,128)(2,1)S(1)}, bf16[192,768]{1,0:T(8,128)(2,1)S(1)}, bf16[128,1152]{1,0:T(8,128)(2,1)S(1)}, bf16[128,768]{1,0:T(8,128)(2,1)S(1)}, f32[192,128]{1,0:T(8,128)S(1)}) custom-call(bf16[128,27]{1,0:T(8,128)(2,1)S(1)} %bitcast.18, bf16[256,27]{1,0:T(8,128)(2,1)S(1)} %bitcast.15, f32[1,16]{1,0:T(1,128)S(1)} %bitcast.19), custom_call_target="tpu_custom_call" | custom-call | flops 4000000000 | bytes 1000000 | tf_op jit(solution)/shard_map/band_first/pallas_call | solution.py:384
  11.0 0.0 collective-permute-done.xfar
  11.0 1.4 %collective-permute-done.1.xnear = bf16[512,128]{1,0:T(8,128)(2,1)S(1)} collective-permute-done((bf16[512,128]{1,0:T(8,128)(2,1)S(1)}, bf16[512,128]{1,0:T(8,128)(2,1)S(1)}, u32[]{:S(2)}, u32[]{:S(2)}) %collective-permute-start.1) | collective-permute-done | bytes 131104 | tf_op jit(solution)/shard_map/ppermute | solution.py:350
  12.5 0.3 join_strips.1
  12.8 0.7 %collective-permute-start.2 = (bf16[896,128]{1,0:T(8,128)(2,1)S(1)}, bf16[896,128]{1,0:T(8,128)(2,1)S(1)}, u32[]{:S(2)}, u32[]{:S(2)}) collective-permute-start(bf16[896,128]{1,0:T(8,128)(2,1)S(1)} %get-tuple-element.43), channel_id=1, source_target_pairs={{0,0},{2,4},{4,2},{6,6},{1,1},{3,5},{5,3},{7,7},{8,8},{10,12},{12,... | collective-permute-start | bytes 688136 | tf_op jit(solution)/shard_map/ppermute | solution.py:349
  13.5 2.9 %collective-permute-start.3 = (bf16[896,128]{1,0:T(8,128)(2,1)S(1)}, bf16[896,128]{1,0:T(8,128)(2,1)S(1)}, u32[]{:S(2)}, u32[]{:S(2)}) collective-permute-start(bf16[896,128]{1,0:T(8,128)(2,1)S(1)} %get-tuple-element.44), channel_id=1, source_target_pairs={{0,2},{2,0},{4,6},{6,4},{1,3},{3,1},{5,7},{7,5},{8,10},{10,8},{12,... | collective-permute-start | bytes 688136 | tf_op jit(solution)/shard_map/ppermute | solution.py:350
  16.4 0.0 copy-start.6
  16.4 0.0 copy-start.7
  16.4 0.0 copy-start.8
  16.4 0.0 copy-start.9
  16.4 0.0 copy-start.10
  16.4 0.0 copy-start.11
  16.4 1.2 %own_rows.1 = (bf16[256,2048]{1,0:T(8,128)(2,1)S(1)}, bf16[384,1536]{1,0:T(8,128)(2,1)S(1)}, f32[192,1536]{1,0:T(8,128)S(1)}, f32[128,1024]{1,0:T(8,128)S(1)}) custom-call(bf16[512,128]{1,0:T(8,128)(2,1)S(1)} %collective-permute-done.xfar, bf16[512,128]{1,0:T(8,128)(2,1)S(1)} %collective-permute-done.1.xnear, ...), custom_call_target="tpu_custom_call" | custom-call | flops 1000000000 | bytes 1000000 | tf_op jit(solution)/shard_map/own_rows/pallas_call | solution.py:394
  17.6 0.0 collective-permute-done.2.rfar
  17.6 0.0 collective-permute-done.3.rnear
  17.6 0.0 copy-done.6
  17.7 0.0 copy-done.7
  17.7 0.0 copy-done.8
  17.7 0.0 copy-done.9
  17.7 0.0 copy-done.10
  17.7 0.0 copy-done.11
  17.7 0.0 copy-start.1
  17.7 3.7 %gradients.1 = (bf16[12,192,128]{2,1,0:T(8,128)(2,1)S(1)}, f32[32,384]{1,0:T(8,128)S(1)}) custom-call(bf16[896,128]{1,0:T(8,128)(2,1)S(1)} %collective-permute-done.2.rfar, bf16[896,128]{1,0:T(8,128)(2,1)S(1)} %collective-permute-done.3.rnear, bf16[256,2048]{1,0:T(8,128)(2,1)S(1)} %get-tuple-element.48.fs, bf16[384,1536]{1,0:T(8,128)(2,1)S(1)} %get-tuple-element.49.cs, ...), custom_call_target="tpu_custom_call" | custom-call | flops 2000000000 | bytes 1000000 | tf_op jit(solution)/shard_map/gradients/pallas_call | solution.py:400
  21.4 2.4 %collective-permute-start.4 = (f32[32,384]{1,0:T(8,128)S(1)}, f32[32,384]{1,0:T(8,128)S(1)}, u32[]{:S(2)}, u32[]{:S(2)}) collective-permute-start(f32[32,384]{1,0:T(8,128)S(1)} %get-tuple-element.56.here), channel_id=1, source_target_pairs={{0,2},{2,0},{4,6},{6,4},{1,3},{3,1},{5,7},{7,5},{8,10},{10,8},{12,... | collective-permute-start | bytes 147464 | tf_op jit(solution)/shard_map/ppermute | solution.py:354
  23.8 0.0 copy-done.1
  23.8 0.8 %band_second.1 = (bf16[128,1920]{1,0:T(8,128)(2,1)S(1)}, f32[128,128]{1,0:T(8,128)S(1)}) custom-call(bf16[256,27]{1,0:T(8,128)(2,1)S(1)} %bitcast.16, f32[1,16]{1,0:T(1,128)S(1)} %bitcast.17), custom_call_target="tpu_custom_call" | custom-call | flops 10000000 | bytes 1000000 | tf_op jit(solution)/shard_map/band_second/pallas_call | solution.py:411
  24.7 0.0 collective-permute-done.4.there
  24.7 2.0 %collective-permute-start.5 = (bf16[32,384]{1,0:T(8,128)(2,1)S(1)}, bf16[32,384]{1,0:T(8,128)(2,1)S(1)}, u32[]{:S(2)}, u32[]{:S(2)}) collective-permute-start(bf16[32,384]{1,0:T(8,128)(2,1)S(1)} %add_parts.4.here), channel_id=1, source_target_pairs={{0,4},{2,6},{4,0},{6,2},{1,5},{3,7},{5,1},{7,3},{8,12},{10,14},{12... | collective-permute-start | bytes 73736 | tf_op jit(solution)/shard_map/ppermute | solution.py:354
  26.8 1.9 %collective-permute-done.5.there = bf16[32,384]{1,0:T(8,128)(2,1)S(1)} collective-permute-done((bf16[32,384]{1,0:T(8,128)(2,1)S(1)}, bf16[32,384]{1,0:T(8,128)(2,1)S(1)}, u32[]{:S(2)}, u32[]{:S(2)}) %collective-permute-start.5) | collective-permute-done | bytes 24608 | tf_op jit(solution)/shard_map/ppermute | solution.py:354
  28.7 1.8 %collective-permute-start.6 = (bf16[32,384]{1,0:T(8,128)(2,1)S(1)}, bf16[32,384]{1,0:T(8,128)(2,1)S(1)}, u32[]{:S(2)}, u32[]{:S(2)}) collective-permute-start(bf16[32,384]{1,0:T(8,128)(2,1)S(1)} %add_parts.5.here), channel_id=1, source_target_pairs={{0,8},{8,0},{16,24},{24,16},{1,9},{9,1},{17,25},{25,17},{2,10},{10... | collective-permute-start | bytes 73736 | tf_op jit(solution)/shard_map/ppermute | solution.py:354
  30.5 2.1 %collective-permute-done.6.there = bf16[32,384]{1,0:T(8,128)(2,1)S(1)} collective-permute-done((bf16[32,384]{1,0:T(8,128)(2,1)S(1)}, bf16[32,384]{1,0:T(8,128)(2,1)S(1)}, u32[]{:S(2)}, u32[]{:S(2)}) %collective-permute-start.6) | collective-permute-done | bytes 24608 | tf_op jit(solution)/shard_map/ppermute | solution.py:354
  32.6 1.7 %collective-permute-start.7 = (bf16[32,384]{1,0:T(8,128)(2,1)S(1)}, bf16[32,384]{1,0:T(8,128)(2,1)S(1)}, u32[]{:S(2)}, u32[]{:S(2)}) collective-permute-start(bf16[32,384]{1,0:T(8,128)(2,1)S(1)} %add_parts.6.here), channel_id=1, source_target_pairs={{0,16},{8,24},{16,0},{24,8},{1,17},{9,25},{17,1},{25,9},{2,18},{10... | collective-permute-start | bytes 73736 | tf_op jit(solution)/shard_map/ppermute | solution.py:354
  34.3 3.1 %collective-permute-done.7.there = bf16[32,384]{1,0:T(8,128)(2,1)S(1)} collective-permute-done((bf16[32,384]{1,0:T(8,128)(2,1)S(1)}, bf16[32,384]{1,0:T(8,128)(2,1)S(1)}, u32[]{:S(2)}, u32[]{:S(2)}) %collective-permute-start.7) | collective-permute-done | bytes 24608 | tf_op jit(solution)/shard_map/ppermute | solution.py:354
  37.4 1.6 %collective-permute-start.8 = (bf16[32,384]{1,0:T(8,128)(2,1)S(1)}, bf16[32,384]{1,0:T(8,128)(2,1)S(1)}, u32[]{:S(2)}, u32[]{:S(2)}) collective-permute-start(bf16[32,384]{1,0:T(8,128)(2,1)S(1)} %add_parts.7.total), channel_id=1, source_target_pairs={{0,1},{1,0},{2,3},{3,2},{4,5},{5,4},{6,7},{7,6},{8,9},{9,8},{10,11... | collective-permute-start | bytes 73736 | tf_op jit(solution)/shard_map/ppermute | solution.py:354
  38.9 1.6 %closure.1 = bf16[1,16,8,8,128]{4,3,2,1,0:T(8,128)(2,1)} custom-call(bf16[12,192,128]{2,1,0:T(8,128)(2,1)S(1)} %get-tuple-element.54.hidden, bf16[128,1920]{1,0:T(8,128)(2,1)S(1)} %get-tuple-element.60.t2, f32[128,128]{1,0:T(8,128)S(1)} %get-tuple-element.61.b2), custom_call_target="tpu_custom_call" | custom-call | flops 1000000000 | bytes 1000000 | tf_op jit(solution)/shard_map/closure/pallas_call | solution.py:415
  40.5 0.8 %collective-permute-done.8.last = bf16[32,384]{1,0:T(8,128)(2,1)S(1)} collective-permute-done((bf16[32,384]{1,0:T(8,128)(2,1)S(1)}, bf16[32,384]{1,0:T(8,128)(2,1)S(1)}, u32[]{:S(2)}, u32[]{:S(2)}) %collective-permute-start.8) | collective-permute-done | bytes 24608 | tf_op jit(solution)/shard_map/ppermute | solution.py:354
  41.3 0.8 %finish.1 = (f32[128,27]{1,0:T(8,128)}, f32[256,27]{1,0:T(8,128)}, f32[1,16]{1,0:T(1,128)}) custom-call(bf16[32,384]{1,0:T(8,128)(2,1)S(1)} %add_parts.7.total, bf16[32,384]{1,0:T(8,128)(2,1)S(1)} %collective-permute-done.8.last), custom_call_target="tpu_custom_call" | custom-call | flops 10000000 | bytes 1000000 | tf_op jit(solution)/shard_map/finish/pallas_call | solution.py:426
  (4 shorter events, 0.1 us)
Async XLA Ops:
  0.6 8.6 %copy-start = (bf16[27,16,16]{0,2,1:T(8,128)(2,1)S(1)}, bf16[27,16,16]{0,2,1:T(8,128)(2,1)}, u32[]{:S(2)}) copy-start(bf16[27,16,16]{0,2,1:T(8,128)(2,1)} %param.15) | copy-start | bytes 41476
  0.6 1.0 %copy-start.2 = (bf16[1,16,8,8,128]{4,3,2,1,0:T(8,128)(2,1)S(1)}, bf16[1,16,8,8,128]{4,3,2,1,0:T(8,128)(2,1)}, u32[]{:S(2)}) copy-start(bf16[1,16,8,8,128]{4,3,2,1,0:T(8,128)(2,1)} %cot.1) | copy-start | bytes 786436
  1.6 0.9 %copy-start.3 = (bf16[1,8,8,8,128]{4,3,2,1,0:T(8,128)(2,1)S(1)}, bf16[1,8,8,8,128]{4,3,2,1,0:T(8,128)(2,1)}, u32[]{:S(2)}) copy-start(bf16[1,8,8,8,128]{4,3,2,1,0:T(8,128)(2,1)} %fields.1) | copy-start | bytes 393220
  2.5 6.7 %copy-start.4 = (bf16[27,16,8]{0,2,1:T(8,128)(2,1)S(1)}, bf16[27,16,8]{0,2,1:T(8,128)(2,1)}, u32[]{:S(2)}) copy-start(bf16[27,16,8]{0,2,1:T(8,128)(2,1)} %param.13) | copy-start | bytes 20740
  2.5 6.7 %copy-start.5 = (f32[16]{0:T(128)S(1)}, f32[16]{0:T(128)}, u32[]{:S(2)}) copy-start(f32[16]{0:T(128)} %param.14) | copy-start | bytes 196
  2.7 8.4 %collective-permute-start = (bf16[512,128]{1,0:T(8,128)(2,1)S(1)}, bf16[512,128]{1,0:T(8,128)(2,1)S(1)}, u32[]{:S(2)}, u32[]{:S(2)}) collective-permute-start(bf16[512,128]{1,0:T(8,128)(2,1)S(1)} %get-tuple-element.35), channel_id=1, source_target_pairs={{0,0},{8,16},{16,8},{24,24},{1,1},{9,17},{17,9},{25,25},{2,2},{10,... | collective-permute-start | bytes 393224 | tf_op jit(solution)/shard_map/ppermute | solution.py:349
  3.3 9.1 %collective-permute-start.1 = (bf16[512,128]{1,0:T(8,128)(2,1)S(1)}, bf16[512,128]{1,0:T(8,128)(2,1)S(1)}, u32[]{:S(2)}, u32[]{:S(2)}) collective-permute-start(bf16[512,128]{1,0:T(8,128)(2,1)S(1)} %get-tuple-element.36), channel_id=1, source_target_pairs={{0,8},{8,0},{16,24},{24,16},{1,9},{9,1},{17,25},{25,17},{2,10},{10... | collective-permute-start | bytes 393224 | tf_op jit(solution)/shard_map/ppermute | solution.py:350
  12.8 4.8 %collective-permute-start.2 = (bf16[896,128]{1,0:T(8,128)(2,1)S(1)}, bf16[896,128]{1,0:T(8,128)(2,1)S(1)}, u32[]{:S(2)}, u32[]{:S(2)}) collective-permute-start(bf16[896,128]{1,0:T(8,128)(2,1)S(1)} %get-tuple-element.43), channel_id=1, source_target_pairs={{0,0},{2,4},{4,2},{6,6},{1,1},{3,5},{5,3},{7,7},{8,8},{10,12},{12,... | collective-permute-start | bytes 688136 | tf_op jit(solution)/shard_map/ppermute | solution.py:349
  13.5 4.2 %collective-permute-start.3 = (bf16[896,128]{1,0:T(8,128)(2,1)S(1)}, bf16[896,128]{1,0:T(8,128)(2,1)S(1)}, u32[]{:S(2)}, u32[]{:S(2)}) collective-permute-start(bf16[896,128]{1,0:T(8,128)(2,1)S(1)} %get-tuple-element.44), channel_id=1, source_target_pairs={{0,2},{2,0},{4,6},{6,4},{1,3},{3,1},{5,7},{7,5},{8,10},{10,8},{12,... | collective-permute-start | bytes 688136 | tf_op jit(solution)/shard_map/ppermute | solution.py:350
  16.4 1.2 %copy-start.6 = (bf16[128,768]{1,0:T(8,128)(2,1)S(1)}, bf16[128,768]{1,0:T(8,128)(2,1)}, u32[]{:S(2)}) copy-start(bf16[128,768]{1,0:T(8,128)(2,1)} %constant.15.clone.rep2) | copy-start | bytes 589828
  16.4 1.2 %copy-start.7 = (bf16[640,128]{1,0:T(8,128)(2,1)S(1)}, bf16[640,128]{1,0:T(8,128)(2,1)}, u32[]{:S(2)}) copy-start(bf16[640,128]{1,0:T(8,128)(2,1)} %constant.13.clone.e2t) | copy-start | bytes 491524
  16.4 1.3 %copy-start.8 = (bf16[384,128]{1,0:T(8,128)(2,1)S(1)}, bf16[384,128]{1,0:T(8,128)(2,1)}, u32[]{:S(2)}) copy-start(bf16[384,128]{1,0:T(8,128)(2,1)} %constant.12.clone.e1t) | copy-start | bytes 294916
  16.4 1.3 %copy-start.9 = (bf16[128,384]{1,0:T(8,128)(2,1)S(1)}, bf16[128,384]{1,0:T(8,128)(2,1)}, u32[]{:S(2)}) copy-start(bf16[128,384]{1,0:T(8,128)(2,1)} %constant.14.clone.rep1) | copy-start | bytes 294916
  16.4 1.3 %copy-start.10 = (f32[1,640]{1,0:T(1,128)S(1)}, f32[1,640]{1,0:T(1,128)}, u32[]{:S(2)}) copy-start(f32[1,640]{1,0:T(1,128)} %constant.17.clone.y2) | copy-start | bytes 7684
  16.4 1.3 %copy-start.11 = (f32[1,384]{1,0:T(1,128)S(1)}, f32[1,384]{1,0:T(1,128)}, u32[]{:S(2)}) copy-start(f32[1,384]{1,0:T(1,128)} %constant.16.clone.y1) | copy-start | bytes 4612
  17.7 6.1 %copy-start.1 = (f32[16]{0:T(128)S(1)}, f32[16]{0:T(128)}, u32[]{:S(2)}) copy-start(f32[16]{0:T(128)} %param.16) | copy-start | bytes 196
  21.4 3.3 %collective-permute-start.4 = (f32[32,384]{1,0:T(8,128)S(1)}, f32[32,384]{1,0:T(8,128)S(1)}, u32[]{:S(2)}, u32[]{:S(2)}) collective-permute-start(f32[32,384]{1,0:T(8,128)S(1)} %get-tuple-element.56.here), channel_id=1, source_target_pairs={{0,2},{2,0},{4,6},{6,4},{1,3},{3,1},{5,7},{7,5},{8,10},{10,8},{12,... | collective-permute-start | bytes 147464 | tf_op jit(solution)/shard_map/ppermute | solution.py:354
  24.7 3.9 %collective-permute-start.5 = (bf16[32,384]{1,0:T(8,128)(2,1)S(1)}, bf16[32,384]{1,0:T(8,128)(2,1)S(1)}, u32[]{:S(2)}, u32[]{:S(2)}) collective-permute-start(bf16[32,384]{1,0:T(8,128)(2,1)S(1)} %add_parts.4.here), channel_id=1, source_target_pairs={{0,4},{2,6},{4,0},{6,2},{1,5},{3,7},{5,1},{7,3},{8,12},{10,14},{12... | collective-permute-start | bytes 73736 | tf_op jit(solution)/shard_map/ppermute | solution.py:354
  28.7 3.9 %collective-permute-start.6 = (bf16[32,384]{1,0:T(8,128)(2,1)S(1)}, bf16[32,384]{1,0:T(8,128)(2,1)S(1)}, u32[]{:S(2)}, u32[]{:S(2)}) collective-permute-start(bf16[32,384]{1,0:T(8,128)(2,1)S(1)} %add_parts.5.here), channel_id=1, source_target_pairs={{0,8},{8,0},{16,24},{24,16},{1,9},{9,1},{17,25},{25,17},{2,10},{10... | collective-permute-start | bytes 73736 | tf_op jit(solution)/shard_map/ppermute | solution.py:354
  32.6 4.8 %collective-permute-start.7 = (bf16[32,384]{1,0:T(8,128)(2,1)S(1)}, bf16[32,384]{1,0:T(8,128)(2,1)S(1)}, u32[]{:S(2)}, u32[]{:S(2)}) collective-permute-start(bf16[32,384]{1,0:T(8,128)(2,1)S(1)} %add_parts.6.here), channel_id=1, source_target_pairs={{0,16},{8,24},{16,0},{24,8},{1,17},{9,25},{17,1},{25,9},{2,18},{10... | collective-permute-start | bytes 73736 | tf_op jit(solution)/shard_map/ppermute | solution.py:354
  37.4 3.9 %collective-permute-start.8 = (bf16[32,384]{1,0:T(8,128)(2,1)S(1)}, bf16[32,384]{1,0:T(8,128)(2,1)S(1)}, u32[]{:S(2)}, u32[]{:S(2)}) collective-permute-start(bf16[32,384]{1,0:T(8,128)(2,1)S(1)} %add_parts.7.total), channel_id=1, source_target_pairs={{0,1},{1,0},{2,3},{3,2},{4,5},{5,4},{6,7},{7,6},{8,9},{9,8},{10,11... | collective-permute-start | bytes 73736 | tf_op jit(solution)/shard_map/ppermute | solution.py:354

commit v8 on v7

--- a/solution.py
+++ b/solution.py
@@ -24,20 +24,25 @@
     return n % CH, n // CH
 
 
-def rim(width):
+def rim(channels):
     def of(n):
-        side, n = n // 32, n % 32
-        return n // width, n % width + side * (8 + width) - width
+        side, n = n // (2 * channels), n % (2 * channels)
+        return n // 2, n % 2 + 10 * side - 2
     return of
+
+
+def deep_rim(n):
+    part, n = n // 16, n % 16
+    return n // 2, n % 2 + 10 * (part // 2) - 2 + (part % 2) * (4 * (part // 2) - 2)
 
 
 def table(channels, total, places):
     e = np.zeros((total, 128), np.float32)
     ys = np.full((1, total), FAR, np.float32)
     for c in range(3):
-        for of, count, start in places:
-            ch, y = of(np.arange(count))
-            at = start + c * (128 if start == 0 or channels == CI else 64) + np.arange(count)
+        for of, start, step in places:
+            ch, y = of(np.arange(step))
+            at = start + c * step + np.arange(step)
             e[at, c * channels + ch] = 1
             ys[0, at] = y
     return e, ys
@@ -56,17 +61,15 @@
     return jnp.where(lane < 3 * step, of(lane % step)[1], FAR)
 
 
-def place(rows, wanted, of, side=None):
+def place(rows, wanted, of, size, slot):
     row, lane = iota(rows, 128)
-    if side is None:
-        return one_hot(of(lane)[0] == wanted(row))
-    return one_hot((of(lane % 64)[0] == wanted(row)) & (lane // 64 == side))
+    return one_hot((of(lane % size)[0] == wanted(row)) & (lane // size == slot))
 
 
 def row_table(rows, own):
     row, lane = iota(rows, CH)
     own_c, own_y = own(row)
-    rim_c, rim_y = rim(2)(row - 128)
+    rim_c, rim_y = rim(CH)(row - 128)
     channel, y = jnp.where(row < 128, own_c, rim_c), jnp.where(row < 128, own_y, rim_y)
     return one_hot(channel == lane), y[:, :1]
 
@@ -76,13 +79,11 @@
     return v.reshape(v.shape[0] * v.shape[1], v.shape[2])
 
 
-def pick_rows(channels, width):
-    half = channels * width
-    row = lax.broadcasted_iota(jnp.int32, (2 * half, channels * 8), 0)
-    col = lax.broadcasted_iota(jnp.int32, (2 * half, channels * 8), 1)
-    side = jnp.where(row >= half, 1, 0)
-    q = row - side * half
-    return jnp.where(col == (q // width) * 8 + (8 - width) * side + q % width, 1.0, 0.0).astype(BF16)
+def pick_rows(channels, low, high):
+    half = channels * 2
+    row, col = iota(2 * half, channels * 8)
+    side = row // half
+    return one_hot(col == (row % half // 2) * 8 + low + (high - low) * side + row % 2)
 
 
 def partners(index, count):
@@ -120,16 +121,22 @@
     return f, [low for low, _ in rims] + inner + [high for _, high in rims]
 
 
-def join_kernel(counts, xfar, xnear, fields, cot, near, far):
+def join_kernel(counts, xfar, xnear, fields, cot, near, far, near_outer, far_outer):
     up_first = lax.axis_index("radial") % 2 == 0
     f, c = x_planes(fields.shape[0], fields, cot, xnear, xfar, counts[0])
-    at = 0
-    for rows, pick in ((f, pick_rows(CI, 4)), (c, pick_rows(CH, 2))):
+    inner, outer = pick_rows(CI, 0, 6), pick_rows(CI, 2, 4)
+    ends = f[:2] + f[-2:]
+    work = [(inner, f[2:-2], near, far), (pick_rows(CH, 0, 6), c, near, far)]
+    work += [(inner, ends, near_outer, far_outer), (outer, ends + f[2:-2], near_outer, far_outer)]
+    at = {}
+    for pick, rows, near_out, far_out in work:
+        half = pick.shape[0] // 2
         for v in rows:
             got = jnp.dot(pick, v.astype(BF16), preferred_element_type=F32)
-            near[at:at + 32] = jnp.where(up_first, got[32:], got[:32]).astype(BF16)
-            far[at:at + 32] = jnp.where(up_first, got[:32], got[32:]).astype(BF16)
-            at += 32
+            start = at.get(id(near_out), 0)
+            near_out[start:start + half] = jnp.where(up_first, got[half:], got[:half]).astype(BF16)
+            far_out[start:start + half] = jnp.where(up_first, got[:half], got[half:]).astype(BF16)
+            at[id(near_out)] = start + half
 
 
 def spread(w, by_row, flip):
@@ -156,14 +163,11 @@
     return total.astype(BF16)
 
 
-def halves(parts, wanted, of):
-    left, right = (place(parts[0].shape[1], wanted, of, side) for side in range(2))
-    return jnp.concatenate([dots([(parts[0], left), (parts[1], right)]), dots([(parts[2], left)])], axis=1)
-
-
-def wholes(parts, wanted, of):
-    at = place(parts[0].shape[1], wanted, of)
-    return jnp.concatenate([dots([(v, at)]) for v in parts], axis=1)
+def packed(parts, wanted, of, size):
+    per = 128 // size
+    places = [place(parts[0].shape[1], wanted, of, size, slot) for slot in range(min(per, 3))]
+    tiles = [range(first, min(first + per, 3)) for first in range(0, 3, per)]
+    return jnp.concatenate([dots([(parts[c], places[c % per]) for c in tile]) for tile in tiles], axis=1)
 
 
 def band(wide, expand, ys, rows_y, t):
@@ -181,24 +185,23 @@
     out[...] = jnp.broadcast_to(column, out.shape)
 
 
-def band_first_kernel(w1, w2, bias, t1o, t1r, tbo, tbr, b1):
+def band_kernel(w1, w2, first_bias, second_bias, t1o, t1r, t1d, tbo, tbr, t2, b1, b2):
     expand, rows_y = row_table(192, y_first)
     parts = spread(w1, True, False)
-    band(halves(parts, lambda n: n % CI, natural), expand, lane_y(natural, 256, 64), rows_y, t1o)
-    band(halves(parts, lambda n: n % CI, rim(4)), expand, lane_y(rim(4), 256, 64), rows_y, t1r)
+    for of, step, t in ((natural, 64, t1o), (rim(CI), 32, t1r), (deep_rim, 64, t1d)):
+        wide = packed(parts, lambda n: n % CI, of, step)
+        band(wide, expand, lane_y(of, wide.shape[1], step), rows_y, t)
     parts = spread(w2, False, True)
-    band(wholes(parts, lambda n: n // CH, natural), expand, lane_y(natural, 384, 128), rows_y, tbo)
-    band(halves(parts, lambda n: n // CH, rim(2)), expand, lane_y(rim(2), 256, 64), rows_y, tbr)
-    repeat_bias(bias, expand, b1)
-
-
-def band_second_kernel(w2, bias, t2, b2):
+    for of, step, t in ((natural, 128, tbo), (rim(CH), 64, tbr)):
+        wide = packed(parts, lambda n: n // CH, of, step)
+        band(wide, expand, lane_y(of, wide.shape[1], step), rows_y, t)
+    repeat_bias(first_bias, expand, b1)
     expand, rows_y = row_table(128, natural)
     parts = spread(w2, True, False)
-    wide = [wholes(parts, lambda n: n % CH, y_first), halves(parts, lambda n: n % CH, rim(2))]
-    ys = jnp.concatenate([lane_y(y_first, 384, 128), lane_y(rim(2), 256, 64)], axis=1)
+    wide = [packed(parts, lambda n: n % CH, of, step) for of, step in ((y_first, 128), (rim(CH), 64))]
+    ys = jnp.concatenate([lane_y(y_first, 384, 128), lane_y(rim(CH), 256, 64)], axis=1)
     band(jnp.concatenate(wide, axis=1), expand, ys, rows_y, t2)
-    repeat_bias(bias, expand, b2)
+    repeat_bias(second_bias, expand, b2)
 
 
 def shifted(v):
@@ -228,7 +231,8 @@
             for n, piece in enumerate(shifted(v)):
                 ref[n * v.shape[0]:(n + 1) * v.shape[0], p * Z:(p + 1) * Z] = piece
     fs[192:] = jnp.zeros((64, fs.shape[1]), BF16)
-    pre[...] = jnp.dot(t1[...], stacked(fs, pre.shape[1]), preferred_element_type=F32) + b1[:, :1]
+    rows = jnp.concatenate([fs[:, a * 256 + 256:a * 256 + 256 + pre.shape[1]] for a in range(3)], axis=0)
+    pre[...] = jnp.dot(t1[:128], rows, preferred_element_type=F32) + b1[:128, :1]
     back[...] = jnp.dot(tb[...], stacked(cs, back.shape[1]), preferred_element_type=F32)
 
 
@@ -238,42 +242,36 @@
     return jnp.dot(high, w, preferred_element_type=F32) + jnp.dot(low, w, preferred_element_type=F32)
 
 
+def gelu_share(pre):
+    return 0.5 * (1.0 + lax.erf(pre * 0.7071067811865476))
+
+
 def rim_kernel(counts, rfar, rnear, fs, cs, pre_own, back_own, t1, tb, e1t, e2t, rep1, rep2, y1, y2,
                hidden_out, payload, fr, cr, taps):
-    count = hidden_out.shape[0] - 4
+    count = hidden_out.shape[0]
     lanes = count * Z
-    stream, radial = lax.axis_index("stream"), lax.axis_index("radial")
+    radial = lax.axis_index("radial")
     at = 0
-    for ref in (fr, cr):
-        for p in range(ref.shape[1] // Z):
-            low, high = sides(radial, counts[1], rnear[at:at + 32], rfar[at:at + 32])
+    for ref, half in ((fr, 16), (cr, 32)):
+        for p in range(count + 4):
+            low, high = sides(radial, counts[1], rnear[at:at + half], rfar[at:at + half])
             for n, piece in enumerate(shifted(jnp.concatenate([low, high], axis=0))):
-                ref[n * 64:(n + 1) * 64, p * Z:(p + 1) * Z] = piece
-            at += 32
-        ref[192:] = jnp.zeros((64, ref.shape[1]), BF16)
-    pre = pre_own[...] + jnp.dot(t1[...], stacked(fr, lanes + 4 * Z), preferred_element_type=F32)
-    share = 0.5 * (1.0 + lax.erf(pre * 0.7071067811865476))
+                ref[n * 2 * half:(n + 1) * 2 * half, p * Z:(p + 1) * Z] = piece
+            at += half
+        ref[6 * half:] = jnp.zeros((2 * half, ref.shape[1]), BF16)
+    pre = pre_own[...] + jnp.dot(t1[...], stacked(fr, lanes), preferred_element_type=F32)
+    share = gelu_share(pre)
     hidden = (pre * share).astype(BF16)
-    zero = jnp.zeros((), BF16)
-    rims = (jnp.where(radial > 0, hidden[128:160], zero), jnp.where(radial < counts[1] - 1, hidden[160:], zero))
-    for p in range(count + 4):
-        at = slice(p * Z, (p + 1) * Z)
-        rows = jnp.concatenate([hidden[:128, at], rims[0][:, at], rims[1][:, at]], axis=0)
-        if p < 2:
-            rows = jnp.where(stream > 0, rows, zero)
-        elif p >= count + 2:
-            rows = jnp.where(stream < counts[0] - 1, rows, zero)
-        hidden_out[p] = rows
-    at = slice(2 * Z, 2 * Z + lanes)
-    pre, share, hidden = pre[:128, at], share[:128, at], hidden[:128, at]
+    for x in range(count):
+        hidden_out[x] = hidden[:, x * Z:(x + 1) * Z]
     back = back_own[...] + jnp.dot(tb[...], stacked(cr, lanes), preferred_element_type=F32)
     dpre = (back * (share + pre * jnp.exp(-0.5 * pre * pre) * 0.3989422804014327)).astype(BF16)
     over_lanes = (((1,), (1,)), ((), ()))
     ones, twos = [], []
     for a in range(3):
         at = slice((a + 1) * 256, (a + 1) * 256 + lanes)
-        rows = [ref[n * 64:(n + 1) * 64, at] for n in range(3) for ref in (fs, fr)]
-        g1 = lax.dot_general(dpre, jnp.concatenate(rows, axis=0), over_lanes, preferred_element_type=F32)
+        rows = jnp.concatenate([fs[:, at], fr[:, a * 256:a * 256 + lanes]], axis=0)
+        g1 = lax.dot_general(dpre, rows, over_lanes, preferred_element_type=F32)
         at = slice(a * 256, a * 256 + lanes)
         rows = jnp.concatenate([cs[:, at], cr[:, at]], axis=0)
         g2 = lax.dot_general(hidden, rows, over_lanes, preferred_element_type=F32)
@@ -303,6 +301,43 @@
     payload[...] = jnp.concatenate([taps[n] for n in range(3)], axis=1)
 
 
+def hidden_rim_kernel(counts, rfar, rnear, rfar_outer, rnear_outer, hidden, fs, t1o, t1d, b1, hidden_out, fr):
+    count = hidden.shape[0]
+    stream, radial = lax.axis_index("stream"), lax.axis_index("radial")
+    for p in range(count + 8):
+        end = p if p < 2 else p - count - 4 if p >= count + 6 else None
+        if end is None:
+            near, outer = (rnear, rfar, (p - 2) * 16), (rnear_outer, rfar_outer, 128 + (p - 2) * 16)
+        else:
+            near, outer = (rnear_outer, rfar_outer, end * 16), (rnear_outer, rfar_outer, 64 + end * 16)
+        parts = [sides(radial, counts[1], n[at:at + 16], f[at:at + 16]) for n, f, at in (near, outer)]
+        rows = jnp.concatenate([part[side] for side in range(2) for part in parts], axis=0)
+        for n, piece in enumerate(shifted(rows)):
+            fr[n * 64:(n + 1) * 64, p * Z:(p + 1) * Z] = piece
+    fr[192:] = jnp.zeros((64, fr.shape[1]), BF16)
+
+    def gelu(rows, lanes):
+        total = b1[rows, :1]
+        for t, ref in ((t1o, fs), (t1d, fr)):
+            cells = [jnp.concatenate([ref[:, a * 256 + at:a * 256 + at + size] for at, size in lanes], axis=1) for a in range(3)]
+            total = total + jnp.dot(t[rows], jnp.concatenate(cells, axis=0), preferred_element_type=F32)
+        return total * gelu_share(total)
+
+    own = gelu(slice(0, 128), ((0, 2 * Z), ((count + 2) * Z, 2 * Z)))
+    rims = gelu(slice(128, 192), ((0, (count + 4) * Z),))
+    rims = jnp.concatenate([jnp.where(radial > 0, rims[:32], 0.0), jnp.where(radial < counts[1] - 1, rims[32:], 0.0)], axis=0)
+    for p in range(count + 4):
+        rim_rows = rims[:, p * Z:(p + 1) * Z]
+        if 2 <= p < count + 2:
+            hidden_out[p, :128] = hidden[p - 2]
+            hidden_out[p, 128:] = rim_rows.astype(BF16)
+        else:
+            at = p if p < 2 else p - count
+            inside = stream > 0 if p < 2 else stream < counts[0] - 1
+            rows = jnp.concatenate([own[:, at * Z:(at + 1) * Z], rim_rows], axis=0)
+            hidden_out[p] = jnp.where(inside, rows, 0.0).astype(BF16)
+
+
 def closure_kernel(hidden, t2, b2, closure, hs):
     count = closure.shape[2]
     for p in range(count + 4):
@@ -359,8 +394,8 @@
 
 
 def local(fields, first_weight, first_bias, second_weight, second_bias, cotangent):
-    e1t, y1 = table(CI, 384, ((natural, 64, 0), (rim(4), 64, 64)))
-    e2t, y2 = table(CH, 640, ((natural, 128, 0), (rim(2), 64, 384)))
+    e1t, y1 = table(CI, 384, ((natural, 0, 64), (rim(CI), 256, 32)))
+    e2t, y2 = table(CH, 640, ((natural, 0, 128), (rim(CH), 384, 64)))
     rep1, rep2 = np.zeros((128, 384), np.float32), np.zeros((128, 768), np.float32)
     for c in range(3):
         rep1[c * CI:(c + 1) * CI, c * 128:(c + 1) * 128] = np.tile(np.eye(CI), (1, CH))
@@ -381,41 +416,51 @@
     xnear, xfar = exchange(near, far, "stream")
     wide = (planes + 4) * Z
     counts = (lax.axis_size("stream"), lax.axis_size("radial"))
-    t1o, t1r, tbo, tbr, b1 = call(
-        band_first_kernel,
-        (shape(192, 768), shape(192, 768), shape(128, 1152), shape(128, 768), shape(192, 128, dtype=F32)),
-        "band_first",
+    t1o, t1r, t1d, tbo, tbr, t2, b1, b2 = call(
+        band_kernel,
+        (shape(192, 768), shape(128, 384), shape(192, 768), shape(128, 1152), shape(128, 768), shape(128, 1920),
+         shape(192, 128, dtype=F32), shape(128, 128, dtype=F32)),
+        "band_matrices",
         flops=4_000_000_000,
-    )(w1, w2, first_bias[None])
+    )(w1, w2, first_bias[None], second_bias[None])
     xfar, xnear, t1o, tbo = lax.optimization_barrier((xfar, xnear, t1o, tbo))
-    near, far = call(functools.partial(join_kernel, counts), (shape((2 * planes + 12) * 32, Z),) * 2, "join_strips")(
-        xfar, xnear, f_rows, c_rows)
+    inner, outer = (planes + 4) * 48, 128 + (planes + 4) * 16
+    near, far, near_outer, far_outer = call(
+        functools.partial(join_kernel, counts), (shape(inner, Z), shape(inner, Z), shape(outer, Z), shape(outer, Z)), "join_strips"
+    )(xfar, xnear, f_rows, c_rows)
     rnear, rfar = exchange(near, far, "radial")
+    rnear_outer, rfar_outer = exchange(near_outer, far_outer, "radial")
     fs, cs, pre, back = call(
         functools.partial(own_kernel, counts),
-        (shape(256, wide + 4 * Z), shape(384, wide), shape(192, wide, dtype=F32), shape(128, planes * Z, dtype=F32)),
+        (shape(256, wide + 4 * Z), shape(384, wide), shape(128, planes * Z, dtype=F32), shape(128, planes * Z, dtype=F32)),
         "own_rows",
         flops=1_000_000_000,
     )(xfar, xnear, f_rows, c_rows, t1o, tbo, b1)
     hidden, payload = call(
         functools.partial(rim_kernel, counts),
-        (shape(planes + 4, 192, Z), shape(32, 384, dtype=F32)),
+        (shape(planes, 128, Z), shape(32, 384, dtype=F32)),
         "gradients",
-        (pltpu.VMEM((256, wide + 4 * Z), BF16), pltpu.VMEM((256, wide), BF16), pltpu.VMEM((3, 32, 128), F32)),
+        (pltpu.VMEM((128, wide), BF16), pltpu.VMEM((256, wide), BF16), pltpu.VMEM((3, 32, 128), F32)),
         flops=2_000_000_000,
     )(rfar, rnear, fs, cs, pre, back, t1r, tbr, *const(e1t, e2t, rep1, rep2), *const(y1, y2, dtype=F32))
 
     steps = [(axis, 1 << n) for axis in ("radial", "stream", "snap") for n in range((lax.axis_size(axis) - 1).bit_length())]
-    payload, w2 = lax.optimization_barrier((payload, w2))
     arrived = swap(payload, *steps[0])
-    t2, b2 = call(band_second_kernel, (shape(128, 1920), shape(128, 128, dtype=F32)), "band_second")(
-        w2, second_bias[None])
-    payload, t2, b2 = lax.optimization_barrier((add(payload, arrived), t2, b2))
+    payload = add(payload, arrived)
     arrived = swap(payload, *steps[1])
+    hidden = call(
+        functools.partial(hidden_rim_kernel, counts),
+        shape(planes + 4, 192, Z),
+        "hidden_rim",
+        (pltpu.VMEM((256, wide + 4 * Z), BF16),),
+        flops=1_000_000_000,
+    )(rfar, rnear, rfar_outer, rnear_outer, hidden, fs, t1o, t1d, b1)
+    payload, hidden = lax.optimization_barrier((add(payload, arrived), hidden))
+    arrived = swap(payload, *steps[2])
     closure = call(
         closure_kernel, shape(*cotangent.shape), "closure", (pltpu.VMEM((640, wide), BF16),), flops=1_000_000_000
     )(hidden, t2, b2)
-    for step in steps[2:]:
+    for step in steps[3:]:
         payload = add(payload, arrived)
         arrived = swap(payload, *step)
 

time: 42.3 us -> 41.6 us (0.983)
  waiting for transfers between devices: 9.28 us -> 8.45 us
  Pallas kernels: 10.3 us -> 11 us
  starting transfers between devices: 19.7 us -> 19.2 us
    ppermute x5, starting transfers between devices: 9.53 us -> 6.97 us  [swap(): lax.ppermute(v, axis, [(i, i ^ mask) for i in range(lax.axis_size(axis))])]
    ppermute x2 -> x3, starting transfers between devices: 8.84 us -> 10.2 us  [exchange(): return (lax.ppermute(near, axis, [(i, i ^ 1) for i in range(count)]), far)]
    ppermute x2 -> x3, waiting for transfers between devices: 1.42 us -> 0.5 us  [exchange(): return (lax.ppermute(near, axis, [(i, i ^ 1) for i in range(count)]), far)]
    pallas_call x4, Pallas kernels: 6.62 us -> 7.46 us  [the longest x1 3.13 us: local(): call(functools.partial(rim_kernel, counts), (shape(planes, 128, Z), shape...]
    ppermute x2 -> x3, starting transfers between devices: 1.34 us -> 1.99 us  [exchange(): far = lax.ppermute(far, axis, shifted_pairs)]
  transfers between devices with their start and end apart: 9 -> 11, of which waited for: 5 -> 6; matrix products, arithmetic and copies ran while one was open for 0% -> 0% of each run, Pallas kernels for 13% -> 23%
where the time goes in v8:
time: 41.6 us; the launch traced here: 41.3 us
  starting transfers between devices  19.2 us (46%)
  Pallas kernels  11 us (26%)
  waiting for transfers between devices  8.45 us (20%)
  local copies, waits for them, and re-layouts  1.98 us (5%)
  between operations  0.8 us (2%)
    ppermute x3, starting transfers between devices, exchange(): return (lax.ppermute(near, axis, [(i, i ^ 1) for i in range(count)]), far)  10.2 us
    ppermute x5, waiting for transfers between devices, swap(): lax.ppermute(v, axis, [(i, i ^ mask) for i in range(lax.axis_size(axis))])  7.94 us
    ppermute x5, starting transfers between devices, swap(): lax.ppermute(v, axis, [(i, i ^ mask) for i in range(lax.axis_size(axis))])  6.97 us
    pallas_call x1, Pallas kernels, local(): call(functools.partial(rim_kernel, counts), (shape(planes, 128, Z), shape...  3.13 us
    pallas_call x1, Pallas kernels, local(): call(band_kernel, (shape(192, 768), shape(128, 384), shape(192, 768), sha...  2.69 us
    ppermute x3, starting transfers between devices, exchange(): far = lax.ppermute(far, axis, shifted_pairs)  1.99 us
    unnamed x24, local copies, waits for them, and re-layouts  1.98 us
    pallas_call x1, Pallas kernels, local(): call(closure_kernel, shape(*cotangent.shape), 'closure', (pltpu.VMEM((640...  1.57 us
  transfers between devices with their start and end apart: 11, of which 6 were waited for; matrix products, arithmetic and copies ran while one was open for 0% of the time, Pallas kernels for 23%

profile of v8, /device:TPU:0, one launch (start us, length us, event | category | flops | bytes accessed | tf_op | source)
XLA Modules:
  0.0 41.3 jit_solution(10421352374533604151)
XLA Ops:
  0.6 0.0 copy-start
  0.6 0.9 %copy-done = bf16[1,16,8,8,128]{4,3,2,1,0:T(8,128)(2,1)S(1)} copy-done((bf16[1,16,8,8,128]{4,3,2,1,0:T(8,128)(2,1)S(1)}, bf16[1,16,8,8,128]{4,3,2,1,0:T(8,128)(2,1)}, u32[]{:S(2)}) %copy-start) | copy-done | bytes 262168
  1.6 0.0 copy-start.1
  1.6 0.9 %copy-done.1 = bf16[1,8,8,8,128]{4,3,2,1,0:T(8,128)(2,1)S(1)} copy-done((bf16[1,8,8,8,128]{4,3,2,1,0:T(8,128)(2,1)S(1)}, bf16[1,8,8,8,128]{4,3,2,1,0:T(8,128)(2,1)}, u32[]{:S(2)}) %copy-start.1) | copy-done | bytes 131096
  2.5 0.0 copy-start.2
  2.5 0.0 copy-start.3
  2.5 0.0 copy-start.4
  2.5 0.0 copy-start.5
  2.5 0.1 pack_strips.1
  2.6 0.7 %collective-permute-start = (bf16[512,128]{1,0:T(8,128)(2,1)S(1)}, bf16[512,128]{1,0:T(8,128)(2,1)S(1)}, u32[]{:S(2)}, u32[]{:S(2)}) collective-permute-start(bf16[512,128]{1,0:T(8,128)(2,1)S(1)} %get-tuple-element.35), channel_id=1, source_target_pairs={{0,0},{8,16},{16,8},{24,24},{1,1},{9,17},{17,9},{25,25},{2,2},{10,... | collective-permute-start | bytes 393224 | tf_op jit(solution)/shard_map/ppermute | solution.py:384
  3.3 5.9 %collective-permute-start.1 = (bf16[512,128]{1,0:T(8,128)(2,1)S(1)}, bf16[512,128]{1,0:T(8,128)(2,1)S(1)}, u32[]{:S(2)}, u32[]{:S(2)}) collective-permute-start(bf16[512,128]{1,0:T(8,128)(2,1)S(1)} %get-tuple-element.36), channel_id=1, source_target_pairs={{0,8},{8,0},{16,24},{24,16},{1,9},{9,1},{17,25},{25,17},{2,10},{10... | collective-permute-start | bytes 393224 | tf_op jit(solution)/shard_map/ppermute | solution.py:385
  9.2 0.0 copy-done.2
  9.2 0.0 copy-done.3
  9.2 0.0 copy-done.4
  9.2 0.0 copy-done.5
  9.2 2.7 %band_matrices.1 = (bf16[192,768]{1,0:T(8,128)(2,1)S(1)}, bf16[128,384]{1,0:T(8,128)(2,1)S(1)}, bf16[192,768]{1,0:T(8,128)(2,1)S(1)}, bf16[128,1152]{1,0:T(8,128...) custom-call(bf16[128,27]{1,0:T(8,128)(2,1)S(1)} %bitcast.16, ...), custom_call_target="tpu_custom_call" | custom-call | flops 4000000000 | bytes 1000000 | tf_op jit(solution)/shard_map/band_matrices/pallas_call | solution.py:419
  11.9 0.0 collective-permute-done.xfar
  11.9 0.5 %collective-permute-done.1.xnear = bf16[512,128]{1,0:T(8,128)(2,1)S(1)} collective-permute-done((bf16[512,128]{1,0:T(8,128)(2,1)S(1)}, bf16[512,128]{1,0:T(8,128)(2,1)S(1)}, u32[]{:S(2)}, u32[]{:S(2)}) %collective-permute-start.1) | collective-permute-done | bytes 131104 | tf_op jit(solution)/shard_map/ppermute | solution.py:385
  12.4 0.4 join_strips.1
  12.8 0.7 %collective-permute-start.2 = (bf16[576,128]{1,0:T(8,128)(2,1)S(1)}, bf16[576,128]{1,0:T(8,128)(2,1)S(1)}, u32[]{:S(2)}, u32[]{:S(2)}) collective-permute-start(bf16[576,128]{1,0:T(8,128)(2,1)S(1)} %get-tuple-element.43), channel_id=1, source_target_pairs={{0,0},{2,4},{4,2},{6,6},{1,1},{3,5},{5,3},{7,7},{8,8},{10,12},{12,... | collective-permute-start | bytes 442376 | tf_op jit(solution)/shard_map/ppermute | solution.py:384
  13.5 2.9 %collective-permute-start.3 = (bf16[576,128]{1,0:T(8,128)(2,1)S(1)}, bf16[576,128]{1,0:T(8,128)(2,1)S(1)}, u32[]{:S(2)}, u32[]{:S(2)}) collective-permute-start(bf16[576,128]{1,0:T(8,128)(2,1)S(1)} %get-tuple-element.44), channel_id=1, source_target_pairs={{0,2},{2,0},{4,6},{6,4},{1,3},{3,1},{5,7},{7,5},{8,10},{10,8},{12,... | collective-permute-start | bytes 442376 | tf_op jit(solution)/shard_map/ppermute | solution.py:385
  16.4 0.7 %collective-permute-start.6 = (bf16[320,128]{1,0:T(8,128)(2,1)S(1)}, bf16[320,128]{1,0:T(8,128)(2,1)S(1)}, u32[]{:S(2)}, u32[]{:S(2)}) collective-permute-start(bf16[320,128]{1,0:T(8,128)(2,1)S(1)} %get-tuple-element.55), channel_id=1, source_target_pairs={{0,0},{2,4},{4,2},{6,6},{1,1},{3,5},{5,3},{7,7},{8,8},{10,12},{12,... | collective-permute-start | bytes 245768 | tf_op jit(solution)/shard_map/ppermute | solution.py:384
  17.1 1.3 %collective-permute-start.7 = (bf16[320,128]{1,0:T(8,128)(2,1)S(1)}, bf16[320,128]{1,0:T(8,128)(2,1)S(1)}, u32[]{:S(2)}, u32[]{:S(2)}) collective-permute-start(bf16[320,128]{1,0:T(8,128)(2,1)S(1)} %get-tuple-element.56), channel_id=1, source_target_pairs={{0,2},{2,0},{4,6},{6,4},{1,3},{3,1},{5,7},{7,5},{8,10},{10,8},{12,... | collective-permute-start | bytes 245768 | tf_op jit(solution)/shard_map/ppermute | solution.py:385
  18.4 0.0 copy-start.6
  18.4 0.0 copy-start.7
  18.4 0.0 copy-start.8
  18.4 0.0 copy-start.9
  18.4 0.0 copy-start.10
  18.5 0.0 copy-start.11
  18.5 0.9 %own_rows.1 = (bf16[256,2048]{1,0:T(8,128)(2,1)S(1)}, bf16[384,1536]{1,0:T(8,128)(2,1)S(1)}, f32[128,1024]{1,0:T(8,128)S(1)}, f32[128,1024]{1,0:T(8,128)S(1)}) custom-call(bf16[512,128]{1,0:T(8,128)(2,1)S(1)} %collective-permute-done.xfar, bf16[512,128]{1,0:T(8,128)(2,1)S(1)} %collective-permute-done.1.xnear, ...), custom_call_target="tpu_custom_call" | custom-call | flops 1000000000 | bytes 1000000 | tf_op jit(solution)/shard_map/own_rows/pallas_call | solution.py:433
  19.4 0.0 collective-permute-done.2.rfar
  19.4 0.0 collective-permute-done.3.rnear
  19.4 0.0 copy-done.6
  19.4 0.0 copy-done.7
  19.5 0.0 copy-done.8
  19.5 0.0 copy-done.9
  19.5 0.0 copy-done.10
  19.6 0.0 copy-done.11
  19.6 3.1 %gradients.1 = (bf16[8,128,128]{2,1,0:T(8,128)(2,1)S(1)}, f32[32,384]{1,0:T(8,128)S(1)}) custom-call(bf16[576,128]{1,0:T(8,128)(2,1)S(1)} %collective-permute-done.2.rfar, bf16[576,128]{1,0:T(8,128)(2,1)S(1)} %collective-permute-done.3.rnear, bf16[256,2048]{1,0:T(8,128)(2,1)S(1)} %get-tuple-element.48.fs, bf16[384,1536]{1,0:T(8,128)(2,1)S(1)} %get-tuple-element.49.cs, ...), custom_call_target="tpu_custom_call" | custom-call | flops 2000000000 | bytes 1000000 | tf_op jit(solution)/shard_map/gradients/pallas_call | solution.py:439
  22.7 0.1 collective-permute-start.4
  22.8 1.2 %collective-permute-done.4.there = f32[32,384]{1,0:T(8,128)S(1)} collective-permute-done((f32[32,384]{1,0:T(8,128)S(1)}, f32[32,384]{1,0:T(8,128)S(1)}, u32[]{:S(2)}, u32[]{:S(2)}) %collective-permute-start.4) | collective-permute-done | bytes 49184 | tf_op jit(solution)/shard_map/ppermute | solution.py:389
  24.0 1.8 %collective-permute-start.5 = (bf16[32,384]{1,0:T(8,128)(2,1)S(1)}, bf16[32,384]{1,0:T(8,128)(2,1)S(1)}, u32[]{:S(2)}, u32[]{:S(2)}) collective-permute-start(bf16[32,384]{1,0:T(8,128)(2,1)S(1)} %add_parts.4.here), channel_id=1, source_target_pairs={{0,4},{2,6},{4,0},{6,2},{1,5},{3,7},{5,1},{7,3},{8,12},{10,14},{12... | collective-permute-start | bytes 73736 | tf_op jit(solution)/shard_map/ppermute | solution.py:389
  25.8 0.0 collective-permute-done.6.rfar_outer
  25.8 0.0 collective-permute-done.7.rnear_outer
  25.9 1.3 %hidden_rim.1.hidden = bf16[12,192,128]{2,1,0:T(8,128)(2,1)S(1)} custom-call(bf16[576,128]{1,0:T(8,128)(2,1)S(1)} %collective-permute-done.2.rfar, bf16[576,128]{1,0:T(8,128)(2,1)S(1)} %collective-permute-done.3.rnear, bf16[320,128]{1,0:T(8,128)(2,1)S(1)} %collective-permute-done.6.rfar_outer, bf16[320,128]{1,0:T(8,128)(2,1)S(1)} %collective-permute-done.7.rnear_outer, ...), custom_call_target="tpu_custom_call" | custom-call | flops 1000000000 | bytes 1000000 | tf_op jit(solution)/shard_map/hidden_rim/pallas_call | solution.py:451
  27.1 0.8 %collective-permute-done.5.there = bf16[32,384]{1,0:T(8,128)(2,1)S(1)} collective-permute-done((bf16[32,384]{1,0:T(8,128)(2,1)S(1)}, bf16[32,384]{1,0:T(8,128)(2,1)S(1)}, u32[]{:S(2)}, u32[]{:S(2)}) %collective-permute-start.5) | collective-permute-done | bytes 24608 | tf_op jit(solution)/shard_map/ppermute | solution.py:389
  27.9 1.8 %collective-permute-start.8 = (bf16[32,384]{1,0:T(8,128)(2,1)S(1)}, bf16[32,384]{1,0:T(8,128)(2,1)S(1)}, u32[]{:S(2)}, u32[]{:S(2)}) collective-permute-start(bf16[32,384]{1,0:T(8,128)(2,1)S(1)} %add_parts.5.here), channel_id=1, source_target_pairs={{0,8},{8,0},{16,24},{24,16},{1,9},{9,1},{17,25},{25,17},{2,10},{10... | collective-permute-start | bytes 73736 | tf_op jit(solution)/shard_map/ppermute | solution.py:389
  29.7 2.1 %collective-permute-done.8.there = bf16[32,384]{1,0:T(8,128)(2,1)S(1)} collective-permute-done((bf16[32,384]{1,0:T(8,128)(2,1)S(1)}, bf16[32,384]{1,0:T(8,128)(2,1)S(1)}, u32[]{:S(2)}, u32[]{:S(2)}) %collective-permute-start.8) | collective-permute-done | bytes 24608 | tf_op jit(solution)/shard_map/ppermute | solution.py:389
  31.8 1.7 %collective-permute-start.9 = (bf16[32,384]{1,0:T(8,128)(2,1)S(1)}, bf16[32,384]{1,0:T(8,128)(2,1)S(1)}, u32[]{:S(2)}, u32[]{:S(2)}) collective-permute-start(bf16[32,384]{1,0:T(8,128)(2,1)S(1)} %add_parts.6.here), channel_id=1, source_target_pairs={{0,16},{8,24},{16,0},{24,8},{1,17},{9,25},{17,1},{25,9},{2,18},{10... | collective-permute-start | bytes 73736 | tf_op jit(solution)/shard_map/ppermute | solution.py:389
  33.5 3.1 %collective-permute-done.9.there = bf16[32,384]{1,0:T(8,128)(2,1)S(1)} collective-permute-done((bf16[32,384]{1,0:T(8,128)(2,1)S(1)}, bf16[32,384]{1,0:T(8,128)(2,1)S(1)}, u32[]{:S(2)}, u32[]{:S(2)}) %collective-permute-start.9) | collective-permute-done | bytes 24608 | tf_op jit(solution)/shard_map/ppermute | solution.py:389
  36.6 1.6 %collective-permute-start.10 = (bf16[32,384]{1,0:T(8,128)(2,1)S(1)}, bf16[32,384]{1,0:T(8,128)(2,1)S(1)}, u32[]{:S(2)}, u32[]{:S(2)}) collective-permute-start(bf16[32,384]{1,0:T(8,128)(2,1)S(1)} %add_parts.7.total), channel_id=1, source_target_pairs={{0,1},{1,0},{2,3},{3,2},{4,5},{5,4},{6,7},{7,6},{8,9},{9,8},{10,11... | collective-permute-start | bytes 73736 | tf_op jit(solution)/shard_map/ppermute | solution.py:389
  38.2 1.6 %closure.1 = bf16[1,16,8,8,128]{4,3,2,1,0:T(8,128)(2,1)} custom-call(bf16[12,192,128]{2,1,0:T(8,128)(2,1)S(1)} %hidden_rim.1.hidden, bf16[128,1920]{1,0:T(8,128)(2,1)S(1)} %get-tuple-element.60.t2, f32[128,128]{1,0:T(8,128)S(1)} %get-tuple-element.61.b2), custom_call_target="tpu_custom_call" | custom-call | flops 1000000000 | bytes 1000000 | tf_op jit(solution)/shard_map/closure/pallas_call | solution.py:460
  39.8 0.8 %collective-permute-done.10.last = bf16[32,384]{1,0:T(8,128)(2,1)S(1)} collective-permute-done((bf16[32,384]{1,0:T(8,128)(2,1)S(1)}, bf16[32,384]{1,0:T(8,128)(2,1)S(1)}, u32[]{:S(2)}, u32[]{:S(2)}) %collective-permute-start.10) | collective-permute-done | bytes 24608 | tf_op jit(solution)/shard_map/ppermute | solution.py:389
  40.5 0.8 %finish.1 = (f32[128,27]{1,0:T(8,128)}, f32[256,27]{1,0:T(8,128)}, f32[1,16]{1,0:T(1,128)}) custom-call(bf16[32,384]{1,0:T(8,128)(2,1)S(1)} %add_parts.7.total, bf16[32,384]{1,0:T(8,128)(2,1)S(1)} %collective-permute-done.10.last), custom_call_target="tpu_custom_call" | custom-call | flops 10000000 | bytes 1000000 | tf_op jit(solution)/shard_map/finish/pallas_call | solution.py:471
  (4 shorter events, 0.1 us)
Async XLA Ops:
  0.6 1.0 %copy-start = (bf16[1,16,8,8,128]{4,3,2,1,0:T(8,128)(2,1)S(1)}, bf16[1,16,8,8,128]{4,3,2,1,0:T(8,128)(2,1)}, u32[]{:S(2)}) copy-start(bf16[1,16,8,8,128]{4,3,2,1,0:T(8,128)(2,1)} %cot.1) | copy-start | bytes 786436
  1.6 0.9 %copy-start.1 = (bf16[1,8,8,8,128]{4,3,2,1,0:T(8,128)(2,1)S(1)}, bf16[1,8,8,8,128]{4,3,2,1,0:T(8,128)(2,1)}, u32[]{:S(2)}) copy-start(bf16[1,8,8,8,128]{4,3,2,1,0:T(8,128)(2,1)} %fields.1) | copy-start | bytes 393220
  2.5 6.7 %copy-start.2 = (bf16[27,16,16]{0,2,1:T(8,128)(2,1)S(1)}, bf16[27,16,16]{0,2,1:T(8,128)(2,1)}, u32[]{:S(2)}) copy-start(bf16[27,16,16]{0,2,1:T(8,128)(2,1)} %param.15) | copy-start | bytes 41476
  2.5 6.7 %copy-start.3 = (bf16[27,16,8]{0,2,1:T(8,128)(2,1)S(1)}, bf16[27,16,8]{0,2,1:T(8,128)(2,1)}, u32[]{:S(2)}) copy-start(bf16[27,16,8]{0,2,1:T(8,128)(2,1)} %param.13) | copy-start | bytes 20740
  2.5 6.7 %copy-start.4 = (f32[16]{0:T(128)S(1)}, f32[16]{0:T(128)}, u32[]{:S(2)}) copy-start(f32[16]{0:T(128)} %param.14) | copy-start | bytes 196
  2.5 6.7 %copy-start.5 = (f32[16]{0:T(128)S(1)}, f32[16]{0:T(128)}, u32[]{:S(2)}) copy-start(f32[16]{0:T(128)} %param.16) | copy-start | bytes 196
  2.6 9.3 %collective-permute-start = (bf16[512,128]{1,0:T(8,128)(2,1)S(1)}, bf16[512,128]{1,0:T(8,128)(2,1)S(1)}, u32[]{:S(2)}, u32[]{:S(2)}) collective-permute-start(bf16[512,128]{1,0:T(8,128)(2,1)S(1)} %get-tuple-element.35), channel_id=1, source_target_pairs={{0,0},{8,16},{16,8},{24,24},{1,1},{9,17},{17,9},{25,25},{2,2},{10,... | collective-permute-start | bytes 393224 | tf_op jit(solution)/shard_map/ppermute | solution.py:384
  3.3 9.1 %collective-permute-start.1 = (bf16[512,128]{1,0:T(8,128)(2,1)S(1)}, bf16[512,128]{1,0:T(8,128)(2,1)S(1)}, u32[]{:S(2)}, u32[]{:S(2)}) collective-permute-start(bf16[512,128]{1,0:T(8,128)(2,1)S(1)} %get-tuple-element.36), channel_id=1, source_target_pairs={{0,8},{8,0},{16,24},{24,16},{1,9},{9,1},{17,25},{25,17},{2,10},{10... | collective-permute-start | bytes 393224 | tf_op jit(solution)/shard_map/ppermute | solution.py:385
  12.8 6.6 %collective-permute-start.2 = (bf16[576,128]{1,0:T(8,128)(2,1)S(1)}, bf16[576,128]{1,0:T(8,128)(2,1)S(1)}, u32[]{:S(2)}, u32[]{:S(2)}) collective-permute-start(bf16[576,128]{1,0:T(8,128)(2,1)S(1)} %get-tuple-element.43), channel_id=1, source_target_pairs={{0,0},{2,4},{4,2},{6,6},{1,1},{3,5},{5,3},{7,7},{8,8},{10,12},{12,... | collective-permute-start | bytes 442376 | tf_op jit(solution)/shard_map/ppermute | solution.py:384
  13.5 5.9 %collective-permute-start.3 = (bf16[576,128]{1,0:T(8,128)(2,1)S(1)}, bf16[576,128]{1,0:T(8,128)(2,1)S(1)}, u32[]{:S(2)}, u32[]{:S(2)}) collective-permute-start(bf16[576,128]{1,0:T(8,128)(2,1)S(1)} %get-tuple-element.44), channel_id=1, source_target_pairs={{0,2},{2,0},{4,6},{6,4},{1,3},{3,1},{5,7},{7,5},{8,10},{10,8},{12,... | collective-permute-start | bytes 442376 | tf_op jit(solution)/shard_map/ppermute | solution.py:385
  16.4 9.4 %collective-permute-start.6 = (bf16[320,128]{1,0:T(8,128)(2,1)S(1)}, bf16[320,128]{1,0:T(8,128)(2,1)S(1)}, u32[]{:S(2)}, u32[]{:S(2)}) collective-permute-start(bf16[320,128]{1,0:T(8,128)(2,1)S(1)} %get-tuple-element.55), channel_id=1, source_target_pairs={{0,0},{2,4},{4,2},{6,6},{1,1},{3,5},{5,3},{7,7},{8,8},{10,12},{12,... | collective-permute-start | bytes 245768 | tf_op jit(solution)/shard_map/ppermute | solution.py:384
  17.1 8.8 %collective-permute-start.7 = (bf16[320,128]{1,0:T(8,128)(2,1)S(1)}, bf16[320,128]{1,0:T(8,128)(2,1)S(1)}, u32[]{:S(2)}, u32[]{:S(2)}) collective-permute-start(bf16[320,128]{1,0:T(8,128)(2,1)S(1)} %get-tuple-element.56), channel_id=1, source_target_pairs={{0,2},{2,0},{4,6},{6,4},{1,3},{3,1},{5,7},{7,5},{8,10},{10,8},{12,... | collective-permute-start | bytes 245768 | tf_op jit(solution)/shard_map/ppermute | solution.py:385
  18.4 1.0 %copy-start.6 = (bf16[128,768]{1,0:T(8,128)(2,1)S(1)}, bf16[128,768]{1,0:T(8,128)(2,1)}, u32[]{:S(2)}) copy-start(bf16[128,768]{1,0:T(8,128)(2,1)} %constant.15.clone.rep2) | copy-start | bytes 589828
  18.4 1.0 %copy-start.7 = (bf16[640,128]{1,0:T(8,128)(2,1)S(1)}, bf16[640,128]{1,0:T(8,128)(2,1)}, u32[]{:S(2)}) copy-start(bf16[640,128]{1,0:T(8,128)(2,1)} %constant.13.clone.e2t) | copy-start | bytes 491524
  18.4 1.1 %copy-start.8 = (bf16[384,128]{1,0:T(8,128)(2,1)S(1)}, bf16[384,128]{1,0:T(8,128)(2,1)}, u32[]{:S(2)}) copy-start(bf16[384,128]{1,0:T(8,128)(2,1)} %constant.12.clone.e1t) | copy-start | bytes 294916
  18.4 1.1 %copy-start.9 = (bf16[128,384]{1,0:T(8,128)(2,1)S(1)}, bf16[128,384]{1,0:T(8,128)(2,1)}, u32[]{:S(2)}) copy-start(bf16[128,384]{1,0:T(8,128)(2,1)} %constant.14.clone.rep1) | copy-start | bytes 294916
  18.4 1.1 %copy-start.10 = (f32[1,640]{1,0:T(1,128)S(1)}, f32[1,640]{1,0:T(1,128)}, u32[]{:S(2)}) copy-start(f32[1,640]{1,0:T(1,128)} %constant.17.clone.y2) | copy-start | bytes 7684
  18.5 1.1 %copy-start.11 = (f32[1,384]{1,0:T(1,128)S(1)}, f32[1,384]{1,0:T(1,128)}, u32[]{:S(2)}) copy-start(f32[1,384]{1,0:T(1,128)} %constant.16.clone.y1) | copy-start | bytes 4612
  22.7 1.3 %collective-permute-start.4 = (f32[32,384]{1,0:T(8,128)S(1)}, f32[32,384]{1,0:T(8,128)S(1)}, u32[]{:S(2)}, u32[]{:S(2)}) collective-permute-start(f32[32,384]{1,0:T(8,128)S(1)} %get-tuple-element.54.here), channel_id=1, source_target_pairs={{0,2},{2,0},{4,6},{6,4},{1,3},{3,1},{5,7},{7,5},{8,10},{10,8},{12,... | collective-permute-start | bytes 147464 | tf_op jit(solution)/shard_map/ppermute | solution.py:389
  24.0 3.9 %collective-permute-start.5 = (bf16[32,384]{1,0:T(8,128)(2,1)S(1)}, bf16[32,384]{1,0:T(8,128)(2,1)S(1)}, u32[]{:S(2)}, u32[]{:S(2)}) collective-permute-start(bf16[32,384]{1,0:T(8,128)(2,1)S(1)} %add_parts.4.here), channel_id=1, source_target_pairs={{0,4},{2,6},{4,0},{6,2},{1,5},{3,7},{5,1},{7,3},{8,12},{10,14},{12... | collective-permute-start | bytes 73736 | tf_op jit(solution)/shard_map/ppermute | solution.py:389
  27.9 3.9 %collective-permute-start.8 = (bf16[32,384]{1,0:T(8,128)(2,1)S(1)}, bf16[32,384]{1,0:T(8,128)(2,1)S(1)}, u32[]{:S(2)}, u32[]{:S(2)}) collective-permute-start(bf16[32,384]{1,0:T(8,128)(2,1)S(1)} %add_parts.5.here), channel_id=1, source_target_pairs={{0,8},{8,0},{16,24},{24,16},{1,9},{9,1},{17,25},{25,17},{2,10},{10... | collective-permute-start | bytes 73736 | tf_op jit(solution)/shard_map/ppermute | solution.py:389
  31.8 4.8 %collective-permute-start.9 = (bf16[32,384]{1,0:T(8,128)(2,1)S(1)}, bf16[32,384]{1,0:T(8,128)(2,1)S(1)}, u32[]{:S(2)}, u32[]{:S(2)}) collective-permute-start(bf16[32,384]{1,0:T(8,128)(2,1)S(1)} %add_parts.6.here), channel_id=1, source_target_pairs={{0,16},{8,24},{16,0},{24,8},{1,17},{9,25},{17,1},{25,9},{2,18},{10... | collective-permute-start | bytes 73736 | tf_op jit(solution)/shard_map/ppermute | solution.py:389
  36.6 3.9 %collective-permute-start.10 = (bf16[32,384]{1,0:T(8,128)(2,1)S(1)}, bf16[32,384]{1,0:T(8,128)(2,1)S(1)}, u32[]{:S(2)}, u32[]{:S(2)}) collective-permute-start(bf16[32,384]{1,0:T(8,128)(2,1)S(1)} %add_parts.7.total), channel_id=1, source_target_pairs={{0,1},{1,0},{2,3},{3,2},{4,5},{5,4},{6,7},{7,6},{8,9},{9,8},{10,11... | collective-permute-start | bytes 73736 | tf_op jit(solution)/shard_map/ppermute | solution.py:389

commit v9 on v8

--- a/solution.py
+++ b/solution.py
@@ -121,22 +121,27 @@
     return f, [low for low, _ in rims] + inner + [high for _, high in rims]
 
 
-def join_kernel(counts, xfar, xnear, fields, cot, near, far, near_outer, far_outer):
+def pick_strips(work, near, far):
     up_first = lax.axis_index("radial") % 2 == 0
-    f, c = x_planes(fields.shape[0], fields, cot, xnear, xfar, counts[0])
-    inner, outer = pick_rows(CI, 0, 6), pick_rows(CI, 2, 4)
-    ends = f[:2] + f[-2:]
-    work = [(inner, f[2:-2], near, far), (pick_rows(CH, 0, 6), c, near, far)]
-    work += [(inner, ends, near_outer, far_outer), (outer, ends + f[2:-2], near_outer, far_outer)]
-    at = {}
-    for pick, rows, near_out, far_out in work:
+    at = 0
+    for pick, rows in work:
         half = pick.shape[0] // 2
         for v in rows:
             got = jnp.dot(pick, v.astype(BF16), preferred_element_type=F32)
-            start = at.get(id(near_out), 0)
-            near_out[start:start + half] = jnp.where(up_first, got[half:], got[:half]).astype(BF16)
-            far_out[start:start + half] = jnp.where(up_first, got[:half], got[half:]).astype(BF16)
-            at[id(near_out)] = start + half
+            near[at:at + half] = jnp.where(up_first, got[half:], got[:half]).astype(BF16)
+            far[at:at + half] = jnp.where(up_first, got[:half], got[half:]).astype(BF16)
+            at += half
+
+
+def join_kernel(counts, xfar, xnear, fields, cot, near, far):
+    f, c = x_planes(fields.shape[0], fields, cot, xnear, xfar, counts[0])
+    pick_strips([(pick_rows(CI, 0, 6), f[2:-2]), (pick_rows(CH, 0, 6), c)], near, far)
+
+
+def join_outer_kernel(counts, xfar, xnear, fields, cot, near, far):
+    f, _ = x_planes(fields.shape[0], fields, cot, xnear, xfar, counts[0])
+    ends = f[:2] + f[-2:]
+    pick_strips([(pick_rows(CI, 0, 6), ends), (pick_rows(CI, 2, 4), ends + f[2:-2])], near, far)
 
 
 def spread(w, by_row, flip):
@@ -347,15 +352,23 @@
         closure[0, :, x] = out[:, x * Z:(x + 1) * Z].reshape(CH, 8, Z)
 
 
-def add_kernel(here, there, total):
-    s = here[...].astype(F32) + there[...].astype(F32)
+def summed(parts):
+    parts = [part[...].astype(F32) for part in parts]
+    while len(parts) > 1:
+        parts = [v + w for v, w in zip(parts[::2], parts[1::2])]
+    return parts[0]
+
+
+def add_kernel(*refs):
+    s = summed(refs[:-1])
     lost = s - s.astype(BF16).astype(F32)
     row = lax.broadcasted_iota(jnp.int32, s.shape, 0)
-    total[...] = (s + jnp.where(row == 28, pltpu.roll(lost, 1, 0), 0.0)).astype(BF16)
-
-
-def finish_kernel(norm, total, last, first, second, bias):
-    scaled = (total[...].astype(F32) + last[...].astype(F32)) * norm
+    refs[-1][...] = (s + jnp.where(row == 28, pltpu.roll(lost, 1, 0), 0.0)).astype(BF16)
+
+
+def finish_kernel(norm, *refs):
+    *parts, first, second, bias = refs
+    scaled = summed(parts) * norm
     flipped = jnp.transpose(scaled)
     first[...] = flipped[:128, :27]
     second[...] = flipped[128:, :27]
@@ -385,12 +398,22 @@
     return lax.ppermute(near, axis, [(i, i ^ 1) for i in range(count)]), far
 
 
-def swap(v, axis, mask):
-    return lax.ppermute(v, axis, [(i, i ^ mask) for i in range(lax.axis_size(axis))])
-
-
-def add(v, w):
-    return call(add_kernel, shape(*v.shape), "add_parts")(v, w)
+def swap(v, axis, masks):
+    count = lax.axis_size(axis)
+    return [lax.ppermute(v, axis, [(i, i ^ mask) for i in range(count)]) for mask in masks]
+
+
+def add(v, arrived):
+    return call(add_kernel, shape(*v.shape), "add_parts")(v, *arrived)
+
+
+def rounds(axis, most):
+    found, step = [], 1
+    while step < lax.axis_size(axis):
+        masks = [step * n for n in range(1, most if step * most <= lax.axis_size(axis) else 2)]
+        found.append((axis, masks))
+        step *= len(masks) + 1
+    return found
 
 
 def local(fields, first_weight, first_bias, second_weight, second_bias, cotangent):
@@ -424,12 +447,9 @@
         flops=4_000_000_000,
     )(w1, w2, first_bias[None], second_bias[None])
     xfar, xnear, t1o, tbo = lax.optimization_barrier((xfar, xnear, t1o, tbo))
-    inner, outer = (planes + 4) * 48, 128 + (planes + 4) * 16
-    near, far, near_outer, far_outer = call(
-        functools.partial(join_kernel, counts), (shape(inner, Z), shape(inner, Z), shape(outer, Z), shape(outer, Z)), "join_strips"
-    )(xfar, xnear, f_rows, c_rows)
+    inner, outer = shape((planes + 4) * 48, Z), shape(128 + (planes + 4) * 16, Z)
+    near, far = call(functools.partial(join_kernel, counts), (inner, inner), "join_strips")(xfar, xnear, f_rows, c_rows)
     rnear, rfar = exchange(near, far, "radial")
-    rnear_outer, rfar_outer = exchange(near_outer, far_outer, "radial")
     fs, cs, pre, back = call(
         functools.partial(own_kernel, counts),
         (shape(256, wide + 4 * Z), shape(384, wide), shape(128, planes * Z, dtype=F32), shape(128, planes * Z, dtype=F32)),
@@ -444,10 +464,16 @@
         flops=2_000_000_000,
     )(rfar, rnear, fs, cs, pre, back, t1r, tbr, *const(e1t, e2t, rep1, rep2), *const(y1, y2, dtype=F32))
 
-    steps = [(axis, 1 << n) for axis in ("radial", "stream", "snap") for n in range((lax.axis_size(axis) - 1).bit_length())]
+    steps = rounds("radial", 2) + rounds("stream", 4) + rounds("snap", 2)
     arrived = swap(payload, *steps[0])
+    payload, f_rows = lax.optimization_barrier((add(payload, arrived), f_rows))
+    arrived = swap(payload, *steps[1])
+    near_outer, far_outer = call(
+        functools.partial(join_outer_kernel, counts), (outer, outer), "join_outer", flops=1_000_000_000
+    )(xfar, xnear, f_rows, c_rows)
+    rnear_outer, rfar_outer = exchange(near_outer, far_outer, "radial")
     payload = add(payload, arrived)
-    arrived = swap(payload, *steps[1])
+    arrived = swap(payload, *steps[2])
     hidden = call(
         functools.partial(hidden_rim_kernel, counts),
         shape(planes + 4, 192, Z),
@@ -456,11 +482,11 @@
         flops=1_000_000_000,
     )(rfar, rnear, rfar_outer, rnear_outer, hidden, fs, t1o, t1d, b1)
     payload, hidden = lax.optimization_barrier((add(payload, arrived), hidden))
-    arrived = swap(payload, *steps[2])
+    arrived = swap(payload, *steps[3])
     closure = call(
         closure_kernel, shape(*cotangent.shape), "closure", (pltpu.VMEM((640, wide), BF16),), flops=1_000_000_000
     )(hidden, t2, b2)
-    for step in steps[3:]:
+    for step in steps[4:]:
         payload = add(payload, arrived)
         arrived = swap(payload, *step)
 
@@ -472,7 +498,7 @@
         functools.partial(finish_kernel, norm),
         (shape(CH * CI, 27, dtype=F32), shape(CH * CH, 27, dtype=F32), shape(1, CH, dtype=F32)),
         "finish",
-    )(payload, arrived)
+    )(payload, *arrived)
     first = first.reshape(CH, CI, 27).transpose(2, 0, 1)
     second = second.reshape(CH, CH, 27).transpose(2, 0, 1)
     return (closure, first, second, bias[0])

time: 41.6 us -> 44.7 us (1.075)
  starting transfers between devices: 19.2 us -> 22 us
    ppermute x3, starting transfers between devices: 10.2 us -> 12.2 us  [exchange(): return (lax.ppermute(near, axis, [(i, i ^ 1) for i in range(count)]), far)]
    ppermute x5 -> x6, starting transfers between devices: 6.97 us -> 7.76 us  [swap(): lax.ppermute(v, axis, [(i, i ^ mask) for i in range(count)])]
    ppermute x5 -> x6, waiting for transfers between devices: 7.94 us -> 8.11 us  [swap(): lax.ppermute(v, axis, [(i, i ^ mask) for i in range(count)])]
  transfers between devices with their start and end apart: 11 -> 12, of which waited for: 6 -> 7; matrix products, arithmetic and copies ran while one was open for 0% -> 0% of each run, Pallas kernels for 23% -> 12%
where the time goes in v9:
time: 44.7 us; the launch traced here: 44.5 us
  starting transfers between devices  22 us (49%)
  Pallas kernels  11 us (25%)
  waiting for transfers between devices  8.63 us (19%)
  local copies, waits for them, and re-layouts  1.98 us (4%)
  between operations  0.81 us (2%)
    ppermute x3, starting transfers between devices, exchange(): return (lax.ppermute(near, axis, [(i, i ^ 1) for i in range(count)]), far)  12.2 us
    ppermute x6, waiting for transfers between devices, swap(): lax.ppermute(v, axis, [(i, i ^ mask) for i in range(count)])  8.11 us
    ppermute x6, starting transfers between devices, swap(): lax.ppermute(v, axis, [(i, i ^ mask) for i in range(count)])  7.76 us
    pallas_call x1, Pallas kernels, local(): call(functools.partial(rim_kernel, counts), (shape(planes, 128, Z), shape...  3.11 us
    pallas_call x1, Pallas kernels, local(): call(band_kernel, (shape(192, 768), shape(128, 384), shape(192, 768), sha...  2.69 us
    ppermute x3, starting transfers between devices, exchange(): far = lax.ppermute(far, axis, shifted_pairs)  2 us
    unnamed x24, local copies, waits for them, and re-layouts  1.98 us
    pallas_call x1, Pallas kernels, local(): call(closure_kernel, shape(*cotangent.shape), 'closure', (pltpu.VMEM((640...  1.57 us
  transfers between devices with their start and end apart: 12, of which 7 were waited for; matrix products, arithmetic and copies ran while one was open for 0% of the time, Pallas kernels for 12%

profile of v9, /device:TPU:0, one launch (start us, length us, event | category | flops | bytes accessed | tf_op | source)
XLA Modules:
  0.0 44.5 jit_solution(730853334118123869)
XLA Ops:
  0.6 0.0 copy-start
  0.6 0.9 %copy-done = bf16[1,16,8,8,128]{4,3,2,1,0:T(8,128)(2,1)S(1)} copy-done((bf16[1,16,8,8,128]{4,3,2,1,0:T(8,128)(2,1)S(1)}, bf16[1,16,8,8,128]{4,3,2,1,0:T(8,128)(2,1)}, u32[]{:S(2)}) %copy-start) | copy-done | bytes 262168
  1.6 0.0 copy-start.1
  1.6 0.9 %copy-done.1 = bf16[1,8,8,8,128]{4,3,2,1,0:T(8,128)(2,1)S(1)} copy-done((bf16[1,8,8,8,128]{4,3,2,1,0:T(8,128)(2,1)S(1)}, bf16[1,8,8,8,128]{4,3,2,1,0:T(8,128)(2,1)}, u32[]{:S(2)}) %copy-start.1) | copy-done | bytes 131096
  2.5 0.0 copy-start.2
  2.5 0.0 copy-start.3
  2.5 0.0 copy-start.4
  2.5 0.0 copy-start.5
  2.5 0.1 pack_strips.1
  2.6 0.7 %collective-permute-start = (bf16[512,128]{1,0:T(8,128)(2,1)S(1)}, bf16[512,128]{1,0:T(8,128)(2,1)S(1)}, u32[]{:S(2)}, u32[]{:S(2)}) collective-permute-start(bf16[512,128]{1,0:T(8,128)(2,1)S(1)} %get-tuple-element.37), channel_id=1, source_target_pairs={{0,0},{8,16},{16,8},{24,24},{1,1},{9,17},{17,9},{25,25},{2,2},{10,... | collective-permute-start | bytes 393224 | tf_op jit(solution)/shard_map/ppermute | solution.py:397
  3.3 5.9 %collective-permute-start.1 = (bf16[512,128]{1,0:T(8,128)(2,1)S(1)}, bf16[512,128]{1,0:T(8,128)(2,1)S(1)}, u32[]{:S(2)}, u32[]{:S(2)}) collective-permute-start(bf16[512,128]{1,0:T(8,128)(2,1)S(1)} %get-tuple-element.38), channel_id=1, source_target_pairs={{0,8},{8,0},{16,24},{24,16},{1,9},{9,1},{17,25},{25,17},{2,10},{10... | collective-permute-start | bytes 393224 | tf_op jit(solution)/shard_map/ppermute | solution.py:398
  9.2 0.0 copy-done.2
  9.2 0.0 copy-done.3
  9.2 0.0 copy-done.4
  9.2 0.0 copy-done.5
  9.2 2.7 %band_matrices.1 = (bf16[192,768]{1,0:T(8,128)(2,1)S(1)}, bf16[128,384]{1,0:T(8,128)(2,1)S(1)}, bf16[192,768]{1,0:T(8,128)(2,1)S(1)}, bf16[128,1152]{1,0:T(8,128...) custom-call(bf16[128,27]{1,0:T(8,128)(2,1)S(1)} %bitcast.16, ...), custom_call_target="tpu_custom_call" | custom-call | flops 4000000000 | bytes 1000000 | tf_op jit(solution)/shard_map/band_matrices/pallas_call | solution.py:442
  11.9 0.0 collective-permute-done.xfar
  11.9 0.5 %collective-permute-done.1.xnear = bf16[512,128]{1,0:T(8,128)(2,1)S(1)} collective-permute-done((bf16[512,128]{1,0:T(8,128)(2,1)S(1)}, bf16[512,128]{1,0:T(8,128)(2,1)S(1)}, u32[]{:S(2)}, u32[]{:S(2)}) %collective-permute-start.1) | collective-permute-done | bytes 131104 | tf_op jit(solution)/shard_map/ppermute | solution.py:398
  12.4 0.3 join_strips.1
  12.7 0.7 %collective-permute-start.2 = (bf16[576,128]{1,0:T(8,128)(2,1)S(1)}, bf16[576,128]{1,0:T(8,128)(2,1)S(1)}, u32[]{:S(2)}, u32[]{:S(2)}) collective-permute-start(bf16[576,128]{1,0:T(8,128)(2,1)S(1)} %get-tuple-element.45), channel_id=1, source_target_pairs={{0,0},{2,4},{4,2},{6,6},{1,1},{3,5},{5,3},{7,7},{8,8},{10,12},{12,... | collective-permute-start | bytes 442376 | tf_op jit(solution)/shard_map/ppermute | solution.py:397
  13.4 2.9 %collective-permute-start.3 = (bf16[576,128]{1,0:T(8,128)(2,1)S(1)}, bf16[576,128]{1,0:T(8,128)(2,1)S(1)}, u32[]{:S(2)}, u32[]{:S(2)}) collective-permute-start(bf16[576,128]{1,0:T(8,128)(2,1)S(1)} %get-tuple-element.46), channel_id=1, source_target_pairs={{0,2},{2,0},{4,6},{6,4},{1,3},{3,1},{5,7},{7,5},{8,10},{10,8},{12,... | collective-permute-start | bytes 442376 | tf_op jit(solution)/shard_map/ppermute | solution.py:398
  16.3 0.0 copy-start.6
  16.3 0.0 copy-start.7
  16.3 0.0 copy-start.8
  16.4 0.0 copy-start.9
  16.4 0.0 copy-start.10
  16.4 0.0 copy-start.11
  16.4 0.9 %own_rows.1 = (bf16[256,2048]{1,0:T(8,128)(2,1)S(1)}, bf16[384,1536]{1,0:T(8,128)(2,1)S(1)}, f32[128,1024]{1,0:T(8,128)S(1)}, f32[128,1024]{1,0:T(8,128)S(1)}) custom-call(bf16[512,128]{1,0:T(8,128)(2,1)S(1)} %collective-permute-done.xfar, bf16[512,128]{1,0:T(8,128)(2,1)S(1)} %collective-permute-done.1.xnear, ...), custom_call_target="tpu_custom_call" | custom-call | flops 1000000000 | bytes 1000000 | tf_op jit(solution)/shard_map/own_rows/pallas_call | solution.py:453
  17.3 0.0 collective-permute-done.2.rfar
  17.3 0.0 collective-permute-done.3.rnear
  17.4 0.0 copy-done.6
  17.4 0.0 copy-done.7
  17.4 0.0 copy-done.8
  17.4 0.0 copy-done.9
  17.5 0.0 copy-done.10
  17.5 0.0 copy-done.11
  17.5 3.1 %gradients.1 = (bf16[8,128,128]{2,1,0:T(8,128)(2,1)S(1)}, f32[32,384]{1,0:T(8,128)S(1)}) custom-call(bf16[576,128]{1,0:T(8,128)(2,1)S(1)} %collective-permute-done.2.rfar, bf16[576,128]{1,0:T(8,128)(2,1)S(1)} %collective-permute-done.3.rnear, bf16[256,2048]{1,0:T(8,128)(2,1)S(1)} %get-tuple-element.50.fs, bf16[384,1536]{1,0:T(8,128)(2,1)S(1)} %get-tuple-element.51.cs, ...), custom_call_target="tpu_custom_call" | custom-call | flops 2000000000 | bytes 1000000 | tf_op jit(solution)/shard_map/gradients/pallas_call | solution.py:459
  20.6 1.7 %collective-permute-start.4 = (f32[32,384]{1,0:T(8,128)S(1)}, f32[32,384]{1,0:T(8,128)S(1)}, u32[]{:S(2)}, u32[]{:S(2)}) collective-permute-start(f32[32,384]{1,0:T(8,128)S(1)} %get-tuple-element.56.refs_0_), channel_id=1, source_target_pairs={{0,2},{2,0},{4,6},{6,4},{1,3},{3,1},{5,7},{7,5},{8,10},{10,8},{12,... | collective-permute-start | bytes 147464 | tf_op jit(solution)/shard_map/ppermute | solution.py:403
  22.3 0.9 %collective-permute-done.4.refs_1_ = f32[32,384]{1,0:T(8,128)S(1)} collective-permute-done((f32[32,384]{1,0:T(8,128)S(1)}, f32[32,384]{1,0:T(8,128)S(1)}, u32[]{:S(2)}, u32[]{:S(2)}) %collective-permute-start.4) | collective-permute-done | bytes 49184 | tf_op jit(solution)/shard_map/ppermute | solution.py:403
  23.2 0.2 join_outer.1
  23.5 0.7 %collective-permute-start.9 = (bf16[320,128]{1,0:T(8,128)(2,1)S(1)}, bf16[320,128]{1,0:T(8,128)(2,1)S(1)}, u32[]{:S(2)}, u32[]{:S(2)}) collective-permute-start(bf16[320,128]{1,0:T(8,128)(2,1)S(1)} %get-tuple-element.59), channel_id=1, source_target_pairs={{0,0},{2,4},{4,2},{6,6},{1,1},{3,5},{5,3},{7,7},{8,8},{10,12},{12,... | collective-permute-start | bytes 245768 | tf_op jit(solution)/shard_map/ppermute | solution.py:397
  24.1 3.4 %collective-permute-start.10 = (bf16[320,128]{1,0:T(8,128)(2,1)S(1)}, bf16[320,128]{1,0:T(8,128)(2,1)S(1)}, u32[]{:S(2)}, u32[]{:S(2)}) collective-permute-start(bf16[320,128]{1,0:T(8,128)(2,1)S(1)} %get-tuple-element.60), channel_id=1, source_target_pairs={{0,2},{2,0},{4,6},{6,4},{1,3},{3,1},{5,7},{7,5},{8,10},{10,8},{12,... | collective-permute-start | bytes 245768 | tf_op jit(solution)/shard_map/ppermute | solution.py:398
  27.5 0.0 collective-permute-start.5
  27.5 3.8 %collective-permute-done.5.refs_1_ = bf16[32,384]{1,0:T(8,128)(2,1)S(1)} collective-permute-done((bf16[32,384]{1,0:T(8,128)(2,1)S(1)}, bf16[32,384]{1,0:T(8,128)(2,1)S(1)}, u32[]{:S(2)}, u32[]{:S(2)}) %collective-permute-start.5) | collective-permute-done | bytes 24608 | tf_op jit(solution)/shard_map/ppermute | solution.py:403
  31.4 1.4 %collective-permute-start.8 = (bf16[32,384]{1,0:T(8,128)(2,1)S(1)}, bf16[32,384]{1,0:T(8,128)(2,1)S(1)}, u32[]{:S(2)}, u32[]{:S(2)}) collective-permute-start(bf16[32,384]{1,0:T(8,128)(2,1)S(1)} %add_parts.4.refs_0_), channel_id=1, source_target_pairs={{0,24},{8,16},{16,8},{24,0},{1,25},{9,17},{17,9},{25,1},{2,26},{10... | collective-permute-start | bytes 73736 | tf_op jit(solution)/shard_map/ppermute | solution.py:403
  32.8 1.9 %collective-permute-start.7 = (bf16[32,384]{1,0:T(8,128)(2,1)S(1)}, bf16[32,384]{1,0:T(8,128)(2,1)S(1)}, u32[]{:S(2)}, u32[]{:S(2)}) collective-permute-start(bf16[32,384]{1,0:T(8,128)(2,1)S(1)} %add_parts.4.refs_0_), channel_id=1, source_target_pairs={{0,16},{8,24},{16,0},{24,8},{1,17},{9,25},{17,1},{25,9},{2,18},{10... | collective-permute-start | bytes 73736 | tf_op jit(solution)/shard_map/ppermute | solution.py:403
  34.6 1.2 %collective-permute-start.6 = (bf16[32,384]{1,0:T(8,128)(2,1)S(1)}, bf16[32,384]{1,0:T(8,128)(2,1)S(1)}, u32[]{:S(2)}, u32[]{:S(2)}) collective-permute-start(bf16[32,384]{1,0:T(8,128)(2,1)S(1)} %add_parts.4.refs_0_), channel_id=1, source_target_pairs={{0,8},{8,0},{16,24},{24,16},{1,9},{9,1},{17,25},{25,17},{2,10},{10... | collective-permute-start | bytes 73736 | tf_op jit(solution)/shard_map/ppermute | solution.py:403
  35.8 1.2 %collective-permute-done.8.refs_3_ = bf16[32,384]{1,0:T(8,128)(2,1)S(1)} collective-permute-done((bf16[32,384]{1,0:T(8,128)(2,1)S(1)}, bf16[32,384]{1,0:T(8,128)(2,1)S(1)}, u32[]{:S(2)}, u32[]{:S(2)}) %collective-permute-start.8) | collective-permute-done | bytes 24608 | tf_op jit(solution)/shard_map/ppermute | solution.py:403
  37.1 0.4 %collective-permute-done.7.refs_2_ = bf16[32,384]{1,0:T(8,128)(2,1)S(1)} collective-permute-done((bf16[32,384]{1,0:T(8,128)(2,1)S(1)}, bf16[32,384]{1,0:T(8,128)(2,1)S(1)}, u32[]{:S(2)}, u32[]{:S(2)}) %collective-permute-start.7) | collective-permute-done | bytes 24608 | tf_op jit(solution)/shard_map/ppermute | solution.py:403
  37.5 1.0 %collective-permute-done.6.refs_1_ = bf16[32,384]{1,0:T(8,128)(2,1)S(1)} collective-permute-done((bf16[32,384]{1,0:T(8,128)(2,1)S(1)}, bf16[32,384]{1,0:T(8,128)(2,1)S(1)}, u32[]{:S(2)}, u32[]{:S(2)}) %collective-permute-start.6) | collective-permute-done | bytes 24608 | tf_op jit(solution)/shard_map/ppermute | solution.py:403
  38.5 0.0 collective-permute-done.9.rfar_outer
  38.5 0.0 collective-permute-done.10.rnear_outer
  38.5 1.2 %hidden_rim.1.hidden = bf16[12,192,128]{2,1,0:T(8,128)(2,1)S(1)} custom-call(bf16[576,128]{1,0:T(8,128)(2,1)S(1)} %collective-permute-done.2.rfar, bf16[576,128]{1,0:T(8,128)(2,1)S(1)} %collective-permute-done.3.rnear, bf16[320,128]{1,0:T(8,128)(2,1)S(1)} %collective-permute-done.9.rfar_outer, bf16[320,128]{1,0:T(8,128)(2,1)S(1)} %collective-permute-done.10.rnear_outer, ...), custom_call_target="tpu_custom_call" | custom-call | flops 1000000000 | bytes 1000000 | tf_op jit(solution)/shard_map/hidden_rim/pallas_call | solution.py:477
  39.8 1.6 %collective-permute-start.11 = (bf16[32,384]{1,0:T(8,128)(2,1)S(1)}, bf16[32,384]{1,0:T(8,128)(2,1)S(1)}, u32[]{:S(2)}, u32[]{:S(2)}) collective-permute-start(bf16[32,384]{1,0:T(8,128)(2,1)S(1)} %add_parts.5.refs_0_), channel_id=1, source_target_pairs={{0,1},{1,0},{2,3},{3,2},{4,5},{5,4},{6,7},{7,6},{8,9},{9,8},{10,11... | collective-permute-start | bytes 73736 | tf_op jit(solution)/shard_map/ppermute | solution.py:403
  41.3 1.6 %closure.1 = bf16[1,16,8,8,128]{4,3,2,1,0:T(8,128)(2,1)} custom-call(bf16[12,192,128]{2,1,0:T(8,128)(2,1)S(1)} %hidden_rim.1.hidden, bf16[128,1920]{1,0:T(8,128)(2,1)S(1)} %get-tuple-element.64.t2, f32[128,128]{1,0:T(8,128)S(1)} %get-tuple-element.65.b2), custom_call_target="tpu_custom_call" | custom-call | flops 1000000000 | bytes 1000000 | tf_op jit(solution)/shard_map/closure/pallas_call | solution.py:486
  42.9 0.8 %collective-permute-done.11.refs_1_ = bf16[32,384]{1,0:T(8,128)(2,1)S(1)} collective-permute-done((bf16[32,384]{1,0:T(8,128)(2,1)S(1)}, bf16[32,384]{1,0:T(8,128)(2,1)S(1)}, u32[]{:S(2)}, u32[]{:S(2)}) %collective-permute-start.11) | collective-permute-done | bytes 24608 | tf_op jit(solution)/shard_map/ppermute | solution.py:403
  43.7 0.8 %finish.1 = (f32[128,27]{1,0:T(8,128)}, f32[256,27]{1,0:T(8,128)}, f32[1,16]{1,0:T(1,128)}) custom-call(bf16[32,384]{1,0:T(8,128)(2,1)S(1)} %add_parts.5.refs_0_, bf16[32,384]{1,0:T(8,128)(2,1)S(1)} %collective-permute-done.11.refs_1_), custom_call_target="tpu_custom_call" | custom-call | flops 10000000 | bytes 1000000 | tf_op jit(solution)/shard_map/finish/pallas_call | solution.py:497
  (3 shorter events, 0.1 us)
Async XLA Ops:
  0.6 1.0 %copy-start = (bf16[1,16,8,8,128]{4,3,2,1,0:T(8,128)(2,1)S(1)}, bf16[1,16,8,8,128]{4,3,2,1,0:T(8,128)(2,1)}, u32[]{:S(2)}) copy-start(bf16[1,16,8,8,128]{4,3,2,1,0:T(8,128)(2,1)} %cot.1) | copy-start | bytes 786436
  1.6 0.9 %copy-start.1 = (bf16[1,8,8,8,128]{4,3,2,1,0:T(8,128)(2,1)S(1)}, bf16[1,8,8,8,128]{4,3,2,1,0:T(8,128)(2,1)}, u32[]{:S(2)}) copy-start(bf16[1,8,8,8,128]{4,3,2,1,0:T(8,128)(2,1)} %fields.1) | copy-start | bytes 393220
  2.5 6.7 %copy-start.2 = (bf16[27,16,16]{0,2,1:T(8,128)(2,1)S(1)}, bf16[27,16,16]{0,2,1:T(8,128)(2,1)}, u32[]{:S(2)}) copy-start(bf16[27,16,16]{0,2,1:T(8,128)(2,1)} %param.15) | copy-start | bytes 41476
  2.5 6.7 %copy-start.3 = (bf16[27,16,8]{0,2,1:T(8,128)(2,1)S(1)}, bf16[27,16,8]{0,2,1:T(8,128)(2,1)}, u32[]{:S(2)}) copy-start(bf16[27,16,8]{0,2,1:T(8,128)(2,1)} %param.13) | copy-start | bytes 20740
  2.5 6.7 %copy-start.4 = (f32[16]{0:T(128)S(1)}, f32[16]{0:T(128)}, u32[]{:S(2)}) copy-start(f32[16]{0:T(128)} %param.14) | copy-start | bytes 196
  2.5 6.7 %copy-start.5 = (f32[16]{0:T(128)S(1)}, f32[16]{0:T(128)}, u32[]{:S(2)}) copy-start(f32[16]{0:T(128)} %param.16) | copy-start | bytes 196
  2.6 9.3 %collective-permute-start = (bf16[512,128]{1,0:T(8,128)(2,1)S(1)}, bf16[512,128]{1,0:T(8,128)(2,1)S(1)}, u32[]{:S(2)}, u32[]{:S(2)}) collective-permute-start(bf16[512,128]{1,0:T(8,128)(2,1)S(1)} %get-tuple-element.37), channel_id=1, source_target_pairs={{0,0},{8,16},{16,8},{24,24},{1,1},{9,17},{17,9},{25,25},{2,2},{10,... | collective-permute-start | bytes 393224 | tf_op jit(solution)/shard_map/ppermute | solution.py:397
  3.3 9.1 %collective-permute-start.1 = (bf16[512,128]{1,0:T(8,128)(2,1)S(1)}, bf16[512,128]{1,0:T(8,128)(2,1)S(1)}, u32[]{:S(2)}, u32[]{:S(2)}) collective-permute-start(bf16[512,128]{1,0:T(8,128)(2,1)S(1)} %get-tuple-element.38), channel_id=1, source_target_pairs={{0,8},{8,0},{16,24},{24,16},{1,9},{9,1},{17,25},{25,17},{2,10},{10... | collective-permute-start | bytes 393224 | tf_op jit(solution)/shard_map/ppermute | solution.py:398
  12.7 4.6 %collective-permute-start.2 = (bf16[576,128]{1,0:T(8,128)(2,1)S(1)}, bf16[576,128]{1,0:T(8,128)(2,1)S(1)}, u32[]{:S(2)}, u32[]{:S(2)}) collective-permute-start(bf16[576,128]{1,0:T(8,128)(2,1)S(1)} %get-tuple-element.45), channel_id=1, source_target_pairs={{0,0},{2,4},{4,2},{6,6},{1,1},{3,5},{5,3},{7,7},{8,8},{10,12},{12,... | collective-permute-start | bytes 442376 | tf_op jit(solution)/shard_map/ppermute | solution.py:397
  13.4 3.9 %collective-permute-start.3 = (bf16[576,128]{1,0:T(8,128)(2,1)S(1)}, bf16[576,128]{1,0:T(8,128)(2,1)S(1)}, u32[]{:S(2)}, u32[]{:S(2)}) collective-permute-start(bf16[576,128]{1,0:T(8,128)(2,1)S(1)} %get-tuple-element.46), channel_id=1, source_target_pairs={{0,2},{2,0},{4,6},{6,4},{1,3},{3,1},{5,7},{7,5},{8,10},{10,8},{12,... | collective-permute-start | bytes 442376 | tf_op jit(solution)/shard_map/ppermute | solution.py:398
  16.3 1.0 %copy-start.6 = (bf16[128,768]{1,0:T(8,128)(2,1)S(1)}, bf16[128,768]{1,0:T(8,128)(2,1)}, u32[]{:S(2)}) copy-start(bf16[128,768]{1,0:T(8,128)(2,1)} %constant.15.clone.rep2) | copy-start | bytes 589828
  16.3 1.0 %copy-start.7 = (bf16[640,128]{1,0:T(8,128)(2,1)S(1)}, bf16[640,128]{1,0:T(8,128)(2,1)}, u32[]{:S(2)}) copy-start(bf16[640,128]{1,0:T(8,128)(2,1)} %constant.13.clone.e2t) | copy-start | bytes 491524
  16.3 1.1 %copy-start.8 = (bf16[128,384]{1,0:T(8,128)(2,1)S(1)}, bf16[128,384]{1,0:T(8,128)(2,1)}, u32[]{:S(2)}) copy-start(bf16[128,384]{1,0:T(8,128)(2,1)} %constant.14.clone.rep1) | copy-start | bytes 294916
  16.4 1.1 %copy-start.9 = (bf16[384,128]{1,0:T(8,128)(2,1)S(1)}, bf16[384,128]{1,0:T(8,128)(2,1)}, u32[]{:S(2)}) copy-start(bf16[384,128]{1,0:T(8,128)(2,1)} %constant.12.clone.e1t) | copy-start | bytes 294916
  16.4 1.1 %copy-start.10 = (f32[1,640]{1,0:T(1,128)S(1)}, f32[1,640]{1,0:T(1,128)}, u32[]{:S(2)}) copy-start(f32[1,640]{1,0:T(1,128)} %constant.17.clone.y2) | copy-start | bytes 7684
  16.4 1.1 %copy-start.11 = (f32[1,384]{1,0:T(1,128)S(1)}, f32[1,384]{1,0:T(1,128)}, u32[]{:S(2)}) copy-start(f32[1,384]{1,0:T(1,128)} %constant.16.clone.y1) | copy-start | bytes 4612
  20.6 2.6 %collective-permute-start.4 = (f32[32,384]{1,0:T(8,128)S(1)}, f32[32,384]{1,0:T(8,128)S(1)}, u32[]{:S(2)}, u32[]{:S(2)}) collective-permute-start(f32[32,384]{1,0:T(8,128)S(1)} %get-tuple-element.56.refs_0_), channel_id=1, source_target_pairs={{0,2},{2,0},{4,6},{6,4},{1,3},{3,1},{5,7},{7,5},{8,10},{10,8},{12,... | collective-permute-start | bytes 147464 | tf_op jit(solution)/shard_map/ppermute | solution.py:403
  23.5 15.1 %collective-permute-start.9 = (bf16[320,128]{1,0:T(8,128)(2,1)S(1)}, bf16[320,128]{1,0:T(8,128)(2,1)S(1)}, u32[]{:S(2)}, u32[]{:S(2)}) collective-permute-start(bf16[320,128]{1,0:T(8,128)(2,1)S(1)} %get-tuple-element.59), channel_id=1, source_target_pairs={{0,0},{2,4},{4,2},{6,6},{1,1},{3,5},{5,3},{7,7},{8,8},{10,12},{12,... | collective-permute-start | bytes 245768 | tf_op jit(solution)/shard_map/ppermute | solution.py:397
  24.1 14.4 %collective-permute-start.10 = (bf16[320,128]{1,0:T(8,128)(2,1)S(1)}, bf16[320,128]{1,0:T(8,128)(2,1)S(1)}, u32[]{:S(2)}, u32[]{:S(2)}) collective-permute-start(bf16[320,128]{1,0:T(8,128)(2,1)S(1)} %get-tuple-element.60), channel_id=1, source_target_pairs={{0,2},{2,0},{4,6},{6,4},{1,3},{3,1},{5,7},{7,5},{8,10},{10,8},{12,... | collective-permute-start | bytes 245768 | tf_op jit(solution)/shard_map/ppermute | solution.py:398
  27.5 3.8 %collective-permute-start.5 = (bf16[32,384]{1,0:T(8,128)(2,1)S(1)}, bf16[32,384]{1,0:T(8,128)(2,1)S(1)}, u32[]{:S(2)}, u32[]{:S(2)}) collective-permute-start(bf16[32,384]{1,0:T(8,128)(2,1)S(1)} %add_parts.3.refs_0_), channel_id=1, source_target_pairs={{0,4},{2,6},{4,0},{6,2},{1,5},{3,7},{5,1},{7,3},{8,12},{10,14},{12... | collective-permute-start | bytes 73736 | tf_op jit(solution)/shard_map/ppermute | solution.py:403
  31.4 5.7 %collective-permute-start.8 = (bf16[32,384]{1,0:T(8,128)(2,1)S(1)}, bf16[32,384]{1,0:T(8,128)(2,1)S(1)}, u32[]{:S(2)}, u32[]{:S(2)}) collective-permute-start(bf16[32,384]{1,0:T(8,128)(2,1)S(1)} %add_parts.4.refs_0_), channel_id=1, source_target_pairs={{0,24},{8,16},{16,8},{24,0},{1,25},{9,17},{17,9},{25,1},{2,26},{10... | collective-permute-start | bytes 73736 | tf_op jit(solution)/shard_map/ppermute | solution.py:403
  32.8 4.7 %collective-permute-start.7 = (bf16[32,384]{1,0:T(8,128)(2,1)S(1)}, bf16[32,384]{1,0:T(8,128)(2,1)S(1)}, u32[]{:S(2)}, u32[]{:S(2)}) collective-permute-start(bf16[32,384]{1,0:T(8,128)(2,1)S(1)} %add_parts.4.refs_0_), channel_id=1, source_target_pairs={{0,16},{8,24},{16,0},{24,8},{1,17},{9,25},{17,1},{25,9},{2,18},{10... | collective-permute-start | bytes 73736 | tf_op jit(solution)/shard_map/ppermute | solution.py:403
  34.6 3.8 %collective-permute-start.6 = (bf16[32,384]{1,0:T(8,128)(2,1)S(1)}, bf16[32,384]{1,0:T(8,128)(2,1)S(1)}, u32[]{:S(2)}, u32[]{:S(2)}) collective-permute-start(bf16[32,384]{1,0:T(8,128)(2,1)S(1)} %add_parts.4.refs_0_), channel_id=1, source_target_pairs={{0,8},{8,0},{16,24},{24,16},{1,9},{9,1},{17,25},{25,17},{2,10},{10... | collective-permute-start | bytes 73736 | tf_op jit(solution)/shard_map/ppermute | solution.py:403
  39.8 3.9 %collective-permute-start.11 = (bf16[32,384]{1,0:T(8,128)(2,1)S(1)}, bf16[32,384]{1,0:T(8,128)(2,1)S(1)}, u32[]{:S(2)}, u32[]{:S(2)}) collective-permute-start(bf16[32,384]{1,0:T(8,128)(2,1)S(1)} %add_parts.5.refs_0_), channel_id=1, source_target_pairs={{0,1},{1,0},{2,3},{3,2},{4,5},{5,4},{6,7},{7,6},{8,9},{9,8},{10,11... | collective-permute-start | bytes 73736 | tf_op jit(solution)/shard_map/ppermute | solution.py:403

commit v10 on v9

--- a/solution.py
+++ b/solution.py
@@ -391,10 +391,12 @@
     return jax.ShapeDtypeStruct(dims, dtype)
 
 
-def exchange(near, far, axis):
+def exchange(near, far, axis, ends=True):
     count = lax.axis_size(axis)
-    shifted_pairs = [(i, min(max(i - 1 + 2 * (i % 2), 0), count - 1)) for i in range(count)]
-    far = lax.ppermute(far, axis, shifted_pairs)
+    pairs = [(i, i - 1 + 2 * (i % 2)) for i in range(1, count - 1)]
+    if ends:
+        pairs = [(0, 0), *pairs, (count - 1, count - 1)]
+    far = lax.ppermute(far, axis, pairs)
     return lax.ppermute(near, axis, [(i, i ^ 1) for i in range(count)]), far
 
 
@@ -449,7 +451,10 @@
     xfar, xnear, t1o, tbo = lax.optimization_barrier((xfar, xnear, t1o, tbo))
     inner, outer = shape((planes + 4) * 48, Z), shape(128 + (planes + 4) * 16, Z)
     near, far = call(functools.partial(join_kernel, counts), (inner, inner), "join_strips")(xfar, xnear, f_rows, c_rows)
-    rnear, rfar = exchange(near, far, "radial")
+    rnear, rfar = exchange(near, far, "radial", ends=False)
+    near_outer, far_outer = call(functools.partial(join_outer_kernel, counts), (outer, outer), "join_outer")(
+        xfar, xnear, f_rows, c_rows)
+    rnear_outer, rfar_outer = exchange(near_outer, far_outer, "radial", ends=False)
     fs, cs, pre, back = call(
         functools.partial(own_kernel, counts),
         (shape(256, wide + 4 * Z), shape(384, wide), shape(128, planes * Z, dtype=F32), shape(128, planes * Z, dtype=F32)),
@@ -466,14 +471,8 @@
 
     steps = rounds("radial", 2) + rounds("stream", 4) + rounds("snap", 2)
     arrived = swap(payload, *steps[0])
-    payload, f_rows = lax.optimization_barrier((add(payload, arrived), f_rows))
+    payload = add(payload, arrived)
     arrived = swap(payload, *steps[1])
-    near_outer, far_outer = call(
-        functools.partial(join_outer_kernel, counts), (outer, outer), "join_outer", flops=1_000_000_000
-    )(xfar, xnear, f_rows, c_rows)
-    rnear_outer, rfar_outer = exchange(near_outer, far_outer, "radial")
-    payload = add(payload, arrived)
-    arrived = swap(payload, *steps[2])
     hidden = call(
         functools.partial(hidden_rim_kernel, counts),
         shape(planes + 4, 192, Z),
@@ -482,6 +481,8 @@
         flops=1_000_000_000,
     )(rfar, rnear, rfar_outer, rnear_outer, hidden, fs, t1o, t1d, b1)
     payload, hidden = lax.optimization_barrier((add(payload, arrived), hidden))
+    arrived = swap(payload, *steps[2])
+    payload = add(payload, arrived)
     arrived = swap(payload, *steps[3])
     closure = call(
         closure_kernel, shape(*cotangent.shape), "closure", (pltpu.VMEM((640, wide), BF16),), flops=1_000_000_000

time: 44.7 us -> 40 us (0.89)
  waiting for transfers between devices: 8.63 us -> 5.77 us
  starting transfers between devices: 22 us -> 20.1 us
    ppermute x6, waiting for transfers between devices: 8.11 us -> 5.26 us  [swap(): lax.ppermute(v, axis, [(i, i ^ mask) for i in range(count)])]
    ppermute x3, starting transfers between devices: 12.2 us -> 10.2 us  [exchange(): return (lax.ppermute(near, axis, [(i, i ^ 1) for i in range(count)]), far)]
  transfers between devices with their start and end apart: 12 -> 12, of which waited for: 7 -> 6; matrix products, arithmetic and copies ran while one was open for 0% -> 0% of each run, Pallas kernels for 12% -> 25%
where the time goes in v10:
time: 40 us; the launch traced here: 39.8 us
  starting transfers between devices  20.1 us (50%)
  Pallas kernels  11.1 us (28%)
  waiting for transfers between devices  5.77 us (14%)
  local copies, waits for them, and re-layouts  1.98 us (5%)
  between operations  0.81 us (2%)
    ppermute x3, starting transfers between devices, exchange(): return (lax.ppermute(near, axis, [(i, i ^ 1) for i in range(count)]), far)  10.2 us
    ppermute x6, starting transfers between devices, swap(): lax.ppermute(v, axis, [(i, i ^ mask) for i in range(count)])  7.96 us
    ppermute x6, waiting for transfers between devices, swap(): lax.ppermute(v, axis, [(i, i ^ mask) for i in range(count)])  5.26 us
    pallas_call x1, Pallas kernels, local(): call(functools.partial(rim_kernel, counts), (shape(planes, 128, Z), shape...  3.13 us
    pallas_call x1, Pallas kernels, local(): call(band_kernel, (shape(192, 768), shape(128, 384), shape(192, 768), sha...  2.69 us
    ppermute x3, starting transfers between devices, exchange(): far = lax.ppermute(far, axis, pairs)  2 us
    unnamed x24, local copies, waits for them, and re-layouts  1.98 us
    pallas_call x1, Pallas kernels, local(): call(closure_kernel, shape(*cotangent.shape), 'closure', (pltpu.VMEM((640...  1.56 us
  transfers between devices with their start and end apart: 12, of which 6 were waited for; matrix products, arithmetic and copies ran while one was open for 0% of the time, Pallas kernels for 25%

profile of v10, /device:TPU:0, one launch (start us, length us, event | category | flops | bytes accessed | tf_op | source)
XLA Modules:
  0.0 39.8 jit_solution(9599204504188649374)
XLA Ops:
  0.6 0.0 copy-start
  0.6 0.9 %copy-done = bf16[1,16,8,8,128]{4,3,2,1,0:T(8,128)(2,1)S(1)} copy-done((bf16[1,16,8,8,128]{4,3,2,1,0:T(8,128)(2,1)S(1)}, bf16[1,16,8,8,128]{4,3,2,1,0:T(8,128)(2,1)}, u32[]{:S(2)}) %copy-start) | copy-done | bytes 262168
  1.6 0.0 copy-start.1
  1.6 0.9 %copy-done.1 = bf16[1,8,8,8,128]{4,3,2,1,0:T(8,128)(2,1)S(1)} copy-done((bf16[1,8,8,8,128]{4,3,2,1,0:T(8,128)(2,1)S(1)}, bf16[1,8,8,8,128]{4,3,2,1,0:T(8,128)(2,1)}, u32[]{:S(2)}) %copy-start.1) | copy-done | bytes 131096
  2.5 0.0 copy-start.2
  2.5 0.0 copy-start.3
  2.5 0.0 copy-start.4
  2.5 0.0 copy-start.5
  2.5 0.1 pack_strips.1
  2.6 0.7 %collective-permute-start = (bf16[512,128]{1,0:T(8,128)(2,1)S(1)}, bf16[512,128]{1,0:T(8,128)(2,1)S(1)}, u32[]{:S(2)}, u32[]{:S(2)}) collective-permute-start(bf16[512,128]{1,0:T(8,128)(2,1)S(1)} %get-tuple-element.35), channel_id=1, source_target_pairs={{0,0},{8,16},{16,8},{24,24},{1,1},{9,17},{17,9},{25,25},{2,2},{10,... | collective-permute-start | bytes 393224 | tf_op jit(solution)/shard_map/ppermute | solution.py:399
  3.3 5.9 %collective-permute-start.1 = (bf16[512,128]{1,0:T(8,128)(2,1)S(1)}, bf16[512,128]{1,0:T(8,128)(2,1)S(1)}, u32[]{:S(2)}, u32[]{:S(2)}) collective-permute-start(bf16[512,128]{1,0:T(8,128)(2,1)S(1)} %get-tuple-element.36), channel_id=1, source_target_pairs={{0,8},{8,0},{16,24},{24,16},{1,9},{9,1},{17,25},{25,17},{2,10},{10... | collective-permute-start | bytes 393224 | tf_op jit(solution)/shard_map/ppermute | solution.py:400
  9.2 0.0 copy-done.2
  9.2 0.0 copy-done.3
  9.2 0.0 copy-done.4
  9.2 0.0 copy-done.5
  9.2 2.7 %band_matrices.1 = (bf16[192,768]{1,0:T(8,128)(2,1)S(1)}, bf16[128,384]{1,0:T(8,128)(2,1)S(1)}, bf16[192,768]{1,0:T(8,128)(2,1)S(1)}, bf16[128,1152]{1,0:T(8,128...) custom-call(bf16[128,27]{1,0:T(8,128)(2,1)S(1)} %bitcast.16, ...), custom_call_target="tpu_custom_call" | custom-call | flops 4000000000 | bytes 1000000 | tf_op jit(solution)/shard_map/band_matrices/pallas_call | solution.py:444
  11.9 0.0 collective-permute-done.xfar
  11.9 0.5 %collective-permute-done.1.xnear = bf16[512,128]{1,0:T(8,128)(2,1)S(1)} collective-permute-done((bf16[512,128]{1,0:T(8,128)(2,1)S(1)}, bf16[512,128]{1,0:T(8,128)(2,1)S(1)}, u32[]{:S(2)}, u32[]{:S(2)}) %collective-permute-start.1) | collective-permute-done | bytes 131104 | tf_op jit(solution)/shard_map/ppermute | solution.py:400
  12.4 0.3 join_strips.1
  12.7 0.7 %collective-permute-start.2 = (bf16[576,128]{1,0:T(8,128)(2,1)S(1)}, bf16[576,128]{1,0:T(8,128)(2,1)S(1)}, u32[]{:S(2)}, u32[]{:S(2)}) collective-permute-start(bf16[576,128]{1,0:T(8,128)(2,1)S(1)} %get-tuple-element.43), channel_id=1, source_target_pairs={{2,4},{4,2},{3,5},{5,3},{10,12},{12,10},{11,13},{13,11},{18,20},{2... | collective-permute-start | bytes 442376 | tf_op jit(solution)/shard_map/ppermute | solution.py:399
  13.4 2.9 %collective-permute-start.3 = (bf16[576,128]{1,0:T(8,128)(2,1)S(1)}, bf16[576,128]{1,0:T(8,128)(2,1)S(1)}, u32[]{:S(2)}, u32[]{:S(2)}) collective-permute-start(bf16[576,128]{1,0:T(8,128)(2,1)S(1)} %get-tuple-element.44), channel_id=1, source_target_pairs={{0,2},{2,0},{4,6},{6,4},{1,3},{3,1},{5,7},{7,5},{8,10},{10,8},{12,... | collective-permute-start | bytes 442376 | tf_op jit(solution)/shard_map/ppermute | solution.py:400
  16.3 0.2 join_outer.1
  16.6 0.7 %collective-permute-start.6 = (bf16[320,128]{1,0:T(8,128)(2,1)S(1)}, bf16[320,128]{1,0:T(8,128)(2,1)S(1)}, u32[]{:S(2)}, u32[]{:S(2)}) collective-permute-start(bf16[320,128]{1,0:T(8,128)(2,1)S(1)} %get-tuple-element.55), channel_id=1, source_target_pairs={{2,4},{4,2},{3,5},{5,3},{10,12},{12,10},{11,13},{13,11},{18,20},{2... | collective-permute-start | bytes 245768 | tf_op jit(solution)/shard_map/ppermute | solution.py:399
  17.2 1.3 %collective-permute-start.7 = (bf16[320,128]{1,0:T(8,128)(2,1)S(1)}, bf16[320,128]{1,0:T(8,128)(2,1)S(1)}, u32[]{:S(2)}, u32[]{:S(2)}) collective-permute-start(bf16[320,128]{1,0:T(8,128)(2,1)S(1)} %get-tuple-element.56), channel_id=1, source_target_pairs={{0,2},{2,0},{4,6},{6,4},{1,3},{3,1},{5,7},{7,5},{8,10},{10,8},{12,... | collective-permute-start | bytes 245768 | tf_op jit(solution)/shard_map/ppermute | solution.py:400
  18.6 0.0 copy-start.6
  18.6 0.0 copy-start.7
  18.6 0.0 copy-start.8
  18.6 0.0 copy-start.9
  18.6 0.0 copy-start.10
  18.6 0.0 copy-start.11
  18.6 0.9 %own_rows.1 = (bf16[256,2048]{1,0:T(8,128)(2,1)S(1)}, bf16[384,1536]{1,0:T(8,128)(2,1)S(1)}, f32[128,1024]{1,0:T(8,128)S(1)}, f32[128,1024]{1,0:T(8,128)S(1)}) custom-call(bf16[512,128]{1,0:T(8,128)(2,1)S(1)} %collective-permute-done.xfar, bf16[512,128]{1,0:T(8,128)(2,1)S(1)} %collective-permute-done.1.xnear, ...), custom_call_target="tpu_custom_call" | custom-call | flops 1000000000 | bytes 1000000 | tf_op jit(solution)/shard_map/own_rows/pallas_call | solution.py:458
  19.6 0.0 collective-permute-done.2.rfar
  19.6 0.0 collective-permute-done.3.rnear
  19.6 0.0 copy-done.6
  19.6 0.0 copy-done.7
  19.6 0.0 copy-done.8
  19.6 0.0 copy-done.9
  19.7 0.0 copy-done.10
  19.7 0.0 copy-done.11
  19.7 3.1 %gradients.1 = (bf16[8,128,128]{2,1,0:T(8,128)(2,1)S(1)}, f32[32,384]{1,0:T(8,128)S(1)}) custom-call(bf16[576,128]{1,0:T(8,128)(2,1)S(1)} %collective-permute-done.2.rfar, bf16[576,128]{1,0:T(8,128)(2,1)S(1)} %collective-permute-done.3.rnear, bf16[256,2048]{1,0:T(8,128)(2,1)S(1)} %get-tuple-element.48.fs, bf16[384,1536]{1,0:T(8,128)(2,1)S(1)} %get-tuple-element.49.cs, ...), custom_call_target="tpu_custom_call" | custom-call | flops 2000000000 | bytes 1000000 | tf_op jit(solution)/shard_map/gradients/pallas_call | solution.py:464
  22.8 0.1 collective-permute-start.4
  22.9 1.2 %collective-permute-done.4.refs_1_ = f32[32,384]{1,0:T(8,128)S(1)} collective-permute-done((f32[32,384]{1,0:T(8,128)S(1)}, f32[32,384]{1,0:T(8,128)S(1)}, u32[]{:S(2)}, u32[]{:S(2)}) %collective-permute-start.4) | collective-permute-done | bytes 49184 | tf_op jit(solution)/shard_map/ppermute | solution.py:405
  24.1 1.8 %collective-permute-start.5 = (bf16[32,384]{1,0:T(8,128)(2,1)S(1)}, bf16[32,384]{1,0:T(8,128)(2,1)S(1)}, u32[]{:S(2)}, u32[]{:S(2)}) collective-permute-start(bf16[32,384]{1,0:T(8,128)(2,1)S(1)} %add_parts.3.refs_0_), channel_id=1, source_target_pairs={{0,4},{2,6},{4,0},{6,2},{1,5},{3,7},{5,1},{7,3},{8,12},{10,14},{12... | collective-permute-start | bytes 73736 | tf_op jit(solution)/shard_map/ppermute | solution.py:405
  26.0 0.0 collective-permute-done.6.rfar_outer
  26.0 0.0 collective-permute-done.7.rnear_outer
  26.0 1.3 %hidden_rim.1.hidden = bf16[12,192,128]{2,1,0:T(8,128)(2,1)S(1)} custom-call(bf16[576,128]{1,0:T(8,128)(2,1)S(1)} %collective-permute-done.2.rfar, bf16[576,128]{1,0:T(8,128)(2,1)S(1)} %collective-permute-done.3.rnear, bf16[320,128]{1,0:T(8,128)(2,1)S(1)} %collective-permute-done.6.rfar_outer, bf16[320,128]{1,0:T(8,128)(2,1)S(1)} %collective-permute-done.7.rnear_outer, ...), custom_call_target="tpu_custom_call" | custom-call | flops 1000000000 | bytes 1000000 | tf_op jit(solution)/shard_map/hidden_rim/pallas_call | solution.py:476
  27.3 0.8 %collective-permute-done.5.refs_1_ = bf16[32,384]{1,0:T(8,128)(2,1)S(1)} collective-permute-done((bf16[32,384]{1,0:T(8,128)(2,1)S(1)}, bf16[32,384]{1,0:T(8,128)(2,1)S(1)}, u32[]{:S(2)}, u32[]{:S(2)}) %collective-permute-start.5) | collective-permute-done | bytes 24608 | tf_op jit(solution)/shard_map/ppermute | solution.py:405
  28.1 1.4 %collective-permute-start.10 = (bf16[32,384]{1,0:T(8,128)(2,1)S(1)}, bf16[32,384]{1,0:T(8,128)(2,1)S(1)}, u32[]{:S(2)}, u32[]{:S(2)}) collective-permute-start(bf16[32,384]{1,0:T(8,128)(2,1)S(1)} %add_parts.4.refs_0_), channel_id=1, source_target_pairs={{0,24},{8,16},{16,8},{24,0},{1,25},{9,17},{17,9},{25,1},{2,26},{10... | collective-permute-start | bytes 73736 | tf_op jit(solution)/shard_map/ppermute | solution.py:405
  29.5 0.8 %collective-permute-start.8 = (bf16[32,384]{1,0:T(8,128)(2,1)S(1)}, bf16[32,384]{1,0:T(8,128)(2,1)S(1)}, u32[]{:S(2)}, u32[]{:S(2)}) collective-permute-start(bf16[32,384]{1,0:T(8,128)(2,1)S(1)} %add_parts.4.refs_0_), channel_id=1, source_target_pairs={{0,8},{8,0},{16,24},{24,16},{1,9},{9,1},{17,25},{25,17},{2,10},{10... | collective-permute-start | bytes 73736 | tf_op jit(solution)/shard_map/ppermute | solution.py:405
  30.3 2.2 %collective-permute-start.9 = (bf16[32,384]{1,0:T(8,128)(2,1)S(1)}, bf16[32,384]{1,0:T(8,128)(2,1)S(1)}, u32[]{:S(2)}, u32[]{:S(2)}) collective-permute-start(bf16[32,384]{1,0:T(8,128)(2,1)S(1)} %add_parts.4.refs_0_), channel_id=1, source_target_pairs={{0,16},{8,24},{16,0},{24,8},{1,17},{9,25},{17,1},{25,9},{2,18},{10... | collective-permute-start | bytes 73736 | tf_op jit(solution)/shard_map/ppermute | solution.py:405
  32.5 1.2 %collective-permute-done.10.refs_3_ = bf16[32,384]{1,0:T(8,128)(2,1)S(1)} collective-permute-done((bf16[32,384]{1,0:T(8,128)(2,1)S(1)}, bf16[32,384]{1,0:T(8,128)(2,1)S(1)}, u32[]{:S(2)}, u32[]{:S(2)}) %collective-permute-start.10) | collective-permute-done | bytes 24608 | tf_op jit(solution)/shard_map/ppermute | solution.py:405
  33.7 0.0 collective-permute-done.8.refs_1_
  33.8 1.3 %collective-permute-done.9.refs_2_ = bf16[32,384]{1,0:T(8,128)(2,1)S(1)} collective-permute-done((bf16[32,384]{1,0:T(8,128)(2,1)S(1)}, bf16[32,384]{1,0:T(8,128)(2,1)S(1)}, u32[]{:S(2)}, u32[]{:S(2)}) %collective-permute-start.9) | collective-permute-done | bytes 24608 | tf_op jit(solution)/shard_map/ppermute | solution.py:405
  35.1 1.6 %collective-permute-start.11 = (bf16[32,384]{1,0:T(8,128)(2,1)S(1)}, bf16[32,384]{1,0:T(8,128)(2,1)S(1)}, u32[]{:S(2)}, u32[]{:S(2)}) collective-permute-start(bf16[32,384]{1,0:T(8,128)(2,1)S(1)} %add_parts.5.refs_0_), channel_id=1, source_target_pairs={{0,1},{1,0},{2,3},{3,2},{4,5},{5,4},{6,7},{7,6},{8,9},{9,8},{10,11... | collective-permute-start | bytes 73736 | tf_op jit(solution)/shard_map/ppermute | solution.py:405
  36.6 1.6 %closure.1 = bf16[1,16,8,8,128]{4,3,2,1,0:T(8,128)(2,1)} custom-call(bf16[12,192,128]{2,1,0:T(8,128)(2,1)S(1)} %hidden_rim.1.hidden, bf16[128,1920]{1,0:T(8,128)(2,1)S(1)} %get-tuple-element.60.t2, f32[128,128]{1,0:T(8,128)S(1)} %get-tuple-element.61.b2), custom_call_target="tpu_custom_call" | custom-call | flops 1000000000 | bytes 1000000 | tf_op jit(solution)/shard_map/closure/pallas_call | solution.py:487
  38.2 0.8 %collective-permute-done.11.refs_1_ = bf16[32,384]{1,0:T(8,128)(2,1)S(1)} collective-permute-done((bf16[32,384]{1,0:T(8,128)(2,1)S(1)}, bf16[32,384]{1,0:T(8,128)(2,1)S(1)}, u32[]{:S(2)}, u32[]{:S(2)}) %collective-permute-start.11) | collective-permute-done | bytes 24608 | tf_op jit(solution)/shard_map/ppermute | solution.py:405
  39.0 0.8 %finish.1 = (f32[128,27]{1,0:T(8,128)}, f32[256,27]{1,0:T(8,128)}, f32[1,16]{1,0:T(1,128)}) custom-call(bf16[32,384]{1,0:T(8,128)(2,1)S(1)} %add_parts.5.refs_0_, bf16[32,384]{1,0:T(8,128)(2,1)S(1)} %collective-permute-done.11.refs_1_), custom_call_target="tpu_custom_call" | custom-call | flops 10000000 | bytes 1000000 | tf_op jit(solution)/shard_map/finish/pallas_call | solution.py:498
  (3 shorter events, 0.1 us)
Async XLA Ops:
  0.6 1.0 %copy-start = (bf16[1,16,8,8,128]{4,3,2,1,0:T(8,128)(2,1)S(1)}, bf16[1,16,8,8,128]{4,3,2,1,0:T(8,128)(2,1)}, u32[]{:S(2)}) copy-start(bf16[1,16,8,8,128]{4,3,2,1,0:T(8,128)(2,1)} %cot.1) | copy-start | bytes 786436
  1.6 0.9 %copy-start.1 = (bf16[1,8,8,8,128]{4,3,2,1,0:T(8,128)(2,1)S(1)}, bf16[1,8,8,8,128]{4,3,2,1,0:T(8,128)(2,1)}, u32[]{:S(2)}) copy-start(bf16[1,8,8,8,128]{4,3,2,1,0:T(8,128)(2,1)} %fields.1) | copy-start | bytes 393220
  2.5 6.7 %copy-start.2 = (bf16[27,16,16]{0,2,1:T(8,128)(2,1)S(1)}, bf16[27,16,16]{0,2,1:T(8,128)(2,1)}, u32[]{:S(2)}) copy-start(bf16[27,16,16]{0,2,1:T(8,128)(2,1)} %param.15) | copy-start | bytes 41476
  2.5 6.7 %copy-start.3 = (bf16[27,16,8]{0,2,1:T(8,128)(2,1)S(1)}, bf16[27,16,8]{0,2,1:T(8,128)(2,1)}, u32[]{:S(2)}) copy-start(bf16[27,16,8]{0,2,1:T(8,128)(2,1)} %param.13) | copy-start | bytes 20740
  2.5 6.7 %copy-start.4 = (f32[16]{0:T(128)S(1)}, f32[16]{0:T(128)}, u32[]{:S(2)}) copy-start(f32[16]{0:T(128)} %param.14) | copy-start | bytes 196
  2.5 6.7 %copy-start.5 = (f32[16]{0:T(128)S(1)}, f32[16]{0:T(128)}, u32[]{:S(2)}) copy-start(f32[16]{0:T(128)} %param.16) | copy-start | bytes 196
  2.6 9.3 %collective-permute-start = (bf16[512,128]{1,0:T(8,128)(2,1)S(1)}, bf16[512,128]{1,0:T(8,128)(2,1)S(1)}, u32[]{:S(2)}, u32[]{:S(2)}) collective-permute-start(bf16[512,128]{1,0:T(8,128)(2,1)S(1)} %get-tuple-element.35), channel_id=1, source_target_pairs={{0,0},{8,16},{16,8},{24,24},{1,1},{9,17},{17,9},{25,25},{2,2},{10,... | collective-permute-start | bytes 393224 | tf_op jit(solution)/shard_map/ppermute | solution.py:399
  3.3 9.1 %collective-permute-start.1 = (bf16[512,128]{1,0:T(8,128)(2,1)S(1)}, bf16[512,128]{1,0:T(8,128)(2,1)S(1)}, u32[]{:S(2)}, u32[]{:S(2)}) collective-permute-start(bf16[512,128]{1,0:T(8,128)(2,1)S(1)} %get-tuple-element.36), channel_id=1, source_target_pairs={{0,8},{8,0},{16,24},{24,16},{1,9},{9,1},{17,25},{25,17},{2,10},{10... | collective-permute-start | bytes 393224 | tf_op jit(solution)/shard_map/ppermute | solution.py:400
  12.7 6.8 %collective-permute-start.2 = (bf16[576,128]{1,0:T(8,128)(2,1)S(1)}, bf16[576,128]{1,0:T(8,128)(2,1)S(1)}, u32[]{:S(2)}, u32[]{:S(2)}) collective-permute-start(bf16[576,128]{1,0:T(8,128)(2,1)S(1)} %get-tuple-element.43), channel_id=1, source_target_pairs={{2,4},{4,2},{3,5},{5,3},{10,12},{12,10},{11,13},{13,11},{18,20},{2... | collective-permute-start | bytes 442376 | tf_op jit(solution)/shard_map/ppermute | solution.py:399
  13.4 6.2 %collective-permute-start.3 = (bf16[576,128]{1,0:T(8,128)(2,1)S(1)}, bf16[576,128]{1,0:T(8,128)(2,1)S(1)}, u32[]{:S(2)}, u32[]{:S(2)}) collective-permute-start(bf16[576,128]{1,0:T(8,128)(2,1)S(1)} %get-tuple-element.44), channel_id=1, source_target_pairs={{0,2},{2,0},{4,6},{6,4},{1,3},{3,1},{5,7},{7,5},{8,10},{10,8},{12,... | collective-permute-start | bytes 442376 | tf_op jit(solution)/shard_map/ppermute | solution.py:400
  16.6 9.4 %collective-permute-start.6 = (bf16[320,128]{1,0:T(8,128)(2,1)S(1)}, bf16[320,128]{1,0:T(8,128)(2,1)S(1)}, u32[]{:S(2)}, u32[]{:S(2)}) collective-permute-start(bf16[320,128]{1,0:T(8,128)(2,1)S(1)} %get-tuple-element.55), channel_id=1, source_target_pairs={{2,4},{4,2},{3,5},{5,3},{10,12},{12,10},{11,13},{13,11},{18,20},{2... | collective-permute-start | bytes 245768 | tf_op jit(solution)/shard_map/ppermute | solution.py:399
  17.2 8.8 %collective-permute-start.7 = (bf16[320,128]{1,0:T(8,128)(2,1)S(1)}, bf16[320,128]{1,0:T(8,128)(2,1)S(1)}, u32[]{:S(2)}, u32[]{:S(2)}) collective-permute-start(bf16[320,128]{1,0:T(8,128)(2,1)S(1)} %get-tuple-element.56), channel_id=1, source_target_pairs={{0,2},{2,0},{4,6},{6,4},{1,3},{3,1},{5,7},{7,5},{8,10},{10,8},{12,... | collective-permute-start | bytes 245768 | tf_op jit(solution)/shard_map/ppermute | solution.py:400
  18.6 1.0 %copy-start.6 = (bf16[128,768]{1,0:T(8,128)(2,1)S(1)}, bf16[128,768]{1,0:T(8,128)(2,1)}, u32[]{:S(2)}) copy-start(bf16[128,768]{1,0:T(8,128)(2,1)} %constant.15.clone.rep2) | copy-start | bytes 589828
  18.6 1.0 %copy-start.7 = (bf16[640,128]{1,0:T(8,128)(2,1)S(1)}, bf16[640,128]{1,0:T(8,128)(2,1)}, u32[]{:S(2)}) copy-start(bf16[640,128]{1,0:T(8,128)(2,1)} %constant.13.clone.e2t) | copy-start | bytes 491524
  18.6 1.1 %copy-start.8 = (bf16[384,128]{1,0:T(8,128)(2,1)S(1)}, bf16[384,128]{1,0:T(8,128)(2,1)}, u32[]{:S(2)}) copy-start(bf16[384,128]{1,0:T(8,128)(2,1)} %constant.12.clone.e1t) | copy-start | bytes 294916
  18.6 1.1 %copy-start.9 = (bf16[128,384]{1,0:T(8,128)(2,1)S(1)}, bf16[128,384]{1,0:T(8,128)(2,1)}, u32[]{:S(2)}) copy-start(bf16[128,384]{1,0:T(8,128)(2,1)} %constant.14.clone.rep1) | copy-start | bytes 294916
  18.6 1.1 %copy-start.10 = (f32[1,640]{1,0:T(1,128)S(1)}, f32[1,640]{1,0:T(1,128)}, u32[]{:S(2)}) copy-start(f32[1,640]{1,0:T(1,128)} %constant.17.clone.y2) | copy-start | bytes 7684
  18.6 1.1 %copy-start.11 = (f32[1,384]{1,0:T(1,128)S(1)}, f32[1,384]{1,0:T(1,128)}, u32[]{:S(2)}) copy-start(f32[1,384]{1,0:T(1,128)} %constant.16.clone.y1) | copy-start | bytes 4612
  22.8 1.3 %collective-permute-start.4 = (f32[32,384]{1,0:T(8,128)S(1)}, f32[32,384]{1,0:T(8,128)S(1)}, u32[]{:S(2)}, u32[]{:S(2)}) collective-permute-start(f32[32,384]{1,0:T(8,128)S(1)} %get-tuple-element.54.refs_0_), channel_id=1, source_target_pairs={{0,2},{2,0},{4,6},{6,4},{1,3},{3,1},{5,7},{7,5},{8,10},{10,8},{12,... | collective-permute-start | bytes 147464 | tf_op jit(solution)/shard_map/ppermute | solution.py:405
  24.1 3.9 %collective-permute-start.5 = (bf16[32,384]{1,0:T(8,128)(2,1)S(1)}, bf16[32,384]{1,0:T(8,128)(2,1)S(1)}, u32[]{:S(2)}, u32[]{:S(2)}) collective-permute-start(bf16[32,384]{1,0:T(8,128)(2,1)S(1)} %add_parts.3.refs_0_), channel_id=1, source_target_pairs={{0,4},{2,6},{4,0},{6,2},{1,5},{3,7},{5,1},{7,3},{8,12},{10,14},{12... | collective-permute-start | bytes 73736 | tf_op jit(solution)/shard_map/ppermute | solution.py:405
  28.1 5.7 %collective-permute-start.10 = (bf16[32,384]{1,0:T(8,128)(2,1)S(1)}, bf16[32,384]{1,0:T(8,128)(2,1)S(1)}, u32[]{:S(2)}, u32[]{:S(2)}) collective-permute-start(bf16[32,384]{1,0:T(8,128)(2,1)S(1)} %add_parts.4.refs_0_), channel_id=1, source_target_pairs={{0,24},{8,16},{16,8},{24,0},{1,25},{9,17},{17,9},{25,1},{2,26},{10... | collective-permute-start | bytes 73736 | tf_op jit(solution)/shard_map/ppermute | solution.py:405
  29.5 4.3 %collective-permute-start.8 = (bf16[32,384]{1,0:T(8,128)(2,1)S(1)}, bf16[32,384]{1,0:T(8,128)(2,1)S(1)}, u32[]{:S(2)}, u32[]{:S(2)}) collective-permute-start(bf16[32,384]{1,0:T(8,128)(2,1)S(1)} %add_parts.4.refs_0_), channel_id=1, source_target_pairs={{0,8},{8,0},{16,24},{24,16},{1,9},{9,1},{17,25},{25,17},{2,10},{10... | collective-permute-start | bytes 73736 | tf_op jit(solution)/shard_map/ppermute | solution.py:405
  30.3 4.7 %collective-permute-start.9 = (bf16[32,384]{1,0:T(8,128)(2,1)S(1)}, bf16[32,384]{1,0:T(8,128)(2,1)S(1)}, u32[]{:S(2)}, u32[]{:S(2)}) collective-permute-start(bf16[32,384]{1,0:T(8,128)(2,1)S(1)} %add_parts.4.refs_0_), channel_id=1, source_target_pairs={{0,16},{8,24},{16,0},{24,8},{1,17},{9,25},{17,1},{25,9},{2,18},{10... | collective-permute-start | bytes 73736 | tf_op jit(solution)/shard_map/ppermute | solution.py:405
  35.1 3.9 %collective-permute-start.11 = (bf16[32,384]{1,0:T(8,128)(2,1)S(1)}, bf16[32,384]{1,0:T(8,128)(2,1)S(1)}, u32[]{:S(2)}, u32[]{:S(2)}) collective-permute-start(bf16[32,384]{1,0:T(8,128)(2,1)S(1)} %add_parts.5.refs_0_), channel_id=1, source_target_pairs={{0,1},{1,0},{2,3},{3,2},{4,5},{5,4},{6,7},{7,6},{8,9},{9,8},{10,11... | collective-permute-start | bytes 73736 | tf_op jit(solution)/shard_map/ppermute | solution.py:405

commit v11 on v10

--- a/solution.py
+++ b/solution.py
@@ -74,8 +74,8 @@
     return one_hot(channel == lane), y[:, :1]
 
 
-def plane(ref, x):
-    v = ref[0, :, x].astype(F32)
+def plane(ref, channels, x):
+    v = ref[channels, x].astype(F32)
     return v.reshape(v.shape[0] * v.shape[1], v.shape[2])
 
 
@@ -97,11 +97,11 @@
     return jnp.where(below, low, 0.0), jnp.where(above, high, 0.0)
 
 
-def pack_kernel(fields, cot, near, far, f_rows, c_rows):
+def pack_kernel(inputs, near, far, f_rows, c_rows):
     up_first = lax.axis_index("stream") % 2 == 0
-    count, at = fields.shape[2], 0
-    for ref, out, width in ((fields, f_rows, 4), (cot, c_rows, 2)):
-        rows = [plane(ref, x) for x in range(count)]
+    count, at = inputs.shape[1], 0
+    for channels, out, width in ((slice(0, CI), f_rows, 4), (slice(CI, CI + CH), c_rows, 2)):
+        rows = [plane(inputs, channels, x) for x in range(count)]
         for x, v in enumerate(rows):
             out[x] = v.astype(BF16)
         for low, high in zip(rows[:width], rows[count - width:]):
@@ -437,7 +437,7 @@
         (shape(512, Z), shape(512, Z), shape(planes, CI * 8, Z), shape(planes, CH * 8, Z)),
         "pack_strips",
         flops=4_000_000_000,
-    )(fields, cotangent)
+    )(jnp.concatenate([fields[0], cotangent[0]], axis=0))
     xnear, xfar = exchange(near, far, "stream")
     wide = (planes + 4) * Z
     counts = (lax.axis_size("stream"), lax.axis_size("radial"))
@@ -452,15 +452,16 @@
     inner, outer = shape((planes + 4) * 48, Z), shape(128 + (planes + 4) * 16, Z)
     near, far = call(functools.partial(join_kernel, counts), (inner, inner), "join_strips")(xfar, xnear, f_rows, c_rows)
     rnear, rfar = exchange(near, far, "radial", ends=False)
-    near_outer, far_outer = call(functools.partial(join_outer_kernel, counts), (outer, outer), "join_outer")(
-        xfar, xnear, f_rows, c_rows)
-    rnear_outer, rfar_outer = exchange(near_outer, far_outer, "radial", ends=False)
     fs, cs, pre, back = call(
         functools.partial(own_kernel, counts),
         (shape(256, wide + 4 * Z), shape(384, wide), shape(128, planes * Z, dtype=F32), shape(128, planes * Z, dtype=F32)),
         "own_rows",
         flops=1_000_000_000,
     )(xfar, xnear, f_rows, c_rows, t1o, tbo, b1)
+    f_rows, fs = lax.optimization_barrier((f_rows, fs))
+    near_outer, far_outer = call(functools.partial(join_outer_kernel, counts), (outer, outer), "join_outer")(
+        xfar, xnear, f_rows, c_rows)
+    rnear_outer, rfar_outer = exchange(near_outer, far_outer, "radial", ends=False)
     hidden, payload = call(
         functools.partial(rim_kernel, counts),
         (shape(planes, 128, Z), shape(32, 384, dtype=F32)),

time: 40 us -> 39.1 us (0.978)
  local copies, waits for them, and re-layouts: 1.98 us -> 0.05 us
  other arithmetic: 0 us -> 1.02 us
    unnamed x24 -> x20, local copies, waits for them, and re-layouts: 1.98 us -> 0.05 us
    concatenate x0 -> x1, other arithmetic: none -> 1.02 us  [local(): jnp.concatenate([fields[0], cotangent[0]], axis=0)]
where the time goes in v11:
time: 39.1 us; the launch traced here: 38.9 us
  starting transfers between devices  20.2 us (52%)
  Pallas kernels  11.1 us (28%)
  waiting for transfers between devices  5.78 us (15%)
  other arithmetic  1.02 us (3%)
  between operations  0.84 us (2%)
    ppermute x3, starting transfers between devices, exchange(): return (lax.ppermute(near, axis, [(i, i ^ 1) for i in range(count)]), far)  10.2 us
    ppermute x6, starting transfers between devices, swap(): lax.ppermute(v, axis, [(i, i ^ mask) for i in range(count)])  7.94 us
    ppermute x6, waiting for transfers between devices, swap(): lax.ppermute(v, axis, [(i, i ^ mask) for i in range(count)])  5.28 us
    pallas_call x1, Pallas kernels, local(): call(functools.partial(rim_kernel, counts), (shape(planes, 128, Z), shape...  3.14 us
    pallas_call x1, Pallas kernels, local(): call(band_kernel, (shape(192, 768), shape(128, 384), shape(192, 768), sha...  2.7 us
    ppermute x3, starting transfers between devices, exchange(): far = lax.ppermute(far, axis, pairs)  2 us
    pallas_call x1, Pallas kernels, local(): call(closure_kernel, shape(*cotangent.shape), 'closure', (pltpu.VMEM((640...  1.56 us
    pallas_call x1, Pallas kernels, local(): call(functools.partial(hidden_rim_kernel, counts), shape(planes + 4, 192,...  1.26 us
  transfers between devices with their start and end apart: 12, of which 6 were waited for; matrix products, arithmetic and copies ran while one was open for 0% of the time, Pallas kernels for 25%

profile of v11, /device:TPU:0, one launch (start us, length us, event | category | flops | bytes accessed | tf_op | source)
XLA Modules:
  0.0 38.9 jit_solution(13333759599245755803)
XLA Ops:
  0.6 1.0 %pad_maximum_fusion.inputs = bf16[24,8,8,128]{3,2,1,0:T(8,128)(2,1)S(1)} fusion(bf16[16,8,8,128]{3,2,1,0:T(8,128)(2,1)} %bitcast.21, bf16[8,8,8,128]{3,2,1,0:T(8,128)(2,1)} %bitcast.22), kind=kLoop, calls=%fused_computation | loop fusion | flops 196608 | bytes 786432 | tf_op jit(solution)/shard_map/concatenate | solution.py:440
  1.7 0.0 copy-start
  1.7 0.0 copy-start.1
  1.7 0.0 copy-start.2
  1.7 0.0 copy-start.3
  1.7 0.1 pack_strips.1
  1.8 0.7 %collective-permute-start = (bf16[512,128]{1,0:T(8,128)(2,1)S(1)}, bf16[512,128]{1,0:T(8,128)(2,1)S(1)}, u32[]{:S(2)}, u32[]{:S(2)}) collective-permute-start(bf16[512,128]{1,0:T(8,128)(2,1)S(1)} %get-tuple-element.37), channel_id=1, source_target_pairs={{0,0},{8,16},{16,8},{24,24},{1,1},{9,17},{17,9},{25,25},{2,2},{10,... | collective-permute-start | bytes 393224 | tf_op jit(solution)/shard_map/ppermute | solution.py:399
  2.5 5.9 %collective-permute-start.1 = (bf16[512,128]{1,0:T(8,128)(2,1)S(1)}, bf16[512,128]{1,0:T(8,128)(2,1)S(1)}, u32[]{:S(2)}, u32[]{:S(2)}) collective-permute-start(bf16[512,128]{1,0:T(8,128)(2,1)S(1)} %get-tuple-element.38), channel_id=1, source_target_pairs={{0,8},{8,0},{16,24},{24,16},{1,9},{9,1},{17,25},{25,17},{2,10},{10... | collective-permute-start | bytes 393224 | tf_op jit(solution)/shard_map/ppermute | solution.py:400
  8.4 0.0 copy-done
  8.4 0.0 copy-done.1
  8.4 0.0 copy-done.2
  8.4 0.0 copy-done.3
  8.4 2.7 %band_matrices.1 = (bf16[192,768]{1,0:T(8,128)(2,1)S(1)}, bf16[128,384]{1,0:T(8,128)(2,1)S(1)}, bf16[192,768]{1,0:T(8,128)(2,1)S(1)}, bf16[128,1152]{1,0:T(8,128...) custom-call(bf16[128,27]{1,0:T(8,128)(2,1)S(1)} %bitcast.18, ...), custom_call_target="tpu_custom_call" | custom-call | flops 4000000000 | bytes 1000000 | tf_op jit(solution)/shard_map/band_matrices/pallas_call | solution.py:444
  11.1 0.0 collective-permute-done.xfar
  11.1 0.5 %collective-permute-done.1.xnear = bf16[512,128]{1,0:T(8,128)(2,1)S(1)} collective-permute-done((bf16[512,128]{1,0:T(8,128)(2,1)S(1)}, bf16[512,128]{1,0:T(8,128)(2,1)S(1)}, u32[]{:S(2)}, u32[]{:S(2)}) %collective-permute-start.1) | collective-permute-done | bytes 131104 | tf_op jit(solution)/shard_map/ppermute | solution.py:400
  11.6 0.3 join_strips.1
  11.9 0.7 %collective-permute-start.2 = (bf16[576,128]{1,0:T(8,128)(2,1)S(1)}, bf16[576,128]{1,0:T(8,128)(2,1)S(1)}, u32[]{:S(2)}, u32[]{:S(2)}) collective-permute-start(bf16[576,128]{1,0:T(8,128)(2,1)S(1)} %get-tuple-element.45), channel_id=1, source_target_pairs={{2,4},{4,2},{3,5},{5,3},{10,12},{12,10},{11,13},{13,11},{18,20},{2... | collective-permute-start | bytes 442376 | tf_op jit(solution)/shard_map/ppermute | solution.py:399
  12.6 2.9 %collective-permute-start.3 = (bf16[576,128]{1,0:T(8,128)(2,1)S(1)}, bf16[576,128]{1,0:T(8,128)(2,1)S(1)}, u32[]{:S(2)}, u32[]{:S(2)}) collective-permute-start(bf16[576,128]{1,0:T(8,128)(2,1)S(1)} %get-tuple-element.46), channel_id=1, source_target_pairs={{0,2},{2,0},{4,6},{6,4},{1,3},{3,1},{5,7},{7,5},{8,10},{10,8},{12,... | collective-permute-start | bytes 442376 | tf_op jit(solution)/shard_map/ppermute | solution.py:400
  15.5 0.0 copy-start.4
  15.5 0.0 copy-start.5
  15.6 0.0 copy-start.6
  15.6 0.0 copy-start.7
  15.6 0.0 copy-start.8
  15.6 0.0 copy-start.9
  15.6 0.9 %own_rows.1 = (bf16[256,2048]{1,0:T(8,128)(2,1)S(1)}, bf16[384,1536]{1,0:T(8,128)(2,1)S(1)}, f32[128,1024]{1,0:T(8,128)S(1)}, f32[128,1024]{1,0:T(8,128)S(1)}) custom-call(bf16[512,128]{1,0:T(8,128)(2,1)S(1)} %collective-permute-done.xfar, bf16[512,128]{1,0:T(8,128)(2,1)S(1)} %collective-permute-done.1.xnear, ...), custom_call_target="tpu_custom_call" | custom-call | flops 1000000000 | bytes 1000000 | tf_op jit(solution)/shard_map/own_rows/pallas_call | solution.py:455
  16.5 0.2 join_outer.1
  16.8 0.7 %collective-permute-start.6 = (bf16[320,128]{1,0:T(8,128)(2,1)S(1)}, bf16[320,128]{1,0:T(8,128)(2,1)S(1)}, u32[]{:S(2)}, u32[]{:S(2)}) collective-permute-start(bf16[320,128]{1,0:T(8,128)(2,1)S(1)} %get-tuple-element.59), channel_id=1, source_target_pairs={{2,4},{4,2},{3,5},{5,3},{10,12},{12,10},{11,13},{13,11},{18,20},{2... | collective-permute-start | bytes 245768 | tf_op jit(solution)/shard_map/ppermute | solution.py:399
  17.4 1.4 %collective-permute-start.7 = (bf16[320,128]{1,0:T(8,128)(2,1)S(1)}, bf16[320,128]{1,0:T(8,128)(2,1)S(1)}, u32[]{:S(2)}, u32[]{:S(2)}) collective-permute-start(bf16[320,128]{1,0:T(8,128)(2,1)S(1)} %get-tuple-element.60), channel_id=1, source_target_pairs={{0,2},{2,0},{4,6},{6,4},{1,3},{3,1},{5,7},{7,5},{8,10},{10,8},{12,... | collective-permute-start | bytes 245768 | tf_op jit(solution)/shard_map/ppermute | solution.py:400
  18.8 0.0 collective-permute-done.2.rfar
  18.8 0.0 collective-permute-done.3.rnear
  18.8 0.0 copy-done.4
  18.8 0.0 copy-done.5
  18.8 0.0 copy-done.6
  18.8 0.0 copy-done.7
  18.8 0.0 copy-done.8
  18.9 0.0 copy-done.9
  18.9 3.1 %gradients.1 = (bf16[8,128,128]{2,1,0:T(8,128)(2,1)S(1)}, f32[32,384]{1,0:T(8,128)S(1)}) custom-call(bf16[576,128]{1,0:T(8,128)(2,1)S(1)} %collective-permute-done.2.rfar, bf16[576,128]{1,0:T(8,128)(2,1)S(1)} %collective-permute-done.3.rnear, bf16[256,2048]{1,0:T(8,128)(2,1)S(1)} %get-tuple-element.51.fs, bf16[384,1536]{1,0:T(8,128)(2,1)S(1)} %get-tuple-element.52.cs, ...), custom_call_target="tpu_custom_call" | custom-call | flops 2000000000 | bytes 1000000 | tf_op jit(solution)/shard_map/gradients/pallas_call | solution.py:465
  22.0 0.1 collective-permute-start.4
  22.1 1.2 %collective-permute-done.4.refs_1_ = f32[32,384]{1,0:T(8,128)S(1)} collective-permute-done((f32[32,384]{1,0:T(8,128)S(1)}, f32[32,384]{1,0:T(8,128)S(1)}, u32[]{:S(2)}, u32[]{:S(2)}) %collective-permute-start.4) | collective-permute-done | bytes 49184 | tf_op jit(solution)/shard_map/ppermute | solution.py:405
  23.3 1.8 %collective-permute-start.5 = (bf16[32,384]{1,0:T(8,128)(2,1)S(1)}, bf16[32,384]{1,0:T(8,128)(2,1)S(1)}, u32[]{:S(2)}, u32[]{:S(2)}) collective-permute-start(bf16[32,384]{1,0:T(8,128)(2,1)S(1)} %add_parts.3.refs_0_), channel_id=1, source_target_pairs={{0,4},{2,6},{4,0},{6,2},{1,5},{3,7},{5,1},{7,3},{8,12},{10,14},{12... | collective-permute-start | bytes 73736 | tf_op jit(solution)/shard_map/ppermute | solution.py:405
  25.2 0.0 collective-permute-done.6.rfar_outer
  25.2 0.0 collective-permute-done.7.rnear_outer
  25.2 1.3 %hidden_rim.1.hidden = bf16[12,192,128]{2,1,0:T(8,128)(2,1)S(1)} custom-call(bf16[576,128]{1,0:T(8,128)(2,1)S(1)} %collective-permute-done.2.rfar, bf16[576,128]{1,0:T(8,128)(2,1)S(1)} %collective-permute-done.3.rnear, bf16[320,128]{1,0:T(8,128)(2,1)S(1)} %collective-permute-done.6.rfar_outer, bf16[320,128]{1,0:T(8,128)(2,1)S(1)} %collective-permute-done.7.rnear_outer, ...), custom_call_target="tpu_custom_call" | custom-call | flops 1000000000 | bytes 1000000 | tf_op jit(solution)/shard_map/hidden_rim/pallas_call | solution.py:477
  26.4 0.8 %collective-permute-done.5.refs_1_ = bf16[32,384]{1,0:T(8,128)(2,1)S(1)} collective-permute-done((bf16[32,384]{1,0:T(8,128)(2,1)S(1)}, bf16[32,384]{1,0:T(8,128)(2,1)S(1)}, u32[]{:S(2)}, u32[]{:S(2)}) %collective-permute-start.5) | collective-permute-done | bytes 24608 | tf_op jit(solution)/shard_map/ppermute | solution.py:405
  27.2 1.4 %collective-permute-start.10 = (bf16[32,384]{1,0:T(8,128)(2,1)S(1)}, bf16[32,384]{1,0:T(8,128)(2,1)S(1)}, u32[]{:S(2)}, u32[]{:S(2)}) collective-permute-start(bf16[32,384]{1,0:T(8,128)(2,1)S(1)} %add_parts.4.refs_0_), channel_id=1, source_target_pairs={{0,24},{8,16},{16,8},{24,0},{1,25},{9,17},{17,9},{25,1},{2,26},{10... | collective-permute-start | bytes 73736 | tf_op jit(solution)/shard_map/ppermute | solution.py:405
  28.6 0.8 %collective-permute-start.8 = (bf16[32,384]{1,0:T(8,128)(2,1)S(1)}, bf16[32,384]{1,0:T(8,128)(2,1)S(1)}, u32[]{:S(2)}, u32[]{:S(2)}) collective-permute-start(bf16[32,384]{1,0:T(8,128)(2,1)S(1)} %add_parts.4.refs_0_), channel_id=1, source_target_pairs={{0,8},{8,0},{16,24},{24,16},{1,9},{9,1},{17,25},{25,17},{2,10},{10... | collective-permute-start | bytes 73736 | tf_op jit(solution)/shard_map/ppermute | solution.py:405
  29.5 2.2 %collective-permute-start.9 = (bf16[32,384]{1,0:T(8,128)(2,1)S(1)}, bf16[32,384]{1,0:T(8,128)(2,1)S(1)}, u32[]{:S(2)}, u32[]{:S(2)}) collective-permute-start(bf16[32,384]{1,0:T(8,128)(2,1)S(1)} %add_parts.4.refs_0_), channel_id=1, source_target_pairs={{0,16},{8,24},{16,0},{24,8},{1,17},{9,25},{17,1},{25,9},{2,18},{10... | collective-permute-start | bytes 73736 | tf_op jit(solution)/shard_map/ppermute | solution.py:405
  31.7 1.2 %collective-permute-done.10.refs_3_ = bf16[32,384]{1,0:T(8,128)(2,1)S(1)} collective-permute-done((bf16[32,384]{1,0:T(8,128)(2,1)S(1)}, bf16[32,384]{1,0:T(8,128)(2,1)S(1)}, u32[]{:S(2)}, u32[]{:S(2)}) %collective-permute-start.10) | collective-permute-done | bytes 24608 | tf_op jit(solution)/shard_map/ppermute | solution.py:405
  32.9 0.0 collective-permute-done.8.refs_1_
  32.9 1.3 %collective-permute-done.9.refs_2_ = bf16[32,384]{1,0:T(8,128)(2,1)S(1)} collective-permute-done((bf16[32,384]{1,0:T(8,128)(2,1)S(1)}, bf16[32,384]{1,0:T(8,128)(2,1)S(1)}, u32[]{:S(2)}, u32[]{:S(2)}) %collective-permute-start.9) | collective-permute-done | bytes 24608 | tf_op jit(solution)/shard_map/ppermute | solution.py:405
  34.2 1.6 %collective-permute-start.11 = (bf16[32,384]{1,0:T(8,128)(2,1)S(1)}, bf16[32,384]{1,0:T(8,128)(2,1)S(1)}, u32[]{:S(2)}, u32[]{:S(2)}) collective-permute-start(bf16[32,384]{1,0:T(8,128)(2,1)S(1)} %add_parts.5.refs_0_), channel_id=1, source_target_pairs={{0,1},{1,0},{2,3},{3,2},{4,5},{5,4},{6,7},{7,6},{8,9},{9,8},{10,11... | collective-permute-start | bytes 73736 | tf_op jit(solution)/shard_map/ppermute | solution.py:405
  35.8 1.6 %closure.1 = bf16[1,16,8,8,128]{4,3,2,1,0:T(8,128)(2,1)} custom-call(bf16[12,192,128]{2,1,0:T(8,128)(2,1)S(1)} %hidden_rim.1.hidden, bf16[128,1920]{1,0:T(8,128)(2,1)S(1)} %get-tuple-element.64.t2, f32[128,128]{1,0:T(8,128)S(1)} %get-tuple-element.65.b2), custom_call_target="tpu_custom_call" | custom-call | flops 1000000000 | bytes 1000000 | tf_op jit(solution)/shard_map/closure/pallas_call | solution.py:488
  37.4 0.8 %collective-permute-done.11.refs_1_ = bf16[32,384]{1,0:T(8,128)(2,1)S(1)} collective-permute-done((bf16[32,384]{1,0:T(8,128)(2,1)S(1)}, bf16[32,384]{1,0:T(8,128)(2,1)S(1)}, u32[]{:S(2)}, u32[]{:S(2)}) %collective-permute-start.11) | collective-permute-done | bytes 24608 | tf_op jit(solution)/shard_map/ppermute | solution.py:405
  38.1 0.8 %finish.1 = (f32[128,27]{1,0:T(8,128)}, f32[256,27]{1,0:T(8,128)}, f32[1,16]{1,0:T(1,128)}) custom-call(bf16[32,384]{1,0:T(8,128)(2,1)S(1)} %add_parts.5.refs_0_, bf16[32,384]{1,0:T(8,128)(2,1)S(1)} %collective-permute-done.11.refs_1_), custom_call_target="tpu_custom_call" | custom-call | flops 10000000 | bytes 1000000 | tf_op jit(solution)/shard_map/finish/pallas_call | solution.py:499
  (3 shorter events, 0.1 us)
Async XLA Ops:
  1.7 6.8 %copy-start = (bf16[27,16,16]{0,2,1:T(8,128)(2,1)S(1)}, bf16[27,16,16]{0,2,1:T(8,128)(2,1)}, u32[]{:S(2)}) copy-start(bf16[27,16,16]{0,2,1:T(8,128)(2,1)} %param.15) | copy-start | bytes 41476
  1.7 6.8 %copy-start.1 = (bf16[27,16,8]{0,2,1:T(8,128)(2,1)S(1)}, bf16[27,16,8]{0,2,1:T(8,128)(2,1)}, u32[]{:S(2)}) copy-start(bf16[27,16,8]{0,2,1:T(8,128)(2,1)} %param.13) | copy-start | bytes 20740
  1.7 6.7 %copy-start.2 = (f32[16]{0:T(128)S(1)}, f32[16]{0:T(128)}, u32[]{:S(2)}) copy-start(f32[16]{0:T(128)} %param.14) | copy-start | bytes 196
  1.7 6.7 %copy-start.3 = (f32[16]{0:T(128)S(1)}, f32[16]{0:T(128)}, u32[]{:S(2)}) copy-start(f32[16]{0:T(128)} %param.16) | copy-start | bytes 196
  1.8 9.3 %collective-permute-start = (bf16[512,128]{1,0:T(8,128)(2,1)S(1)}, bf16[512,128]{1,0:T(8,128)(2,1)S(1)}, u32[]{:S(2)}, u32[]{:S(2)}) collective-permute-start(bf16[512,128]{1,0:T(8,128)(2,1)S(1)} %get-tuple-element.37), channel_id=1, source_target_pairs={{0,0},{8,16},{16,8},{24,24},{1,1},{9,17},{17,9},{25,25},{2,2},{10,... | collective-permute-start | bytes 393224 | tf_op jit(solution)/shard_map/ppermute | solution.py:399
  2.5 9.1 %collective-permute-start.1 = (bf16[512,128]{1,0:T(8,128)(2,1)S(1)}, bf16[512,128]{1,0:T(8,128)(2,1)S(1)}, u32[]{:S(2)}, u32[]{:S(2)}) collective-permute-start(bf16[512,128]{1,0:T(8,128)(2,1)S(1)} %get-tuple-element.38), channel_id=1, source_target_pairs={{0,8},{8,0},{16,24},{24,16},{1,9},{9,1},{17,25},{25,17},{2,10},{10... | collective-permute-start | bytes 393224 | tf_op jit(solution)/shard_map/ppermute | solution.py:400
  11.9 6.9 %collective-permute-start.2 = (bf16[576,128]{1,0:T(8,128)(2,1)S(1)}, bf16[576,128]{1,0:T(8,128)(2,1)S(1)}, u32[]{:S(2)}, u32[]{:S(2)}) collective-permute-start(bf16[576,128]{1,0:T(8,128)(2,1)S(1)} %get-tuple-element.45), channel_id=1, source_target_pairs={{2,4},{4,2},{3,5},{5,3},{10,12},{12,10},{11,13},{13,11},{18,20},{2... | collective-permute-start | bytes 442376 | tf_op jit(solution)/shard_map/ppermute | solution.py:399
  12.6 6.2 %collective-permute-start.3 = (bf16[576,128]{1,0:T(8,128)(2,1)S(1)}, bf16[576,128]{1,0:T(8,128)(2,1)S(1)}, u32[]{:S(2)}, u32[]{:S(2)}) collective-permute-start(bf16[576,128]{1,0:T(8,128)(2,1)S(1)} %get-tuple-element.46), channel_id=1, source_target_pairs={{0,2},{2,0},{4,6},{6,4},{1,3},{3,1},{5,7},{7,5},{8,10},{10,8},{12,... | collective-permute-start | bytes 442376 | tf_op jit(solution)/shard_map/ppermute | solution.py:400
  15.5 3.3 %copy-start.4 = (bf16[128,768]{1,0:T(8,128)(2,1)S(1)}, bf16[128,768]{1,0:T(8,128)(2,1)}, u32[]{:S(2)}) copy-start(bf16[128,768]{1,0:T(8,128)(2,1)} %constant.15.clone.rep2) | copy-start | bytes 589828
  15.5 3.3 %copy-start.5 = (bf16[640,128]{1,0:T(8,128)(2,1)S(1)}, bf16[640,128]{1,0:T(8,128)(2,1)}, u32[]{:S(2)}) copy-start(bf16[640,128]{1,0:T(8,128)(2,1)} %constant.13.clone.e2t) | copy-start | bytes 491524
  15.6 3.3 %copy-start.6 = (bf16[384,128]{1,0:T(8,128)(2,1)S(1)}, bf16[384,128]{1,0:T(8,128)(2,1)}, u32[]{:S(2)}) copy-start(bf16[384,128]{1,0:T(8,128)(2,1)} %constant.12.clone.e1t) | copy-start | bytes 294916
  15.6 3.3 %copy-start.7 = (bf16[128,384]{1,0:T(8,128)(2,1)S(1)}, bf16[128,384]{1,0:T(8,128)(2,1)}, u32[]{:S(2)}) copy-start(bf16[128,384]{1,0:T(8,128)(2,1)} %constant.14.clone.rep1) | copy-start | bytes 294916
  15.6 3.3 %copy-start.8 = (f32[1,640]{1,0:T(1,128)S(1)}, f32[1,640]{1,0:T(1,128)}, u32[]{:S(2)}) copy-start(f32[1,640]{1,0:T(1,128)} %constant.17.clone.y2) | copy-start | bytes 7684
  15.6 3.3 %copy-start.9 = (f32[1,384]{1,0:T(1,128)S(1)}, f32[1,384]{1,0:T(1,128)}, u32[]{:S(2)}) copy-start(f32[1,384]{1,0:T(1,128)} %constant.16.clone.y1) | copy-start | bytes 4612
  16.8 8.4 %collective-permute-start.6 = (bf16[320,128]{1,0:T(8,128)(2,1)S(1)}, bf16[320,128]{1,0:T(8,128)(2,1)S(1)}, u32[]{:S(2)}, u32[]{:S(2)}) collective-permute-start(bf16[320,128]{1,0:T(8,128)(2,1)S(1)} %get-tuple-element.59), channel_id=1, source_target_pairs={{2,4},{4,2},{3,5},{5,3},{10,12},{12,10},{11,13},{13,11},{18,20},{2... | collective-permute-start | bytes 245768 | tf_op jit(solution)/shard_map/ppermute | solution.py:399
  17.4 7.7 %collective-permute-start.7 = (bf16[320,128]{1,0:T(8,128)(2,1)S(1)}, bf16[320,128]{1,0:T(8,128)(2,1)S(1)}, u32[]{:S(2)}, u32[]{:S(2)}) collective-permute-start(bf16[320,128]{1,0:T(8,128)(2,1)S(1)} %get-tuple-element.60), channel_id=1, source_target_pairs={{0,2},{2,0},{4,6},{6,4},{1,3},{3,1},{5,7},{7,5},{8,10},{10,8},{12,... | collective-permute-start | bytes 245768 | tf_op jit(solution)/shard_map/ppermute | solution.py:400
  22.0 1.3 %collective-permute-start.4 = (f32[32,384]{1,0:T(8,128)S(1)}, f32[32,384]{1,0:T(8,128)S(1)}, u32[]{:S(2)}, u32[]{:S(2)}) collective-permute-start(f32[32,384]{1,0:T(8,128)S(1)} %get-tuple-element.57.refs_0_), channel_id=1, source_target_pairs={{0,2},{2,0},{4,6},{6,4},{1,3},{3,1},{5,7},{7,5},{8,10},{10,8},{12,... | collective-permute-start | bytes 147464 | tf_op jit(solution)/shard_map/ppermute | solution.py:405
  23.3 3.9 %collective-permute-start.5 = (bf16[32,384]{1,0:T(8,128)(2,1)S(1)}, bf16[32,384]{1,0:T(8,128)(2,1)S(1)}, u32[]{:S(2)}, u32[]{:S(2)}) collective-permute-start(bf16[32,384]{1,0:T(8,128)(2,1)S(1)} %add_parts.3.refs_0_), channel_id=1, source_target_pairs={{0,4},{2,6},{4,0},{6,2},{1,5},{3,7},{5,1},{7,3},{8,12},{10,14},{12... | collective-permute-start | bytes 73736 | tf_op jit(solution)/shard_map/ppermute | solution.py:405
  27.2 5.7 %collective-permute-start.10 = (bf16[32,384]{1,0:T(8,128)(2,1)S(1)}, bf16[32,384]{1,0:T(8,128)(2,1)S(1)}, u32[]{:S(2)}, u32[]{:S(2)}) collective-permute-start(bf16[32,384]{1,0:T(8,128)(2,1)S(1)} %add_parts.4.refs_0_), channel_id=1, source_target_pairs={{0,24},{8,16},{16,8},{24,0},{1,25},{9,17},{17,9},{25,1},{2,26},{10... | collective-permute-start | bytes 73736 | tf_op jit(solution)/shard_map/ppermute | solution.py:405
  28.6 4.3 %collective-permute-start.8 = (bf16[32,384]{1,0:T(8,128)(2,1)S(1)}, bf16[32,384]{1,0:T(8,128)(2,1)S(1)}, u32[]{:S(2)}, u32[]{:S(2)}) collective-permute-start(bf16[32,384]{1,0:T(8,128)(2,1)S(1)} %add_parts.4.refs_0_), channel_id=1, source_target_pairs={{0,8},{8,0},{16,24},{24,16},{1,9},{9,1},{17,25},{25,17},{2,10},{10... | collective-permute-start | bytes 73736 | tf_op jit(solution)/shard_map/ppermute | solution.py:405
  29.5 4.7 %collective-permute-start.9 = (bf16[32,384]{1,0:T(8,128)(2,1)S(1)}, bf16[32,384]{1,0:T(8,128)(2,1)S(1)}, u32[]{:S(2)}, u32[]{:S(2)}) collective-permute-start(bf16[32,384]{1,0:T(8,128)(2,1)S(1)} %add_parts.4.refs_0_), channel_id=1, source_target_pairs={{0,16},{8,24},{16,0},{24,8},{1,17},{9,25},{17,1},{25,9},{2,18},{10... | collective-permute-start | bytes 73736 | tf_op jit(solution)/shard_map/ppermute | solution.py:405
  34.2 3.9 %collective-permute-start.11 = (bf16[32,384]{1,0:T(8,128)(2,1)S(1)}, bf16[32,384]{1,0:T(8,128)(2,1)S(1)}, u32[]{:S(2)}, u32[]{:S(2)}) collective-permute-start(bf16[32,384]{1,0:T(8,128)(2,1)S(1)} %add_parts.5.refs_0_), channel_id=1, source_target_pairs={{0,1},{1,0},{2,3},{3,2},{4,5},{5,4},{6,7},{7,6},{8,9},{9,8},{10,11... | collective-permute-start | bytes 73736 | tf_op jit(solution)/shard_map/ppermute | solution.py:405

commit v12 on v11

--- a/solution.py
+++ b/solution.py
@@ -251,7 +251,7 @@
     return 0.5 * (1.0 + lax.erf(pre * 0.7071067811865476))
 
 
-def rim_kernel(counts, rfar, rnear, fs, cs, pre_own, back_own, t1, tb, e1t, e2t, rep1, rep2, y1, y2,
+def rim_kernel(counts, rnear, rfar, fs, cs, pre_own, back_own, t1, tb, e1t, e2t, rep1, rep2, y1, y2,
                hidden_out, payload, fr, cr, taps):
     count = hidden_out.shape[0]
     lanes = count * Z
@@ -306,7 +306,7 @@
     payload[...] = jnp.concatenate([taps[n] for n in range(3)], axis=1)
 
 
-def hidden_rim_kernel(counts, rfar, rnear, rfar_outer, rnear_outer, hidden, fs, t1o, t1d, b1, hidden_out, fr):
+def hidden_rim_kernel(counts, rnear, rfar, rnear_outer, rfar_outer, hidden, fs, t1o, t1d, b1, hidden_out, fr):
     count = hidden.shape[0]
     stream, radial = lax.axis_index("stream"), lax.axis_index("radial")
     for p in range(count + 8):
@@ -468,7 +468,7 @@
         "gradients",
         (pltpu.VMEM((128, wide), BF16), pltpu.VMEM((256, wide), BF16), pltpu.VMEM((3, 32, 128), F32)),
         flops=2_000_000_000,
-    )(rfar, rnear, fs, cs, pre, back, t1r, tbr, *const(e1t, e2t, rep1, rep2), *const(y1, y2, dtype=F32))
+    )(rnear, rfar, fs, cs, pre, back, t1r, tbr, *const(e1t, e2t, rep1, rep2), *const(y1, y2, dtype=F32))
 
     steps = rounds("radial", 2) + rounds("stream", 4) + rounds("snap", 2)
     arrived = swap(payload, *steps[0])
@@ -480,7 +480,7 @@
         "hidden_rim",
         (pltpu.VMEM((256, wide + 4 * Z), BF16),),
         flops=1_000_000_000,
-    )(rfar, rnear, rfar_outer, rnear_outer, hidden, fs, t1o, t1d, b1)
+    )(rnear, rfar, rnear_outer, rfar_outer, hidden, fs, t1o, t1d, b1)
     payload, hidden = lax.optimization_barrier((add(payload, arrived), hidden))
     arrived = swap(payload, *steps[2])
     payload = add(payload, arrived)

time: 39.1 us -> 39.4 us (level)
    ppermute x6, starting transfers between devices: 7.94 us -> 9.4 us  [swap(): lax.ppermute(v, axis, [(i, i ^ mask) for i in range(count)])]
    ppermute x3, starting transfers between devices: 10.2 us -> 8.91 us  [exchange(): return (lax.ppermute(near, axis, [(i, i ^ 1) for i in range(count)]), far)]
where the time goes in v12:
time: 39.4 us; the launch traced here: 39.2 us
  starting transfers between devices  20.3 us (52%)
  Pallas kernels  11.1 us (28%)
  waiting for transfers between devices  5.84 us (15%)
  other arithmetic  1.02 us (3%)
  between operations  0.89 us (2%)
    ppermute x6, starting transfers between devices, swap(): lax.ppermute(v, axis, [(i, i ^ mask) for i in range(count)])  9.4 us
    ppermute x3, starting transfers between devices, exchange(): return (lax.ppermute(near, axis, [(i, i ^ 1) for i in range(count)]), far)  8.91 us
    ppermute x6, waiting for transfers between devices, swap(): lax.ppermute(v, axis, [(i, i ^ mask) for i in range(count)])  5.34 us
    pallas_call x1, Pallas kernels, local(): call(functools.partial(rim_kernel, counts), (shape(planes, 128, Z), shape...  3.13 us
    pallas_call x1, Pallas kernels, local(): call(band_kernel, (shape(192, 768), shape(128, 384), shape(192, 768), sha...  2.7 us
    ppermute x3, starting transfers between devices, exchange(): far = lax.ppermute(far, axis, pairs)  1.99 us
    pallas_call x1, Pallas kernels, local(): call(closure_kernel, shape(*cotangent.shape), 'closure', (pltpu.VMEM((640...  1.56 us
    pallas_call x1, Pallas kernels, local(): call(functools.partial(hidden_rim_kernel, counts), shape(planes + 4, 192,...  1.27 us
  transfers between devices with their start and end apart: 12, of which 6 were waited for; matrix products, arithmetic and copies ran while one was open for 0% of the time, Pallas kernels for 25%

profile of v12, /device:TPU:0, one launch (start us, length us, event | category | flops | bytes accessed | tf_op | source)
XLA Modules:
  0.0 39.2 jit_solution(18304917005785559773)
XLA Ops:
  0.6 1.0 %pad_maximum_fusion.inputs = bf16[24,8,8,128]{3,2,1,0:T(8,128)(2,1)S(1)} fusion(bf16[16,8,8,128]{3,2,1,0:T(8,128)(2,1)} %bitcast.21, bf16[8,8,8,128]{3,2,1,0:T(8,128)(2,1)} %bitcast.22), kind=kLoop, calls=%fused_computation | loop fusion | flops 196608 | bytes 786432 | tf_op jit(solution)/shard_map/concatenate | solution.py:440
  1.7 0.0 copy-start
  1.7 0.0 copy-start.1
  1.7 0.0 copy-start.2
  1.7 0.0 copy-start.3
  1.7 0.1 pack_strips.1
  1.8 0.7 %collective-permute-start = (bf16[512,128]{1,0:T(8,128)(2,1)S(1)}, bf16[512,128]{1,0:T(8,128)(2,1)S(1)}, u32[]{:S(2)}, u32[]{:S(2)}) collective-permute-start(bf16[512,128]{1,0:T(8,128)(2,1)S(1)} %get-tuple-element.37), channel_id=1, source_target_pairs={{0,0},{8,16},{16,8},{24,24},{1,1},{9,17},{17,9},{25,25},{2,2},{10,... | collective-permute-start | bytes 393224 | tf_op jit(solution)/shard_map/ppermute | solution.py:399
  2.5 5.9 %collective-permute-start.1 = (bf16[512,128]{1,0:T(8,128)(2,1)S(1)}, bf16[512,128]{1,0:T(8,128)(2,1)S(1)}, u32[]{:S(2)}, u32[]{:S(2)}) collective-permute-start(bf16[512,128]{1,0:T(8,128)(2,1)S(1)} %get-tuple-element.38), channel_id=1, source_target_pairs={{0,8},{8,0},{16,24},{24,16},{1,9},{9,1},{17,25},{25,17},{2,10},{10... | collective-permute-start | bytes 393224 | tf_op jit(solution)/shard_map/ppermute | solution.py:400
  8.4 0.0 copy-done
  8.4 0.0 copy-done.1
  8.4 0.0 copy-done.2
  8.4 0.0 copy-done.3
  8.4 2.7 %band_matrices.1 = (bf16[192,768]{1,0:T(8,128)(2,1)S(1)}, bf16[128,384]{1,0:T(8,128)(2,1)S(1)}, bf16[192,768]{1,0:T(8,128)(2,1)S(1)}, bf16[128,1152]{1,0:T(8,128...) custom-call(bf16[128,27]{1,0:T(8,128)(2,1)S(1)} %bitcast.18, ...), custom_call_target="tpu_custom_call" | custom-call | flops 4000000000 | bytes 1000000 | tf_op jit(solution)/shard_map/band_matrices/pallas_call | solution.py:444
  11.1 0.0 collective-permute-done.xfar
  11.1 0.5 %collective-permute-done.1.xnear = bf16[512,128]{1,0:T(8,128)(2,1)S(1)} collective-permute-done((bf16[512,128]{1,0:T(8,128)(2,1)S(1)}, bf16[512,128]{1,0:T(8,128)(2,1)S(1)}, u32[]{:S(2)}, u32[]{:S(2)}) %collective-permute-start.1) | collective-permute-done | bytes 131104 | tf_op jit(solution)/shard_map/ppermute | solution.py:400
  11.6 0.3 join_strips.1
  11.9 0.1 collective-permute-start.2
  12.0 0.7 %collective-permute-start.3 = (bf16[576,128]{1,0:T(8,128)(2,1)S(1)}, bf16[576,128]{1,0:T(8,128)(2,1)S(1)}, u32[]{:S(2)}, u32[]{:S(2)}) collective-permute-start(bf16[576,128]{1,0:T(8,128)(2,1)S(1)} %get-tuple-element.46), channel_id=1, source_target_pairs={{2,4},{4,2},{3,5},{5,3},{10,12},{12,10},{11,13},{13,11},{18,20},{2... | collective-permute-start | bytes 442376 | tf_op jit(solution)/shard_map/ppermute | solution.py:399
  12.7 0.0 copy-start.4
  12.7 0.0 copy-start.5
  12.7 0.0 copy-start.6
  12.7 0.0 copy-start.7
  12.7 0.0 copy-start.8
  12.8 0.0 copy-start.9
  12.8 0.9 %own_rows.1 = (bf16[256,2048]{1,0:T(8,128)(2,1)S(1)}, bf16[384,1536]{1,0:T(8,128)(2,1)S(1)}, f32[128,1024]{1,0:T(8,128)S(1)}, f32[128,1024]{1,0:T(8,128)S(1)}) custom-call(bf16[512,128]{1,0:T(8,128)(2,1)S(1)} %collective-permute-done.xfar, bf16[512,128]{1,0:T(8,128)(2,1)S(1)} %collective-permute-done.1.xnear, ...), custom_call_target="tpu_custom_call" | custom-call | flops 1000000000 | bytes 1000000 | tf_op jit(solution)/shard_map/own_rows/pallas_call | solution.py:455
  13.7 0.2 join_outer.1
  13.9 2.9 %collective-permute-start.6 = (bf16[320,128]{1,0:T(8,128)(2,1)S(1)}, bf16[320,128]{1,0:T(8,128)(2,1)S(1)}, u32[]{:S(2)}, u32[]{:S(2)}) collective-permute-start(bf16[320,128]{1,0:T(8,128)(2,1)S(1)} %get-tuple-element.59), channel_id=1, source_target_pairs={{0,2},{2,0},{4,6},{6,4},{1,3},{3,1},{5,7},{7,5},{8,10},{10,8},{12,... | collective-permute-start | bytes 245768 | tf_op jit(solution)/shard_map/ppermute | solution.py:400
  16.9 0.7 %collective-permute-start.7 = (bf16[320,128]{1,0:T(8,128)(2,1)S(1)}, bf16[320,128]{1,0:T(8,128)(2,1)S(1)}, u32[]{:S(2)}, u32[]{:S(2)}) collective-permute-start(bf16[320,128]{1,0:T(8,128)(2,1)S(1)} %get-tuple-element.60), channel_id=1, source_target_pairs={{2,4},{4,2},{3,5},{5,3},{10,12},{12,10},{11,13},{13,11},{18,20},{2... | collective-permute-start | bytes 245768 | tf_op jit(solution)/shard_map/ppermute | solution.py:399
  17.5 0.0 collective-permute-done.2.rnear
  17.5 0.0 collective-permute-done.3.rfar
  17.6 0.0 copy-done.4
  17.6 0.0 copy-done.5
  17.6 0.0 copy-done.6
  17.6 0.0 copy-done.7
  17.6 0.0 copy-done.8
  17.6 0.0 copy-done.9
  17.6 3.1 %gradients.1 = (bf16[8,128,128]{2,1,0:T(8,128)(2,1)S(1)}, f32[32,384]{1,0:T(8,128)S(1)}) custom-call(bf16[576,128]{1,0:T(8,128)(2,1)S(1)} %collective-permute-done.2.rnear, bf16[576,128]{1,0:T(8,128)(2,1)S(1)} %collective-permute-done.3.rfar, bf16[256,2048]{1,0:T(8,128)(2,1)S(1)} %get-tuple-element.51.fs, bf16[384,1536]{1,0:T(8,128)(2,1)S(1)} %get-tuple-element.52.cs, ...), custom_call_target="tpu_custom_call" | custom-call | flops 2000000000 | bytes 1000000 | tf_op jit(solution)/shard_map/gradients/pallas_call | solution.py:465
  20.8 1.9 %collective-permute-start.4 = (f32[32,384]{1,0:T(8,128)S(1)}, f32[32,384]{1,0:T(8,128)S(1)}, u32[]{:S(2)}, u32[]{:S(2)}) collective-permute-start(f32[32,384]{1,0:T(8,128)S(1)} %get-tuple-element.57.refs_0_), channel_id=1, source_target_pairs={{0,2},{2,0},{4,6},{6,4},{1,3},{3,1},{5,7},{7,5},{8,10},{10,8},{12,... | collective-permute-start | bytes 147464 | tf_op jit(solution)/shard_map/ppermute | solution.py:405
  22.7 0.9 %collective-permute-done.4.refs_1_ = f32[32,384]{1,0:T(8,128)S(1)} collective-permute-done((f32[32,384]{1,0:T(8,128)S(1)}, f32[32,384]{1,0:T(8,128)S(1)}, u32[]{:S(2)}, u32[]{:S(2)}) %collective-permute-start.4) | collective-permute-done | bytes 49184 | tf_op jit(solution)/shard_map/ppermute | solution.py:405
  23.6 1.4 %collective-permute-start.5 = (bf16[32,384]{1,0:T(8,128)(2,1)S(1)}, bf16[32,384]{1,0:T(8,128)(2,1)S(1)}, u32[]{:S(2)}, u32[]{:S(2)}) collective-permute-start(bf16[32,384]{1,0:T(8,128)(2,1)S(1)} %add_parts.3.refs_0_), channel_id=1, source_target_pairs={{0,4},{2,6},{4,0},{6,2},{1,5},{3,7},{5,1},{7,3},{8,12},{10,14},{12... | collective-permute-start | bytes 73736 | tf_op jit(solution)/shard_map/ppermute | solution.py:405
  25.0 0.0 collective-permute-done.6.rnear_outer
  25.0 0.0 collective-permute-done.7.rfar_outer
  25.0 1.3 %hidden_rim.1.hidden = bf16[12,192,128]{2,1,0:T(8,128)(2,1)S(1)} custom-call(bf16[576,128]{1,0:T(8,128)(2,1)S(1)} %collective-permute-done.2.rnear, bf16[576,128]{1,0:T(8,128)(2,1)S(1)} %collective-permute-done.3.rfar, bf16[320,128]{1,0:T(8,128)(2,1)S(1)} %collective-permute-done.6.rnear_outer, bf16[320,128]{1,0:T(8,128)(2,1)S(1)} %collective-permute-done.7.rfar_outer, ...), custom_call_target="tpu_custom_call" | custom-call | flops 1000000000 | bytes 1000000 | tf_op jit(solution)/shard_map/hidden_rim/pallas_call | solution.py:477
  26.3 1.2 %collective-permute-done.5.refs_1_ = bf16[32,384]{1,0:T(8,128)(2,1)S(1)} collective-permute-done((bf16[32,384]{1,0:T(8,128)(2,1)S(1)}, bf16[32,384]{1,0:T(8,128)(2,1)S(1)}, u32[]{:S(2)}, u32[]{:S(2)}) %collective-permute-start.5) | collective-permute-done | bytes 24608 | tf_op jit(solution)/shard_map/ppermute | solution.py:405
  27.5 1.4 %collective-permute-start.10 = (bf16[32,384]{1,0:T(8,128)(2,1)S(1)}, bf16[32,384]{1,0:T(8,128)(2,1)S(1)}, u32[]{:S(2)}, u32[]{:S(2)}) collective-permute-start(bf16[32,384]{1,0:T(8,128)(2,1)S(1)} %add_parts.4.refs_0_), channel_id=1, source_target_pairs={{0,24},{8,16},{16,8},{24,0},{1,25},{9,17},{17,9},{25,1},{2,26},{10... | collective-permute-start | bytes 73736 | tf_op jit(solution)/shard_map/ppermute | solution.py:405
  28.9 0.8 %collective-permute-start.8 = (bf16[32,384]{1,0:T(8,128)(2,1)S(1)}, bf16[32,384]{1,0:T(8,128)(2,1)S(1)}, u32[]{:S(2)}, u32[]{:S(2)}) collective-permute-start(bf16[32,384]{1,0:T(8,128)(2,1)S(1)} %add_parts.4.refs_0_), channel_id=1, source_target_pairs={{0,8},{8,0},{16,24},{24,16},{1,9},{9,1},{17,25},{25,17},{2,10},{10... | collective-permute-start | bytes 73736 | tf_op jit(solution)/shard_map/ppermute | solution.py:405
  29.8 2.2 %collective-permute-start.9 = (bf16[32,384]{1,0:T(8,128)(2,1)S(1)}, bf16[32,384]{1,0:T(8,128)(2,1)S(1)}, u32[]{:S(2)}, u32[]{:S(2)}) collective-permute-start(bf16[32,384]{1,0:T(8,128)(2,1)S(1)} %add_parts.4.refs_0_), channel_id=1, source_target_pairs={{0,16},{8,24},{16,0},{24,8},{1,17},{9,25},{17,1},{25,9},{2,18},{10... | collective-permute-start | bytes 73736 | tf_op jit(solution)/shard_map/ppermute | solution.py:405
  32.0 1.2 %collective-permute-done.10.refs_3_ = bf16[32,384]{1,0:T(8,128)(2,1)S(1)} collective-permute-done((bf16[32,384]{1,0:T(8,128)(2,1)S(1)}, bf16[32,384]{1,0:T(8,128)(2,1)S(1)}, u32[]{:S(2)}, u32[]{:S(2)}) %collective-permute-start.10) | collective-permute-done | bytes 24608 | tf_op jit(solution)/shard_map/ppermute | solution.py:405
  33.2 0.0 collective-permute-done.8.refs_1_
  33.2 1.3 %collective-permute-done.9.refs_2_ = bf16[32,384]{1,0:T(8,128)(2,1)S(1)} collective-permute-done((bf16[32,384]{1,0:T(8,128)(2,1)S(1)}, bf16[32,384]{1,0:T(8,128)(2,1)S(1)}, u32[]{:S(2)}, u32[]{:S(2)}) %collective-permute-start.9) | collective-permute-done | bytes 24608 | tf_op jit(solution)/shard_map/ppermute | solution.py:405
  34.5 1.6 %collective-permute-start.11 = (bf16[32,384]{1,0:T(8,128)(2,1)S(1)}, bf16[32,384]{1,0:T(8,128)(2,1)S(1)}, u32[]{:S(2)}, u32[]{:S(2)}) collective-permute-start(bf16[32,384]{1,0:T(8,128)(2,1)S(1)} %add_parts.5.refs_0_), channel_id=1, source_target_pairs={{0,1},{1,0},{2,3},{3,2},{4,5},{5,4},{6,7},{7,6},{8,9},{9,8},{10,11... | collective-permute-start | bytes 73736 | tf_op jit(solution)/shard_map/ppermute | solution.py:405
  36.1 1.6 %closure.1 = bf16[1,16,8,8,128]{4,3,2,1,0:T(8,128)(2,1)} custom-call(bf16[12,192,128]{2,1,0:T(8,128)(2,1)S(1)} %hidden_rim.1.hidden, bf16[128,1920]{1,0:T(8,128)(2,1)S(1)} %get-tuple-element.64.t2, f32[128,128]{1,0:T(8,128)S(1)} %get-tuple-element.65.b2), custom_call_target="tpu_custom_call" | custom-call | flops 1000000000 | bytes 1000000 | tf_op jit(solution)/shard_map/closure/pallas_call | solution.py:488
  37.6 0.8 %collective-permute-done.11.refs_1_ = bf16[32,384]{1,0:T(8,128)(2,1)S(1)} collective-permute-done((bf16[32,384]{1,0:T(8,128)(2,1)S(1)}, bf16[32,384]{1,0:T(8,128)(2,1)S(1)}, u32[]{:S(2)}, u32[]{:S(2)}) %collective-permute-start.11) | collective-permute-done | bytes 24608 | tf_op jit(solution)/shard_map/ppermute | solution.py:405
  38.4 0.8 %finish.1 = (f32[128,27]{1,0:T(8,128)}, f32[256,27]{1,0:T(8,128)}, f32[1,16]{1,0:T(1,128)}) custom-call(bf16[32,384]{1,0:T(8,128)(2,1)S(1)} %add_parts.5.refs_0_, bf16[32,384]{1,0:T(8,128)(2,1)S(1)} %collective-permute-done.11.refs_1_), custom_call_target="tpu_custom_call" | custom-call | flops 10000000 | bytes 1000000 | tf_op jit(solution)/shard_map/finish/pallas_call | solution.py:499
  (3 shorter events, 0.1 us)
Async XLA Ops:
  1.7 6.8 %copy-start = (bf16[27,16,16]{0,2,1:T(8,128)(2,1)S(1)}, bf16[27,16,16]{0,2,1:T(8,128)(2,1)}, u32[]{:S(2)}) copy-start(bf16[27,16,16]{0,2,1:T(8,128)(2,1)} %param.15) | copy-start | bytes 41476
  1.7 6.8 %copy-start.1 = (bf16[27,16,8]{0,2,1:T(8,128)(2,1)S(1)}, bf16[27,16,8]{0,2,1:T(8,128)(2,1)}, u32[]{:S(2)}) copy-start(bf16[27,16,8]{0,2,1:T(8,128)(2,1)} %param.13) | copy-start | bytes 20740
  1.7 6.7 %copy-start.2 = (f32[16]{0:T(128)S(1)}, f32[16]{0:T(128)}, u32[]{:S(2)}) copy-start(f32[16]{0:T(128)} %param.14) | copy-start | bytes 196
  1.7 6.7 %copy-start.3 = (f32[16]{0:T(128)S(1)}, f32[16]{0:T(128)}, u32[]{:S(2)}) copy-start(f32[16]{0:T(128)} %param.16) | copy-start | bytes 196
  1.8 9.3 %collective-permute-start = (bf16[512,128]{1,0:T(8,128)(2,1)S(1)}, bf16[512,128]{1,0:T(8,128)(2,1)S(1)}, u32[]{:S(2)}, u32[]{:S(2)}) collective-permute-start(bf16[512,128]{1,0:T(8,128)(2,1)S(1)} %get-tuple-element.37), channel_id=1, source_target_pairs={{0,0},{8,16},{16,8},{24,24},{1,1},{9,17},{17,9},{25,25},{2,2},{10,... | collective-permute-start | bytes 393224 | tf_op jit(solution)/shard_map/ppermute | solution.py:399
  2.5 9.1 %collective-permute-start.1 = (bf16[512,128]{1,0:T(8,128)(2,1)S(1)}, bf16[512,128]{1,0:T(8,128)(2,1)S(1)}, u32[]{:S(2)}, u32[]{:S(2)}) collective-permute-start(bf16[512,128]{1,0:T(8,128)(2,1)S(1)} %get-tuple-element.38), channel_id=1, source_target_pairs={{0,8},{8,0},{16,24},{24,16},{1,9},{9,1},{17,25},{25,17},{2,10},{10... | collective-permute-start | bytes 393224 | tf_op jit(solution)/shard_map/ppermute | solution.py:400
  11.9 5.6 %collective-permute-start.2 = (bf16[576,128]{1,0:T(8,128)(2,1)S(1)}, bf16[576,128]{1,0:T(8,128)(2,1)S(1)}, u32[]{:S(2)}, u32[]{:S(2)}) collective-permute-start(bf16[576,128]{1,0:T(8,128)(2,1)S(1)} %get-tuple-element.45), channel_id=1, source_target_pairs={{0,2},{2,0},{4,6},{6,4},{1,3},{3,1},{5,7},{7,5},{8,10},{10,8},{12,... | collective-permute-start | bytes 442376 | tf_op jit(solution)/shard_map/ppermute | solution.py:400
  12.0 5.5 %collective-permute-start.3 = (bf16[576,128]{1,0:T(8,128)(2,1)S(1)}, bf16[576,128]{1,0:T(8,128)(2,1)S(1)}, u32[]{:S(2)}, u32[]{:S(2)}) collective-permute-start(bf16[576,128]{1,0:T(8,128)(2,1)S(1)} %get-tuple-element.46), channel_id=1, source_target_pairs={{2,4},{4,2},{3,5},{5,3},{10,12},{12,10},{11,13},{13,11},{18,20},{2... | collective-permute-start | bytes 442376 | tf_op jit(solution)/shard_map/ppermute | solution.py:399
  12.7 4.9 %copy-start.4 = (bf16[128,768]{1,0:T(8,128)(2,1)S(1)}, bf16[128,768]{1,0:T(8,128)(2,1)}, u32[]{:S(2)}) copy-start(bf16[128,768]{1,0:T(8,128)(2,1)} %constant.15.clone.rep2) | copy-start | bytes 589828
  12.7 4.9 %copy-start.5 = (bf16[640,128]{1,0:T(8,128)(2,1)S(1)}, bf16[640,128]{1,0:T(8,128)(2,1)}, u32[]{:S(2)}) copy-start(bf16[640,128]{1,0:T(8,128)(2,1)} %constant.13.clone.e2t) | copy-start | bytes 491524
  12.7 4.9 %copy-start.6 = (bf16[384,128]{1,0:T(8,128)(2,1)S(1)}, bf16[384,128]{1,0:T(8,128)(2,1)}, u32[]{:S(2)}) copy-start(bf16[384,128]{1,0:T(8,128)(2,1)} %constant.12.clone.e1t) | copy-start | bytes 294916
  12.7 4.9 %copy-start.7 = (bf16[128,384]{1,0:T(8,128)(2,1)S(1)}, bf16[128,384]{1,0:T(8,128)(2,1)}, u32[]{:S(2)}) copy-start(bf16[128,384]{1,0:T(8,128)(2,1)} %constant.14.clone.rep1) | copy-start | bytes 294916
  12.7 4.9 %copy-start.8 = (f32[1,640]{1,0:T(1,128)S(1)}, f32[1,640]{1,0:T(1,128)}, u32[]{:S(2)}) copy-start(f32[1,640]{1,0:T(1,128)} %constant.17.clone.y2) | copy-start | bytes 7684
  12.8 4.9 %copy-start.9 = (f32[1,384]{1,0:T(1,128)S(1)}, f32[1,384]{1,0:T(1,128)}, u32[]{:S(2)}) copy-start(f32[1,384]{1,0:T(1,128)} %constant.16.clone.y1) | copy-start | bytes 4612
  13.9 11.1 %collective-permute-start.6 = (bf16[320,128]{1,0:T(8,128)(2,1)S(1)}, bf16[320,128]{1,0:T(8,128)(2,1)S(1)}, u32[]{:S(2)}, u32[]{:S(2)}) collective-permute-start(bf16[320,128]{1,0:T(8,128)(2,1)S(1)} %get-tuple-element.59), channel_id=1, source_target_pairs={{0,2},{2,0},{4,6},{6,4},{1,3},{3,1},{5,7},{7,5},{8,10},{10,8},{12,... | collective-permute-start | bytes 245768 | tf_op jit(solution)/shard_map/ppermute | solution.py:400
  16.9 8.2 %collective-permute-start.7 = (bf16[320,128]{1,0:T(8,128)(2,1)S(1)}, bf16[320,128]{1,0:T(8,128)(2,1)S(1)}, u32[]{:S(2)}, u32[]{:S(2)}) collective-permute-start(bf16[320,128]{1,0:T(8,128)(2,1)S(1)} %get-tuple-element.60), channel_id=1, source_target_pairs={{2,4},{4,2},{3,5},{5,3},{10,12},{12,10},{11,13},{13,11},{18,20},{2... | collective-permute-start | bytes 245768 | tf_op jit(solution)/shard_map/ppermute | solution.py:399
  20.8 2.8 %collective-permute-start.4 = (f32[32,384]{1,0:T(8,128)S(1)}, f32[32,384]{1,0:T(8,128)S(1)}, u32[]{:S(2)}, u32[]{:S(2)}) collective-permute-start(f32[32,384]{1,0:T(8,128)S(1)} %get-tuple-element.57.refs_0_), channel_id=1, source_target_pairs={{0,2},{2,0},{4,6},{6,4},{1,3},{3,1},{5,7},{7,5},{8,10},{10,8},{12,... | collective-permute-start | bytes 147464 | tf_op jit(solution)/shard_map/ppermute | solution.py:405
  23.6 3.9 %collective-permute-start.5 = (bf16[32,384]{1,0:T(8,128)(2,1)S(1)}, bf16[32,384]{1,0:T(8,128)(2,1)S(1)}, u32[]{:S(2)}, u32[]{:S(2)}) collective-permute-start(bf16[32,384]{1,0:T(8,128)(2,1)S(1)} %add_parts.3.refs_0_), channel_id=1, source_target_pairs={{0,4},{2,6},{4,0},{6,2},{1,5},{3,7},{5,1},{7,3},{8,12},{10,14},{12... | collective-permute-start | bytes 73736 | tf_op jit(solution)/shard_map/ppermute | solution.py:405
  27.5 5.7 %collective-permute-start.10 = (bf16[32,384]{1,0:T(8,128)(2,1)S(1)}, bf16[32,384]{1,0:T(8,128)(2,1)S(1)}, u32[]{:S(2)}, u32[]{:S(2)}) collective-permute-start(bf16[32,384]{1,0:T(8,128)(2,1)S(1)} %add_parts.4.refs_0_), channel_id=1, source_target_pairs={{0,24},{8,16},{16,8},{24,0},{1,25},{9,17},{17,9},{25,1},{2,26},{10... | collective-permute-start | bytes 73736 | tf_op jit(solution)/shard_map/ppermute | solution.py:405
  28.9 4.3 %collective-permute-start.8 = (bf16[32,384]{1,0:T(8,128)(2,1)S(1)}, bf16[32,384]{1,0:T(8,128)(2,1)S(1)}, u32[]{:S(2)}, u32[]{:S(2)}) collective-permute-start(bf16[32,384]{1,0:T(8,128)(2,1)S(1)} %add_parts.4.refs_0_), channel_id=1, source_target_pairs={{0,8},{8,0},{16,24},{24,16},{1,9},{9,1},{17,25},{25,17},{2,10},{10... | collective-permute-start | bytes 73736 | tf_op jit(solution)/shard_map/ppermute | solution.py:405
  29.8 4.7 %collective-permute-start.9 = (bf16[32,384]{1,0:T(8,128)(2,1)S(1)}, bf16[32,384]{1,0:T(8,128)(2,1)S(1)}, u32[]{:S(2)}, u32[]{:S(2)}) collective-permute-start(bf16[32,384]{1,0:T(8,128)(2,1)S(1)} %add_parts.4.refs_0_), channel_id=1, source_target_pairs={{0,16},{8,24},{16,0},{24,8},{1,17},{9,25},{17,1},{25,9},{2,18},{10... | collective-permute-start | bytes 73736 | tf_op jit(solution)/shard_map/ppermute | solution.py:405
  34.5 3.9 %collective-permute-start.11 = (bf16[32,384]{1,0:T(8,128)(2,1)S(1)}, bf16[32,384]{1,0:T(8,128)(2,1)S(1)}, u32[]{:S(2)}, u32[]{:S(2)}) collective-permute-start(bf16[32,384]{1,0:T(8,128)(2,1)S(1)} %add_parts.5.refs_0_), channel_id=1, source_target_pairs={{0,1},{1,0},{2,3},{3,2},{4,5},{5,4},{6,7},{7,6},{8,9},{9,8},{10,11... | collective-permute-start | bytes 73736 | tf_op jit(solution)/shard_map/ppermute | solution.py:405

commit v13 on v11

--- a/solution.py
+++ b/solution.py
@@ -391,11 +391,10 @@
     return jax.ShapeDtypeStruct(dims, dtype)
 
 
-def exchange(near, far, axis, ends=True):
+def exchange(near, far, axis, ends):
     count = lax.axis_size(axis)
     pairs = [(i, i - 1 + 2 * (i % 2)) for i in range(1, count - 1)]
-    if ends:
-        pairs = [(0, 0), *pairs, (count - 1, count - 1)]
+    pairs += [(0, count - 1), (count - 1, 0)] if ends else [(0, 0), (count - 1, count - 1)]
     far = lax.ppermute(far, axis, pairs)
     return lax.ppermute(near, axis, [(i, i ^ 1) for i in range(count)]), far
 
@@ -438,7 +437,7 @@
         "pack_strips",
         flops=4_000_000_000,
     )(jnp.concatenate([fields[0], cotangent[0]], axis=0))
-    xnear, xfar = exchange(near, far, "stream")
+    xnear, xfar = exchange(near, far, "stream", False)
     wide = (planes + 4) * Z
     counts = (lax.axis_size("stream"), lax.axis_size("radial"))
     t1o, t1r, t1d, tbo, tbr, t2, b1, b2 = call(
@@ -451,7 +450,7 @@
     xfar, xnear, t1o, tbo = lax.optimization_barrier((xfar, xnear, t1o, tbo))
     inner, outer = shape((planes + 4) * 48, Z), shape(128 + (planes + 4) * 16, Z)
     near, far = call(functools.partial(join_kernel, counts), (inner, inner), "join_strips")(xfar, xnear, f_rows, c_rows)
-    rnear, rfar = exchange(near, far, "radial", ends=False)
+    rnear, rfar = exchange(near, far, "radial", True)
     fs, cs, pre, back = call(
         functools.partial(own_kernel, counts),
         (shape(256, wide + 4 * Z), shape(384, wide), shape(128, planes * Z, dtype=F32), shape(128, planes * Z, dtype=F32)),
@@ -461,7 +460,7 @@
     f_rows, fs = lax.optimization_barrier((f_rows, fs))
     near_outer, far_outer = call(functools.partial(join_outer_kernel, counts), (outer, outer), "join_outer")(
         xfar, xnear, f_rows, c_rows)
-    rnear_outer, rfar_outer = exchange(near_outer, far_outer, "radial", ends=False)
+    rnear_outer, rfar_outer = exchange(near_outer, far_outer, "radial", True)
     hidden, payload = call(
         functools.partial(rim_kernel, counts),
         (shape(planes, 128, Z), shape(32, 384, dtype=F32)),

time: 39.1 us -> 38.4 us (0.982)
  starting transfers between devices: 20.2 us -> 16.3 us
  waiting for transfers between devices: 5.78 us -> 8.97 us
    ppermute x3, waiting for transfers between devices: 0.01 us -> 2.54 us  [exchange(): far = lax.ppermute(far, axis, pairs)]
    ppermute x3, starting transfers between devices: 10.2 us -> 7.95 us  [exchange(): return (lax.ppermute(near, axis, [(i, i ^ 1) for i in range(count)]), far)]
    ppermute x3, starting transfers between devices: 2 us -> 1.02 us  [exchange(): far = lax.ppermute(far, axis, pairs)]
    ppermute x6, starting transfers between devices: 7.94 us -> 7.29 us  [swap(): lax.ppermute(v, axis, [(i, i ^ mask) for i in range(count)])]
    ppermute x6, waiting for transfers between devices: 5.28 us -> 5.93 us  [swap(): lax.ppermute(v, axis, [(i, i ^ mask) for i in range(count)])]
  transfers between devices with their start and end apart: 12 -> 12, of which waited for: 6 -> 7; matrix products, arithmetic and copies ran while one was open for 0% -> 0% of each run, Pallas kernels for 25% -> 26%
where the time goes in v13:
time: 38.4 us; the launch traced here: 38.2 us
  starting transfers between devices  16.3 us (42%)
  Pallas kernels  11.1 us (29%)
  waiting for transfers between devices  8.97 us (23%)
  other arithmetic  1.02 us (3%)
  between operations  0.81 us (2%)
    ppermute x3, starting transfers between devices, exchange(): return (lax.ppermute(near, axis, [(i, i ^ 1) for i in range(count)]), far)  7.95 us
    ppermute x6, starting transfers between devices, swap(): lax.ppermute(v, axis, [(i, i ^ mask) for i in range(count)])  7.29 us
    ppermute x6, waiting for transfers between devices, swap(): lax.ppermute(v, axis, [(i, i ^ mask) for i in range(count)])  5.93 us
    pallas_call x1, Pallas kernels, local(): call(functools.partial(rim_kernel, counts), (shape(planes, 128, Z), shape...  3.14 us
    pallas_call x1, Pallas kernels, local(): call(band_kernel, (shape(192, 768), shape(128, 384), shape(192, 768), sha...  2.7 us
    ppermute x3, waiting for transfers between devices, exchange(): far = lax.ppermute(far, axis, pairs)  2.54 us
    pallas_call x1, Pallas kernels, local(): call(closure_kernel, shape(*cotangent.shape), 'closure', (pltpu.VMEM((640...  1.56 us
    pallas_call x1, Pallas kernels, local(): call(functools.partial(hidden_rim_kernel, counts), shape(planes + 4, 192,...  1.26 us
  transfers between devices with their start and end apart: 12, of which 7 were waited for; matrix products, arithmetic and copies ran while one was open for 0% of the time, Pallas kernels for 26%

profile of v13, /device:TPU:0, one launch (start us, length us, event | category | flops | bytes accessed | tf_op | source)
XLA Modules:
  0.0 38.2 jit_solution(1655136274611944677)
XLA Ops:
  0.6 1.0 %pad_maximum_fusion.inputs = bf16[24,8,8,128]{3,2,1,0:T(8,128)(2,1)S(1)} fusion(bf16[16,8,8,128]{3,2,1,0:T(8,128)(2,1)} %bitcast.21, bf16[8,8,8,128]{3,2,1,0:T(8,128)(2,1)} %bitcast.22), kind=kLoop, calls=%fused_computation | loop fusion | flops 196608 | bytes 786432 | tf_op jit(solution)/shard_map/concatenate | solution.py:439
  1.7 0.0 copy-start
  1.7 0.0 copy-start.1
  1.7 0.0 copy-start.2
  1.7 0.0 copy-start.3
  1.7 0.1 pack_strips.1
  1.8 0.7 %collective-permute-start = (bf16[512,128]{1,0:T(8,128)(2,1)S(1)}, bf16[512,128]{1,0:T(8,128)(2,1)S(1)}, u32[]{:S(2)}, u32[]{:S(2)}) collective-permute-start(bf16[512,128]{1,0:T(8,128)(2,1)S(1)} %get-tuple-element.37), channel_id=1, source_target_pairs={{8,16},{16,8},{0,0},{24,24},{9,17},{17,9},{1,1},{25,25},{10,18},{1... | collective-permute-start | bytes 393224 | tf_op jit(solution)/shard_map/ppermute | solution.py:398
  2.5 5.9 %collective-permute-start.1 = (bf16[512,128]{1,0:T(8,128)(2,1)S(1)}, bf16[512,128]{1,0:T(8,128)(2,1)S(1)}, u32[]{:S(2)}, u32[]{:S(2)}) collective-permute-start(bf16[512,128]{1,0:T(8,128)(2,1)S(1)} %get-tuple-element.38), channel_id=1, source_target_pairs={{0,8},{8,0},{16,24},{24,16},{1,9},{9,1},{17,25},{25,17},{2,10},{10... | collective-permute-start | bytes 393224 | tf_op jit(solution)/shard_map/ppermute | solution.py:399
  8.4 0.0 copy-done
  8.4 0.0 copy-done.1
  8.4 0.0 copy-done.2
  8.4 0.0 copy-done.3
  8.4 2.7 %band_matrices.1 = (bf16[192,768]{1,0:T(8,128)(2,1)S(1)}, bf16[128,384]{1,0:T(8,128)(2,1)S(1)}, bf16[192,768]{1,0:T(8,128)(2,1)S(1)}, bf16[128,1152]{1,0:T(8,128...) custom-call(bf16[128,27]{1,0:T(8,128)(2,1)S(1)} %bitcast.18, ...), custom_call_target="tpu_custom_call" | custom-call | flops 4000000000 | bytes 1000000 | tf_op jit(solution)/shard_map/band_matrices/pallas_call | solution.py:443
  11.1 0.0 collective-permute-done.xfar
  11.1 0.5 %collective-permute-done.1.xnear = bf16[512,128]{1,0:T(8,128)(2,1)S(1)} collective-permute-done((bf16[512,128]{1,0:T(8,128)(2,1)S(1)}, bf16[512,128]{1,0:T(8,128)(2,1)S(1)}, u32[]{:S(2)}, u32[]{:S(2)}) %collective-permute-start.1) | collective-permute-done | bytes 131104 | tf_op jit(solution)/shard_map/ppermute | solution.py:399
  11.6 0.3 join_strips.1
  11.9 0.2 collective-permute-start.2
  12.1 1.5 %collective-permute-start.3 = (bf16[576,128]{1,0:T(8,128)(2,1)S(1)}, bf16[576,128]{1,0:T(8,128)(2,1)S(1)}, u32[]{:S(2)}, u32[]{:S(2)}) collective-permute-start(bf16[576,128]{1,0:T(8,128)(2,1)S(1)} %get-tuple-element.46), channel_id=1, source_target_pairs={{0,2},{2,0},{4,6},{6,4},{1,3},{3,1},{5,7},{7,5},{8,10},{10,8},{12,... | collective-permute-start | bytes 442376 | tf_op jit(solution)/shard_map/ppermute | solution.py:399
  13.6 0.0 copy-start.4
  13.6 0.0 copy-start.5
  13.6 0.0 copy-start.6
  13.6 0.0 copy-start.7
  13.6 0.0 copy-start.8
  13.7 0.0 copy-start.9
  13.7 0.9 %own_rows.1 = (bf16[256,2048]{1,0:T(8,128)(2,1)S(1)}, bf16[384,1536]{1,0:T(8,128)(2,1)S(1)}, f32[128,1024]{1,0:T(8,128)S(1)}, f32[128,1024]{1,0:T(8,128)S(1)}) custom-call(bf16[512,128]{1,0:T(8,128)(2,1)S(1)} %collective-permute-done.xfar, bf16[512,128]{1,0:T(8,128)(2,1)S(1)} %collective-permute-done.1.xnear, ...), custom_call_target="tpu_custom_call" | custom-call | flops 1000000000 | bytes 1000000 | tf_op jit(solution)/shard_map/own_rows/pallas_call | solution.py:454
  14.6 0.2 join_outer.1
  14.8 0.2 collective-permute-start.6
  15.0 0.5 %collective-permute-start.7 = (bf16[320,128]{1,0:T(8,128)(2,1)S(1)}, bf16[320,128]{1,0:T(8,128)(2,1)S(1)}, u32[]{:S(2)}, u32[]{:S(2)}) collective-permute-start(bf16[320,128]{1,0:T(8,128)(2,1)S(1)} %get-tuple-element.60), channel_id=1, source_target_pairs={{0,2},{2,0},{4,6},{6,4},{1,3},{3,1},{5,7},{7,5},{8,10},{10,8},{12,... | collective-permute-start | bytes 245768 | tf_op jit(solution)/shard_map/ppermute | solution.py:399
  15.5 2.5 %collective-permute-done.2.rfar = bf16[576,128]{1,0:T(8,128)(2,1)S(1)} collective-permute-done((bf16[576,128]{1,0:T(8,128)(2,1)S(1)}, bf16[576,128]{1,0:T(8,128)(2,1)S(1)}, u32[]{:S(2)}, u32[]{:S(2)}) %collective-permute-start.2) | collective-permute-done | bytes 147488 | tf_op jit(solution)/shard_map/ppermute | solution.py:398
  18.1 0.0 collective-permute-done.3.rnear
  18.1 0.0 copy-done.4
  18.1 0.0 copy-done.5
  18.1 0.0 copy-done.6
  18.1 0.0 copy-done.7
  18.1 0.0 copy-done.8
  18.1 0.0 copy-done.9
  18.1 3.1 %gradients.1 = (bf16[8,128,128]{2,1,0:T(8,128)(2,1)S(1)}, f32[32,384]{1,0:T(8,128)S(1)}) custom-call(bf16[576,128]{1,0:T(8,128)(2,1)S(1)} %collective-permute-done.2.rfar, bf16[576,128]{1,0:T(8,128)(2,1)S(1)} %collective-permute-done.3.rnear, bf16[256,2048]{1,0:T(8,128)(2,1)S(1)} %get-tuple-element.51.fs, bf16[384,1536]{1,0:T(8,128)(2,1)S(1)} %get-tuple-element.52.cs, ...), custom_call_target="tpu_custom_call" | custom-call | flops 2000000000 | bytes 1000000 | tf_op jit(solution)/shard_map/gradients/pallas_call | solution.py:464
  21.3 0.3 collective-permute-start.4
  21.6 1.0 %collective-permute-done.4.refs_1_ = f32[32,384]{1,0:T(8,128)S(1)} collective-permute-done((f32[32,384]{1,0:T(8,128)S(1)}, f32[32,384]{1,0:T(8,128)S(1)}, u32[]{:S(2)}, u32[]{:S(2)}) %collective-permute-start.4) | collective-permute-done | bytes 49184 | tf_op jit(solution)/shard_map/ppermute | solution.py:404
  22.6 0.9 %collective-permute-start.5 = (bf16[32,384]{1,0:T(8,128)(2,1)S(1)}, bf16[32,384]{1,0:T(8,128)(2,1)S(1)}, u32[]{:S(2)}, u32[]{:S(2)}) collective-permute-start(bf16[32,384]{1,0:T(8,128)(2,1)S(1)} %add_parts.3.refs_0_), channel_id=1, source_target_pairs={{0,4},{2,6},{4,0},{6,2},{1,5},{3,7},{5,1},{7,3},{8,12},{10,14},{12... | collective-permute-start | bytes 73736 | tf_op jit(solution)/shard_map/ppermute | solution.py:404
  23.5 0.0 collective-permute-done.6.rfar_outer
  23.5 0.0 collective-permute-done.7.rnear_outer
  23.5 1.3 %hidden_rim.1.hidden = bf16[12,192,128]{2,1,0:T(8,128)(2,1)S(1)} custom-call(bf16[576,128]{1,0:T(8,128)(2,1)S(1)} %collective-permute-done.2.rfar, bf16[576,128]{1,0:T(8,128)(2,1)S(1)} %collective-permute-done.3.rnear, bf16[320,128]{1,0:T(8,128)(2,1)S(1)} %collective-permute-done.6.rfar_outer, bf16[320,128]{1,0:T(8,128)(2,1)S(1)} %collective-permute-done.7.rnear_outer, ...), custom_call_target="tpu_custom_call" | custom-call | flops 1000000000 | bytes 1000000 | tf_op jit(solution)/shard_map/hidden_rim/pallas_call | solution.py:476
  24.8 1.7 %collective-permute-done.5.refs_1_ = bf16[32,384]{1,0:T(8,128)(2,1)S(1)} collective-permute-done((bf16[32,384]{1,0:T(8,128)(2,1)S(1)}, bf16[32,384]{1,0:T(8,128)(2,1)S(1)}, u32[]{:S(2)}, u32[]{:S(2)}) %collective-permute-start.5) | collective-permute-done | bytes 24608 | tf_op jit(solution)/shard_map/ppermute | solution.py:404
  26.5 1.4 %collective-permute-start.10 = (bf16[32,384]{1,0:T(8,128)(2,1)S(1)}, bf16[32,384]{1,0:T(8,128)(2,1)S(1)}, u32[]{:S(2)}, u32[]{:S(2)}) collective-permute-start(bf16[32,384]{1,0:T(8,128)(2,1)S(1)} %add_parts.4.refs_0_), channel_id=1, source_target_pairs={{0,24},{8,16},{16,8},{24,0},{1,25},{9,17},{17,9},{25,1},{2,26},{10... | collective-permute-start | bytes 73736 | tf_op jit(solution)/shard_map/ppermute | solution.py:404
  27.9 0.8 %collective-permute-start.8 = (bf16[32,384]{1,0:T(8,128)(2,1)S(1)}, bf16[32,384]{1,0:T(8,128)(2,1)S(1)}, u32[]{:S(2)}, u32[]{:S(2)}) collective-permute-start(bf16[32,384]{1,0:T(8,128)(2,1)S(1)} %add_parts.4.refs_0_), channel_id=1, source_target_pairs={{0,8},{8,0},{16,24},{24,16},{1,9},{9,1},{17,25},{25,17},{2,10},{10... | collective-permute-start | bytes 73736 | tf_op jit(solution)/shard_map/ppermute | solution.py:404
  28.8 2.2 %collective-permute-start.9 = (bf16[32,384]{1,0:T(8,128)(2,1)S(1)}, bf16[32,384]{1,0:T(8,128)(2,1)S(1)}, u32[]{:S(2)}, u32[]{:S(2)}) collective-permute-start(bf16[32,384]{1,0:T(8,128)(2,1)S(1)} %add_parts.4.refs_0_), channel_id=1, source_target_pairs={{0,16},{8,24},{16,0},{24,8},{1,17},{9,25},{17,1},{25,9},{2,18},{10... | collective-permute-start | bytes 73736 | tf_op jit(solution)/shard_map/ppermute | solution.py:404
  30.9 1.2 %collective-permute-done.10.refs_3_ = bf16[32,384]{1,0:T(8,128)(2,1)S(1)} collective-permute-done((bf16[32,384]{1,0:T(8,128)(2,1)S(1)}, bf16[32,384]{1,0:T(8,128)(2,1)S(1)}, u32[]{:S(2)}, u32[]{:S(2)}) %collective-permute-start.10) | collective-permute-done | bytes 24608 | tf_op jit(solution)/shard_map/ppermute | solution.py:404
  32.2 0.0 collective-permute-done.8.refs_1_
  32.2 1.3 %collective-permute-done.9.refs_2_ = bf16[32,384]{1,0:T(8,128)(2,1)S(1)} collective-permute-done((bf16[32,384]{1,0:T(8,128)(2,1)S(1)}, bf16[32,384]{1,0:T(8,128)(2,1)S(1)}, u32[]{:S(2)}, u32[]{:S(2)}) %collective-permute-start.9) | collective-permute-done | bytes 24608 | tf_op jit(solution)/shard_map/ppermute | solution.py:404
  33.5 1.6 %collective-permute-start.11 = (bf16[32,384]{1,0:T(8,128)(2,1)S(1)}, bf16[32,384]{1,0:T(8,128)(2,1)S(1)}, u32[]{:S(2)}, u32[]{:S(2)}) collective-permute-start(bf16[32,384]{1,0:T(8,128)(2,1)S(1)} %add_parts.5.refs_0_), channel_id=1, source_target_pairs={{0,1},{1,0},{2,3},{3,2},{4,5},{5,4},{6,7},{7,6},{8,9},{9,8},{10,11... | collective-permute-start | bytes 73736 | tf_op jit(solution)/shard_map/ppermute | solution.py:404
  35.1 1.6 %closure.1 = bf16[1,16,8,8,128]{4,3,2,1,0:T(8,128)(2,1)} custom-call(bf16[12,192,128]{2,1,0:T(8,128)(2,1)S(1)} %hidden_rim.1.hidden, bf16[128,1920]{1,0:T(8,128)(2,1)S(1)} %get-tuple-element.64.t2, f32[128,128]{1,0:T(8,128)S(1)} %get-tuple-element.65.b2), custom_call_target="tpu_custom_call" | custom-call | flops 1000000000 | bytes 1000000 | tf_op jit(solution)/shard_map/closure/pallas_call | solution.py:487
  36.6 0.8 %collective-permute-done.11.refs_1_ = bf16[32,384]{1,0:T(8,128)(2,1)S(1)} collective-permute-done((bf16[32,384]{1,0:T(8,128)(2,1)S(1)}, bf16[32,384]{1,0:T(8,128)(2,1)S(1)}, u32[]{:S(2)}, u32[]{:S(2)}) %collective-permute-start.11) | collective-permute-done | bytes 24608 | tf_op jit(solution)/shard_map/ppermute | solution.py:404
  37.4 0.8 %finish.1 = (f32[128,27]{1,0:T(8,128)}, f32[256,27]{1,0:T(8,128)}, f32[1,16]{1,0:T(1,128)}) custom-call(bf16[32,384]{1,0:T(8,128)(2,1)S(1)} %add_parts.5.refs_0_, bf16[32,384]{1,0:T(8,128)(2,1)S(1)} %collective-permute-done.11.refs_1_), custom_call_target="tpu_custom_call" | custom-call | flops 10000000 | bytes 1000000 | tf_op jit(solution)/shard_map/finish/pallas_call | solution.py:498
  (3 shorter events, 0.1 us)
Async XLA Ops:
  1.7 6.8 %copy-start = (bf16[27,16,16]{0,2,1:T(8,128)(2,1)S(1)}, bf16[27,16,16]{0,2,1:T(8,128)(2,1)}, u32[]{:S(2)}) copy-start(bf16[27,16,16]{0,2,1:T(8,128)(2,1)} %param.15) | copy-start | bytes 41476
  1.7 6.8 %copy-start.1 = (bf16[27,16,8]{0,2,1:T(8,128)(2,1)S(1)}, bf16[27,16,8]{0,2,1:T(8,128)(2,1)}, u32[]{:S(2)}) copy-start(bf16[27,16,8]{0,2,1:T(8,128)(2,1)} %param.13) | copy-start | bytes 20740
  1.7 6.7 %copy-start.2 = (f32[16]{0:T(128)S(1)}, f32[16]{0:T(128)}, u32[]{:S(2)}) copy-start(f32[16]{0:T(128)} %param.14) | copy-start | bytes 196
  1.7 6.7 %copy-start.3 = (f32[16]{0:T(128)S(1)}, f32[16]{0:T(128)}, u32[]{:S(2)}) copy-start(f32[16]{0:T(128)} %param.16) | copy-start | bytes 196
  1.8 9.3 %collective-permute-start = (bf16[512,128]{1,0:T(8,128)(2,1)S(1)}, bf16[512,128]{1,0:T(8,128)(2,1)S(1)}, u32[]{:S(2)}, u32[]{:S(2)}) collective-permute-start(bf16[512,128]{1,0:T(8,128)(2,1)S(1)} %get-tuple-element.37), channel_id=1, source_target_pairs={{8,16},{16,8},{0,0},{24,24},{9,17},{17,9},{1,1},{25,25},{10,18},{1... | collective-permute-start | bytes 393224 | tf_op jit(solution)/shard_map/ppermute | solution.py:398
  2.5 9.1 %collective-permute-start.1 = (bf16[512,128]{1,0:T(8,128)(2,1)S(1)}, bf16[512,128]{1,0:T(8,128)(2,1)S(1)}, u32[]{:S(2)}, u32[]{:S(2)}) collective-permute-start(bf16[512,128]{1,0:T(8,128)(2,1)S(1)} %get-tuple-element.38), channel_id=1, source_target_pairs={{0,8},{8,0},{16,24},{24,16},{1,9},{9,1},{17,25},{25,17},{2,10},{10... | collective-permute-start | bytes 393224 | tf_op jit(solution)/shard_map/ppermute | solution.py:399
  11.9 6.1 %collective-permute-start.2 = (bf16[576,128]{1,0:T(8,128)(2,1)S(1)}, bf16[576,128]{1,0:T(8,128)(2,1)S(1)}, u32[]{:S(2)}, u32[]{:S(2)}) collective-permute-start(bf16[576,128]{1,0:T(8,128)(2,1)S(1)} %get-tuple-element.45), channel_id=1, source_target_pairs={{2,4},{4,2},{0,6},{6,0},{3,5},{5,3},{1,7},{7,1},{10,12},{12,10},{8... | collective-permute-start | bytes 442376 | tf_op jit(solution)/shard_map/ppermute | solution.py:398
  12.1 6.0 %collective-permute-start.3 = (bf16[576,128]{1,0:T(8,128)(2,1)S(1)}, bf16[576,128]{1,0:T(8,128)(2,1)S(1)}, u32[]{:S(2)}, u32[]{:S(2)}) collective-permute-start(bf16[576,128]{1,0:T(8,128)(2,1)S(1)} %get-tuple-element.46), channel_id=1, source_target_pairs={{0,2},{2,0},{4,6},{6,4},{1,3},{3,1},{5,7},{7,5},{8,10},{10,8},{12,... | collective-permute-start | bytes 442376 | tf_op jit(solution)/shard_map/ppermute | solution.py:399
  13.6 4.4 %copy-start.4 = (bf16[128,768]{1,0:T(8,128)(2,1)S(1)}, bf16[128,768]{1,0:T(8,128)(2,1)}, u32[]{:S(2)}) copy-start(bf16[128,768]{1,0:T(8,128)(2,1)} %constant.15.clone.rep2) | copy-start | bytes 589828
  13.6 4.4 %copy-start.5 = (bf16[640,128]{1,0:T(8,128)(2,1)S(1)}, bf16[640,128]{1,0:T(8,128)(2,1)}, u32[]{:S(2)}) copy-start(bf16[640,128]{1,0:T(8,128)(2,1)} %constant.13.clone.e2t) | copy-start | bytes 491524
  13.6 4.4 %copy-start.6 = (bf16[384,128]{1,0:T(8,128)(2,1)S(1)}, bf16[384,128]{1,0:T(8,128)(2,1)}, u32[]{:S(2)}) copy-start(bf16[384,128]{1,0:T(8,128)(2,1)} %constant.12.clone.e1t) | copy-start | bytes 294916
  13.6 4.5 %copy-start.7 = (bf16[128,384]{1,0:T(8,128)(2,1)S(1)}, bf16[128,384]{1,0:T(8,128)(2,1)}, u32[]{:S(2)}) copy-start(bf16[128,384]{1,0:T(8,128)(2,1)} %constant.14.clone.rep1) | copy-start | bytes 294916
  13.6 4.5 %copy-start.8 = (f32[1,640]{1,0:T(1,128)S(1)}, f32[1,640]{1,0:T(1,128)}, u32[]{:S(2)}) copy-start(f32[1,640]{1,0:T(1,128)} %constant.17.clone.y2) | copy-start | bytes 7684
  13.7 4.5 %copy-start.9 = (f32[1,384]{1,0:T(1,128)S(1)}, f32[1,384]{1,0:T(1,128)}, u32[]{:S(2)}) copy-start(f32[1,384]{1,0:T(1,128)} %constant.16.clone.y1) | copy-start | bytes 4612
  14.8 8.7 %collective-permute-start.6 = (bf16[320,128]{1,0:T(8,128)(2,1)S(1)}, bf16[320,128]{1,0:T(8,128)(2,1)S(1)}, u32[]{:S(2)}, u32[]{:S(2)}) collective-permute-start(bf16[320,128]{1,0:T(8,128)(2,1)S(1)} %get-tuple-element.59), channel_id=1, source_target_pairs={{2,4},{4,2},{0,6},{6,0},{3,5},{5,3},{1,7},{7,1},{10,12},{12,10},{8... | collective-permute-start | bytes 245768 | tf_op jit(solution)/shard_map/ppermute | solution.py:398
  15.0 8.5 %collective-permute-start.7 = (bf16[320,128]{1,0:T(8,128)(2,1)S(1)}, bf16[320,128]{1,0:T(8,128)(2,1)S(1)}, u32[]{:S(2)}, u32[]{:S(2)}) collective-permute-start(bf16[320,128]{1,0:T(8,128)(2,1)S(1)} %get-tuple-element.60), channel_id=1, source_target_pairs={{0,2},{2,0},{4,6},{6,4},{1,3},{3,1},{5,7},{7,5},{8,10},{10,8},{12,... | collective-permute-start | bytes 245768 | tf_op jit(solution)/shard_map/ppermute | solution.py:399
  21.3 1.3 %collective-permute-start.4 = (f32[32,384]{1,0:T(8,128)S(1)}, f32[32,384]{1,0:T(8,128)S(1)}, u32[]{:S(2)}, u32[]{:S(2)}) collective-permute-start(f32[32,384]{1,0:T(8,128)S(1)} %get-tuple-element.57.refs_0_), channel_id=1, source_target_pairs={{0,2},{2,0},{4,6},{6,4},{1,3},{3,1},{5,7},{7,5},{8,10},{10,8},{12,... | collective-permute-start | bytes 147464 | tf_op jit(solution)/shard_map/ppermute | solution.py:404
  22.6 3.9 %collective-permute-start.5 = (bf16[32,384]{1,0:T(8,128)(2,1)S(1)}, bf16[32,384]{1,0:T(8,128)(2,1)S(1)}, u32[]{:S(2)}, u32[]{:S(2)}) collective-permute-start(bf16[32,384]{1,0:T(8,128)(2,1)S(1)} %add_parts.3.refs_0_), channel_id=1, source_target_pairs={{0,4},{2,6},{4,0},{6,2},{1,5},{3,7},{5,1},{7,3},{8,12},{10,14},{12... | collective-permute-start | bytes 73736 | tf_op jit(solution)/shard_map/ppermute | solution.py:404
  26.5 5.7 %collective-permute-start.10 = (bf16[32,384]{1,0:T(8,128)(2,1)S(1)}, bf16[32,384]{1,0:T(8,128)(2,1)S(1)}, u32[]{:S(2)}, u32[]{:S(2)}) collective-permute-start(bf16[32,384]{1,0:T(8,128)(2,1)S(1)} %add_parts.4.refs_0_), channel_id=1, source_target_pairs={{0,24},{8,16},{16,8},{24,0},{1,25},{9,17},{17,9},{25,1},{2,26},{10... | collective-permute-start | bytes 73736 | tf_op jit(solution)/shard_map/ppermute | solution.py:404
  27.9 4.3 %collective-permute-start.8 = (bf16[32,384]{1,0:T(8,128)(2,1)S(1)}, bf16[32,384]{1,0:T(8,128)(2,1)S(1)}, u32[]{:S(2)}, u32[]{:S(2)}) collective-permute-start(bf16[32,384]{1,0:T(8,128)(2,1)S(1)} %add_parts.4.refs_0_), channel_id=1, source_target_pairs={{0,8},{8,0},{16,24},{24,16},{1,9},{9,1},{17,25},{25,17},{2,10},{10... | collective-permute-start | bytes 73736 | tf_op jit(solution)/shard_map/ppermute | solution.py:404
  28.8 4.7 %collective-permute-start.9 = (bf16[32,384]{1,0:T(8,128)(2,1)S(1)}, bf16[32,384]{1,0:T(8,128)(2,1)S(1)}, u32[]{:S(2)}, u32[]{:S(2)}) collective-permute-start(bf16[32,384]{1,0:T(8,128)(2,1)S(1)} %add_parts.4.refs_0_), channel_id=1, source_target_pairs={{0,16},{8,24},{16,0},{24,8},{1,17},{9,25},{17,1},{25,9},{2,18},{10... | collective-permute-start | bytes 73736 | tf_op jit(solution)/shard_map/ppermute | solution.py:404
  33.5 3.9 %collective-permute-start.11 = (bf16[32,384]{1,0:T(8,128)(2,1)S(1)}, bf16[32,384]{1,0:T(8,128)(2,1)S(1)}, u32[]{:S(2)}, u32[]{:S(2)}) collective-permute-start(bf16[32,384]{1,0:T(8,128)(2,1)S(1)} %add_parts.5.refs_0_), channel_id=1, source_target_pairs={{0,1},{1,0},{2,3},{3,2},{4,5},{5,4},{6,7},{7,6},{8,9},{9,8},{10,11... | collective-permute-start | bytes 73736 | tf_op jit(solution)/shard_map/ppermute | solution.py:404

commit v14 on v13

--- a/solution.py
+++ b/solution.py
@@ -391,11 +391,15 @@
     return jax.ShapeDtypeStruct(dims, dtype)
 
 
-def exchange(near, far, axis, ends):
-    count = lax.axis_size(axis)
-    pairs = [(i, i - 1 + 2 * (i % 2)) for i in range(1, count - 1)]
-    pairs += [(0, count - 1), (count - 1, 0)] if ends else [(0, 0), (count - 1, count - 1)]
-    far = lax.ppermute(far, axis, pairs)
+def exchange(near, far, axis, other):
+    count, others = lax.axis_size(axis), lax.axis_size(other)
+    pairs = []
+    for i in range(count):
+        for j in range(others):
+            end = i in (0, count - 1)
+            to = (i, j ^ 1 if others % 2 == 0 else j) if end else (i - 1 + 2 * (i % 2), j)
+            pairs.append((i * others + j, to[0] * others + to[1]))
+    far = lax.ppermute(far, (axis, other), pairs)
     return lax.ppermute(near, axis, [(i, i ^ 1) for i in range(count)]), far
 
 
@@ -437,7 +441,7 @@
         "pack_strips",
         flops=4_000_000_000,
     )(jnp.concatenate([fields[0], cotangent[0]], axis=0))
-    xnear, xfar = exchange(near, far, "stream", False)
+    xnear, xfar = exchange(near, far, "stream", "radial")
     wide = (planes + 4) * Z
     counts = (lax.axis_size("stream"), lax.axis_size("radial"))
     t1o, t1r, t1d, tbo, tbr, t2, b1, b2 = call(
@@ -450,7 +454,7 @@
     xfar, xnear, t1o, tbo = lax.optimization_barrier((xfar, xnear, t1o, tbo))
     inner, outer = shape((planes + 4) * 48, Z), shape(128 + (planes + 4) * 16, Z)
     near, far = call(functools.partial(join_kernel, counts), (inner, inner), "join_strips")(xfar, xnear, f_rows, c_rows)
-    rnear, rfar = exchange(near, far, "radial", True)
+    rnear, rfar = exchange(near, far, "radial", "snap")
     fs, cs, pre, back = call(
         functools.partial(own_kernel, counts),
         (shape(256, wide + 4 * Z), shape(384, wide), shape(128, planes * Z, dtype=F32), shape(128, planes * Z, dtype=F32)),
@@ -460,7 +464,7 @@
     f_rows, fs = lax.optimization_barrier((f_rows, fs))
     near_outer, far_outer = call(functools.partial(join_outer_kernel, counts), (outer, outer), "join_outer")(
         xfar, xnear, f_rows, c_rows)
-    rnear_outer, rfar_outer = exchange(near_outer, far_outer, "radial", True)
+    rnear_outer, rfar_outer = exchange(near_outer, far_outer, "radial", "snap")
     hidden, payload = call(
         functools.partial(rim_kernel, counts),
         (shape(planes, 128, Z), shape(32, 384, dtype=F32)),

time: 38.4 us -> 36.5 us (0.951)
  starting transfers between devices: 16.3 us -> 15 us
  waiting for transfers between devices: 8.97 us -> 8.32 us
    ppermute x3, starting transfers between devices: 7.95 us -> 4.29 us  [exchange(): return (lax.ppermute(near, axis, [(i, i ^ 1) for i in range(count)]), far)]
    ppermute x3, starting transfers between devices: 1.02 us -> 3.63 us  [exchange(): far = lax.ppermute(far, (axis, other), pairs)]
    ppermute x3, waiting for transfers between devices: 2.54 us -> 0.75 us  [exchange(): far = lax.ppermute(far, (axis, other), pairs)]
    ppermute x6, waiting for transfers between devices: 5.93 us -> 7.08 us  [swap(): lax.ppermute(v, axis, [(i, i ^ mask) for i in range(count)])]
  transfers between devices with their start and end apart: 12 -> 12, of which waited for: 7 -> 8; matrix products, arithmetic and copies ran while one was open for 0% -> 0% of each run, Pallas kernels for 26% -> 27%
where the time goes in v14:
time: 36.5 us; the launch traced here: 36.3 us
  starting transfers between devices  15 us (41%)
  Pallas kernels  11.1 us (30%)
  waiting for transfers between devices  8.32 us (23%)
  other arithmetic  1.02 us (3%)
  between operations  0.81 us (2%)
    ppermute x6, starting transfers between devices, swap(): lax.ppermute(v, axis, [(i, i ^ mask) for i in range(count)])  7.1 us
    ppermute x6, waiting for transfers between devices, swap(): lax.ppermute(v, axis, [(i, i ^ mask) for i in range(count)])  7.08 us
    ppermute x3, starting transfers between devices, exchange(): return (lax.ppermute(near, axis, [(i, i ^ 1) for i in range(count)]), far)  4.29 us
    ppermute x3, starting transfers between devices, exchange(): far = lax.ppermute(far, (axis, other), pairs)  3.63 us
    pallas_call x1, Pallas kernels, local(): call(functools.partial(rim_kernel, counts), (shape(planes, 128, Z), shape...  3.13 us
    pallas_call x1, Pallas kernels, local(): call(band_kernel, (shape(192, 768), shape(128, 384), shape(192, 768), sha...  2.7 us
    pallas_call x1, Pallas kernels, local(): call(closure_kernel, shape(*cotangent.shape), 'closure', (pltpu.VMEM((640...  1.56 us
    pallas_call x1, Pallas kernels, local(): call(functools.partial(hidden_rim_kernel, counts), shape(planes + 4, 192,...  1.26 us
  transfers between devices with their start and end apart: 12, of which 8 were waited for; matrix products, arithmetic and copies ran while one was open for 0% of the time, Pallas kernels for 27%

profile of v14, /device:TPU:0, one launch (start us, length us, event | category | flops | bytes accessed | tf_op | source)
XLA Modules:
  0.0 36.3 jit_solution(3611532053135575781)
XLA Ops:
  0.6 1.0 %pad_maximum_fusion.inputs = bf16[24,8,8,128]{3,2,1,0:T(8,128)(2,1)S(1)} fusion(bf16[16,8,8,128]{3,2,1,0:T(8,128)(2,1)} %bitcast.21, bf16[8,8,8,128]{3,2,1,0:T(8,128)(2,1)} %bitcast.22), kind=kLoop, calls=%fused_computation | loop fusion | flops 196608 | bytes 786432 | tf_op jit(solution)/shard_map/concatenate | solution.py:443
  1.7 0.0 copy-start
  1.7 0.0 copy-start.1
  1.7 0.0 copy-start.2
  1.7 0.0 copy-start.3
  1.7 0.1 pack_strips.1
  1.8 0.5 %collective-permute-start = (bf16[512,128]{1,0:T(8,128)(2,1)S(1)}, bf16[512,128]{1,0:T(8,128)(2,1)S(1)}, u32[]{:S(2)}, u32[]{:S(2)}) collective-permute-start(bf16[512,128]{1,0:T(8,128)(2,1)S(1)} %get-tuple-element.37), channel_id=1, source_target_pairs={{0,2},{2,0},{4,6},{6,4},{8,16},{10,18},{12,20},{14,22},{16,8},{18,... | collective-permute-start | bytes 393224 | tf_op jit(solution)/shard_map/ppermute | solution.py:402
  2.4 4.1 %collective-permute-start.1 = (bf16[512,128]{1,0:T(8,128)(2,1)S(1)}, bf16[512,128]{1,0:T(8,128)(2,1)S(1)}, u32[]{:S(2)}, u32[]{:S(2)}) collective-permute-start(bf16[512,128]{1,0:T(8,128)(2,1)S(1)} %get-tuple-element.38), channel_id=1, source_target_pairs={{0,8},{8,0},{16,24},{24,16},{1,9},{9,1},{17,25},{25,17},{2,10},{10... | collective-permute-start | bytes 393224 | tf_op jit(solution)/shard_map/ppermute | solution.py:403
  6.5 0.0 copy-done
  6.5 0.0 copy-done.1
  6.5 0.0 copy-done.2
  6.5 0.0 copy-done.3
  6.5 2.7 %band_matrices.1 = (bf16[192,768]{1,0:T(8,128)(2,1)S(1)}, bf16[128,384]{1,0:T(8,128)(2,1)S(1)}, bf16[192,768]{1,0:T(8,128)(2,1)S(1)}, bf16[128,1152]{1,0:T(8,128...) custom-call(bf16[128,27]{1,0:T(8,128)(2,1)S(1)} %bitcast.18, ...), custom_call_target="tpu_custom_call" | custom-call | flops 4000000000 | bytes 1000000 | tf_op jit(solution)/shard_map/band_matrices/pallas_call | solution.py:447
  9.2 0.0 collective-permute-done.xfar
  9.2 0.5 %collective-permute-done.1.xnear = bf16[512,128]{1,0:T(8,128)(2,1)S(1)} collective-permute-done((bf16[512,128]{1,0:T(8,128)(2,1)S(1)}, bf16[512,128]{1,0:T(8,128)(2,1)S(1)}, u32[]{:S(2)}, u32[]{:S(2)}) %collective-permute-start.1) | collective-permute-done | bytes 131104 | tf_op jit(solution)/shard_map/ppermute | solution.py:403
  9.7 0.3 join_strips.1
  10.0 1.6 %collective-permute-start.2 = (bf16[576,128]{1,0:T(8,128)(2,1)S(1)}, bf16[576,128]{1,0:T(8,128)(2,1)S(1)}, u32[]{:S(2)}, u32[]{:S(2)}) collective-permute-start(bf16[576,128]{1,0:T(8,128)(2,1)S(1)} %get-tuple-element.45), channel_id=1, source_target_pairs={{0,1},{1,0},{2,4},{3,5},{4,2},{5,3},{6,7},{7,6},{8,9},{9,8},{10,12... | collective-permute-start | bytes 442376 | tf_op jit(solution)/shard_map/ppermute | solution.py:402
  11.6 0.1 collective-permute-start.3
  11.7 0.0 copy-start.4
  11.7 0.0 copy-start.5
  11.7 0.0 copy-start.6
  11.7 0.0 copy-start.7
  11.7 0.0 copy-start.8
  11.7 0.0 copy-start.9
  11.7 0.9 %own_rows.1 = (bf16[256,2048]{1,0:T(8,128)(2,1)S(1)}, bf16[384,1536]{1,0:T(8,128)(2,1)S(1)}, f32[128,1024]{1,0:T(8,128)S(1)}, f32[128,1024]{1,0:T(8,128)S(1)}) custom-call(bf16[512,128]{1,0:T(8,128)(2,1)S(1)} %collective-permute-done.xfar, bf16[512,128]{1,0:T(8,128)(2,1)S(1)} %collective-permute-done.1.xnear, ...), custom_call_target="tpu_custom_call" | custom-call | flops 1000000000 | bytes 1000000 | tf_op jit(solution)/shard_map/own_rows/pallas_call | solution.py:458
  12.7 0.2 join_outer.1
  12.9 1.6 %collective-permute-start.6 = (bf16[320,128]{1,0:T(8,128)(2,1)S(1)}, bf16[320,128]{1,0:T(8,128)(2,1)S(1)}, u32[]{:S(2)}, u32[]{:S(2)}) collective-permute-start(bf16[320,128]{1,0:T(8,128)(2,1)S(1)} %get-tuple-element.59), channel_id=1, source_target_pairs={{0,1},{1,0},{2,4},{3,5},{4,2},{5,3},{6,7},{7,6},{8,9},{9,8},{10,12... | collective-permute-start | bytes 245768 | tf_op jit(solution)/shard_map/ppermute | solution.py:402
  14.5 0.0 collective-permute-start.7
  14.5 0.7 %collective-permute-done.2.rfar = bf16[576,128]{1,0:T(8,128)(2,1)S(1)} collective-permute-done((bf16[576,128]{1,0:T(8,128)(2,1)S(1)}, bf16[576,128]{1,0:T(8,128)(2,1)S(1)}, u32[]{:S(2)}, u32[]{:S(2)}) %collective-permute-start.2) | collective-permute-done | bytes 147488 | tf_op jit(solution)/shard_map/ppermute | solution.py:402
  15.2 0.0 collective-permute-done.3.rnear
  15.2 0.0 copy-done.4
  15.2 0.0 copy-done.5
  15.2 0.0 copy-done.6
  15.2 0.0 copy-done.7
  15.3 0.0 copy-done.8
  15.3 0.0 copy-done.9
  15.3 3.1 %gradients.1 = (bf16[8,128,128]{2,1,0:T(8,128)(2,1)S(1)}, f32[32,384]{1,0:T(8,128)S(1)}) custom-call(bf16[576,128]{1,0:T(8,128)(2,1)S(1)} %collective-permute-done.2.rfar, bf16[576,128]{1,0:T(8,128)(2,1)S(1)} %collective-permute-done.3.rnear, bf16[256,2048]{1,0:T(8,128)(2,1)S(1)} %get-tuple-element.51.fs, bf16[384,1536]{1,0:T(8,128)(2,1)S(1)} %get-tuple-element.52.cs, ...), custom_call_target="tpu_custom_call" | custom-call | flops 2000000000 | bytes 1000000 | tf_op jit(solution)/shard_map/gradients/pallas_call | solution.py:468
  18.4 0.1 collective-permute-start.4
  18.5 1.2 %collective-permute-done.4.refs_1_ = f32[32,384]{1,0:T(8,128)S(1)} collective-permute-done((f32[32,384]{1,0:T(8,128)S(1)}, f32[32,384]{1,0:T(8,128)S(1)}, u32[]{:S(2)}, u32[]{:S(2)}) %collective-permute-start.4) | collective-permute-done | bytes 49184 | tf_op jit(solution)/shard_map/ppermute | solution.py:408
  19.7 1.0 %collective-permute-start.5 = (bf16[32,384]{1,0:T(8,128)(2,1)S(1)}, bf16[32,384]{1,0:T(8,128)(2,1)S(1)}, u32[]{:S(2)}, u32[]{:S(2)}) collective-permute-start(bf16[32,384]{1,0:T(8,128)(2,1)S(1)} %add_parts.3.refs_0_), channel_id=1, source_target_pairs={{0,4},{2,6},{4,0},{6,2},{1,5},{3,7},{5,1},{7,3},{8,12},{10,14},{12... | collective-permute-start | bytes 73736 | tf_op jit(solution)/shard_map/ppermute | solution.py:408
  20.7 0.0 collective-permute-done.6.rfar_outer
  20.7 0.0 collective-permute-done.7.rnear_outer
  20.7 1.3 %hidden_rim.1.hidden = bf16[12,192,128]{2,1,0:T(8,128)(2,1)S(1)} custom-call(bf16[576,128]{1,0:T(8,128)(2,1)S(1)} %collective-permute-done.2.rfar, bf16[576,128]{1,0:T(8,128)(2,1)S(1)} %collective-permute-done.3.rnear, bf16[320,128]{1,0:T(8,128)(2,1)S(1)} %collective-permute-done.6.rfar_outer, bf16[320,128]{1,0:T(8,128)(2,1)S(1)} %collective-permute-done.7.rnear_outer, ...), custom_call_target="tpu_custom_call" | custom-call | flops 1000000000 | bytes 1000000 | tf_op jit(solution)/shard_map/hidden_rim/pallas_call | solution.py:480
  22.0 1.6 %collective-permute-done.5.refs_1_ = bf16[32,384]{1,0:T(8,128)(2,1)S(1)} collective-permute-done((bf16[32,384]{1,0:T(8,128)(2,1)S(1)}, bf16[32,384]{1,0:T(8,128)(2,1)S(1)}, u32[]{:S(2)}, u32[]{:S(2)}) %collective-permute-start.5) | collective-permute-done | bytes 24608 | tf_op jit(solution)/shard_map/ppermute | solution.py:408
  23.6 3.2 %collective-permute-start.10 = (bf16[32,384]{1,0:T(8,128)(2,1)S(1)}, bf16[32,384]{1,0:T(8,128)(2,1)S(1)}, u32[]{:S(2)}, u32[]{:S(2)}) collective-permute-start(bf16[32,384]{1,0:T(8,128)(2,1)S(1)} %add_parts.4.refs_0_), channel_id=1, source_target_pairs={{0,24},{8,16},{16,8},{24,0},{1,25},{9,17},{17,9},{25,1},{2,26},{10... | collective-permute-start | bytes 73736 | tf_op jit(solution)/shard_map/ppermute | solution.py:408
  26.9 0.0 collective-permute-start.8
  26.9 1.2 %collective-permute-start.9 = (bf16[32,384]{1,0:T(8,128)(2,1)S(1)}, bf16[32,384]{1,0:T(8,128)(2,1)S(1)}, u32[]{:S(2)}, u32[]{:S(2)}) collective-permute-start(bf16[32,384]{1,0:T(8,128)(2,1)S(1)} %add_parts.4.refs_0_), channel_id=1, source_target_pairs={{0,16},{8,24},{16,0},{24,8},{1,17},{9,25},{17,1},{25,9},{2,18},{10... | collective-permute-start | bytes 73736 | tf_op jit(solution)/shard_map/ppermute | solution.py:408
  28.1 1.3 %collective-permute-done.10.refs_3_ = bf16[32,384]{1,0:T(8,128)(2,1)S(1)} collective-permute-done((bf16[32,384]{1,0:T(8,128)(2,1)S(1)}, bf16[32,384]{1,0:T(8,128)(2,1)S(1)}, u32[]{:S(2)}, u32[]{:S(2)}) %collective-permute-start.10) | collective-permute-done | bytes 24608 | tf_op jit(solution)/shard_map/ppermute | solution.py:408
  29.4 1.3 %collective-permute-done.8.refs_1_ = bf16[32,384]{1,0:T(8,128)(2,1)S(1)} collective-permute-done((bf16[32,384]{1,0:T(8,128)(2,1)S(1)}, bf16[32,384]{1,0:T(8,128)(2,1)S(1)}, u32[]{:S(2)}, u32[]{:S(2)}) %collective-permute-start.8) | collective-permute-done | bytes 24608 | tf_op jit(solution)/shard_map/ppermute | solution.py:408
  30.7 0.9 %collective-permute-done.9.refs_2_ = bf16[32,384]{1,0:T(8,128)(2,1)S(1)} collective-permute-done((bf16[32,384]{1,0:T(8,128)(2,1)S(1)}, bf16[32,384]{1,0:T(8,128)(2,1)S(1)}, u32[]{:S(2)}, u32[]{:S(2)}) %collective-permute-start.9) | collective-permute-done | bytes 24608 | tf_op jit(solution)/shard_map/ppermute | solution.py:408
  31.6 1.6 %collective-permute-start.11 = (bf16[32,384]{1,0:T(8,128)(2,1)S(1)}, bf16[32,384]{1,0:T(8,128)(2,1)S(1)}, u32[]{:S(2)}, u32[]{:S(2)}) collective-permute-start(bf16[32,384]{1,0:T(8,128)(2,1)S(1)} %add_parts.5.refs_0_), channel_id=1, source_target_pairs={{0,1},{1,0},{2,3},{3,2},{4,5},{5,4},{6,7},{7,6},{8,9},{9,8},{10,11... | collective-permute-start | bytes 73736 | tf_op jit(solution)/shard_map/ppermute | solution.py:408
  33.2 1.6 %closure.1 = bf16[1,16,8,8,128]{4,3,2,1,0:T(8,128)(2,1)} custom-call(bf16[12,192,128]{2,1,0:T(8,128)(2,1)S(1)} %hidden_rim.1.hidden, bf16[128,1920]{1,0:T(8,128)(2,1)S(1)} %get-tuple-element.64.t2, f32[128,128]{1,0:T(8,128)S(1)} %get-tuple-element.65.b2), custom_call_target="tpu_custom_call" | custom-call | flops 1000000000 | bytes 1000000 | tf_op jit(solution)/shard_map/closure/pallas_call | solution.py:491
  34.7 0.8 %collective-permute-done.11.refs_1_ = bf16[32,384]{1,0:T(8,128)(2,1)S(1)} collective-permute-done((bf16[32,384]{1,0:T(8,128)(2,1)S(1)}, bf16[32,384]{1,0:T(8,128)(2,1)S(1)}, u32[]{:S(2)}, u32[]{:S(2)}) %collective-permute-start.11) | collective-permute-done | bytes 24608 | tf_op jit(solution)/shard_map/ppermute | solution.py:408
  35.5 0.8 %finish.1 = (f32[128,27]{1,0:T(8,128)}, f32[256,27]{1,0:T(8,128)}, f32[1,16]{1,0:T(1,128)}) custom-call(bf16[32,384]{1,0:T(8,128)(2,1)S(1)} %add_parts.5.refs_0_, bf16[32,384]{1,0:T(8,128)(2,1)S(1)} %collective-permute-done.11.refs_1_), custom_call_target="tpu_custom_call" | custom-call | flops 10000000 | bytes 1000000 | tf_op jit(solution)/shard_map/finish/pallas_call | solution.py:502
  (3 shorter events, 0.1 us)
Async XLA Ops:
  1.7 4.8 %copy-start = (bf16[27,16,16]{0,2,1:T(8,128)(2,1)S(1)}, bf16[27,16,16]{0,2,1:T(8,128)(2,1)}, u32[]{:S(2)}) copy-start(bf16[27,16,16]{0,2,1:T(8,128)(2,1)} %param.15) | copy-start | bytes 41476
  1.7 4.8 %copy-start.1 = (bf16[27,16,8]{0,2,1:T(8,128)(2,1)S(1)}, bf16[27,16,8]{0,2,1:T(8,128)(2,1)}, u32[]{:S(2)}) copy-start(bf16[27,16,8]{0,2,1:T(8,128)(2,1)} %param.13) | copy-start | bytes 20740
  1.7 4.8 %copy-start.2 = (f32[16]{0:T(128)S(1)}, f32[16]{0:T(128)}, u32[]{:S(2)}) copy-start(f32[16]{0:T(128)} %param.14) | copy-start | bytes 196
  1.7 4.8 %copy-start.3 = (f32[16]{0:T(128)S(1)}, f32[16]{0:T(128)}, u32[]{:S(2)}) copy-start(f32[16]{0:T(128)} %param.16) | copy-start | bytes 196
  1.8 7.4 %collective-permute-start = (bf16[512,128]{1,0:T(8,128)(2,1)S(1)}, bf16[512,128]{1,0:T(8,128)(2,1)S(1)}, u32[]{:S(2)}, u32[]{:S(2)}) collective-permute-start(bf16[512,128]{1,0:T(8,128)(2,1)S(1)} %get-tuple-element.37), channel_id=1, source_target_pairs={{0,2},{2,0},{4,6},{6,4},{8,16},{10,18},{12,20},{14,22},{16,8},{18,... | collective-permute-start | bytes 393224 | tf_op jit(solution)/shard_map/ppermute | solution.py:402
  2.4 7.4 %collective-permute-start.1 = (bf16[512,128]{1,0:T(8,128)(2,1)S(1)}, bf16[512,128]{1,0:T(8,128)(2,1)S(1)}, u32[]{:S(2)}, u32[]{:S(2)}) collective-permute-start(bf16[512,128]{1,0:T(8,128)(2,1)S(1)} %get-tuple-element.38), channel_id=1, source_target_pairs={{0,8},{8,0},{16,24},{24,16},{1,9},{9,1},{17,25},{25,17},{2,10},{10... | collective-permute-start | bytes 393224 | tf_op jit(solution)/shard_map/ppermute | solution.py:403
  10.0 5.2 %collective-permute-start.2 = (bf16[576,128]{1,0:T(8,128)(2,1)S(1)}, bf16[576,128]{1,0:T(8,128)(2,1)S(1)}, u32[]{:S(2)}, u32[]{:S(2)}) collective-permute-start(bf16[576,128]{1,0:T(8,128)(2,1)S(1)} %get-tuple-element.45), channel_id=1, source_target_pairs={{0,1},{1,0},{2,4},{3,5},{4,2},{5,3},{6,7},{7,6},{8,9},{9,8},{10,12... | collective-permute-start | bytes 442376 | tf_op jit(solution)/shard_map/ppermute | solution.py:402
  11.6 3.7 %collective-permute-start.3 = (bf16[576,128]{1,0:T(8,128)(2,1)S(1)}, bf16[576,128]{1,0:T(8,128)(2,1)S(1)}, u32[]{:S(2)}, u32[]{:S(2)}) collective-permute-start(bf16[576,128]{1,0:T(8,128)(2,1)S(1)} %get-tuple-element.46), channel_id=1, source_target_pairs={{0,2},{2,0},{4,6},{6,4},{1,3},{3,1},{5,7},{7,5},{8,10},{10,8},{12,... | collective-permute-start | bytes 442376 | tf_op jit(solution)/shard_map/ppermute | solution.py:403
  11.7 3.5 %copy-start.4 = (bf16[128,768]{1,0:T(8,128)(2,1)S(1)}, bf16[128,768]{1,0:T(8,128)(2,1)}, u32[]{:S(2)}) copy-start(bf16[128,768]{1,0:T(8,128)(2,1)} %constant.15.clone.rep2) | copy-start | bytes 589828
  11.7 3.5 %copy-start.5 = (bf16[640,128]{1,0:T(8,128)(2,1)S(1)}, bf16[640,128]{1,0:T(8,128)(2,1)}, u32[]{:S(2)}) copy-start(bf16[640,128]{1,0:T(8,128)(2,1)} %constant.13.clone.e2t) | copy-start | bytes 491524
  11.7 3.5 %copy-start.6 = (bf16[384,128]{1,0:T(8,128)(2,1)S(1)}, bf16[384,128]{1,0:T(8,128)(2,1)}, u32[]{:S(2)}) copy-start(bf16[384,128]{1,0:T(8,128)(2,1)} %constant.12.clone.e1t) | copy-start | bytes 294916
  11.7 3.5 %copy-start.7 = (bf16[128,384]{1,0:T(8,128)(2,1)S(1)}, bf16[128,384]{1,0:T(8,128)(2,1)}, u32[]{:S(2)}) copy-start(bf16[128,384]{1,0:T(8,128)(2,1)} %constant.14.clone.rep1) | copy-start | bytes 294916
  11.7 3.5 %copy-start.8 = (f32[1,640]{1,0:T(1,128)S(1)}, f32[1,640]{1,0:T(1,128)}, u32[]{:S(2)}) copy-start(f32[1,640]{1,0:T(1,128)} %constant.17.clone.y2) | copy-start | bytes 7684
  11.7 3.5 %copy-start.9 = (f32[1,384]{1,0:T(1,128)S(1)}, f32[1,384]{1,0:T(1,128)}, u32[]{:S(2)}) copy-start(f32[1,384]{1,0:T(1,128)} %constant.16.clone.y1) | copy-start | bytes 4612
  12.9 7.8 %collective-permute-start.6 = (bf16[320,128]{1,0:T(8,128)(2,1)S(1)}, bf16[320,128]{1,0:T(8,128)(2,1)S(1)}, u32[]{:S(2)}, u32[]{:S(2)}) collective-permute-start(bf16[320,128]{1,0:T(8,128)(2,1)S(1)} %get-tuple-element.59), channel_id=1, source_target_pairs={{0,1},{1,0},{2,4},{3,5},{4,2},{5,3},{6,7},{7,6},{8,9},{9,8},{10,12... | collective-permute-start | bytes 245768 | tf_op jit(solution)/shard_map/ppermute | solution.py:402
  14.5 6.3 %collective-permute-start.7 = (bf16[320,128]{1,0:T(8,128)(2,1)S(1)}, bf16[320,128]{1,0:T(8,128)(2,1)S(1)}, u32[]{:S(2)}, u32[]{:S(2)}) collective-permute-start(bf16[320,128]{1,0:T(8,128)(2,1)S(1)} %get-tuple-element.60), channel_id=1, source_target_pairs={{0,2},{2,0},{4,6},{6,4},{1,3},{3,1},{5,7},{7,5},{8,10},{10,8},{12,... | collective-permute-start | bytes 245768 | tf_op jit(solution)/shard_map/ppermute | solution.py:403
  18.4 1.3 %collective-permute-start.4 = (f32[32,384]{1,0:T(8,128)S(1)}, f32[32,384]{1,0:T(8,128)S(1)}, u32[]{:S(2)}, u32[]{:S(2)}) collective-permute-start(f32[32,384]{1,0:T(8,128)S(1)} %get-tuple-element.57.refs_0_), channel_id=1, source_target_pairs={{0,2},{2,0},{4,6},{6,4},{1,3},{3,1},{5,7},{7,5},{8,10},{10,8},{12,... | collective-permute-start | bytes 147464 | tf_op jit(solution)/shard_map/ppermute | solution.py:408
  19.7 3.9 %collective-permute-start.5 = (bf16[32,384]{1,0:T(8,128)(2,1)S(1)}, bf16[32,384]{1,0:T(8,128)(2,1)S(1)}, u32[]{:S(2)}, u32[]{:S(2)}) collective-permute-start(bf16[32,384]{1,0:T(8,128)(2,1)S(1)} %add_parts.3.refs_0_), channel_id=1, source_target_pairs={{0,4},{2,6},{4,0},{6,2},{1,5},{3,7},{5,1},{7,3},{8,12},{10,14},{12... | collective-permute-start | bytes 73736 | tf_op jit(solution)/shard_map/ppermute | solution.py:408
  23.6 5.7 %collective-permute-start.10 = (bf16[32,384]{1,0:T(8,128)(2,1)S(1)}, bf16[32,384]{1,0:T(8,128)(2,1)S(1)}, u32[]{:S(2)}, u32[]{:S(2)}) collective-permute-start(bf16[32,384]{1,0:T(8,128)(2,1)S(1)} %add_parts.4.refs_0_), channel_id=1, source_target_pairs={{0,24},{8,16},{16,8},{24,0},{1,25},{9,17},{17,9},{25,1},{2,26},{10... | collective-permute-start | bytes 73736 | tf_op jit(solution)/shard_map/ppermute | solution.py:408
  26.9 3.8 %collective-permute-start.8 = (bf16[32,384]{1,0:T(8,128)(2,1)S(1)}, bf16[32,384]{1,0:T(8,128)(2,1)S(1)}, u32[]{:S(2)}, u32[]{:S(2)}) collective-permute-start(bf16[32,384]{1,0:T(8,128)(2,1)S(1)} %add_parts.4.refs_0_), channel_id=1, source_target_pairs={{0,8},{8,0},{16,24},{24,16},{1,9},{9,1},{17,25},{25,17},{2,10},{10... | collective-permute-start | bytes 73736 | tf_op jit(solution)/shard_map/ppermute | solution.py:408
  26.9 4.7 %collective-permute-start.9 = (bf16[32,384]{1,0:T(8,128)(2,1)S(1)}, bf16[32,384]{1,0:T(8,128)(2,1)S(1)}, u32[]{:S(2)}, u32[]{:S(2)}) collective-permute-start(bf16[32,384]{1,0:T(8,128)(2,1)S(1)} %add_parts.4.refs_0_), channel_id=1, source_target_pairs={{0,16},{8,24},{16,0},{24,8},{1,17},{9,25},{17,1},{25,9},{2,18},{10... | collective-permute-start | bytes 73736 | tf_op jit(solution)/shard_map/ppermute | solution.py:408
  31.6 3.9 %collective-permute-start.11 = (bf16[32,384]{1,0:T(8,128)(2,1)S(1)}, bf16[32,384]{1,0:T(8,128)(2,1)S(1)}, u32[]{:S(2)}, u32[]{:S(2)}) collective-permute-start(bf16[32,384]{1,0:T(8,128)(2,1)S(1)} %add_parts.5.refs_0_), channel_id=1, source_target_pairs={{0,1},{1,0},{2,3},{3,2},{4,5},{5,4},{6,7},{7,6},{8,9},{9,8},{10,11... | collective-permute-start | bytes 73736 | tf_op jit(solution)/shard_map/ppermute | solution.py:408

commit v15 on v14

--- a/solution.py
+++ b/solution.py
@@ -190,10 +190,10 @@
     out[...] = jnp.broadcast_to(column, out.shape)
 
 
-def band_kernel(w1, w2, first_bias, second_bias, t1o, t1r, t1d, tbo, tbr, t2, b1, b2):
+def band_first_kernel(w1, w2, first_bias, t1o, t1r, tbo, tbr, b1):
     expand, rows_y = row_table(192, y_first)
     parts = spread(w1, True, False)
-    for of, step, t in ((natural, 64, t1o), (rim(CI), 32, t1r), (deep_rim, 64, t1d)):
+    for of, step, t in ((natural, 64, t1o), (rim(CI), 32, t1r)):
         wide = packed(parts, lambda n: n % CI, of, step)
         band(wide, expand, lane_y(of, wide.shape[1], step), rows_y, t)
     parts = spread(w2, False, True)
@@ -201,6 +201,12 @@
         wide = packed(parts, lambda n: n // CH, of, step)
         band(wide, expand, lane_y(of, wide.shape[1], step), rows_y, t)
     repeat_bias(first_bias, expand, b1)
+
+
+def band_second_kernel(w1, w2, second_bias, t1d, t2, b2):
+    expand, rows_y = row_table(192, y_first)
+    wide = packed(spread(w1, True, False), lambda n: n % CI, deep_rim, 64)
+    band(wide, expand, lane_y(deep_rim, wide.shape[1], 64), rows_y, t1d)
     expand, rows_y = row_table(128, natural)
     parts = spread(w2, True, False)
     wide = [packed(parts, lambda n: n % CH, of, step) for of, step in ((y_first, 128), (rim(CH), 64))]
@@ -444,13 +450,12 @@
     xnear, xfar = exchange(near, far, "stream", "radial")
     wide = (planes + 4) * Z
     counts = (lax.axis_size("stream"), lax.axis_size("radial"))
-    t1o, t1r, t1d, tbo, tbr, t2, b1, b2 = call(
-        band_kernel,
-        (shape(192, 768), shape(128, 384), shape(192, 768), shape(128, 1152), shape(128, 768), shape(128, 1920),
-         shape(192, 128, dtype=F32), shape(128, 128, dtype=F32)),
-        "band_matrices",
+    t1o, t1r, tbo, tbr, b1 = call(
+        band_first_kernel,
+        (shape(192, 768), shape(128, 384), shape(128, 1152), shape(128, 768), shape(192, 128, dtype=F32)),
+        "band_first",
         flops=4_000_000_000,
-    )(w1, w2, first_bias[None], second_bias[None])
+    )(w1, w2, first_bias[None])
     xfar, xnear, t1o, tbo = lax.optimization_barrier((xfar, xnear, t1o, tbo))
     inner, outer = shape((planes + 4) * 48, Z), shape(128 + (planes + 4) * 16, Z)
     near, far = call(functools.partial(join_kernel, counts), (inner, inner), "join_strips")(xfar, xnear, f_rows, c_rows)
@@ -475,8 +480,16 @@
 
     steps = rounds("radial", 2) + rounds("stream", 4) + rounds("snap", 2)
     arrived = swap(payload, *steps[0])
-    payload = add(payload, arrived)
+    payload, w2 = lax.optimization_barrier((add(payload, arrived), w2))
     arrived = swap(payload, *steps[1])
+    t1d, t2, b2 = call(
+        band_second_kernel,
+        (shape(192, 768), shape(128, 1920), shape(128, 128, dtype=F32)),
+        "band_second",
+        flops=1_000_000_000,
+    )(w1, w2, second_bias[None])
+    payload, t1d, t2, b2 = lax.optimization_barrier((add(payload, arrived), t1d, t2, b2))
+    arrived = swap(payload, *steps[2])
     hidden = call(
         functools.partial(hidden_rim_kernel, counts),
         shape(planes + 4, 192, Z),
@@ -485,8 +498,6 @@
         flops=1_000_000_000,
     )(rfar, rnear, rfar_outer, rnear_outer, hidden, fs, t1o, t1d, b1)
     payload, hidden = lax.optimization_barrier((add(payload, arrived), hidden))
-    arrived = swap(payload, *steps[2])
-    payload = add(payload, arrived)
     arrived = swap(payload, *steps[3])
     closure = call(
         closure_kernel, shape(*cotangent.shape), "closure", (pltpu.VMEM((640, wide), BF16),), flops=1_000_000_000

time: 36.5 us -> 39 us (1.068)
  waiting for transfers between devices: 8.32 us -> 11.6 us
  starting transfers between devices: 15 us -> 14 us
    ppermute x3, waiting for transfers between devices: 0.75 us -> 2.51 us  [exchange(): far = lax.ppermute(far, (axis, other), pairs)]
    ppermute x6, starting transfers between devices: 7.1 us -> 5.6 us  [swap(): lax.ppermute(v, axis, [(i, i ^ mask) for i in range(count)])]
    ppermute x3, waiting for transfers between devices: 0.49 us -> 1.52 us  [exchange(): return (lax.ppermute(near, axis, [(i, i ^ 1) for i in range(count)]), far)]
    ppermute x3, starting transfers between devices: 4.29 us -> 4.85 us  [exchange(): return (lax.ppermute(near, axis, [(i, i ^ 1) for i in range(count)]), far)]
    ppermute x6, waiting for transfers between devices: 7.08 us -> 7.57 us  [swap(): lax.ppermute(v, axis, [(i, i ^ mask) for i in range(count)])]
    pallas_call x1 -> x2, Pallas kernels: 2.7 us -> 2.93 us  [the longest x1 1.67 us: local(): call(band_first_kernel, (shape(192, 768), shape(128, 384), shape(128, 115...]
  transfers between devices with their start and end apart: 12 -> 12, of which waited for: 8 -> 6; matrix products, arithmetic and copies ran while one was open for 0% -> 0% of each run, Pallas kernels for 27% -> 18%
where the time goes in v15:
time: 39 us; the launch traced here: 38.8 us
  starting transfers between devices  14 us (36%)
  waiting for transfers between devices  11.6 us (30%)
  Pallas kernels  11.3 us (29%)
  other arithmetic  1.02 us (3%)
  between operations  0.83 us (2%)
    ppermute x6, waiting for transfers between devices, swap(): lax.ppermute(v, axis, [(i, i ^ mask) for i in range(count)])  7.57 us
    ppermute x6, starting transfers between devices, swap(): lax.ppermute(v, axis, [(i, i ^ mask) for i in range(count)])  5.6 us
    ppermute x3, starting transfers between devices, exchange(): return (lax.ppermute(near, axis, [(i, i ^ 1) for i in range(count)]), far)  4.85 us
    ppermute x3, starting transfers between devices, exchange(): far = lax.ppermute(far, (axis, other), pairs)  3.57 us
    pallas_call x1, Pallas kernels, local(): call(functools.partial(rim_kernel, counts), (shape(planes, 128, Z), shape...  3.14 us
    ppermute x3, waiting for transfers between devices, exchange(): far = lax.ppermute(far, (axis, other), pairs)  2.51 us
    pallas_call x1, Pallas kernels, local(): call(band_first_kernel, (shape(192, 768), shape(128, 384), shape(128, 115...  1.67 us
    pallas_call x1, Pallas kernels, local(): call(closure_kernel, shape(*cotangent.shape), 'closure', (pltpu.VMEM((640...  1.57 us
  transfers between devices with their start and end apart: 12, of which 6 were waited for; matrix products, arithmetic and copies ran while one was open for 0% of the time, Pallas kernels for 18%

profile of v15, /device:TPU:0, one launch (start us, length us, event | category | flops | bytes accessed | tf_op | source)
XLA Modules:
  0.0 38.8 jit_solution(129901647078054292)
XLA Ops:
  0.6 1.0 %pad_maximum_fusion.inputs = bf16[24,8,8,128]{3,2,1,0:T(8,128)(2,1)S(1)} fusion(bf16[16,8,8,128]{3,2,1,0:T(8,128)(2,1)} %bitcast.23, bf16[8,8,8,128]{3,2,1,0:T(8,128)(2,1)} %bitcast.24), kind=kLoop, calls=%fused_computation | loop fusion | flops 196608 | bytes 786432 | tf_op jit(solution)/shard_map/concatenate | solution.py:449
  1.7 0.0 copy-start
  1.7 0.0 copy-start.1
  1.7 0.0 copy-start.2
  1.7 0.1 pack_strips.1
  1.8 0.5 %collective-permute-start = (bf16[512,128]{1,0:T(8,128)(2,1)S(1)}, bf16[512,128]{1,0:T(8,128)(2,1)S(1)}, u32[]{:S(2)}, u32[]{:S(2)}) collective-permute-start(bf16[512,128]{1,0:T(8,128)(2,1)S(1)} %get-tuple-element.43), channel_id=1, source_target_pairs={{0,2},{2,0},{4,6},{6,4},{8,16},{10,18},{12,20},{14,22},{16,8},{18,... | collective-permute-start | bytes 393224 | tf_op jit(solution)/shard_map/ppermute | solution.py:408
  2.3 4.1 %collective-permute-start.1 = (bf16[512,128]{1,0:T(8,128)(2,1)S(1)}, bf16[512,128]{1,0:T(8,128)(2,1)S(1)}, u32[]{:S(2)}, u32[]{:S(2)}) collective-permute-start(bf16[512,128]{1,0:T(8,128)(2,1)S(1)} %get-tuple-element.44), channel_id=1, source_target_pairs={{0,8},{8,0},{16,24},{24,16},{1,9},{9,1},{17,25},{25,17},{2,10},{10... | collective-permute-start | bytes 393224 | tf_op jit(solution)/shard_map/ppermute | solution.py:409
  6.5 0.0 copy-done
  6.5 0.0 copy-done.1
  6.5 0.0 copy-done.2
  6.5 1.7 %band_first.1 = (bf16[192,768]{1,0:T(8,128)(2,1)S(1)}, bf16[128,384]{1,0:T(8,128)(2,1)S(1)}, bf16[128,1152]{1,0:T(8,128)(2,1)S(1)}, bf16[128,768]{1,0:T(8,128)(2,1)S(1)}, f32[192,128]{1,0:T(8,128)S(1)}) custom-call(bf16[128,27]{1,0:T(8,128)(2,1)S(1)} %bitcast.19, bf16[256,27]{1,0:T(8,128)(2,1)S(1)} %bitcast.17, f32[1,16]{1,0:T(1,128)S(1)} %bitcast.21), custom_call_target="tpu_custom_call" | custom-call | flops 4000000000 | bytes 1000000 | tf_op jit(solution)/shard_map/band_first/pallas_call | solution.py:453
  8.2 0.0 collective-permute-done.xfar
  8.2 1.5 %collective-permute-done.1.xnear = bf16[512,128]{1,0:T(8,128)(2,1)S(1)} collective-permute-done((bf16[512,128]{1,0:T(8,128)(2,1)S(1)}, bf16[512,128]{1,0:T(8,128)(2,1)S(1)}, u32[]{:S(2)}, u32[]{:S(2)}) %collective-permute-start.1) | collective-permute-done | bytes 131104 | tf_op jit(solution)/shard_map/ppermute | solution.py:409
  9.7 0.3 join_strips.1
  10.0 1.6 %collective-permute-start.2 = (bf16[576,128]{1,0:T(8,128)(2,1)S(1)}, bf16[576,128]{1,0:T(8,128)(2,1)S(1)}, u32[]{:S(2)}, u32[]{:S(2)}) collective-permute-start(bf16[576,128]{1,0:T(8,128)(2,1)S(1)} %get-tuple-element.51), channel_id=1, source_target_pairs={{0,1},{1,0},{2,4},{3,5},{4,2},{5,3},{6,7},{7,6},{8,9},{9,8},{10,12... | collective-permute-start | bytes 442376 | tf_op jit(solution)/shard_map/ppermute | solution.py:408
  11.6 0.1 collective-permute-start.3
  11.7 0.0 copy-start.4
  11.7 0.0 copy-start.5
  11.7 0.0 copy-start.6
  11.7 0.0 copy-start.7
  11.7 0.0 copy-start.8
  11.7 0.0 copy-start.9
  11.7 1.0 %own_rows.1 = (bf16[256,2048]{1,0:T(8,128)(2,1)S(1)}, bf16[384,1536]{1,0:T(8,128)(2,1)S(1)}, f32[128,1024]{1,0:T(8,128)S(1)}, f32[128,1024]{1,0:T(8,128)S(1)}) custom-call(bf16[512,128]{1,0:T(8,128)(2,1)S(1)} %collective-permute-done.xfar, bf16[512,128]{1,0:T(8,128)(2,1)S(1)} %collective-permute-done.1.xnear, ...), custom_call_target="tpu_custom_call" | custom-call | flops 1000000000 | bytes 1000000 | tf_op jit(solution)/shard_map/own_rows/pallas_call | solution.py:463
  12.7 2.5 %collective-permute-done.2.rfar = bf16[576,128]{1,0:T(8,128)(2,1)S(1)} collective-permute-done((bf16[576,128]{1,0:T(8,128)(2,1)S(1)}, bf16[576,128]{1,0:T(8,128)(2,1)S(1)}, u32[]{:S(2)}, u32[]{:S(2)}) %collective-permute-start.2) | collective-permute-done | bytes 147488 | tf_op jit(solution)/shard_map/ppermute | solution.py:408
  15.2 0.0 collective-permute-done.3.rnear
  15.2 0.0 copy-done.4
  15.2 0.0 copy-done.5
  15.2 0.0 copy-done.6
  15.2 0.0 copy-done.7
  15.2 0.0 copy-done.8
  15.2 0.0 copy-done.9
  15.3 0.0 copy-start.3
  15.3 3.1 %gradients.1 = (bf16[8,128,128]{2,1,0:T(8,128)(2,1)S(1)}, f32[32,384]{1,0:T(8,128)S(1)}) custom-call(bf16[576,128]{1,0:T(8,128)(2,1)S(1)} %collective-permute-done.2.rfar, bf16[576,128]{1,0:T(8,128)(2,1)S(1)} %collective-permute-done.3.rnear, bf16[256,2048]{1,0:T(8,128)(2,1)S(1)} %get-tuple-element.57.fs, bf16[384,1536]{1,0:T(8,128)(2,1)S(1)} %get-tuple-element.58.cs, ...), custom_call_target="tpu_custom_call" | custom-call | flops 2000000000 | bytes 1000000 | tf_op jit(solution)/shard_map/gradients/pallas_call | solution.py:473
  18.4 0.1 collective-permute-start.4
  18.5 0.2 join_outer.1
  18.7 0.6 %collective-permute-start.10 = (bf16[320,128]{1,0:T(8,128)(2,1)S(1)}, bf16[320,128]{1,0:T(8,128)(2,1)S(1)}, u32[]{:S(2)}, u32[]{:S(2)}) collective-permute-start(bf16[320,128]{1,0:T(8,128)(2,1)S(1)} %get-tuple-element.72), channel_id=1, source_target_pairs={{0,2},{2,0},{4,6},{6,4},{1,3},{3,1},{5,7},{7,5},{8,10},{10,8},{12,... | collective-permute-start | bytes 245768 | tf_op jit(solution)/shard_map/ppermute | solution.py:409
  19.3 1.5 %collective-permute-start.9 = (bf16[320,128]{1,0:T(8,128)(2,1)S(1)}, bf16[320,128]{1,0:T(8,128)(2,1)S(1)}, u32[]{:S(2)}, u32[]{:S(2)}) collective-permute-start(bf16[320,128]{1,0:T(8,128)(2,1)S(1)} %get-tuple-element.71), channel_id=1, source_target_pairs={{0,1},{1,0},{2,4},{3,5},{4,2},{5,3},{6,7},{7,6},{8,9},{9,8},{10,12... | collective-permute-start | bytes 245768 | tf_op jit(solution)/shard_map/ppermute | solution.py:408
  20.8 0.0 collective-permute-done.4.refs_1_
  20.8 0.3 collective-permute-start.5
  21.1 0.0 copy-done.3
  21.1 1.3 %band_second.1 = (bf16[192,768]{1,0:T(8,128)(2,1)S(1)}, bf16[128,1920]{1,0:T(8,128)(2,1)S(1)}, f32[128,128]{1,0:T(8,128)S(1)}) custom-call(bf16[128,27]{1,0:T(8,128)(2,1)S(1)} %bitcast.20, bf16[256,27]{1,0:T(8,128)(2,1)S(1)} %bitcast.18, f32[1,16]{1,0:T(1,128)S(1)} %bitcast.22), custom_call_target="tpu_custom_call" | custom-call | flops 1000000000 | bytes 1000000 | tf_op jit(solution)/shard_map/band_second/pallas_call | solution.py:485
  22.3 2.3 %collective-permute-done.5.refs_1_ = bf16[32,384]{1,0:T(8,128)(2,1)S(1)} collective-permute-done((bf16[32,384]{1,0:T(8,128)(2,1)S(1)}, bf16[32,384]{1,0:T(8,128)(2,1)S(1)}, u32[]{:S(2)}, u32[]{:S(2)}) %collective-permute-start.5) | collective-permute-done | bytes 24608 | tf_op jit(solution)/shard_map/ppermute | solution.py:414
  24.7 1.8 %collective-permute-start.6 = (bf16[32,384]{1,0:T(8,128)(2,1)S(1)}, bf16[32,384]{1,0:T(8,128)(2,1)S(1)}, u32[]{:S(2)}, u32[]{:S(2)}) collective-permute-start(bf16[32,384]{1,0:T(8,128)(2,1)S(1)} %add_parts.4.refs_0_), channel_id=1, source_target_pairs={{0,8},{8,0},{16,24},{24,16},{1,9},{9,1},{17,25},{25,17},{2,10},{10... | collective-permute-start | bytes 73736 | tf_op jit(solution)/shard_map/ppermute | solution.py:414
  26.5 2.0 %collective-permute-start.7 = (bf16[32,384]{1,0:T(8,128)(2,1)S(1)}, bf16[32,384]{1,0:T(8,128)(2,1)S(1)}, u32[]{:S(2)}, u32[]{:S(2)}) collective-permute-start(bf16[32,384]{1,0:T(8,128)(2,1)S(1)} %add_parts.4.refs_0_), channel_id=1, source_target_pairs={{0,16},{8,24},{16,0},{24,8},{1,17},{9,25},{17,1},{25,9},{2,18},{10... | collective-permute-start | bytes 73736 | tf_op jit(solution)/shard_map/ppermute | solution.py:414
  28.5 0.7 %collective-permute-start.8 = (bf16[32,384]{1,0:T(8,128)(2,1)S(1)}, bf16[32,384]{1,0:T(8,128)(2,1)S(1)}, u32[]{:S(2)}, u32[]{:S(2)}) collective-permute-start(bf16[32,384]{1,0:T(8,128)(2,1)S(1)} %add_parts.4.refs_0_), channel_id=1, source_target_pairs={{0,24},{8,16},{16,8},{24,0},{1,25},{9,17},{17,9},{25,1},{2,26},{10... | collective-permute-start | bytes 73736 | tf_op jit(solution)/shard_map/ppermute | solution.py:414
  29.2 0.0 collective-permute-done.10.rnear_outer
  29.2 0.0 collective-permute-done.9.rfar_outer
  29.2 1.2 %hidden_rim.1.hidden = bf16[12,192,128]{2,1,0:T(8,128)(2,1)S(1)} custom-call(bf16[576,128]{1,0:T(8,128)(2,1)S(1)} %collective-permute-done.2.rfar, bf16[576,128]{1,0:T(8,128)(2,1)S(1)} %collective-permute-done.3.rnear, bf16[320,128]{1,0:T(8,128)(2,1)S(1)} %collective-permute-done.9.rfar_outer, bf16[320,128]{1,0:T(8,128)(2,1)S(1)} %collective-permute-done.10.rnear_outer, ...), custom_call_target="tpu_custom_call" | custom-call | flops 1000000000 | bytes 1000000 | tf_op jit(solution)/shard_map/hidden_rim/pallas_call | solution.py:493
  30.4 0.0 collective-permute-done.6.refs_1_
  30.4 0.8 %collective-permute-done.7.refs_2_ = bf16[32,384]{1,0:T(8,128)(2,1)S(1)} collective-permute-done((bf16[32,384]{1,0:T(8,128)(2,1)S(1)}, bf16[32,384]{1,0:T(8,128)(2,1)S(1)}, u32[]{:S(2)}, u32[]{:S(2)}) %collective-permute-start.7) | collective-permute-done | bytes 24608 | tf_op jit(solution)/shard_map/ppermute | solution.py:414
  31.3 2.9 %collective-permute-done.8.refs_3_ = bf16[32,384]{1,0:T(8,128)(2,1)S(1)} collective-permute-done((bf16[32,384]{1,0:T(8,128)(2,1)S(1)}, bf16[32,384]{1,0:T(8,128)(2,1)S(1)}, u32[]{:S(2)}, u32[]{:S(2)}) %collective-permute-start.8) | collective-permute-done | bytes 24608 | tf_op jit(solution)/shard_map/ppermute | solution.py:414
  34.2 0.8 %collective-permute-start.11 = (bf16[32,384]{1,0:T(8,128)(2,1)S(1)}, bf16[32,384]{1,0:T(8,128)(2,1)S(1)}, u32[]{:S(2)}, u32[]{:S(2)}) collective-permute-start(bf16[32,384]{1,0:T(8,128)(2,1)S(1)} %add_parts.5.refs_0_), channel_id=1, source_target_pairs={{0,1},{1,0},{2,3},{3,2},{4,5},{5,4},{6,7},{7,6},{8,9},{9,8},{10,11... | collective-permute-start | bytes 73736 | tf_op jit(solution)/shard_map/ppermute | solution.py:414
  35.0 1.6 %closure.1 = bf16[1,16,8,8,128]{4,3,2,1,0:T(8,128)(2,1)} custom-call(bf16[12,192,128]{2,1,0:T(8,128)(2,1)S(1)} %hidden_rim.1.hidden, bf16[128,1920]{1,0:T(8,128)(2,1)S(1)} %get-tuple-element.76.t2, f32[128,128]{1,0:T(8,128)S(1)} %get-tuple-element.77.b2), custom_call_target="tpu_custom_call" | custom-call | flops 1000000000 | bytes 1000000 | tf_op jit(solution)/shard_map/closure/pallas_call | solution.py:502
  36.5 1.5 %collective-permute-done.11.refs_1_ = bf16[32,384]{1,0:T(8,128)(2,1)S(1)} collective-permute-done((bf16[32,384]{1,0:T(8,128)(2,1)S(1)}, bf16[32,384]{1,0:T(8,128)(2,1)S(1)}, u32[]{:S(2)}, u32[]{:S(2)}) %collective-permute-start.11) | collective-permute-done | bytes 24608 | tf_op jit(solution)/shard_map/ppermute | solution.py:414
  38.0 0.8 %finish.1 = (f32[128,27]{1,0:T(8,128)}, f32[256,27]{1,0:T(8,128)}, f32[1,16]{1,0:T(1,128)}) custom-call(bf16[32,384]{1,0:T(8,128)(2,1)S(1)} %add_parts.5.refs_0_, bf16[32,384]{1,0:T(8,128)(2,1)S(1)} %collective-permute-done.11.refs_1_), custom_call_target="tpu_custom_call" | custom-call | flops 10000000 | bytes 1000000 | tf_op jit(solution)/shard_map/finish/pallas_call | solution.py:513
  (3 shorter events, 0.1 us)
Async XLA Ops:
  1.7 4.8 %copy-start = (bf16[27,16,16]{0,2,1:T(8,128)(2,1)S(1)}, bf16[27,16,16]{0,2,1:T(8,128)(2,1)}, u32[]{:S(2)}) copy-start(bf16[27,16,16]{0,2,1:T(8,128)(2,1)} %param.15) | copy-start | bytes 41476
  1.7 4.8 %copy-start.1 = (bf16[27,16,8]{0,2,1:T(8,128)(2,1)S(1)}, bf16[27,16,8]{0,2,1:T(8,128)(2,1)}, u32[]{:S(2)}) copy-start(bf16[27,16,8]{0,2,1:T(8,128)(2,1)} %param.13) | copy-start | bytes 20740
  1.7 4.8 %copy-start.2 = (f32[16]{0:T(128)S(1)}, f32[16]{0:T(128)}, u32[]{:S(2)}) copy-start(f32[16]{0:T(128)} %param.14) | copy-start | bytes 196
  1.8 6.4 %collective-permute-start = (bf16[512,128]{1,0:T(8,128)(2,1)S(1)}, bf16[512,128]{1,0:T(8,128)(2,1)S(1)}, u32[]{:S(2)}, u32[]{:S(2)}) collective-permute-start(bf16[512,128]{1,0:T(8,128)(2,1)S(1)} %get-tuple-element.43), channel_id=1, source_target_pairs={{0,2},{2,0},{4,6},{6,4},{8,16},{10,18},{12,20},{14,22},{16,8},{18,... | collective-permute-start | bytes 393224 | tf_op jit(solution)/shard_map/ppermute | solution.py:408
  2.3 7.4 %collective-permute-start.1 = (bf16[512,128]{1,0:T(8,128)(2,1)S(1)}, bf16[512,128]{1,0:T(8,128)(2,1)S(1)}, u32[]{:S(2)}, u32[]{:S(2)}) collective-permute-start(bf16[512,128]{1,0:T(8,128)(2,1)S(1)} %get-tuple-element.44), channel_id=1, source_target_pairs={{0,8},{8,0},{16,24},{24,16},{1,9},{9,1},{17,25},{25,17},{2,10},{10... | collective-permute-start | bytes 393224 | tf_op jit(solution)/shard_map/ppermute | solution.py:409
  10.0 5.2 %collective-permute-start.2 = (bf16[576,128]{1,0:T(8,128)(2,1)S(1)}, bf16[576,128]{1,0:T(8,128)(2,1)S(1)}, u32[]{:S(2)}, u32[]{:S(2)}) collective-permute-start(bf16[576,128]{1,0:T(8,128)(2,1)S(1)} %get-tuple-element.51), channel_id=1, source_target_pairs={{0,1},{1,0},{2,4},{3,5},{4,2},{5,3},{6,7},{7,6},{8,9},{9,8},{10,12... | collective-permute-start | bytes 442376 | tf_op jit(solution)/shard_map/ppermute | solution.py:408
  11.6 3.7 %collective-permute-start.3 = (bf16[576,128]{1,0:T(8,128)(2,1)S(1)}, bf16[576,128]{1,0:T(8,128)(2,1)S(1)}, u32[]{:S(2)}, u32[]{:S(2)}) collective-permute-start(bf16[576,128]{1,0:T(8,128)(2,1)S(1)} %get-tuple-element.52), channel_id=1, source_target_pairs={{0,2},{2,0},{4,6},{6,4},{1,3},{3,1},{5,7},{7,5},{8,10},{10,8},{12,... | collective-permute-start | bytes 442376 | tf_op jit(solution)/shard_map/ppermute | solution.py:409
  11.7 3.5 %copy-start.4 = (bf16[128,768]{1,0:T(8,128)(2,1)S(1)}, bf16[128,768]{1,0:T(8,128)(2,1)}, u32[]{:S(2)}) copy-start(bf16[128,768]{1,0:T(8,128)(2,1)} %constant.15.clone.rep2) | copy-start | bytes 589828
  11.7 3.5 %copy-start.5 = (bf16[640,128]{1,0:T(8,128)(2,1)S(1)}, bf16[640,128]{1,0:T(8,128)(2,1)}, u32[]{:S(2)}) copy-start(bf16[640,128]{1,0:T(8,128)(2,1)} %constant.13.clone.e2t) | copy-start | bytes 491524
  11.7 3.5 %copy-start.6 = (bf16[384,128]{1,0:T(8,128)(2,1)S(1)}, bf16[384,128]{1,0:T(8,128)(2,1)}, u32[]{:S(2)}) copy-start(bf16[384,128]{1,0:T(8,128)(2,1)} %constant.12.clone.e1t) | copy-start | bytes 294916
  11.7 3.5 %copy-start.7 = (bf16[128,384]{1,0:T(8,128)(2,1)S(1)}, bf16[128,384]{1,0:T(8,128)(2,1)}, u32[]{:S(2)}) copy-start(bf16[128,384]{1,0:T(8,128)(2,1)} %constant.14.clone.rep1) | copy-start | bytes 294916
  11.7 3.5 %copy-start.8 = (f32[1,640]{1,0:T(1,128)S(1)}, f32[1,640]{1,0:T(1,128)}, u32[]{:S(2)}) copy-start(f32[1,640]{1,0:T(1,128)} %constant.17.clone.y2) | copy-start | bytes 7684
  11.7 3.5 %copy-start.9 = (f32[1,384]{1,0:T(1,128)S(1)}, f32[1,384]{1,0:T(1,128)}, u32[]{:S(2)}) copy-start(f32[1,384]{1,0:T(1,128)} %constant.16.clone.y1) | copy-start | bytes 4612
  15.3 5.8 %copy-start.3 = (f32[16]{0:T(128)S(1)}, f32[16]{0:T(128)}, u32[]{:S(2)}) copy-start(f32[16]{0:T(128)} %param.16) | copy-start | bytes 196
  18.4 2.4 %collective-permute-start.4 = (f32[32,384]{1,0:T(8,128)S(1)}, f32[32,384]{1,0:T(8,128)S(1)}, u32[]{:S(2)}, u32[]{:S(2)}) collective-permute-start(f32[32,384]{1,0:T(8,128)S(1)} %get-tuple-element.63.refs_0_), channel_id=1, source_target_pairs={{0,2},{2,0},{4,6},{6,4},{1,3},{3,1},{5,7},{7,5},{8,10},{10,8},{12,... | collective-permute-start | bytes 147464 | tf_op jit(solution)/shard_map/ppermute | solution.py:414
  18.7 10.4 %collective-permute-start.10 = (bf16[320,128]{1,0:T(8,128)(2,1)S(1)}, bf16[320,128]{1,0:T(8,128)(2,1)S(1)}, u32[]{:S(2)}, u32[]{:S(2)}) collective-permute-start(bf16[320,128]{1,0:T(8,128)(2,1)S(1)} %get-tuple-element.72), channel_id=1, source_target_pairs={{0,2},{2,0},{4,6},{6,4},{1,3},{3,1},{5,7},{7,5},{8,10},{10,8},{12,... | collective-permute-start | bytes 245768 | tf_op jit(solution)/shard_map/ppermute | solution.py:409
  19.3 9.9 %collective-permute-start.9 = (bf16[320,128]{1,0:T(8,128)(2,1)S(1)}, bf16[320,128]{1,0:T(8,128)(2,1)S(1)}, u32[]{:S(2)}, u32[]{:S(2)}) collective-permute-start(bf16[320,128]{1,0:T(8,128)(2,1)S(1)} %get-tuple-element.71), channel_id=1, source_target_pairs={{0,1},{1,0},{2,4},{3,5},{4,2},{5,3},{6,7},{7,6},{8,9},{9,8},{10,12... | collective-permute-start | bytes 245768 | tf_op jit(solution)/shard_map/ppermute | solution.py:408
  20.8 3.9 %collective-permute-start.5 = (bf16[32,384]{1,0:T(8,128)(2,1)S(1)}, bf16[32,384]{1,0:T(8,128)(2,1)S(1)}, u32[]{:S(2)}, u32[]{:S(2)}) collective-permute-start(bf16[32,384]{1,0:T(8,128)(2,1)S(1)} %add_parts.3.refs_0_), channel_id=1, source_target_pairs={{0,4},{2,6},{4,0},{6,2},{1,5},{3,7},{5,1},{7,3},{8,12},{10,14},{12... | collective-permute-start | bytes 73736 | tf_op jit(solution)/shard_map/ppermute | solution.py:414
  24.7 5.7 %collective-permute-start.6 = (bf16[32,384]{1,0:T(8,128)(2,1)S(1)}, bf16[32,384]{1,0:T(8,128)(2,1)S(1)}, u32[]{:S(2)}, u32[]{:S(2)}) collective-permute-start(bf16[32,384]{1,0:T(8,128)(2,1)S(1)} %add_parts.4.refs_0_), channel_id=1, source_target_pairs={{0,8},{8,0},{16,24},{24,16},{1,9},{9,1},{17,25},{25,17},{2,10},{10... | collective-permute-start | bytes 73736 | tf_op jit(solution)/shard_map/ppermute | solution.py:414
  26.5 4.7 %collective-permute-start.7 = (bf16[32,384]{1,0:T(8,128)(2,1)S(1)}, bf16[32,384]{1,0:T(8,128)(2,1)S(1)}, u32[]{:S(2)}, u32[]{:S(2)}) collective-permute-start(bf16[32,384]{1,0:T(8,128)(2,1)S(1)} %add_parts.4.refs_0_), channel_id=1, source_target_pairs={{0,16},{8,24},{16,0},{24,8},{1,17},{9,25},{17,1},{25,9},{2,18},{10... | collective-permute-start | bytes 73736 | tf_op jit(solution)/shard_map/ppermute | solution.py:414
  28.5 5.6 %collective-permute-start.8 = (bf16[32,384]{1,0:T(8,128)(2,1)S(1)}, bf16[32,384]{1,0:T(8,128)(2,1)S(1)}, u32[]{:S(2)}, u32[]{:S(2)}) collective-permute-start(bf16[32,384]{1,0:T(8,128)(2,1)S(1)} %add_parts.4.refs_0_), channel_id=1, source_target_pairs={{0,24},{8,16},{16,8},{24,0},{1,25},{9,17},{17,9},{25,1},{2,26},{10... | collective-permute-start | bytes 73736 | tf_op jit(solution)/shard_map/ppermute | solution.py:414
  34.2 3.9 %collective-permute-start.11 = (bf16[32,384]{1,0:T(8,128)(2,1)S(1)}, bf16[32,384]{1,0:T(8,128)(2,1)S(1)}, u32[]{:S(2)}, u32[]{:S(2)}) collective-permute-start(bf16[32,384]{1,0:T(8,128)(2,1)S(1)} %add_parts.5.refs_0_), channel_id=1, source_target_pairs={{0,1},{1,0},{2,3},{3,2},{4,5},{5,4},{6,7},{7,6},{8,9},{9,8},{10,11... | collective-permute-start | bytes 73736 | tf_op jit(solution)/shard_map/ppermute | solution.py:414

commit v16 on v14

--- a/solution.py
+++ b/solution.py
@@ -239,6 +239,12 @@
     rows = jnp.concatenate([fs[:, a * 256 + 256:a * 256 + 256 + pre.shape[1]] for a in range(3)], axis=0)
     pre[...] = jnp.dot(t1[:128], rows, preferred_element_type=F32) + b1[:128, :1]
     back[...] = jnp.dot(tb[...], stacked(cs, back.shape[1]), preferred_element_type=F32)
+
+
+def rounded(s):
+    lost = s - s.astype(BF16).astype(F32)
+    row = lax.broadcasted_iota(jnp.int32, s.shape, 0)
+    return (s + jnp.where(row == 28, pltpu.roll(lost, 1, 0), 0.0)).astype(BF16)
 
 
 def two_dots(v, w):
@@ -303,7 +309,7 @@
     row = lax.broadcasted_iota(jnp.int32, (CH, 128), 0)
     lane = lax.broadcasted_iota(jnp.int32, (CH, 128), 1)
     taps[0, 27:28] = jnp.sum(jnp.where(row == lane, bias, 0.0), axis=0, keepdims=True)
-    payload[...] = jnp.concatenate([taps[n] for n in range(3)], axis=1)
+    payload[...] = rounded(jnp.concatenate([taps[n] for n in range(3)], axis=1))
 
 
 def hidden_rim_kernel(counts, rfar, rnear, rfar_outer, rnear_outer, hidden, fs, t1o, t1d, b1, hidden_out, fr):
@@ -360,10 +366,7 @@
 
 
 def add_kernel(*refs):
-    s = summed(refs[:-1])
-    lost = s - s.astype(BF16).astype(F32)
-    row = lax.broadcasted_iota(jnp.int32, s.shape, 0)
-    refs[-1][...] = (s + jnp.where(row == 28, pltpu.roll(lost, 1, 0), 0.0)).astype(BF16)
+    refs[-1][...] = rounded(summed(refs[:-1]))
 
 
 def finish_kernel(norm, *refs):
@@ -393,13 +396,15 @@
 
 def exchange(near, far, axis, other):
     count, others = lax.axis_size(axis), lax.axis_size(other)
+    axes = tuple(name for name in ("stream", "radial", "snap") if name in (axis, other))
+    flat = (others, 1) if axes[0] == axis else (1, count)
     pairs = []
     for i in range(count):
         for j in range(others):
             end = i in (0, count - 1)
             to = (i, j ^ 1 if others % 2 == 0 else j) if end else (i - 1 + 2 * (i % 2), j)
-            pairs.append((i * others + j, to[0] * others + to[1]))
-    far = lax.ppermute(far, (axis, other), pairs)
+            pairs.append((i * flat[0] + j * flat[1], to[0] * flat[0] + to[1] * flat[1]))
+    far = lax.ppermute(far, axes, pairs)
     return lax.ppermute(near, axis, [(i, i ^ 1) for i in range(count)]), far
 
 
@@ -454,7 +459,7 @@
     xfar, xnear, t1o, tbo = lax.optimization_barrier((xfar, xnear, t1o, tbo))
     inner, outer = shape((planes + 4) * 48, Z), shape(128 + (planes + 4) * 16, Z)
     near, far = call(functools.partial(join_kernel, counts), (inner, inner), "join_strips")(xfar, xnear, f_rows, c_rows)
-    rnear, rfar = exchange(near, far, "radial", "snap")
+    rnear, rfar = exchange(near, far, "radial", "stream")
     fs, cs, pre, back = call(
         functools.partial(own_kernel, counts),
         (shape(256, wide + 4 * Z), shape(384, wide), shape(128, planes * Z, dtype=F32), shape(128, planes * Z, dtype=F32)),
@@ -464,19 +469,17 @@
     f_rows, fs = lax.optimization_barrier((f_rows, fs))
     near_outer, far_outer = call(functools.partial(join_outer_kernel, counts), (outer, outer), "join_outer")(
         xfar, xnear, f_rows, c_rows)
-    rnear_outer, rfar_outer = exchange(near_outer, far_outer, "radial", "snap")
+    rnear_outer, rfar_outer = exchange(near_outer, far_outer, "radial", "stream")
     hidden, payload = call(
         functools.partial(rim_kernel, counts),
-        (shape(planes, 128, Z), shape(32, 384, dtype=F32)),
+        (shape(planes, 128, Z), shape(32, 384)),
         "gradients",
         (pltpu.VMEM((128, wide), BF16), pltpu.VMEM((256, wide), BF16), pltpu.VMEM((3, 32, 128), F32)),
         flops=2_000_000_000,
     )(rfar, rnear, fs, cs, pre, back, t1r, tbr, *const(e1t, e2t, rep1, rep2), *const(y1, y2, dtype=F32))
 
-    steps = rounds("radial", 2) + rounds("stream", 4) + rounds("snap", 2)
+    steps = rounds("radial", 4) + rounds("stream", 4) + rounds("snap", 2)
     arrived = swap(payload, *steps[0])
-    payload = add(payload, arrived)
-    arrived = swap(payload, *steps[1])
     hidden = call(
         functools.partial(hidden_rim_kernel, counts),
         shape(planes + 4, 192, Z),
@@ -485,13 +488,13 @@
         flops=1_000_000_000,
     )(rfar, rnear, rfar_outer, rnear_outer, hidden, fs, t1o, t1d, b1)
     payload, hidden = lax.optimization_barrier((add(payload, arrived), hidden))
+    arrived = swap(payload, *steps[1])
+    payload = add(payload, arrived)
     arrived = swap(payload, *steps[2])
-    payload = add(payload, arrived)
-    arrived = swap(payload, *steps[3])
     closure = call(
         closure_kernel, shape(*cotangent.shape), "closure", (pltpu.VMEM((640, wide), BF16),), flops=1_000_000_000
     )(hidden, t2, b2)
-    for step in steps[4:]:
+    for step in steps[3:]:
         payload = add(payload, arrived)
         arrived = swap(payload, *step)
 

time: 36.5 us -> 35.7 us (0.978)
  waiting for transfers between devices: 8.32 us -> 6.68 us
  starting transfers between devices: 15 us -> 15.9 us
    ppermute x6 -> x7, waiting for transfers between devices: 7.08 us -> 5.7 us  [swap(): lax.ppermute(v, axis, [(i, i ^ mask) for i in range(count)])]
    ppermute x6 -> x7, starting transfers between devices: 7.1 us -> 7.68 us  [swap(): lax.ppermute(v, axis, [(i, i ^ mask) for i in range(count)])]
    ppermute x3, starting transfers between devices: 3.63 us -> 4.02 us  [exchange(): far = lax.ppermute(far, axes, pairs)]
  transfers between devices with their start and end apart: 12 -> 13, of which waited for: 8 -> 8; matrix products, arithmetic and copies ran while one was open for 0% -> 0% of each run, Pallas kernels for 27% -> 28%
where the time goes in v16:
time: 35.7 us; the launch traced here: 35.5 us
  starting transfers between devices  15.9 us (45%)
  Pallas kernels  11.1 us (31%)
  waiting for transfers between devices  6.68 us (19%)
  other arithmetic  1.02 us (3%)
  between operations  0.82 us (2%)
    ppermute x7, starting transfers between devices, swap(): lax.ppermute(v, axis, [(i, i ^ mask) for i in range(count)])  7.68 us
    ppermute x7, waiting for transfers between devices, swap(): lax.ppermute(v, axis, [(i, i ^ mask) for i in range(count)])  5.7 us
    ppermute x3, starting transfers between devices, exchange(): return (lax.ppermute(near, axis, [(i, i ^ 1) for i in range(count)]), far)  4.15 us
    ppermute x3, starting transfers between devices, exchange(): far = lax.ppermute(far, axes, pairs)  4.02 us
    pallas_call x1, Pallas kernels, local(): call(functools.partial(rim_kernel, counts), (shape(planes, 128, Z), shape...  3.14 us
    pallas_call x1, Pallas kernels, local(): call(band_kernel, (shape(192, 768), shape(128, 384), shape(192, 768), sha...  2.7 us
    pallas_call x1, Pallas kernels, local(): call(closure_kernel, shape(*cotangent.shape), 'closure', (pltpu.VMEM((640...  1.56 us
    pallas_call x1, Pallas kernels, local(): call(functools.partial(hidden_rim_kernel, counts), shape(planes + 4, 192,...  1.26 us
  transfers between devices with their start and end apart: 13, of which 8 were waited for; matrix products, arithmetic and copies ran while one was open for 0% of the time, Pallas kernels for 28%

profile of v16, /device:TPU:0, one launch (start us, length us, event | category | flops | bytes accessed | tf_op | source)
XLA Modules:
  0.0 35.5 jit_solution(4260093510103200212)
XLA Ops:
  0.6 1.0 %pad_maximum_fusion.inputs = bf16[24,8,8,128]{3,2,1,0:T(8,128)(2,1)S(1)} fusion(bf16[16,8,8,128]{3,2,1,0:T(8,128)(2,1)} %bitcast.21, bf16[8,8,8,128]{3,2,1,0:T(8,128)(2,1)} %bitcast.22), kind=kLoop, calls=%fused_computation | loop fusion | flops 196608 | bytes 786432 | tf_op jit(solution)/shard_map/concatenate | solution.py:448
  1.7 0.0 copy-start
  1.7 0.0 copy-start.1
  1.7 0.0 copy-start.2
  1.7 0.0 copy-start.3
  1.7 0.1 pack_strips.1
  1.8 0.5 %collective-permute-start = (bf16[512,128]{1,0:T(8,128)(2,1)S(1)}, bf16[512,128]{1,0:T(8,128)(2,1)S(1)}, u32[]{:S(2)}, u32[]{:S(2)}) collective-permute-start(bf16[512,128]{1,0:T(8,128)(2,1)S(1)} %get-tuple-element.37), channel_id=1, source_target_pairs={{0,2},{2,0},{4,6},{6,4},{8,16},{10,18},{12,20},{14,22},{16,8},{18,... | collective-permute-start | bytes 393224 | tf_op jit(solution)/shard_map/ppermute | solution.py:407
  2.4 4.1 %collective-permute-start.1 = (bf16[512,128]{1,0:T(8,128)(2,1)S(1)}, bf16[512,128]{1,0:T(8,128)(2,1)S(1)}, u32[]{:S(2)}, u32[]{:S(2)}) collective-permute-start(bf16[512,128]{1,0:T(8,128)(2,1)S(1)} %get-tuple-element.38), channel_id=1, source_target_pairs={{0,8},{8,0},{16,24},{24,16},{1,9},{9,1},{17,25},{25,17},{2,10},{10... | collective-permute-start | bytes 393224 | tf_op jit(solution)/shard_map/ppermute | solution.py:408
  6.5 0.0 copy-done
  6.5 0.0 copy-done.1
  6.5 0.0 copy-done.2
  6.5 0.0 copy-done.3
  6.5 2.7 %band_matrices.1 = (bf16[192,768]{1,0:T(8,128)(2,1)S(1)}, bf16[128,384]{1,0:T(8,128)(2,1)S(1)}, bf16[192,768]{1,0:T(8,128)(2,1)S(1)}, bf16[128,1152]{1,0:T(8,128...) custom-call(bf16[128,27]{1,0:T(8,128)(2,1)S(1)} %bitcast.18, ...), custom_call_target="tpu_custom_call" | custom-call | flops 4000000000 | bytes 1000000 | tf_op jit(solution)/shard_map/band_matrices/pallas_call | solution.py:452
  9.2 0.0 collective-permute-done.xfar
  9.2 0.5 %collective-permute-done.1.xnear = bf16[512,128]{1,0:T(8,128)(2,1)S(1)} collective-permute-done((bf16[512,128]{1,0:T(8,128)(2,1)S(1)}, bf16[512,128]{1,0:T(8,128)(2,1)S(1)}, u32[]{:S(2)}, u32[]{:S(2)}) %collective-permute-start.1) | collective-permute-done | bytes 131104 | tf_op jit(solution)/shard_map/ppermute | solution.py:408
  9.7 0.3 join_strips.1
  10.0 1.8 %collective-permute-start.2 = (bf16[576,128]{1,0:T(8,128)(2,1)S(1)}, bf16[576,128]{1,0:T(8,128)(2,1)S(1)}, u32[]{:S(2)}, u32[]{:S(2)}) collective-permute-start(bf16[576,128]{1,0:T(8,128)(2,1)S(1)} %get-tuple-element.45), channel_id=1, source_target_pairs={{0,8},{8,0},{16,24},{24,16},{2,4},{10,12},{18,20},{26,28},{4,2},{1... | collective-permute-start | bytes 442376 | tf_op jit(solution)/shard_map/ppermute | solution.py:407
  11.8 0.0 collective-permute-start.3
  11.8 0.0 copy-start.4
  11.8 0.0 copy-start.5
  11.8 0.0 copy-start.6
  11.8 0.0 copy-start.7
  11.9 0.0 copy-start.8
  11.9 0.0 copy-start.9
  11.9 0.9 %own_rows.1 = (bf16[256,2048]{1,0:T(8,128)(2,1)S(1)}, bf16[384,1536]{1,0:T(8,128)(2,1)S(1)}, f32[128,1024]{1,0:T(8,128)S(1)}, f32[128,1024]{1,0:T(8,128)S(1)}) custom-call(bf16[512,128]{1,0:T(8,128)(2,1)S(1)} %collective-permute-done.xfar, bf16[512,128]{1,0:T(8,128)(2,1)S(1)} %collective-permute-done.1.xnear, ...), custom_call_target="tpu_custom_call" | custom-call | flops 1000000000 | bytes 1000000 | tf_op jit(solution)/shard_map/own_rows/pallas_call | solution.py:463
  12.8 0.2 join_outer.1
  13.1 1.7 %collective-permute-start.7 = (bf16[320,128]{1,0:T(8,128)(2,1)S(1)}, bf16[320,128]{1,0:T(8,128)(2,1)S(1)}, u32[]{:S(2)}, u32[]{:S(2)}) collective-permute-start(bf16[320,128]{1,0:T(8,128)(2,1)S(1)} %get-tuple-element.59), channel_id=1, source_target_pairs={{0,8},{8,0},{16,24},{24,16},{2,4},{10,12},{18,20},{26,28},{4,2},{1... | collective-permute-start | bytes 245768 | tf_op jit(solution)/shard_map/ppermute | solution.py:407
  14.7 0.0 collective-permute-start.8
  14.7 0.5 %collective-permute-done.2.rfar = bf16[576,128]{1,0:T(8,128)(2,1)S(1)} collective-permute-done((bf16[576,128]{1,0:T(8,128)(2,1)S(1)}, bf16[576,128]{1,0:T(8,128)(2,1)S(1)}, u32[]{:S(2)}, u32[]{:S(2)}) %collective-permute-start.2) | collective-permute-done | bytes 147488 | tf_op jit(solution)/shard_map/ppermute | solution.py:407
  15.2 0.0 collective-permute-done.3.rnear
  15.2 0.0 copy-done.4
  15.2 0.0 copy-done.5
  15.2 0.0 copy-done.6
  15.2 0.0 copy-done.7
  15.3 0.0 copy-done.8
  15.3 0.0 copy-done.9
  15.3 3.1 %gradients.1 = (bf16[8,128,128]{2,1,0:T(8,128)(2,1)S(1)}, bf16[32,384]{1,0:T(8,128)(2,1)S(1)}) custom-call(bf16[576,128]{1,0:T(8,128)(2,1)S(1)} %collective-permute-done.2.rfar, bf16[576,128]{1,0:T(8,128)(2,1)S(1)} %collective-permute-done.3.rnear, bf16[256,2048]{1,0:T(8,128)(2,1)S(1)} %get-tuple-element.51.fs, bf16[384,1536]{1,0:T(8,128)(2,1)S(1)} %get-tuple-element.52.cs, ...), custom_call_target="tpu_custom_call" | custom-call | flops 2000000000 | bytes 1000000 | tf_op jit(solution)/shard_map/gradients/pallas_call | solution.py:473
  18.4 0.1 collective-permute-start.4
  18.5 1.0 %collective-permute-start.5 = (bf16[32,384]{1,0:T(8,128)(2,1)S(1)}, bf16[32,384]{1,0:T(8,128)(2,1)S(1)}, u32[]{:S(2)}, u32[]{:S(2)}) collective-permute-start(bf16[32,384]{1,0:T(8,128)(2,1)S(1)} %get-tuple-element.57.refs_0_), channel_id=1, source_target_pairs={{0,4},{2,6},{4,0},{6,2},{1,5},{3,7},{5,1},{7,3},{8,12},{10,14},{12... | collective-permute-start | bytes 73736 | tf_op jit(solution)/shard_map/ppermute | solution.py:413
  19.5 0.9 %collective-permute-start.6 = (bf16[32,384]{1,0:T(8,128)(2,1)S(1)}, bf16[32,384]{1,0:T(8,128)(2,1)S(1)}, u32[]{:S(2)}, u32[]{:S(2)}) collective-permute-start(bf16[32,384]{1,0:T(8,128)(2,1)S(1)} %get-tuple-element.57.refs_0_), channel_id=1, source_target_pairs={{0,6},{2,4},{4,2},{6,0},{1,7},{3,5},{5,3},{7,1},{8,14},{10,12},{12... | collective-permute-start | bytes 73736 | tf_op jit(solution)/shard_map/ppermute | solution.py:413
  20.4 0.0 collective-permute-done.7.rfar_outer
  20.4 0.0 collective-permute-done.8.rnear_outer
  20.4 1.3 %hidden_rim.1.hidden = bf16[12,192,128]{2,1,0:T(8,128)(2,1)S(1)} custom-call(bf16[576,128]{1,0:T(8,128)(2,1)S(1)} %collective-permute-done.2.rfar, bf16[576,128]{1,0:T(8,128)(2,1)S(1)} %collective-permute-done.3.rnear, bf16[320,128]{1,0:T(8,128)(2,1)S(1)} %collective-permute-done.7.rfar_outer, bf16[320,128]{1,0:T(8,128)(2,1)S(1)} %collective-permute-done.8.rnear_outer, ...), custom_call_target="tpu_custom_call" | custom-call | flops 1000000000 | bytes 1000000 | tf_op jit(solution)/shard_map/hidden_rim/pallas_call | solution.py:483
  21.6 0.0 collective-permute-done.4.refs_1_
  21.6 0.7 %collective-permute-done.5.refs_2_ = bf16[32,384]{1,0:T(8,128)(2,1)S(1)} collective-permute-done((bf16[32,384]{1,0:T(8,128)(2,1)S(1)}, bf16[32,384]{1,0:T(8,128)(2,1)S(1)}, u32[]{:S(2)}, u32[]{:S(2)}) %collective-permute-start.5) | collective-permute-done | bytes 24608 | tf_op jit(solution)/shard_map/ppermute | solution.py:413
  22.4 0.4 %collective-permute-done.6.refs_3_ = bf16[32,384]{1,0:T(8,128)(2,1)S(1)} collective-permute-done((bf16[32,384]{1,0:T(8,128)(2,1)S(1)}, bf16[32,384]{1,0:T(8,128)(2,1)S(1)}, u32[]{:S(2)}, u32[]{:S(2)}) %collective-permute-start.6) | collective-permute-done | bytes 24608 | tf_op jit(solution)/shard_map/ppermute | solution.py:413
  22.8 2.0 %collective-permute-start.10 = (bf16[32,384]{1,0:T(8,128)(2,1)S(1)}, bf16[32,384]{1,0:T(8,128)(2,1)S(1)}, u32[]{:S(2)}, u32[]{:S(2)}) collective-permute-start(bf16[32,384]{1,0:T(8,128)(2,1)S(1)} %add_parts.2.refs_0_), channel_id=1, source_target_pairs={{0,16},{8,24},{16,0},{24,8},{1,17},{9,25},{17,1},{25,9},{2,18},{10... | collective-permute-start | bytes 73736 | tf_op jit(solution)/shard_map/ppermute | solution.py:413
  24.8 2.1 %collective-permute-start.11 = (bf16[32,384]{1,0:T(8,128)(2,1)S(1)}, bf16[32,384]{1,0:T(8,128)(2,1)S(1)}, u32[]{:S(2)}, u32[]{:S(2)}) collective-permute-start(bf16[32,384]{1,0:T(8,128)(2,1)S(1)} %add_parts.2.refs_0_), channel_id=1, source_target_pairs={{0,24},{8,16},{16,8},{24,0},{1,25},{9,17},{17,9},{25,1},{2,26},{10... | collective-permute-start | bytes 73736 | tf_op jit(solution)/shard_map/ppermute | solution.py:413
  27.0 0.0 collective-permute-start.9
  27.0 0.6 %collective-permute-done.10.refs_2_ = bf16[32,384]{1,0:T(8,128)(2,1)S(1)} collective-permute-done((bf16[32,384]{1,0:T(8,128)(2,1)S(1)}, bf16[32,384]{1,0:T(8,128)(2,1)S(1)}, u32[]{:S(2)}, u32[]{:S(2)}) %collective-permute-start.10) | collective-permute-done | bytes 24608 | tf_op jit(solution)/shard_map/ppermute | solution.py:413
  27.6 2.9 %collective-permute-done.11.refs_3_ = bf16[32,384]{1,0:T(8,128)(2,1)S(1)} collective-permute-done((bf16[32,384]{1,0:T(8,128)(2,1)S(1)}, bf16[32,384]{1,0:T(8,128)(2,1)S(1)}, u32[]{:S(2)}, u32[]{:S(2)}) %collective-permute-start.11) | collective-permute-done | bytes 24608 | tf_op jit(solution)/shard_map/ppermute | solution.py:413
  30.4 0.3 collective-permute-done.9.refs_1_
  30.8 1.6 %collective-permute-start.12 = (bf16[32,384]{1,0:T(8,128)(2,1)S(1)}, bf16[32,384]{1,0:T(8,128)(2,1)S(1)}, u32[]{:S(2)}, u32[]{:S(2)}) collective-permute-start(bf16[32,384]{1,0:T(8,128)(2,1)S(1)} %add_parts.3.refs_0_), channel_id=1, source_target_pairs={{0,1},{1,0},{2,3},{3,2},{4,5},{5,4},{6,7},{7,6},{8,9},{9,8},{10,11... | collective-permute-start | bytes 73736 | tf_op jit(solution)/shard_map/ppermute | solution.py:413
  32.4 1.6 %closure.1 = bf16[1,16,8,8,128]{4,3,2,1,0:T(8,128)(2,1)} custom-call(bf16[12,192,128]{2,1,0:T(8,128)(2,1)S(1)} %hidden_rim.1.hidden, bf16[128,1920]{1,0:T(8,128)(2,1)S(1)} %get-tuple-element.64.t2, f32[128,128]{1,0:T(8,128)S(1)} %get-tuple-element.65.b2), custom_call_target="tpu_custom_call" | custom-call | flops 1000000000 | bytes 1000000 | tf_op jit(solution)/shard_map/closure/pallas_call | solution.py:494
  33.9 0.8 %collective-permute-done.12.refs_1_ = bf16[32,384]{1,0:T(8,128)(2,1)S(1)} collective-permute-done((bf16[32,384]{1,0:T(8,128)(2,1)S(1)}, bf16[32,384]{1,0:T(8,128)(2,1)S(1)}, u32[]{:S(2)}, u32[]{:S(2)}) %collective-permute-start.12) | collective-permute-done | bytes 24608 | tf_op jit(solution)/shard_map/ppermute | solution.py:413
  34.7 0.8 %finish.1 = (f32[128,27]{1,0:T(8,128)}, f32[256,27]{1,0:T(8,128)}, f32[1,16]{1,0:T(1,128)}) custom-call(bf16[32,384]{1,0:T(8,128)(2,1)S(1)} %add_parts.3.refs_0_, bf16[32,384]{1,0:T(8,128)(2,1)S(1)} %collective-permute-done.12.refs_1_), custom_call_target="tpu_custom_call" | custom-call | flops 10000000 | bytes 1000000 | tf_op jit(solution)/shard_map/finish/pallas_call | solution.py:505
  (2 shorter events, 0.0 us)
Async XLA Ops:
  1.7 4.8 %copy-start = (bf16[27,16,16]{0,2,1:T(8,128)(2,1)S(1)}, bf16[27,16,16]{0,2,1:T(8,128)(2,1)}, u32[]{:S(2)}) copy-start(bf16[27,16,16]{0,2,1:T(8,128)(2,1)} %param.15) | copy-start | bytes 41476
  1.7 4.8 %copy-start.1 = (bf16[27,16,8]{0,2,1:T(8,128)(2,1)S(1)}, bf16[27,16,8]{0,2,1:T(8,128)(2,1)}, u32[]{:S(2)}) copy-start(bf16[27,16,8]{0,2,1:T(8,128)(2,1)} %param.13) | copy-start | bytes 20740
  1.7 4.8 %copy-start.2 = (f32[16]{0:T(128)S(1)}, f32[16]{0:T(128)}, u32[]{:S(2)}) copy-start(f32[16]{0:T(128)} %param.14) | copy-start | bytes 196
  1.7 4.8 %copy-start.3 = (f32[16]{0:T(128)S(1)}, f32[16]{0:T(128)}, u32[]{:S(2)}) copy-start(f32[16]{0:T(128)} %param.16) | copy-start | bytes 196
  1.8 7.4 %collective-permute-start = (bf16[512,128]{1,0:T(8,128)(2,1)S(1)}, bf16[512,128]{1,0:T(8,128)(2,1)S(1)}, u32[]{:S(2)}, u32[]{:S(2)}) collective-permute-start(bf16[512,128]{1,0:T(8,128)(2,1)S(1)} %get-tuple-element.37), channel_id=1, source_target_pairs={{0,2},{2,0},{4,6},{6,4},{8,16},{10,18},{12,20},{14,22},{16,8},{18,... | collective-permute-start | bytes 393224 | tf_op jit(solution)/shard_map/ppermute | solution.py:407
  2.4 7.4 %collective-permute-start.1 = (bf16[512,128]{1,0:T(8,128)(2,1)S(1)}, bf16[512,128]{1,0:T(8,128)(2,1)S(1)}, u32[]{:S(2)}, u32[]{:S(2)}) collective-permute-start(bf16[512,128]{1,0:T(8,128)(2,1)S(1)} %get-tuple-element.38), channel_id=1, source_target_pairs={{0,8},{8,0},{16,24},{24,16},{1,9},{9,1},{17,25},{25,17},{2,10},{10... | collective-permute-start | bytes 393224 | tf_op jit(solution)/shard_map/ppermute | solution.py:408
  10.0 5.2 %collective-permute-start.2 = (bf16[576,128]{1,0:T(8,128)(2,1)S(1)}, bf16[576,128]{1,0:T(8,128)(2,1)S(1)}, u32[]{:S(2)}, u32[]{:S(2)}) collective-permute-start(bf16[576,128]{1,0:T(8,128)(2,1)S(1)} %get-tuple-element.45), channel_id=1, source_target_pairs={{0,8},{8,0},{16,24},{24,16},{2,4},{10,12},{18,20},{26,28},{4,2},{1... | collective-permute-start | bytes 442376 | tf_op jit(solution)/shard_map/ppermute | solution.py:407
  11.8 3.4 %collective-permute-start.3 = (bf16[576,128]{1,0:T(8,128)(2,1)S(1)}, bf16[576,128]{1,0:T(8,128)(2,1)S(1)}, u32[]{:S(2)}, u32[]{:S(2)}) collective-permute-start(bf16[576,128]{1,0:T(8,128)(2,1)S(1)} %get-tuple-element.46), channel_id=1, source_target_pairs={{0,2},{2,0},{4,6},{6,4},{1,3},{3,1},{5,7},{7,5},{8,10},{10,8},{12,... | collective-permute-start | bytes 442376 | tf_op jit(solution)/shard_map/ppermute | solution.py:408
  11.8 3.4 %copy-start.4 = (bf16[128,768]{1,0:T(8,128)(2,1)S(1)}, bf16[128,768]{1,0:T(8,128)(2,1)}, u32[]{:S(2)}) copy-start(bf16[128,768]{1,0:T(8,128)(2,1)} %constant.15.clone.rep2) | copy-start | bytes 589828
  11.8 3.4 %copy-start.5 = (bf16[640,128]{1,0:T(8,128)(2,1)S(1)}, bf16[640,128]{1,0:T(8,128)(2,1)}, u32[]{:S(2)}) copy-start(bf16[640,128]{1,0:T(8,128)(2,1)} %constant.13.clone.e2t) | copy-start | bytes 491524
  11.8 3.4 %copy-start.6 = (bf16[384,128]{1,0:T(8,128)(2,1)S(1)}, bf16[384,128]{1,0:T(8,128)(2,1)}, u32[]{:S(2)}) copy-start(bf16[384,128]{1,0:T(8,128)(2,1)} %constant.12.clone.e1t) | copy-start | bytes 294916
  11.8 3.4 %copy-start.7 = (bf16[128,384]{1,0:T(8,128)(2,1)S(1)}, bf16[128,384]{1,0:T(8,128)(2,1)}, u32[]{:S(2)}) copy-start(bf16[128,384]{1,0:T(8,128)(2,1)} %constant.14.clone.rep1) | copy-start | bytes 294916
  11.9 3.4 %copy-start.8 = (f32[1,640]{1,0:T(1,128)S(1)}, f32[1,640]{1,0:T(1,128)}, u32[]{:S(2)}) copy-start(f32[1,640]{1,0:T(1,128)} %constant.17.clone.y2) | copy-start | bytes 7684
  11.9 3.4 %copy-start.9 = (f32[1,384]{1,0:T(1,128)S(1)}, f32[1,384]{1,0:T(1,128)}, u32[]{:S(2)}) copy-start(f32[1,384]{1,0:T(1,128)} %constant.16.clone.y1) | copy-start | bytes 4612
  13.1 7.3 %collective-permute-start.7 = (bf16[320,128]{1,0:T(8,128)(2,1)S(1)}, bf16[320,128]{1,0:T(8,128)(2,1)S(1)}, u32[]{:S(2)}, u32[]{:S(2)}) collective-permute-start(bf16[320,128]{1,0:T(8,128)(2,1)S(1)} %get-tuple-element.59), channel_id=1, source_target_pairs={{0,8},{8,0},{16,24},{24,16},{2,4},{10,12},{18,20},{26,28},{4,2},{1... | collective-permute-start | bytes 245768 | tf_op jit(solution)/shard_map/ppermute | solution.py:407
  14.7 5.6 %collective-permute-start.8 = (bf16[320,128]{1,0:T(8,128)(2,1)S(1)}, bf16[320,128]{1,0:T(8,128)(2,1)S(1)}, u32[]{:S(2)}, u32[]{:S(2)}) collective-permute-start(bf16[320,128]{1,0:T(8,128)(2,1)S(1)} %get-tuple-element.60), channel_id=1, source_target_pairs={{0,2},{2,0},{4,6},{6,4},{1,3},{3,1},{5,7},{7,5},{8,10},{10,8},{12,... | collective-permute-start | bytes 245768 | tf_op jit(solution)/shard_map/ppermute | solution.py:408
  18.4 3.2 %collective-permute-start.4 = (bf16[32,384]{1,0:T(8,128)(2,1)S(1)}, bf16[32,384]{1,0:T(8,128)(2,1)S(1)}, u32[]{:S(2)}, u32[]{:S(2)}) collective-permute-start(bf16[32,384]{1,0:T(8,128)(2,1)S(1)} %get-tuple-element.57.refs_0_), channel_id=1, source_target_pairs={{0,2},{2,0},{4,6},{6,4},{1,3},{3,1},{5,7},{7,5},{8,10},{10,8},{12,... | collective-permute-start | bytes 73736 | tf_op jit(solution)/shard_map/ppermute | solution.py:413
  18.5 3.9 %collective-permute-start.5 = (bf16[32,384]{1,0:T(8,128)(2,1)S(1)}, bf16[32,384]{1,0:T(8,128)(2,1)S(1)}, u32[]{:S(2)}, u32[]{:S(2)}) collective-permute-start(bf16[32,384]{1,0:T(8,128)(2,1)S(1)} %get-tuple-element.57.refs_0_), channel_id=1, source_target_pairs={{0,4},{2,6},{4,0},{6,2},{1,5},{3,7},{5,1},{7,3},{8,12},{10,14},{12... | collective-permute-start | bytes 73736 | tf_op jit(solution)/shard_map/ppermute | solution.py:413
  19.5 3.3 %collective-permute-start.6 = (bf16[32,384]{1,0:T(8,128)(2,1)S(1)}, bf16[32,384]{1,0:T(8,128)(2,1)S(1)}, u32[]{:S(2)}, u32[]{:S(2)}) collective-permute-start(bf16[32,384]{1,0:T(8,128)(2,1)S(1)} %get-tuple-element.57.refs_0_), channel_id=1, source_target_pairs={{0,6},{2,4},{4,2},{6,0},{1,7},{3,5},{5,3},{7,1},{8,14},{10,12},{12... | collective-permute-start | bytes 73736 | tf_op jit(solution)/shard_map/ppermute | solution.py:413
  22.8 4.8 %collective-permute-start.10 = (bf16[32,384]{1,0:T(8,128)(2,1)S(1)}, bf16[32,384]{1,0:T(8,128)(2,1)S(1)}, u32[]{:S(2)}, u32[]{:S(2)}) collective-permute-start(bf16[32,384]{1,0:T(8,128)(2,1)S(1)} %add_parts.2.refs_0_), channel_id=1, source_target_pairs={{0,16},{8,24},{16,0},{24,8},{1,17},{9,25},{17,1},{25,9},{2,18},{10... | collective-permute-start | bytes 73736 | tf_op jit(solution)/shard_map/ppermute | solution.py:413
  24.8 5.6 %collective-permute-start.11 = (bf16[32,384]{1,0:T(8,128)(2,1)S(1)}, bf16[32,384]{1,0:T(8,128)(2,1)S(1)}, u32[]{:S(2)}, u32[]{:S(2)}) collective-permute-start(bf16[32,384]{1,0:T(8,128)(2,1)S(1)} %add_parts.2.refs_0_), channel_id=1, source_target_pairs={{0,24},{8,16},{16,8},{24,0},{1,25},{9,17},{17,9},{25,1},{2,26},{10... | collective-permute-start | bytes 73736 | tf_op jit(solution)/shard_map/ppermute | solution.py:413
  27.0 3.8 %collective-permute-start.9 = (bf16[32,384]{1,0:T(8,128)(2,1)S(1)}, bf16[32,384]{1,0:T(8,128)(2,1)S(1)}, u32[]{:S(2)}, u32[]{:S(2)}) collective-permute-start(bf16[32,384]{1,0:T(8,128)(2,1)S(1)} %add_parts.2.refs_0_), channel_id=1, source_target_pairs={{0,8},{8,0},{16,24},{24,16},{1,9},{9,1},{17,25},{25,17},{2,10},{10... | collective-permute-start | bytes 73736 | tf_op jit(solution)/shard_map/ppermute | solution.py:413
  30.8 3.9 %collective-permute-start.12 = (bf16[32,384]{1,0:T(8,128)(2,1)S(1)}, bf16[32,384]{1,0:T(8,128)(2,1)S(1)}, u32[]{:S(2)}, u32[]{:S(2)}) collective-permute-start(bf16[32,384]{1,0:T(8,128)(2,1)S(1)} %add_parts.3.refs_0_), channel_id=1, source_target_pairs={{0,1},{1,0},{2,3},{3,2},{4,5},{5,4},{6,7},{7,6},{8,9},{9,8},{10,11... | collective-permute-start | bytes 73736 | tf_op jit(solution)/shard_map/ppermute | solution.py:413

commit v17 on v16

--- a/solution.py
+++ b/solution.py
@@ -228,17 +228,39 @@
     return jnp.concatenate([ref[:, a * 256:a * 256 + lanes] for a in range(3)], axis=0)
 
 
-def own_kernel(counts, xfar, xnear, fields, cot, t1, tb, b1, fs, cs, pre, back):
-    count = fields.shape[0]
+def gelu_share(pre):
+    return 0.5 * (1.0 + lax.erf(pre * 0.7071067811865476))
+
+
+def gelu_slope(pre, share):
+    return share + pre * jnp.exp(-0.5 * pre * pre) * 0.3989422804014327
+
+
+def edges(v):
+    return jnp.concatenate([v[:32], v[96:128]], axis=0)
+
+
+def whole(edge, middle):
+    return jnp.concatenate([edge[:32], middle, edge[32:]], axis=0)
+
+
+def own_kernel(counts, xfar, xnear, fields, cot, t1, tb, b1, fs, cs, pre, back, hidden, dpre):
+    count, lanes = fields.shape[0], pre.shape[1]
     f, c = x_planes(count, fields, cot, xnear, xfar, counts[0])
     for ref, rows in ((fs, f), (cs, c)):
         for p, v in enumerate(rows):
             for n, piece in enumerate(shifted(v)):
                 ref[n * v.shape[0]:(n + 1) * v.shape[0], p * Z:(p + 1) * Z] = piece
     fs[192:] = jnp.zeros((64, fs.shape[1]), BF16)
-    rows = jnp.concatenate([fs[:, a * 256 + 256:a * 256 + 256 + pre.shape[1]] for a in range(3)], axis=0)
-    pre[...] = jnp.dot(t1[:128], rows, preferred_element_type=F32) + b1[:128, :1]
-    back[...] = jnp.dot(tb[...], stacked(cs, back.shape[1]), preferred_element_type=F32)
+    rows = jnp.concatenate([fs[:, a * 256 + 256:a * 256 + 256 + lanes] for a in range(3)], axis=0)
+    first = jnp.dot(t1[:128], rows, preferred_element_type=F32) + b1[:128, :1]
+    second = jnp.dot(tb[...], stacked(cs, lanes), preferred_element_type=F32)
+    pre[...] = edges(first)
+    back[...] = edges(second)
+    first, second = first[32:96], second[32:96]
+    share = gelu_share(first)
+    hidden[...] = (first * share).astype(BF16)
+    dpre[...] = (second * gelu_slope(first, share)).astype(BF16)
 
 
 def rounded(s):
@@ -253,11 +275,7 @@
     return jnp.dot(high, w, preferred_element_type=F32) + jnp.dot(low, w, preferred_element_type=F32)
 
 
-def gelu_share(pre):
-    return 0.5 * (1.0 + lax.erf(pre * 0.7071067811865476))
-
-
-def rim_kernel(counts, rfar, rnear, fs, cs, pre_own, back_own, t1, tb, e1t, e2t, rep1, rep2, y1, y2,
+def rim_kernel(counts, rfar, rnear, fs, cs, pre_own, back_own, hidden_own, dpre_own, t1, tb, e1t, e2t, rep1, rep2, y1, y2,
                hidden_out, payload, fr, cr, taps):
     count = hidden_out.shape[0]
     lanes = count * Z
@@ -270,13 +288,13 @@
                 ref[n * 2 * half:(n + 1) * 2 * half, p * Z:(p + 1) * Z] = piece
             at += half
         ref[6 * half:] = jnp.zeros((2 * half, ref.shape[1]), BF16)
-    pre = pre_own[...] + jnp.dot(t1[...], stacked(fr, lanes), preferred_element_type=F32)
+    pre = pre_own[...] + jnp.dot(edges(t1), stacked(fr, lanes), preferred_element_type=F32)
     share = gelu_share(pre)
-    hidden = (pre * share).astype(BF16)
+    hidden = whole((pre * share).astype(BF16), hidden_own[...])
     for x in range(count):
         hidden_out[x] = hidden[:, x * Z:(x + 1) * Z]
-    back = back_own[...] + jnp.dot(tb[...], stacked(cr, lanes), preferred_element_type=F32)
-    dpre = (back * (share + pre * jnp.exp(-0.5 * pre * pre) * 0.3989422804014327)).astype(BF16)
+    back = back_own[...] + jnp.dot(edges(tb), stacked(cr, lanes), preferred_element_type=F32)
+    dpre = whole((back * gelu_slope(pre, share)).astype(BF16), dpre_own[...])
     over_lanes = (((1,), (1,)), ((), ()))
     ones, twos = [], []
     for a in range(3):
@@ -460,9 +478,10 @@
     inner, outer = shape((planes + 4) * 48, Z), shape(128 + (planes + 4) * 16, Z)
     near, far = call(functools.partial(join_kernel, counts), (inner, inner), "join_strips")(xfar, xnear, f_rows, c_rows)
     rnear, rfar = exchange(near, far, "radial", "stream")
-    fs, cs, pre, back = call(
+    half, half_f32 = shape(64, planes * Z), shape(64, planes * Z, dtype=F32)
+    fs, cs, pre, back, hidden, dpre = call(
         functools.partial(own_kernel, counts),
-        (shape(256, wide + 4 * Z), shape(384, wide), shape(128, planes * Z, dtype=F32), shape(128, planes * Z, dtype=F32)),
+        (shape(256, wide + 4 * Z), shape(384, wide), half_f32, half_f32, half, half),
         "own_rows",
         flops=1_000_000_000,
     )(xfar, xnear, f_rows, c_rows, t1o, tbo, b1)
@@ -476,7 +495,7 @@
         "gradients",
         (pltpu.VMEM((128, wide), BF16), pltpu.VMEM((256, wide), BF16), pltpu.VMEM((3, 32, 128), F32)),
         flops=2_000_000_000,
-    )(rfar, rnear, fs, cs, pre, back, t1r, tbr, *const(e1t, e2t, rep1, rep2), *const(y1, y2, dtype=F32))
+    )(rfar, rnear, fs, cs, pre, back, hidden, dpre, t1r, tbr, *const(e1t, e2t, rep1, rep2), *const(y1, y2, dtype=F32))
 
     steps = rounds("radial", 4) + rounds("stream", 4) + rounds("snap", 2)
     arrived = swap(payload, *steps[0])

time: 35.7 us -> 35.7 us (level)
  no operation moved by 1% of the time
where the time goes in v17:
time: 35.7 us; the launch traced here: 35.5 us
  starting transfers between devices  15.8 us (44%)
  Pallas kernels  11.1 us (31%)
  waiting for transfers between devices  6.71 us (19%)
  other arithmetic  1.02 us (3%)
  between operations  0.82 us (2%)
    ppermute x7, starting transfers between devices, swap(): lax.ppermute(v, axis, [(i, i ^ mask) for i in range(count)])  7.67 us
    ppermute x7, waiting for transfers between devices, swap(): lax.ppermute(v, axis, [(i, i ^ mask) for i in range(count)])  5.72 us
    ppermute x3, starting transfers between devices, exchange(): return (lax.ppermute(near, axis, [(i, i ^ 1) for i in range(count)]), far)  4.15 us
    ppermute x3, starting transfers between devices, exchange(): far = lax.ppermute(far, axes, pairs)  4.02 us
    pallas_call x1, Pallas kernels, local(): call(functools.partial(rim_kernel, counts), (shape(planes, 128, Z), shape...  3.13 us
    pallas_call x1, Pallas kernels, local(): call(band_kernel, (shape(192, 768), shape(128, 384), shape(192, 768), sha...  2.7 us
    pallas_call x1, Pallas kernels, local(): call(closure_kernel, shape(*cotangent.shape), 'closure', (pltpu.VMEM((640...  1.56 us
    pallas_call x1, Pallas kernels, local(): call(functools.partial(hidden_rim_kernel, counts), shape(planes + 4, 192,...  1.27 us
  transfers between devices with their start and end apart: 13, of which 8 were waited for; matrix products, arithmetic and copies ran while one was open for 0% of the time, Pallas kernels for 28%

profile of v17, /device:TPU:0, one launch (start us, length us, event | category | flops | bytes accessed | tf_op | source)
XLA Modules:
  0.0 35.5 jit_solution(2978808964301448226)
XLA Ops:
  0.6 1.0 %pad_maximum_fusion.inputs = bf16[24,8,8,128]{3,2,1,0:T(8,128)(2,1)S(1)} fusion(bf16[16,8,8,128]{3,2,1,0:T(8,128)(2,1)} %bitcast.21, bf16[8,8,8,128]{3,2,1,0:T(8,128)(2,1)} %bitcast.22), kind=kLoop, calls=%fused_computation | loop fusion | flops 196608 | bytes 786432 | tf_op jit(solution)/shard_map/concatenate | solution.py:466
  1.7 0.0 copy-start
  1.7 0.0 copy-start.1
  1.7 0.0 copy-start.2
  1.7 0.0 copy-start.3
  1.7 0.1 pack_strips.1
  1.8 0.5 %collective-permute-start = (bf16[512,128]{1,0:T(8,128)(2,1)S(1)}, bf16[512,128]{1,0:T(8,128)(2,1)S(1)}, u32[]{:S(2)}, u32[]{:S(2)}) collective-permute-start(bf16[512,128]{1,0:T(8,128)(2,1)S(1)} %get-tuple-element.39), channel_id=1, source_target_pairs={{0,2},{2,0},{4,6},{6,4},{8,16},{10,18},{12,20},{14,22},{16,8},{18,... | collective-permute-start | bytes 393224 | tf_op jit(solution)/shard_map/ppermute | solution.py:425
  2.4 4.1 %collective-permute-start.1 = (bf16[512,128]{1,0:T(8,128)(2,1)S(1)}, bf16[512,128]{1,0:T(8,128)(2,1)S(1)}, u32[]{:S(2)}, u32[]{:S(2)}) collective-permute-start(bf16[512,128]{1,0:T(8,128)(2,1)S(1)} %get-tuple-element.40), channel_id=1, source_target_pairs={{0,8},{8,0},{16,24},{24,16},{1,9},{9,1},{17,25},{25,17},{2,10},{10... | collective-permute-start | bytes 393224 | tf_op jit(solution)/shard_map/ppermute | solution.py:426
  6.5 0.0 copy-done
  6.5 0.0 copy-done.1
  6.5 0.0 copy-done.2
  6.5 0.0 copy-done.3
  6.5 2.7 %band_matrices.1 = (bf16[192,768]{1,0:T(8,128)(2,1)S(1)}, bf16[128,384]{1,0:T(8,128)(2,1)S(1)}, bf16[192,768]{1,0:T(8,128)(2,1)S(1)}, bf16[128,1152]{1,0:T(8,128...) custom-call(bf16[128,27]{1,0:T(8,128)(2,1)S(1)} %bitcast.18, ...), custom_call_target="tpu_custom_call" | custom-call | flops 4000000000 | bytes 1000000 | tf_op jit(solution)/shard_map/band_matrices/pallas_call | solution.py:470
  9.2 0.0 collective-permute-done.xfar
  9.2 0.5 %collective-permute-done.1.xnear = bf16[512,128]{1,0:T(8,128)(2,1)S(1)} collective-permute-done((bf16[512,128]{1,0:T(8,128)(2,1)S(1)}, bf16[512,128]{1,0:T(8,128)(2,1)S(1)}, u32[]{:S(2)}, u32[]{:S(2)}) %collective-permute-start.1) | collective-permute-done | bytes 131104 | tf_op jit(solution)/shard_map/ppermute | solution.py:426
  9.7 0.3 join_strips.1
  10.0 1.8 %collective-permute-start.2 = (bf16[576,128]{1,0:T(8,128)(2,1)S(1)}, bf16[576,128]{1,0:T(8,128)(2,1)S(1)}, u32[]{:S(2)}, u32[]{:S(2)}) collective-permute-start(bf16[576,128]{1,0:T(8,128)(2,1)S(1)} %get-tuple-element.47), channel_id=1, source_target_pairs={{0,8},{8,0},{16,24},{24,16},{2,4},{10,12},{18,20},{26,28},{4,2},{1... | collective-permute-start | bytes 442376 | tf_op jit(solution)/shard_map/ppermute | solution.py:425
  11.8 0.0 collective-permute-start.3
  11.8 0.0 copy-start.4
  11.8 0.0 copy-start.5
  11.8 0.0 copy-start.6
  11.8 0.0 copy-start.7
  11.9 0.0 copy-start.8
  11.9 0.0 copy-start.9
  11.9 0.9 %own_rows.1 = (bf16[256,2048]{1,0:T(8,128)(2,1)S(1)}, bf16[384,1536]{1,0:T(8,128)(2,1)S(1)}, f32[64,1024]{1,0:T(8,128)S(1)}, f32[64,1024]{1,0:T(8,128)S(1)}, bf1...) custom-call(bf16[512,128]{1,0:T(8,128)(2,1)S(1)} %collective-permute-done.xfar, ...), custom_call_target="tpu_custom_call" | custom-call | flops 1000000000 | bytes 1000000 | tf_op jit(solution)/shard_map/own_rows/pallas_call | solution.py:482
  12.8 0.2 join_outer.1
  13.0 1.7 %collective-permute-start.7 = (bf16[320,128]{1,0:T(8,128)(2,1)S(1)}, bf16[320,128]{1,0:T(8,128)(2,1)S(1)}, u32[]{:S(2)}, u32[]{:S(2)}) collective-permute-start(bf16[320,128]{1,0:T(8,128)(2,1)S(1)} %get-tuple-element.63), channel_id=1, source_target_pairs={{0,8},{8,0},{16,24},{24,16},{2,4},{10,12},{18,20},{26,28},{4,2},{1... | collective-permute-start | bytes 245768 | tf_op jit(solution)/shard_map/ppermute | solution.py:425
  14.7 0.0 collective-permute-start.8
  14.7 0.5 %collective-permute-done.2.rfar = bf16[576,128]{1,0:T(8,128)(2,1)S(1)} collective-permute-done((bf16[576,128]{1,0:T(8,128)(2,1)S(1)}, bf16[576,128]{1,0:T(8,128)(2,1)S(1)}, u32[]{:S(2)}, u32[]{:S(2)}) %collective-permute-start.2) | collective-permute-done | bytes 147488 | tf_op jit(solution)/shard_map/ppermute | solution.py:425
  15.2 0.0 collective-permute-done.3.rnear
  15.2 0.0 copy-done.4
  15.2 0.0 copy-done.5
  15.2 0.0 copy-done.6
  15.2 0.0 copy-done.7
  15.3 0.0 copy-done.8
  15.3 0.0 copy-done.9
  15.3 3.1 %gradients.1 = (bf16[8,128,128]{2,1,0:T(8,128)(2,1)S(1)}, bf16[32,384]{1,0:T(8,128)(2,1)S(1)}) custom-call(bf16[576,128]{1,0:T(8,128)(2,1)S(1)} %collective-permute-done.2.rfar, bf16[576,128]{1,0:T(8,128)(2,1)S(1)} %collective-permute-done.3.rnear, bf16[256,2048]{1,0:T(8,128)(2,1)S(1)} %get-tuple-element.53.fs, bf16[384,1536]{1,0:T(8,128)(2,1)S(1)} %get-tuple-element.54.cs, ...), custom_call_target="tpu_custom_call" | custom-call | flops 2000000000 | bytes 1000000 | tf_op jit(solution)/shard_map/gradients/pallas_call | solution.py:492
  18.4 0.1 collective-permute-start.4
  18.5 1.0 %collective-permute-start.5 = (bf16[32,384]{1,0:T(8,128)(2,1)S(1)}, bf16[32,384]{1,0:T(8,128)(2,1)S(1)}, u32[]{:S(2)}, u32[]{:S(2)}) collective-permute-start(bf16[32,384]{1,0:T(8,128)(2,1)S(1)} %get-tuple-element.61.refs_0_), channel_id=1, source_target_pairs={{0,4},{2,6},{4,0},{6,2},{1,5},{3,7},{5,1},{7,3},{8,12},{10,14},{12... | collective-permute-start | bytes 73736 | tf_op jit(solution)/shard_map/ppermute | solution.py:431
  19.5 0.8 %collective-permute-start.6 = (bf16[32,384]{1,0:T(8,128)(2,1)S(1)}, bf16[32,384]{1,0:T(8,128)(2,1)S(1)}, u32[]{:S(2)}, u32[]{:S(2)}) collective-permute-start(bf16[32,384]{1,0:T(8,128)(2,1)S(1)} %get-tuple-element.61.refs_0_), channel_id=1, source_target_pairs={{0,6},{2,4},{4,2},{6,0},{1,7},{3,5},{5,3},{7,1},{8,14},{10,12},{12... | collective-permute-start | bytes 73736 | tf_op jit(solution)/shard_map/ppermute | solution.py:431
  20.3 0.0 collective-permute-done.7.rfar_outer
  20.4 0.0 collective-permute-done.8.rnear_outer
  20.4 1.3 %hidden_rim.1.hidden = bf16[12,192,128]{2,1,0:T(8,128)(2,1)S(1)} custom-call(bf16[576,128]{1,0:T(8,128)(2,1)S(1)} %collective-permute-done.2.rfar, bf16[576,128]{1,0:T(8,128)(2,1)S(1)} %collective-permute-done.3.rnear, bf16[320,128]{1,0:T(8,128)(2,1)S(1)} %collective-permute-done.7.rfar_outer, bf16[320,128]{1,0:T(8,128)(2,1)S(1)} %collective-permute-done.8.rnear_outer, ...), custom_call_target="tpu_custom_call" | custom-call | flops 1000000000 | bytes 1000000 | tf_op jit(solution)/shard_map/hidden_rim/pallas_call | solution.py:502
  21.6 0.0 collective-permute-done.4.refs_1_
  21.6 0.7 %collective-permute-done.5.refs_2_ = bf16[32,384]{1,0:T(8,128)(2,1)S(1)} collective-permute-done((bf16[32,384]{1,0:T(8,128)(2,1)S(1)}, bf16[32,384]{1,0:T(8,128)(2,1)S(1)}, u32[]{:S(2)}, u32[]{:S(2)}) %collective-permute-start.5) | collective-permute-done | bytes 24608 | tf_op jit(solution)/shard_map/ppermute | solution.py:431
  22.4 0.4 %collective-permute-done.6.refs_3_ = bf16[32,384]{1,0:T(8,128)(2,1)S(1)} collective-permute-done((bf16[32,384]{1,0:T(8,128)(2,1)S(1)}, bf16[32,384]{1,0:T(8,128)(2,1)S(1)}, u32[]{:S(2)}, u32[]{:S(2)}) %collective-permute-start.6) | collective-permute-done | bytes 24608 | tf_op jit(solution)/shard_map/ppermute | solution.py:431
  22.8 2.0 %collective-permute-start.10 = (bf16[32,384]{1,0:T(8,128)(2,1)S(1)}, bf16[32,384]{1,0:T(8,128)(2,1)S(1)}, u32[]{:S(2)}, u32[]{:S(2)}) collective-permute-start(bf16[32,384]{1,0:T(8,128)(2,1)S(1)} %add_parts.2.refs_0_), channel_id=1, source_target_pairs={{0,16},{8,24},{16,0},{24,8},{1,17},{9,25},{17,1},{25,9},{2,18},{10... | collective-permute-start | bytes 73736 | tf_op jit(solution)/shard_map/ppermute | solution.py:431
  24.8 2.1 %collective-permute-start.11 = (bf16[32,384]{1,0:T(8,128)(2,1)S(1)}, bf16[32,384]{1,0:T(8,128)(2,1)S(1)}, u32[]{:S(2)}, u32[]{:S(2)}) collective-permute-start(bf16[32,384]{1,0:T(8,128)(2,1)S(1)} %add_parts.2.refs_0_), channel_id=1, source_target_pairs={{0,24},{8,16},{16,8},{24,0},{1,25},{9,17},{17,9},{25,1},{2,26},{10... | collective-permute-start | bytes 73736 | tf_op jit(solution)/shard_map/ppermute | solution.py:431
  27.0 0.0 collective-permute-start.9
  27.0 0.6 %collective-permute-done.10.refs_2_ = bf16[32,384]{1,0:T(8,128)(2,1)S(1)} collective-permute-done((bf16[32,384]{1,0:T(8,128)(2,1)S(1)}, bf16[32,384]{1,0:T(8,128)(2,1)S(1)}, u32[]{:S(2)}, u32[]{:S(2)}) %collective-permute-start.10) | collective-permute-done | bytes 24608 | tf_op jit(solution)/shard_map/ppermute | solution.py:431
  27.6 2.9 %collective-permute-done.11.refs_3_ = bf16[32,384]{1,0:T(8,128)(2,1)S(1)} collective-permute-done((bf16[32,384]{1,0:T(8,128)(2,1)S(1)}, bf16[32,384]{1,0:T(8,128)(2,1)S(1)}, u32[]{:S(2)}, u32[]{:S(2)}) %collective-permute-start.11) | collective-permute-done | bytes 24608 | tf_op jit(solution)/shard_map/ppermute | solution.py:431
  30.4 0.3 collective-permute-done.9.refs_1_
  30.8 1.5 %collective-permute-start.12 = (bf16[32,384]{1,0:T(8,128)(2,1)S(1)}, bf16[32,384]{1,0:T(8,128)(2,1)S(1)}, u32[]{:S(2)}, u32[]{:S(2)}) collective-permute-start(bf16[32,384]{1,0:T(8,128)(2,1)S(1)} %add_parts.3.refs_0_), channel_id=1, source_target_pairs={{0,1},{1,0},{2,3},{3,2},{4,5},{5,4},{6,7},{7,6},{8,9},{9,8},{10,11... | collective-permute-start | bytes 73736 | tf_op jit(solution)/shard_map/ppermute | solution.py:431
  32.4 1.6 %closure.1 = bf16[1,16,8,8,128]{4,3,2,1,0:T(8,128)(2,1)} custom-call(bf16[12,192,128]{2,1,0:T(8,128)(2,1)S(1)} %hidden_rim.1.hidden, bf16[128,1920]{1,0:T(8,128)(2,1)S(1)} %get-tuple-element.68.t2, f32[128,128]{1,0:T(8,128)S(1)} %get-tuple-element.69.b2), custom_call_target="tpu_custom_call" | custom-call | flops 1000000000 | bytes 1000000 | tf_op jit(solution)/shard_map/closure/pallas_call | solution.py:513
  33.9 0.8 %collective-permute-done.12.refs_1_ = bf16[32,384]{1,0:T(8,128)(2,1)S(1)} collective-permute-done((bf16[32,384]{1,0:T(8,128)(2,1)S(1)}, bf16[32,384]{1,0:T(8,128)(2,1)S(1)}, u32[]{:S(2)}, u32[]{:S(2)}) %collective-permute-start.12) | collective-permute-done | bytes 24608 | tf_op jit(solution)/shard_map/ppermute | solution.py:431
  34.7 0.8 %finish.1 = (f32[128,27]{1,0:T(8,128)}, f32[256,27]{1,0:T(8,128)}, f32[1,16]{1,0:T(1,128)}) custom-call(bf16[32,384]{1,0:T(8,128)(2,1)S(1)} %add_parts.3.refs_0_, bf16[32,384]{1,0:T(8,128)(2,1)S(1)} %collective-permute-done.12.refs_1_), custom_call_target="tpu_custom_call" | custom-call | flops 10000000 | bytes 1000000 | tf_op jit(solution)/shard_map/finish/pallas_call | solution.py:524
  (2 shorter events, 0.0 us)
Async XLA Ops:
  1.7 4.8 %copy-start = (bf16[27,16,16]{0,2,1:T(8,128)(2,1)S(1)}, bf16[27,16,16]{0,2,1:T(8,128)(2,1)}, u32[]{:S(2)}) copy-start(bf16[27,16,16]{0,2,1:T(8,128)(2,1)} %param.15) | copy-start | bytes 41476
  1.7 4.8 %copy-start.1 = (bf16[27,16,8]{0,2,1:T(8,128)(2,1)S(1)}, bf16[27,16,8]{0,2,1:T(8,128)(2,1)}, u32[]{:S(2)}) copy-start(bf16[27,16,8]{0,2,1:T(8,128)(2,1)} %param.13) | copy-start | bytes 20740
  1.7 4.8 %copy-start.2 = (f32[16]{0:T(128)S(1)}, f32[16]{0:T(128)}, u32[]{:S(2)}) copy-start(f32[16]{0:T(128)} %param.14) | copy-start | bytes 196
  1.7 4.8 %copy-start.3 = (f32[16]{0:T(128)S(1)}, f32[16]{0:T(128)}, u32[]{:S(2)}) copy-start(f32[16]{0:T(128)} %param.16) | copy-start | bytes 196
  1.8 7.4 %collective-permute-start = (bf16[512,128]{1,0:T(8,128)(2,1)S(1)}, bf16[512,128]{1,0:T(8,128)(2,1)S(1)}, u32[]{:S(2)}, u32[]{:S(2)}) collective-permute-start(bf16[512,128]{1,0:T(8,128)(2,1)S(1)} %get-tuple-element.39), channel_id=1, source_target_pairs={{0,2},{2,0},{4,6},{6,4},{8,16},{10,18},{12,20},{14,22},{16,8},{18,... | collective-permute-start | bytes 393224 | tf_op jit(solution)/shard_map/ppermute | solution.py:425
  2.4 7.4 %collective-permute-start.1 = (bf16[512,128]{1,0:T(8,128)(2,1)S(1)}, bf16[512,128]{1,0:T(8,128)(2,1)S(1)}, u32[]{:S(2)}, u32[]{:S(2)}) collective-permute-start(bf16[512,128]{1,0:T(8,128)(2,1)S(1)} %get-tuple-element.40), channel_id=1, source_target_pairs={{0,8},{8,0},{16,24},{24,16},{1,9},{9,1},{17,25},{25,17},{2,10},{10... | collective-permute-start | bytes 393224 | tf_op jit(solution)/shard_map/ppermute | solution.py:426
  10.0 5.2 %collective-permute-start.2 = (bf16[576,128]{1,0:T(8,128)(2,1)S(1)}, bf16[576,128]{1,0:T(8,128)(2,1)S(1)}, u32[]{:S(2)}, u32[]{:S(2)}) collective-permute-start(bf16[576,128]{1,0:T(8,128)(2,1)S(1)} %get-tuple-element.47), channel_id=1, source_target_pairs={{0,8},{8,0},{16,24},{24,16},{2,4},{10,12},{18,20},{26,28},{4,2},{1... | collective-permute-start | bytes 442376 | tf_op jit(solution)/shard_map/ppermute | solution.py:425
  11.8 3.4 %collective-permute-start.3 = (bf16[576,128]{1,0:T(8,128)(2,1)S(1)}, bf16[576,128]{1,0:T(8,128)(2,1)S(1)}, u32[]{:S(2)}, u32[]{:S(2)}) collective-permute-start(bf16[576,128]{1,0:T(8,128)(2,1)S(1)} %get-tuple-element.48), channel_id=1, source_target_pairs={{0,2},{2,0},{4,6},{6,4},{1,3},{3,1},{5,7},{7,5},{8,10},{10,8},{12,... | collective-permute-start | bytes 442376 | tf_op jit(solution)/shard_map/ppermute | solution.py:426
  11.8 3.4 %copy-start.4 = (bf16[128,768]{1,0:T(8,128)(2,1)S(1)}, bf16[128,768]{1,0:T(8,128)(2,1)}, u32[]{:S(2)}) copy-start(bf16[128,768]{1,0:T(8,128)(2,1)} %constant.15.clone.rep2) | copy-start | bytes 589828
  11.8 3.4 %copy-start.5 = (bf16[640,128]{1,0:T(8,128)(2,1)S(1)}, bf16[640,128]{1,0:T(8,128)(2,1)}, u32[]{:S(2)}) copy-start(bf16[640,128]{1,0:T(8,128)(2,1)} %constant.13.clone.e2t) | copy-start | bytes 491524
  11.8 3.4 %copy-start.6 = (bf16[384,128]{1,0:T(8,128)(2,1)S(1)}, bf16[384,128]{1,0:T(8,128)(2,1)}, u32[]{:S(2)}) copy-start(bf16[384,128]{1,0:T(8,128)(2,1)} %constant.12.clone.e1t) | copy-start | bytes 294916
  11.8 3.4 %copy-start.7 = (bf16[128,384]{1,0:T(8,128)(2,1)S(1)}, bf16[128,384]{1,0:T(8,128)(2,1)}, u32[]{:S(2)}) copy-start(bf16[128,384]{1,0:T(8,128)(2,1)} %constant.14.clone.rep1) | copy-start | bytes 294916
  11.9 3.4 %copy-start.8 = (f32[1,640]{1,0:T(1,128)S(1)}, f32[1,640]{1,0:T(1,128)}, u32[]{:S(2)}) copy-start(f32[1,640]{1,0:T(1,128)} %constant.17.clone.y2) | copy-start | bytes 7684
  11.9 3.4 %copy-start.9 = (f32[1,384]{1,0:T(1,128)S(1)}, f32[1,384]{1,0:T(1,128)}, u32[]{:S(2)}) copy-start(f32[1,384]{1,0:T(1,128)} %constant.16.clone.y1) | copy-start | bytes 4612
  13.0 7.3 %collective-permute-start.7 = (bf16[320,128]{1,0:T(8,128)(2,1)S(1)}, bf16[320,128]{1,0:T(8,128)(2,1)S(1)}, u32[]{:S(2)}, u32[]{:S(2)}) collective-permute-start(bf16[320,128]{1,0:T(8,128)(2,1)S(1)} %get-tuple-element.63), channel_id=1, source_target_pairs={{0,8},{8,0},{16,24},{24,16},{2,4},{10,12},{18,20},{26,28},{4,2},{1... | collective-permute-start | bytes 245768 | tf_op jit(solution)/shard_map/ppermute | solution.py:425
  14.7 5.6 %collective-permute-start.8 = (bf16[320,128]{1,0:T(8,128)(2,1)S(1)}, bf16[320,128]{1,0:T(8,128)(2,1)S(1)}, u32[]{:S(2)}, u32[]{:S(2)}) collective-permute-start(bf16[320,128]{1,0:T(8,128)(2,1)S(1)} %get-tuple-element.64), channel_id=1, source_target_pairs={{0,2},{2,0},{4,6},{6,4},{1,3},{3,1},{5,7},{7,5},{8,10},{10,8},{12,... | collective-permute-start | bytes 245768 | tf_op jit(solution)/shard_map/ppermute | solution.py:426
  18.4 3.2 %collective-permute-start.4 = (bf16[32,384]{1,0:T(8,128)(2,1)S(1)}, bf16[32,384]{1,0:T(8,128)(2,1)S(1)}, u32[]{:S(2)}, u32[]{:S(2)}) collective-permute-start(bf16[32,384]{1,0:T(8,128)(2,1)S(1)} %get-tuple-element.61.refs_0_), channel_id=1, source_target_pairs={{0,2},{2,0},{4,6},{6,4},{1,3},{3,1},{5,7},{7,5},{8,10},{10,8},{12,... | collective-permute-start | bytes 73736 | tf_op jit(solution)/shard_map/ppermute | solution.py:431
  18.5 3.9 %collective-permute-start.5 = (bf16[32,384]{1,0:T(8,128)(2,1)S(1)}, bf16[32,384]{1,0:T(8,128)(2,1)S(1)}, u32[]{:S(2)}, u32[]{:S(2)}) collective-permute-start(bf16[32,384]{1,0:T(8,128)(2,1)S(1)} %get-tuple-element.61.refs_0_), channel_id=1, source_target_pairs={{0,4},{2,6},{4,0},{6,2},{1,5},{3,7},{5,1},{7,3},{8,12},{10,14},{12... | collective-permute-start | bytes 73736 | tf_op jit(solution)/shard_map/ppermute | solution.py:431
  19.5 3.3 %collective-permute-start.6 = (bf16[32,384]{1,0:T(8,128)(2,1)S(1)}, bf16[32,384]{1,0:T(8,128)(2,1)S(1)}, u32[]{:S(2)}, u32[]{:S(2)}) collective-permute-start(bf16[32,384]{1,0:T(8,128)(2,1)S(1)} %get-tuple-element.61.refs_0_), channel_id=1, source_target_pairs={{0,6},{2,4},{4,2},{6,0},{1,7},{3,5},{5,3},{7,1},{8,14},{10,12},{12... | collective-permute-start | bytes 73736 | tf_op jit(solution)/shard_map/ppermute | solution.py:431
  22.8 4.8 %collective-permute-start.10 = (bf16[32,384]{1,0:T(8,128)(2,1)S(1)}, bf16[32,384]{1,0:T(8,128)(2,1)S(1)}, u32[]{:S(2)}, u32[]{:S(2)}) collective-permute-start(bf16[32,384]{1,0:T(8,128)(2,1)S(1)} %add_parts.2.refs_0_), channel_id=1, source_target_pairs={{0,16},{8,24},{16,0},{24,8},{1,17},{9,25},{17,1},{25,9},{2,18},{10... | collective-permute-start | bytes 73736 | tf_op jit(solution)/shard_map/ppermute | solution.py:431
  24.8 5.6 %collective-permute-start.11 = (bf16[32,384]{1,0:T(8,128)(2,1)S(1)}, bf16[32,384]{1,0:T(8,128)(2,1)S(1)}, u32[]{:S(2)}, u32[]{:S(2)}) collective-permute-start(bf16[32,384]{1,0:T(8,128)(2,1)S(1)} %add_parts.2.refs_0_), channel_id=1, source_target_pairs={{0,24},{8,16},{16,8},{24,0},{1,25},{9,17},{17,9},{25,1},{2,26},{10... | collective-permute-start | bytes 73736 | tf_op jit(solution)/shard_map/ppermute | solution.py:431
  27.0 3.8 %collective-permute-start.9 = (bf16[32,384]{1,0:T(8,128)(2,1)S(1)}, bf16[32,384]{1,0:T(8,128)(2,1)S(1)}, u32[]{:S(2)}, u32[]{:S(2)}) collective-permute-start(bf16[32,384]{1,0:T(8,128)(2,1)S(1)} %add_parts.2.refs_0_), channel_id=1, source_target_pairs={{0,8},{8,0},{16,24},{24,16},{1,9},{9,1},{17,25},{25,17},{2,10},{10... | collective-permute-start | bytes 73736 | tf_op jit(solution)/shard_map/ppermute | solution.py:431
  30.8 3.9 %collective-permute-start.12 = (bf16[32,384]{1,0:T(8,128)(2,1)S(1)}, bf16[32,384]{1,0:T(8,128)(2,1)S(1)}, u32[]{:S(2)}, u32[]{:S(2)}) collective-permute-start(bf16[32,384]{1,0:T(8,128)(2,1)S(1)} %add_parts.3.refs_0_), channel_id=1, source_target_pairs={{0,1},{1,0},{2,3},{3,2},{4,5},{5,4},{6,7},{7,6},{8,9},{9,8},{10,11... | collective-permute-start | bytes 73736 | tf_op jit(solution)/shard_map/ppermute | solution.py:431

commit v18 on v17

--- a/solution.py
+++ b/solution.py
@@ -297,13 +297,22 @@
     dpre = whole((back * gelu_slope(pre, share)).astype(BF16), dpre_own[...])
     over_lanes = (((1,), (1,)), ((), ()))
     ones, twos = [], []
+    sums = [[None] * 3, [None] * 3]
+    for pair in range(count // 2 + 2):
+        taps_here = [a for a in range(3) if 0 <= pair - a < count // 2]
+        at = slice(pair * 256, (pair + 1) * 256)
+        shifted_rows = (
+            jnp.concatenate([fs[:, (pair + 1) * 256:(pair + 2) * 256], fr[:, at]], axis=0),
+            jnp.concatenate([cs[:, at], cr[:, at]], axis=0),
+        )
+        for here, rows, total in zip((dpre, hidden), shifted_rows, sums):
+            here = jnp.concatenate([here[:, (pair - a) * 256:(pair - a + 1) * 256] for a in taps_here], axis=0)
+            got = lax.dot_general(here, rows, over_lanes, preferred_element_type=F32)
+            for n, a in enumerate(taps_here):
+                part = got[n * 128:(n + 1) * 128]
+                total[a] = part if total[a] is None else total[a] + part
     for a in range(3):
-        at = slice((a + 1) * 256, (a + 1) * 256 + lanes)
-        rows = jnp.concatenate([fs[:, at], fr[:, a * 256:a * 256 + lanes]], axis=0)
-        g1 = lax.dot_general(dpre, rows, over_lanes, preferred_element_type=F32)
-        at = slice(a * 256, a * 256 + lanes)
-        rows = jnp.concatenate([cs[:, at], cr[:, at]], axis=0)
-        g2 = lax.dot_general(hidden, rows, over_lanes, preferred_element_type=F32)
+        g1, g2 = sums[0][a], sums[1][a]
         for b in range(3):
             for g, ys, out in ((g1, y1, ones), (g2, y2, twos)):
                 total = jnp.zeros((CH, g.shape[1]), F32)

time: 35.7 us -> 35.2 us (0.986)
  Pallas kernels: 11.1 us -> 10.6 us
    pallas_call x1, Pallas kernels: 3.13 us -> 2.7 us  [local(): call(functools.partial(rim_kernel, counts), (shape(planes, 128, Z), shape...]
  transfers between devices with their start and end apart: 13 -> 13, of which waited for: 8 -> 8; matrix products, arithmetic and copies ran while one was open for 0% -> 0% of each run, Pallas kernels for 28% -> 27%
where the time goes in v18:
time: 35.2 us; the launch traced here: 35.1 us
  starting transfers between devices  15.9 us (45%)
  Pallas kernels  10.6 us (30%)
  waiting for transfers between devices  6.68 us (19%)
  other arithmetic  1.02 us (3%)
  between operations  0.82 us (2%)
    ppermute x7, starting transfers between devices, swap(): lax.ppermute(v, axis, [(i, i ^ mask) for i in range(count)])  7.68 us
    ppermute x7, waiting for transfers between devices, swap(): lax.ppermute(v, axis, [(i, i ^ mask) for i in range(count)])  5.69 us
    ppermute x3, starting transfers between devices, exchange(): return (lax.ppermute(near, axis, [(i, i ^ 1) for i in range(count)]), far)  4.15 us
    ppermute x3, starting transfers between devices, exchange(): far = lax.ppermute(far, axes, pairs)  4.02 us
    pallas_call x1, Pallas kernels, local(): call(functools.partial(rim_kernel, counts), (shape(planes, 128, Z), shape...  2.7 us
    pallas_call x1, Pallas kernels, local(): call(band_kernel, (shape(192, 768), shape(128, 384), shape(192, 768), sha...  2.7 us
    pallas_call x1, Pallas kernels, local(): call(closure_kernel, shape(*cotangent.shape), 'closure', (pltpu.VMEM((640...  1.57 us
    pallas_call x1, Pallas kernels, local(): call(functools.partial(hidden_rim_kernel, counts), shape(planes + 4, 192,...  1.27 us
  transfers between devices with their start and end apart: 13, of which 8 were waited for; matrix products, arithmetic and copies ran while one was open for 0% of the time, Pallas kernels for 27%

profile of v18, /device:TPU:0, one launch (start us, length us, event | category | flops | bytes accessed | tf_op | source)
XLA Modules:
  0.0 35.1 jit_solution(4581258422628979267)
XLA Ops:
  0.6 1.0 %pad_maximum_fusion.inputs = bf16[24,8,8,128]{3,2,1,0:T(8,128)(2,1)S(1)} fusion(bf16[16,8,8,128]{3,2,1,0:T(8,128)(2,1)} %bitcast.21, bf16[8,8,8,128]{3,2,1,0:T(8,128)(2,1)} %bitcast.22), kind=kLoop, calls=%fused_computation | loop fusion | flops 196608 | bytes 786432 | tf_op jit(solution)/shard_map/concatenate | solution.py:475
  1.7 0.0 copy-start
  1.7 0.0 copy-start.1
  1.7 0.0 copy-start.2
  1.7 0.0 copy-start.3
  1.7 0.1 pack_strips.1
  1.8 0.5 %collective-permute-start = (bf16[512,128]{1,0:T(8,128)(2,1)S(1)}, bf16[512,128]{1,0:T(8,128)(2,1)S(1)}, u32[]{:S(2)}, u32[]{:S(2)}) collective-permute-start(bf16[512,128]{1,0:T(8,128)(2,1)S(1)} %get-tuple-element.39), channel_id=1, source_target_pairs={{0,2},{2,0},{4,6},{6,4},{8,16},{10,18},{12,20},{14,22},{16,8},{18,... | collective-permute-start | bytes 393224 | tf_op jit(solution)/shard_map/ppermute | solution.py:434
  2.4 4.1 %collective-permute-start.1 = (bf16[512,128]{1,0:T(8,128)(2,1)S(1)}, bf16[512,128]{1,0:T(8,128)(2,1)S(1)}, u32[]{:S(2)}, u32[]{:S(2)}) collective-permute-start(bf16[512,128]{1,0:T(8,128)(2,1)S(1)} %get-tuple-element.40), channel_id=1, source_target_pairs={{0,8},{8,0},{16,24},{24,16},{1,9},{9,1},{17,25},{25,17},{2,10},{10... | collective-permute-start | bytes 393224 | tf_op jit(solution)/shard_map/ppermute | solution.py:435
  6.5 0.0 copy-done
  6.5 0.0 copy-done.1
  6.5 0.0 copy-done.2
  6.5 0.0 copy-done.3
  6.5 2.7 %band_matrices.1 = (bf16[192,768]{1,0:T(8,128)(2,1)S(1)}, bf16[128,384]{1,0:T(8,128)(2,1)S(1)}, bf16[192,768]{1,0:T(8,128)(2,1)S(1)}, bf16[128,1152]{1,0:T(8,128...) custom-call(bf16[128,27]{1,0:T(8,128)(2,1)S(1)} %bitcast.18, ...), custom_call_target="tpu_custom_call" | custom-call | flops 4000000000 | bytes 1000000 | tf_op jit(solution)/shard_map/band_matrices/pallas_call | solution.py:479
  9.2 0.0 collective-permute-done.xfar
  9.2 0.5 %collective-permute-done.1.xnear = bf16[512,128]{1,0:T(8,128)(2,1)S(1)} collective-permute-done((bf16[512,128]{1,0:T(8,128)(2,1)S(1)}, bf16[512,128]{1,0:T(8,128)(2,1)S(1)}, u32[]{:S(2)}, u32[]{:S(2)}) %collective-permute-start.1) | collective-permute-done | bytes 131104 | tf_op jit(solution)/shard_map/ppermute | solution.py:435
  9.7 0.3 join_strips.1
  10.0 1.8 %collective-permute-start.2 = (bf16[576,128]{1,0:T(8,128)(2,1)S(1)}, bf16[576,128]{1,0:T(8,128)(2,1)S(1)}, u32[]{:S(2)}, u32[]{:S(2)}) collective-permute-start(bf16[576,128]{1,0:T(8,128)(2,1)S(1)} %get-tuple-element.47), channel_id=1, source_target_pairs={{0,8},{8,0},{16,24},{24,16},{2,4},{10,12},{18,20},{26,28},{4,2},{1... | collective-permute-start | bytes 442376 | tf_op jit(solution)/shard_map/ppermute | solution.py:434
  11.8 0.0 collective-permute-start.3
  11.8 0.0 copy-start.4
  11.8 0.0 copy-start.5
  11.8 0.0 copy-start.6
  11.8 0.0 copy-start.7
  11.9 0.0 copy-start.8
  11.9 0.0 copy-start.9
  11.9 0.9 %own_rows.1 = (bf16[256,2048]{1,0:T(8,128)(2,1)S(1)}, bf16[384,1536]{1,0:T(8,128)(2,1)S(1)}, f32[64,1024]{1,0:T(8,128)S(1)}, f32[64,1024]{1,0:T(8,128)S(1)}, bf1...) custom-call(bf16[512,128]{1,0:T(8,128)(2,1)S(1)} %collective-permute-done.xfar, ...), custom_call_target="tpu_custom_call" | custom-call | flops 1000000000 | bytes 1000000 | tf_op jit(solution)/shard_map/own_rows/pallas_call | solution.py:491
  12.8 0.2 join_outer.1
  13.0 1.7 %collective-permute-start.7 = (bf16[320,128]{1,0:T(8,128)(2,1)S(1)}, bf16[320,128]{1,0:T(8,128)(2,1)S(1)}, u32[]{:S(2)}, u32[]{:S(2)}) collective-permute-start(bf16[320,128]{1,0:T(8,128)(2,1)S(1)} %get-tuple-element.63), channel_id=1, source_target_pairs={{0,8},{8,0},{16,24},{24,16},{2,4},{10,12},{18,20},{26,28},{4,2},{1... | collective-permute-start | bytes 245768 | tf_op jit(solution)/shard_map/ppermute | solution.py:434
  14.7 0.0 collective-permute-start.8
  14.7 0.5 %collective-permute-done.2.rfar = bf16[576,128]{1,0:T(8,128)(2,1)S(1)} collective-permute-done((bf16[576,128]{1,0:T(8,128)(2,1)S(1)}, bf16[576,128]{1,0:T(8,128)(2,1)S(1)}, u32[]{:S(2)}, u32[]{:S(2)}) %collective-permute-start.2) | collective-permute-done | bytes 147488 | tf_op jit(solution)/shard_map/ppermute | solution.py:434
  15.2 0.0 collective-permute-done.3.rnear
  15.2 0.0 copy-done.4
  15.2 0.0 copy-done.5
  15.2 0.0 copy-done.6
  15.2 0.0 copy-done.7
  15.3 0.0 copy-done.8
  15.3 0.0 copy-done.9
  15.3 2.7 %gradients.1 = (bf16[8,128,128]{2,1,0:T(8,128)(2,1)S(1)}, bf16[32,384]{1,0:T(8,128)(2,1)S(1)}) custom-call(bf16[576,128]{1,0:T(8,128)(2,1)S(1)} %collective-permute-done.2.rfar, bf16[576,128]{1,0:T(8,128)(2,1)S(1)} %collective-permute-done.3.rnear, bf16[256,2048]{1,0:T(8,128)(2,1)S(1)} %get-tuple-element.53.fs, bf16[384,1536]{1,0:T(8,128)(2,1)S(1)} %get-tuple-element.54.cs, ...), custom_call_target="tpu_custom_call" | custom-call | flops 2000000000 | bytes 1000000 | tf_op jit(solution)/shard_map/gradients/pallas_call | solution.py:501
  18.0 0.1 collective-permute-start.4
  18.1 1.0 %collective-permute-start.5 = (bf16[32,384]{1,0:T(8,128)(2,1)S(1)}, bf16[32,384]{1,0:T(8,128)(2,1)S(1)}, u32[]{:S(2)}, u32[]{:S(2)}) collective-permute-start(bf16[32,384]{1,0:T(8,128)(2,1)S(1)} %get-tuple-element.61.refs_0_), channel_id=1, source_target_pairs={{0,4},{2,6},{4,0},{6,2},{1,5},{3,7},{5,1},{7,3},{8,12},{10,14},{12... | collective-permute-start | bytes 73736 | tf_op jit(solution)/shard_map/ppermute | solution.py:440
  19.1 0.9 %collective-permute-start.6 = (bf16[32,384]{1,0:T(8,128)(2,1)S(1)}, bf16[32,384]{1,0:T(8,128)(2,1)S(1)}, u32[]{:S(2)}, u32[]{:S(2)}) collective-permute-start(bf16[32,384]{1,0:T(8,128)(2,1)S(1)} %get-tuple-element.61.refs_0_), channel_id=1, source_target_pairs={{0,6},{2,4},{4,2},{6,0},{1,7},{3,5},{5,3},{7,1},{8,14},{10,12},{12... | collective-permute-start | bytes 73736 | tf_op jit(solution)/shard_map/ppermute | solution.py:440
  19.9 0.0 collective-permute-done.7.rfar_outer
  19.9 0.0 collective-permute-done.8.rnear_outer
  19.9 1.3 %hidden_rim.1.hidden = bf16[12,192,128]{2,1,0:T(8,128)(2,1)S(1)} custom-call(bf16[576,128]{1,0:T(8,128)(2,1)S(1)} %collective-permute-done.2.rfar, bf16[576,128]{1,0:T(8,128)(2,1)S(1)} %collective-permute-done.3.rnear, bf16[320,128]{1,0:T(8,128)(2,1)S(1)} %collective-permute-done.7.rfar_outer, bf16[320,128]{1,0:T(8,128)(2,1)S(1)} %collective-permute-done.8.rnear_outer, ...), custom_call_target="tpu_custom_call" | custom-call | flops 1000000000 | bytes 1000000 | tf_op jit(solution)/shard_map/hidden_rim/pallas_call | solution.py:511
  21.2 0.0 collective-permute-done.4.refs_1_
  21.2 0.7 %collective-permute-done.5.refs_2_ = bf16[32,384]{1,0:T(8,128)(2,1)S(1)} collective-permute-done((bf16[32,384]{1,0:T(8,128)(2,1)S(1)}, bf16[32,384]{1,0:T(8,128)(2,1)S(1)}, u32[]{:S(2)}, u32[]{:S(2)}) %collective-permute-start.5) | collective-permute-done | bytes 24608 | tf_op jit(solution)/shard_map/ppermute | solution.py:440
  22.0 0.4 %collective-permute-done.6.refs_3_ = bf16[32,384]{1,0:T(8,128)(2,1)S(1)} collective-permute-done((bf16[32,384]{1,0:T(8,128)(2,1)S(1)}, bf16[32,384]{1,0:T(8,128)(2,1)S(1)}, u32[]{:S(2)}, u32[]{:S(2)}) %collective-permute-start.6) | collective-permute-done | bytes 24608 | tf_op jit(solution)/shard_map/ppermute | solution.py:440
  22.3 2.0 %collective-permute-start.10 = (bf16[32,384]{1,0:T(8,128)(2,1)S(1)}, bf16[32,384]{1,0:T(8,128)(2,1)S(1)}, u32[]{:S(2)}, u32[]{:S(2)}) collective-permute-start(bf16[32,384]{1,0:T(8,128)(2,1)S(1)} %add_parts.2.refs_0_), channel_id=1, source_target_pairs={{0,16},{8,24},{16,0},{24,8},{1,17},{9,25},{17,1},{25,9},{2,18},{10... | collective-permute-start | bytes 73736 | tf_op jit(solution)/shard_map/ppermute | solution.py:440
  24.4 2.1 %collective-permute-start.11 = (bf16[32,384]{1,0:T(8,128)(2,1)S(1)}, bf16[32,384]{1,0:T(8,128)(2,1)S(1)}, u32[]{:S(2)}, u32[]{:S(2)}) collective-permute-start(bf16[32,384]{1,0:T(8,128)(2,1)S(1)} %add_parts.2.refs_0_), channel_id=1, source_target_pairs={{0,24},{8,16},{16,8},{24,0},{1,25},{9,17},{17,9},{25,1},{2,26},{10... | collective-permute-start | bytes 73736 | tf_op jit(solution)/shard_map/ppermute | solution.py:440
  26.5 0.0 collective-permute-start.9
  26.5 0.6 %collective-permute-done.10.refs_2_ = bf16[32,384]{1,0:T(8,128)(2,1)S(1)} collective-permute-done((bf16[32,384]{1,0:T(8,128)(2,1)S(1)}, bf16[32,384]{1,0:T(8,128)(2,1)S(1)}, u32[]{:S(2)}, u32[]{:S(2)}) %collective-permute-start.10) | collective-permute-done | bytes 24608 | tf_op jit(solution)/shard_map/ppermute | solution.py:440
  27.1 2.9 %collective-permute-done.11.refs_3_ = bf16[32,384]{1,0:T(8,128)(2,1)S(1)} collective-permute-done((bf16[32,384]{1,0:T(8,128)(2,1)S(1)}, bf16[32,384]{1,0:T(8,128)(2,1)S(1)}, u32[]{:S(2)}, u32[]{:S(2)}) %collective-permute-start.11) | collective-permute-done | bytes 24608 | tf_op jit(solution)/shard_map/ppermute | solution.py:440
  30.0 0.3 collective-permute-done.9.refs_1_
  30.4 1.6 %collective-permute-start.12 = (bf16[32,384]{1,0:T(8,128)(2,1)S(1)}, bf16[32,384]{1,0:T(8,128)(2,1)S(1)}, u32[]{:S(2)}, u32[]{:S(2)}) collective-permute-start(bf16[32,384]{1,0:T(8,128)(2,1)S(1)} %add_parts.3.refs_0_), channel_id=1, source_target_pairs={{0,1},{1,0},{2,3},{3,2},{4,5},{5,4},{6,7},{7,6},{8,9},{9,8},{10,11... | collective-permute-start | bytes 73736 | tf_op jit(solution)/shard_map/ppermute | solution.py:440
  31.9 1.6 %closure.1 = bf16[1,16,8,8,128]{4,3,2,1,0:T(8,128)(2,1)} custom-call(bf16[12,192,128]{2,1,0:T(8,128)(2,1)S(1)} %hidden_rim.1.hidden, bf16[128,1920]{1,0:T(8,128)(2,1)S(1)} %get-tuple-element.68.t2, f32[128,128]{1,0:T(8,128)S(1)} %get-tuple-element.69.b2), custom_call_target="tpu_custom_call" | custom-call | flops 1000000000 | bytes 1000000 | tf_op jit(solution)/shard_map/closure/pallas_call | solution.py:522
  33.5 0.8 %collective-permute-done.12.refs_1_ = bf16[32,384]{1,0:T(8,128)(2,1)S(1)} collective-permute-done((bf16[32,384]{1,0:T(8,128)(2,1)S(1)}, bf16[32,384]{1,0:T(8,128)(2,1)S(1)}, u32[]{:S(2)}, u32[]{:S(2)}) %collective-permute-start.12) | collective-permute-done | bytes 24608 | tf_op jit(solution)/shard_map/ppermute | solution.py:440
  34.3 0.8 %finish.1 = (f32[128,27]{1,0:T(8,128)}, f32[256,27]{1,0:T(8,128)}, f32[1,16]{1,0:T(1,128)}) custom-call(bf16[32,384]{1,0:T(8,128)(2,1)S(1)} %add_parts.3.refs_0_, bf16[32,384]{1,0:T(8,128)(2,1)S(1)} %collective-permute-done.12.refs_1_), custom_call_target="tpu_custom_call" | custom-call | flops 10000000 | bytes 1000000 | tf_op jit(solution)/shard_map/finish/pallas_call | solution.py:533
  (2 shorter events, 0.0 us)
Async XLA Ops:
  1.7 4.8 %copy-start = (bf16[27,16,16]{0,2,1:T(8,128)(2,1)S(1)}, bf16[27,16,16]{0,2,1:T(8,128)(2,1)}, u32[]{:S(2)}) copy-start(bf16[27,16,16]{0,2,1:T(8,128)(2,1)} %param.15) | copy-start | bytes 41476
  1.7 4.8 %copy-start.1 = (bf16[27,16,8]{0,2,1:T(8,128)(2,1)S(1)}, bf16[27,16,8]{0,2,1:T(8,128)(2,1)}, u32[]{:S(2)}) copy-start(bf16[27,16,8]{0,2,1:T(8,128)(2,1)} %param.13) | copy-start | bytes 20740
  1.7 4.8 %copy-start.2 = (f32[16]{0:T(128)S(1)}, f32[16]{0:T(128)}, u32[]{:S(2)}) copy-start(f32[16]{0:T(128)} %param.14) | copy-start | bytes 196
  1.7 4.8 %copy-start.3 = (f32[16]{0:T(128)S(1)}, f32[16]{0:T(128)}, u32[]{:S(2)}) copy-start(f32[16]{0:T(128)} %param.16) | copy-start | bytes 196
  1.8 7.4 %collective-permute-start = (bf16[512,128]{1,0:T(8,128)(2,1)S(1)}, bf16[512,128]{1,0:T(8,128)(2,1)S(1)}, u32[]{:S(2)}, u32[]{:S(2)}) collective-permute-start(bf16[512,128]{1,0:T(8,128)(2,1)S(1)} %get-tuple-element.39), channel_id=1, source_target_pairs={{0,2},{2,0},{4,6},{6,4},{8,16},{10,18},{12,20},{14,22},{16,8},{18,... | collective-permute-start | bytes 393224 | tf_op jit(solution)/shard_map/ppermute | solution.py:434
  2.4 7.4 %collective-permute-start.1 = (bf16[512,128]{1,0:T(8,128)(2,1)S(1)}, bf16[512,128]{1,0:T(8,128)(2,1)S(1)}, u32[]{:S(2)}, u32[]{:S(2)}) collective-permute-start(bf16[512,128]{1,0:T(8,128)(2,1)S(1)} %get-tuple-element.40), channel_id=1, source_target_pairs={{0,8},{8,0},{16,24},{24,16},{1,9},{9,1},{17,25},{25,17},{2,10},{10... | collective-permute-start | bytes 393224 | tf_op jit(solution)/shard_map/ppermute | solution.py:435
  10.0 5.2 %collective-permute-start.2 = (bf16[576,128]{1,0:T(8,128)(2,1)S(1)}, bf16[576,128]{1,0:T(8,128)(2,1)S(1)}, u32[]{:S(2)}, u32[]{:S(2)}) collective-permute-start(bf16[576,128]{1,0:T(8,128)(2,1)S(1)} %get-tuple-element.47), channel_id=1, source_target_pairs={{0,8},{8,0},{16,24},{24,16},{2,4},{10,12},{18,20},{26,28},{4,2},{1... | collective-permute-start | bytes 442376 | tf_op jit(solution)/shard_map/ppermute | solution.py:434
  11.8 3.4 %collective-permute-start.3 = (bf16[576,128]{1,0:T(8,128)(2,1)S(1)}, bf16[576,128]{1,0:T(8,128)(2,1)S(1)}, u32[]{:S(2)}, u32[]{:S(2)}) collective-permute-start(bf16[576,128]{1,0:T(8,128)(2,1)S(1)} %get-tuple-element.48), channel_id=1, source_target_pairs={{0,2},{2,0},{4,6},{6,4},{1,3},{3,1},{5,7},{7,5},{8,10},{10,8},{12,... | collective-permute-start | bytes 442376 | tf_op jit(solution)/shard_map/ppermute | solution.py:435
  11.8 3.4 %copy-start.4 = (bf16[128,768]{1,0:T(8,128)(2,1)S(1)}, bf16[128,768]{1,0:T(8,128)(2,1)}, u32[]{:S(2)}) copy-start(bf16[128,768]{1,0:T(8,128)(2,1)} %constant.15.clone.rep2) | copy-start | bytes 589828
  11.8 3.4 %copy-start.5 = (bf16[640,128]{1,0:T(8,128)(2,1)S(1)}, bf16[640,128]{1,0:T(8,128)(2,1)}, u32[]{:S(2)}) copy-start(bf16[640,128]{1,0:T(8,128)(2,1)} %constant.13.clone.e2t) | copy-start | bytes 491524
  11.8 3.4 %copy-start.6 = (bf16[384,128]{1,0:T(8,128)(2,1)S(1)}, bf16[384,128]{1,0:T(8,128)(2,1)}, u32[]{:S(2)}) copy-start(bf16[384,128]{1,0:T(8,128)(2,1)} %constant.12.clone.e1t) | copy-start | bytes 294916
  11.8 3.4 %copy-start.7 = (bf16[128,384]{1,0:T(8,128)(2,1)S(1)}, bf16[128,384]{1,0:T(8,128)(2,1)}, u32[]{:S(2)}) copy-start(bf16[128,384]{1,0:T(8,128)(2,1)} %constant.14.clone.rep1) | copy-start | bytes 294916
  11.9 3.4 %copy-start.8 = (f32[1,640]{1,0:T(1,128)S(1)}, f32[1,640]{1,0:T(1,128)}, u32[]{:S(2)}) copy-start(f32[1,640]{1,0:T(1,128)} %constant.17.clone.y2) | copy-start | bytes 7684
  11.9 3.4 %copy-start.9 = (f32[1,384]{1,0:T(1,128)S(1)}, f32[1,384]{1,0:T(1,128)}, u32[]{:S(2)}) copy-start(f32[1,384]{1,0:T(1,128)} %constant.16.clone.y1) | copy-start | bytes 4612
  13.0 6.9 %collective-permute-start.7 = (bf16[320,128]{1,0:T(8,128)(2,1)S(1)}, bf16[320,128]{1,0:T(8,128)(2,1)S(1)}, u32[]{:S(2)}, u32[]{:S(2)}) collective-permute-start(bf16[320,128]{1,0:T(8,128)(2,1)S(1)} %get-tuple-element.63), channel_id=1, source_target_pairs={{0,8},{8,0},{16,24},{24,16},{2,4},{10,12},{18,20},{26,28},{4,2},{1... | collective-permute-start | bytes 245768 | tf_op jit(solution)/shard_map/ppermute | solution.py:434
  14.7 5.2 %collective-permute-start.8 = (bf16[320,128]{1,0:T(8,128)(2,1)S(1)}, bf16[320,128]{1,0:T(8,128)(2,1)S(1)}, u32[]{:S(2)}, u32[]{:S(2)}) collective-permute-start(bf16[320,128]{1,0:T(8,128)(2,1)S(1)} %get-tuple-element.64), channel_id=1, source_target_pairs={{0,2},{2,0},{4,6},{6,4},{1,3},{3,1},{5,7},{7,5},{8,10},{10,8},{12,... | collective-permute-start | bytes 245768 | tf_op jit(solution)/shard_map/ppermute | solution.py:435
  18.0 3.2 %collective-permute-start.4 = (bf16[32,384]{1,0:T(8,128)(2,1)S(1)}, bf16[32,384]{1,0:T(8,128)(2,1)S(1)}, u32[]{:S(2)}, u32[]{:S(2)}) collective-permute-start(bf16[32,384]{1,0:T(8,128)(2,1)S(1)} %get-tuple-element.61.refs_0_), channel_id=1, source_target_pairs={{0,2},{2,0},{4,6},{6,4},{1,3},{3,1},{5,7},{7,5},{8,10},{10,8},{12,... | collective-permute-start | bytes 73736 | tf_op jit(solution)/shard_map/ppermute | solution.py:440
  18.1 3.9 %collective-permute-start.5 = (bf16[32,384]{1,0:T(8,128)(2,1)S(1)}, bf16[32,384]{1,0:T(8,128)(2,1)S(1)}, u32[]{:S(2)}, u32[]{:S(2)}) collective-permute-start(bf16[32,384]{1,0:T(8,128)(2,1)S(1)} %get-tuple-element.61.refs_0_), channel_id=1, source_target_pairs={{0,4},{2,6},{4,0},{6,2},{1,5},{3,7},{5,1},{7,3},{8,12},{10,14},{12... | collective-permute-start | bytes 73736 | tf_op jit(solution)/shard_map/ppermute | solution.py:440
  19.1 3.3 %collective-permute-start.6 = (bf16[32,384]{1,0:T(8,128)(2,1)S(1)}, bf16[32,384]{1,0:T(8,128)(2,1)S(1)}, u32[]{:S(2)}, u32[]{:S(2)}) collective-permute-start(bf16[32,384]{1,0:T(8,128)(2,1)S(1)} %get-tuple-element.61.refs_0_), channel_id=1, source_target_pairs={{0,6},{2,4},{4,2},{6,0},{1,7},{3,5},{5,3},{7,1},{8,14},{10,12},{12... | collective-permute-start | bytes 73736 | tf_op jit(solution)/shard_map/ppermute | solution.py:440
  22.3 4.8 %collective-permute-start.10 = (bf16[32,384]{1,0:T(8,128)(2,1)S(1)}, bf16[32,384]{1,0:T(8,128)(2,1)S(1)}, u32[]{:S(2)}, u32[]{:S(2)}) collective-permute-start(bf16[32,384]{1,0:T(8,128)(2,1)S(1)} %add_parts.2.refs_0_), channel_id=1, source_target_pairs={{0,16},{8,24},{16,0},{24,8},{1,17},{9,25},{17,1},{25,9},{2,18},{10... | collective-permute-start | bytes 73736 | tf_op jit(solution)/shard_map/ppermute | solution.py:440
  24.4 5.6 %collective-permute-start.11 = (bf16[32,384]{1,0:T(8,128)(2,1)S(1)}, bf16[32,384]{1,0:T(8,128)(2,1)S(1)}, u32[]{:S(2)}, u32[]{:S(2)}) collective-permute-start(bf16[32,384]{1,0:T(8,128)(2,1)S(1)} %add_parts.2.refs_0_), channel_id=1, source_target_pairs={{0,24},{8,16},{16,8},{24,0},{1,25},{9,17},{17,9},{25,1},{2,26},{10... | collective-permute-start | bytes 73736 | tf_op jit(solution)/shard_map/ppermute | solution.py:440
  26.5 3.8 %collective-permute-start.9 = (bf16[32,384]{1,0:T(8,128)(2,1)S(1)}, bf16[32,384]{1,0:T(8,128)(2,1)S(1)}, u32[]{:S(2)}, u32[]{:S(2)}) collective-permute-start(bf16[32,384]{1,0:T(8,128)(2,1)S(1)} %add_parts.2.refs_0_), channel_id=1, source_target_pairs={{0,8},{8,0},{16,24},{24,16},{1,9},{9,1},{17,25},{25,17},{2,10},{10... | collective-permute-start | bytes 73736 | tf_op jit(solution)/shard_map/ppermute | solution.py:440
  30.4 3.9 %collective-permute-start.12 = (bf16[32,384]{1,0:T(8,128)(2,1)S(1)}, bf16[32,384]{1,0:T(8,128)(2,1)S(1)}, u32[]{:S(2)}, u32[]{:S(2)}) collective-permute-start(bf16[32,384]{1,0:T(8,128)(2,1)S(1)} %add_parts.3.refs_0_), channel_id=1, source_target_pairs={{0,1},{1,0},{2,3},{3,2},{4,5},{5,4},{6,7},{7,6},{8,9},{9,8},{10,11... | collective-permute-start | bytes 73736 | tf_op jit(solution)/shard_map/ppermute | solution.py:440

commit v19 on v18

--- a/solution.py
+++ b/solution.py
@@ -121,27 +121,35 @@
     return f, [low for low, _ in rims] + inner + [high for _, high in rims]
 
 
-def pick_strips(work, near, far):
+def pick_strips(work, near, far, near_at=0):
     up_first = lax.axis_index("radial") % 2 == 0
     at = 0
     for pick, rows in work:
         half = pick.shape[0] // 2
         for v in rows:
             got = jnp.dot(pick, v.astype(BF16), preferred_element_type=F32)
-            near[at:at + half] = jnp.where(up_first, got[half:], got[:half]).astype(BF16)
-            far[at:at + half] = jnp.where(up_first, got[:half], got[half:]).astype(BF16)
+            if near is not None:
+                start = near_at + at
+                near[start:start + half] = jnp.where(up_first, got[half:], got[:half]).astype(BF16)
+            if far is not None:
+                far[at:at + half] = jnp.where(up_first, got[:half], got[half:]).astype(BF16)
             at += half
+
+
+def outer_strips(f):
+    ends = f[:2] + f[-2:]
+    return [(pick_rows(CI, 0, 6), ends), (pick_rows(CI, 2, 4), ends + f[2:-2])]
 
 
 def join_kernel(counts, xfar, xnear, fields, cot, near, far):
     f, c = x_planes(fields.shape[0], fields, cot, xnear, xfar, counts[0])
     pick_strips([(pick_rows(CI, 0, 6), f[2:-2]), (pick_rows(CH, 0, 6), c)], near, far)
-
-
-def join_outer_kernel(counts, xfar, xnear, fields, cot, near, far):
+    pick_strips(outer_strips(f), near, None, far.shape[0])
+
+
+def join_outer_kernel(counts, xfar, xnear, fields, cot, far):
     f, _ = x_planes(fields.shape[0], fields, cot, xnear, xfar, counts[0])
-    ends = f[:2] + f[-2:]
-    pick_strips([(pick_rows(CI, 0, 6), ends), (pick_rows(CI, 2, 4), ends + f[2:-2])], near, far)
+    pick_strips(outer_strips(f), None, far)
 
 
 def spread(w, by_row, flip):
@@ -339,16 +347,16 @@
     payload[...] = rounded(jnp.concatenate([taps[n] for n in range(3)], axis=1))
 
 
-def hidden_rim_kernel(counts, rfar, rnear, rfar_outer, rnear_outer, hidden, fs, t1o, t1d, b1, hidden_out, fr):
-    count = hidden.shape[0]
+def hidden_rim_kernel(counts, rfar, rnear, rfar_outer, hidden, fs, t1o, t1d, b1, hidden_out, fr):
+    count, inner = hidden.shape[0], rfar.shape[0]
     stream, radial = lax.axis_index("stream"), lax.axis_index("radial")
     for p in range(count + 8):
         end = p if p < 2 else p - count - 4 if p >= count + 6 else None
         if end is None:
-            near, outer = (rnear, rfar, (p - 2) * 16), (rnear_outer, rfar_outer, 128 + (p - 2) * 16)
+            near, outer = (0, rfar, (p - 2) * 16), (inner, rfar_outer, 128 + (p - 2) * 16)
         else:
-            near, outer = (rnear_outer, rfar_outer, end * 16), (rnear_outer, rfar_outer, 64 + end * 16)
-        parts = [sides(radial, counts[1], n[at:at + 16], f[at:at + 16]) for n, f, at in (near, outer)]
+            near, outer = (inner, rfar_outer, end * 16), (inner, rfar_outer, 64 + end * 16)
+        parts = [sides(radial, counts[1], rnear[n + at:n + at + 16], f[at:at + 16]) for n, f, at in (near, outer)]
         rows = jnp.concatenate([part[side] for side in range(2) for part in parts], axis=0)
         for n, piece in enumerate(shifted(rows)):
             fr[n * 64:(n + 1) * 64, p * Z:(p + 1) * Z] = piece
@@ -421,7 +429,7 @@
     return jax.ShapeDtypeStruct(dims, dtype)
 
 
-def exchange(near, far, axis, other):
+def send_far(far, axis, other):
     count, others = lax.axis_size(axis), lax.axis_size(other)
     axes = tuple(name for name in ("stream", "radial", "snap") if name in (axis, other))
     flat = (others, 1) if axes[0] == axis else (1, count)
@@ -431,8 +439,12 @@
             end = i in (0, count - 1)
             to = (i, j ^ 1 if others % 2 == 0 else j) if end else (i - 1 + 2 * (i % 2), j)
             pairs.append((i * flat[0] + j * flat[1], to[0] * flat[0] + to[1] * flat[1]))
-    far = lax.ppermute(far, axes, pairs)
-    return lax.ppermute(near, axis, [(i, i ^ 1) for i in range(count)]), far
+    return lax.ppermute(far, axes, pairs)
+
+
+def exchange(near, far, axis, other):
+    far = send_far(far, axis, other)
+    return lax.ppermute(near, axis, [(i, i ^ 1) for i in range(lax.axis_size(axis))]), far
 
 
 def swap(v, axis, masks):
@@ -484,8 +496,10 @@
         flops=4_000_000_000,
     )(w1, w2, first_bias[None], second_bias[None])
     xfar, xnear, t1o, tbo = lax.optimization_barrier((xfar, xnear, t1o, tbo))
-    inner, outer = shape((planes + 4) * 48, Z), shape(128 + (planes + 4) * 16, Z)
-    near, far = call(functools.partial(join_kernel, counts), (inner, inner), "join_strips")(xfar, xnear, f_rows, c_rows)
+    inner, outer = (planes + 4) * 48, 128 + (planes + 4) * 16
+    near, far = call(
+        functools.partial(join_kernel, counts), (shape(inner + outer, Z), shape(inner, Z)), "join_strips"
+    )(xfar, xnear, f_rows, c_rows)
     rnear, rfar = exchange(near, far, "radial", "stream")
     half, half_f32 = shape(64, planes * Z), shape(64, planes * Z, dtype=F32)
     fs, cs, pre, back, hidden, dpre = call(
@@ -495,9 +509,9 @@
         flops=1_000_000_000,
     )(xfar, xnear, f_rows, c_rows, t1o, tbo, b1)
     f_rows, fs = lax.optimization_barrier((f_rows, fs))
-    near_outer, far_outer = call(functools.partial(join_outer_kernel, counts), (outer, outer), "join_outer")(
+    far_outer = call(functools.partial(join_outer_kernel, counts), shape(outer, Z), "join_outer")(
         xfar, xnear, f_rows, c_rows)
-    rnear_outer, rfar_outer = exchange(near_outer, far_outer, "radial", "stream")
+    rfar_outer = send_far(far_outer, "radial", "stream")
     hidden, payload = call(
         functools.partial(rim_kernel, counts),
         (shape(planes, 128, Z), shape(32, 384)),
@@ -514,7 +528,7 @@
         "hidden_rim",
         (pltpu.VMEM((256, wide + 4 * Z), BF16),),
         flops=1_000_000_000,
-    )(rfar, rnear, rfar_outer, rnear_outer, hidden, fs, t1o, t1d, b1)
+    )(rfar, rnear, rfar_outer, hidden, fs, t1o, t1d, b1)
     payload, hidden = lax.optimization_barrier((add(payload, arrived), hidden))
     arrived = swap(payload, *steps[1])
     payload = add(payload, arrived)

time: 35.2 us -> 35.6 us (1.011)
  waiting for transfers between devices: 6.68 us -> 7.98 us
  starting transfers between devices: 15.9 us -> 14.9 us
    ppermute x6 -> x5, waiting for transfers between devices: 0.99 us -> 2.35 us  [the longest x3 1.86 us: send_far(): return lax.ppermute(far, axes, pairs)]
    ppermute x6 -> x5, starting transfers between devices: 8.17 us -> 6.89 us  [the longest x2 4.22 us: exchange(): lax.ppermute(near, axis, [(i, i ^ 1) for i in range(lax.axis_size(axis))])]
  transfers between devices with their start and end apart: 13 -> 12, of which waited for: 8 -> 8; matrix products, arithmetic and copies ran while one was open for 0% -> 0% of each run, Pallas kernels for 27% -> 26%
where the time goes in v19:
time: 35.6 us; the launch traced here: 35.5 us
  starting transfers between devices  14.9 us (42%)
  Pallas kernels  10.7 us (30%)
  waiting for transfers between devices  7.98 us (22%)
  other arithmetic  1.02 us (3%)
  between operations  0.82 us (2%)
    ppermute x7, starting transfers between devices, swap(): lax.ppermute(v, axis, [(i, i ^ mask) for i in range(count)])  8 us
    ppermute x7, waiting for transfers between devices, swap(): lax.ppermute(v, axis, [(i, i ^ mask) for i in range(count)])  5.63 us
    ppermute x2, starting transfers between devices, exchange(): lax.ppermute(near, axis, [(i, i ^ 1) for i in range(lax.axis_size(axis))])  4.22 us
    pallas_call x1, Pallas kernels, local(): call(functools.partial(rim_kernel, counts), (shape(planes, 128, Z), shape...  2.7 us
    pallas_call x1, Pallas kernels, local(): call(band_kernel, (shape(192, 768), shape(128, 384), shape(192, 768), sha...  2.7 us
    ppermute x3, starting transfers between devices, send_far(): return lax.ppermute(far, axes, pairs)  2.67 us
    ppermute x3, waiting for transfers between devices, send_far(): return lax.ppermute(far, axes, pairs)  1.86 us
    pallas_call x1, Pallas kernels, local(): call(closure_kernel, shape(*cotangent.shape), 'closure', (pltpu.VMEM((640...  1.57 us
  transfers between devices with their start and end apart: 12, of which 8 were waited for; matrix products, arithmetic and copies ran while one was open for 0% of the time, Pallas kernels for 26%

profile of v19, /device:TPU:0, one launch (start us, length us, event | category | flops | bytes accessed | tf_op | source)
XLA Modules:
  0.0 35.5 jit_solution(6227971508055701451)
XLA Ops:
  0.6 1.0 %pad_maximum_fusion.inputs = bf16[24,8,8,128]{3,2,1,0:T(8,128)(2,1)S(1)} fusion(bf16[16,8,8,128]{3,2,1,0:T(8,128)(2,1)} %bitcast.21, bf16[8,8,8,128]{3,2,1,0:T(8,128)(2,1)} %bitcast.22), kind=kLoop, calls=%fused_computation | loop fusion | flops 196608 | bytes 786432 | tf_op jit(solution)/shard_map/concatenate | solution.py:487
  1.7 0.0 copy-start
  1.7 0.0 copy-start.1
  1.7 0.0 copy-start.2
  1.7 0.0 copy-start.3
  1.7 0.1 pack_strips.1
  1.8 0.5 %collective-permute-start = (bf16[512,128]{1,0:T(8,128)(2,1)S(1)}, bf16[512,128]{1,0:T(8,128)(2,1)S(1)}, u32[]{:S(2)}, u32[]{:S(2)}) collective-permute-start(bf16[512,128]{1,0:T(8,128)(2,1)S(1)} %get-tuple-element.37), channel_id=1, source_target_pairs={{0,2},{2,0},{4,6},{6,4},{8,16},{10,18},{12,20},{14,22},{16,8},{18,... | collective-permute-start | bytes 393224 | tf_op jit(solution)/shard_map/ppermute | solution.py:442
  2.4 4.1 %collective-permute-start.1 = (bf16[512,128]{1,0:T(8,128)(2,1)S(1)}, bf16[512,128]{1,0:T(8,128)(2,1)S(1)}, u32[]{:S(2)}, u32[]{:S(2)}) collective-permute-start(bf16[512,128]{1,0:T(8,128)(2,1)S(1)} %get-tuple-element.38), channel_id=1, source_target_pairs={{0,8},{8,0},{16,24},{24,16},{1,9},{9,1},{17,25},{25,17},{2,10},{10... | collective-permute-start | bytes 393224 | tf_op jit(solution)/shard_map/ppermute | solution.py:447
  6.5 0.0 copy-done
  6.5 0.0 copy-done.1
  6.5 0.0 copy-done.2
  6.5 0.0 copy-done.3
  6.5 2.7 %band_matrices.1 = (bf16[192,768]{1,0:T(8,128)(2,1)S(1)}, bf16[128,384]{1,0:T(8,128)(2,1)S(1)}, bf16[192,768]{1,0:T(8,128)(2,1)S(1)}, bf16[128,1152]{1,0:T(8,128...) custom-call(bf16[128,27]{1,0:T(8,128)(2,1)S(1)} %bitcast.18, ...), custom_call_target="tpu_custom_call" | custom-call | flops 4000000000 | bytes 1000000 | tf_op jit(solution)/shard_map/band_matrices/pallas_call | solution.py:491
  9.2 0.0 collective-permute-done.xfar
  9.2 0.5 %collective-permute-done.1.xnear = bf16[512,128]{1,0:T(8,128)(2,1)S(1)} collective-permute-done((bf16[512,128]{1,0:T(8,128)(2,1)S(1)}, bf16[512,128]{1,0:T(8,128)(2,1)S(1)}, u32[]{:S(2)}, u32[]{:S(2)}) %collective-permute-start.1) | collective-permute-done | bytes 131104 | tf_op jit(solution)/shard_map/ppermute | solution.py:447
  9.7 0.4 %join_strips.1 = (bf16[896,128]{1,0:T(8,128)(2,1)S(1)}, bf16[576,128]{1,0:T(8,128)(2,1)S(1)}) custom-call(bf16[512,128]{1,0:T(8,128)(2,1)S(1)} %collective-permute-done.xfar, bf16[512,128]{1,0:T(8,128)(2,1)S(1)} %collective-permute-done.1.xnear, bf16[8,64,128]{2,1,0:T(8,128)(2,1)S(1)} %get-tuple-element.60.fields, bf16[8,128,128]{2,1,0:T(8,128)(2,1)S(1)} %get-tuple-element.44.cot), custom_call_target="tpu_custom_call" | custom-call | flops 10000000 | bytes 1000000 | tf_op jit(solution)/shard_map/join_strips/pallas_call | solution.py:500
  10.1 0.1 collective-permute-start.3
  10.2 1.8 %collective-permute-start.2 = (bf16[576,128]{1,0:T(8,128)(2,1)S(1)}, bf16[576,128]{1,0:T(8,128)(2,1)S(1)}, u32[]{:S(2)}, u32[]{:S(2)}) collective-permute-start(bf16[576,128]{1,0:T(8,128)(2,1)S(1)} %get-tuple-element.45), channel_id=1, source_target_pairs={{0,8},{8,0},{16,24},{24,16},{2,4},{10,12},{18,20},{26,28},{4,2},{1... | collective-permute-start | bytes 442376 | tf_op jit(solution)/shard_map/ppermute | solution.py:442
  12.0 0.0 copy-start.4
  12.0 0.0 copy-start.5
  12.0 0.0 copy-start.6
  12.0 0.0 copy-start.7
  12.0 0.0 copy-start.8
  12.0 0.0 copy-start.9
  12.0 0.9 %own_rows.1 = (bf16[256,2048]{1,0:T(8,128)(2,1)S(1)}, bf16[384,1536]{1,0:T(8,128)(2,1)S(1)}, f32[64,1024]{1,0:T(8,128)S(1)}, f32[64,1024]{1,0:T(8,128)S(1)}, bf1...) custom-call(bf16[512,128]{1,0:T(8,128)(2,1)S(1)} %collective-permute-done.xfar, ...), custom_call_target="tpu_custom_call" | custom-call | flops 1000000000 | bytes 1000000 | tf_op jit(solution)/shard_map/own_rows/pallas_call | solution.py:505
  13.0 0.2 join_outer.1
  13.2 0.3 collective-permute-start.7
  13.5 1.9 %collective-permute-done.2.rfar = bf16[576,128]{1,0:T(8,128)(2,1)S(1)} collective-permute-done((bf16[576,128]{1,0:T(8,128)(2,1)S(1)}, bf16[576,128]{1,0:T(8,128)(2,1)S(1)}, u32[]{:S(2)}, u32[]{:S(2)}) %collective-permute-start.2) | collective-permute-done | bytes 147488 | tf_op jit(solution)/shard_map/ppermute | solution.py:442
  15.4 0.0 collective-permute-done.3.rnear
  15.4 0.0 copy-done.4
  15.4 0.0 copy-done.5
  15.4 0.0 copy-done.6
  15.4 0.0 copy-done.7
  15.4 0.0 copy-done.8
  15.4 0.0 copy-done.9
  15.4 2.7 %gradients.1 = (bf16[8,128,128]{2,1,0:T(8,128)(2,1)S(1)}, bf16[32,384]{1,0:T(8,128)(2,1)S(1)}) custom-call(bf16[576,128]{1,0:T(8,128)(2,1)S(1)} %collective-permute-done.2.rfar, bf16[896,128]{1,0:T(8,128)(2,1)S(1)} %collective-permute-done.3.rnear, bf16[256,2048]{1,0:T(8,128)(2,1)S(1)} %get-tuple-element.51.fs, bf16[384,1536]{1,0:T(8,128)(2,1)S(1)} %get-tuple-element.52.cs, ...), custom_call_target="tpu_custom_call" | custom-call | flops 2000000000 | bytes 1000000 | tf_op jit(solution)/shard_map/gradients/pallas_call | solution.py:515
  18.1 0.2 collective-permute-start.4
  18.3 1.0 %collective-permute-start.5 = (bf16[32,384]{1,0:T(8,128)(2,1)S(1)}, bf16[32,384]{1,0:T(8,128)(2,1)S(1)}, u32[]{:S(2)}, u32[]{:S(2)}) collective-permute-start(bf16[32,384]{1,0:T(8,128)(2,1)S(1)} %get-tuple-element.59.refs_0_), channel_id=1, source_target_pairs={{0,4},{2,6},{4,0},{6,2},{1,5},{3,7},{5,1},{7,3},{8,12},{10,14},{12... | collective-permute-start | bytes 73736 | tf_op jit(solution)/shard_map/ppermute | solution.py:452
  19.3 0.8 %collective-permute-start.6 = (bf16[32,384]{1,0:T(8,128)(2,1)S(1)}, bf16[32,384]{1,0:T(8,128)(2,1)S(1)}, u32[]{:S(2)}, u32[]{:S(2)}) collective-permute-start(bf16[32,384]{1,0:T(8,128)(2,1)S(1)} %get-tuple-element.59.refs_0_), channel_id=1, source_target_pairs={{0,6},{2,4},{4,2},{6,0},{1,7},{3,5},{5,3},{7,1},{8,14},{10,12},{12... | collective-permute-start | bytes 73736 | tf_op jit(solution)/shard_map/ppermute | solution.py:452
  20.1 0.0 collective-permute-done.7.rfar_outer
  20.1 1.3 %hidden_rim.1.hidden = bf16[12,192,128]{2,1,0:T(8,128)(2,1)S(1)} custom-call(bf16[576,128]{1,0:T(8,128)(2,1)S(1)} %collective-permute-done.2.rfar, bf16[896,128]{1,0:T(8,128)(2,1)S(1)} %collective-permute-done.3.rnear, bf16[320,128]{1,0:T(8,128)(2,1)S(1)} %collective-permute-done.7.rfar_outer, bf16[8,128,128]{2,1,0:T(8,128)(2,1)S(1)} %get-tuple-element.61.hidden, ...), custom_call_target="tpu_custom_call" | custom-call | flops 1000000000 | bytes 1000000 | tf_op jit(solution)/shard_map/hidden_rim/pallas_call | solution.py:525
  21.4 0.0 collective-permute-done.4.refs_1_
  21.4 0.8 %collective-permute-done.5.refs_2_ = bf16[32,384]{1,0:T(8,128)(2,1)S(1)} collective-permute-done((bf16[32,384]{1,0:T(8,128)(2,1)S(1)}, bf16[32,384]{1,0:T(8,128)(2,1)S(1)}, u32[]{:S(2)}, u32[]{:S(2)}) %collective-permute-start.5) | collective-permute-done | bytes 24608 | tf_op jit(solution)/shard_map/ppermute | solution.py:452
  22.1 0.4 %collective-permute-done.6.refs_3_ = bf16[32,384]{1,0:T(8,128)(2,1)S(1)} collective-permute-done((bf16[32,384]{1,0:T(8,128)(2,1)S(1)}, bf16[32,384]{1,0:T(8,128)(2,1)S(1)}, u32[]{:S(2)}, u32[]{:S(2)}) %collective-permute-start.6) | collective-permute-done | bytes 24608 | tf_op jit(solution)/shard_map/ppermute | solution.py:452
  22.6 3.2 %collective-permute-start.10 = (bf16[32,384]{1,0:T(8,128)(2,1)S(1)}, bf16[32,384]{1,0:T(8,128)(2,1)S(1)}, u32[]{:S(2)}, u32[]{:S(2)}) collective-permute-start(bf16[32,384]{1,0:T(8,128)(2,1)S(1)} %add_parts.2.refs_0_), channel_id=1, source_target_pairs={{0,24},{8,16},{16,8},{24,0},{1,25},{9,17},{17,9},{25,1},{2,26},{10... | collective-permute-start | bytes 73736 | tf_op jit(solution)/shard_map/ppermute | solution.py:452
  25.8 0.0 collective-permute-start.8
  25.8 1.3 %collective-permute-start.9 = (bf16[32,384]{1,0:T(8,128)(2,1)S(1)}, bf16[32,384]{1,0:T(8,128)(2,1)S(1)}, u32[]{:S(2)}, u32[]{:S(2)}) collective-permute-start(bf16[32,384]{1,0:T(8,128)(2,1)S(1)} %add_parts.2.refs_0_), channel_id=1, source_target_pairs={{0,16},{8,24},{16,0},{24,8},{1,17},{9,25},{17,1},{25,9},{2,18},{10... | collective-permute-start | bytes 73736 | tf_op jit(solution)/shard_map/ppermute | solution.py:452
  27.0 1.2 %collective-permute-done.10.refs_3_ = bf16[32,384]{1,0:T(8,128)(2,1)S(1)} collective-permute-done((bf16[32,384]{1,0:T(8,128)(2,1)S(1)}, bf16[32,384]{1,0:T(8,128)(2,1)S(1)}, u32[]{:S(2)}, u32[]{:S(2)}) %collective-permute-start.10) | collective-permute-done | bytes 24608 | tf_op jit(solution)/shard_map/ppermute | solution.py:452
  28.3 1.4 %collective-permute-done.8.refs_1_ = bf16[32,384]{1,0:T(8,128)(2,1)S(1)} collective-permute-done((bf16[32,384]{1,0:T(8,128)(2,1)S(1)}, bf16[32,384]{1,0:T(8,128)(2,1)S(1)}, u32[]{:S(2)}, u32[]{:S(2)}) %collective-permute-start.8) | collective-permute-done | bytes 24608 | tf_op jit(solution)/shard_map/ppermute | solution.py:452
  29.7 1.1 %collective-permute-done.9.refs_2_ = bf16[32,384]{1,0:T(8,128)(2,1)S(1)} collective-permute-done((bf16[32,384]{1,0:T(8,128)(2,1)S(1)}, bf16[32,384]{1,0:T(8,128)(2,1)S(1)}, u32[]{:S(2)}, u32[]{:S(2)}) %collective-permute-start.9) | collective-permute-done | bytes 24608 | tf_op jit(solution)/shard_map/ppermute | solution.py:452
  30.8 1.6 %collective-permute-start.11 = (bf16[32,384]{1,0:T(8,128)(2,1)S(1)}, bf16[32,384]{1,0:T(8,128)(2,1)S(1)}, u32[]{:S(2)}, u32[]{:S(2)}) collective-permute-start(bf16[32,384]{1,0:T(8,128)(2,1)S(1)} %add_parts.3.refs_0_), channel_id=1, source_target_pairs={{0,1},{1,0},{2,3},{3,2},{4,5},{5,4},{6,7},{7,6},{8,9},{9,8},{10,11... | collective-permute-start | bytes 73736 | tf_op jit(solution)/shard_map/ppermute | solution.py:452
  32.4 1.6 %closure.1 = bf16[1,16,8,8,128]{4,3,2,1,0:T(8,128)(2,1)} custom-call(bf16[12,192,128]{2,1,0:T(8,128)(2,1)S(1)} %hidden_rim.1.hidden, bf16[128,1920]{1,0:T(8,128)(2,1)S(1)} %get-tuple-element.64.t2, f32[128,128]{1,0:T(8,128)S(1)} %get-tuple-element.65.b2), custom_call_target="tpu_custom_call" | custom-call | flops 1000000000 | bytes 1000000 | tf_op jit(solution)/shard_map/closure/pallas_call | solution.py:536
  33.9 0.7 %collective-permute-done.11.refs_1_ = bf16[32,384]{1,0:T(8,128)(2,1)S(1)} collective-permute-done((bf16[32,384]{1,0:T(8,128)(2,1)S(1)}, bf16[32,384]{1,0:T(8,128)(2,1)S(1)}, u32[]{:S(2)}, u32[]{:S(2)}) %collective-permute-start.11) | collective-permute-done | bytes 24608 | tf_op jit(solution)/shard_map/ppermute | solution.py:452
  34.7 0.8 %finish.1 = (f32[128,27]{1,0:T(8,128)}, f32[256,27]{1,0:T(8,128)}, f32[1,16]{1,0:T(1,128)}) custom-call(bf16[32,384]{1,0:T(8,128)(2,1)S(1)} %add_parts.3.refs_0_, bf16[32,384]{1,0:T(8,128)(2,1)S(1)} %collective-permute-done.11.refs_1_), custom_call_target="tpu_custom_call" | custom-call | flops 10000000 | bytes 1000000 | tf_op jit(solution)/shard_map/finish/pallas_call | solution.py:547
  (2 shorter events, 0.0 us)
Async XLA Ops:
  1.7 4.8 %copy-start = (bf16[27,16,16]{0,2,1:T(8,128)(2,1)S(1)}, bf16[27,16,16]{0,2,1:T(8,128)(2,1)}, u32[]{:S(2)}) copy-start(bf16[27,16,16]{0,2,1:T(8,128)(2,1)} %param.15) | copy-start | bytes 41476
  1.7 4.8 %copy-start.1 = (bf16[27,16,8]{0,2,1:T(8,128)(2,1)S(1)}, bf16[27,16,8]{0,2,1:T(8,128)(2,1)}, u32[]{:S(2)}) copy-start(bf16[27,16,8]{0,2,1:T(8,128)(2,1)} %param.13) | copy-start | bytes 20740
  1.7 4.8 %copy-start.2 = (f32[16]{0:T(128)S(1)}, f32[16]{0:T(128)}, u32[]{:S(2)}) copy-start(f32[16]{0:T(128)} %param.14) | copy-start | bytes 196
  1.7 4.8 %copy-start.3 = (f32[16]{0:T(128)S(1)}, f32[16]{0:T(128)}, u32[]{:S(2)}) copy-start(f32[16]{0:T(128)} %param.16) | copy-start | bytes 196
  1.8 7.4 %collective-permute-start = (bf16[512,128]{1,0:T(8,128)(2,1)S(1)}, bf16[512,128]{1,0:T(8,128)(2,1)S(1)}, u32[]{:S(2)}, u32[]{:S(2)}) collective-permute-start(bf16[512,128]{1,0:T(8,128)(2,1)S(1)} %get-tuple-element.37), channel_id=1, source_target_pairs={{0,2},{2,0},{4,6},{6,4},{8,16},{10,18},{12,20},{14,22},{16,8},{18,... | collective-permute-start | bytes 393224 | tf_op jit(solution)/shard_map/ppermute | solution.py:442
  2.4 7.4 %collective-permute-start.1 = (bf16[512,128]{1,0:T(8,128)(2,1)S(1)}, bf16[512,128]{1,0:T(8,128)(2,1)S(1)}, u32[]{:S(2)}, u32[]{:S(2)}) collective-permute-start(bf16[512,128]{1,0:T(8,128)(2,1)S(1)} %get-tuple-element.38), channel_id=1, source_target_pairs={{0,8},{8,0},{16,24},{24,16},{1,9},{9,1},{17,25},{25,17},{2,10},{10... | collective-permute-start | bytes 393224 | tf_op jit(solution)/shard_map/ppermute | solution.py:447
  10.1 5.3 %collective-permute-start.3 = (bf16[896,128]{1,0:T(8,128)(2,1)S(1)}, bf16[896,128]{1,0:T(8,128)(2,1)S(1)}, u32[]{:S(2)}, u32[]{:S(2)}) collective-permute-start(bf16[896,128]{1,0:T(8,128)(2,1)S(1)} %get-tuple-element.46), channel_id=1, source_target_pairs={{0,2},{2,0},{4,6},{6,4},{1,3},{3,1},{5,7},{7,5},{8,10},{10,8},{12,... | collective-permute-start | bytes 688136 | tf_op jit(solution)/shard_map/ppermute | solution.py:447
  10.2 5.2 %collective-permute-start.2 = (bf16[576,128]{1,0:T(8,128)(2,1)S(1)}, bf16[576,128]{1,0:T(8,128)(2,1)S(1)}, u32[]{:S(2)}, u32[]{:S(2)}) collective-permute-start(bf16[576,128]{1,0:T(8,128)(2,1)S(1)} %get-tuple-element.45), channel_id=1, source_target_pairs={{0,8},{8,0},{16,24},{24,16},{2,4},{10,12},{18,20},{26,28},{4,2},{1... | collective-permute-start | bytes 442376 | tf_op jit(solution)/shard_map/ppermute | solution.py:442
  12.0 3.4 %copy-start.4 = (bf16[128,768]{1,0:T(8,128)(2,1)S(1)}, bf16[128,768]{1,0:T(8,128)(2,1)}, u32[]{:S(2)}) copy-start(bf16[128,768]{1,0:T(8,128)(2,1)} %constant.15.clone.rep2) | copy-start | bytes 589828
  12.0 3.4 %copy-start.5 = (bf16[640,128]{1,0:T(8,128)(2,1)S(1)}, bf16[640,128]{1,0:T(8,128)(2,1)}, u32[]{:S(2)}) copy-start(bf16[640,128]{1,0:T(8,128)(2,1)} %constant.13.clone.e2t) | copy-start | bytes 491524
  12.0 3.4 %copy-start.6 = (bf16[384,128]{1,0:T(8,128)(2,1)S(1)}, bf16[384,128]{1,0:T(8,128)(2,1)}, u32[]{:S(2)}) copy-start(bf16[384,128]{1,0:T(8,128)(2,1)} %constant.12.clone.e1t) | copy-start | bytes 294916
  12.0 3.4 %copy-start.7 = (bf16[128,384]{1,0:T(8,128)(2,1)S(1)}, bf16[128,384]{1,0:T(8,128)(2,1)}, u32[]{:S(2)}) copy-start(bf16[128,384]{1,0:T(8,128)(2,1)} %constant.14.clone.rep1) | copy-start | bytes 294916
  12.0 3.4 %copy-start.8 = (f32[1,640]{1,0:T(1,128)S(1)}, f32[1,640]{1,0:T(1,128)}, u32[]{:S(2)}) copy-start(f32[1,640]{1,0:T(1,128)} %constant.17.clone.y2) | copy-start | bytes 7684
  12.0 3.4 %copy-start.9 = (f32[1,384]{1,0:T(1,128)S(1)}, f32[1,384]{1,0:T(1,128)}, u32[]{:S(2)}) copy-start(f32[1,384]{1,0:T(1,128)} %constant.16.clone.y1) | copy-start | bytes 4612
  13.2 6.9 %collective-permute-start.7 = (bf16[320,128]{1,0:T(8,128)(2,1)S(1)}, bf16[320,128]{1,0:T(8,128)(2,1)S(1)}, u32[]{:S(2)}, u32[]{:S(2)}) collective-permute-start(bf16[320,128]{1,0:T(8,128)(2,1)S(1)} %join_outer.1), channel_id=1, source_target_pairs={{0,8},{8,0},{16,24},{24,16},{2,4},{10,12},{18,20},{26,28},{4,2},{1... | collective-permute-start | bytes 245768 | tf_op jit(solution)/shard_map/ppermute | solution.py:442
  18.1 3.2 %collective-permute-start.4 = (bf16[32,384]{1,0:T(8,128)(2,1)S(1)}, bf16[32,384]{1,0:T(8,128)(2,1)S(1)}, u32[]{:S(2)}, u32[]{:S(2)}) collective-permute-start(bf16[32,384]{1,0:T(8,128)(2,1)S(1)} %get-tuple-element.59.refs_0_), channel_id=1, source_target_pairs={{0,2},{2,0},{4,6},{6,4},{1,3},{3,1},{5,7},{7,5},{8,10},{10,8},{12,... | collective-permute-start | bytes 73736 | tf_op jit(solution)/shard_map/ppermute | solution.py:452
  18.3 3.8 %collective-permute-start.5 = (bf16[32,384]{1,0:T(8,128)(2,1)S(1)}, bf16[32,384]{1,0:T(8,128)(2,1)S(1)}, u32[]{:S(2)}, u32[]{:S(2)}) collective-permute-start(bf16[32,384]{1,0:T(8,128)(2,1)S(1)} %get-tuple-element.59.refs_0_), channel_id=1, source_target_pairs={{0,4},{2,6},{4,0},{6,2},{1,5},{3,7},{5,1},{7,3},{8,12},{10,14},{12... | collective-permute-start | bytes 73736 | tf_op jit(solution)/shard_map/ppermute | solution.py:452
  19.3 3.3 %collective-permute-start.6 = (bf16[32,384]{1,0:T(8,128)(2,1)S(1)}, bf16[32,384]{1,0:T(8,128)(2,1)S(1)}, u32[]{:S(2)}, u32[]{:S(2)}) collective-permute-start(bf16[32,384]{1,0:T(8,128)(2,1)S(1)} %get-tuple-element.59.refs_0_), channel_id=1, source_target_pairs={{0,6},{2,4},{4,2},{6,0},{1,7},{3,5},{5,3},{7,1},{8,14},{10,12},{12... | collective-permute-start | bytes 73736 | tf_op jit(solution)/shard_map/ppermute | solution.py:452
  22.6 5.7 %collective-permute-start.10 = (bf16[32,384]{1,0:T(8,128)(2,1)S(1)}, bf16[32,384]{1,0:T(8,128)(2,1)S(1)}, u32[]{:S(2)}, u32[]{:S(2)}) collective-permute-start(bf16[32,384]{1,0:T(8,128)(2,1)S(1)} %add_parts.2.refs_0_), channel_id=1, source_target_pairs={{0,24},{8,16},{16,8},{24,0},{1,25},{9,17},{17,9},{25,1},{2,26},{10... | collective-permute-start | bytes 73736 | tf_op jit(solution)/shard_map/ppermute | solution.py:452
  25.8 3.9 %collective-permute-start.8 = (bf16[32,384]{1,0:T(8,128)(2,1)S(1)}, bf16[32,384]{1,0:T(8,128)(2,1)S(1)}, u32[]{:S(2)}, u32[]{:S(2)}) collective-permute-start(bf16[32,384]{1,0:T(8,128)(2,1)S(1)} %add_parts.2.refs_0_), channel_id=1, source_target_pairs={{0,8},{8,0},{16,24},{24,16},{1,9},{9,1},{17,25},{25,17},{2,10},{10... | collective-permute-start | bytes 73736 | tf_op jit(solution)/shard_map/ppermute | solution.py:452
  25.8 5.0 %collective-permute-start.9 = (bf16[32,384]{1,0:T(8,128)(2,1)S(1)}, bf16[32,384]{1,0:T(8,128)(2,1)S(1)}, u32[]{:S(2)}, u32[]{:S(2)}) collective-permute-start(bf16[32,384]{1,0:T(8,128)(2,1)S(1)} %add_parts.2.refs_0_), channel_id=1, source_target_pairs={{0,16},{8,24},{16,0},{24,8},{1,17},{9,25},{17,1},{25,9},{2,18},{10... | collective-permute-start | bytes 73736 | tf_op jit(solution)/shard_map/ppermute | solution.py:452
  30.8 3.9 %collective-permute-start.11 = (bf16[32,384]{1,0:T(8,128)(2,1)S(1)}, bf16[32,384]{1,0:T(8,128)(2,1)S(1)}, u32[]{:S(2)}, u32[]{:S(2)}) collective-permute-start(bf16[32,384]{1,0:T(8,128)(2,1)S(1)} %add_parts.3.refs_0_), channel_id=1, source_target_pairs={{0,1},{1,0},{2,3},{3,2},{4,5},{5,4},{6,7},{7,6},{8,9},{9,8},{10,11... | collective-permute-start | bytes 73736 | tf_op jit(solution)/shard_map/ppermute | solution.py:452

commit v20 on v18

--- a/solution.py
+++ b/solution.py
@@ -440,6 +440,13 @@
     return [lax.ppermute(v, axis, [(i, i ^ mask) for i in range(count)]) for mask in masks]
 
 
+def stream_round(v):
+    count, others = lax.axis_size("stream"), lax.axis_size("radial")
+    pairs = [(i * others + j, (i ^ (2 + (j + 1) % 2)) * others + j) for i in range(count) for j in range(others)]
+    apart = lax.ppermute(v, ("stream", "radial"), pairs)
+    return [*swap(v, "stream", [1]), apart, *swap(apart, "radial", [1])]
+
+
 def add(v, arrived):
     return call(add_kernel, shape(*v.shape), "add_parts")(v, *arrived)
 
@@ -506,7 +513,7 @@
         flops=2_000_000_000,
     )(rfar, rnear, fs, cs, pre, back, hidden, dpre, t1r, tbr, *const(e1t, e2t, rep1, rep2), *const(y1, y2, dtype=F32))
 
-    steps = rounds("radial", 4) + rounds("stream", 4) + rounds("snap", 2)
+    steps = rounds("radial", 4) + rounds("stream", 4)[1:] + rounds("snap", 2)
     arrived = swap(payload, *steps[0])
     hidden = call(
         functools.partial(hidden_rim_kernel, counts),
@@ -516,13 +523,12 @@
         flops=1_000_000_000,
     )(rfar, rnear, rfar_outer, rnear_outer, hidden, fs, t1o, t1d, b1)
     payload, hidden = lax.optimization_barrier((add(payload, arrived), hidden))
+    payload = add(payload, stream_round(payload))
     arrived = swap(payload, *steps[1])
-    payload = add(payload, arrived)
-    arrived = swap(payload, *steps[2])
     closure = call(
         closure_kernel, shape(*cotangent.shape), "closure", (pltpu.VMEM((640, wide), BF16),), flops=1_000_000_000
     )(hidden, t2, b2)
-    for step in steps[3:]:
+    for step in steps[2:]:
         payload = add(payload, arrived)
         arrived = swap(payload, *step)
 

time: 35.2 us -> 34.3 us (0.974)
  starting transfers between devices: 15.9 us -> 14.9 us
    ppermute x7 -> x6, starting transfers between devices: 7.68 us -> 3.5 us  [swap(): lax.ppermute(v, axis, [(i, i ^ mask) for i in range(count)])]
    ppermute x0 -> x1, starting transfers between devices: none -> 3.23 us  [stream_round(): apart = lax.ppermute(v, ('stream', 'radial'), pairs)]
    ppermute x0 -> x1, waiting for transfers between devices: none -> 2.47 us  [stream_round(): apart = lax.ppermute(v, ('stream', 'radial'), pairs)]
    ppermute x7 -> x6, waiting for transfers between devices: 5.69 us -> 3.23 us  [swap(): lax.ppermute(v, axis, [(i, i ^ mask) for i in range(count)])]
  transfers between devices with their start and end apart: 13 -> 13, of which waited for: 8 -> 7; matrix products, arithmetic and copies ran while one was open for 0% -> 0% of each run, Pallas kernels for 27% -> 28%
where the time goes in v20:
time: 34.3 us; the launch traced here: 34.1 us
  starting transfers between devices  14.9 us (43%)
  Pallas kernels  10.6 us (31%)
  waiting for transfers between devices  6.68 us (19%)
  other arithmetic  1.02 us (3%)
  between operations  0.83 us (2%)
    ppermute x3, starting transfers between devices, exchange(): return (lax.ppermute(near, axis, [(i, i ^ 1) for i in range(count)]), far)  4.15 us
    ppermute x3, starting transfers between devices, exchange(): far = lax.ppermute(far, axes, pairs)  4.02 us
    ppermute x6, starting transfers between devices, swap(): lax.ppermute(v, axis, [(i, i ^ mask) for i in range(count)])  3.5 us
    ppermute x1, starting transfers between devices, stream_round(): apart = lax.ppermute(v, ('stream', 'radial'), pairs)  3.23 us
    ppermute x6, waiting for transfers between devices, swap(): lax.ppermute(v, axis, [(i, i ^ mask) for i in range(count)])  3.23 us
    pallas_call x1, Pallas kernels, local(): call(functools.partial(rim_kernel, counts), (shape(planes, 128, Z), shape...  2.7 us
    pallas_call x1, Pallas kernels, local(): call(band_kernel, (shape(192, 768), shape(128, 384), shape(192, 768), sha...  2.7 us
    ppermute x1, waiting for transfers between devices, stream_round(): apart = lax.ppermute(v, ('stream', 'radial'), pairs)  2.47 us
  transfers between devices with their start and end apart: 13, of which 7 were waited for; matrix products, arithmetic and copies ran while one was open for 0% of the time, Pallas kernels for 28%

profile of v20, /device:TPU:0, one launch (start us, length us, event | category | flops | bytes accessed | tf_op | source)
XLA Modules:
  0.0 34.1 jit_solution(12727800363631363170)
XLA Ops:
  0.6 1.0 %pad_maximum_fusion.inputs = bf16[24,8,8,128]{3,2,1,0:T(8,128)(2,1)S(1)} fusion(bf16[16,8,8,128]{3,2,1,0:T(8,128)(2,1)} %bitcast.21, bf16[8,8,8,128]{3,2,1,0:T(8,128)(2,1)} %bitcast.22), kind=kLoop, calls=%fused_computation | loop fusion | flops 196608 | bytes 786432 | tf_op jit(solution)/shard_map/concatenate | solution.py:482
  1.7 0.0 copy-start
  1.7 0.0 copy-start.1
  1.7 0.0 copy-start.2
  1.7 0.0 copy-start.3
  1.7 0.1 pack_strips.1
  1.8 0.5 %collective-permute-start = (bf16[512,128]{1,0:T(8,128)(2,1)S(1)}, bf16[512,128]{1,0:T(8,128)(2,1)S(1)}, u32[]{:S(2)}, u32[]{:S(2)}) collective-permute-start(bf16[512,128]{1,0:T(8,128)(2,1)S(1)} %get-tuple-element.39), channel_id=1, source_target_pairs={{0,2},{2,0},{4,6},{6,4},{8,16},{10,18},{12,20},{14,22},{16,8},{18,... | collective-permute-start | bytes 393224 | tf_op jit(solution)/shard_map/ppermute | solution.py:434
  2.4 4.1 %collective-permute-start.1 = (bf16[512,128]{1,0:T(8,128)(2,1)S(1)}, bf16[512,128]{1,0:T(8,128)(2,1)S(1)}, u32[]{:S(2)}, u32[]{:S(2)}) collective-permute-start(bf16[512,128]{1,0:T(8,128)(2,1)S(1)} %get-tuple-element.40), channel_id=1, source_target_pairs={{0,8},{8,0},{16,24},{24,16},{1,9},{9,1},{17,25},{25,17},{2,10},{10... | collective-permute-start | bytes 393224 | tf_op jit(solution)/shard_map/ppermute | solution.py:435
  6.5 0.0 copy-done
  6.5 0.0 copy-done.1
  6.5 0.0 copy-done.2
  6.5 0.0 copy-done.3
  6.5 2.7 %band_matrices.1 = (bf16[192,768]{1,0:T(8,128)(2,1)S(1)}, bf16[128,384]{1,0:T(8,128)(2,1)S(1)}, bf16[192,768]{1,0:T(8,128)(2,1)S(1)}, bf16[128,1152]{1,0:T(8,128...) custom-call(bf16[128,27]{1,0:T(8,128)(2,1)S(1)} %bitcast.18, ...), custom_call_target="tpu_custom_call" | custom-call | flops 4000000000 | bytes 1000000 | tf_op jit(solution)/shard_map/band_matrices/pallas_call | solution.py:486
  9.2 0.0 collective-permute-done.xfar
  9.2 0.5 %collective-permute-done.1.xnear = bf16[512,128]{1,0:T(8,128)(2,1)S(1)} collective-permute-done((bf16[512,128]{1,0:T(8,128)(2,1)S(1)}, bf16[512,128]{1,0:T(8,128)(2,1)S(1)}, u32[]{:S(2)}, u32[]{:S(2)}) %collective-permute-start.1) | collective-permute-done | bytes 131104 | tf_op jit(solution)/shard_map/ppermute | solution.py:435
  9.7 0.3 join_strips.1
  10.0 1.8 %collective-permute-start.2 = (bf16[576,128]{1,0:T(8,128)(2,1)S(1)}, bf16[576,128]{1,0:T(8,128)(2,1)S(1)}, u32[]{:S(2)}, u32[]{:S(2)}) collective-permute-start(bf16[576,128]{1,0:T(8,128)(2,1)S(1)} %get-tuple-element.47), channel_id=1, source_target_pairs={{0,8},{8,0},{16,24},{24,16},{2,4},{10,12},{18,20},{26,28},{4,2},{1... | collective-permute-start | bytes 442376 | tf_op jit(solution)/shard_map/ppermute | solution.py:434
  11.8 0.0 collective-permute-start.3
  11.8 0.0 copy-start.4
  11.8 0.0 copy-start.5
  11.8 0.0 copy-start.6
  11.8 0.0 copy-start.7
  11.9 0.0 copy-start.8
  11.9 0.0 copy-start.9
  11.9 0.9 %own_rows.1 = (bf16[256,2048]{1,0:T(8,128)(2,1)S(1)}, bf16[384,1536]{1,0:T(8,128)(2,1)S(1)}, f32[64,1024]{1,0:T(8,128)S(1)}, f32[64,1024]{1,0:T(8,128)S(1)}, bf1...) custom-call(bf16[512,128]{1,0:T(8,128)(2,1)S(1)} %collective-permute-done.xfar, ...), custom_call_target="tpu_custom_call" | custom-call | flops 1000000000 | bytes 1000000 | tf_op jit(solution)/shard_map/own_rows/pallas_call | solution.py:498
  12.8 0.2 join_outer.1
  13.0 1.7 %collective-permute-start.7 = (bf16[320,128]{1,0:T(8,128)(2,1)S(1)}, bf16[320,128]{1,0:T(8,128)(2,1)S(1)}, u32[]{:S(2)}, u32[]{:S(2)}) collective-permute-start(bf16[320,128]{1,0:T(8,128)(2,1)S(1)} %get-tuple-element.63), channel_id=1, source_target_pairs={{0,8},{8,0},{16,24},{24,16},{2,4},{10,12},{18,20},{26,28},{4,2},{1... | collective-permute-start | bytes 245768 | tf_op jit(solution)/shard_map/ppermute | solution.py:434
  14.7 0.0 collective-permute-start.8
  14.7 0.5 %collective-permute-done.2.rfar = bf16[576,128]{1,0:T(8,128)(2,1)S(1)} collective-permute-done((bf16[576,128]{1,0:T(8,128)(2,1)S(1)}, bf16[576,128]{1,0:T(8,128)(2,1)S(1)}, u32[]{:S(2)}, u32[]{:S(2)}) %collective-permute-start.2) | collective-permute-done | bytes 147488 | tf_op jit(solution)/shard_map/ppermute | solution.py:434
  15.2 0.0 collective-permute-done.3.rnear
  15.2 0.0 copy-done.4
  15.2 0.0 copy-done.5
  15.2 0.0 copy-done.6
  15.2 0.0 copy-done.7
  15.3 0.0 copy-done.8
  15.3 0.0 copy-done.9
  15.3 2.7 %gradients.1 = (bf16[8,128,128]{2,1,0:T(8,128)(2,1)S(1)}, bf16[32,384]{1,0:T(8,128)(2,1)S(1)}) custom-call(bf16[576,128]{1,0:T(8,128)(2,1)S(1)} %collective-permute-done.2.rfar, bf16[576,128]{1,0:T(8,128)(2,1)S(1)} %collective-permute-done.3.rnear, bf16[256,2048]{1,0:T(8,128)(2,1)S(1)} %get-tuple-element.53.fs, bf16[384,1536]{1,0:T(8,128)(2,1)S(1)} %get-tuple-element.54.cs, ...), custom_call_target="tpu_custom_call" | custom-call | flops 2000000000 | bytes 1000000 | tf_op jit(solution)/shard_map/gradients/pallas_call | solution.py:508
  18.0 0.1 collective-permute-start.4
  18.1 1.0 %collective-permute-start.5 = (bf16[32,384]{1,0:T(8,128)(2,1)S(1)}, bf16[32,384]{1,0:T(8,128)(2,1)S(1)}, u32[]{:S(2)}, u32[]{:S(2)}) collective-permute-start(bf16[32,384]{1,0:T(8,128)(2,1)S(1)} %get-tuple-element.61.refs_0_), channel_id=1, source_target_pairs={{0,4},{2,6},{4,0},{6,2},{1,5},{3,7},{5,1},{7,3},{8,12},{10,14},{12... | collective-permute-start | bytes 73736 | tf_op jit(solution)/shard_map/ppermute | solution.py:440
  19.1 0.9 %collective-permute-start.6 = (bf16[32,384]{1,0:T(8,128)(2,1)S(1)}, bf16[32,384]{1,0:T(8,128)(2,1)S(1)}, u32[]{:S(2)}, u32[]{:S(2)}) collective-permute-start(bf16[32,384]{1,0:T(8,128)(2,1)S(1)} %get-tuple-element.61.refs_0_), channel_id=1, source_target_pairs={{0,6},{2,4},{4,2},{6,0},{1,7},{3,5},{5,3},{7,1},{8,14},{10,12},{12... | collective-permute-start | bytes 73736 | tf_op jit(solution)/shard_map/ppermute | solution.py:440
  19.9 0.0 collective-permute-done.7.rfar_outer
  19.9 0.0 collective-permute-done.8.rnear_outer
  19.9 1.3 %hidden_rim.1.hidden = bf16[12,192,128]{2,1,0:T(8,128)(2,1)S(1)} custom-call(bf16[576,128]{1,0:T(8,128)(2,1)S(1)} %collective-permute-done.2.rfar, bf16[576,128]{1,0:T(8,128)(2,1)S(1)} %collective-permute-done.3.rnear, bf16[320,128]{1,0:T(8,128)(2,1)S(1)} %collective-permute-done.7.rfar_outer, bf16[320,128]{1,0:T(8,128)(2,1)S(1)} %collective-permute-done.8.rnear_outer, ...), custom_call_target="tpu_custom_call" | custom-call | flops 1000000000 | bytes 1000000 | tf_op jit(solution)/shard_map/hidden_rim/pallas_call | solution.py:518
  21.2 0.0 collective-permute-done.4.refs_1_
  21.2 0.7 %collective-permute-done.5.refs_2_ = bf16[32,384]{1,0:T(8,128)(2,1)S(1)} collective-permute-done((bf16[32,384]{1,0:T(8,128)(2,1)S(1)}, bf16[32,384]{1,0:T(8,128)(2,1)S(1)}, u32[]{:S(2)}, u32[]{:S(2)}) %collective-permute-start.5) | collective-permute-done | bytes 24608 | tf_op jit(solution)/shard_map/ppermute | solution.py:440
  22.0 0.4 %collective-permute-done.6.refs_3_ = bf16[32,384]{1,0:T(8,128)(2,1)S(1)} collective-permute-done((bf16[32,384]{1,0:T(8,128)(2,1)S(1)}, bf16[32,384]{1,0:T(8,128)(2,1)S(1)}, u32[]{:S(2)}, u32[]{:S(2)}) %collective-permute-start.6) | collective-permute-done | bytes 24608 | tf_op jit(solution)/shard_map/ppermute | solution.py:440
  22.3 3.2 %collective-permute-start.10 = (bf16[32,384]{1,0:T(8,128)(2,1)S(1)}, bf16[32,384]{1,0:T(8,128)(2,1)S(1)}, u32[]{:S(2)}, u32[]{:S(2)}) collective-permute-start(bf16[32,384]{1,0:T(8,128)(2,1)S(1)} %add_parts.2.refs_0_), channel_id=1, source_target_pairs={{0,24},{2,18},{4,28},{6,22},{8,16},{10,26},{12,20},{14,30},{16,8},... | collective-permute-start | bytes 73736 | tf_op jit(solution)/shard_map/ppermute | solution.py:446
  25.6 0.0 collective-permute-start.9
  25.6 2.5 %collective-permute-done.10.refs_2_ = bf16[32,384]{1,0:T(8,128)(2,1)S(1)} collective-permute-done((bf16[32,384]{1,0:T(8,128)(2,1)S(1)}, bf16[32,384]{1,0:T(8,128)(2,1)S(1)}, u32[]{:S(2)}, u32[]{:S(2)}) %collective-permute-start.10) | collective-permute-done | bytes 24608 | tf_op jit(solution)/shard_map/ppermute | solution.py:446
  28.0 0.0 collective-permute-start.11
  28.1 1.4 %collective-permute-done.9.refs_1_ = bf16[32,384]{1,0:T(8,128)(2,1)S(1)} collective-permute-done((bf16[32,384]{1,0:T(8,128)(2,1)S(1)}, bf16[32,384]{1,0:T(8,128)(2,1)S(1)}, u32[]{:S(2)}, u32[]{:S(2)}) %collective-permute-start.9) | collective-permute-done | bytes 24608 | tf_op jit(solution)/shard_map/ppermute | solution.py:440
  29.4 0.0 collective-permute-done.11.refs_3_
  29.4 1.6 %collective-permute-start.12 = (bf16[32,384]{1,0:T(8,128)(2,1)S(1)}, bf16[32,384]{1,0:T(8,128)(2,1)S(1)}, u32[]{:S(2)}, u32[]{:S(2)}) collective-permute-start(bf16[32,384]{1,0:T(8,128)(2,1)S(1)} %add_parts.3.refs_0_), channel_id=1, source_target_pairs={{0,1},{1,0},{2,3},{3,2},{4,5},{5,4},{6,7},{7,6},{8,9},{9,8},{10,11... | collective-permute-start | bytes 73736 | tf_op jit(solution)/shard_map/ppermute | solution.py:440
  31.0 1.6 %closure.1 = bf16[1,16,8,8,128]{4,3,2,1,0:T(8,128)(2,1)} custom-call(bf16[12,192,128]{2,1,0:T(8,128)(2,1)S(1)} %hidden_rim.1.hidden, bf16[128,1920]{1,0:T(8,128)(2,1)S(1)} %get-tuple-element.68.t2, f32[128,128]{1,0:T(8,128)S(1)} %get-tuple-element.69.b2), custom_call_target="tpu_custom_call" | custom-call | flops 1000000000 | bytes 1000000 | tf_op jit(solution)/shard_map/closure/pallas_call | solution.py:528
  32.6 0.8 %collective-permute-done.12.refs_1_ = bf16[32,384]{1,0:T(8,128)(2,1)S(1)} collective-permute-done((bf16[32,384]{1,0:T(8,128)(2,1)S(1)}, bf16[32,384]{1,0:T(8,128)(2,1)S(1)}, u32[]{:S(2)}, u32[]{:S(2)}) %collective-permute-start.12) | collective-permute-done | bytes 24608 | tf_op jit(solution)/shard_map/ppermute | solution.py:440
  33.3 0.8 %finish.1 = (f32[128,27]{1,0:T(8,128)}, f32[256,27]{1,0:T(8,128)}, f32[1,16]{1,0:T(1,128)}) custom-call(bf16[32,384]{1,0:T(8,128)(2,1)S(1)} %add_parts.3.refs_0_, bf16[32,384]{1,0:T(8,128)(2,1)S(1)} %collective-permute-done.12.refs_1_), custom_call_target="tpu_custom_call" | custom-call | flops 10000000 | bytes 1000000 | tf_op jit(solution)/shard_map/finish/pallas_call | solution.py:539
  (2 shorter events, 0.0 us)
Async XLA Ops:
  1.7 4.8 %copy-start = (bf16[27,16,16]{0,2,1:T(8,128)(2,1)S(1)}, bf16[27,16,16]{0,2,1:T(8,128)(2,1)}, u32[]{:S(2)}) copy-start(bf16[27,16,16]{0,2,1:T(8,128)(2,1)} %param.15) | copy-start | bytes 41476
  1.7 4.8 %copy-start.1 = (bf16[27,16,8]{0,2,1:T(8,128)(2,1)S(1)}, bf16[27,16,8]{0,2,1:T(8,128)(2,1)}, u32[]{:S(2)}) copy-start(bf16[27,16,8]{0,2,1:T(8,128)(2,1)} %param.13) | copy-start | bytes 20740
  1.7 4.8 %copy-start.2 = (f32[16]{0:T(128)S(1)}, f32[16]{0:T(128)}, u32[]{:S(2)}) copy-start(f32[16]{0:T(128)} %param.14) | copy-start | bytes 196
  1.7 4.8 %copy-start.3 = (f32[16]{0:T(128)S(1)}, f32[16]{0:T(128)}, u32[]{:S(2)}) copy-start(f32[16]{0:T(128)} %param.16) | copy-start | bytes 196
  1.8 7.4 %collective-permute-start = (bf16[512,128]{1,0:T(8,128)(2,1)S(1)}, bf16[512,128]{1,0:T(8,128)(2,1)S(1)}, u32[]{:S(2)}, u32[]{:S(2)}) collective-permute-start(bf16[512,128]{1,0:T(8,128)(2,1)S(1)} %get-tuple-element.39), channel_id=1, source_target_pairs={{0,2},{2,0},{4,6},{6,4},{8,16},{10,18},{12,20},{14,22},{16,8},{18,... | collective-permute-start | bytes 393224 | tf_op jit(solution)/shard_map/ppermute | solution.py:434
  2.4 7.4 %collective-permute-start.1 = (bf16[512,128]{1,0:T(8,128)(2,1)S(1)}, bf16[512,128]{1,0:T(8,128)(2,1)S(1)}, u32[]{:S(2)}, u32[]{:S(2)}) collective-permute-start(bf16[512,128]{1,0:T(8,128)(2,1)S(1)} %get-tuple-element.40), channel_id=1, source_target_pairs={{0,8},{8,0},{16,24},{24,16},{1,9},{9,1},{17,25},{25,17},{2,10},{10... | collective-permute-start | bytes 393224 | tf_op jit(solution)/shard_map/ppermute | solution.py:435
  10.0 5.2 %collective-permute-start.2 = (bf16[576,128]{1,0:T(8,128)(2,1)S(1)}, bf16[576,128]{1,0:T(8,128)(2,1)S(1)}, u32[]{:S(2)}, u32[]{:S(2)}) collective-permute-start(bf16[576,128]{1,0:T(8,128)(2,1)S(1)} %get-tuple-element.47), channel_id=1, source_target_pairs={{0,8},{8,0},{16,24},{24,16},{2,4},{10,12},{18,20},{26,28},{4,2},{1... | collective-permute-start | bytes 442376 | tf_op jit(solution)/shard_map/ppermute | solution.py:434
  11.8 3.4 %collective-permute-start.3 = (bf16[576,128]{1,0:T(8,128)(2,1)S(1)}, bf16[576,128]{1,0:T(8,128)(2,1)S(1)}, u32[]{:S(2)}, u32[]{:S(2)}) collective-permute-start(bf16[576,128]{1,0:T(8,128)(2,1)S(1)} %get-tuple-element.48), channel_id=1, source_target_pairs={{0,2},{2,0},{4,6},{6,4},{1,3},{3,1},{5,7},{7,5},{8,10},{10,8},{12,... | collective-permute-start | bytes 442376 | tf_op jit(solution)/shard_map/ppermute | solution.py:435
  11.8 3.4 %copy-start.4 = (bf16[128,768]{1,0:T(8,128)(2,1)S(1)}, bf16[128,768]{1,0:T(8,128)(2,1)}, u32[]{:S(2)}) copy-start(bf16[128,768]{1,0:T(8,128)(2,1)} %constant.15.clone.rep2) | copy-start | bytes 589828
  11.8 3.4 %copy-start.5 = (bf16[640,128]{1,0:T(8,128)(2,1)S(1)}, bf16[640,128]{1,0:T(8,128)(2,1)}, u32[]{:S(2)}) copy-start(bf16[640,128]{1,0:T(8,128)(2,1)} %constant.13.clone.e2t) | copy-start | bytes 491524
  11.8 3.4 %copy-start.6 = (bf16[384,128]{1,0:T(8,128)(2,1)S(1)}, bf16[384,128]{1,0:T(8,128)(2,1)}, u32[]{:S(2)}) copy-start(bf16[384,128]{1,0:T(8,128)(2,1)} %constant.12.clone.e1t) | copy-start | bytes 294916
  11.8 3.4 %copy-start.7 = (bf16[128,384]{1,0:T(8,128)(2,1)S(1)}, bf16[128,384]{1,0:T(8,128)(2,1)}, u32[]{:S(2)}) copy-start(bf16[128,384]{1,0:T(8,128)(2,1)} %constant.14.clone.rep1) | copy-start | bytes 294916
  11.9 3.4 %copy-start.8 = (f32[1,640]{1,0:T(1,128)S(1)}, f32[1,640]{1,0:T(1,128)}, u32[]{:S(2)}) copy-start(f32[1,640]{1,0:T(1,128)} %constant.17.clone.y2) | copy-start | bytes 7684
  11.9 3.4 %copy-start.9 = (f32[1,384]{1,0:T(1,128)S(1)}, f32[1,384]{1,0:T(1,128)}, u32[]{:S(2)}) copy-start(f32[1,384]{1,0:T(1,128)} %constant.16.clone.y1) | copy-start | bytes 4612
  13.0 6.9 %collective-permute-start.7 = (bf16[320,128]{1,0:T(8,128)(2,1)S(1)}, bf16[320,128]{1,0:T(8,128)(2,1)S(1)}, u32[]{:S(2)}, u32[]{:S(2)}) collective-permute-start(bf16[320,128]{1,0:T(8,128)(2,1)S(1)} %get-tuple-element.63), channel_id=1, source_target_pairs={{0,8},{8,0},{16,24},{24,16},{2,4},{10,12},{18,20},{26,28},{4,2},{1... | collective-permute-start | bytes 245768 | tf_op jit(solution)/shard_map/ppermute | solution.py:434
  14.7 5.2 %collective-permute-start.8 = (bf16[320,128]{1,0:T(8,128)(2,1)S(1)}, bf16[320,128]{1,0:T(8,128)(2,1)S(1)}, u32[]{:S(2)}, u32[]{:S(2)}) collective-permute-start(bf16[320,128]{1,0:T(8,128)(2,1)S(1)} %get-tuple-element.64), channel_id=1, source_target_pairs={{0,2},{2,0},{4,6},{6,4},{1,3},{3,1},{5,7},{7,5},{8,10},{10,8},{12,... | collective-permute-start | bytes 245768 | tf_op jit(solution)/shard_map/ppermute | solution.py:435
  18.0 3.2 %collective-permute-start.4 = (bf16[32,384]{1,0:T(8,128)(2,1)S(1)}, bf16[32,384]{1,0:T(8,128)(2,1)S(1)}, u32[]{:S(2)}, u32[]{:S(2)}) collective-permute-start(bf16[32,384]{1,0:T(8,128)(2,1)S(1)} %get-tuple-element.61.refs_0_), channel_id=1, source_target_pairs={{0,2},{2,0},{4,6},{6,4},{1,3},{3,1},{5,7},{7,5},{8,10},{10,8},{12,... | collective-permute-start | bytes 73736 | tf_op jit(solution)/shard_map/ppermute | solution.py:440
  18.1 3.9 %collective-permute-start.5 = (bf16[32,384]{1,0:T(8,128)(2,1)S(1)}, bf16[32,384]{1,0:T(8,128)(2,1)S(1)}, u32[]{:S(2)}, u32[]{:S(2)}) collective-permute-start(bf16[32,384]{1,0:T(8,128)(2,1)S(1)} %get-tuple-element.61.refs_0_), channel_id=1, source_target_pairs={{0,4},{2,6},{4,0},{6,2},{1,5},{3,7},{5,1},{7,3},{8,12},{10,14},{12... | collective-permute-start | bytes 73736 | tf_op jit(solution)/shard_map/ppermute | solution.py:440
  19.1 3.3 %collective-permute-start.6 = (bf16[32,384]{1,0:T(8,128)(2,1)S(1)}, bf16[32,384]{1,0:T(8,128)(2,1)S(1)}, u32[]{:S(2)}, u32[]{:S(2)}) collective-permute-start(bf16[32,384]{1,0:T(8,128)(2,1)S(1)} %get-tuple-element.61.refs_0_), channel_id=1, source_target_pairs={{0,6},{2,4},{4,2},{6,0},{1,7},{3,5},{5,3},{7,1},{8,14},{10,12},{12... | collective-permute-start | bytes 73736 | tf_op jit(solution)/shard_map/ppermute | solution.py:440
  22.3 5.7 %collective-permute-start.10 = (bf16[32,384]{1,0:T(8,128)(2,1)S(1)}, bf16[32,384]{1,0:T(8,128)(2,1)S(1)}, u32[]{:S(2)}, u32[]{:S(2)}) collective-permute-start(bf16[32,384]{1,0:T(8,128)(2,1)S(1)} %add_parts.2.refs_0_), channel_id=1, source_target_pairs={{0,24},{2,18},{4,28},{6,22},{8,16},{10,26},{12,20},{14,30},{16,8},... | collective-permute-start | bytes 73736 | tf_op jit(solution)/shard_map/ppermute | solution.py:446
  25.6 3.8 %collective-permute-start.9 = (bf16[32,384]{1,0:T(8,128)(2,1)S(1)}, bf16[32,384]{1,0:T(8,128)(2,1)S(1)}, u32[]{:S(2)}, u32[]{:S(2)}) collective-permute-start(bf16[32,384]{1,0:T(8,128)(2,1)S(1)} %add_parts.2.refs_0_), channel_id=1, source_target_pairs={{0,8},{8,0},{16,24},{24,16},{1,9},{9,1},{17,25},{25,17},{2,10},{10... | collective-permute-start | bytes 73736 | tf_op jit(solution)/shard_map/ppermute | solution.py:440
  28.0 1.4 %collective-permute-start.11 = (bf16[32,384]{1,0:T(8,128)(2,1)S(1)}, bf16[32,384]{1,0:T(8,128)(2,1)S(1)}, u32[]{:S(2)}, u32[]{:S(2)}) collective-permute-start(bf16[32,384]{1,0:T(8,128)(2,1)S(1)} %collective-permute-done.10.refs_2_), channel_id=1, source_target_pairs={{0,2},{2,0},{4,6},{6,4},{1,3},{3,1},{5,7},{7,5},{8,10},{10,8},{12,... | collective-permute-start | bytes 73736 | tf_op jit(solution)/shard_map/ppermute | solution.py:440
  29.4 3.9 %collective-permute-start.12 = (bf16[32,384]{1,0:T(8,128)(2,1)S(1)}, bf16[32,384]{1,0:T(8,128)(2,1)S(1)}, u32[]{:S(2)}, u32[]{:S(2)}) collective-permute-start(bf16[32,384]{1,0:T(8,128)(2,1)S(1)} %add_parts.3.refs_0_), channel_id=1, source_target_pairs={{0,1},{1,0},{2,3},{3,2},{4,5},{5,4},{6,7},{7,6},{8,9},{9,8},{10,11... | collective-permute-start | bytes 73736 | tf_op jit(solution)/shard_map/ppermute | solution.py:440

commit v21 on v20

--- a/solution.py
+++ b/solution.py
@@ -442,9 +442,9 @@
 
 def stream_round(v):
     count, others = lax.axis_size("stream"), lax.axis_size("radial")
-    pairs = [(i * others + j, (i ^ (2 + (j + 1) % 2)) * others + j) for i in range(count) for j in range(others)]
+    pairs = [(i * others + j, (i ^ (1 + j % 2)) * others + j) for i in range(count) for j in range(others)]
     apart = lax.ppermute(v, ("stream", "radial"), pairs)
-    return [*swap(v, "stream", [1]), apart, *swap(apart, "radial", [1])]
+    return [*swap(v, "stream", [3]), apart, *swap(apart, "radial", [1])]
 
 
 def add(v, arrived):

time: 34.3 us -> 34.7 us (1.012)
    ppermute x6, waiting for transfers between devices: 3.23 us -> 5.16 us  [swap(): lax.ppermute(v, axis, [(i, i ^ mask) for i in range(count)])]
    ppermute x1, waiting for transfers between devices: 2.47 us -> 0.66 us  [stream_round(): apart = lax.ppermute(v, ('stream', 'radial'), pairs)]
    ppermute x6, starting transfers between devices: 3.5 us -> 5.18 us  [swap(): lax.ppermute(v, axis, [(i, i ^ mask) for i in range(count)])]
    ppermute x1, starting transfers between devices: 3.23 us -> 1.82 us  [stream_round(): apart = lax.ppermute(v, ('stream', 'radial'), pairs)]
  transfers between devices with their start and end apart: 13 -> 13, of which waited for: 7 -> 7; matrix products, arithmetic and copies ran while one was open for 0% -> 0% of each run, Pallas kernels for 28% -> 27%
where the time goes in v21:
time: 34.7 us; the launch traced here: 34.5 us
  starting transfers between devices  15.2 us (44%)
  Pallas kernels  10.6 us (31%)
  waiting for transfers between devices  6.8 us (20%)
  other arithmetic  1.02 us (3%)
  between operations  0.83 us (2%)
    ppermute x6, starting transfers between devices, swap(): lax.ppermute(v, axis, [(i, i ^ mask) for i in range(count)])  5.18 us
    ppermute x6, waiting for transfers between devices, swap(): lax.ppermute(v, axis, [(i, i ^ mask) for i in range(count)])  5.16 us
    ppermute x3, starting transfers between devices, exchange(): return (lax.ppermute(near, axis, [(i, i ^ 1) for i in range(count)]), far)  4.15 us
    ppermute x3, starting transfers between devices, exchange(): far = lax.ppermute(far, axes, pairs)  4.02 us
    pallas_call x1, Pallas kernels, local(): call(functools.partial(rim_kernel, counts), (shape(planes, 128, Z), shape...  2.7 us
    pallas_call x1, Pallas kernels, local(): call(band_kernel, (shape(192, 768), shape(128, 384), shape(192, 768), sha...  2.7 us
    ppermute x1, starting transfers between devices, stream_round(): apart = lax.ppermute(v, ('stream', 'radial'), pairs)  1.82 us
    pallas_call x1, Pallas kernels, local(): call(closure_kernel, shape(*cotangent.shape), 'closure', (pltpu.VMEM((640...  1.57 us
  transfers between devices with their start and end apart: 13, of which 7 were waited for; matrix products, arithmetic and copies ran while one was open for 0% of the time, Pallas kernels for 27%

profile of v21, /device:TPU:0, one launch (start us, length us, event | category | flops | bytes accessed | tf_op | source)
XLA Modules:
  0.0 34.5 jit_solution(9414465475222620704)
XLA Ops:
  0.6 1.0 %pad_maximum_fusion.inputs = bf16[24,8,8,128]{3,2,1,0:T(8,128)(2,1)S(1)} fusion(bf16[16,8,8,128]{3,2,1,0:T(8,128)(2,1)} %bitcast.21, bf16[8,8,8,128]{3,2,1,0:T(8,128)(2,1)} %bitcast.22), kind=kLoop, calls=%fused_computation | loop fusion | flops 196608 | bytes 786432 | tf_op jit(solution)/shard_map/concatenate | solution.py:482
  1.7 0.0 copy-start
  1.7 0.0 copy-start.1
  1.7 0.0 copy-start.2
  1.7 0.0 copy-start.3
  1.7 0.1 pack_strips.1
  1.8 0.5 %collective-permute-start = (bf16[512,128]{1,0:T(8,128)(2,1)S(1)}, bf16[512,128]{1,0:T(8,128)(2,1)S(1)}, u32[]{:S(2)}, u32[]{:S(2)}) collective-permute-start(bf16[512,128]{1,0:T(8,128)(2,1)S(1)} %get-tuple-element.39), channel_id=1, source_target_pairs={{0,2},{2,0},{4,6},{6,4},{8,16},{10,18},{12,20},{14,22},{16,8},{18,... | collective-permute-start | bytes 393224 | tf_op jit(solution)/shard_map/ppermute | solution.py:434
  2.4 4.1 %collective-permute-start.1 = (bf16[512,128]{1,0:T(8,128)(2,1)S(1)}, bf16[512,128]{1,0:T(8,128)(2,1)S(1)}, u32[]{:S(2)}, u32[]{:S(2)}) collective-permute-start(bf16[512,128]{1,0:T(8,128)(2,1)S(1)} %get-tuple-element.40), channel_id=1, source_target_pairs={{0,8},{8,0},{16,24},{24,16},{1,9},{9,1},{17,25},{25,17},{2,10},{10... | collective-permute-start | bytes 393224 | tf_op jit(solution)/shard_map/ppermute | solution.py:435
  6.5 0.0 copy-done
  6.5 0.0 copy-done.1
  6.5 0.0 copy-done.2
  6.5 0.0 copy-done.3
  6.5 2.7 %band_matrices.1 = (bf16[192,768]{1,0:T(8,128)(2,1)S(1)}, bf16[128,384]{1,0:T(8,128)(2,1)S(1)}, bf16[192,768]{1,0:T(8,128)(2,1)S(1)}, bf16[128,1152]{1,0:T(8,128...) custom-call(bf16[128,27]{1,0:T(8,128)(2,1)S(1)} %bitcast.18, ...), custom_call_target="tpu_custom_call" | custom-call | flops 4000000000 | bytes 1000000 | tf_op jit(solution)/shard_map/band_matrices/pallas_call | solution.py:486
  9.2 0.0 collective-permute-done.xfar
  9.2 0.5 %collective-permute-done.1.xnear = bf16[512,128]{1,0:T(8,128)(2,1)S(1)} collective-permute-done((bf16[512,128]{1,0:T(8,128)(2,1)S(1)}, bf16[512,128]{1,0:T(8,128)(2,1)S(1)}, u32[]{:S(2)}, u32[]{:S(2)}) %collective-permute-start.1) | collective-permute-done | bytes 131104 | tf_op jit(solution)/shard_map/ppermute | solution.py:435
  9.7 0.3 join_strips.1
  10.0 1.8 %collective-permute-start.2 = (bf16[576,128]{1,0:T(8,128)(2,1)S(1)}, bf16[576,128]{1,0:T(8,128)(2,1)S(1)}, u32[]{:S(2)}, u32[]{:S(2)}) collective-permute-start(bf16[576,128]{1,0:T(8,128)(2,1)S(1)} %get-tuple-element.47), channel_id=1, source_target_pairs={{0,8},{8,0},{16,24},{24,16},{2,4},{10,12},{18,20},{26,28},{4,2},{1... | collective-permute-start | bytes 442376 | tf_op jit(solution)/shard_map/ppermute | solution.py:434
  11.8 0.0 collective-permute-start.3
  11.8 0.0 copy-start.4
  11.8 0.0 copy-start.5
  11.8 0.0 copy-start.6
  11.8 0.0 copy-start.7
  11.9 0.0 copy-start.8
  11.9 0.0 copy-start.9
  11.9 0.9 %own_rows.1 = (bf16[256,2048]{1,0:T(8,128)(2,1)S(1)}, bf16[384,1536]{1,0:T(8,128)(2,1)S(1)}, f32[64,1024]{1,0:T(8,128)S(1)}, f32[64,1024]{1,0:T(8,128)S(1)}, bf1...) custom-call(bf16[512,128]{1,0:T(8,128)(2,1)S(1)} %collective-permute-done.xfar, ...), custom_call_target="tpu_custom_call" | custom-call | flops 1000000000 | bytes 1000000 | tf_op jit(solution)/shard_map/own_rows/pallas_call | solution.py:498
  12.8 0.2 join_outer.1
  13.0 1.7 %collective-permute-start.7 = (bf16[320,128]{1,0:T(8,128)(2,1)S(1)}, bf16[320,128]{1,0:T(8,128)(2,1)S(1)}, u32[]{:S(2)}, u32[]{:S(2)}) collective-permute-start(bf16[320,128]{1,0:T(8,128)(2,1)S(1)} %get-tuple-element.63), channel_id=1, source_target_pairs={{0,8},{8,0},{16,24},{24,16},{2,4},{10,12},{18,20},{26,28},{4,2},{1... | collective-permute-start | bytes 245768 | tf_op jit(solution)/shard_map/ppermute | solution.py:434
  14.7 0.0 collective-permute-start.8
  14.7 0.5 %collective-permute-done.2.rfar = bf16[576,128]{1,0:T(8,128)(2,1)S(1)} collective-permute-done((bf16[576,128]{1,0:T(8,128)(2,1)S(1)}, bf16[576,128]{1,0:T(8,128)(2,1)S(1)}, u32[]{:S(2)}, u32[]{:S(2)}) %collective-permute-start.2) | collective-permute-done | bytes 147488 | tf_op jit(solution)/shard_map/ppermute | solution.py:434
  15.2 0.0 collective-permute-done.3.rnear
  15.2 0.0 copy-done.4
  15.2 0.0 copy-done.5
  15.2 0.0 copy-done.6
  15.2 0.0 copy-done.7
  15.3 0.0 copy-done.8
  15.3 0.0 copy-done.9
  15.3 2.7 %gradients.1 = (bf16[8,128,128]{2,1,0:T(8,128)(2,1)S(1)}, bf16[32,384]{1,0:T(8,128)(2,1)S(1)}) custom-call(bf16[576,128]{1,0:T(8,128)(2,1)S(1)} %collective-permute-done.2.rfar, bf16[576,128]{1,0:T(8,128)(2,1)S(1)} %collective-permute-done.3.rnear, bf16[256,2048]{1,0:T(8,128)(2,1)S(1)} %get-tuple-element.53.fs, bf16[384,1536]{1,0:T(8,128)(2,1)S(1)} %get-tuple-element.54.cs, ...), custom_call_target="tpu_custom_call" | custom-call | flops 2000000000 | bytes 1000000 | tf_op jit(solution)/shard_map/gradients/pallas_call | solution.py:508
  18.0 0.1 collective-permute-start.4
  18.1 1.0 %collective-permute-start.5 = (bf16[32,384]{1,0:T(8,128)(2,1)S(1)}, bf16[32,384]{1,0:T(8,128)(2,1)S(1)}, u32[]{:S(2)}, u32[]{:S(2)}) collective-permute-start(bf16[32,384]{1,0:T(8,128)(2,1)S(1)} %get-tuple-element.61.refs_0_), channel_id=1, source_target_pairs={{0,4},{2,6},{4,0},{6,2},{1,5},{3,7},{5,1},{7,3},{8,12},{10,14},{12... | collective-permute-start | bytes 73736 | tf_op jit(solution)/shard_map/ppermute | solution.py:440
  19.1 0.9 %collective-permute-start.6 = (bf16[32,384]{1,0:T(8,128)(2,1)S(1)}, bf16[32,384]{1,0:T(8,128)(2,1)S(1)}, u32[]{:S(2)}, u32[]{:S(2)}) collective-permute-start(bf16[32,384]{1,0:T(8,128)(2,1)S(1)} %get-tuple-element.61.refs_0_), channel_id=1, source_target_pairs={{0,6},{2,4},{4,2},{6,0},{1,7},{3,5},{5,3},{7,1},{8,14},{10,12},{12... | collective-permute-start | bytes 73736 | tf_op jit(solution)/shard_map/ppermute | solution.py:440
  19.9 0.0 collective-permute-done.7.rfar_outer
  19.9 0.0 collective-permute-done.8.rnear_outer
  19.9 1.3 %hidden_rim.1.hidden = bf16[12,192,128]{2,1,0:T(8,128)(2,1)S(1)} custom-call(bf16[576,128]{1,0:T(8,128)(2,1)S(1)} %collective-permute-done.2.rfar, bf16[576,128]{1,0:T(8,128)(2,1)S(1)} %collective-permute-done.3.rnear, bf16[320,128]{1,0:T(8,128)(2,1)S(1)} %collective-permute-done.7.rfar_outer, bf16[320,128]{1,0:T(8,128)(2,1)S(1)} %collective-permute-done.8.rnear_outer, ...), custom_call_target="tpu_custom_call" | custom-call | flops 1000000000 | bytes 1000000 | tf_op jit(solution)/shard_map/hidden_rim/pallas_call | solution.py:518
  21.2 0.0 collective-permute-done.4.refs_1_
  21.2 0.7 %collective-permute-done.5.refs_2_ = bf16[32,384]{1,0:T(8,128)(2,1)S(1)} collective-permute-done((bf16[32,384]{1,0:T(8,128)(2,1)S(1)}, bf16[32,384]{1,0:T(8,128)(2,1)S(1)}, u32[]{:S(2)}, u32[]{:S(2)}) %collective-permute-start.5) | collective-permute-done | bytes 24608 | tf_op jit(solution)/shard_map/ppermute | solution.py:440
  22.0 0.4 %collective-permute-done.6.refs_3_ = bf16[32,384]{1,0:T(8,128)(2,1)S(1)} collective-permute-done((bf16[32,384]{1,0:T(8,128)(2,1)S(1)}, bf16[32,384]{1,0:T(8,128)(2,1)S(1)}, u32[]{:S(2)}, u32[]{:S(2)}) %collective-permute-start.6) | collective-permute-done | bytes 24608 | tf_op jit(solution)/shard_map/ppermute | solution.py:440
  22.3 1.8 %collective-permute-start.10 = (bf16[32,384]{1,0:T(8,128)(2,1)S(1)}, bf16[32,384]{1,0:T(8,128)(2,1)S(1)}, u32[]{:S(2)}, u32[]{:S(2)}) collective-permute-start(bf16[32,384]{1,0:T(8,128)(2,1)S(1)} %add_parts.2.refs_0_), channel_id=1, source_target_pairs={{0,8},{2,18},{4,12},{6,22},{8,0},{10,26},{12,4},{14,30},{16,24},{1... | collective-permute-start | bytes 73736 | tf_op jit(solution)/shard_map/ppermute | solution.py:446
  24.2 1.7 %collective-permute-start.9 = (bf16[32,384]{1,0:T(8,128)(2,1)S(1)}, bf16[32,384]{1,0:T(8,128)(2,1)S(1)}, u32[]{:S(2)}, u32[]{:S(2)}) collective-permute-start(bf16[32,384]{1,0:T(8,128)(2,1)S(1)} %add_parts.2.refs_0_), channel_id=1, source_target_pairs={{0,24},{8,16},{16,8},{24,0},{1,25},{9,17},{17,9},{25,1},{2,26},{10... | collective-permute-start | bytes 73736 | tf_op jit(solution)/shard_map/ppermute | solution.py:440
  25.8 0.7 %collective-permute-done.10.refs_2_ = bf16[32,384]{1,0:T(8,128)(2,1)S(1)} collective-permute-done((bf16[32,384]{1,0:T(8,128)(2,1)S(1)}, bf16[32,384]{1,0:T(8,128)(2,1)S(1)}, u32[]{:S(2)}, u32[]{:S(2)}) %collective-permute-start.10) | collective-permute-done | bytes 24608 | tf_op jit(solution)/shard_map/ppermute | solution.py:446
  26.5 0.0 collective-permute-start.11
  26.5 3.3 %collective-permute-done.9.refs_1_ = bf16[32,384]{1,0:T(8,128)(2,1)S(1)} collective-permute-done((bf16[32,384]{1,0:T(8,128)(2,1)S(1)}, bf16[32,384]{1,0:T(8,128)(2,1)S(1)}, u32[]{:S(2)}, u32[]{:S(2)}) %collective-permute-start.9) | collective-permute-done | bytes 24608 | tf_op jit(solution)/shard_map/ppermute | solution.py:440
  29.8 0.0 collective-permute-done.11.refs_3_
  29.8 1.6 %collective-permute-start.12 = (bf16[32,384]{1,0:T(8,128)(2,1)S(1)}, bf16[32,384]{1,0:T(8,128)(2,1)S(1)}, u32[]{:S(2)}, u32[]{:S(2)}) collective-permute-start(bf16[32,384]{1,0:T(8,128)(2,1)S(1)} %add_parts.3.refs_0_), channel_id=1, source_target_pairs={{0,1},{1,0},{2,3},{3,2},{4,5},{5,4},{6,7},{7,6},{8,9},{9,8},{10,11... | collective-permute-start | bytes 73736 | tf_op jit(solution)/shard_map/ppermute | solution.py:440
  31.4 1.6 %closure.1 = bf16[1,16,8,8,128]{4,3,2,1,0:T(8,128)(2,1)} custom-call(bf16[12,192,128]{2,1,0:T(8,128)(2,1)S(1)} %hidden_rim.1.hidden, bf16[128,1920]{1,0:T(8,128)(2,1)S(1)} %get-tuple-element.68.t2, f32[128,128]{1,0:T(8,128)S(1)} %get-tuple-element.69.b2), custom_call_target="tpu_custom_call" | custom-call | flops 1000000000 | bytes 1000000 | tf_op jit(solution)/shard_map/closure/pallas_call | solution.py:528
  32.9 0.8 %collective-permute-done.12.refs_1_ = bf16[32,384]{1,0:T(8,128)(2,1)S(1)} collective-permute-done((bf16[32,384]{1,0:T(8,128)(2,1)S(1)}, bf16[32,384]{1,0:T(8,128)(2,1)S(1)}, u32[]{:S(2)}, u32[]{:S(2)}) %collective-permute-start.12) | collective-permute-done | bytes 24608 | tf_op jit(solution)/shard_map/ppermute | solution.py:440
  33.7 0.8 %finish.1 = (f32[128,27]{1,0:T(8,128)}, f32[256,27]{1,0:T(8,128)}, f32[1,16]{1,0:T(1,128)}) custom-call(bf16[32,384]{1,0:T(8,128)(2,1)S(1)} %add_parts.3.refs_0_, bf16[32,384]{1,0:T(8,128)(2,1)S(1)} %collective-permute-done.12.refs_1_), custom_call_target="tpu_custom_call" | custom-call | flops 10000000 | bytes 1000000 | tf_op jit(solution)/shard_map/finish/pallas_call | solution.py:539
  (2 shorter events, 0.0 us)
Async XLA Ops:
  1.7 4.8 %copy-start = (bf16[27,16,16]{0,2,1:T(8,128)(2,1)S(1)}, bf16[27,16,16]{0,2,1:T(8,128)(2,1)}, u32[]{:S(2)}) copy-start(bf16[27,16,16]{0,2,1:T(8,128)(2,1)} %param.15) | copy-start | bytes 41476
  1.7 4.8 %copy-start.1 = (bf16[27,16,8]{0,2,1:T(8,128)(2,1)S(1)}, bf16[27,16,8]{0,2,1:T(8,128)(2,1)}, u32[]{:S(2)}) copy-start(bf16[27,16,8]{0,2,1:T(8,128)(2,1)} %param.13) | copy-start | bytes 20740
  1.7 4.8 %copy-start.2 = (f32[16]{0:T(128)S(1)}, f32[16]{0:T(128)}, u32[]{:S(2)}) copy-start(f32[16]{0:T(128)} %param.14) | copy-start | bytes 196
  1.7 4.8 %copy-start.3 = (f32[16]{0:T(128)S(1)}, f32[16]{0:T(128)}, u32[]{:S(2)}) copy-start(f32[16]{0:T(128)} %param.16) | copy-start | bytes 196
  1.8 7.4 %collective-permute-start = (bf16[512,128]{1,0:T(8,128)(2,1)S(1)}, bf16[512,128]{1,0:T(8,128)(2,1)S(1)}, u32[]{:S(2)}, u32[]{:S(2)}) collective-permute-start(bf16[512,128]{1,0:T(8,128)(2,1)S(1)} %get-tuple-element.39), channel_id=1, source_target_pairs={{0,2},{2,0},{4,6},{6,4},{8,16},{10,18},{12,20},{14,22},{16,8},{18,... | collective-permute-start | bytes 393224 | tf_op jit(solution)/shard_map/ppermute | solution.py:434
  2.4 7.4 %collective-permute-start.1 = (bf16[512,128]{1,0:T(8,128)(2,1)S(1)}, bf16[512,128]{1,0:T(8,128)(2,1)S(1)}, u32[]{:S(2)}, u32[]{:S(2)}) collective-permute-start(bf16[512,128]{1,0:T(8,128)(2,1)S(1)} %get-tuple-element.40), channel_id=1, source_target_pairs={{0,8},{8,0},{16,24},{24,16},{1,9},{9,1},{17,25},{25,17},{2,10},{10... | collective-permute-start | bytes 393224 | tf_op jit(solution)/shard_map/ppermute | solution.py:435
  10.0 5.2 %collective-permute-start.2 = (bf16[576,128]{1,0:T(8,128)(2,1)S(1)}, bf16[576,128]{1,0:T(8,128)(2,1)S(1)}, u32[]{:S(2)}, u32[]{:S(2)}) collective-permute-start(bf16[576,128]{1,0:T(8,128)(2,1)S(1)} %get-tuple-element.47), channel_id=1, source_target_pairs={{0,8},{8,0},{16,24},{24,16},{2,4},{10,12},{18,20},{26,28},{4,2},{1... | collective-permute-start | bytes 442376 | tf_op jit(solution)/shard_map/ppermute | solution.py:434
  11.8 3.4 %collective-permute-start.3 = (bf16[576,128]{1,0:T(8,128)(2,1)S(1)}, bf16[576,128]{1,0:T(8,128)(2,1)S(1)}, u32[]{:S(2)}, u32[]{:S(2)}) collective-permute-start(bf16[576,128]{1,0:T(8,128)(2,1)S(1)} %get-tuple-element.48), channel_id=1, source_target_pairs={{0,2},{2,0},{4,6},{6,4},{1,3},{3,1},{5,7},{7,5},{8,10},{10,8},{12,... | collective-permute-start | bytes 442376 | tf_op jit(solution)/shard_map/ppermute | solution.py:435
  11.8 3.4 %copy-start.4 = (bf16[128,768]{1,0:T(8,128)(2,1)S(1)}, bf16[128,768]{1,0:T(8,128)(2,1)}, u32[]{:S(2)}) copy-start(bf16[128,768]{1,0:T(8,128)(2,1)} %constant.15.clone.rep2) | copy-start | bytes 589828
  11.8 3.4 %copy-start.5 = (bf16[640,128]{1,0:T(8,128)(2,1)S(1)}, bf16[640,128]{1,0:T(8,128)(2,1)}, u32[]{:S(2)}) copy-start(bf16[640,128]{1,0:T(8,128)(2,1)} %constant.13.clone.e2t) | copy-start | bytes 491524
  11.8 3.4 %copy-start.6 = (bf16[384,128]{1,0:T(8,128)(2,1)S(1)}, bf16[384,128]{1,0:T(8,128)(2,1)}, u32[]{:S(2)}) copy-start(bf16[384,128]{1,0:T(8,128)(2,1)} %constant.12.clone.e1t) | copy-start | bytes 294916
  11.8 3.4 %copy-start.7 = (bf16[128,384]{1,0:T(8,128)(2,1)S(1)}, bf16[128,384]{1,0:T(8,128)(2,1)}, u32[]{:S(2)}) copy-start(bf16[128,384]{1,0:T(8,128)(2,1)} %constant.14.clone.rep1) | copy-start | bytes 294916
  11.9 3.4 %copy-start.8 = (f32[1,640]{1,0:T(1,128)S(1)}, f32[1,640]{1,0:T(1,128)}, u32[]{:S(2)}) copy-start(f32[1,640]{1,0:T(1,128)} %constant.17.clone.y2) | copy-start | bytes 7684
  11.9 3.4 %copy-start.9 = (f32[1,384]{1,0:T(1,128)S(1)}, f32[1,384]{1,0:T(1,128)}, u32[]{:S(2)}) copy-start(f32[1,384]{1,0:T(1,128)} %constant.16.clone.y1) | copy-start | bytes 4612
  13.0 6.9 %collective-permute-start.7 = (bf16[320,128]{1,0:T(8,128)(2,1)S(1)}, bf16[320,128]{1,0:T(8,128)(2,1)S(1)}, u32[]{:S(2)}, u32[]{:S(2)}) collective-permute-start(bf16[320,128]{1,0:T(8,128)(2,1)S(1)} %get-tuple-element.63), channel_id=1, source_target_pairs={{0,8},{8,0},{16,24},{24,16},{2,4},{10,12},{18,20},{26,28},{4,2},{1... | collective-permute-start | bytes 245768 | tf_op jit(solution)/shard_map/ppermute | solution.py:434
  14.7 5.2 %collective-permute-start.8 = (bf16[320,128]{1,0:T(8,128)(2,1)S(1)}, bf16[320,128]{1,0:T(8,128)(2,1)S(1)}, u32[]{:S(2)}, u32[]{:S(2)}) collective-permute-start(bf16[320,128]{1,0:T(8,128)(2,1)S(1)} %get-tuple-element.64), channel_id=1, source_target_pairs={{0,2},{2,0},{4,6},{6,4},{1,3},{3,1},{5,7},{7,5},{8,10},{10,8},{12,... | collective-permute-start | bytes 245768 | tf_op jit(solution)/shard_map/ppermute | solution.py:435
  18.0 3.2 %collective-permute-start.4 = (bf16[32,384]{1,0:T(8,128)(2,1)S(1)}, bf16[32,384]{1,0:T(8,128)(2,1)S(1)}, u32[]{:S(2)}, u32[]{:S(2)}) collective-permute-start(bf16[32,384]{1,0:T(8,128)(2,1)S(1)} %get-tuple-element.61.refs_0_), channel_id=1, source_target_pairs={{0,2},{2,0},{4,6},{6,4},{1,3},{3,1},{5,7},{7,5},{8,10},{10,8},{12,... | collective-permute-start | bytes 73736 | tf_op jit(solution)/shard_map/ppermute | solution.py:440
  18.1 3.9 %collective-permute-start.5 = (bf16[32,384]{1,0:T(8,128)(2,1)S(1)}, bf16[32,384]{1,0:T(8,128)(2,1)S(1)}, u32[]{:S(2)}, u32[]{:S(2)}) collective-permute-start(bf16[32,384]{1,0:T(8,128)(2,1)S(1)} %get-tuple-element.61.refs_0_), channel_id=1, source_target_pairs={{0,4},{2,6},{4,0},{6,2},{1,5},{3,7},{5,1},{7,3},{8,12},{10,14},{12... | collective-permute-start | bytes 73736 | tf_op jit(solution)/shard_map/ppermute | solution.py:440
  19.1 3.3 %collective-permute-start.6 = (bf16[32,384]{1,0:T(8,128)(2,1)S(1)}, bf16[32,384]{1,0:T(8,128)(2,1)S(1)}, u32[]{:S(2)}, u32[]{:S(2)}) collective-permute-start(bf16[32,384]{1,0:T(8,128)(2,1)S(1)} %get-tuple-element.61.refs_0_), channel_id=1, source_target_pairs={{0,6},{2,4},{4,2},{6,0},{1,7},{3,5},{5,3},{7,1},{8,14},{10,12},{12... | collective-permute-start | bytes 73736 | tf_op jit(solution)/shard_map/ppermute | solution.py:440
  22.3 4.2 %collective-permute-start.10 = (bf16[32,384]{1,0:T(8,128)(2,1)S(1)}, bf16[32,384]{1,0:T(8,128)(2,1)S(1)}, u32[]{:S(2)}, u32[]{:S(2)}) collective-permute-start(bf16[32,384]{1,0:T(8,128)(2,1)S(1)} %add_parts.2.refs_0_), channel_id=1, source_target_pairs={{0,8},{2,18},{4,12},{6,22},{8,0},{10,26},{12,4},{14,30},{16,24},{1... | collective-permute-start | bytes 73736 | tf_op jit(solution)/shard_map/ppermute | solution.py:446
  24.2 5.6 %collective-permute-start.9 = (bf16[32,384]{1,0:T(8,128)(2,1)S(1)}, bf16[32,384]{1,0:T(8,128)(2,1)S(1)}, u32[]{:S(2)}, u32[]{:S(2)}) collective-permute-start(bf16[32,384]{1,0:T(8,128)(2,1)S(1)} %add_parts.2.refs_0_), channel_id=1, source_target_pairs={{0,24},{8,16},{16,8},{24,0},{1,25},{9,17},{17,9},{25,1},{2,26},{10... | collective-permute-start | bytes 73736 | tf_op jit(solution)/shard_map/ppermute | solution.py:440
  26.5 3.3 %collective-permute-start.11 = (bf16[32,384]{1,0:T(8,128)(2,1)S(1)}, bf16[32,384]{1,0:T(8,128)(2,1)S(1)}, u32[]{:S(2)}, u32[]{:S(2)}) collective-permute-start(bf16[32,384]{1,0:T(8,128)(2,1)S(1)} %collective-permute-done.10.refs_2_), channel_id=1, source_target_pairs={{0,2},{2,0},{4,6},{6,4},{1,3},{3,1},{5,7},{7,5},{8,10},{10,8},{12,... | collective-permute-start | bytes 73736 | tf_op jit(solution)/shard_map/ppermute | solution.py:440
  29.8 3.9 %collective-permute-start.12 = (bf16[32,384]{1,0:T(8,128)(2,1)S(1)}, bf16[32,384]{1,0:T(8,128)(2,1)S(1)}, u32[]{:S(2)}, u32[]{:S(2)}) collective-permute-start(bf16[32,384]{1,0:T(8,128)(2,1)S(1)} %add_parts.3.refs_0_), channel_id=1, source_target_pairs={{0,1},{1,0},{2,3},{3,2},{4,5},{5,4},{6,7},{7,6},{8,9},{9,8},{10,11... | collective-permute-start | bytes 73736 | tf_op jit(solution)/shard_map/ppermute | solution.py:440

commit v22 on v20

--- a/solution.py
+++ b/solution.py
@@ -133,9 +133,30 @@
             at += half
 
 
-def join_kernel(counts, xfar, xnear, fields, cot, near, far):
-    f, c = x_planes(fields.shape[0], fields, cot, xnear, xfar, counts[0])
-    pick_strips([(pick_rows(CI, 0, 6), f[2:-2]), (pick_rows(CH, 0, 6), c)], near, far)
+def own_strips_kernel(fields, cot, near, far):
+    planes = range(fields.shape[0])
+    pick_strips([(pick_rows(CI, 0, 6), [fields[x] for x in planes]), (pick_rows(CH, 0, 6), [cot[x] for x in planes])], near, far)
+
+
+def join_kernel(counts, xfar, xnear, near_own, far_own, near, far):
+    up_first = lax.axis_index("radial") % 2 == 0
+    index, count = lax.axis_index("stream"), near_own.shape[0] // 48
+    at = own_at = 0
+    for pick, rows, start, skip, half in ((pick_rows(CI, 0, 6), 64, 0, 2, 16), (pick_rows(CH, 0, 6), 128, 256, 0, 32)):
+        places = [slice(start + n * rows, start + (n + 1) * rows) for n in range(4 if skip else 2)]
+        rims = [sides(index, counts[0], xnear[place], xfar[place]) for place in places]
+        below, above = [low for low, _ in rims[skip:]], [high for _, high in rims[:2]]
+        for offset, part in ((0, below), (count + 2, above)):
+            for n, v in enumerate(part):
+                got = jnp.dot(pick, v.astype(BF16), preferred_element_type=F32)
+                place = slice(at + (offset + n) * half, at + (offset + n + 1) * half)
+                near[place] = jnp.where(up_first, got[half:], got[:half]).astype(BF16)
+                far[place] = jnp.where(up_first, got[:half], got[half:]).astype(BF16)
+        inside = slice(at + 2 * half, at + (2 + count) * half)
+        near[inside] = near_own[own_at:own_at + count * half]
+        far[inside] = far_own[own_at:own_at + count * half]
+        at += (count + 4) * half
+        own_at += count * half
 
 
 def join_outer_kernel(counts, xfar, xnear, fields, cot, near, far):
@@ -490,9 +511,10 @@
         "band_matrices",
         flops=4_000_000_000,
     )(w1, w2, first_bias[None], second_bias[None])
+    near_own, far_own = call(own_strips_kernel, (shape(planes * 48, Z),) * 2, "own_strips")(f_rows, c_rows)
     xfar, xnear, t1o, tbo = lax.optimization_barrier((xfar, xnear, t1o, tbo))
     inner, outer = shape((planes + 4) * 48, Z), shape(128 + (planes + 4) * 16, Z)
-    near, far = call(functools.partial(join_kernel, counts), (inner, inner), "join_strips")(xfar, xnear, f_rows, c_rows)
+    near, far = call(functools.partial(join_kernel, counts), (inner, inner), "join_strips")(xfar, xnear, near_own, far_own)
     rnear, rfar = exchange(near, far, "radial", "stream")
     half, half_f32 = shape(64, planes * Z), shape(64, planes * Z, dtype=F32)
     fs, cs, pre, back, hidden, dpre = call(

time: 34.3 us -> 34.2 us (level)
  no operation moved by 1% of the time
where the time goes in v22:
time: 34.2 us; the launch traced here: 34 us
  starting transfers between devices  14.9 us (44%)
  Pallas kernels  10.8 us (32%)
  waiting for transfers between devices  6.45 us (19%)
  other arithmetic  1.02 us (3%)
  between operations  0.83 us (2%)
    ppermute x3, starting transfers between devices, exchange(): return (lax.ppermute(near, axis, [(i, i ^ 1) for i in range(count)]), far)  4.15 us
    ppermute x3, starting transfers between devices, exchange(): far = lax.ppermute(far, axes, pairs)  4.02 us
    ppermute x6, starting transfers between devices, swap(): lax.ppermute(v, axis, [(i, i ^ mask) for i in range(count)])  3.5 us
    ppermute x1, starting transfers between devices, stream_round(): apart = lax.ppermute(v, ('stream', 'radial'), pairs)  3.23 us
    ppermute x6, waiting for transfers between devices, swap(): lax.ppermute(v, axis, [(i, i ^ mask) for i in range(count)])  3.23 us
    pallas_call x1, Pallas kernels, local(): call(functools.partial(rim_kernel, counts), (shape(planes, 128, Z), shape...  2.7 us
    pallas_call x1, Pallas kernels, local(): call(band_kernel, (shape(192, 768), shape(128, 384), shape(192, 768), sha...  2.7 us
    ppermute x1, waiting for transfers between devices, stream_round(): apart = lax.ppermute(v, ('stream', 'radial'), pairs)  2.47 us
  transfers between devices with their start and end apart: 13, of which 7 were waited for; matrix products, arithmetic and copies ran while one was open for 0% of the time, Pallas kernels for 28%

profile of v22, /device:TPU:0, one launch (start us, length us, event | category | flops | bytes accessed | tf_op | source)
XLA Modules:
  0.0 34.0 jit_solution(1809794258638943750)
XLA Ops:
  0.6 1.0 %pad_maximum_fusion.inputs = bf16[24,8,8,128]{3,2,1,0:T(8,128)(2,1)S(1)} fusion(bf16[16,8,8,128]{3,2,1,0:T(8,128)(2,1)} %bitcast.21, bf16[8,8,8,128]{3,2,1,0:T(8,128)(2,1)} %bitcast.22), kind=kLoop, calls=%fused_computation | loop fusion | flops 196608 | bytes 786432 | tf_op jit(solution)/shard_map/concatenate | solution.py:503
  1.7 0.0 copy-start
  1.7 0.0 copy-start.1
  1.7 0.0 copy-start.2
  1.7 0.0 copy-start.3
  1.7 0.1 pack_strips.1
  1.8 0.5 %collective-permute-start = (bf16[512,128]{1,0:T(8,128)(2,1)S(1)}, bf16[512,128]{1,0:T(8,128)(2,1)S(1)}, u32[]{:S(2)}, u32[]{:S(2)}) collective-permute-start(bf16[512,128]{1,0:T(8,128)(2,1)S(1)} %get-tuple-element.41), channel_id=1, source_target_pairs={{0,2},{2,0},{4,6},{6,4},{8,16},{10,18},{12,20},{14,22},{16,8},{18,... | collective-permute-start | bytes 393224 | tf_op jit(solution)/shard_map/ppermute | solution.py:455
  2.4 4.1 %collective-permute-start.1 = (bf16[512,128]{1,0:T(8,128)(2,1)S(1)}, bf16[512,128]{1,0:T(8,128)(2,1)S(1)}, u32[]{:S(2)}, u32[]{:S(2)}) collective-permute-start(bf16[512,128]{1,0:T(8,128)(2,1)S(1)} %get-tuple-element.42), channel_id=1, source_target_pairs={{0,8},{8,0},{16,24},{24,16},{1,9},{9,1},{17,25},{25,17},{2,10},{10... | collective-permute-start | bytes 393224 | tf_op jit(solution)/shard_map/ppermute | solution.py:456
  6.5 0.0 copy-done
  6.5 0.0 copy-done.1
  6.5 0.0 copy-done.2
  6.5 0.0 copy-done.3
  6.5 2.7 %band_matrices.1 = (bf16[192,768]{1,0:T(8,128)(2,1)S(1)}, bf16[128,384]{1,0:T(8,128)(2,1)S(1)}, bf16[192,768]{1,0:T(8,128)(2,1)S(1)}, bf16[128,1152]{1,0:T(8,128...) custom-call(bf16[128,27]{1,0:T(8,128)(2,1)S(1)} %bitcast.18, ...), custom_call_target="tpu_custom_call" | custom-call | flops 4000000000 | bytes 1000000 | tf_op jit(solution)/shard_map/band_matrices/pallas_call | solution.py:507
  9.2 0.2 own_strips.1
  9.5 0.0 collective-permute-done.xfar
  9.5 0.3 collective-permute-done.1.xnear
  9.7 0.2 join_strips.1
  9.9 1.8 %collective-permute-start.2 = (bf16[576,128]{1,0:T(8,128)(2,1)S(1)}, bf16[576,128]{1,0:T(8,128)(2,1)S(1)}, u32[]{:S(2)}, u32[]{:S(2)}) collective-permute-start(bf16[576,128]{1,0:T(8,128)(2,1)S(1)} %get-tuple-element.51), channel_id=1, source_target_pairs={{0,8},{8,0},{16,24},{24,16},{2,4},{10,12},{18,20},{26,28},{4,2},{1... | collective-permute-start | bytes 442376 | tf_op jit(solution)/shard_map/ppermute | solution.py:455
  11.7 0.0 collective-permute-start.3
  11.7 0.0 copy-start.4
  11.7 0.0 copy-start.5
  11.7 0.0 copy-start.6
  11.7 0.0 copy-start.7
  11.8 0.0 copy-start.8
  11.8 0.0 copy-start.9
  11.8 0.9 %own_rows.1 = (bf16[256,2048]{1,0:T(8,128)(2,1)S(1)}, bf16[384,1536]{1,0:T(8,128)(2,1)S(1)}, f32[64,1024]{1,0:T(8,128)S(1)}, f32[64,1024]{1,0:T(8,128)S(1)}, bf1...) custom-call(bf16[512,128]{1,0:T(8,128)(2,1)S(1)} %collective-permute-done.xfar, ...), custom_call_target="tpu_custom_call" | custom-call | flops 1000000000 | bytes 1000000 | tf_op jit(solution)/shard_map/own_rows/pallas_call | solution.py:520
  12.7 0.2 join_outer.1
  12.9 1.7 %collective-permute-start.7 = (bf16[320,128]{1,0:T(8,128)(2,1)S(1)}, bf16[320,128]{1,0:T(8,128)(2,1)S(1)}, u32[]{:S(2)}, u32[]{:S(2)}) collective-permute-start(bf16[320,128]{1,0:T(8,128)(2,1)S(1)} %get-tuple-element.67), channel_id=1, source_target_pairs={{0,8},{8,0},{16,24},{24,16},{2,4},{10,12},{18,20},{26,28},{4,2},{1... | collective-permute-start | bytes 245768 | tf_op jit(solution)/shard_map/ppermute | solution.py:455
  14.6 0.0 collective-permute-start.8
  14.6 0.5 %collective-permute-done.2.rfar = bf16[576,128]{1,0:T(8,128)(2,1)S(1)} collective-permute-done((bf16[576,128]{1,0:T(8,128)(2,1)S(1)}, bf16[576,128]{1,0:T(8,128)(2,1)S(1)}, u32[]{:S(2)}, u32[]{:S(2)}) %collective-permute-start.2) | collective-permute-done | bytes 147488 | tf_op jit(solution)/shard_map/ppermute | solution.py:455
  15.1 0.0 collective-permute-done.3.rnear
  15.1 0.0 copy-done.4
  15.1 0.0 copy-done.5
  15.1 0.0 copy-done.6
  15.1 0.0 copy-done.7
  15.1 0.0 copy-done.8
  15.2 0.0 copy-done.9
  15.2 2.7 %gradients.1 = (bf16[8,128,128]{2,1,0:T(8,128)(2,1)S(1)}, bf16[32,384]{1,0:T(8,128)(2,1)S(1)}) custom-call(bf16[576,128]{1,0:T(8,128)(2,1)S(1)} %collective-permute-done.2.rfar, bf16[576,128]{1,0:T(8,128)(2,1)S(1)} %collective-permute-done.3.rnear, bf16[256,2048]{1,0:T(8,128)(2,1)S(1)} %get-tuple-element.57.fs, bf16[384,1536]{1,0:T(8,128)(2,1)S(1)} %get-tuple-element.58.cs, ...), custom_call_target="tpu_custom_call" | custom-call | flops 2000000000 | bytes 1000000 | tf_op jit(solution)/shard_map/gradients/pallas_call | solution.py:530
  17.9 0.1 collective-permute-start.4
  18.0 1.0 %collective-permute-start.5 = (bf16[32,384]{1,0:T(8,128)(2,1)S(1)}, bf16[32,384]{1,0:T(8,128)(2,1)S(1)}, u32[]{:S(2)}, u32[]{:S(2)}) collective-permute-start(bf16[32,384]{1,0:T(8,128)(2,1)S(1)} %get-tuple-element.65.refs_0_), channel_id=1, source_target_pairs={{0,4},{2,6},{4,0},{6,2},{1,5},{3,7},{5,1},{7,3},{8,12},{10,14},{12... | collective-permute-start | bytes 73736 | tf_op jit(solution)/shard_map/ppermute | solution.py:461
  19.0 0.9 %collective-permute-start.6 = (bf16[32,384]{1,0:T(8,128)(2,1)S(1)}, bf16[32,384]{1,0:T(8,128)(2,1)S(1)}, u32[]{:S(2)}, u32[]{:S(2)}) collective-permute-start(bf16[32,384]{1,0:T(8,128)(2,1)S(1)} %get-tuple-element.65.refs_0_), channel_id=1, source_target_pairs={{0,6},{2,4},{4,2},{6,0},{1,7},{3,5},{5,3},{7,1},{8,14},{10,12},{12... | collective-permute-start | bytes 73736 | tf_op jit(solution)/shard_map/ppermute | solution.py:461
  19.8 0.0 collective-permute-done.7.rfar_outer
  19.8 0.0 collective-permute-done.8.rnear_outer
  19.8 1.3 %hidden_rim.1.hidden = bf16[12,192,128]{2,1,0:T(8,128)(2,1)S(1)} custom-call(bf16[576,128]{1,0:T(8,128)(2,1)S(1)} %collective-permute-done.2.rfar, bf16[576,128]{1,0:T(8,128)(2,1)S(1)} %collective-permute-done.3.rnear, bf16[320,128]{1,0:T(8,128)(2,1)S(1)} %collective-permute-done.7.rfar_outer, bf16[320,128]{1,0:T(8,128)(2,1)S(1)} %collective-permute-done.8.rnear_outer, ...), custom_call_target="tpu_custom_call" | custom-call | flops 1000000000 | bytes 1000000 | tf_op jit(solution)/shard_map/hidden_rim/pallas_call | solution.py:540
  21.1 0.0 collective-permute-done.4.refs_1_
  21.1 0.7 %collective-permute-done.5.refs_2_ = bf16[32,384]{1,0:T(8,128)(2,1)S(1)} collective-permute-done((bf16[32,384]{1,0:T(8,128)(2,1)S(1)}, bf16[32,384]{1,0:T(8,128)(2,1)S(1)}, u32[]{:S(2)}, u32[]{:S(2)}) %collective-permute-start.5) | collective-permute-done | bytes 24608 | tf_op jit(solution)/shard_map/ppermute | solution.py:461
  21.9 0.4 %collective-permute-done.6.refs_3_ = bf16[32,384]{1,0:T(8,128)(2,1)S(1)} collective-permute-done((bf16[32,384]{1,0:T(8,128)(2,1)S(1)}, bf16[32,384]{1,0:T(8,128)(2,1)S(1)}, u32[]{:S(2)}, u32[]{:S(2)}) %collective-permute-start.6) | collective-permute-done | bytes 24608 | tf_op jit(solution)/shard_map/ppermute | solution.py:461
  22.2 3.2 %collective-permute-start.10 = (bf16[32,384]{1,0:T(8,128)(2,1)S(1)}, bf16[32,384]{1,0:T(8,128)(2,1)S(1)}, u32[]{:S(2)}, u32[]{:S(2)}) collective-permute-start(bf16[32,384]{1,0:T(8,128)(2,1)S(1)} %add_parts.2.refs_0_), channel_id=1, source_target_pairs={{0,24},{2,18},{4,28},{6,22},{8,16},{10,26},{12,20},{14,30},{16,8},... | collective-permute-start | bytes 73736 | tf_op jit(solution)/shard_map/ppermute | solution.py:467
  25.5 0.0 collective-permute-start.9
  25.5 2.5 %collective-permute-done.10.refs_2_ = bf16[32,384]{1,0:T(8,128)(2,1)S(1)} collective-permute-done((bf16[32,384]{1,0:T(8,128)(2,1)S(1)}, bf16[32,384]{1,0:T(8,128)(2,1)S(1)}, u32[]{:S(2)}, u32[]{:S(2)}) %collective-permute-start.10) | collective-permute-done | bytes 24608 | tf_op jit(solution)/shard_map/ppermute | solution.py:467
  27.9 0.0 collective-permute-start.11
  28.0 1.4 %collective-permute-done.9.refs_1_ = bf16[32,384]{1,0:T(8,128)(2,1)S(1)} collective-permute-done((bf16[32,384]{1,0:T(8,128)(2,1)S(1)}, bf16[32,384]{1,0:T(8,128)(2,1)S(1)}, u32[]{:S(2)}, u32[]{:S(2)}) %collective-permute-start.9) | collective-permute-done | bytes 24608 | tf_op jit(solution)/shard_map/ppermute | solution.py:461
  29.3 0.0 collective-permute-done.11.refs_3_
  29.3 1.6 %collective-permute-start.12 = (bf16[32,384]{1,0:T(8,128)(2,1)S(1)}, bf16[32,384]{1,0:T(8,128)(2,1)S(1)}, u32[]{:S(2)}, u32[]{:S(2)}) collective-permute-start(bf16[32,384]{1,0:T(8,128)(2,1)S(1)} %add_parts.3.refs_0_), channel_id=1, source_target_pairs={{0,1},{1,0},{2,3},{3,2},{4,5},{5,4},{6,7},{7,6},{8,9},{9,8},{10,11... | collective-permute-start | bytes 73736 | tf_op jit(solution)/shard_map/ppermute | solution.py:461
  30.9 1.6 %closure.1 = bf16[1,16,8,8,128]{4,3,2,1,0:T(8,128)(2,1)} custom-call(bf16[12,192,128]{2,1,0:T(8,128)(2,1)S(1)} %hidden_rim.1.hidden, bf16[128,1920]{1,0:T(8,128)(2,1)S(1)} %get-tuple-element.72.t2, f32[128,128]{1,0:T(8,128)S(1)} %get-tuple-element.73.b2), custom_call_target="tpu_custom_call" | custom-call | flops 1000000000 | bytes 1000000 | tf_op jit(solution)/shard_map/closure/pallas_call | solution.py:550
  32.5 0.8 %collective-permute-done.12.refs_1_ = bf16[32,384]{1,0:T(8,128)(2,1)S(1)} collective-permute-done((bf16[32,384]{1,0:T(8,128)(2,1)S(1)}, bf16[32,384]{1,0:T(8,128)(2,1)S(1)}, u32[]{:S(2)}, u32[]{:S(2)}) %collective-permute-start.12) | collective-permute-done | bytes 24608 | tf_op jit(solution)/shard_map/ppermute | solution.py:461
  33.2 0.8 %finish.1 = (f32[128,27]{1,0:T(8,128)}, f32[256,27]{1,0:T(8,128)}, f32[1,16]{1,0:T(1,128)}) custom-call(bf16[32,384]{1,0:T(8,128)(2,1)S(1)} %add_parts.3.refs_0_, bf16[32,384]{1,0:T(8,128)(2,1)S(1)} %collective-permute-done.12.refs_1_), custom_call_target="tpu_custom_call" | custom-call | flops 10000000 | bytes 1000000 | tf_op jit(solution)/shard_map/finish/pallas_call | solution.py:561
  (2 shorter events, 0.0 us)
Async XLA Ops:
  1.7 4.8 %copy-start = (bf16[27,16,16]{0,2,1:T(8,128)(2,1)S(1)}, bf16[27,16,16]{0,2,1:T(8,128)(2,1)}, u32[]{:S(2)}) copy-start(bf16[27,16,16]{0,2,1:T(8,128)(2,1)} %param.15) | copy-start | bytes 41476
  1.7 4.8 %copy-start.1 = (bf16[27,16,8]{0,2,1:T(8,128)(2,1)S(1)}, bf16[27,16,8]{0,2,1:T(8,128)(2,1)}, u32[]{:S(2)}) copy-start(bf16[27,16,8]{0,2,1:T(8,128)(2,1)} %param.13) | copy-start | bytes 20740
  1.7 4.8 %copy-start.2 = (f32[16]{0:T(128)S(1)}, f32[16]{0:T(128)}, u32[]{:S(2)}) copy-start(f32[16]{0:T(128)} %param.14) | copy-start | bytes 196
  1.7 4.8 %copy-start.3 = (f32[16]{0:T(128)S(1)}, f32[16]{0:T(128)}, u32[]{:S(2)}) copy-start(f32[16]{0:T(128)} %param.16) | copy-start | bytes 196
  1.8 7.6 %collective-permute-start = (bf16[512,128]{1,0:T(8,128)(2,1)S(1)}, bf16[512,128]{1,0:T(8,128)(2,1)S(1)}, u32[]{:S(2)}, u32[]{:S(2)}) collective-permute-start(bf16[512,128]{1,0:T(8,128)(2,1)S(1)} %get-tuple-element.41), channel_id=1, source_target_pairs={{0,2},{2,0},{4,6},{6,4},{8,16},{10,18},{12,20},{14,22},{16,8},{18,... | collective-permute-start | bytes 393224 | tf_op jit(solution)/shard_map/ppermute | solution.py:455
  2.4 7.4 %collective-permute-start.1 = (bf16[512,128]{1,0:T(8,128)(2,1)S(1)}, bf16[512,128]{1,0:T(8,128)(2,1)S(1)}, u32[]{:S(2)}, u32[]{:S(2)}) collective-permute-start(bf16[512,128]{1,0:T(8,128)(2,1)S(1)} %get-tuple-element.42), channel_id=1, source_target_pairs={{0,8},{8,0},{16,24},{24,16},{1,9},{9,1},{17,25},{25,17},{2,10},{10... | collective-permute-start | bytes 393224 | tf_op jit(solution)/shard_map/ppermute | solution.py:456
  9.9 5.2 %collective-permute-start.2 = (bf16[576,128]{1,0:T(8,128)(2,1)S(1)}, bf16[576,128]{1,0:T(8,128)(2,1)S(1)}, u32[]{:S(2)}, u32[]{:S(2)}) collective-permute-start(bf16[576,128]{1,0:T(8,128)(2,1)S(1)} %get-tuple-element.51), channel_id=1, source_target_pairs={{0,8},{8,0},{16,24},{24,16},{2,4},{10,12},{18,20},{26,28},{4,2},{1... | collective-permute-start | bytes 442376 | tf_op jit(solution)/shard_map/ppermute | solution.py:455
  11.7 3.4 %collective-permute-start.3 = (bf16[576,128]{1,0:T(8,128)(2,1)S(1)}, bf16[576,128]{1,0:T(8,128)(2,1)S(1)}, u32[]{:S(2)}, u32[]{:S(2)}) collective-permute-start(bf16[576,128]{1,0:T(8,128)(2,1)S(1)} %get-tuple-element.52), channel_id=1, source_target_pairs={{0,2},{2,0},{4,6},{6,4},{1,3},{3,1},{5,7},{7,5},{8,10},{10,8},{12,... | collective-permute-start | bytes 442376 | tf_op jit(solution)/shard_map/ppermute | solution.py:456
  11.7 3.4 %copy-start.4 = (bf16[128,768]{1,0:T(8,128)(2,1)S(1)}, bf16[128,768]{1,0:T(8,128)(2,1)}, u32[]{:S(2)}) copy-start(bf16[128,768]{1,0:T(8,128)(2,1)} %constant.15.clone.rep2) | copy-start | bytes 589828
  11.7 3.4 %copy-start.5 = (bf16[640,128]{1,0:T(8,128)(2,1)S(1)}, bf16[640,128]{1,0:T(8,128)(2,1)}, u32[]{:S(2)}) copy-start(bf16[640,128]{1,0:T(8,128)(2,1)} %constant.13.clone.e2t) | copy-start | bytes 491524
  11.7 3.4 %copy-start.6 = (bf16[384,128]{1,0:T(8,128)(2,1)S(1)}, bf16[384,128]{1,0:T(8,128)(2,1)}, u32[]{:S(2)}) copy-start(bf16[384,128]{1,0:T(8,128)(2,1)} %constant.12.clone.e1t) | copy-start | bytes 294916
  11.7 3.4 %copy-start.7 = (bf16[128,384]{1,0:T(8,128)(2,1)S(1)}, bf16[128,384]{1,0:T(8,128)(2,1)}, u32[]{:S(2)}) copy-start(bf16[128,384]{1,0:T(8,128)(2,1)} %constant.14.clone.rep1) | copy-start | bytes 294916
  11.8 3.4 %copy-start.8 = (f32[1,640]{1,0:T(1,128)S(1)}, f32[1,640]{1,0:T(1,128)}, u32[]{:S(2)}) copy-start(f32[1,640]{1,0:T(1,128)} %constant.17.clone.y2) | copy-start | bytes 7684
  11.8 3.4 %copy-start.9 = (f32[1,384]{1,0:T(1,128)S(1)}, f32[1,384]{1,0:T(1,128)}, u32[]{:S(2)}) copy-start(f32[1,384]{1,0:T(1,128)} %constant.16.clone.y1) | copy-start | bytes 4612
  12.9 6.9 %collective-permute-start.7 = (bf16[320,128]{1,0:T(8,128)(2,1)S(1)}, bf16[320,128]{1,0:T(8,128)(2,1)S(1)}, u32[]{:S(2)}, u32[]{:S(2)}) collective-permute-start(bf16[320,128]{1,0:T(8,128)(2,1)S(1)} %get-tuple-element.67), channel_id=1, source_target_pairs={{0,8},{8,0},{16,24},{24,16},{2,4},{10,12},{18,20},{26,28},{4,2},{1... | collective-permute-start | bytes 245768 | tf_op jit(solution)/shard_map/ppermute | solution.py:455
  14.6 5.2 %collective-permute-start.8 = (bf16[320,128]{1,0:T(8,128)(2,1)S(1)}, bf16[320,128]{1,0:T(8,128)(2,1)S(1)}, u32[]{:S(2)}, u32[]{:S(2)}) collective-permute-start(bf16[320,128]{1,0:T(8,128)(2,1)S(1)} %get-tuple-element.68), channel_id=1, source_target_pairs={{0,2},{2,0},{4,6},{6,4},{1,3},{3,1},{5,7},{7,5},{8,10},{10,8},{12,... | collective-permute-start | bytes 245768 | tf_op jit(solution)/shard_map/ppermute | solution.py:456
  17.9 3.2 %collective-permute-start.4 = (bf16[32,384]{1,0:T(8,128)(2,1)S(1)}, bf16[32,384]{1,0:T(8,128)(2,1)S(1)}, u32[]{:S(2)}, u32[]{:S(2)}) collective-permute-start(bf16[32,384]{1,0:T(8,128)(2,1)S(1)} %get-tuple-element.65.refs_0_), channel_id=1, source_target_pairs={{0,2},{2,0},{4,6},{6,4},{1,3},{3,1},{5,7},{7,5},{8,10},{10,8},{12,... | collective-permute-start | bytes 73736 | tf_op jit(solution)/shard_map/ppermute | solution.py:461
  18.0 3.9 %collective-permute-start.5 = (bf16[32,384]{1,0:T(8,128)(2,1)S(1)}, bf16[32,384]{1,0:T(8,128)(2,1)S(1)}, u32[]{:S(2)}, u32[]{:S(2)}) collective-permute-start(bf16[32,384]{1,0:T(8,128)(2,1)S(1)} %get-tuple-element.65.refs_0_), channel_id=1, source_target_pairs={{0,4},{2,6},{4,0},{6,2},{1,5},{3,7},{5,1},{7,3},{8,12},{10,14},{12... | collective-permute-start | bytes 73736 | tf_op jit(solution)/shard_map/ppermute | solution.py:461
  19.0 3.3 %collective-permute-start.6 = (bf16[32,384]{1,0:T(8,128)(2,1)S(1)}, bf16[32,384]{1,0:T(8,128)(2,1)S(1)}, u32[]{:S(2)}, u32[]{:S(2)}) collective-permute-start(bf16[32,384]{1,0:T(8,128)(2,1)S(1)} %get-tuple-element.65.refs_0_), channel_id=1, source_target_pairs={{0,6},{2,4},{4,2},{6,0},{1,7},{3,5},{5,3},{7,1},{8,14},{10,12},{12... | collective-permute-start | bytes 73736 | tf_op jit(solution)/shard_map/ppermute | solution.py:461
  22.2 5.7 %collective-permute-start.10 = (bf16[32,384]{1,0:T(8,128)(2,1)S(1)}, bf16[32,384]{1,0:T(8,128)(2,1)S(1)}, u32[]{:S(2)}, u32[]{:S(2)}) collective-permute-start(bf16[32,384]{1,0:T(8,128)(2,1)S(1)} %add_parts.2.refs_0_), channel_id=1, source_target_pairs={{0,24},{2,18},{4,28},{6,22},{8,16},{10,26},{12,20},{14,30},{16,8},... | collective-permute-start | bytes 73736 | tf_op jit(solution)/shard_map/ppermute | solution.py:467
  25.5 3.8 %collective-permute-start.9 = (bf16[32,384]{1,0:T(8,128)(2,1)S(1)}, bf16[32,384]{1,0:T(8,128)(2,1)S(1)}, u32[]{:S(2)}, u32[]{:S(2)}) collective-permute-start(bf16[32,384]{1,0:T(8,128)(2,1)S(1)} %add_parts.2.refs_0_), channel_id=1, source_target_pairs={{0,8},{8,0},{16,24},{24,16},{1,9},{9,1},{17,25},{25,17},{2,10},{10... | collective-permute-start | bytes 73736 | tf_op jit(solution)/shard_map/ppermute | solution.py:461
  27.9 1.4 %collective-permute-start.11 = (bf16[32,384]{1,0:T(8,128)(2,1)S(1)}, bf16[32,384]{1,0:T(8,128)(2,1)S(1)}, u32[]{:S(2)}, u32[]{:S(2)}) collective-permute-start(bf16[32,384]{1,0:T(8,128)(2,1)S(1)} %collective-permute-done.10.refs_2_), channel_id=1, source_target_pairs={{0,2},{2,0},{4,6},{6,4},{1,3},{3,1},{5,7},{7,5},{8,10},{10,8},{12,... | collective-permute-start | bytes 73736 | tf_op jit(solution)/shard_map/ppermute | solution.py:461
  29.3 3.9 %collective-permute-start.12 = (bf16[32,384]{1,0:T(8,128)(2,1)S(1)}, bf16[32,384]{1,0:T(8,128)(2,1)S(1)}, u32[]{:S(2)}, u32[]{:S(2)}) collective-permute-start(bf16[32,384]{1,0:T(8,128)(2,1)S(1)} %add_parts.3.refs_0_), channel_id=1, source_target_pairs={{0,1},{1,0},{2,3},{3,2},{4,5},{5,4},{6,7},{7,6},{8,9},{9,8},{10,11... | collective-permute-start | bytes 73736 | tf_op jit(solution)/shard_map/ppermute | solution.py:461

commit v23 on v20

--- a/solution.py
+++ b/solution.py
@@ -133,12 +133,12 @@
             at += half
 
 
-def join_kernel(counts, xfar, xnear, fields, cot, near, far):
+def join_kernel(counts, xnear, xfar, fields, cot, near, far):
     f, c = x_planes(fields.shape[0], fields, cot, xnear, xfar, counts[0])
     pick_strips([(pick_rows(CI, 0, 6), f[2:-2]), (pick_rows(CH, 0, 6), c)], near, far)
 
 
-def join_outer_kernel(counts, xfar, xnear, fields, cot, near, far):
+def join_outer_kernel(counts, xnear, xfar, fields, cot, near, far):
     f, _ = x_planes(fields.shape[0], fields, cot, xnear, xfar, counts[0])
     ends = f[:2] + f[-2:]
     pick_strips([(pick_rows(CI, 0, 6), ends), (pick_rows(CI, 2, 4), ends + f[2:-2])], near, far)
@@ -244,7 +244,7 @@
     return jnp.concatenate([edge[:32], middle, edge[32:]], axis=0)
 
 
-def own_kernel(counts, xfar, xnear, fields, cot, t1, tb, b1, fs, cs, pre, back, hidden, dpre):
+def own_kernel(counts, xnear, xfar, fields, cot, t1, tb, b1, fs, cs, pre, back, hidden, dpre):
     count, lanes = fields.shape[0], pre.shape[1]
     f, c = x_planes(count, fields, cot, xnear, xfar, counts[0])
     for ref, rows in ((fs, f), (cs, c)):
@@ -490,9 +490,9 @@
         "band_matrices",
         flops=4_000_000_000,
     )(w1, w2, first_bias[None], second_bias[None])
-    xfar, xnear, t1o, tbo = lax.optimization_barrier((xfar, xnear, t1o, tbo))
+    xnear, xfar, t1o, tbo = lax.optimization_barrier((xnear, xfar, t1o, tbo))
     inner, outer = shape((planes + 4) * 48, Z), shape(128 + (planes + 4) * 16, Z)
-    near, far = call(functools.partial(join_kernel, counts), (inner, inner), "join_strips")(xfar, xnear, f_rows, c_rows)
+    near, far = call(functools.partial(join_kernel, counts), (inner, inner), "join_strips")(xnear, xfar, f_rows, c_rows)
     rnear, rfar = exchange(near, far, "radial", "stream")
     half, half_f32 = shape(64, planes * Z), shape(64, planes * Z, dtype=F32)
     fs, cs, pre, back, hidden, dpre = call(
@@ -500,10 +500,10 @@
         (shape(256, wide + 4 * Z), shape(384, wide), half_f32, half_f32, half, half),
         "own_rows",
         flops=1_000_000_000,
-    )(xfar, xnear, f_rows, c_rows, t1o, tbo, b1)
+    )(xnear, xfar, f_rows, c_rows, t1o, tbo, b1)
     f_rows, fs = lax.optimization_barrier((f_rows, fs))
     near_outer, far_outer = call(functools.partial(join_outer_kernel, counts), (outer, outer), "join_outer")(
-        xfar, xnear, f_rows, c_rows)
+        xnear, xfar, f_rows, c_rows)
     rnear_outer, rfar_outer = exchange(near_outer, far_outer, "radial", "stream")
     hidden, payload = call(
         functools.partial(rim_kernel, counts),

time: 34.3 us -> 33.9 us (0.988)
  waiting for transfers between devices: 6.68 us -> 6.2 us
    ppermute x3, starting transfers between devices: 4.15 us -> 3.09 us  [exchange(): return (lax.ppermute(near, axis, [(i, i ^ 1) for i in range(count)]), far)]
    ppermute x6, starting transfers between devices: 3.5 us -> 4.35 us  [swap(): lax.ppermute(v, axis, [(i, i ^ mask) for i in range(count)])]
    ppermute x3, starting transfers between devices: 4.02 us -> 4.62 us  [exchange(): far = lax.ppermute(far, axes, pairs)]
    ppermute x1, waiting for transfers between devices: 2.47 us -> 2.08 us  [stream_round(): apart = lax.ppermute(v, ('stream', 'radial'), pairs)]
where the time goes in v23:
time: 33.9 us; the launch traced here: 33.7 us
  starting transfers between devices  15 us (44%)
  Pallas kernels  10.6 us (31%)
  waiting for transfers between devices  6.2 us (18%)
  other arithmetic  1.02 us (3%)
  between operations  0.83 us (2%)
    ppermute x3, starting transfers between devices, exchange(): far = lax.ppermute(far, axes, pairs)  4.62 us
    ppermute x6, starting transfers between devices, swap(): lax.ppermute(v, axis, [(i, i ^ mask) for i in range(count)])  4.35 us
    ppermute x6, waiting for transfers between devices, swap(): lax.ppermute(v, axis, [(i, i ^ mask) for i in range(count)])  3.12 us
    ppermute x3, starting transfers between devices, exchange(): return (lax.ppermute(near, axis, [(i, i ^ 1) for i in range(count)]), far)  3.09 us
    ppermute x1, starting transfers between devices, stream_round(): apart = lax.ppermute(v, ('stream', 'radial'), pairs)  2.94 us
    pallas_call x1, Pallas kernels, local(): call(functools.partial(rim_kernel, counts), (shape(planes, 128, Z), shape...  2.7 us
    pallas_call x1, Pallas kernels, local(): call(band_kernel, (shape(192, 768), shape(128, 384), shape(192, 768), sha...  2.7 us
    ppermute x1, waiting for transfers between devices, stream_round(): apart = lax.ppermute(v, ('stream', 'radial'), pairs)  2.08 us
  transfers between devices with their start and end apart: 13, of which 7 were waited for; matrix products, arithmetic and copies ran while one was open for 0% of the time, Pallas kernels for 28%

profile of v23, /device:TPU:0, one launch (start us, length us, event | category | flops | bytes accessed | tf_op | source)
XLA Modules:
  0.0 33.7 jit_solution(4906810952582867558)
XLA Ops:
  0.6 1.0 %pad_maximum_fusion.inputs = bf16[24,8,8,128]{3,2,1,0:T(8,128)(2,1)S(1)} fusion(bf16[16,8,8,128]{3,2,1,0:T(8,128)(2,1)} %bitcast.21, bf16[8,8,8,128]{3,2,1,0:T(8,128)(2,1)} %bitcast.22), kind=kLoop, calls=%fused_computation | loop fusion | flops 196608 | bytes 786432 | tf_op jit(solution)/shard_map/concatenate | solution.py:482
  1.7 0.0 copy-start
  1.7 0.0 copy-start.1
  1.7 0.0 copy-start.2
  1.7 0.0 copy-start.3
  1.7 0.1 pack_strips.1
  1.8 3.1 %collective-permute-start = (bf16[512,128]{1,0:T(8,128)(2,1)S(1)}, bf16[512,128]{1,0:T(8,128)(2,1)S(1)}, u32[]{:S(2)}, u32[]{:S(2)}) collective-permute-start(bf16[512,128]{1,0:T(8,128)(2,1)S(1)} %get-tuple-element.39), channel_id=1, source_target_pairs={{0,8},{8,0},{16,24},{24,16},{1,9},{9,1},{17,25},{25,17},{2,10},{10... | collective-permute-start | bytes 393224 | tf_op jit(solution)/shard_map/ppermute | solution.py:435
  4.9 0.0 collective-permute-start.1
  4.9 0.0 copy-done
  4.9 0.0 copy-done.1
  4.9 0.0 copy-done.2
  4.9 0.0 copy-done.3
  5.0 2.7 %band_matrices.1 = (bf16[192,768]{1,0:T(8,128)(2,1)S(1)}, bf16[128,384]{1,0:T(8,128)(2,1)S(1)}, bf16[192,768]{1,0:T(8,128)(2,1)S(1)}, bf16[128,1152]{1,0:T(8,128...) custom-call(bf16[128,27]{1,0:T(8,128)(2,1)S(1)} %bitcast.18, ...), custom_call_target="tpu_custom_call" | custom-call | flops 4000000000 | bytes 1000000 | tf_op jit(solution)/shard_map/band_matrices/pallas_call | solution.py:486
  7.7 0.8 %collective-permute-done.xnear = bf16[512,128]{1,0:T(8,128)(2,1)S(1)} collective-permute-done((bf16[512,128]{1,0:T(8,128)(2,1)S(1)}, bf16[512,128]{1,0:T(8,128)(2,1)S(1)}, u32[]{:S(2)}, u32[]{:S(2)}) %collective-permute-start) | collective-permute-done | bytes 131104 | tf_op jit(solution)/shard_map/ppermute | solution.py:435
  8.4 0.0 collective-permute-done.1.xfar
  8.4 0.3 join_strips.1
  8.7 2.9 %collective-permute-start.2 = (bf16[576,128]{1,0:T(8,128)(2,1)S(1)}, bf16[576,128]{1,0:T(8,128)(2,1)S(1)}, u32[]{:S(2)}, u32[]{:S(2)}) collective-permute-start(bf16[576,128]{1,0:T(8,128)(2,1)S(1)} %get-tuple-element.47), channel_id=1, source_target_pairs={{0,8},{8,0},{16,24},{24,16},{2,4},{10,12},{18,20},{26,28},{4,2},{1... | collective-permute-start | bytes 442376 | tf_op jit(solution)/shard_map/ppermute | solution.py:434
  11.7 0.0 collective-permute-start.3
  11.7 0.0 copy-start.4
  11.7 0.0 copy-start.5
  11.7 0.0 copy-start.6
  11.7 0.0 copy-start.7
  11.7 0.0 copy-start.8
  11.7 0.0 copy-start.9
  11.7 0.9 %own_rows.1 = (bf16[256,2048]{1,0:T(8,128)(2,1)S(1)}, bf16[384,1536]{1,0:T(8,128)(2,1)S(1)}, f32[64,1024]{1,0:T(8,128)S(1)}, f32[64,1024]{1,0:T(8,128)S(1)}, bf1...) custom-call(bf16[512,128]{1,0:T(8,128)(2,1)S(1)} %collective-permute-done.xnear, ...), custom_call_target="tpu_custom_call" | custom-call | flops 1000000000 | bytes 1000000 | tf_op jit(solution)/shard_map/own_rows/pallas_call | solution.py:498
  12.6 0.2 join_outer.1
  12.9 1.7 %collective-permute-start.7 = (bf16[320,128]{1,0:T(8,128)(2,1)S(1)}, bf16[320,128]{1,0:T(8,128)(2,1)S(1)}, u32[]{:S(2)}, u32[]{:S(2)}) collective-permute-start(bf16[320,128]{1,0:T(8,128)(2,1)S(1)} %get-tuple-element.63), channel_id=1, source_target_pairs={{0,8},{8,0},{16,24},{24,16},{2,4},{10,12},{18,20},{26,28},{4,2},{1... | collective-permute-start | bytes 245768 | tf_op jit(solution)/shard_map/ppermute | solution.py:434
  14.5 0.0 collective-permute-start.8
  14.6 0.2 collective-permute-done.2.rfar
  14.8 0.0 collective-permute-done.3.rnear
  14.8 0.0 copy-done.4
  14.8 0.0 copy-done.5
  14.8 0.0 copy-done.6
  14.8 0.0 copy-done.7
  14.8 0.0 copy-done.8
  14.8 0.0 copy-done.9
  14.8 2.7 %gradients.1 = (bf16[8,128,128]{2,1,0:T(8,128)(2,1)S(1)}, bf16[32,384]{1,0:T(8,128)(2,1)S(1)}) custom-call(bf16[576,128]{1,0:T(8,128)(2,1)S(1)} %collective-permute-done.2.rfar, bf16[576,128]{1,0:T(8,128)(2,1)S(1)} %collective-permute-done.3.rnear, bf16[256,2048]{1,0:T(8,128)(2,1)S(1)} %get-tuple-element.53.fs, bf16[384,1536]{1,0:T(8,128)(2,1)S(1)} %get-tuple-element.54.cs, ...), custom_call_target="tpu_custom_call" | custom-call | flops 2000000000 | bytes 1000000 | tf_op jit(solution)/shard_map/gradients/pallas_call | solution.py:508
  17.5 0.4 %collective-permute-start.4 = (bf16[32,384]{1,0:T(8,128)(2,1)S(1)}, bf16[32,384]{1,0:T(8,128)(2,1)S(1)}, u32[]{:S(2)}, u32[]{:S(2)}) collective-permute-start(bf16[32,384]{1,0:T(8,128)(2,1)S(1)} %get-tuple-element.61.refs_0_), channel_id=1, source_target_pairs={{0,2},{2,0},{4,6},{6,4},{1,3},{3,1},{5,7},{7,5},{8,10},{10,8},{12,... | collective-permute-start | bytes 73736 | tf_op jit(solution)/shard_map/ppermute | solution.py:440
  17.9 0.5 %collective-permute-start.5 = (bf16[32,384]{1,0:T(8,128)(2,1)S(1)}, bf16[32,384]{1,0:T(8,128)(2,1)S(1)}, u32[]{:S(2)}, u32[]{:S(2)}) collective-permute-start(bf16[32,384]{1,0:T(8,128)(2,1)S(1)} %get-tuple-element.61.refs_0_), channel_id=1, source_target_pairs={{0,4},{2,6},{4,0},{6,2},{1,5},{3,7},{5,1},{7,3},{8,12},{10,14},{12... | collective-permute-start | bytes 73736 | tf_op jit(solution)/shard_map/ppermute | solution.py:440
  18.4 1.1 %collective-permute-start.6 = (bf16[32,384]{1,0:T(8,128)(2,1)S(1)}, bf16[32,384]{1,0:T(8,128)(2,1)S(1)}, u32[]{:S(2)}, u32[]{:S(2)}) collective-permute-start(bf16[32,384]{1,0:T(8,128)(2,1)S(1)} %get-tuple-element.61.refs_0_), channel_id=1, source_target_pairs={{0,6},{2,4},{4,2},{6,0},{1,7},{3,5},{5,3},{7,1},{8,14},{10,12},{12... | collective-permute-start | bytes 73736 | tf_op jit(solution)/shard_map/ppermute | solution.py:440
  19.5 0.0 collective-permute-done.7.rfar_outer
  19.5 0.0 collective-permute-done.8.rnear_outer
  19.5 1.3 %hidden_rim.1.hidden = bf16[12,192,128]{2,1,0:T(8,128)(2,1)S(1)} custom-call(bf16[576,128]{1,0:T(8,128)(2,1)S(1)} %collective-permute-done.2.rfar, bf16[576,128]{1,0:T(8,128)(2,1)S(1)} %collective-permute-done.3.rnear, bf16[320,128]{1,0:T(8,128)(2,1)S(1)} %collective-permute-done.7.rfar_outer, bf16[320,128]{1,0:T(8,128)(2,1)S(1)} %collective-permute-done.8.rnear_outer, ...), custom_call_target="tpu_custom_call" | custom-call | flops 1000000000 | bytes 1000000 | tf_op jit(solution)/shard_map/hidden_rim/pallas_call | solution.py:518
  20.7 0.0 collective-permute-done.4.refs_1_
  20.8 1.2 %collective-permute-done.5.refs_2_ = bf16[32,384]{1,0:T(8,128)(2,1)S(1)} collective-permute-done((bf16[32,384]{1,0:T(8,128)(2,1)S(1)}, bf16[32,384]{1,0:T(8,128)(2,1)S(1)}, u32[]{:S(2)}, u32[]{:S(2)}) %collective-permute-start.5) | collective-permute-done | bytes 24608 | tf_op jit(solution)/shard_map/ppermute | solution.py:440
  21.9 0.0 collective-permute-done.6.refs_3_
  21.9 2.9 %collective-permute-start.10 = (bf16[32,384]{1,0:T(8,128)(2,1)S(1)}, bf16[32,384]{1,0:T(8,128)(2,1)S(1)}, u32[]{:S(2)}, u32[]{:S(2)}) collective-permute-start(bf16[32,384]{1,0:T(8,128)(2,1)S(1)} %add_parts.2.refs_0_), channel_id=1, source_target_pairs={{0,24},{2,18},{4,28},{6,22},{8,16},{10,26},{12,20},{14,30},{16,8},... | collective-permute-start | bytes 73736 | tf_op jit(solution)/shard_map/ppermute | solution.py:446
  24.9 0.9 %collective-permute-start.9 = (bf16[32,384]{1,0:T(8,128)(2,1)S(1)}, bf16[32,384]{1,0:T(8,128)(2,1)S(1)}, u32[]{:S(2)}, u32[]{:S(2)}) collective-permute-start(bf16[32,384]{1,0:T(8,128)(2,1)S(1)} %add_parts.2.refs_0_), channel_id=1, source_target_pairs={{0,8},{8,0},{16,24},{24,16},{1,9},{9,1},{17,25},{25,17},{2,10},{10... | collective-permute-start | bytes 73736 | tf_op jit(solution)/shard_map/ppermute | solution.py:440
  25.7 2.1 %collective-permute-done.10.refs_2_ = bf16[32,384]{1,0:T(8,128)(2,1)S(1)} collective-permute-done((bf16[32,384]{1,0:T(8,128)(2,1)S(1)}, bf16[32,384]{1,0:T(8,128)(2,1)S(1)}, u32[]{:S(2)}, u32[]{:S(2)}) %collective-permute-start.10) | collective-permute-done | bytes 24608 | tf_op jit(solution)/shard_map/ppermute | solution.py:446
  27.8 0.0 collective-permute-start.11
  27.8 0.9 %collective-permute-done.9.refs_1_ = bf16[32,384]{1,0:T(8,128)(2,1)S(1)} collective-permute-done((bf16[32,384]{1,0:T(8,128)(2,1)S(1)}, bf16[32,384]{1,0:T(8,128)(2,1)S(1)}, u32[]{:S(2)}, u32[]{:S(2)}) %collective-permute-start.9) | collective-permute-done | bytes 24608 | tf_op jit(solution)/shard_map/ppermute | solution.py:440
  28.7 0.3 collective-permute-done.11.refs_3_
  29.0 1.6 %collective-permute-start.12 = (bf16[32,384]{1,0:T(8,128)(2,1)S(1)}, bf16[32,384]{1,0:T(8,128)(2,1)S(1)}, u32[]{:S(2)}, u32[]{:S(2)}) collective-permute-start(bf16[32,384]{1,0:T(8,128)(2,1)S(1)} %add_parts.3.refs_0_), channel_id=1, source_target_pairs={{0,1},{1,0},{2,3},{3,2},{4,5},{5,4},{6,7},{7,6},{8,9},{9,8},{10,11... | collective-permute-start | bytes 73736 | tf_op jit(solution)/shard_map/ppermute | solution.py:440
  30.6 1.6 %closure.1 = bf16[1,16,8,8,128]{4,3,2,1,0:T(8,128)(2,1)} custom-call(bf16[12,192,128]{2,1,0:T(8,128)(2,1)S(1)} %hidden_rim.1.hidden, bf16[128,1920]{1,0:T(8,128)(2,1)S(1)} %get-tuple-element.68.t2, f32[128,128]{1,0:T(8,128)S(1)} %get-tuple-element.69.b2), custom_call_target="tpu_custom_call" | custom-call | flops 1000000000 | bytes 1000000 | tf_op jit(solution)/shard_map/closure/pallas_call | solution.py:528
  32.2 0.8 %collective-permute-done.12.refs_1_ = bf16[32,384]{1,0:T(8,128)(2,1)S(1)} collective-permute-done((bf16[32,384]{1,0:T(8,128)(2,1)S(1)}, bf16[32,384]{1,0:T(8,128)(2,1)S(1)}, u32[]{:S(2)}, u32[]{:S(2)}) %collective-permute-start.12) | collective-permute-done | bytes 24608 | tf_op jit(solution)/shard_map/ppermute | solution.py:440
  32.9 0.8 %finish.1 = (f32[128,27]{1,0:T(8,128)}, f32[256,27]{1,0:T(8,128)}, f32[1,16]{1,0:T(1,128)}) custom-call(bf16[32,384]{1,0:T(8,128)(2,1)S(1)} %add_parts.3.refs_0_, bf16[32,384]{1,0:T(8,128)(2,1)S(1)} %collective-permute-done.12.refs_1_), custom_call_target="tpu_custom_call" | custom-call | flops 10000000 | bytes 1000000 | tf_op jit(solution)/shard_map/finish/pallas_call | solution.py:539
  (2 shorter events, 0.0 us)
Async XLA Ops:
  1.7 3.3 %copy-start = (bf16[27,16,16]{0,2,1:T(8,128)(2,1)S(1)}, bf16[27,16,16]{0,2,1:T(8,128)(2,1)}, u32[]{:S(2)}) copy-start(bf16[27,16,16]{0,2,1:T(8,128)(2,1)} %param.15) | copy-start | bytes 41476
  1.7 3.3 %copy-start.1 = (bf16[27,16,8]{0,2,1:T(8,128)(2,1)S(1)}, bf16[27,16,8]{0,2,1:T(8,128)(2,1)}, u32[]{:S(2)}) copy-start(bf16[27,16,8]{0,2,1:T(8,128)(2,1)} %param.13) | copy-start | bytes 20740
  1.7 3.3 %copy-start.2 = (f32[16]{0:T(128)S(1)}, f32[16]{0:T(128)}, u32[]{:S(2)}) copy-start(f32[16]{0:T(128)} %param.14) | copy-start | bytes 196
  1.7 3.3 %copy-start.3 = (f32[16]{0:T(128)S(1)}, f32[16]{0:T(128)}, u32[]{:S(2)}) copy-start(f32[16]{0:T(128)} %param.16) | copy-start | bytes 196
  1.8 6.6 %collective-permute-start = (bf16[512,128]{1,0:T(8,128)(2,1)S(1)}, bf16[512,128]{1,0:T(8,128)(2,1)S(1)}, u32[]{:S(2)}, u32[]{:S(2)}) collective-permute-start(bf16[512,128]{1,0:T(8,128)(2,1)S(1)} %get-tuple-element.39), channel_id=1, source_target_pairs={{0,8},{8,0},{16,24},{24,16},{1,9},{9,1},{17,25},{25,17},{2,10},{10... | collective-permute-start | bytes 393224 | tf_op jit(solution)/shard_map/ppermute | solution.py:435
  4.9 3.5 %collective-permute-start.1 = (bf16[512,128]{1,0:T(8,128)(2,1)S(1)}, bf16[512,128]{1,0:T(8,128)(2,1)S(1)}, u32[]{:S(2)}, u32[]{:S(2)}) collective-permute-start(bf16[512,128]{1,0:T(8,128)(2,1)S(1)} %get-tuple-element.40), channel_id=1, source_target_pairs={{0,2},{2,0},{4,6},{6,4},{8,16},{10,18},{12,20},{14,22},{16,8},{18,... | collective-permute-start | bytes 393224 | tf_op jit(solution)/shard_map/ppermute | solution.py:434
  8.7 6.1 %collective-permute-start.2 = (bf16[576,128]{1,0:T(8,128)(2,1)S(1)}, bf16[576,128]{1,0:T(8,128)(2,1)S(1)}, u32[]{:S(2)}, u32[]{:S(2)}) collective-permute-start(bf16[576,128]{1,0:T(8,128)(2,1)S(1)} %get-tuple-element.47), channel_id=1, source_target_pairs={{0,8},{8,0},{16,24},{24,16},{2,4},{10,12},{18,20},{26,28},{4,2},{1... | collective-permute-start | bytes 442376 | tf_op jit(solution)/shard_map/ppermute | solution.py:434
  11.7 3.1 %collective-permute-start.3 = (bf16[576,128]{1,0:T(8,128)(2,1)S(1)}, bf16[576,128]{1,0:T(8,128)(2,1)S(1)}, u32[]{:S(2)}, u32[]{:S(2)}) collective-permute-start(bf16[576,128]{1,0:T(8,128)(2,1)S(1)} %get-tuple-element.48), channel_id=1, source_target_pairs={{0,2},{2,0},{4,6},{6,4},{1,3},{3,1},{5,7},{7,5},{8,10},{10,8},{12,... | collective-permute-start | bytes 442376 | tf_op jit(solution)/shard_map/ppermute | solution.py:435
  11.7 3.1 %copy-start.4 = (bf16[128,768]{1,0:T(8,128)(2,1)S(1)}, bf16[128,768]{1,0:T(8,128)(2,1)}, u32[]{:S(2)}) copy-start(bf16[128,768]{1,0:T(8,128)(2,1)} %constant.15.clone.rep2) | copy-start | bytes 589828
  11.7 3.1 %copy-start.5 = (bf16[640,128]{1,0:T(8,128)(2,1)S(1)}, bf16[640,128]{1,0:T(8,128)(2,1)}, u32[]{:S(2)}) copy-start(bf16[640,128]{1,0:T(8,128)(2,1)} %constant.13.clone.e2t) | copy-start | bytes 491524
  11.7 3.1 %copy-start.6 = (bf16[384,128]{1,0:T(8,128)(2,1)S(1)}, bf16[384,128]{1,0:T(8,128)(2,1)}, u32[]{:S(2)}) copy-start(bf16[384,128]{1,0:T(8,128)(2,1)} %constant.12.clone.e1t) | copy-start | bytes 294916
  11.7 3.1 %copy-start.7 = (bf16[128,384]{1,0:T(8,128)(2,1)S(1)}, bf16[128,384]{1,0:T(8,128)(2,1)}, u32[]{:S(2)}) copy-start(bf16[128,384]{1,0:T(8,128)(2,1)} %constant.14.clone.rep1) | copy-start | bytes 294916
  11.7 3.1 %copy-start.8 = (f32[1,640]{1,0:T(1,128)S(1)}, f32[1,640]{1,0:T(1,128)}, u32[]{:S(2)}) copy-start(f32[1,640]{1,0:T(1,128)} %constant.17.clone.y2) | copy-start | bytes 7684
  11.7 3.1 %copy-start.9 = (f32[1,384]{1,0:T(1,128)S(1)}, f32[1,384]{1,0:T(1,128)}, u32[]{:S(2)}) copy-start(f32[1,384]{1,0:T(1,128)} %constant.16.clone.y1) | copy-start | bytes 4612
  12.9 6.6 %collective-permute-start.7 = (bf16[320,128]{1,0:T(8,128)(2,1)S(1)}, bf16[320,128]{1,0:T(8,128)(2,1)S(1)}, u32[]{:S(2)}, u32[]{:S(2)}) collective-permute-start(bf16[320,128]{1,0:T(8,128)(2,1)S(1)} %get-tuple-element.63), channel_id=1, source_target_pairs={{0,8},{8,0},{16,24},{24,16},{2,4},{10,12},{18,20},{26,28},{4,2},{1... | collective-permute-start | bytes 245768 | tf_op jit(solution)/shard_map/ppermute | solution.py:434
  14.5 4.9 %collective-permute-start.8 = (bf16[320,128]{1,0:T(8,128)(2,1)S(1)}, bf16[320,128]{1,0:T(8,128)(2,1)S(1)}, u32[]{:S(2)}, u32[]{:S(2)}) collective-permute-start(bf16[320,128]{1,0:T(8,128)(2,1)S(1)} %get-tuple-element.64), channel_id=1, source_target_pairs={{0,2},{2,0},{4,6},{6,4},{1,3},{3,1},{5,7},{7,5},{8,10},{10,8},{12,... | collective-permute-start | bytes 245768 | tf_op jit(solution)/shard_map/ppermute | solution.py:435
  17.5 3.2 %collective-permute-start.4 = (bf16[32,384]{1,0:T(8,128)(2,1)S(1)}, bf16[32,384]{1,0:T(8,128)(2,1)S(1)}, u32[]{:S(2)}, u32[]{:S(2)}) collective-permute-start(bf16[32,384]{1,0:T(8,128)(2,1)S(1)} %get-tuple-element.61.refs_0_), channel_id=1, source_target_pairs={{0,2},{2,0},{4,6},{6,4},{1,3},{3,1},{5,7},{7,5},{8,10},{10,8},{12,... | collective-permute-start | bytes 73736 | tf_op jit(solution)/shard_map/ppermute | solution.py:440
  17.9 4.0 %collective-permute-start.5 = (bf16[32,384]{1,0:T(8,128)(2,1)S(1)}, bf16[32,384]{1,0:T(8,128)(2,1)S(1)}, u32[]{:S(2)}, u32[]{:S(2)}) collective-permute-start(bf16[32,384]{1,0:T(8,128)(2,1)S(1)} %get-tuple-element.61.refs_0_), channel_id=1, source_target_pairs={{0,4},{2,6},{4,0},{6,2},{1,5},{3,7},{5,1},{7,3},{8,12},{10,14},{12... | collective-permute-start | bytes 73736 | tf_op jit(solution)/shard_map/ppermute | solution.py:440
  18.4 3.5 %collective-permute-start.6 = (bf16[32,384]{1,0:T(8,128)(2,1)S(1)}, bf16[32,384]{1,0:T(8,128)(2,1)S(1)}, u32[]{:S(2)}, u32[]{:S(2)}) collective-permute-start(bf16[32,384]{1,0:T(8,128)(2,1)S(1)} %get-tuple-element.61.refs_0_), channel_id=1, source_target_pairs={{0,6},{2,4},{4,2},{6,0},{1,7},{3,5},{5,3},{7,1},{8,14},{10,12},{12... | collective-permute-start | bytes 73736 | tf_op jit(solution)/shard_map/ppermute | solution.py:440
  21.9 5.9 %collective-permute-start.10 = (bf16[32,384]{1,0:T(8,128)(2,1)S(1)}, bf16[32,384]{1,0:T(8,128)(2,1)S(1)}, u32[]{:S(2)}, u32[]{:S(2)}) collective-permute-start(bf16[32,384]{1,0:T(8,128)(2,1)S(1)} %add_parts.2.refs_0_), channel_id=1, source_target_pairs={{0,24},{2,18},{4,28},{6,22},{8,16},{10,26},{12,20},{14,30},{16,8},... | collective-permute-start | bytes 73736 | tf_op jit(solution)/shard_map/ppermute | solution.py:446
  24.9 3.8 %collective-permute-start.9 = (bf16[32,384]{1,0:T(8,128)(2,1)S(1)}, bf16[32,384]{1,0:T(8,128)(2,1)S(1)}, u32[]{:S(2)}, u32[]{:S(2)}) collective-permute-start(bf16[32,384]{1,0:T(8,128)(2,1)S(1)} %add_parts.2.refs_0_), channel_id=1, source_target_pairs={{0,8},{8,0},{16,24},{24,16},{1,9},{9,1},{17,25},{25,17},{2,10},{10... | collective-permute-start | bytes 73736 | tf_op jit(solution)/shard_map/ppermute | solution.py:440
  27.8 1.2 %collective-permute-start.11 = (bf16[32,384]{1,0:T(8,128)(2,1)S(1)}, bf16[32,384]{1,0:T(8,128)(2,1)S(1)}, u32[]{:S(2)}, u32[]{:S(2)}) collective-permute-start(bf16[32,384]{1,0:T(8,128)(2,1)S(1)} %collective-permute-done.10.refs_2_), channel_id=1, source_target_pairs={{0,2},{2,0},{4,6},{6,4},{1,3},{3,1},{5,7},{7,5},{8,10},{10,8},{12,... | collective-permute-start | bytes 73736 | tf_op jit(solution)/shard_map/ppermute | solution.py:440
  29.0 3.9 %collective-permute-start.12 = (bf16[32,384]{1,0:T(8,128)(2,1)S(1)}, bf16[32,384]{1,0:T(8,128)(2,1)S(1)}, u32[]{:S(2)}, u32[]{:S(2)}) collective-permute-start(bf16[32,384]{1,0:T(8,128)(2,1)S(1)} %add_parts.3.refs_0_), channel_id=1, source_target_pairs={{0,1},{1,0},{2,3},{3,2},{4,5},{5,4},{6,7},{7,6},{8,9},{9,8},{10,11... | collective-permute-start | bytes 73736 | tf_op jit(solution)/shard_map/ppermute | solution.py:440

commit v24 on v22

--- a/solution.py
+++ b/solution.py
@@ -138,7 +138,7 @@
     pick_strips([(pick_rows(CI, 0, 6), [fields[x] for x in planes]), (pick_rows(CH, 0, 6), [cot[x] for x in planes])], near, far)
 
 
-def join_kernel(counts, xfar, xnear, near_own, far_own, near, far):
+def join_kernel(counts, xnear, xfar, near_own, far_own, near, far):
     up_first = lax.axis_index("radial") % 2 == 0
     index, count = lax.axis_index("stream"), near_own.shape[0] // 48
     at = own_at = 0
@@ -159,7 +159,7 @@
         own_at += count * half
 
 
-def join_outer_kernel(counts, xfar, xnear, fields, cot, near, far):
+def join_outer_kernel(counts, xnear, xfar, fields, cot, near, far):
     f, _ = x_planes(fields.shape[0], fields, cot, xnear, xfar, counts[0])
     ends = f[:2] + f[-2:]
     pick_strips([(pick_rows(CI, 0, 6), ends), (pick_rows(CI, 2, 4), ends + f[2:-2])], near, far)
@@ -265,7 +265,7 @@
     return jnp.concatenate([edge[:32], middle, edge[32:]], axis=0)
 
 
-def own_kernel(counts, xfar, xnear, fields, cot, t1, tb, b1, fs, cs, pre, back, hidden, dpre):
+def own_kernel(counts, xnear, xfar, fields, cot, t1, tb, b1, fs, cs, pre, back, hidden, dpre):
     count, lanes = fields.shape[0], pre.shape[1]
     f, c = x_planes(count, fields, cot, xnear, xfar, counts[0])
     for ref, rows in ((fs, f), (cs, c)):
@@ -512,9 +512,9 @@
         flops=4_000_000_000,
     )(w1, w2, first_bias[None], second_bias[None])
     near_own, far_own = call(own_strips_kernel, (shape(planes * 48, Z),) * 2, "own_strips")(f_rows, c_rows)
-    xfar, xnear, t1o, tbo = lax.optimization_barrier((xfar, xnear, t1o, tbo))
+    xnear, xfar, t1o, tbo = lax.optimization_barrier((xnear, xfar, t1o, tbo))
     inner, outer = shape((planes + 4) * 48, Z), shape(128 + (planes + 4) * 16, Z)
-    near, far = call(functools.partial(join_kernel, counts), (inner, inner), "join_strips")(xfar, xnear, near_own, far_own)
+    near, far = call(functools.partial(join_kernel, counts), (inner, inner), "join_strips")(xnear, xfar, near_own, far_own)
     rnear, rfar = exchange(near, far, "radial", "stream")
     half, half_f32 = shape(64, planes * Z), shape(64, planes * Z, dtype=F32)
     fs, cs, pre, back, hidden, dpre = call(
@@ -522,10 +522,10 @@
         (shape(256, wide + 4 * Z), shape(384, wide), half_f32, half_f32, half, half),
         "own_rows",
         flops=1_000_000_000,
-    )(xfar, xnear, f_rows, c_rows, t1o, tbo, b1)
+    )(xnear, xfar, f_rows, c_rows, t1o, tbo, b1)
     f_rows, fs = lax.optimization_barrier((f_rows, fs))
     near_outer, far_outer = call(functools.partial(join_outer_kernel, counts), (outer, outer), "join_outer")(
-        xfar, xnear, f_rows, c_rows)
+        xnear, xfar, f_rows, c_rows)
     rnear_outer, rfar_outer = exchange(near_outer, far_outer, "radial", "stream")
     hidden, payload = call(
         functools.partial(rim_kernel, counts),

time: 34.2 us -> 33.8 us (0.988)
  waiting for transfers between devices: 6.45 us -> 5.96 us
    ppermute x3, starting transfers between devices: 4.15 us -> 3.09 us  [exchange(): return (lax.ppermute(near, axis, [(i, i ^ 1) for i in range(count)]), far)]
    ppermute x6, starting transfers between devices: 3.5 us -> 4.35 us  [swap(): lax.ppermute(v, axis, [(i, i ^ mask) for i in range(count)])]
    ppermute x3, starting transfers between devices: 4.02 us -> 4.62 us  [exchange(): far = lax.ppermute(far, axes, pairs)]
    ppermute x1, waiting for transfers between devices: 2.47 us -> 2.08 us  [stream_round(): apart = lax.ppermute(v, ('stream', 'radial'), pairs)]
  transfers between devices with their start and end apart: 13 -> 13, of which waited for: 7 -> 7; matrix products, arithmetic and copies ran while one was open for 0% -> 0% of each run, Pallas kernels for 28% -> 29%
where the time goes in v24:
time: 33.8 us; the launch traced here: 33.6 us
  starting transfers between devices  15 us (44%)
  Pallas kernels  10.8 us (32%)
  waiting for transfers between devices  5.96 us (18%)
  other arithmetic  1.02 us (3%)
  between operations  0.84 us (2%)
    ppermute x3, starting transfers between devices, exchange(): far = lax.ppermute(far, axes, pairs)  4.62 us
    ppermute x6, starting transfers between devices, swap(): lax.ppermute(v, axis, [(i, i ^ mask) for i in range(count)])  4.35 us
    ppermute x6, waiting for transfers between devices, swap(): lax.ppermute(v, axis, [(i, i ^ mask) for i in range(count)])  3.12 us
    ppermute x3, starting transfers between devices, exchange(): return (lax.ppermute(near, axis, [(i, i ^ 1) for i in range(count)]), far)  3.09 us
    ppermute x1, starting transfers between devices, stream_round(): apart = lax.ppermute(v, ('stream', 'radial'), pairs)  2.94 us
    pallas_call x1, Pallas kernels, local(): call(functools.partial(rim_kernel, counts), (shape(planes, 128, Z), shape...  2.7 us
    pallas_call x1, Pallas kernels, local(): call(band_kernel, (shape(192, 768), shape(128, 384), shape(192, 768), sha...  2.7 us
    ppermute x1, waiting for transfers between devices, stream_round(): apart = lax.ppermute(v, ('stream', 'radial'), pairs)  2.08 us
  transfers between devices with their start and end apart: 13, of which 7 were waited for; matrix products, arithmetic and copies ran while one was open for 0% of the time, Pallas kernels for 29%

profile of v24, /device:TPU:0, one launch (start us, length us, event | category | flops | bytes accessed | tf_op | source)
XLA Modules:
  0.0 33.6 jit_solution(2172885036460269354)
XLA Ops:
  0.6 1.0 %pad_maximum_fusion.inputs = bf16[24,8,8,128]{3,2,1,0:T(8,128)(2,1)S(1)} fusion(bf16[16,8,8,128]{3,2,1,0:T(8,128)(2,1)} %bitcast.21, bf16[8,8,8,128]{3,2,1,0:T(8,128)(2,1)} %bitcast.22), kind=kLoop, calls=%fused_computation | loop fusion | flops 196608 | bytes 786432 | tf_op jit(solution)/shard_map/concatenate | solution.py:503
  1.7 0.0 copy-start
  1.7 0.0 copy-start.1
  1.7 0.0 copy-start.2
  1.7 0.0 copy-start.3
  1.7 0.1 pack_strips.1
  1.8 3.1 %collective-permute-start = (bf16[512,128]{1,0:T(8,128)(2,1)S(1)}, bf16[512,128]{1,0:T(8,128)(2,1)S(1)}, u32[]{:S(2)}, u32[]{:S(2)}) collective-permute-start(bf16[512,128]{1,0:T(8,128)(2,1)S(1)} %get-tuple-element.41), channel_id=1, source_target_pairs={{0,8},{8,0},{16,24},{24,16},{1,9},{9,1},{17,25},{25,17},{2,10},{10... | collective-permute-start | bytes 393224 | tf_op jit(solution)/shard_map/ppermute | solution.py:456
  4.9 0.0 collective-permute-start.1
  4.9 0.0 copy-done
  4.9 0.0 copy-done.1
  4.9 0.0 copy-done.2
  4.9 0.0 copy-done.3
  5.0 2.7 %band_matrices.1 = (bf16[192,768]{1,0:T(8,128)(2,1)S(1)}, bf16[128,384]{1,0:T(8,128)(2,1)S(1)}, bf16[192,768]{1,0:T(8,128)(2,1)S(1)}, bf16[128,1152]{1,0:T(8,128...) custom-call(bf16[128,27]{1,0:T(8,128)(2,1)S(1)} %bitcast.18, ...), custom_call_target="tpu_custom_call" | custom-call | flops 4000000000 | bytes 1000000 | tf_op jit(solution)/shard_map/band_matrices/pallas_call | solution.py:507
  7.7 0.2 own_strips.1
  7.9 0.5 %collective-permute-done.xnear = bf16[512,128]{1,0:T(8,128)(2,1)S(1)} collective-permute-done((bf16[512,128]{1,0:T(8,128)(2,1)S(1)}, bf16[512,128]{1,0:T(8,128)(2,1)S(1)}, u32[]{:S(2)}, u32[]{:S(2)}) %collective-permute-start) | collective-permute-done | bytes 131104 | tf_op jit(solution)/shard_map/ppermute | solution.py:456
  8.4 0.0 collective-permute-done.1.xfar
  8.4 0.2 join_strips.1
  8.6 2.9 %collective-permute-start.2 = (bf16[576,128]{1,0:T(8,128)(2,1)S(1)}, bf16[576,128]{1,0:T(8,128)(2,1)S(1)}, u32[]{:S(2)}, u32[]{:S(2)}) collective-permute-start(bf16[576,128]{1,0:T(8,128)(2,1)S(1)} %get-tuple-element.51), channel_id=1, source_target_pairs={{0,8},{8,0},{16,24},{24,16},{2,4},{10,12},{18,20},{26,28},{4,2},{1... | collective-permute-start | bytes 442376 | tf_op jit(solution)/shard_map/ppermute | solution.py:455
  11.6 0.0 collective-permute-start.3
  11.6 0.0 copy-start.4
  11.6 0.0 copy-start.5
  11.6 0.0 copy-start.6
  11.6 0.0 copy-start.7
  11.6 0.0 copy-start.8
  11.6 0.0 copy-start.9
  11.6 0.9 %own_rows.1 = (bf16[256,2048]{1,0:T(8,128)(2,1)S(1)}, bf16[384,1536]{1,0:T(8,128)(2,1)S(1)}, f32[64,1024]{1,0:T(8,128)S(1)}, f32[64,1024]{1,0:T(8,128)S(1)}, bf1...) custom-call(bf16[512,128]{1,0:T(8,128)(2,1)S(1)} %collective-permute-done.xnear, ...), custom_call_target="tpu_custom_call" | custom-call | flops 1000000000 | bytes 1000000 | tf_op jit(solution)/shard_map/own_rows/pallas_call | solution.py:520
  12.5 0.2 join_outer.1
  12.8 1.7 %collective-permute-start.7 = (bf16[320,128]{1,0:T(8,128)(2,1)S(1)}, bf16[320,128]{1,0:T(8,128)(2,1)S(1)}, u32[]{:S(2)}, u32[]{:S(2)}) collective-permute-start(bf16[320,128]{1,0:T(8,128)(2,1)S(1)} %get-tuple-element.67), channel_id=1, source_target_pairs={{0,8},{8,0},{16,24},{24,16},{2,4},{10,12},{18,20},{26,28},{4,2},{1... | collective-permute-start | bytes 245768 | tf_op jit(solution)/shard_map/ppermute | solution.py:455
  14.4 0.0 collective-permute-start.8
  14.5 0.2 collective-permute-done.2.rfar
  14.7 0.0 collective-permute-done.3.rnear
  14.7 0.0 copy-done.4
  14.7 0.0 copy-done.5
  14.7 0.0 copy-done.6
  14.7 0.0 copy-done.7
  14.7 0.0 copy-done.8
  14.7 0.0 copy-done.9
  14.7 2.7 %gradients.1 = (bf16[8,128,128]{2,1,0:T(8,128)(2,1)S(1)}, bf16[32,384]{1,0:T(8,128)(2,1)S(1)}) custom-call(bf16[576,128]{1,0:T(8,128)(2,1)S(1)} %collective-permute-done.2.rfar, bf16[576,128]{1,0:T(8,128)(2,1)S(1)} %collective-permute-done.3.rnear, bf16[256,2048]{1,0:T(8,128)(2,1)S(1)} %get-tuple-element.57.fs, bf16[384,1536]{1,0:T(8,128)(2,1)S(1)} %get-tuple-element.58.cs, ...), custom_call_target="tpu_custom_call" | custom-call | flops 2000000000 | bytes 1000000 | tf_op jit(solution)/shard_map/gradients/pallas_call | solution.py:530
  17.4 0.4 %collective-permute-start.4 = (bf16[32,384]{1,0:T(8,128)(2,1)S(1)}, bf16[32,384]{1,0:T(8,128)(2,1)S(1)}, u32[]{:S(2)}, u32[]{:S(2)}) collective-permute-start(bf16[32,384]{1,0:T(8,128)(2,1)S(1)} %get-tuple-element.65.refs_0_), channel_id=1, source_target_pairs={{0,2},{2,0},{4,6},{6,4},{1,3},{3,1},{5,7},{7,5},{8,10},{10,8},{12,... | collective-permute-start | bytes 73736 | tf_op jit(solution)/shard_map/ppermute | solution.py:461
  17.8 0.5 %collective-permute-start.5 = (bf16[32,384]{1,0:T(8,128)(2,1)S(1)}, bf16[32,384]{1,0:T(8,128)(2,1)S(1)}, u32[]{:S(2)}, u32[]{:S(2)}) collective-permute-start(bf16[32,384]{1,0:T(8,128)(2,1)S(1)} %get-tuple-element.65.refs_0_), channel_id=1, source_target_pairs={{0,4},{2,6},{4,0},{6,2},{1,5},{3,7},{5,1},{7,3},{8,12},{10,14},{12... | collective-permute-start | bytes 73736 | tf_op jit(solution)/shard_map/ppermute | solution.py:461
  18.3 1.1 %collective-permute-start.6 = (bf16[32,384]{1,0:T(8,128)(2,1)S(1)}, bf16[32,384]{1,0:T(8,128)(2,1)S(1)}, u32[]{:S(2)}, u32[]{:S(2)}) collective-permute-start(bf16[32,384]{1,0:T(8,128)(2,1)S(1)} %get-tuple-element.65.refs_0_), channel_id=1, source_target_pairs={{0,6},{2,4},{4,2},{6,0},{1,7},{3,5},{5,3},{7,1},{8,14},{10,12},{12... | collective-permute-start | bytes 73736 | tf_op jit(solution)/shard_map/ppermute | solution.py:461
  19.4 0.0 collective-permute-done.7.rfar_outer
  19.4 0.0 collective-permute-done.8.rnear_outer
  19.4 1.3 %hidden_rim.1.hidden = bf16[12,192,128]{2,1,0:T(8,128)(2,1)S(1)} custom-call(bf16[576,128]{1,0:T(8,128)(2,1)S(1)} %collective-permute-done.2.rfar, bf16[576,128]{1,0:T(8,128)(2,1)S(1)} %collective-permute-done.3.rnear, bf16[320,128]{1,0:T(8,128)(2,1)S(1)} %collective-permute-done.7.rfar_outer, bf16[320,128]{1,0:T(8,128)(2,1)S(1)} %collective-permute-done.8.rnear_outer, ...), custom_call_target="tpu_custom_call" | custom-call | flops 1000000000 | bytes 1000000 | tf_op jit(solution)/shard_map/hidden_rim/pallas_call | solution.py:540
  20.6 0.0 collective-permute-done.4.refs_1_
  20.7 1.2 %collective-permute-done.5.refs_2_ = bf16[32,384]{1,0:T(8,128)(2,1)S(1)} collective-permute-done((bf16[32,384]{1,0:T(8,128)(2,1)S(1)}, bf16[32,384]{1,0:T(8,128)(2,1)S(1)}, u32[]{:S(2)}, u32[]{:S(2)}) %collective-permute-start.5) | collective-permute-done | bytes 24608 | tf_op jit(solution)/shard_map/ppermute | solution.py:461
  21.8 0.0 collective-permute-done.6.refs_3_
  21.8 2.9 %collective-permute-start.10 = (bf16[32,384]{1,0:T(8,128)(2,1)S(1)}, bf16[32,384]{1,0:T(8,128)(2,1)S(1)}, u32[]{:S(2)}, u32[]{:S(2)}) collective-permute-start(bf16[32,384]{1,0:T(8,128)(2,1)S(1)} %add_parts.2.refs_0_), channel_id=1, source_target_pairs={{0,24},{2,18},{4,28},{6,22},{8,16},{10,26},{12,20},{14,30},{16,8},... | collective-permute-start | bytes 73736 | tf_op jit(solution)/shard_map/ppermute | solution.py:467
  24.8 0.9 %collective-permute-start.9 = (bf16[32,384]{1,0:T(8,128)(2,1)S(1)}, bf16[32,384]{1,0:T(8,128)(2,1)S(1)}, u32[]{:S(2)}, u32[]{:S(2)}) collective-permute-start(bf16[32,384]{1,0:T(8,128)(2,1)S(1)} %add_parts.2.refs_0_), channel_id=1, source_target_pairs={{0,8},{8,0},{16,24},{24,16},{1,9},{9,1},{17,25},{25,17},{2,10},{10... | collective-permute-start | bytes 73736 | tf_op jit(solution)/shard_map/ppermute | solution.py:461
  25.6 2.1 %collective-permute-done.10.refs_2_ = bf16[32,384]{1,0:T(8,128)(2,1)S(1)} collective-permute-done((bf16[32,384]{1,0:T(8,128)(2,1)S(1)}, bf16[32,384]{1,0:T(8,128)(2,1)S(1)}, u32[]{:S(2)}, u32[]{:S(2)}) %collective-permute-start.10) | collective-permute-done | bytes 24608 | tf_op jit(solution)/shard_map/ppermute | solution.py:467
  27.7 0.0 collective-permute-start.11
  27.7 0.9 %collective-permute-done.9.refs_1_ = bf16[32,384]{1,0:T(8,128)(2,1)S(1)} collective-permute-done((bf16[32,384]{1,0:T(8,128)(2,1)S(1)}, bf16[32,384]{1,0:T(8,128)(2,1)S(1)}, u32[]{:S(2)}, u32[]{:S(2)}) %collective-permute-start.9) | collective-permute-done | bytes 24608 | tf_op jit(solution)/shard_map/ppermute | solution.py:461
  28.6 0.3 collective-permute-done.11.refs_3_
  28.9 1.6 %collective-permute-start.12 = (bf16[32,384]{1,0:T(8,128)(2,1)S(1)}, bf16[32,384]{1,0:T(8,128)(2,1)S(1)}, u32[]{:S(2)}, u32[]{:S(2)}) collective-permute-start(bf16[32,384]{1,0:T(8,128)(2,1)S(1)} %add_parts.3.refs_0_), channel_id=1, source_target_pairs={{0,1},{1,0},{2,3},{3,2},{4,5},{5,4},{6,7},{7,6},{8,9},{9,8},{10,11... | collective-permute-start | bytes 73736 | tf_op jit(solution)/shard_map/ppermute | solution.py:461
  30.5 1.6 %closure.1 = bf16[1,16,8,8,128]{4,3,2,1,0:T(8,128)(2,1)} custom-call(bf16[12,192,128]{2,1,0:T(8,128)(2,1)S(1)} %hidden_rim.1.hidden, bf16[128,1920]{1,0:T(8,128)(2,1)S(1)} %get-tuple-element.72.t2, f32[128,128]{1,0:T(8,128)S(1)} %get-tuple-element.73.b2), custom_call_target="tpu_custom_call" | custom-call | flops 1000000000 | bytes 1000000 | tf_op jit(solution)/shard_map/closure/pallas_call | solution.py:550
  32.1 0.8 %collective-permute-done.12.refs_1_ = bf16[32,384]{1,0:T(8,128)(2,1)S(1)} collective-permute-done((bf16[32,384]{1,0:T(8,128)(2,1)S(1)}, bf16[32,384]{1,0:T(8,128)(2,1)S(1)}, u32[]{:S(2)}, u32[]{:S(2)}) %collective-permute-start.12) | collective-permute-done | bytes 24608 | tf_op jit(solution)/shard_map/ppermute | solution.py:461
  32.8 0.8 %finish.1 = (f32[128,27]{1,0:T(8,128)}, f32[256,27]{1,0:T(8,128)}, f32[1,16]{1,0:T(1,128)}) custom-call(bf16[32,384]{1,0:T(8,128)(2,1)S(1)} %add_parts.3.refs_0_, bf16[32,384]{1,0:T(8,128)(2,1)S(1)} %collective-permute-done.12.refs_1_), custom_call_target="tpu_custom_call" | custom-call | flops 10000000 | bytes 1000000 | tf_op jit(solution)/shard_map/finish/pallas_call | solution.py:561
  (2 shorter events, 0.0 us)
Async XLA Ops:
  1.7 3.3 %copy-start = (bf16[27,16,16]{0,2,1:T(8,128)(2,1)S(1)}, bf16[27,16,16]{0,2,1:T(8,128)(2,1)}, u32[]{:S(2)}) copy-start(bf16[27,16,16]{0,2,1:T(8,128)(2,1)} %param.15) | copy-start | bytes 41476
  1.7 3.3 %copy-start.1 = (bf16[27,16,8]{0,2,1:T(8,128)(2,1)S(1)}, bf16[27,16,8]{0,2,1:T(8,128)(2,1)}, u32[]{:S(2)}) copy-start(bf16[27,16,8]{0,2,1:T(8,128)(2,1)} %param.13) | copy-start | bytes 20740
  1.7 3.3 %copy-start.2 = (f32[16]{0:T(128)S(1)}, f32[16]{0:T(128)}, u32[]{:S(2)}) copy-start(f32[16]{0:T(128)} %param.14) | copy-start | bytes 196
  1.7 3.3 %copy-start.3 = (f32[16]{0:T(128)S(1)}, f32[16]{0:T(128)}, u32[]{:S(2)}) copy-start(f32[16]{0:T(128)} %param.16) | copy-start | bytes 196
  1.8 6.6 %collective-permute-start = (bf16[512,128]{1,0:T(8,128)(2,1)S(1)}, bf16[512,128]{1,0:T(8,128)(2,1)S(1)}, u32[]{:S(2)}, u32[]{:S(2)}) collective-permute-start(bf16[512,128]{1,0:T(8,128)(2,1)S(1)} %get-tuple-element.41), channel_id=1, source_target_pairs={{0,8},{8,0},{16,24},{24,16},{1,9},{9,1},{17,25},{25,17},{2,10},{10... | collective-permute-start | bytes 393224 | tf_op jit(solution)/shard_map/ppermute | solution.py:456
  4.9 3.5 %collective-permute-start.1 = (bf16[512,128]{1,0:T(8,128)(2,1)S(1)}, bf16[512,128]{1,0:T(8,128)(2,1)S(1)}, u32[]{:S(2)}, u32[]{:S(2)}) collective-permute-start(bf16[512,128]{1,0:T(8,128)(2,1)S(1)} %get-tuple-element.42), channel_id=1, source_target_pairs={{0,2},{2,0},{4,6},{6,4},{8,16},{10,18},{12,20},{14,22},{16,8},{18,... | collective-permute-start | bytes 393224 | tf_op jit(solution)/shard_map/ppermute | solution.py:455
  8.6 6.1 %collective-permute-start.2 = (bf16[576,128]{1,0:T(8,128)(2,1)S(1)}, bf16[576,128]{1,0:T(8,128)(2,1)S(1)}, u32[]{:S(2)}, u32[]{:S(2)}) collective-permute-start(bf16[576,128]{1,0:T(8,128)(2,1)S(1)} %get-tuple-element.51), channel_id=1, source_target_pairs={{0,8},{8,0},{16,24},{24,16},{2,4},{10,12},{18,20},{26,28},{4,2},{1... | collective-permute-start | bytes 442376 | tf_op jit(solution)/shard_map/ppermute | solution.py:455
  11.6 3.1 %collective-permute-start.3 = (bf16[576,128]{1,0:T(8,128)(2,1)S(1)}, bf16[576,128]{1,0:T(8,128)(2,1)S(1)}, u32[]{:S(2)}, u32[]{:S(2)}) collective-permute-start(bf16[576,128]{1,0:T(8,128)(2,1)S(1)} %get-tuple-element.52), channel_id=1, source_target_pairs={{0,2},{2,0},{4,6},{6,4},{1,3},{3,1},{5,7},{7,5},{8,10},{10,8},{12,... | collective-permute-start | bytes 442376 | tf_op jit(solution)/shard_map/ppermute | solution.py:456
  11.6 3.1 %copy-start.4 = (bf16[128,768]{1,0:T(8,128)(2,1)S(1)}, bf16[128,768]{1,0:T(8,128)(2,1)}, u32[]{:S(2)}) copy-start(bf16[128,768]{1,0:T(8,128)(2,1)} %constant.15.clone.rep2) | copy-start | bytes 589828
  11.6 3.1 %copy-start.5 = (bf16[640,128]{1,0:T(8,128)(2,1)S(1)}, bf16[640,128]{1,0:T(8,128)(2,1)}, u32[]{:S(2)}) copy-start(bf16[640,128]{1,0:T(8,128)(2,1)} %constant.13.clone.e2t) | copy-start | bytes 491524
  11.6 3.1 %copy-start.6 = (bf16[384,128]{1,0:T(8,128)(2,1)S(1)}, bf16[384,128]{1,0:T(8,128)(2,1)}, u32[]{:S(2)}) copy-start(bf16[384,128]{1,0:T(8,128)(2,1)} %constant.12.clone.e1t) | copy-start | bytes 294916
  11.6 3.1 %copy-start.7 = (bf16[128,384]{1,0:T(8,128)(2,1)S(1)}, bf16[128,384]{1,0:T(8,128)(2,1)}, u32[]{:S(2)}) copy-start(bf16[128,384]{1,0:T(8,128)(2,1)} %constant.14.clone.rep1) | copy-start | bytes 294916
  11.6 3.1 %copy-start.8 = (f32[1,640]{1,0:T(1,128)S(1)}, f32[1,640]{1,0:T(1,128)}, u32[]{:S(2)}) copy-start(f32[1,640]{1,0:T(1,128)} %constant.17.clone.y2) | copy-start | bytes 7684
  11.6 3.1 %copy-start.9 = (f32[1,384]{1,0:T(1,128)S(1)}, f32[1,384]{1,0:T(1,128)}, u32[]{:S(2)}) copy-start(f32[1,384]{1,0:T(1,128)} %constant.16.clone.y1) | copy-start | bytes 4612
  12.8 6.6 %collective-permute-start.7 = (bf16[320,128]{1,0:T(8,128)(2,1)S(1)}, bf16[320,128]{1,0:T(8,128)(2,1)S(1)}, u32[]{:S(2)}, u32[]{:S(2)}) collective-permute-start(bf16[320,128]{1,0:T(8,128)(2,1)S(1)} %get-tuple-element.67), channel_id=1, source_target_pairs={{0,8},{8,0},{16,24},{24,16},{2,4},{10,12},{18,20},{26,28},{4,2},{1... | collective-permute-start | bytes 245768 | tf_op jit(solution)/shard_map/ppermute | solution.py:455
  14.4 4.9 %collective-permute-start.8 = (bf16[320,128]{1,0:T(8,128)(2,1)S(1)}, bf16[320,128]{1,0:T(8,128)(2,1)S(1)}, u32[]{:S(2)}, u32[]{:S(2)}) collective-permute-start(bf16[320,128]{1,0:T(8,128)(2,1)S(1)} %get-tuple-element.68), channel_id=1, source_target_pairs={{0,2},{2,0},{4,6},{6,4},{1,3},{3,1},{5,7},{7,5},{8,10},{10,8},{12,... | collective-permute-start | bytes 245768 | tf_op jit(solution)/shard_map/ppermute | solution.py:456
  17.4 3.2 %collective-permute-start.4 = (bf16[32,384]{1,0:T(8,128)(2,1)S(1)}, bf16[32,384]{1,0:T(8,128)(2,1)S(1)}, u32[]{:S(2)}, u32[]{:S(2)}) collective-permute-start(bf16[32,384]{1,0:T(8,128)(2,1)S(1)} %get-tuple-element.65.refs_0_), channel_id=1, source_target_pairs={{0,2},{2,0},{4,6},{6,4},{1,3},{3,1},{5,7},{7,5},{8,10},{10,8},{12,... | collective-permute-start | bytes 73736 | tf_op jit(solution)/shard_map/ppermute | solution.py:461
  17.8 4.0 %collective-permute-start.5 = (bf16[32,384]{1,0:T(8,128)(2,1)S(1)}, bf16[32,384]{1,0:T(8,128)(2,1)S(1)}, u32[]{:S(2)}, u32[]{:S(2)}) collective-permute-start(bf16[32,384]{1,0:T(8,128)(2,1)S(1)} %get-tuple-element.65.refs_0_), channel_id=1, source_target_pairs={{0,4},{2,6},{4,0},{6,2},{1,5},{3,7},{5,1},{7,3},{8,12},{10,14},{12... | collective-permute-start | bytes 73736 | tf_op jit(solution)/shard_map/ppermute | solution.py:461
  18.3 3.5 %collective-permute-start.6 = (bf16[32,384]{1,0:T(8,128)(2,1)S(1)}, bf16[32,384]{1,0:T(8,128)(2,1)S(1)}, u32[]{:S(2)}, u32[]{:S(2)}) collective-permute-start(bf16[32,384]{1,0:T(8,128)(2,1)S(1)} %get-tuple-element.65.refs_0_), channel_id=1, source_target_pairs={{0,6},{2,4},{4,2},{6,0},{1,7},{3,5},{5,3},{7,1},{8,14},{10,12},{12... | collective-permute-start | bytes 73736 | tf_op jit(solution)/shard_map/ppermute | solution.py:461
  21.8 5.9 %collective-permute-start.10 = (bf16[32,384]{1,0:T(8,128)(2,1)S(1)}, bf16[32,384]{1,0:T(8,128)(2,1)S(1)}, u32[]{:S(2)}, u32[]{:S(2)}) collective-permute-start(bf16[32,384]{1,0:T(8,128)(2,1)S(1)} %add_parts.2.refs_0_), channel_id=1, source_target_pairs={{0,24},{2,18},{4,28},{6,22},{8,16},{10,26},{12,20},{14,30},{16,8},... | collective-permute-start | bytes 73736 | tf_op jit(solution)/shard_map/ppermute | solution.py:467
  24.8 3.8 %collective-permute-start.9 = (bf16[32,384]{1,0:T(8,128)(2,1)S(1)}, bf16[32,384]{1,0:T(8,128)(2,1)S(1)}, u32[]{:S(2)}, u32[]{:S(2)}) collective-permute-start(bf16[32,384]{1,0:T(8,128)(2,1)S(1)} %add_parts.2.refs_0_), channel_id=1, source_target_pairs={{0,8},{8,0},{16,24},{24,16},{1,9},{9,1},{17,25},{25,17},{2,10},{10... | collective-permute-start | bytes 73736 | tf_op jit(solution)/shard_map/ppermute | solution.py:461
  27.7 1.2 %collective-permute-start.11 = (bf16[32,384]{1,0:T(8,128)(2,1)S(1)}, bf16[32,384]{1,0:T(8,128)(2,1)S(1)}, u32[]{:S(2)}, u32[]{:S(2)}) collective-permute-start(bf16[32,384]{1,0:T(8,128)(2,1)S(1)} %collective-permute-done.10.refs_2_), channel_id=1, source_target_pairs={{0,2},{2,0},{4,6},{6,4},{1,3},{3,1},{5,7},{7,5},{8,10},{10,8},{12,... | collective-permute-start | bytes 73736 | tf_op jit(solution)/shard_map/ppermute | solution.py:461
  28.9 3.9 %collective-permute-start.12 = (bf16[32,384]{1,0:T(8,128)(2,1)S(1)}, bf16[32,384]{1,0:T(8,128)(2,1)S(1)}, u32[]{:S(2)}, u32[]{:S(2)}) collective-permute-start(bf16[32,384]{1,0:T(8,128)(2,1)S(1)} %add_parts.3.refs_0_), channel_id=1, source_target_pairs={{0,1},{1,0},{2,3},{3,2},{4,5},{5,4},{6,7},{7,6},{8,9},{9,8},{10,11... | collective-permute-start | bytes 73736 | tf_op jit(solution)/shard_map/ppermute | solution.py:461
